TPU v7x, 32 devices: a whole 2x2x4 slice. The times are simulated.
32 devices in a mesh: seq: 8 (over z, x), exp: 4 (over y, core).
Axes of the slice: x: 2, y: 2, z: 4, core: 2. Of those that a mesh axis runs over, the one named last changes fastest.
Arguments:
- query: bfloat16 [4, 512, 2304], P('exp', 'seq'), may hold values from -40 to 40
- key_value: bfloat16 [4, 512, 2, 2304], P('exp', 'seq'), may hold values from -6 to 6
- residual: bfloat16 [4, 512, 2304], P('exp', 'seq'), may hold values from -6 to 6
- norm_gain: bfloat16 [2304], replicated, may hold values from 0.099609375 to 1.8984375
- segment_ids: int32 [4, 512], P('exp'), may hold values from 0 to 2, as said below
- routes: int32 [4, 512, 2], P('exp', 'seq'), may hold values from 0 to 7, all different within a row; in each aligned block of 64 rows (0 to 63, 64 to 127, ..., all dimensions but the last counted through in order) at most 24 rows name the same one
- gate_weights: float32 [4, 512, 2], P('exp', 'seq'), may hold values from 0.3 to 1
- page_table: int32 [4, 32], P('exp'), may hold values from 0 to 31, each once within a row
- w_gate: bfloat16 [8, 2304, 5760], P('exp', None, 'seq'), may hold values from -0.125 to 0.125
- w_up: bfloat16 [8, 2304, 5760], P('exp', None, 'seq'), may hold values from -0.125 to 0.125
- w_down: bfloat16 [8, 5760, 2304], P('exp', 'seq'), may hold values from -0.078125 to 0.078125
Outputs:
- layer_out: bfloat16 [4, 512, 2304], P('exp', 'seq')
- cache_pages: bfloat16 [4, 32, 16, 4608], P('exp', 'seq')
Inputs may be any that keep to these rules, and one draw needn't show every extreme that they name: `segment_ids`: within a pack the ids start at 0 and rise by 0 or 1 from one token to the next, ending at 2. The two experts of a token differ; among the 64 tokens of one device at most 24 routes name one expert, and in some device exactly 24 do. `page_table`: each row is a permutation of the slots.
All inputs are finite; a program needn't handle non-finite values.
Results may differ from a plain program's by a relative error of at most 0.013.
Values may be sent and summed in bfloat16 or wider, within the bound.
No kernel may reach another device: no remote copies, remote signals or barrier semaphores. Data moves between devices by JAX's collectives and lax.ppermute only.
A program may use at most 128 MiB of HBM per device.

v0:
```python
import math

import jax
import jax.numpy as jnp
from jax import lax
from jax.sharding import PartitionSpec as P

HEADS = 36
HEAD_DIM = 64
EXPERTS = 8
PAGE = 16
CAP = 24


def body(
    query,
    key_value,
    residual,
    norm_gain,
    segment_ids,
    routes,
    gate_weights,
    page_table,
    w_gate,
    w_up,
    w_down,
):
    rows_dev = query.shape[1]
    width = query.shape[2]
    my_seq = lax.axis_index("seq")
    exp_count = lax.axis_size("exp")
    seg_all = segment_ids[0]
    slot_table = page_table[0]
    first_row = my_seq * rows_dev
    query_places = first_row + jnp.arange(rows_dev, dtype=jnp.int32)
    query_segments = lax.dynamic_slice_in_dim(seg_all, first_row, rows_dev)
    queries = query[0].reshape(rows_dev, HEADS, HEAD_DIM)
    scale = 1.0 / math.sqrt(HEAD_DIM)
    first_slot = my_seq * (rows_dev // PAGE)
    cache_rows = jnp.arange(rows_dev, dtype=jnp.int32)
    page_ids = jnp.arange(slot_table.shape[0], dtype=jnp.int32)
    piece = lax.all_gather(key_value, "seq", axis=1, tiled=True)
    run_max = jnp.full((rows_dev, HEADS), -1e30, jnp.float32)
    totals = jnp.zeros((rows_dev, HEADS), jnp.float32)
    summed = jnp.zeros((rows_dev, HEADS, HEAD_DIM), jnp.float32)
    count = piece.shape[1]
    pairs = piece[0]
    key_places = jnp.arange(count, dtype=jnp.int32)
    visible = (query_segments[:, None] == seg_all[None, :]) & (
        key_places[None, :] <= query_places[:, None]
    )
    state = (run_max, totals, summed)
    old_max, old_totals, old_sum = state
    keys_here = pairs[:, 0].reshape(count, HEADS, HEAD_DIM)
    values_here = pairs[:, 1].reshape(count, HEADS, HEAD_DIM)
    scores = (
        jnp.einsum("qhd,khd->qhk", queries, keys_here, preferred_element_type=jnp.float32) * scale
    )
    scores = jnp.where(visible[:, None, :], scores, -jnp.inf)
    new_max = jnp.maximum(old_max, jnp.max(scores, axis=-1))
    probs = jnp.exp(scores - new_max[..., None])
    new_totals = jnp.sum(probs, axis=-1)
    weights = probs.astype(jnp.bfloat16)
    added = jnp.einsum("qhk,khd->qhd", weights, values_here, preferred_element_type=jnp.float32)
    state = (new_max, new_totals, added)
    page_match = (key_places // PAGE)[:, None] == page_ids[None, :]
    slots = jnp.sum(jnp.where(page_match, slot_table[None, :], 0), axis=1)
    local_rows = (slots - first_slot) * PAGE + key_places % PAGE
    placing = (cache_rows[:, None] == local_rows[None, :]).astype(jnp.bfloat16)
    cache = jnp.dot(placing, pairs.reshape(count, 2 * width), preferred_element_type=jnp.float32)
    run_max, totals, summed, cache = state + (cache,)
    context = (summed / totals[..., None]).reshape(rows_dev, width)
    stream = residual[0].astype(jnp.float32) + context
    normed = (
        stream
        * lax.rsqrt(jnp.mean(stream * stream, axis=-1, keepdims=True) + 1e-05)
        * norm_gain.astype(jnp.float32)
    ).astype(jnp.bfloat16)
    flat_routes = routes[0].reshape(rows_dev * 2)
    onehot = (flat_routes[:, None] == jnp.arange(EXPERTS, dtype=jnp.int32)[None, :]).astype(
        jnp.int32
    )
    before = jnp.cumsum(onehot, axis=0) - onehot
    slot = jnp.sum(before * onehot, axis=1)
    target = flat_routes * CAP + slot
    placing = (jnp.arange(EXPERTS * CAP, dtype=jnp.int32)[:, None] == target[None, :]).reshape(
        EXPERTS * CAP, rows_dev, 2
    )
    placing = jnp.sum(placing.astype(jnp.int32), axis=2).astype(jnp.bfloat16)
    outgoing = jnp.dot(placing, normed, preferred_element_type=jnp.float32).astype(jnp.bfloat16)
    local_count = EXPERTS // exp_count
    outgoing = outgoing.reshape(exp_count, local_count, CAP, width)
    arrived = lax.all_to_all(outgoing, "exp", split_axis=0, concat_axis=0, tiled=True)
    piece = lax.all_gather(arrived, "seq", axis=0, tiled=True)
    gate = jnp.einsum("mlcd,ldf->mlcf", piece, w_gate, preferred_element_type=jnp.float32)
    upper = jnp.einsum("mlcd,ldf->mlcf", piece, w_up, preferred_element_type=jnp.float32)
    hidden = (jax.nn.silu(gate) * upper).astype(jnp.bfloat16)
    reduced = lax.psum_scatter(
        jnp.einsum("mlcf,lfd->mlcd", hidden, w_down, preferred_element_type=jnp.float32).astype(
            jnp.bfloat16
        ),
        "seq",
        scatter_dimension=0,
        tiled=True,
    )
    expert_out = lax.all_to_all(reduced, "exp", split_axis=0, concat_axis=0, tiled=True)
    lookup = expert_out.reshape(EXPERTS * CAP, width)
    picked = jnp.take(lookup, target, axis=0).reshape(rows_dev, 2, width)
    mixture = jnp.sum(gate_weights[0][..., None] * picked.astype(jnp.float32), axis=1)
    layer_out = (stream + mixture).astype(jnp.bfloat16)
    cache_out = cache.astype(jnp.bfloat16).reshape(1, rows_dev // PAGE, PAGE, 2 * width)
    return (layer_out[None], cache_out)


def solution(mesh):
    in_specs = (
        P("exp", "seq", None),
        P("exp", "seq", None, None),
        P("exp", "seq", None),
        P(),
        P("exp", None),
        P("exp", "seq", None),
        P("exp", "seq", None),
        P("exp", None),
        P("exp", None, "seq"),
        P("exp", None, "seq"),
        P("exp", "seq", None),
    )
    out_specs = (P("exp", "seq", None), P("exp", "seq", None, None))
    return jax.shard_map(body, mesh=mesh, in_specs=in_specs, out_specs=out_specs, check_vma=False)
```

profile of v0, /device:TPU:0, one launch (start us, length us, event | category | flops | bytes accessed | tf_op | source)
XLA Modules:
  0.0 552.2 jit_solution(10527873955270274651)
XLA Ops:
  7.2 0.7 all-gather.3.cloned.1.call-update
  8.0 0.7 convert_element_type.65
  8.6 0.8 copy.61
  9.4 0.1 reshape_squeeze.18
  9.6 0.1 fusion.40
  9.6 0.2 reduce_window_sum.11
  9.8 0.2 select_reduce_fusion.1
  10.0 0.1 reduce_sum.62
  10.2 1.4 reshape_squeeze.16
  11.7 2.3 copy.65
  13.9 0.7 dynamic-slice_bitcast_fusion
  14.7 1.2 compare_and_fusion
  15.9 0.7 convert_reduce_fusion
  16.6 0.8 fusion.38
  17.4 75.4 %all-gather.3.cloned.1.call-done = bf16[1,512,2,2304]{3,2,0,1:T(2,128)(2,1)} async-done(((bf16[1,64,2,2304]{3,2,0,1:T(2,128)(2,1)}), bf16[1,512,2,2304]{3,2,0,1:T(2,128)(2,1)}) %all-gather.3.cloned.1.call-update) | async-done | bytes 4718608 | tf_op jit(solution)/shard_map/all_gather | solution.py:42
  92.8 11.0 %fusion.54 = (bf16[512,1,2304]{2,1,0:T(2,128)(2,1)}, bf16[512,1,2304]{2,1,0:T(2,128)(2,1)}) fusion(bf16[512,2,2304]{2,1,0:T(2,128)(2,1)} %bitcast.114), kind=kLoop, calls=%fused_computation.82 | loop fusion | bytes 9437184 | tf_op jit(solution)/shard_map/slice | solution.py:54
  103.7 10.8 %copy.56 = bf16[512,1,2304]{0,2,1:T(8,128)(2,1)S(1)} copy(bf16[512,1,2304]{2,1,0:T(2,128)(2,1)} %get-tuple-element.4) | data formatting | bytes 4718592 | tf_op jit(solution)/shard_map/slice | solution.py:54
  114.6 2.9 fusion.11
  117.5 11.0 %copy.58 = bf16[512,1,2304]{0,2,1:T(8,128)(2,1)} copy(bf16[512,1,2304]{2,1,0:T(2,128)(2,1)} %get-tuple-element.5) | data formatting | bytes 4718592 | tf_op jit(solution)/shard_map/slice | solution.py:55
  128.5 3.2 fusion.9
  131.7 3.4 multiply_reduce_fusion.1
  135.2 0.3 copy.64
  135.5 0.5 convolution_convert_fusion.1
  136.0 15.3 %all_to_all.10 = bf16[4,2,24,2304]{3,2,1,0:T(8,128)(2,1)S(1)} all-to-all(bf16[4,2,24,2304]{3,2,1,0:T(8,128)(2,1)S(1)} %bitcast.121), channel_id=1, replica_groups=mesh['seq'=8,'exp'=4] {'exp'}, dimensions={0} | all-to-all | bytes 1769472 | tf_op jit(solution)/shard_map/all_to_all | solution.py:93
  151.2 1.0 copy.66
  152.3 0.2 all-reduce.3.cloned.1.call-start
  152.5 106.0 %all-gather.5.cloned.1.call-done = bf16[32,2,24,2304]{3,2,0,1:T(8,128)(2,1)} async-done(((bf16[4,2,24,2304]{3,2,0,1:T(8,128)(2,1)}), bf16[32,2,24,2304]{3,2,0,1:T(8,128)(2,1)}) %all-gather.5.cloned.1.call-update) | async-done | bytes 7077904 | tf_op jit(solution)/shard_map/all_gather | solution.py:94
  258.4 11.3 %fusion.1 = f32[2,32,24,720]{3,2,1,0:T(8,128)} fusion(bf16[32,2,24,2304]{3,2,0,1:T(8,128)(2,1)} %all-gather.5.cloned.1.call-done, bf16[2,2304,720]{1,2,0:T(8,128)(2,1)} %param.20), kind=kOutput, calls=%fused_computation.3 | convolution fusion | flops 5096079360 | bytes 18137088 | tf_op jit(solution)/shard_map/mlcd,ldf->mlcf/dot_general | solution.py:96
  269.7 21.0 %convert_bitcast_fusion = bf16[32,2,24,2304]{3,2,0,1:T(8,128)(2,1)} fusion(bf16[2,720,2304]{2,1,0:T(8,128)(2,1)} %param.21, f32[2,32,24,720]{3,2,1,0:T(8,128)} %fusion.1, bf16[32,2,24,2304]{3,2,0,1:T(8,128)(2,1)} %all-gather.5.cloned.1.call-done, bf16[2,2304,720]{1,2,0:T(8,128)(2,1)} %param.19), kind=kOutput, calls=%fused_computation.1 | convolution fusion | flops 10202333184 | bytes 31850496 | tf_op jit(solution)/shard_map/mlcf,lfd->mlcd/dot_general | solution.py:99
  290.8 0.6 copy-done.6
  291.4 0.1 copy.68
  291.5 0.1 mul.106
  291.6 0.1 copy.60
  291.7 0.1 copy.63
  291.8 0.6 dynamic-slice.1
  293.1 0.1 select_reduce_fusion
  293.2 229.8 %all-reduce.3.cloned.1.call-done = bf16[32,2,24,2304]{3,2,0,1:T(8,128)(2,1)} async-done(((bf16[32,2,24,2304]{3,2,0,1:T(8,128)(2,1)}), bf16[32,2,24,2304]{3,2,0,1:T(8,128)(2,1)}) %all-reduce.3.cloned.1.call-update) | async-done | bytes 7077904
  522.9 1.2 constant_dynamic-slice_fusion
  524.2 1.0 copy.67
  525.2 3.7 all-to-all-start.1
  528.9 5.2 copy.74
  534.1 0.3 copy.59
  534.5 4.1 convolution_convert_fusion
  538.6 2.8 all-to-all-done.1
  541.3 1.0 gather_fusion
  542.3 0.2 gather.7
  542.5 2.3 multiply_reduce_fusion
  544.8 0.8 fusion.26
  (34 shorter events, 0.3 us)
Async XLA Ops:
  7.2 85.6 %all-gather.3.cloned.1.call-start = ((), (), s32[]{:S(2)}) async-start(), calls=%async_computation.2 | async-start | bytes 5308416 | tf_op jit(solution)/shard_map/all_gather | solution.py:42
  7.9 250.5 %all-gather.5.cloned.1.call-start = ((), (), s32[]{:S(2)}) async-start(), calls=%async_computation.3 | async-start | bytes 7962624 | tf_op jit(solution)/shard_map/all_gather | solution.py:94
  17.4 97.2 %copy-start.3 = (pred[64,512]{1,0:T(8,128)(4,1)}, pred[64,512]{1,0:T(8,128)(4,1)S(1)}, u32[]{:S(2)}) copy-start(pred[64,512]{1,0:T(8,128)(4,1)S(1)} %fusion.38) | copy-start | bytes 98308
  117.5 11.0 %copy-start.4 = (pred[64,512]{1,0:T(8,128)(4,1)S(1)}, pred[64,512]{1,0:T(8,128)(4,1)}, u32[]{:S(2)}) copy-start(pred[64,512]{1,0:T(8,128)(4,1)} %copy-done.3) | copy-start | bytes 98308
  117.5 14.2 %copy-start.2 = (f32[1,64,2304]{1,2,0:T(8,128)S(1)}, f32[1,64,2304]{1,2,0:T(8,128)}, u32[]{:S(2)}) copy-start(f32[1,64,2304]{1,2,0:T(8,128)} %copy.65) | copy-start | bytes 1769476
  128.5 3.2 copy-start.1
  131.7 3.8 copy-start
  131.7 3.8 copy-start.5
  152.3 370.7 %all-reduce.3.cloned.1.call-start = ((), (), s32[]{:S(2)}) async-start(), calls=%async_computation.4 | async-start | bytes 14155776
  290.7 0.7 copy-start.6
  290.7 0.9 copy-start.8
  290.7 1.0 copy-start.7
  290.7 1.1 copy-start.10
  290.7 2.4 copy-start.9
  525.2 16.2 %all-to-all-start.1 = ((bf16[4,2,24,2304]{3,2,1,0:T(8,128)(2,1)}), bf16[4,2,24,2304]{3,2,1,0:T(8,128)(2,1)S(1)}, u32[]{:S(2)}, u32[]{:S(2)}) async-start(bf16[4,2,24,2304]{3,2,1,0:T(8,128)(2,1)} %copy.67), calls=%async_computation.1 | async-start | bytes 1769472 | tf_op jit(solution)/shard_map/all_to_all | solution.py:106
Sparse Core Ops, SparseCore 0:
  10.2 82.5 all-gather.2
  152.4 106.0 all-gather.4
  290.9 232.0 all-reduce.2
where the time goes:
time: 553 us; the launch traced here: 552 us
  waiting for transfers between devices  415 us (75%)
  local copies, waits for them, and re-layouts  50.3 us (9%)
  matrix products  43.1 us (8%)
  blocking collectives  15.3 us (3%)
  between operations  14.7 us (3%)
  other arithmetic  10.3 us (2%)
    unnamed x4, waiting for transfers between devices  230 us
    all_gather x1, waiting for transfers between devices, body(): piece = lax.all_gather(arrived, 'seq', axis=0, tiled=True)  106 us
    all_gather x1, waiting for transfers between devices, body(): piece = lax.all_gather(key_value, 'seq', axis=1, tiled=True)  75.4 us
    slice x2, local copies, waits for them, and re-layouts, body(): keys_here = pairs[:, 0].reshape(count, HEADS, HEAD_DIM)  21.7 us
    dot_general x1, matrix products, body(): jnp.einsum('mlcf,lfd->mlcd', hidden, w_down, preferred_element_type=jnp.f...  21 us
    all_to_all x1, blocking collectives, body(): lax.all_to_all(outgoing, 'exp', split_axis=0, concat_axis=0, tiled=True)  15.3 us
    dot_general x1, matrix products, body(): jnp.einsum('mlcd,ldf->mlcf', piece, w_up, preferred_element_type=jnp.floa...  11.3 us
  transfers between devices with their start and end apart: 4, of which 4 were waited for; matrix products, arithmetic and copies ran while one was open for 4% of the time, Pallas kernels for 0%

commit v1 on v0

v1 whole, which is shorter than its diff:
```python
import functools
import math

import jax
import jax.numpy as jnp
from jax import lax
from jax.experimental import pallas as pl
from jax.experimental.pallas import tpu as pltpu
from jax.sharding import PartitionSpec as P

HEADS = 36
HEAD_DIM = 64
EXPERTS = 8
PAGE = 16
CAP = 24
CHUNK_BLOCKS = 8


def head_ranges(width, n_seq):
    share = width // n_seq
    firsts = [j * share // HEAD_DIM for j in range(n_seq)]
    count = max(-(-(j + 1) * share // HEAD_DIM) - firsts[j] for j in range(n_seq))
    firsts = [min(f, HEADS - count) for f in firsts]
    return share, firsts, count


def attention_kernel(heads, q_rows, packed_ref, seg_row_ref, seg_col_ref, out_ref):
    total = packed_ref.shape[0]
    span = heads * HEAD_DIM
    scale = 1.0 / math.sqrt(HEAD_DIM)
    for start in range(0, total, q_rows):
        end = start + q_rows
        q_place = start + lax.broadcasted_iota(jnp.int32, (q_rows, end), 0)
        k_place = lax.broadcasted_iota(jnp.int32, (q_rows, end), 1)
        visible = (seg_col_ref[start:end, :] == seg_row_ref[:, :end]) & (k_place <= q_place)
        parts = []
        for h in range(heads):
            a = h * HEAD_DIM
            q = packed_ref[start:end, a : a + HEAD_DIM]
            k = packed_ref[:end, span + a : span + a + HEAD_DIM]
            v = packed_ref[:end, 2 * span + a : 2 * span + a + HEAD_DIM]
            s = lax.dot_general(q, k, (((1,), (1,)), ((), ())), preferred_element_type=jnp.float32)
            s = jnp.where(visible, s * scale, -1e30)
            top = jnp.max(s, axis=1, keepdims=True)
            p = jnp.exp(s - top)
            denominator = jnp.sum(p, axis=1, keepdims=True)
            o = jnp.dot(p.astype(jnp.bfloat16), v, preferred_element_type=jnp.float32)
            parts.append((o / denominator).astype(jnp.bfloat16))
        out_ref[start:end, :] = jnp.concatenate(parts, axis=1)


def attention(packed, segments, heads):
    total = packed.shape[0]
    span = heads * HEAD_DIM
    return pl.pallas_call(
        functools.partial(attention_kernel, heads, 128),
        out_shape=jax.ShapeDtypeStruct((total, span), jnp.bfloat16),
        compiler_params=pltpu.CompilerParams(vmem_limit_bytes=40 * 1024 * 1024),
        cost_estimate=pl.CostEstimate(
            flops=4 * total * total * span, bytes_accessed=8 * total * span, transcendentals=total * total * heads
        ),
    )(packed, segments[None, :], segments[:, None])


def expert_kernel(
    local, rows, tokens, first_ref, x_ref, tgt_ref, gates_ref, wg_ref, wu_ref, wd_ref, out_ref, kept_ref
):
    le = pl.program_id(0)
    chunk = pl.program_id(1)

    def selection(which):
        base = (first_ref[0] + which) * CAP
        row_id = lax.broadcasted_iota(jnp.int32, (rows, tokens), 0)
        block = lax.broadcasted_iota(jnp.int32, (1, tokens), 1) // 64
        picks, weights = None, None
        for j in range(2):
            slot = tgt_ref[0, j : j + 1, :] - base
            place = jnp.where((slot >= 0) & (slot < CAP), block * CAP + slot, -1)
            hit = row_id == place
            gate = jnp.where(hit, gates_ref[0, j : j + 1, :], 0.0)
            picks = hit if picks is None else picks | hit
            weights = gate if weights is None else weights + gate
        return picks.astype(jnp.float32).astype(jnp.bfloat16), jnp.sum(weights, axis=1, keepdims=True)

    pick, weight = selection(le)
    chosen = jnp.dot(pick, x_ref[...], preferred_element_type=jnp.float32).astype(jnp.bfloat16)
    gate = jnp.dot(chosen, wg_ref[0], preferred_element_type=jnp.float32)
    upper = jnp.dot(chosen, wu_ref[0], preferred_element_type=jnp.float32)
    hidden = (gate / (1.0 + jnp.exp(-gate)) * upper).astype(jnp.bfloat16)
    y = jnp.dot(hidden, wd_ref[0], preferred_element_type=jnp.float32)
    y = (y * weight).astype(jnp.bfloat16)

    if local > 1:

        @pl.when(le < local - 1)
        def _():
            kept_ref[le, chunk] = y

    @pl.when(le == local - 1)
    def _():
        total = lax.dot_general(pick, y, (((0,), (0,)), ((), ())), preferred_element_type=jnp.float32)
        for other in range(local - 1):
            pick_o, _ = selection(other)
            total += lax.dot_general(
                pick_o, kept_ref[other, chunk], (((0,), (0,)), ((), ())), preferred_element_type=jnp.float32
            )
        out_ref[...] = total.astype(jnp.bfloat16)


def experts(x, tgt, gates, w_gate, w_up, w_down, first):
    local, width, hidden = w_gate.shape
    chunks, _, tokens = tgt.shape
    rows = tokens // 64 * CAP
    last = local - 1
    return pl.pallas_call(
        functools.partial(expert_kernel, local, rows, tokens),
        out_shape=jax.ShapeDtypeStruct(x.shape, jnp.bfloat16),
        grid=(local, chunks),
        in_specs=[
            pl.BlockSpec(memory_space=pltpu.SMEM),
            pl.BlockSpec((tokens, width), lambda e, c: (c, 0)),
            pl.BlockSpec((1, 2, tokens), lambda e, c: (c, 0, 0)),
            pl.BlockSpec((1, 2, tokens), lambda e, c: (c, 0, 0)),
            pl.BlockSpec((1, width, hidden), lambda e, c: (e, 0, 0)),
            pl.BlockSpec((1, width, hidden), lambda e, c: (e, 0, 0)),
            pl.BlockSpec((1, hidden, width), lambda e, c: (e, 0, 0)),
        ],
        out_specs=pl.BlockSpec((tokens, width), lambda e, c: (jnp.where(e == last, c, 0), 0)),
        scratch_shapes=[pltpu.VMEM((max(last, 1), chunks if last else 1, rows, width), jnp.bfloat16)],
        compiler_params=pltpu.CompilerParams(vmem_limit_bytes=58 * 1024 * 1024),
        cost_estimate=pl.CostEstimate(
            flops=6 * local * chunks * rows * width * hidden,
            bytes_accessed=6 * local * width * hidden + 6 * chunks * tokens * width,
            transcendentals=local * chunks * rows * hidden,
        ),
    )(first, x, tgt, gates, w_gate, w_up, w_down)


def body(
    n_seq,
    n_exp,
    query,
    key_value,
    residual,
    norm_gain,
    segment_ids,
    routes,
    gate_weights,
    page_table,
    w_gate,
    w_up,
    w_down,
):
    rows_dev, width = query.shape[1:]
    everyone = ("exp", "seq")
    group = segment_ids.shape[1]
    share, firsts, heads = head_ranges(width, n_seq)
    span = heads * HEAD_DIM

    flat = routes[0].reshape(rows_dev * 2)
    onehot = (flat[:, None] == jnp.arange(EXPERTS, dtype=jnp.int32)[None, :]).astype(jnp.int32)
    before = jnp.cumsum(onehot, axis=0) - onehot
    target = (flat * CAP + jnp.sum(before * onehot, axis=1)).reshape(rows_dev, 2)
    facts = jnp.concatenate([target.astype(jnp.float32), gate_weights[0]], axis=1).T
    facts = lax.all_gather(facts, everyone, axis=0, tiled=False)
    blocks = n_seq * n_exp
    facts = facts.reshape(blocks // CHUNK_BLOCKS, CHUNK_BLOCKS, 4, rows_dev).transpose(0, 2, 1, 3)
    facts = facts.reshape(blocks // CHUNK_BLOCKS, 4, CHUNK_BLOCKS * rows_dev)
    tgt = facts[:, :2].astype(jnp.int32)
    gates = facts[:, 2:]

    keys, values = key_value[0, :, 0], key_value[0, :, 1]

    def spans(a):
        return jnp.stack([a[:, f * HEAD_DIM : f * HEAD_DIM + span] for f in firsts])

    packed = jnp.concatenate([spans(query[0]), spans(keys), spans(values)], axis=2)
    packed = lax.all_to_all(packed, "seq", split_axis=0, concat_axis=0, tiled=True)
    packed = packed.reshape(group, 3 * span)
    context = attention(packed, segment_ids[0], heads)
    context = lax.all_to_all(
        context.reshape(n_seq, rows_dev, span), "seq", split_axis=0, concat_axis=0, tiled=True
    )
    offsets = [j * share - firsts[j] * HEAD_DIM for j in range(n_seq)]

    def unspan(a):
        return jnp.concatenate([a[j][..., offsets[j] : offsets[j] + share] for j in range(n_seq)], axis=-1)

    stream = residual[0].astype(jnp.float32) + unspan(context).astype(jnp.float32)
    normed = (
        stream
        * lax.rsqrt(jnp.mean(stream * stream, axis=-1, keepdims=True) + 1e-05)
        * norm_gain.astype(jnp.float32)
    ).astype(jnp.bfloat16)

    pages = packed[:, span:].reshape(group // PAGE, PAGE, 2 * span)
    slots = jnp.arange(group // PAGE, dtype=jnp.int32)
    order = jnp.sum(jnp.where(page_table[0][None, :] == slots[:, None], slots[None, :], 0), axis=1)
    pages = jnp.take(pages, order, axis=0)
    pages = pages.reshape(n_seq, rows_dev, 2 * span)
    pages = lax.all_to_all(pages, "seq", split_axis=0, concat_axis=0, tiled=True)
    cache = jnp.concatenate([unspan(pages[..., :span]), unspan(pages[..., span:])], axis=-1)
    cache = cache.reshape(1, rows_dev // PAGE, PAGE, 2 * width)

    everything = lax.all_gather(normed, everyone, axis=0, tiled=True)
    first = (lax.axis_index("exp") * (EXPERTS // n_exp)).astype(jnp.int32).reshape(1)
    partial = experts(everything, tgt, gates, w_gate, w_up, w_down, first)
    mixture = lax.psum_scatter(partial, everyone, scatter_dimension=0, tiled=True)
    layer_out = (stream + mixture.astype(jnp.float32)).astype(jnp.bfloat16)
    return (layer_out[None], cache)


def solution(mesh):
    in_specs = (
        P("exp", "seq", None),
        P("exp", "seq", None, None),
        P("exp", "seq", None),
        P(),
        P("exp", None),
        P("exp", "seq", None),
        P("exp", "seq", None),
        P("exp", None),
        P("exp", None, "seq"),
        P("exp", None, "seq"),
        P("exp", "seq", None),
    )
    out_specs = (P("exp", "seq", None), P("exp", "seq", None, None))
    run = functools.partial(body, mesh.shape["seq"], mesh.shape["exp"])
    return jax.shard_map(run, mesh=mesh, in_specs=in_specs, out_specs=out_specs, check_vma=False)
```

time: 553 us -> 344 us (0.62)
  waiting for transfers between devices: 415 us -> 147 us
  blocking collectives: 15.3 us -> 85.3 us
  Pallas kernels: 0 us -> 43.2 us
  matrix products: 43.1 us -> 0 us
  local copies, waits for them, and re-layouts: 50.3 us -> 36 us
  starting transfers between devices: 4.02 us -> 10.9 us
    unnamed x4 -> x2, waiting for transfers between devices: 230 us -> 0.03 us
    all_gather x2 -> x1, waiting for transfers between devices: 181 us -> 0.01 us  [body(): everything = lax.all_gather(normed, everyone, axis=0, tiled=True)]
    reduce_scatter x0 -> x1, waiting for transfers between devices: none -> 110 us  [body(): lax.psum_scatter(partial, everyone, scatter_dimension=0, tiled=True)]
    all_gather x0 -> x1, blocking collectives: none -> 68.2 us  [body(): facts = lax.all_gather(facts, everyone, axis=0, tiled=False)]
    pallas_call x0 -> x2, Pallas kernels: none -> 43.2 us  [the longest x1 37.6 us: experts(): pl.pallas_call(functools.partial(expert_kernel, local, rows, tokens), out...]
    dot_general x6 -> x0, matrix products: 43.1 us -> none  [the longest x1 21 us: body(): jnp.einsum('mlcf,lfd->mlcd', hidden, w_down, preferred_element_type=jnp.f...]
    all_to_all x1 -> x2, waiting for transfers between devices: 2.75 us -> 37.4 us  [the longest x1 25.6 us: body(): lax.all_to_all(packed, 'seq', split_axis=0, concat_axis=0, tiled=True)]
    slice x3 -> x14, local copies, waits for them, and re-layouts: 32.8 us -> 3.77 us  [the longest x1 2.33 us: body(): keys, values = (key_value[0, :, 0], key_value[0, :, 1])]
  transfers between devices with their start and end apart: 4 -> 4, of which waited for: 4 -> 3; matrix products, arithmetic and copies ran while one was open for 4% -> 8% of each run, Pallas kernels for 0% -> 0%
where the time goes in v1:
time: 344 us; the launch traced here: 343 us
  waiting for transfers between devices  147 us (43%)
  blocking collectives  85.3 us (25%)
  Pallas kernels  43.2 us (13%)
  local copies, waits for them, and re-layouts  36 us (10%)
  between operations  14.4 us (4%)
  starting transfers between devices  10.9 us (3%)
  other arithmetic  5.51 us (2%)
    reduce_scatter x1, waiting for transfers between devices, body(): lax.psum_scatter(partial, everyone, scatter_dimension=0, tiled=True)  110 us
    all_gather x1, blocking collectives, body(): facts = lax.all_gather(facts, everyone, axis=0, tiled=False)  68.2 us
    pallas_call x1, Pallas kernels, experts(): pl.pallas_call(functools.partial(expert_kernel, local, rows, tokens), out...  37.6 us
    unnamed x36, local copies, waits for them, and re-layouts  28 us
    all_to_all x1, waiting for transfers between devices, body(): lax.all_to_all(packed, 'seq', split_axis=0, concat_axis=0, tiled=True)  25.6 us
    all_to_all x1, blocking collectives, body(): lax.all_to_all(pages, 'seq', split_axis=0, concat_axis=0, tiled=True)  17.1 us
    all_to_all x1, waiting for transfers between devices, body(): lax.all_to_all(context.reshape(n_seq, rows_dev, span), 'seq', split_axis=...  11.8 us
    all_to_all x1, starting transfers between devices, body(): lax.all_to_all(packed, 'seq', split_axis=0, concat_axis=0, tiled=True)  7.25 us
  transfers between devices with their start and end apart: 4, of which 3 were waited for; matrix products, arithmetic and copies ran while one was open for 8% of the time, Pallas kernels for 0%

profile of v1, /device:TPU:0, one launch (start us, length us, event | category | flops | bytes accessed | tf_op | source)
XLA Modules:
  0.0 342.8 jit_solution(3641370443856554548)
XLA Ops:
  7.2 0.8 fusion.25
  8.0 0.8 fusion.24
  8.8 0.9 fusion.23
  9.7 0.9 fusion.22
  10.7 0.8 fusion.21
  11.5 0.8 fusion.20
  12.3 0.9 fusion.19
  13.2 0.9 fusion.18
  14.1 2.3 fusion.28
  16.5 0.1 copy_bitcast_fusion
  16.6 0.1 fusion.7
  16.7 0.1 fusion.6
  16.8 0.1 fusion.3
  17.1 0.1 fusion.15
  17.2 0.1 fusion.14
  17.3 0.1 fusion.11
  17.5 1.3 pad_maximum_fusion
  18.8 7.3 %all-to-all-start = ((bf16[8,64,960]{2,1,0:T(8,128)(2,1)}), bf16[8,64,960]{2,1,0:T(8,128)(2,1)S(1)}, u32[]{:S(2)}, u32[]{:S(2)}) async-start(bf16[8,64,960]{2,1,0:T(8,128)(2,1)} %pad_maximum_fusion), calls=%async_computation | async-start | bytes 2097152 | tf_op jit(solution)/shard_map/all_to_all | solution.py:178
  26.0 0.1 copy.37.seg_col_ref
  26.2 25.6 %all-to-all-done = bf16[8,64,960]{2,1,0:T(8,128)(2,1)S(1)} async-done(((bf16[8,64,960]{2,1,0:T(8,128)(2,1)}), bf16[8,64,960]{2,1,0:T(8,128)(2,1)S(1)}, u32[]{:S(2)}, u32[]{:S(2)}) %all-to-all-start) | async-done | bytes 983072 | tf_op jit(solution)/shard_map/all_to_all | solution.py:178
  51.8 5.6 %shard_map.122 = bf16[512,320]{1,0:T(8,128)(2,1)} custom-call(bf16[512,960]{1,0:T(8,128)(2,1)S(1)} %bitcast.197, s32[1,512]{1,0:T(1,128)S(1)} %copy-done, s32[512,1]{1,0:T(8,128)S(1)} %copy.37.seg_col_ref), custom_call_target="tpu_custom_call" | custom-call | flops 335544320 | bytes 1310720 | tf_op jit(solution)/shard_map/pallas_call | solution.py:55
  57.4 3.6 %all-to-all-start.1 = ((bf16[8,64,320]{2,1,0:T(8,128)(2,1)}), bf16[8,64,320]{2,1,0:T(8,128)(2,1)S(1)}, u32[]{:S(2)}, u32[]{:S(2)}) async-start(bf16[8,64,320]{2,1,0:T(8,128)(2,1)} %bitcast.30), calls=%async_computation.1 | async-start | bytes 786432 | tf_op jit(solution)/shard_map/all_to_all | solution.py:181
  61.0 11.8 %all-to-all-done.1 = bf16[8,64,320]{2,1,0:T(8,128)(2,1)S(1)} async-done(((bf16[8,64,320]{2,1,0:T(8,128)(2,1)}), bf16[8,64,320]{2,1,0:T(8,128)(2,1)S(1)}, u32[]{:S(2)}, u32[]{:S(2)}) %all-to-all-start.1) | async-done | bytes 327712 | tf_op jit(solution)/shard_map/all_to_all | solution.py:181
  73.2 0.2 concatenate.13
  73.5 0.2 multiply_reduce_fusion
  73.7 0.8 multiply_convert_fusion
  74.6 0.1 copy.38
  74.7 0.1 eq.30
  74.9 0.2 reduce_window_sum.11
  75.1 0.2 select_reduce_fusion
  75.3 0.1 reduce_sum.35
  75.5 68.2 %all-gather.1 = f32[32,4,64]{2,1,0:T(4,128)S(1)} all-gather(f32[1,4,64]{2,1,0:T(4,128)S(1)} %maximum_bitcast_fusion), channel_id=2, replica_groups=mesh['seq'=8,'exp'=4] {'exp','seq'}, dimensions={0}, use_global_device_ids=true | all-gather | bytes 33792 | tf_op jit(solution)/shard_map/all_gather | solution.py:165
  143.8 0.1 reshape.70
  143.8 10.3 %copy.41.wg_ref = bf16[2,2304,720]{2,1,0:T(8,128)(2,1)} copy(bf16[2,2304,720]{1,2,0:T(8,128)(2,1)} %param.19) | data formatting | bytes 13271040 | tf_op args[8]
  154.2 10.2 %copy.42.wu_ref = bf16[2,2304,720]{2,1,0:T(8,128)(2,1)} copy(bf16[2,2304,720]{1,2,0:T(8,128)(2,1)} %param.20) | data formatting | bytes 13271040 | tf_op args[9]
  164.4 0.6 fusion.29
  165.0 37.6 %shard_map.123 = bf16[2048,2304]{1,0:T(8,128)(2,1)} custom-call(s32[1]{0:T(128)} %bitcast.39.first_ref, bf16[2048,2304]{1,0:T(8,128)(2,1)} %all-gather.4.cloned.1.call-done.x_ref, s32[4,2,512]{2,1,0:T(2,128)} %get-tuple-element.29.tgt_ref, f32[4,2,512]{2,1,0:T(2,128)} %get-tuple-element.28.gates_ref, bf16[2,2304,720]{2,1,0:T(8,128)(2,1)} %copy.41.wg_ref, ...), custom_call_target="tpu_custom_call" | custom-call | flops 15288238080 | bytes 48218112 | tf_op jit(solution)/shard_map/pallas_call | solution.py:115
  202.6 0.6 copy-done.5
  203.2 0.1 select_reduce_fusion.1
  203.5 0.1 broadcast_in_dim.38
  203.6 0.4 slice.370
  204.1 0.7 gather_fusion
  204.8 0.2 bitcast_select_fusion
  204.9 17.1 %all_to_all.15 = bf16[8,64,640]{2,1,0:T(8,128)(2,1)S(1)} all-to-all(bf16[8,64,640]{2,1,0:T(8,128)(2,1)S(1)} %bitcast_select_fusion), channel_id=1, replica_groups=mesh['seq'=8,'exp'=4] {'seq'}, dimensions={0} | all-to-all | bytes 1310720 | tf_op jit(solution)/shard_map/all_to_all | solution.py:201
  222.0 0.2 slice_bitcast_fusion
  222.9 1.2 concatenate.15
  224.2 110.0 %reduce-scatter.2.cloned.1.call-done = bf16[64,2304]{1,0:T(8,128)(2,1)} async-done(((bf16[2048,2304]{1,0:T(8,128)(2,1)}), bf16[64,2304]{1,0:T(8,128)(2,1)}) %reduce-scatter.2.cloned.1.call-update) | async-done | bytes 294928 | tf_op jit(solution)/shard_map/reduce_scatter | solution.py:208
  334.2 1.8 fusion
  (51 shorter events, 1.8 us)
Async XLA Ops:
  7.2 18.9 %copy-start = (s32[1,512]{1,0:T(1,128)S(1)}, s32[1,512]{1,0:T(1,128)}, u32[]{:S(2)}) copy-start(s32[1,512]{1,0:T(1,128)} %seg_row_ref.1) | copy-start | bytes 6148
  14.1 46.9 %copy-start.2 = (bf16[2304]{0:T(1024)(128)(2,1)S(1)}, bf16[2304]{0:T(1024)(128)(2,1)}, u32[]{:S(2)}) copy-start(bf16[2304]{0:T(1024)(128)(2,1)} %param.14) | copy-start | bytes 13828
  16.5 57.0 %copy-start.1 = (bf16[1,64,2304]{2,1,0:T(8,128)(2,1)S(1)}, bf16[1,64,2304]{2,1,0:T(8,128)(2,1)}, u32[]{:S(2)}) copy-start(bf16[1,64,2304]{2,1,0:T(8,128)(2,1)} %param.13) | copy-start | bytes 884740
  16.6 58.0 %copy-start.3 = (s32[1,64,2]{1,2,0:T(2,128)S(1)}, s32[1,64,2]{1,2,0:T(2,128)}, u32[]{:S(2)}) copy-start(s32[1,64,2]{1,2,0:T(2,128)} %param.16) | copy-start | bytes 1540
  16.7 58.8 %copy-start.4 = (f32[1,64,2]{1,2,0:T(2,128)S(1)}, f32[1,64,2]{1,2,0:T(2,128)}, u32[]{:S(2)}) copy-start(f32[1,64,2]{1,2,0:T(2,128)} %param.17) | copy-start | bytes 1540
  18.8 33.0 %all-to-all-start = ((bf16[8,64,960]{2,1,0:T(8,128)(2,1)}), bf16[8,64,960]{2,1,0:T(8,128)(2,1)S(1)}, u32[]{:S(2)}, u32[]{:S(2)}) async-start(bf16[8,64,960]{2,1,0:T(8,128)(2,1)} %pad_maximum_fusion), calls=%async_computation | async-start | bytes 2097152 | tf_op jit(solution)/shard_map/all_to_all | solution.py:178
  57.4 15.4 %all-to-all-start.1 = ((bf16[8,64,320]{2,1,0:T(8,128)(2,1)}), bf16[8,64,320]{2,1,0:T(8,128)(2,1)S(1)}, u32[]{:S(2)}, u32[]{:S(2)}) async-start(bf16[8,64,320]{2,1,0:T(8,128)(2,1)} %bitcast.30), calls=%async_computation.1 | async-start | bytes 786432 | tf_op jit(solution)/shard_map/all_to_all | solution.py:181
  61.0 104.0 %all-gather.4.cloned.1.call-start = ((), (), s32[]{:S(2)}) async-start(), calls=%async_computation.4 | async-start | bytes 9732096 | tf_op jit(solution)/shard_map/all_gather | solution.py:205
  74.5 259.6 %reduce-scatter.2.cloned.1.call-start = ((), (), s32[]{:S(2)}) async-start(), calls=%async_computation.5 | async-start | bytes 9732096 | tf_op jit(solution)/shard_map/reduce_scatter | solution.py:208
  202.6 0.7 copy-start.5
Sparse Core Ops, SparseCore 0:
  74.7 81.4 all-gather.3
  202.7 131.3 reduce-scatter.1

commit v2 on v1

--- a/solution.py
+++ b/solution.py
@@ -62,6 +62,10 @@
     )(packed, segments[None, :], segments[:, None])
 
 
+def dot_t(a, b):
+    return lax.dot_general(a, b, (((1,), (1,)), ((), ())), preferred_element_type=jnp.float32)
+
+
 def expert_kernel(
     local, rows, tokens, first_ref, x_ref, tgt_ref, gates_ref, wg_ref, wu_ref, wd_ref, out_ref, kept_ref
 ):
@@ -84,8 +88,8 @@
 
     pick, weight = selection(le)
     chosen = jnp.dot(pick, x_ref[...], preferred_element_type=jnp.float32).astype(jnp.bfloat16)
-    gate = jnp.dot(chosen, wg_ref[0], preferred_element_type=jnp.float32)
-    upper = jnp.dot(chosen, wu_ref[0], preferred_element_type=jnp.float32)
+    gate = dot_t(chosen, wg_ref[0])
+    upper = dot_t(chosen, wu_ref[0])
     hidden = (gate / (1.0 + jnp.exp(-gate)) * upper).astype(jnp.bfloat16)
     y = jnp.dot(hidden, wd_ref[0], preferred_element_type=jnp.float32)
     y = (y * weight).astype(jnp.bfloat16)
@@ -108,7 +112,7 @@
 
 
 def experts(x, tgt, gates, w_gate, w_up, w_down, first):
-    local, width, hidden = w_gate.shape
+    local, hidden, width = w_gate.shape
     chunks, _, tokens = tgt.shape
     rows = tokens // 64 * CAP
     last = local - 1
@@ -121,8 +125,8 @@
             pl.BlockSpec((tokens, width), lambda e, c: (c, 0)),
             pl.BlockSpec((1, 2, tokens), lambda e, c: (c, 0, 0)),
             pl.BlockSpec((1, 2, tokens), lambda e, c: (c, 0, 0)),
-            pl.BlockSpec((1, width, hidden), lambda e, c: (e, 0, 0)),
-            pl.BlockSpec((1, width, hidden), lambda e, c: (e, 0, 0)),
+            pl.BlockSpec((1, hidden, width), lambda e, c: (e, 0, 0)),
+            pl.BlockSpec((1, hidden, width), lambda e, c: (e, 0, 0)),
             pl.BlockSpec((1, hidden, width), lambda e, c: (e, 0, 0)),
         ],
         out_specs=pl.BlockSpec((tokens, width), lambda e, c: (jnp.where(e == last, c, 0), 0)),
@@ -134,6 +138,156 @@
             transcendentals=local * chunks * rows * hidden,
         ),
     )(first, x, tgt, gates, w_gate, w_up, w_down)
+
+
+def chunk_kernel(
+    local, pieces, rows, tokens, parts, first_ref, row_ref, col_ref, wg_ref, wu_ref, wd_ref, *rest
+):
+    piece_refs = rest[:pieces]
+    keep_ref, send_ref, chosen_ref, sum_ref, y_ref = rest[pieces:]
+    le = pl.program_id(0)
+    part = pl.program_id(1)
+    rows_dev = tokens // pieces
+
+    @pl.when(part == 0)
+    def _():
+        base = (first_ref[0] + le) * CAP
+        row_id = lax.broadcasted_iota(jnp.int32, (rows, tokens), 0)
+        shift = lax.broadcasted_iota(jnp.int32, (1, tokens), 1) // rows_dev * CAP
+        pick = None
+        for j in range(2):
+            slot = row_ref[j : j + 1, :].astype(jnp.int32) - base
+            hit = row_id == jnp.where((slot >= 0) & (slot < CAP), shift + slot, -1)
+            pick = hit if pick is None else pick | hit
+        x = jnp.concatenate([p[...] for p in piece_refs], axis=0)
+        pick = pick.astype(jnp.float32).astype(jnp.bfloat16)
+        chosen_ref[...] = jnp.dot(pick, x, preferred_element_type=jnp.float32).astype(jnp.bfloat16)
+
+    chosen = chosen_ref[...]
+    gate = dot_t(chosen, wg_ref[0])
+    upper = dot_t(chosen, wu_ref[0])
+    hidden = (gate / (1.0 + jnp.exp(-gate)) * upper).astype(jnp.bfloat16)
+    y = jnp.dot(hidden, wd_ref[0], preferred_element_type=jnp.float32)
+
+    @pl.when(part == 0)
+    def _():
+        sum_ref[...] = y
+
+    @pl.when((part > 0) & (part < parts - 1))
+    def _():
+        sum_ref[...] += y
+
+    @pl.when(part == parts - 1)
+    def _():
+        base = (first_ref[0] + le) * CAP
+        row_id = lax.broadcasted_iota(jnp.int32, (rows, tokens), 0)
+        shift = lax.broadcasted_iota(jnp.int32, (1, tokens), 1) // rows_dev * CAP
+        weights = jnp.zeros((rows, tokens), jnp.float32)
+        for j in range(2):
+            slot = row_ref[j : j + 1, :].astype(jnp.int32) - base
+            hit = row_id == jnp.where((slot >= 0) & (slot < CAP), shift + slot, -1)
+            weights = weights + jnp.where(hit, row_ref[2 + j : 3 + j, :], 0.0)
+        weight = jnp.sum(weights, axis=1, keepdims=True)
+        y_ref[pl.ds(pl.multiple_of(le * rows, rows), rows), :] = ((sum_ref[...] + y) * weight).astype(jnp.bfloat16)
+
+    @pl.when((part == parts - 1) & (le == local - 1))
+    def _():
+        lane = lax.broadcasted_iota(jnp.int32, (tokens, local * rows), 1)
+        shift = lax.broadcasted_iota(jnp.int32, (tokens, 1), 0) // rows_dev * CAP
+        place = None
+        for e in range(local):
+            base = (first_ref[0] + e) * CAP
+            for j in range(2):
+                slot = col_ref[:, j : j + 1].astype(jnp.int32) - base
+                hit = lane == jnp.where((slot >= 0) & (slot < CAP), e * rows + shift + slot, -1)
+                place = hit if place is None else place | hit
+        place = place.astype(jnp.float32).astype(jnp.bfloat16)
+        half = tokens // 2
+        keep_ref[...] = jnp.dot(place[:half], y_ref[...], preferred_element_type=jnp.float32).astype(jnp.bfloat16)
+        send_ref[...] = jnp.dot(place[half:], y_ref[...], preferred_element_type=jnp.float32).astype(jnp.bfloat16)
+
+
+def chunk_experts(pieces, facts, w_gate, w_up, w_down, first):
+    local, hidden, width = w_gate.shape
+    tokens = facts.shape[1]
+    rows = len(pieces) * CAP
+    parts = 3
+    step = hidden // parts
+    whole = lambda e, f: (0, 0)
+    weights = pl.BlockSpec((1, step, width), lambda e, f: (e, f, 0))
+    piece = pl.BlockSpec(pieces[0].shape, whole)
+    half = jax.ShapeDtypeStruct((tokens // 2, width), jnp.bfloat16)
+    return pl.pallas_call(
+        functools.partial(chunk_kernel, local, len(pieces), rows, tokens, parts),
+        out_shape=(half, half),
+        grid=(local, parts),
+        in_specs=[
+            pl.BlockSpec(memory_space=pltpu.SMEM),
+            pl.BlockSpec((4, tokens), whole),
+            pl.BlockSpec((tokens, 4), whole),
+            weights,
+            weights,
+            weights,
+        ]
+        + [piece] * len(pieces),
+        out_specs=(pl.BlockSpec(half.shape, whole), pl.BlockSpec(half.shape, whole)),
+        scratch_shapes=[
+            pltpu.VMEM((rows, width), jnp.bfloat16),
+            pltpu.VMEM((rows, width), jnp.float32),
+            pltpu.VMEM((local * rows, width), jnp.bfloat16),
+        ],
+        compiler_params=pltpu.CompilerParams(vmem_limit_bytes=48 * 1024 * 1024),
+        cost_estimate=pl.CostEstimate(
+            flops=6 * local * rows * width * hidden,
+            bytes_accessed=6 * local * width * hidden + 4 * tokens * width,
+            transcendentals=local * rows * hidden,
+        ),
+    )(first, facts, facts.T, w_gate, w_up, w_down, *pieces)
+
+
+def swap(a, axis, size, distance):
+    return lax.ppermute(a, axis, [(i, i ^ distance) for i in range(size)])
+
+
+def add(a, b):
+    return (a.astype(jnp.float32) + b.astype(jnp.float32)).astype(jnp.bfloat16)
+
+
+def exchange_experts(normed, facts, w_gate, w_up, w_down, first, n_seq, n_exp):
+    rows_dev, width = normed.shape
+    over = {
+        "x": lambda a: swap(a, "seq", n_seq, 1),
+        "y": lambda a: swap(a, "exp", n_exp, 2),
+        "c": lambda a: swap(a, "exp", n_exp, 1),
+    }
+    distance = {"x": (0, 1), "y": (2, 0), "c": (1, 0)}
+    me_seq, me_exp = lax.axis_index("seq"), lax.axis_index("exp")
+    depth = n_seq // 2
+    mixture = None
+    starts = [normed] + [swap(normed, "seq", n_seq, 2 * k) for k in range(1, depth)]
+    chunks = []
+    for k in range(depth):
+        f, g = ("x", "y") if k % 2 == 0 else ("y", "x")
+        by_f, by_g = over[f](starts[k]), over[g](starts[k])
+        pieces = [starts[k], by_g, by_f, over[g](by_f)]
+        pieces = pieces + [over["c"](p) for p in pieces]
+        hops = [(0, 0), distance[g], distance[f], tuple(i + j for i, j in zip(distance[f], distance[g]))]
+        hops = hops + [(i + 1, j) for i, j in hops]
+        ids = jnp.stack([(me_exp ^ i) * n_seq + (me_seq ^ (j + 2 * k)) for i, j in hops])
+        here = jnp.take(facts, ids, axis=0).transpose(1, 0, 2).reshape(4, len(pieces) * rows_dev)
+        chunks.append((f, g, pieces, here))
+    for k, (f, g, pieces, here) in enumerate(chunks):
+        keep, send = chunk_experts(pieces, here, w_gate, w_up, w_down, first)
+        two = 2 * rows_dev
+        got = over["c"](send)
+        keep, send = add(keep[:two], got[:two]), add(keep[two:], got[two:])
+        got = over[f](send)
+        keep, send = add(keep[:rows_dev], got[:rows_dev]), add(keep[rows_dev:], got[rows_dev:])
+        done = add(keep, over[g](send))
+        if k > 0:
+            done = swap(done, "seq", n_seq, 2 * k)
+        mixture = done.astype(jnp.float32) if mixture is None else mixture + done.astype(jnp.float32)
+    return mixture
 
 
 def body(
@@ -164,10 +318,6 @@
     facts = jnp.concatenate([target.astype(jnp.float32), gate_weights[0]], axis=1).T
     facts = lax.all_gather(facts, everyone, axis=0, tiled=False)
     blocks = n_seq * n_exp
-    facts = facts.reshape(blocks // CHUNK_BLOCKS, CHUNK_BLOCKS, 4, rows_dev).transpose(0, 2, 1, 3)
-    facts = facts.reshape(blocks // CHUNK_BLOCKS, 4, CHUNK_BLOCKS * rows_dev)
-    tgt = facts[:, :2].astype(jnp.int32)
-    gates = facts[:, 2:]
 
     keys, values = key_value[0, :, 0], key_value[0, :, 1]
 
@@ -198,15 +348,29 @@
     order = jnp.sum(jnp.where(page_table[0][None, :] == slots[:, None], slots[None, :], 0), axis=1)
     pages = jnp.take(pages, order, axis=0)
     pages = pages.reshape(n_seq, rows_dev, 2 * span)
-    pages = lax.all_to_all(pages, "seq", split_axis=0, concat_axis=0, tiled=True)
+    if n_seq == 8:
+        others = lax.axis_index("seq") ^ jnp.arange(n_seq, dtype=jnp.int32)
+        pages = jnp.take(pages, others, axis=0)
+        pages = jnp.stack([pages[0]] + [swap(pages[j], "seq", n_seq, j) for j in range(1, n_seq)])
+        pages = jnp.take(pages, others, axis=0)
+    else:
+        pages = lax.all_to_all(pages, "seq", split_axis=0, concat_axis=0, tiled=True)
     cache = jnp.concatenate([unspan(pages[..., :span]), unspan(pages[..., span:])], axis=-1)
     cache = cache.reshape(1, rows_dev // PAGE, PAGE, 2 * width)
 
-    everything = lax.all_gather(normed, everyone, axis=0, tiled=True)
     first = (lax.axis_index("exp") * (EXPERTS // n_exp)).astype(jnp.int32).reshape(1)
-    partial = experts(everything, tgt, gates, w_gate, w_up, w_down, first)
-    mixture = lax.psum_scatter(partial, everyone, scatter_dimension=0, tiled=True)
-    layer_out = (stream + mixture.astype(jnp.float32)).astype(jnp.bfloat16)
+    w_gate, w_up = jnp.swapaxes(w_gate, 1, 2), jnp.swapaxes(w_up, 1, 2)
+    if (n_seq, n_exp) == (8, 4):
+        mixture = exchange_experts(normed, facts, w_gate, w_up, w_down, first, n_seq, n_exp)
+    else:
+        everything = lax.all_gather(normed, everyone, axis=0, tiled=True)
+        facts = facts.reshape(blocks // CHUNK_BLOCKS, CHUNK_BLOCKS, 4, rows_dev).transpose(0, 2, 1, 3)
+        facts = facts.reshape(blocks // CHUNK_BLOCKS, 4, CHUNK_BLOCKS * rows_dev)
+        partial = experts(
+            everything, facts[:, :2].astype(jnp.int32), facts[:, 2:], w_gate, w_up, w_down, first
+        )
+        mixture = lax.psum_scatter(partial, everyone, scatter_dimension=0, tiled=True).astype(jnp.float32)
+    layer_out = (stream + mixture).astype(jnp.bfloat16)
     return (layer_out[None], cache)
 
 

time: 344 us -> 324 us (0.942)
  waiting for transfers between devices: 147 us -> 72.8 us
  starting transfers between devices: 10.9 us -> 60.2 us
  Pallas kernels: 43.2 us -> 65.2 us
  between operations: 14.4 us -> 1.41 us
  blocking collectives: 85.3 us -> 78.8 us
  other arithmetic: 5.51 us -> 11.8 us
    reduce_scatter x1 -> x0, waiting for transfers between devices: 110 us -> none  [body(): lax.psum_scatter(partial, everyone, scatter_dimension=0, tiled=True)]
    ppermute x0 -> x53, waiting for transfers between devices: none -> 71.3 us  [swap(): return lax.ppermute(a, axis, [(i, i ^ distance) for i in range(size)])]
    ppermute x0 -> x53, starting transfers between devices: none -> 49.2 us  [swap(): return lax.ppermute(a, axis, [(i, i ^ distance) for i in range(size)])]
    all_to_all x1, waiting for transfers between devices: 25.6 us -> 0.01 us  [body(): lax.all_to_all(packed, 'seq', split_axis=0, concat_axis=0, tiled=True)]
    pallas_call x1 -> x4, Pallas kernels: 37.6 us -> 59.6 us  [chunk_experts(): pl.pallas_call(functools.partial(chunk_kernel, local, len(pieces), rows,...]
    all_to_all x1 -> x0, blocking collectives: 17.1 us -> none  [body(): lax.all_to_all(pages, 'seq', split_axis=0, concat_axis=0, tiled=True)]
    unnamed x36 -> x94, local copies, waits for them, and re-layouts: 28 us -> 11.2 us
    all_gather x1, blocking collectives: 68.2 us -> 78.8 us  [body(): facts = lax.all_gather(facts, everyone, axis=0, tiled=False)]
  transfers between devices with their start and end apart: 4 -> 55, of which waited for: 3 -> 20; matrix products, arithmetic and copies ran while one was open for 8% -> 11% of each run, Pallas kernels for 0% -> 18%
where the time goes in v2:
time: 324 us; the launch traced here: 323 us
  blocking collectives  78.8 us (24%)
  waiting for transfers between devices  72.8 us (22%)
  Pallas kernels  65.2 us (20%)
  starting transfers between devices  60.2 us (19%)
  local copies, waits for them, and re-layouts  33.2 us (10%)
  other arithmetic  11.8 us (4%)
    all_gather x1, blocking collectives, body(): facts = lax.all_gather(facts, everyone, axis=0, tiled=False)  78.8 us
    ppermute x53, waiting for transfers between devices, swap(): return lax.ppermute(a, axis, [(i, i ^ distance) for i in range(size)])  71.3 us
    pallas_call x4, Pallas kernels, chunk_experts(): pl.pallas_call(functools.partial(chunk_kernel, local, len(pieces), rows,...  59.6 us
    ppermute x53, starting transfers between devices, swap(): return lax.ppermute(a, axis, [(i, i ^ distance) for i in range(size)])  49.2 us
    unnamed x94, local copies, waits for them, and re-layouts  11.2 us
    all_to_all x1, starting transfers between devices, body(): lax.all_to_all(packed, 'seq', split_axis=0, concat_axis=0, tiled=True)  7.4 us
  transfers between devices with their start and end apart: 55, of which 20 were waited for; matrix products, arithmetic and copies ran while one was open for 11% of the time, Pallas kernels for 18%

profile of v2, /device:TPU:0, one launch (start us, length us, event | category | flops | bytes accessed | tf_op | source)
XLA Modules:
  0.0 323.4 jit_solution(8503031225080861627)
XLA Ops:
  0.6 2.3 fusion.4
  4.4 1.3 pad_maximum_fusion
  5.7 7.4 %all-to-all-start = ((bf16[8,64,960]{2,1,0:T(8,128)(2,1)}), bf16[8,64,960]{2,1,0:T(8,128)(2,1)S(1)}, u32[]{:S(2)}, u32[]{:S(2)}) async-start(bf16[8,64,960]{2,1,0:T(8,128)(2,1)} %pad_maximum_fusion), calls=%async_computation | async-start | bytes 2097152 | tf_op jit(solution)/shard_map/all_to_all | solution.py:328
  15.5 78.8 %all-gather.1 = f32[32,4,64]{2,1,0:T(4,128)S(1)} all-gather(f32[1,4,64]{2,1,0:T(4,128)S(1)} %maximum_bitcast_fusion), channel_id=2, replica_groups=mesh['seq'=8,'exp'=4] {'exp','seq'}, dimensions={0}, use_global_device_ids=true | all-gather | bytes 33792 | tf_op jit(solution)/shard_map/all_gather | solution.py:319
  98.7 5.6 %shard_map.122 = bf16[512,320]{1,0:T(8,128)(2,1)} custom-call(bf16[512,960]{1,0:T(8,128)(2,1)S(1)} %bitcast.274, s32[1,512]{1,0:T(1,128)S(1)} %copy-done.10, s32[512,1]{1,0:T(8,128)S(1)} %copy.52.seg_col_ref), custom_call_target="tpu_custom_call" | custom-call | flops 335544320 | bytes 1310720 | tf_op jit(solution)/shard_map/pallas_call | solution.py:55
  104.3 3.6 %all-to-all-start.1 = ((bf16[8,64,320]{2,1,0:T(8,128)(2,1)}), bf16[8,64,320]{2,1,0:T(8,128)(2,1)S(1)}, u32[]{:S(2)}, u32[]{:S(2)}) async-start(bf16[8,64,320]{2,1,0:T(8,128)(2,1)} %bitcast.30), calls=%async_computation.1 | async-start | bytes 786432 | tf_op jit(solution)/shard_map/all_to_all | solution.py:331
  110.4 1.7 collective-permute-start.46
  112.1 1.5 collective-permute-start.47
  113.8 2.7 collective-permute-start.49
  116.5 1.4 collective-permute-start.50
  117.9 1.5 all-to-all-done.1
  120.5 1.9 collective-permute-start.51
  122.3 2.0 collective-permute-start.34
  124.6 10.4 %collective-permute-done.49 = bf16[64,640]{1,0:T(8,128)(2,1)S(1)} collective-permute-done((bf16[64,640]{1,0:T(8,128)(2,1)S(1)}, bf16[64,640]{1,0:T(8,128)(2,1)S(1)}, u32[]{:S(2)}, u32[]{:S(2)}) %collective-permute-start.49) | collective-permute-done | bytes 81952 | tf_op jit(solution)/shard_map/ppermute | solution.py:249
  135.1 4.3 %collective-permute-done.50 = bf16[64,640]{1,0:T(8,128)(2,1)S(1)} collective-permute-done((bf16[64,640]{1,0:T(8,128)(2,1)S(1)}, bf16[64,640]{1,0:T(8,128)(2,1)S(1)}, u32[]{:S(2)}, u32[]{:S(2)}) %collective-permute-start.50) | collective-permute-done | bytes 81952 | tf_op jit(solution)/shard_map/ppermute | solution.py:249
  140.4 5.0 %collective-permute-start.52 = (bf16[64,640]{1,0:T(8,128)(2,1)S(1)}, bf16[64,640]{1,0:T(8,128)(2,1)S(1)}, u32[]{:S(2)}, u32[]{:S(2)}) collective-permute-start(bf16[64,640]{1,0:T(8,128)(2,1)S(1)} %get-tuple-element.44), channel_id=1, source_target_pairs={{0,28},{4,24},{8,20},{12,16},{16,12},{20,8},{24,4},{28,0},{1,29},{... | collective-permute-start | bytes 245768 | tf_op jit(solution)/shard_map/ppermute | solution.py:249
  146.5 1.4 collective-permute-done.52
  149.0 6.9 %collective-permute-done.22.rest_0_ = bf16[64,2304]{1,0:T(8,128)(2,1)S(1)} collective-permute-done((bf16[64,2304]{1,0:T(8,128)(2,1)S(1)}, bf16[64,2304]{1,0:T(8,128)(2,1)S(1)}, u32[]{:S(2)}, u32[]{:S(2)}) %collective-permute-start.22) | collective-permute-done | bytes 294944 | tf_op jit(solution)/shard_map/ppermute | solution.py:249
  155.8 1.5 collective-permute-start.35
  159.5 1.3 collective-permute-start.23
  161.3 1.8 collective-permute-done.35.rest_1_
  163.2 2.4 collective-permute-done.36.rest_2_
  166.6 1.6 bitcast_dynamic-update-slice_fusion.4
  168.2 1.5 bitcast_dynamic-update-slice_fusion.3
  169.8 2.1 collective-permute-done.23.rest_1_
  173.3 2.8 collective-permute-done.11.rest_1_
  176.7 1.4 collective-permute-done.2.rest_3_
  178.8 1.5 bitcast_dynamic-update-slice_fusion.1
  180.3 2.8 collective-permute-done.12.rest_2_
  186.5 15.1 %shard_map.123 = (bf16[256,2304]{1,0:T(8,128)(2,1)S(1)}, bf16[256,2304]{1,0:T(8,128)(2,1)}) custom-call(s32[1]{0:T(128)} %bitcast.39.first_ref, f32[4,512]{1,0:T(4,128)S(1)} %copy.56.row_ref, f32[512,4]{1,0:T(8,128)S(1)} %bitcast.282, bf16[2,720,2304]{2,1,0:T(8,128)(2,1)} %bitcast.284, bf16[2,720,2304]{2,1,0:T(8,128)(2,1)} %bitcast.288, ...), custom_call_target="tpu_custom_call" | custom-call | flops 3822059520 | bytes 24625152 | tf_op jit(solution)/shard_map/pallas_call | solution.py:220
  203.5 2.7 gather_fusion.6
  208.2 15.1 %shard_map.126 = (bf16[256,2304]{1,0:T(8,128)(2,1)S(1)}, bf16[256,2304]{1,0:T(8,128)(2,1)S(1)}) custom-call(s32[1]{0:T(128)} %bitcast.39.first_ref, f32[4,512]{1,0:T(4,128)S(1)} %copy.62.row_ref, f32[512,4]{1,0:T(8,128)S(1)} %bitcast.280, bf16[2,720,2304]{2,1,0:T(8,128)(2,1)} %bitcast.285, bf16[2,720,2304]{2,1,0:T(8,128)(2,1)} %bitcast.289, ...), custom_call_target="tpu_custom_call" | custom-call | flops 3822059520 | bytes 24625152 | tf_op jit(solution)/shard_map/pallas_call | solution.py:220
  224.5 14.9 %shard_map.125 = (bf16[256,2304]{1,0:T(8,128)(2,1)S(1)}, bf16[256,2304]{1,0:T(8,128)(2,1)S(1)}) custom-call(s32[1]{0:T(128)} %bitcast.39.first_ref, f32[4,512]{1,0:T(4,128)S(1)} %copy.60.row_ref, f32[512,4]{1,0:T(8,128)S(1)} %bitcast.278, bf16[2,720,2304]{2,1,0:T(8,128)(2,1)} %bitcast.286, bf16[2,720,2304]{2,1,0:T(8,128)(2,1)} %bitcast.290, ...), custom_call_target="tpu_custom_call" | custom-call | flops 3822059520 | bytes 24625152 | tf_op jit(solution)/shard_map/pallas_call | solution.py:220
  239.9 14.5 %shard_map.124 = (bf16[256,2304]{1,0:T(8,128)(2,1)S(1)}, bf16[256,2304]{1,0:T(8,128)(2,1)S(1)}) custom-call(s32[1]{0:T(128)} %bitcast.39.first_ref, f32[4,512]{1,0:T(4,128)S(1)} %copy.58.row_ref, f32[512,4]{1,0:T(8,128)S(1)} %bitcast.276, bf16[2,720,2304]{2,1,0:T(8,128)(2,1)} %bitcast.287, bf16[2,720,2304]{2,1,0:T(8,128)(2,1)} %bitcast.291, ...), custom_call_target="tpu_custom_call" | custom-call | flops 3822059520 | bytes 24625152 | tf_op jit(solution)/shard_map/pallas_call | solution.py:220
  254.6 1.5 add_convert_fusion.7
  256.1 1.5 collective-permute-start.8
  257.9 1.3 collective-permute-start.43
  261.3 11.0 %collective-permute-done.8 = bf16[128,2304]{1,0:T(8,128)(2,1)S(1)} collective-permute-done((bf16[128,2304]{1,0:T(8,128)(2,1)S(1)}, bf16[128,2304]{1,0:T(8,128)(2,1)S(1)}, u32[]{:S(2)}, u32[]{:S(2)}) %collective-permute-start.8) | collective-permute-done | bytes 589856 | tf_op jit(solution)/shard_map/ppermute | solution.py:249
  272.4 1.3 collective-permute-start.9
  275.3 9.6 %collective-permute-done.31 = bf16[128,2304]{1,0:T(8,128)(2,1)S(1)} collective-permute-done((bf16[128,2304]{1,0:T(8,128)(2,1)S(1)}, bf16[128,2304]{1,0:T(8,128)(2,1)S(1)}, u32[]{:S(2)}, u32[]{:S(2)}) %collective-permute-start.31) | collective-permute-done | bytes 589856 | tf_op jit(solution)/shard_map/ppermute | solution.py:249
  285.0 1.3 collective-permute-start.32
  288.0 3.3 %collective-permute-done.44 = bf16[64,2304]{1,0:T(8,128)(2,1)S(1)} collective-permute-done((bf16[64,2304]{1,0:T(8,128)(2,1)S(1)}, bf16[64,2304]{1,0:T(8,128)(2,1)S(1)}, u32[]{:S(2)}, u32[]{:S(2)}) %collective-permute-start.44) | collective-permute-done | bytes 294944 | tf_op jit(solution)/shard_map/ppermute | solution.py:249
  291.4 2.1 collective-permute-start.45
  293.5 5.1 %collective-permute-done.32 = bf16[64,2304]{1,0:T(8,128)(2,1)S(1)} collective-permute-done((bf16[64,2304]{1,0:T(8,128)(2,1)S(1)}, bf16[64,2304]{1,0:T(8,128)(2,1)S(1)}, u32[]{:S(2)}, u32[]{:S(2)}) %collective-permute-start.32) | collective-permute-done | bytes 294944 | tf_op jit(solution)/shard_map/ppermute | solution.py:249
  299.5 8.7 %collective-permute-start.33 = (bf16[64,2304]{1,0:T(8,128)(2,1)}, bf16[64,2304]{1,0:T(8,128)(2,1)S(1)}, u32[]{:S(2)}, u32[]{:S(2)}) collective-permute-start(bf16[64,2304]{1,0:T(8,128)(2,1)} %add_convert_fusion.12), channel_id=1, source_target_pairs={{0,16},{4,20},{8,24},{12,28},{16,0},{20,4},{24,8},{28,12},{1,17},{... | collective-permute-start | bytes 884744 | tf_op jit(solution)/shard_map/ppermute | solution.py:249
  315.5 2.0 concatenate.15
  317.6 3.7 %collective-permute-done.33 = bf16[64,2304]{1,0:T(8,128)(2,1)S(1)} collective-permute-done((bf16[64,2304]{1,0:T(8,128)(2,1)}, bf16[64,2304]{1,0:T(8,128)(2,1)S(1)}, u32[]{:S(2)}, u32[]{:S(2)}) %collective-permute-start.33) | collective-permute-done | bytes 294944 | tf_op jit(solution)/shard_map/ppermute | solution.py:249
  321.4 2.0 fusion
  (257 shorter events, 44.6 us)
Async XLA Ops:
  5.7 92.6 %all-to-all-start = ((bf16[8,64,960]{2,1,0:T(8,128)(2,1)}), bf16[8,64,960]{2,1,0:T(8,128)(2,1)S(1)}, u32[]{:S(2)}, u32[]{:S(2)}) async-start(bf16[8,64,960]{2,1,0:T(8,128)(2,1)} %pad_maximum_fusion), calls=%async_computation | async-start | bytes 2097152 | tf_op jit(solution)/shard_map/all_to_all | solution.py:328
  104.3 15.1 %all-to-all-start.1 = ((bf16[8,64,320]{2,1,0:T(8,128)(2,1)}), bf16[8,64,320]{2,1,0:T(8,128)(2,1)S(1)}, u32[]{:S(2)}, u32[]{:S(2)}) async-start(bf16[8,64,320]{2,1,0:T(8,128)(2,1)} %bitcast.30), calls=%async_computation.1 | async-start | bytes 786432 | tf_op jit(solution)/shard_map/all_to_all | solution.py:331
  110.4 10.1 %collective-permute-start.46 = (bf16[64,640]{1,0:T(8,128)(2,1)S(1)}, bf16[64,640]{1,0:T(8,128)(2,1)S(1)}, u32[]{:S(2)}, u32[]{:S(2)}) collective-permute-start(bf16[64,640]{1,0:T(8,128)(2,1)S(1)} %get-tuple-element.50), channel_id=1, source_target_pairs={{0,4},{4,0},{8,12},{12,8},{16,20},{20,16},{24,28},{28,24},{1,5},{5... | collective-permute-start | bytes 245768 | tf_op jit(solution)/shard_map/ppermute | solution.py:249
  112.1 10.2 %collective-permute-start.47 = (bf16[64,640]{1,0:T(8,128)(2,1)S(1)}, bf16[64,640]{1,0:T(8,128)(2,1)S(1)}, u32[]{:S(2)}, u32[]{:S(2)}) collective-permute-start(bf16[64,640]{1,0:T(8,128)(2,1)S(1)} %get-tuple-element.49), channel_id=1, source_target_pairs={{0,8},{4,12},{8,0},{12,4},{16,24},{20,28},{24,16},{28,20},{1,9},{5... | collective-permute-start | bytes 245768 | tf_op jit(solution)/shard_map/ppermute | solution.py:249
  113.6 10.8 %collective-permute-start.48 = (bf16[64,640]{1,0:T(8,128)(2,1)S(1)}, bf16[64,640]{1,0:T(8,128)(2,1)}, u32[]{:S(2)}, u32[]{:S(2)}) collective-permute-start(bf16[64,640]{1,0:T(8,128)(2,1)S(1)} %get-tuple-element.48), channel_id=1, source_target_pairs={{0,12},{4,8},{8,4},{12,0},{16,28},{20,24},{24,20},{28,16},{1,13},{... | collective-permute-start | bytes 245768 | tf_op jit(solution)/shard_map/ppermute | solution.py:249
  113.8 21.2 %collective-permute-start.49 = (bf16[64,640]{1,0:T(8,128)(2,1)S(1)}, bf16[64,640]{1,0:T(8,128)(2,1)S(1)}, u32[]{:S(2)}, u32[]{:S(2)}) collective-permute-start(bf16[64,640]{1,0:T(8,128)(2,1)S(1)} %get-tuple-element.47), channel_id=1, source_target_pairs={{0,16},{4,20},{8,24},{12,28},{16,0},{20,4},{24,8},{28,12},{1,17},{... | collective-permute-start | bytes 245768 | tf_op jit(solution)/shard_map/ppermute | solution.py:249
  116.5 22.8 %collective-permute-start.50 = (bf16[64,640]{1,0:T(8,128)(2,1)S(1)}, bf16[64,640]{1,0:T(8,128)(2,1)S(1)}, u32[]{:S(2)}, u32[]{:S(2)}) collective-permute-start(bf16[64,640]{1,0:T(8,128)(2,1)S(1)} %get-tuple-element.46), channel_id=1, source_target_pairs={{0,20},{4,16},{8,28},{12,24},{16,4},{20,0},{24,12},{28,8},{1,21},{... | collective-permute-start | bytes 245768 | tf_op jit(solution)/shard_map/ppermute | solution.py:249
  120.5 19.9 %collective-permute-start.51 = (bf16[64,640]{1,0:T(8,128)(2,1)S(1)}, bf16[64,640]{1,0:T(8,128)(2,1)S(1)}, u32[]{:S(2)}, u32[]{:S(2)}) collective-permute-start(bf16[64,640]{1,0:T(8,128)(2,1)S(1)} %get-tuple-element.45), channel_id=1, source_target_pairs={{0,24},{4,28},{8,16},{12,20},{16,8},{20,12},{24,0},{28,4},{1,25},{... | collective-permute-start | bytes 245768 | tf_op jit(solution)/shard_map/ppermute | solution.py:249
  122.3 26.6 %collective-permute-start.34 = (bf16[64,2304]{1,0:T(8,128)(2,1)S(1)}, bf16[64,2304]{1,0:T(8,128)(2,1)S(1)}, u32[]{:S(2)}, u32[]{:S(2)}) collective-permute-start(bf16[64,2304]{1,0:T(8,128)(2,1)S(1)} %multiply_convert_fusion.rest_0_), channel_id=1, source_target_pairs={{0,24},{4,28},{8,16},{12,20},{16,8},{20,12},{24,0},{28,4},{1,25},{... | collective-permute-start | bytes 884744 | tf_op jit(solution)/shard_map/ppermute | solution.py:249
  124.4 31.5 %collective-permute-start.22 = (bf16[64,2304]{1,0:T(8,128)(2,1)S(1)}, bf16[64,2304]{1,0:T(8,128)(2,1)S(1)}, u32[]{:S(2)}, u32[]{:S(2)}) collective-permute-start(bf16[64,2304]{1,0:T(8,128)(2,1)S(1)} %multiply_convert_fusion.rest_0_), channel_id=1, source_target_pairs={{0,16},{4,20},{8,24},{12,28},{16,0},{20,4},{24,8},{28,12},{1,17},{... | collective-permute-start | bytes 884744 | tf_op jit(solution)/shard_map/ppermute | solution.py:249
  135.0 22.3 %collective-permute-start.10 = (bf16[64,2304]{1,0:T(8,128)(2,1)S(1)}, bf16[64,2304]{1,0:T(8,128)(2,1)S(1)}, u32[]{:S(2)}, u32[]{:S(2)}) collective-permute-start(bf16[64,2304]{1,0:T(8,128)(2,1)S(1)} %multiply_convert_fusion.rest_0_), channel_id=1, source_target_pairs={{0,8},{4,12},{8,0},{12,4},{16,24},{20,28},{24,16},{28,20},{1,9},{5... | collective-permute-start | bytes 884744 | tf_op jit(solution)/shard_map/ppermute | solution.py:249
  139.3 18.7 %collective-permute-start = (bf16[64,2304]{1,0:T(8,128)(2,1)S(1)}, bf16[64,2304]{1,0:T(8,128)(2,1)S(1)}, u32[]{:S(2)}, u32[]{:S(2)}) collective-permute-start(bf16[64,2304]{1,0:T(8,128)(2,1)S(1)} %multiply_convert_fusion.rest_0_), channel_id=1, source_target_pairs={{0,2},{1,3},{2,0},{3,1},{4,6},{5,7},{6,4},{7,5},{8,10},{9,11},{10,... | collective-permute-start | bytes 884744 | tf_op jit(solution)/shard_map/ppermute | solution.py:249
  147.9 11.6 %collective-permute-start.1 = (bf16[64,2304]{1,0:T(8,128)(2,1)S(1)}, bf16[64,2304]{1,0:T(8,128)(2,1)S(1)}, u32[]{:S(2)}, u32[]{:S(2)}) collective-permute-start(bf16[64,2304]{1,0:T(8,128)(2,1)S(1)} %multiply_convert_fusion.rest_0_), channel_id=1, source_target_pairs={{0,4},{4,0},{8,12},{12,8},{16,20},{20,16},{24,28},{28,24},{1,5},{5... | collective-permute-start | bytes 884744 | tf_op jit(solution)/shard_map/ppermute | solution.py:249
  149.0 11.8 %collective-permute-start.3 = (bf16[64,2304]{1,0:T(8,128)(2,1)S(1)}, bf16[64,2304]{1,0:T(8,128)(2,1)S(1)}, u32[]{:S(2)}, u32[]{:S(2)}) collective-permute-start(bf16[64,2304]{1,0:T(8,128)(2,1)S(1)} %multiply_convert_fusion.rest_0_), channel_id=1, source_target_pairs={{0,1},{1,0},{2,3},{3,2},{4,5},{5,4},{6,7},{7,6},{8,9},{9,8},{10,11... | collective-permute-start | bytes 884744 | tf_op jit(solution)/shard_map/ppermute | solution.py:249
  159.5 12.4 %collective-permute-start.23 = (bf16[64,2304]{1,0:T(8,128)(2,1)S(1)}, bf16[64,2304]{1,0:T(8,128)(2,1)}, u32[]{:S(2)}, u32[]{:S(2)}) collective-permute-start(bf16[64,2304]{1,0:T(8,128)(2,1)S(1)} %collective-permute-done.22.rest_0_), channel_id=1, source_target_pairs={{0,2},{1,3},{2,0},{3,1},{4,6},{5,7},{6,4},{7,5},{8,10},{9,11},{10,... | collective-permute-start | bytes 884744 | tf_op jit(solution)/shard_map/ppermute | solution.py:249
  160.7 11.3 %collective-permute-start.24 = (bf16[64,2304]{1,0:T(8,128)(2,1)S(1)}, bf16[64,2304]{1,0:T(8,128)(2,1)}, u32[]{:S(2)}, u32[]{:S(2)}) collective-permute-start(bf16[64,2304]{1,0:T(8,128)(2,1)S(1)} %collective-permute-done.22.rest_0_), channel_id=1, source_target_pairs={{0,4},{4,0},{8,12},{12,8},{16,20},{20,16},{24,28},{28,24},{1,5},{5... | collective-permute-start | bytes 884744 | tf_op jit(solution)/shard_map/ppermute | solution.py:249
  163.2 8.9 %collective-permute-start.26 = (bf16[64,2304]{1,0:T(8,128)(2,1)S(1)}, bf16[64,2304]{1,0:T(8,128)(2,1)S(1)}, u32[]{:S(2)}, u32[]{:S(2)}) collective-permute-start(bf16[64,2304]{1,0:T(8,128)(2,1)S(1)} %collective-permute-done.22.rest_0_), channel_id=1, source_target_pairs={{0,1},{1,0},{2,3},{3,2},{4,5},{5,4},{6,7},{7,6},{8,9},{9,8},{10,11... | collective-permute-start | bytes 884744 | tf_op jit(solution)/shard_map/ppermute | solution.py:249
  165.6 10.6 %collective-permute-start.11 = (bf16[64,2304]{1,0:T(8,128)(2,1)S(1)}, bf16[64,2304]{1,0:T(8,128)(2,1)S(1)}, u32[]{:S(2)}, u32[]{:S(2)}) collective-permute-start(bf16[64,2304]{1,0:T(8,128)(2,1)S(1)} %collective-permute-done.10.rest_0_), channel_id=1, source_target_pairs={{0,4},{4,0},{8,12},{12,8},{16,20},{20,16},{24,28},{28,24},{1,5},{5... | collective-permute-start | bytes 884744 | tf_op jit(solution)/shard_map/ppermute | solution.py:249
  166.6 11.5 %collective-permute-start.2 = (bf16[64,2304]{1,0:T(8,128)(2,1)S(1)}, bf16[64,2304]{1,0:T(8,128)(2,1)S(1)}, u32[]{:S(2)}, u32[]{:S(2)}) collective-permute-start(bf16[64,2304]{1,0:T(8,128)(2,1)S(1)} %collective-permute-done.1.rest_2_), channel_id=1, source_target_pairs={{0,2},{1,3},{2,0},{3,1},{4,6},{5,7},{6,4},{7,5},{8,10},{9,11},{10,... | collective-permute-start | bytes 884744 | tf_op jit(solution)/shard_map/ppermute | solution.py:249
  171.9 11.2 %collective-permute-start.12 = (bf16[64,2304]{1,0:T(8,128)(2,1)S(1)}, bf16[64,2304]{1,0:T(8,128)(2,1)}, u32[]{:S(2)}, u32[]{:S(2)}) collective-permute-start(bf16[64,2304]{1,0:T(8,128)(2,1)S(1)} %collective-permute-done.10.rest_0_), channel_id=1, source_target_pairs={{0,2},{1,3},{2,0},{3,1},{4,6},{5,7},{6,4},{7,5},{8,10},{9,11},{10,... | collective-permute-start | bytes 884744 | tf_op jit(solution)/shard_map/ppermute | solution.py:249
  172.1 11.5 %collective-permute-start.5 = (bf16[64,2304]{1,0:T(8,128)(2,1)S(1)}, bf16[64,2304]{1,0:T(8,128)(2,1)S(1)}, u32[]{:S(2)}, u32[]{:S(2)}) collective-permute-start(bf16[64,2304]{1,0:T(8,128)(2,1)S(1)} %collective-permute-done.1.rest_2_), channel_id=1, source_target_pairs={{0,1},{1,0},{2,3},{3,2},{4,5},{5,4},{6,7},{7,6},{8,9},{9,8},{10,11... | collective-permute-start | bytes 884744 | tf_op jit(solution)/shard_map/ppermute | solution.py:249
  172.8 10.3 %collective-permute-start.4 = (bf16[64,2304]{1,0:T(8,128)(2,1)S(1)}, bf16[64,2304]{1,0:T(8,128)(2,1)S(1)}, u32[]{:S(2)}, u32[]{:S(2)}) collective-permute-start(bf16[64,2304]{1,0:T(8,128)(2,1)S(1)} %collective-permute-done.rest_1_), channel_id=1, source_target_pairs={{0,1},{1,0},{2,3},{3,2},{4,5},{5,4},{6,7},{7,6},{8,9},{9,8},{10,11... | collective-permute-start | bytes 884744 | tf_op jit(solution)/shard_map/ppermute | solution.py:249
  183.1 18.5 %collective-permute-start.14 = (bf16[64,2304]{1,0:T(8,128)(2,1)S(1)}, bf16[64,2304]{1,0:T(8,128)(2,1)S(1)}, u32[]{:S(2)}, u32[]{:S(2)}) collective-permute-start(bf16[64,2304]{1,0:T(8,128)(2,1)S(1)} %collective-permute-done.10.rest_0_), channel_id=1, source_target_pairs={{0,1},{1,0},{2,3},{3,2},{4,5},{5,4},{6,7},{7,6},{8,9},{9,8},{10,11... | collective-permute-start | bytes 884744 | tf_op jit(solution)/shard_map/ppermute | solution.py:249
  183.1 23.1 %collective-permute-start.40 = (bf16[64,2304]{1,0:T(8,128)(2,1)}, bf16[64,2304]{1,0:T(8,128)(2,1)}, u32[]{:S(2)}, u32[]{:S(2)}) collective-permute-start(bf16[64,2304]{1,0:T(8,128)(2,1)} %collective-permute-done.36.rest_2_), channel_id=1, source_target_pairs={{0,1},{1,0},{2,3},{3,2},{4,5},{5,4},{6,7},{7,6},{8,9},{9,8},{10,11... | collective-permute-start | bytes 884744 | tf_op jit(solution)/shard_map/ppermute | solution.py:249
  183.6 22.5 %collective-permute-start.39 = (bf16[64,2304]{1,0:T(8,128)(2,1)}, bf16[64,2304]{1,0:T(8,128)(2,1)}, u32[]{:S(2)}, u32[]{:S(2)}) collective-permute-start(bf16[64,2304]{1,0:T(8,128)(2,1)} %collective-permute-done.35.rest_1_), channel_id=1, source_target_pairs={{0,1},{1,0},{2,3},{3,2},{4,5},{5,4},{6,7},{7,6},{8,9},{9,8},{10,11... | collective-permute-start | bytes 884744 | tf_op jit(solution)/shard_map/ppermute | solution.py:249
  184.7 21.9 %collective-permute-start.25 = (bf16[64,2304]{1,0:T(8,128)(2,1)}, bf16[64,2304]{1,0:T(8,128)(2,1)}, u32[]{:S(2)}, u32[]{:S(2)}) collective-permute-start(bf16[64,2304]{1,0:T(8,128)(2,1)} %collective-permute-done.24.rest_2_), channel_id=1, source_target_pairs={{0,2},{1,3},{2,0},{3,1},{4,6},{5,7},{6,4},{7,5},{8,10},{9,11},{10,... | collective-permute-start | bytes 884744 | tf_op jit(solution)/shard_map/ppermute | solution.py:249
  185.5 21.8 %collective-permute-start.41 = (bf16[64,2304]{1,0:T(8,128)(2,1)}, bf16[64,2304]{1,0:T(8,128)(2,1)}, u32[]{:S(2)}, u32[]{:S(2)}) collective-permute-start(bf16[64,2304]{1,0:T(8,128)(2,1)} %collective-permute-done.37.rest_3_), channel_id=1, source_target_pairs={{0,1},{1,0},{2,3},{3,2},{4,5},{5,4},{6,7},{7,6},{8,9},{9,8},{10,11... | collective-permute-start | bytes 884744 | tf_op jit(solution)/shard_map/ppermute | solution.py:249
  202.3 52.3 %collective-permute-start.7 = (bf16[256,2304]{1,0:T(8,128)(2,1)}, bf16[256,2304]{1,0:T(8,128)(2,1)}, u32[]{:S(2)}, u32[]{:S(2)}) collective-permute-start(bf16[256,2304]{1,0:T(8,128)(2,1)} %get-tuple-element.13), channel_id=1, source_target_pairs={{0,1},{1,0},{2,3},{3,2},{4,5},{5,4},{6,7},{7,6},{8,9},{9,8},{10,11... | collective-permute-start | bytes 3538952 | tf_op jit(solution)/shard_map/ppermute | solution.py:249
  206.1 17.7 %collective-permute-start.28 = (bf16[64,2304]{1,0:T(8,128)(2,1)}, bf16[64,2304]{1,0:T(8,128)(2,1)S(1)}, u32[]{:S(2)}, u32[]{:S(2)}) collective-permute-start(bf16[64,2304]{1,0:T(8,128)(2,1)} %collective-permute-done.24.rest_2_), channel_id=1, source_target_pairs={{0,1},{1,0},{2,3},{3,2},{4,5},{5,4},{6,7},{7,6},{8,9},{9,8},{10,11... | collective-permute-start | bytes 884744 | tf_op jit(solution)/shard_map/ppermute | solution.py:249
  206.2 17.1 %collective-permute-start.27 = (bf16[64,2304]{1,0:T(8,128)(2,1)}, bf16[64,2304]{1,0:T(8,128)(2,1)S(1)}, u32[]{:S(2)}, u32[]{:S(2)}) collective-permute-start(bf16[64,2304]{1,0:T(8,128)(2,1)} %collective-permute-done.23.rest_1_), channel_id=1, source_target_pairs={{0,1},{1,0},{2,3},{3,2},{4,5},{5,4},{6,7},{7,6},{8,9},{9,8},{10,11... | collective-permute-start | bytes 884744 | tf_op jit(solution)/shard_map/ppermute | solution.py:249
  206.7 17.3 %collective-permute-start.13 = (bf16[64,2304]{1,0:T(8,128)(2,1)}, bf16[64,2304]{1,0:T(8,128)(2,1)S(1)}, u32[]{:S(2)}, u32[]{:S(2)}) collective-permute-start(bf16[64,2304]{1,0:T(8,128)(2,1)} %collective-permute-done.12.rest_2_), channel_id=1, source_target_pairs={{0,4},{4,0},{8,12},{12,8},{16,20},{20,16},{24,28},{28,24},{1,5},{5... | collective-permute-start | bytes 884744 | tf_op jit(solution)/shard_map/ppermute | solution.py:249
  207.2 17.1 %collective-permute-start.29 = (bf16[64,2304]{1,0:T(8,128)(2,1)}, bf16[64,2304]{1,0:T(8,128)(2,1)S(1)}, u32[]{:S(2)}, u32[]{:S(2)}) collective-permute-start(bf16[64,2304]{1,0:T(8,128)(2,1)} %collective-permute-done.25.rest_3_), channel_id=1, source_target_pairs={{0,1},{1,0},{2,3},{3,2},{4,5},{5,4},{6,7},{7,6},{8,9},{9,8},{10,11... | collective-permute-start | bytes 884744 | tf_op jit(solution)/shard_map/ppermute | solution.py:249
  223.3 16.6 %collective-permute-start.16 = (bf16[64,2304]{1,0:T(8,128)(2,1)}, bf16[64,2304]{1,0:T(8,128)(2,1)S(1)}, u32[]{:S(2)}, u32[]{:S(2)}) collective-permute-start(bf16[64,2304]{1,0:T(8,128)(2,1)} %collective-permute-done.12.rest_2_), channel_id=1, source_target_pairs={{0,1},{1,0},{2,3},{3,2},{4,5},{5,4},{6,7},{7,6},{8,9},{9,8},{10,11... | collective-permute-start | bytes 884744 | tf_op jit(solution)/shard_map/ppermute | solution.py:249
  223.8 15.6 %collective-permute-start.15 = (bf16[64,2304]{1,0:T(8,128)(2,1)S(1)}, bf16[64,2304]{1,0:T(8,128)(2,1)S(1)}, u32[]{:S(2)}, u32[]{:S(2)}) collective-permute-start(bf16[64,2304]{1,0:T(8,128)(2,1)S(1)} %copy-done.1), channel_id=1, source_target_pairs={{0,1},{1,0},{2,3},{3,2},{4,5},{5,4},{6,7},{7,6},{8,9},{9,8},{10,11... | collective-permute-start | bytes 884744 | tf_op jit(solution)/shard_map/ppermute | solution.py:249
  223.9 16.0 %collective-permute-start.17 = (bf16[64,2304]{1,0:T(8,128)(2,1)S(1)}, bf16[64,2304]{1,0:T(8,128)(2,1)S(1)}, u32[]{:S(2)}, u32[]{:S(2)}) collective-permute-start(bf16[64,2304]{1,0:T(8,128)(2,1)S(1)} %collective-permute-done.13.rest_3_), channel_id=1, source_target_pairs={{0,1},{1,0},{2,3},{3,2},{4,5},{5,4},{6,7},{7,6},{8,9},{9,8},{10,11... | collective-permute-start | bytes 884744 | tf_op jit(solution)/shard_map/ppermute | solution.py:249
  224.4 33.3 %collective-permute-start.42 = (bf16[256,2304]{1,0:T(8,128)(2,1)S(1)}, bf16[256,2304]{1,0:T(8,128)(2,1)S(1)}, u32[]{:S(2)}, u32[]{:S(2)}) collective-permute-start(bf16[256,2304]{1,0:T(8,128)(2,1)S(1)} %get-tuple-element.19), channel_id=1, source_target_pairs={{0,1},{1,0},{2,3},{3,2},{4,5},{5,4},{6,7},{7,6},{8,9},{9,8},{10,11... | collective-permute-start | bytes 3538952 | tf_op jit(solution)/shard_map/ppermute | solution.py:249
  239.4 19.8 %collective-permute-start.30 = (bf16[256,2304]{1,0:T(8,128)(2,1)S(1)}, bf16[256,2304]{1,0:T(8,128)(2,1)S(1)}, u32[]{:S(2)}, u32[]{:S(2)}) collective-permute-start(bf16[256,2304]{1,0:T(8,128)(2,1)S(1)} %get-tuple-element.17), channel_id=1, source_target_pairs={{0,1},{1,0},{2,3},{3,2},{4,5},{5,4},{6,7},{7,6},{8,9},{9,8},{10,11... | collective-permute-start | bytes 3538952 | tf_op jit(solution)/shard_map/ppermute | solution.py:249
  256.1 16.2 %collective-permute-start.8 = (bf16[128,2304]{1,0:T(8,128)(2,1)S(1)}, bf16[128,2304]{1,0:T(8,128)(2,1)S(1)}, u32[]{:S(2)}, u32[]{:S(2)}) collective-permute-start(bf16[128,2304]{1,0:T(8,128)(2,1)S(1)} %get-tuple-element.21), channel_id=1, source_target_pairs={{0,4},{4,0},{8,12},{12,8},{16,20},{20,16},{24,28},{28,24},{1,5},{5... | collective-permute-start | bytes 1769480 | tf_op jit(solution)/shard_map/ppermute | solution.py:249
  257.9 16.2 %collective-permute-start.43 = (bf16[128,2304]{1,0:T(8,128)(2,1)S(1)}, bf16[128,2304]{1,0:T(8,128)(2,1)S(1)}, u32[]{:S(2)}, u32[]{:S(2)}) collective-permute-start(bf16[128,2304]{1,0:T(8,128)(2,1)S(1)} %get-tuple-element.27), channel_id=1, source_target_pairs={{0,2},{1,3},{2,0},{3,1},{4,6},{5,7},{6,4},{7,5},{8,10},{9,11},{10,... | collective-permute-start | bytes 1769480 | tf_op jit(solution)/shard_map/ppermute | solution.py:249
  259.5 25.4 %collective-permute-start.31 = (bf16[128,2304]{1,0:T(8,128)(2,1)S(1)}, bf16[128,2304]{1,0:T(8,128)(2,1)S(1)}, u32[]{:S(2)}, u32[]{:S(2)}) collective-permute-start(bf16[128,2304]{1,0:T(8,128)(2,1)S(1)} %get-tuple-element.25), channel_id=1, source_target_pairs={{0,4},{4,0},{8,12},{12,8},{16,20},{20,16},{24,28},{28,24},{1,5},{5... | collective-permute-start | bytes 1769480 | tf_op jit(solution)/shard_map/ppermute | solution.py:249
  260.4 26.3 %collective-permute-start.19 = (bf16[128,2304]{1,0:T(8,128)(2,1)S(1)}, bf16[128,2304]{1,0:T(8,128)(2,1)S(1)}, u32[]{:S(2)}, u32[]{:S(2)}) collective-permute-start(bf16[128,2304]{1,0:T(8,128)(2,1)S(1)} %get-tuple-element.23), channel_id=1, source_target_pairs={{0,2},{1,3},{2,0},{3,1},{4,6},{5,7},{6,4},{7,5},{8,10},{9,11},{10,... | collective-permute-start | bytes 1769480 | tf_op jit(solution)/shard_map/ppermute | solution.py:249
  272.4 45.2 %collective-permute-start.9 = (bf16[64,2304]{1,0:T(8,128)(2,1)S(1)}, bf16[64,2304]{1,0:T(8,128)(2,1)S(1)}, u32[]{:S(2)}, u32[]{:S(2)}) collective-permute-start(bf16[64,2304]{1,0:T(8,128)(2,1)S(1)} %add_convert_fusion.19), channel_id=1, source_target_pairs={{0,2},{1,3},{2,0},{3,1},{4,6},{5,7},{6,4},{7,5},{8,10},{9,11},{10,... | collective-permute-start | bytes 884744 | tf_op jit(solution)/shard_map/ppermute | solution.py:249
  274.2 17.0 %collective-permute-start.44 = (bf16[64,2304]{1,0:T(8,128)(2,1)S(1)}, bf16[64,2304]{1,0:T(8,128)(2,1)S(1)}, u32[]{:S(2)}, u32[]{:S(2)}) collective-permute-start(bf16[64,2304]{1,0:T(8,128)(2,1)S(1)} %add_convert_fusion.10), channel_id=1, source_target_pairs={{0,4},{4,0},{8,12},{12,8},{16,20},{20,16},{24,28},{28,24},{1,5},{5... | collective-permute-start | bytes 884744 | tf_op jit(solution)/shard_map/ppermute | solution.py:249
  285.0 13.6 %collective-permute-start.32 = (bf16[64,2304]{1,0:T(8,128)(2,1)S(1)}, bf16[64,2304]{1,0:T(8,128)(2,1)S(1)}, u32[]{:S(2)}, u32[]{:S(2)}) collective-permute-start(bf16[64,2304]{1,0:T(8,128)(2,1)S(1)} %add_convert_fusion.13), channel_id=1, source_target_pairs={{0,2},{1,3},{2,0},{3,1},{4,6},{5,7},{6,4},{7,5},{8,10},{9,11},{10,... | collective-permute-start | bytes 884744 | tf_op jit(solution)/shard_map/ppermute | solution.py:249
  286.9 21.3 %collective-permute-start.20 = (bf16[64,2304]{1,0:T(8,128)(2,1)S(1)}, bf16[64,2304]{1,0:T(8,128)(2,1)S(1)}, u32[]{:S(2)}, u32[]{:S(2)}) collective-permute-start(bf16[64,2304]{1,0:T(8,128)(2,1)S(1)} %add_convert_fusion.16), channel_id=1, source_target_pairs={{0,4},{4,0},{8,12},{12,8},{16,20},{20,16},{24,28},{28,24},{1,5},{5... | collective-permute-start | bytes 884744 | tf_op jit(solution)/shard_map/ppermute | solution.py:249
  291.4 26.2 %collective-permute-start.45 = (bf16[64,2304]{1,0:T(8,128)(2,1)S(1)}, bf16[64,2304]{1,0:T(8,128)(2,1)S(1)}, u32[]{:S(2)}, u32[]{:S(2)}) collective-permute-start(bf16[64,2304]{1,0:T(8,128)(2,1)S(1)} %add_convert_fusion.9), channel_id=1, source_target_pairs={{0,24},{4,28},{8,16},{12,20},{16,8},{20,12},{24,0},{28,4},{1,25},{... | collective-permute-start | bytes 884744 | tf_op jit(solution)/shard_map/ppermute | solution.py:249
  299.5 21.8 %collective-permute-start.33 = (bf16[64,2304]{1,0:T(8,128)(2,1)}, bf16[64,2304]{1,0:T(8,128)(2,1)S(1)}, u32[]{:S(2)}, u32[]{:S(2)}) collective-permute-start(bf16[64,2304]{1,0:T(8,128)(2,1)} %add_convert_fusion.12), channel_id=1, source_target_pairs={{0,16},{4,20},{8,24},{12,28},{16,0},{20,4},{24,8},{28,12},{1,17},{... | collective-permute-start | bytes 884744 | tf_op jit(solution)/shard_map/ppermute | solution.py:249
  309.0 12.4 %collective-permute-start.21 = (bf16[64,2304]{1,0:T(8,128)(2,1)}, bf16[64,2304]{1,0:T(8,128)(2,1)}, u32[]{:S(2)}, u32[]{:S(2)}) collective-permute-start(bf16[64,2304]{1,0:T(8,128)(2,1)} %add_convert_fusion.15), channel_id=1, source_target_pairs={{0,8},{4,12},{8,0},{12,4},{16,24},{20,28},{24,16},{28,20},{1,9},{5... | collective-permute-start | bytes 884744 | tf_op jit(solution)/shard_map/ppermute | solution.py:249
  (40 other events, 558.7 us)

commit v3 on v1

--- a/solution.py
+++ b/solution.py
@@ -62,6 +62,10 @@
     )(packed, segments[None, :], segments[:, None])
 
 
+def dot_t(a, b):
+    return lax.dot_general(a, b, (((1,), (1,)), ((), ())), preferred_element_type=jnp.float32)
+
+
 def expert_kernel(
     local, rows, tokens, first_ref, x_ref, tgt_ref, gates_ref, wg_ref, wu_ref, wd_ref, out_ref, kept_ref
 ):
@@ -84,8 +88,8 @@
 
     pick, weight = selection(le)
     chosen = jnp.dot(pick, x_ref[...], preferred_element_type=jnp.float32).astype(jnp.bfloat16)
-    gate = jnp.dot(chosen, wg_ref[0], preferred_element_type=jnp.float32)
-    upper = jnp.dot(chosen, wu_ref[0], preferred_element_type=jnp.float32)
+    gate = dot_t(chosen, wg_ref[0])
+    upper = dot_t(chosen, wu_ref[0])
     hidden = (gate / (1.0 + jnp.exp(-gate)) * upper).astype(jnp.bfloat16)
     y = jnp.dot(hidden, wd_ref[0], preferred_element_type=jnp.float32)
     y = (y * weight).astype(jnp.bfloat16)
@@ -108,7 +112,7 @@
 
 
 def experts(x, tgt, gates, w_gate, w_up, w_down, first):
-    local, width, hidden = w_gate.shape
+    local, hidden, width = w_gate.shape
     chunks, _, tokens = tgt.shape
     rows = tokens // 64 * CAP
     last = local - 1
@@ -121,8 +125,8 @@
             pl.BlockSpec((tokens, width), lambda e, c: (c, 0)),
             pl.BlockSpec((1, 2, tokens), lambda e, c: (c, 0, 0)),
             pl.BlockSpec((1, 2, tokens), lambda e, c: (c, 0, 0)),
-            pl.BlockSpec((1, width, hidden), lambda e, c: (e, 0, 0)),
-            pl.BlockSpec((1, width, hidden), lambda e, c: (e, 0, 0)),
+            pl.BlockSpec((1, hidden, width), lambda e, c: (e, 0, 0)),
+            pl.BlockSpec((1, hidden, width), lambda e, c: (e, 0, 0)),
             pl.BlockSpec((1, hidden, width), lambda e, c: (e, 0, 0)),
         ],
         out_specs=pl.BlockSpec((tokens, width), lambda e, c: (jnp.where(e == last, c, 0), 0)),
@@ -134,6 +138,252 @@
             transcendentals=local * chunks * rows * hidden,
         ),
     )(first, x, tgt, gates, w_gate, w_up, w_down)
+
+
+def norm_kernel(share, offsets, context_ref, residual_ref, gain_ref, facts_ref, stream_ref, piece_ref):
+    n_seq, _, _ = context_ref.shape
+    width = residual_ref.shape[1]
+    parts = [context_ref[j][:, offsets[j] : offsets[j] + share] for j in range(n_seq)]
+    context = jnp.concatenate(parts, axis=1).astype(jnp.float32)
+    stream = residual_ref[...].astype(jnp.float32) + context
+    stream_ref[...] = stream
+    mean = jnp.mean(stream * stream, axis=1, keepdims=True)
+    normed = stream * lax.rsqrt(mean + 1e-05) * gain_ref[...].astype(jnp.float32)
+    piece_ref[:, :width] = normed.astype(jnp.bfloat16)
+    facts = facts_ref[...]
+    lane = lax.broadcasted_iota(jnp.int32, facts.shape, 1)
+    high = facts.astype(jnp.bfloat16).astype(jnp.float32)
+    middle = (facts - high).astype(jnp.bfloat16).astype(jnp.float32)
+    low = facts - high - middle
+    own = jnp.where(lane < 4, high, jnp.where(lane < 6, middle, low))
+    piece_ref[:, width:] = own.astype(jnp.bfloat16)
+
+
+def norm_tokens(context, residual, gain, facts, share, offsets):
+    rows_dev, width = residual.shape
+    return pl.pallas_call(
+        functools.partial(norm_kernel, share, offsets),
+        out_shape=(
+            jax.ShapeDtypeStruct((rows_dev, width), jnp.float32),
+            jax.ShapeDtypeStruct((rows_dev, width + facts.shape[1]), jnp.bfloat16),
+        ),
+        cost_estimate=pl.CostEstimate(
+            flops=10 * rows_dev * width, bytes_accessed=10 * rows_dev * width, transcendentals=rows_dev
+        ),
+    )(context, residual, gain[None, :], facts)
+
+
+def pick_pages_kernel(per_device, first_lane, order_ref, me_ref, packed_ref, late_ref, *out_refs):
+    del late_ref
+    for j, out_ref in enumerate(out_refs):
+        peer = jnp.bitwise_xor(me_ref[0], j)
+        for i in range(per_device):
+            page = order_ref[peer * per_device + i]
+            rows = pl.ds(pl.multiple_of(page * PAGE, PAGE), PAGE)
+            out_ref[i * PAGE : (i + 1) * PAGE, :] = packed_ref[rows, first_lane:]
+
+
+def pick_pages(packed, order, me, late, n_seq, span):
+    rows = packed.shape[0] // n_seq
+    smem = pl.BlockSpec(memory_space=pltpu.SMEM)
+    vmem = pl.BlockSpec(memory_space=pltpu.VMEM)
+    out = jax.ShapeDtypeStruct((rows, 2 * span), jnp.bfloat16)
+    return pl.pallas_call(
+        functools.partial(pick_pages_kernel, rows // PAGE, span),
+        out_shape=(out,) * n_seq,
+        in_specs=[smem, smem, vmem, pl.BlockSpec(memory_space=pl.ANY)],
+        cost_estimate=pl.CostEstimate(flops=0, bytes_accessed=10 * packed.shape[0] * span, transcendentals=0),
+    )(order, me, packed, late)
+
+
+def join_pages_kernel(share, offsets, span, me_ref, *refs):
+    piece_refs, out_ref, all_ref = refs[:-2], refs[-2], refs[-1]
+    for j, ref in enumerate(piece_refs):
+        all_ref[jnp.bitwise_xor(me_ref[0], j)] = ref[...]
+    for part in range(2):
+        parts = [
+            all_ref[j][:, part * span + offsets[j] : part * span + offsets[j] + share]
+            for j in range(len(piece_refs))
+        ]
+        width = share * len(piece_refs)
+        out_ref[:, part * width : (part + 1) * width] = jnp.concatenate(parts, axis=1)
+
+
+def join_pages(pieces, me, share, offsets, span):
+    rows = pieces[0].shape[0]
+    n_seq = len(pieces)
+    return pl.pallas_call(
+        functools.partial(join_pages_kernel, share, offsets, span),
+        out_shape=jax.ShapeDtypeStruct((rows, 2 * share * n_seq), jnp.bfloat16),
+        in_specs=[pl.BlockSpec(memory_space=pltpu.SMEM)] + [pl.BlockSpec(memory_space=pltpu.VMEM)] * n_seq,
+        scratch_shapes=[pltpu.VMEM((n_seq,) + pieces[0].shape, jnp.bfloat16)],
+        cost_estimate=pl.CostEstimate(flops=0, bytes_accessed=8 * rows * n_seq * span, transcendentals=0),
+    )(me, *pieces)
+
+
+def places_of(slots, base, shift):
+    place = -1
+    for slot in slots:
+        slot = slot.astype(jnp.int32) - base
+        place = jnp.where((slot >= 0) & (slot < CAP), shift + slot, place)
+    return place
+
+
+def chunk_kernel(local, pieces, rows, tokens, parts, waits, first_ref, wg_ref, wu_ref, wd_ref, *rest):
+    piece_refs = rest[:pieces]
+    keep_ref, send_ref, chosen_ref, weight_ref, sum_ref, y_ref = rest[pieces + waits :]
+    le = pl.program_id(0)
+    part = pl.program_id(1)
+    rows_dev = tokens // pieces
+    width = wd_ref.shape[2]
+
+    @pl.when(part == 0)
+    def _():
+        base = (first_ref[0] + le) * CAP
+        facts = jnp.concatenate([p[:, width:] for p in piece_refs], axis=0)
+        unit = lax.broadcasted_iota(jnp.int32, (8, 128), 0) == lax.broadcasted_iota(jnp.int32, (8, 128), 1)
+        facts = dot_t(unit.astype(jnp.float32).astype(jnp.bfloat16), facts)
+        shift = lax.broadcasted_iota(jnp.int32, (1, tokens), 1) // rows_dev * CAP
+        row_id = lax.broadcasted_iota(jnp.int32, (rows, tokens), 0)
+        pick, weights = None, None
+        for j in range(2):
+            hit = row_id == places_of([facts[j : j + 1]], base, shift)
+            gate = facts[2 + j : 3 + j] + facts[4 + j : 5 + j] + facts[6 + j : 7 + j]
+            weight = jnp.where(hit, gate, 0.0)
+            pick = hit if pick is None else pick | hit
+            weights = weight if weights is None else weights + weight
+        weight_ref[...] = jnp.sum(weights, axis=1, keepdims=True)
+        pick = pick.astype(jnp.float32).astype(jnp.bfloat16)
+        x = jnp.concatenate([p[:, :width] for p in piece_refs], axis=0)
+        chosen = jnp.dot(pick, x, preferred_element_type=jnp.float32)
+        chosen_ref[...] = chosen.T.astype(jnp.bfloat16)
+
+    chosen = chosen_ref[...]
+    gate = jnp.dot(wg_ref[0], chosen, preferred_element_type=jnp.float32)
+    upper = jnp.dot(wu_ref[0], chosen, preferred_element_type=jnp.float32)
+    hidden = (gate / (1.0 + jnp.exp(-gate)) * upper).T.astype(jnp.bfloat16)
+    y = jnp.dot(hidden, wd_ref[0], preferred_element_type=jnp.float32)
+
+    @pl.when(part == 0)
+    def _():
+        sum_ref[...] = y
+
+    @pl.when((part > 0) & (part < parts - 1))
+    def _():
+        sum_ref[...] += y
+
+    @pl.when(part == parts - 1)
+    def _():
+        here = pl.ds(pl.multiple_of(le * rows, rows), rows)
+        y_ref[here, :] = ((sum_ref[...] + y) * weight_ref[...]).astype(jnp.bfloat16)
+
+    @pl.when((part == parts - 1) & (le == local - 1))
+    def _():
+        facts = jnp.concatenate([p[:, width:] for p in piece_refs], axis=0).astype(jnp.float32)
+        shift = lax.broadcasted_iota(jnp.int32, (tokens, 1), 0) // rows_dev * CAP
+        lane = lax.broadcasted_iota(jnp.int32, (tokens, local * rows), 1)
+        put = None
+        for e in range(local):
+            base = (first_ref[0] + e) * CAP
+            hit = lane == places_of([facts[:, j : j + 1] for j in range(2)], base, shift + e * rows)
+            put = hit if put is None else put | hit
+        put = put.astype(jnp.float32).astype(jnp.bfloat16)
+        half = tokens // 2
+        keep_ref[...] = jnp.dot(put[:half], y_ref[...], preferred_element_type=jnp.float32).astype(jnp.bfloat16)
+        send_ref[...] = jnp.dot(put[half:], y_ref[...], preferred_element_type=jnp.float32).astype(jnp.bfloat16)
+
+
+def chunk_experts(pieces, w_gate, w_up, w_down, first, waits):
+    local, hidden, width = w_gate.shape
+    rows_dev = pieces[0].shape[0]
+    tokens = rows_dev * len(pieces)
+    rows = len(pieces) * CAP
+    parts = 3
+    step = hidden // parts
+    whole = lambda e, f: (0, 0)
+    weights = pl.BlockSpec((1, step, width), lambda e, f: (e, f, 0))
+    piece = pl.BlockSpec(pieces[0].shape, whole)
+    half = jax.ShapeDtypeStruct((tokens // 2, width), jnp.bfloat16)
+    return pl.pallas_call(
+        functools.partial(chunk_kernel, local, len(pieces), rows, tokens, parts, len(waits)),
+        out_shape=(half, half),
+        grid=(local, parts),
+        in_specs=[pl.BlockSpec(memory_space=pltpu.SMEM), weights, weights, weights]
+        + [piece] * len(pieces)
+        + [pl.BlockSpec(memory_space=pl.ANY)] * len(waits),
+        out_specs=(pl.BlockSpec(half.shape, whole), pl.BlockSpec(half.shape, whole)),
+        scratch_shapes=[
+            pltpu.VMEM((width, rows), jnp.bfloat16),
+            pltpu.VMEM((rows, 1), jnp.float32),
+            pltpu.VMEM((rows, width), jnp.float32),
+            pltpu.VMEM((local * rows, width), jnp.bfloat16),
+        ],
+        compiler_params=pltpu.CompilerParams(vmem_limit_bytes=32 * 1024 * 1024),
+        cost_estimate=pl.CostEstimate(
+            flops=6 * local * rows * width * hidden,
+            bytes_accessed=6 * local * width * hidden + 4 * tokens * width,
+            transcendentals=local * rows * hidden,
+        ),
+    )(first, w_gate, w_up, w_down, *pieces, *waits)
+
+
+def swap(a, axis, size, distance):
+    return lax.ppermute(a, axis, [(i, i ^ distance) for i in range(size)])
+
+
+def add(a, b):
+    return (a.astype(jnp.float32) + b.astype(jnp.float32)).astype(jnp.bfloat16)
+
+
+def exchange_experts(piece, w_gate, w_up, w_down, first, n_seq, n_exp, late_work):
+    one = piece.shape[0]
+    two = 2 * one
+    over = {
+        "x": lambda a: swap(a, "seq", n_seq, 1),
+        "y": lambda a: swap(a, "exp", n_exp, 2),
+        "c": lambda a: swap(a, "exp", n_exp, 1),
+    }
+    depth = n_seq // 2
+    axes = [("x", "y") if k % 2 == 0 else ("y", "x") for k in range(depth)]
+    starts = [piece] + [swap(piece, "seq", n_seq, 2 * k) for k in range(1, depth)]
+    gathered = []
+    for k, (f, g) in enumerate(axes):
+        by_f, by_g = over[f](starts[k]), over[g](starts[k])
+        near = [starts[k], by_g, by_f, over[g](by_f)]
+        gathered.append(near + [over["c"](p) for p in near])
+
+    kept, sent, lag = [None] * depth, [None] * depth, [None] * depth
+
+    def after_core(k):
+        got = over["c"](sent[k])
+        kept[k], sent[k] = add(kept[k][:two], got[:two]), add(kept[k][two:], got[two:])
+
+    def after_first(k):
+        got = over[axes[k][0]](sent[k])
+        kept[k], sent[k] = add(kept[k][:one], got[:one]), add(kept[k][one:], got[one:])
+
+    def after_second(k):
+        done = add(kept[k], over[axes[k][1]](sent[k]))
+        kept[k] = swap(done, "seq", n_seq, 2 * k) if k else done
+
+    steps = [after_core, after_first, after_second]
+    other = None
+    for turn in range(depth + len(steps)):
+        for late, stage in enumerate(steps):
+            k = turn - 2 - late
+            if 0 <= k < depth:
+                stage(k)
+        if turn < depth:
+            waits = [sent[k] for k in range(max(turn - 3, 0), turn - 1)]
+            kept[turn], sent[turn] = chunk_experts(gathered[turn], w_gate, w_up, w_down, first, waits)
+        if turn == 1:
+            other = late_work(sent[0])
+    for late, stage in enumerate(steps):
+        for k in range(depth):
+            if depth + len(steps) - 1 - 2 - late < k:
+                stage(k)
+    mixture = sum(k.astype(jnp.float32) for k in kept)
+    return mixture, other
 
 
 def body(
@@ -160,14 +410,7 @@
     flat = routes[0].reshape(rows_dev * 2)
     onehot = (flat[:, None] == jnp.arange(EXPERTS, dtype=jnp.int32)[None, :]).astype(jnp.int32)
     before = jnp.cumsum(onehot, axis=0) - onehot
-    target = (flat * CAP + jnp.sum(before * onehot, axis=1)).reshape(rows_dev, 2)
-    facts = jnp.concatenate([target.astype(jnp.float32), gate_weights[0]], axis=1).T
-    facts = lax.all_gather(facts, everyone, axis=0, tiled=False)
-    blocks = n_seq * n_exp
-    facts = facts.reshape(blocks // CHUNK_BLOCKS, CHUNK_BLOCKS, 4, rows_dev).transpose(0, 2, 1, 3)
-    facts = facts.reshape(blocks // CHUNK_BLOCKS, 4, CHUNK_BLOCKS * rows_dev)
-    tgt = facts[:, :2].astype(jnp.int32)
-    gates = facts[:, 2:]
+    target = (flat * CAP + jnp.sum(before * onehot, axis=1)).reshape(rows_dev, 2).astype(jnp.float32)
 
     keys, values = key_value[0, :, 0], key_value[0, :, 1]
 
@@ -183,31 +426,45 @@
     )
     offsets = [j * share - firsts[j] * HEAD_DIM for j in range(n_seq)]
 
-    def unspan(a):
-        return jnp.concatenate([a[j][..., offsets[j] : offsets[j] + share] for j in range(n_seq)], axis=-1)
-
-    stream = residual[0].astype(jnp.float32) + unspan(context).astype(jnp.float32)
-    normed = (
-        stream
-        * lax.rsqrt(jnp.mean(stream * stream, axis=-1, keepdims=True) + 1e-05)
-        * norm_gain.astype(jnp.float32)
-    ).astype(jnp.bfloat16)
-
-    pages = packed[:, span:].reshape(group // PAGE, PAGE, 2 * span)
+    first = (lax.axis_index("exp") * (EXPERTS // n_exp)).astype(jnp.int32).reshape(1)
+    me = lax.axis_index("seq").astype(jnp.int32).reshape(1)
+    w_gate, w_up = jnp.swapaxes(w_gate, 1, 2), jnp.swapaxes(w_up, 1, 2)
+    gates = gate_weights[0]
+    facts = jnp.concatenate([target, gates, gates, gates], axis=1)
+    facts = jnp.pad(facts, ((0, 0), (0, 128 - facts.shape[1])))
+    stream, piece = norm_tokens(context, residual[0], norm_gain, facts, share, offsets)
+
     slots = jnp.arange(group // PAGE, dtype=jnp.int32)
     order = jnp.sum(jnp.where(page_table[0][None, :] == slots[:, None], slots[None, :], 0), axis=1)
-    pages = jnp.take(pages, order, axis=0)
-    pages = pages.reshape(n_seq, rows_dev, 2 * span)
-    pages = lax.all_to_all(pages, "seq", split_axis=0, concat_axis=0, tiled=True)
-    cache = jnp.concatenate([unspan(pages[..., :span]), unspan(pages[..., span:])], axis=-1)
-    cache = cache.reshape(1, rows_dev // PAGE, PAGE, 2 * width)
-
-    everything = lax.all_gather(normed, everyone, axis=0, tiled=True)
-    first = (lax.axis_index("exp") * (EXPERTS // n_exp)).astype(jnp.int32).reshape(1)
-    partial = experts(everything, tgt, gates, w_gate, w_up, w_down, first)
-    mixture = lax.psum_scatter(partial, everyone, scatter_dimension=0, tiled=True)
-    layer_out = (stream + mixture.astype(jnp.float32)).astype(jnp.bfloat16)
-    return (layer_out[None], cache)
+
+    def fill_cache(late):
+        if n_seq & (n_seq - 1) == 0:
+            pages = pick_pages(packed, order, me, late, n_seq, span)
+            pages = [pages[0]] + [swap(pages[j], "seq", n_seq, j) for j in range(1, n_seq)]
+            return join_pages(pages, me, share, offsets, span)
+        pages = jnp.take(packed[:, span:].reshape(group // PAGE, PAGE, 2 * span), order, axis=0)
+        pages = pages.reshape(n_seq, rows_dev, 2 * span)
+        pages = lax.all_to_all(pages, "seq", split_axis=0, concat_axis=0, tiled=True)
+        parts = [
+            pages[j][:, at + offsets[j] : at + offsets[j] + share] for at in (0, span) for j in range(n_seq)
+        ]
+        return jnp.concatenate(parts, axis=1)
+
+    if (n_seq, n_exp) == (8, 4):
+        mixture, cache = exchange_experts(piece, w_gate, w_up, w_down, first, n_seq, n_exp, fill_cache)
+    else:
+        cache = fill_cache(piece)
+        blocks = n_seq * n_exp
+        everything = lax.all_gather(piece, everyone, axis=0, tiled=True)
+        facts = everything[:, width : width + 8].astype(jnp.float32)
+        facts = facts.reshape(blocks // CHUNK_BLOCKS, CHUNK_BLOCKS * rows_dev, 8).transpose(0, 2, 1)
+        gates = facts[:, 2:4] + facts[:, 4:6] + facts[:, 6:8]
+        partial = experts(
+            everything[:, :width], facts[:, :2].astype(jnp.int32), gates, w_gate, w_up, w_down, first
+        )
+        mixture = lax.psum_scatter(partial, everyone, scatter_dimension=0, tiled=True).astype(jnp.float32)
+    layer_out = (stream + mixture).astype(jnp.bfloat16)
+    return (layer_out[None], cache.reshape(1, rows_dev // PAGE, PAGE, 2 * width))
 
 
 def solution(mesh):

time: 344 us -> 336 us (0.977)
  blocking collectives: 85.3 us -> 0 us
  starting transfers between devices: 10.9 us -> 53.5 us
  Pallas kernels: 43.2 us -> 66 us
  waiting for transfers between devices: 147 us -> 163 us
  between operations: 14.4 us -> 1.27 us
  local copies, waits for them, and re-layouts: 36 us -> 42.3 us
    ppermute x0 -> x53, waiting for transfers between devices: none -> 128 us  [swap(): return lax.ppermute(a, axis, [(i, i ^ distance) for i in range(size)])]
    reduce_scatter x1 -> x0, waiting for transfers between devices: 110 us -> none  [body(): lax.psum_scatter(partial, everyone, scatter_dimension=0, tiled=True)]
    all_gather x1 -> x0, blocking collectives: 68.2 us -> none  [body(): facts = lax.all_gather(facts, everyone, axis=0, tiled=False)]
    ppermute x0 -> x53, starting transfers between devices: none -> 42.4 us  [swap(): return lax.ppermute(a, axis, [(i, i ^ distance) for i in range(size)])]
    pallas_call x1 -> x7, Pallas kernels: 37.6 us -> 60.4 us  [the longest x4 53.8 us: chunk_experts(): pl.pallas_call(functools.partial(chunk_kernel, local, len(pieces), rows,...]
    all_to_all x1 -> x0, blocking collectives: 17.1 us -> none  [body(): lax.all_to_all(pages, 'seq', split_axis=0, concat_axis=0, tiled=True)]
    unnamed x36 -> x136, local copies, waits for them, and re-layouts: 28 us -> 37.9 us
    convert_element_type x3 -> x12, other arithmetic: 0.86 us -> 4.35 us  [the longest x11 4.34 us: add(): return (a.astype(jnp.float32) + b.astype(jnp.float32)).astype(jnp.bfloat16)]
  transfers between devices with their start and end apart: 4 -> 55, of which waited for: 3 -> 19; matrix products, arithmetic and copies ran while one was open for 8% -> 2% of each run, Pallas kernels for 0% -> 17%
where the time goes in v3:
time: 336 us; the launch traced here: 335 us
  waiting for transfers between devices  163 us (49%)
  Pallas kernels  66 us (20%)
  starting transfers between devices  53.5 us (16%)
  local copies, waits for them, and re-layouts  42.3 us (13%)
  other arithmetic  8.74 us (3%)
    ppermute x53, waiting for transfers between devices, swap(): return lax.ppermute(a, axis, [(i, i ^ distance) for i in range(size)])  128 us
    pallas_call x4, Pallas kernels, chunk_experts(): pl.pallas_call(functools.partial(chunk_kernel, local, len(pieces), rows,...  53.8 us
    ppermute x53, starting transfers between devices, swap(): return lax.ppermute(a, axis, [(i, i ^ distance) for i in range(size)])  42.4 us
    unnamed x136, local copies, waits for them, and re-layouts  37.9 us
    all_to_all x1, waiting for transfers between devices, body(): lax.all_to_all(packed, 'seq', split_axis=0, concat_axis=0, tiled=True)  25.4 us
    all_to_all x1, waiting for transfers between devices, body(): lax.all_to_all(context.reshape(n_seq, rows_dev, span), 'seq', split_axis=...  9.8 us
    all_to_all x1, starting transfers between devices, body(): lax.all_to_all(packed, 'seq', split_axis=0, concat_axis=0, tiled=True)  7.38 us
  transfers between devices with their start and end apart: 55, of which 19 were waited for; matrix products, arithmetic and copies ran while one was open for 2% of the time, Pallas kernels for 17%

profile of v3, /device:TPU:0, one launch (start us, length us, event | category | flops | bytes accessed | tf_op | source)
XLA Modules:
  0.0 334.8 jit_solution(9758242040368583666)
XLA Ops:
  0.6 2.3 fusion.3
  5.7 7.4 %all-to-all-start = ((bf16[8,64,960]{2,1,0:T(8,128)(2,1)}), bf16[8,64,960]{2,1,0:T(8,128)(2,1)S(1)}, u32[]{:S(2)}, u32[]{:S(2)}) async-start(bf16[8,64,960]{2,1,0:T(8,128)(2,1)} %pad_maximum_fusion), calls=%async_computation | async-start | bytes 2097152 | tf_op jit(solution)/shard_map/all_to_all | solution.py:421
  13.5 25.4 %all-to-all-done = bf16[8,64,960]{2,1,0:T(8,128)(2,1)S(1)} async-done(((bf16[8,64,960]{2,1,0:T(8,128)(2,1)}), bf16[8,64,960]{2,1,0:T(8,128)(2,1)S(1)}, u32[]{:S(2)}, u32[]{:S(2)}) %all-to-all-start) | async-done | bytes 983072 | tf_op jit(solution)/shard_map/all_to_all | solution.py:421
  38.8 5.6 %shard_map.122 = bf16[512,320]{1,0:T(8,128)(2,1)} custom-call(bf16[512,960]{1,0:T(8,128)(2,1)S(1)} %bitcast.126, s32[1,512]{1,0:T(1,128)S(1)} %copy-done.33, s32[512,1]{1,0:T(8,128)S(1)} %copy.35.seg_col_ref), custom_call_target="tpu_custom_call" | custom-call | flops 335544320 | bytes 1310720 | tf_op jit(solution)/shard_map/pallas_call | solution.py:55
  44.4 3.6 %all-to-all-start.1 = ((bf16[8,64,320]{2,1,0:T(8,128)(2,1)}), bf16[8,64,320]{2,1,0:T(8,128)(2,1)S(1)}, u32[]{:S(2)}, u32[]{:S(2)}) async-start(bf16[8,64,320]{2,1,0:T(8,128)(2,1)} %bitcast.29), calls=%async_computation.1 | async-start | bytes 786432 | tf_op jit(solution)/shard_map/all_to_all | solution.py:424
  50.1 9.8 %all-to-all-done.1.context_ref = bf16[8,64,320]{2,1,0:T(8,128)(2,1)S(1)} async-done(((bf16[8,64,320]{2,1,0:T(8,128)(2,1)}), bf16[8,64,320]{2,1,0:T(8,128)(2,1)S(1)}, u32[]{:S(2)}, u32[]{:S(2)}) %all-to-all-start.1) | async-done | bytes 327712 | tf_op jit(solution)/shard_map/all_to_all | solution.py:424
  60.6 2.2 shard_map.123
  65.8 5.3 %collective-permute-done.1.rest_2_ = bf16[64,2432]{1,0:T(8,128)(2,1)S(1)} collective-permute-done((bf16[64,2432]{1,0:T(8,128)(2,1)}, bf16[64,2432]{1,0:T(8,128)(2,1)S(1)}, u32[]{:S(2)}, u32[]{:S(2)}) %collective-permute-start.1) | collective-permute-done | bytes 311328 | tf_op jit(solution)/shard_map/ppermute | solution.py:331
  74.2 5.0 %collective-permute-done.2.rest_3_ = bf16[64,2432]{1,0:T(8,128)(2,1)S(1)} collective-permute-done((bf16[64,2432]{1,0:T(8,128)(2,1)S(1)}, bf16[64,2432]{1,0:T(8,128)(2,1)S(1)}, u32[]{:S(2)}, u32[]{:S(2)}) %collective-permute-start.2) | collective-permute-done | bytes 311328 | tf_op jit(solution)/shard_map/ppermute | solution.py:331
  80.7 1.5 collective-permute-start.22
  82.6 2.3 collective-permute-start.34
  87.6 2.9 copy-done
  90.5 2.9 copy-done.3
  100.1 12.9 %shard_map.124 = (bf16[256,2304]{1,0:T(8,128)(2,1)S(1)}, bf16[256,2304]{1,0:T(8,128)(2,1)S(1)}) custom-call(s32[1]{0:T(128)} %bitcast.33.first_ref, bf16[2,720,2304]{2,1,0:T(8,128)(2,1)S(1)} %bitcast.118, bf16[2,720,2304]{2,1,0:T(8,128)(2,1)S(1)} %bitcast.122, bf16[2,720,2304]{2,1,0:T(8,128)(2,1)} %wd_ref.7, bf16[64,2432]{1,0:T(8,128)(2,1)S(1)} %copy-done.16, ...), custom_call_target="tpu_custom_call" | custom-call | flops 3822059520 | bytes 24625152 | tf_op jit(solution)/shard_map/pallas_call | solution.py:307
  113.2 1.8 collective-permute-start.11
  115.5 1.7 collective-permute-start.13
  117.2 6.3 %collective-permute-done.11.rest_1_ = bf16[64,2432]{1,0:T(8,128)(2,1)} collective-permute-done((bf16[64,2432]{1,0:T(8,128)(2,1)S(1)}, bf16[64,2432]{1,0:T(8,128)(2,1)}, u32[]{:S(2)}, u32[]{:S(2)}) %collective-permute-start.11) | collective-permute-done | bytes 311328 | tf_op jit(solution)/shard_map/ppermute | solution.py:331
  126.5 3.7 %collective-permute-done.24.rest_2_ = bf16[64,2432]{1,0:T(8,128)(2,1)} collective-permute-done((bf16[64,2432]{1,0:T(8,128)(2,1)}, bf16[64,2432]{1,0:T(8,128)(2,1)}, u32[]{:S(2)}, u32[]{:S(2)}) %collective-permute-start.24) | collective-permute-done | bytes 311328 | tf_op jit(solution)/shard_map/ppermute | solution.py:331
  130.2 6.2 %collective-permute-done.13.rest_3_ = bf16[64,2432]{1,0:T(8,128)(2,1)} collective-permute-done((bf16[64,2432]{1,0:T(8,128)(2,1)S(1)}, bf16[64,2432]{1,0:T(8,128)(2,1)}, u32[]{:S(2)}, u32[]{:S(2)}) %collective-permute-start.13) | collective-permute-done | bytes 311328 | tf_op jit(solution)/shard_map/ppermute | solution.py:331
  139.2 1.7 collective-permute-start.35
  141.4 2.9 copy-done.1
  144.3 2.9 copy-done.4
  151.1 14.4 %shard_map.125 = (bf16[256,2304]{1,0:T(8,128)(2,1)S(1)}, bf16[256,2304]{1,0:T(8,128)(2,1)}) custom-call(s32[1]{0:T(128)} %bitcast.33.first_ref, bf16[2,720,2304]{2,1,0:T(8,128)(2,1)S(1)} %bitcast.119, bf16[2,720,2304]{2,1,0:T(8,128)(2,1)S(1)} %bitcast.123, bf16[2,720,2304]{2,1,0:T(8,128)(2,1)} %wd_ref.7, bf16[64,2432]{1,0:T(8,128)(2,1)S(1)} %copy-done.9, ...), custom_call_target="tpu_custom_call" | custom-call | flops 3822059520 | bytes 24625152 | tf_op jit(solution)/shard_map/pallas_call | solution.py:307
  166.8 2.2 shard_map.128
  170.2 1.6 add_convert_fusion.7
  172.3 7.2 %collective-permute-done.37.rest_3_ = bf16[64,2432]{1,0:T(8,128)(2,1)S(1)} collective-permute-done((bf16[64,2432]{1,0:T(8,128)(2,1)}, bf16[64,2432]{1,0:T(8,128)(2,1)S(1)}, u32[]{:S(2)}, u32[]{:S(2)}) %collective-permute-start.37) | collective-permute-done | bytes 311328 | tf_op jit(solution)/shard_map/ppermute | solution.py:331
  180.1 2.9 copy-done.2
  183.0 2.9 copy-done.5
  185.9 13.2 %shard_map.126 = (bf16[256,2304]{1,0:T(8,128)(2,1)S(1)}, bf16[256,2304]{1,0:T(8,128)(2,1)S(1)}) custom-call(s32[1]{0:T(128)} %bitcast.33.first_ref, bf16[2,720,2304]{2,1,0:T(8,128)(2,1)S(1)} %bitcast.120, bf16[2,720,2304]{2,1,0:T(8,128)(2,1)S(1)} %bitcast.124, bf16[2,720,2304]{2,1,0:T(8,128)(2,1)} %wd_ref.7, ...), custom_call_target="tpu_custom_call" | custom-call | flops 3822059520 | bytes 24625152 | tf_op jit(solution)/shard_map/pallas_call | solution.py:307
  199.5 1.6 add_convert_fusion.5
  201.1 13.3 %collective-permute-done.8 = bf16[128,2304]{1,0:T(8,128)(2,1)S(1)} collective-permute-done((bf16[128,2304]{1,0:T(8,128)(2,1)S(1)}, bf16[128,2304]{1,0:T(8,128)(2,1)S(1)}, u32[]{:S(2)}, u32[]{:S(2)}) %collective-permute-start.8) | collective-permute-done | bytes 589856 | tf_op jit(solution)/shard_map/ppermute | solution.py:331
  216.4 3.2 collective-permute-start.48
  219.7 13.3 %shard_map.127 = (bf16[256,2304]{1,0:T(8,128)(2,1)S(1)}, bf16[256,2304]{1,0:T(8,128)(2,1)S(1)}) custom-call(s32[1]{0:T(128)} %bitcast.33.first_ref, bf16[2,720,2304]{2,1,0:T(8,128)(2,1)S(1)} %bitcast.121, bf16[2,720,2304]{2,1,0:T(8,128)(2,1)S(1)} %bitcast.125, bf16[2,720,2304]{2,1,0:T(8,128)(2,1)} %wd_ref.7, ...), custom_call_target="tpu_custom_call" | custom-call | flops 3822059520 | bytes 24625152 | tf_op jit(solution)/shard_map/pallas_call | solution.py:307
  233.8 8.8 %collective-permute-done.20 = bf16[64,2304]{1,0:T(8,128)(2,1)S(1)} collective-permute-done((bf16[64,2304]{1,0:T(8,128)(2,1)S(1)}, bf16[64,2304]{1,0:T(8,128)(2,1)S(1)}, u32[]{:S(2)}, u32[]{:S(2)}) %collective-permute-start.20) | collective-permute-done | bytes 294944 | tf_op jit(solution)/shard_map/ppermute | solution.py:331
  243.7 14.1 %collective-permute-done.31 = bf16[128,2304]{1,0:T(8,128)(2,1)S(1)} collective-permute-done((bf16[128,2304]{1,0:T(8,128)(2,1)S(1)}, bf16[128,2304]{1,0:T(8,128)(2,1)S(1)}, u32[]{:S(2)}, u32[]{:S(2)}) %collective-permute-start.31) | collective-permute-done | bytes 589856 | tf_op jit(solution)/shard_map/ppermute | solution.py:331
  257.8 1.5 collective-permute-start.43
  259.4 12.1 %collective-permute-done.43 = bf16[128,2304]{1,0:T(8,128)(2,1)S(1)} collective-permute-done((bf16[128,2304]{1,0:T(8,128)(2,1)S(1)}, bf16[128,2304]{1,0:T(8,128)(2,1)S(1)}, u32[]{:S(2)}, u32[]{:S(2)}) %collective-permute-start.43) | collective-permute-done | bytes 589856 | tf_op jit(solution)/shard_map/ppermute | solution.py:331
  271.6 1.5 collective-permute-start.32
  273.2 5.1 %collective-permute-done.32 = bf16[64,2304]{1,0:T(8,128)(2,1)S(1)} collective-permute-done((bf16[64,2304]{1,0:T(8,128)(2,1)S(1)}, bf16[64,2304]{1,0:T(8,128)(2,1)S(1)}, u32[]{:S(2)}, u32[]{:S(2)}) %collective-permute-start.32) | collective-permute-done | bytes 294944 | tf_op jit(solution)/shard_map/ppermute | solution.py:331
  278.7 6.3 %collective-permute-done.44 = bf16[64,2304]{1,0:T(8,128)(2,1)S(1)} collective-permute-done((bf16[64,2304]{1,0:T(8,128)(2,1)S(1)}, bf16[64,2304]{1,0:T(8,128)(2,1)S(1)}, u32[]{:S(2)}, u32[]{:S(2)}) %collective-permute-start.44) | collective-permute-done | bytes 294944 | tf_op jit(solution)/shard_map/ppermute | solution.py:331
  285.0 1.5 collective-permute-start.9
  288.4 2.7 collective-permute-start.45
  291.8 24.0 %collective-permute-done.50.refs_5_ = bf16[64,640]{1,0:T(8,128)(2,1)S(1)} collective-permute-done((bf16[64,640]{1,0:T(8,128)(2,1)S(1)}, bf16[64,640]{1,0:T(8,128)(2,1)S(1)}, u32[]{:S(2)}, u32[]{:S(2)}) %collective-permute-start.50) | collective-permute-done | bytes 81952 | tf_op jit(solution)/shard_map/ppermute | solution.py:331
  317.9 5.5 %collective-permute-done.51.refs_6_ = bf16[64,640]{1,0:T(8,128)(2,1)} collective-permute-done((bf16[64,640]{1,0:T(8,128)(2,1)S(1)}, bf16[64,640]{1,0:T(8,128)(2,1)}, u32[]{:S(2)}, u32[]{:S(2)}) %collective-permute-start.51) | collective-permute-done | bytes 81952 | tf_op jit(solution)/shard_map/ppermute | solution.py:331
  323.3 3.1 collective-permute-start.52
  326.4 4.2 %collective-permute-done.52.refs_7_ = bf16[64,640]{1,0:T(8,128)(2,1)} collective-permute-done((bf16[64,640]{1,0:T(8,128)(2,1)S(1)}, bf16[64,640]{1,0:T(8,128)(2,1)}, u32[]{:S(2)}, u32[]{:S(2)}) %collective-permute-start.52) | collective-permute-done | bytes 81952 | tf_op jit(solution)/shard_map/ppermute | solution.py:331
  330.6 2.2 shard_map.129
  332.8 2.0 fusion
  (237 shorter events, 46.9 us)
Async XLA Ops:
  5.7 33.2 %all-to-all-start = ((bf16[8,64,960]{2,1,0:T(8,128)(2,1)}), bf16[8,64,960]{2,1,0:T(8,128)(2,1)S(1)}, u32[]{:S(2)}, u32[]{:S(2)}) async-start(bf16[8,64,960]{2,1,0:T(8,128)(2,1)} %pad_maximum_fusion), calls=%async_computation | async-start | bytes 2097152 | tf_op jit(solution)/shard_map/all_to_all | solution.py:421
  44.4 15.5 %all-to-all-start.1 = ((bf16[8,64,320]{2,1,0:T(8,128)(2,1)}), bf16[8,64,320]{2,1,0:T(8,128)(2,1)S(1)}, u32[]{:S(2)}, u32[]{:S(2)}) async-start(bf16[8,64,320]{2,1,0:T(8,128)(2,1)} %bitcast.29), calls=%async_computation.1 | async-start | bytes 786432 | tf_op jit(solution)/shard_map/all_to_all | solution.py:424
  62.8 8.3 %collective-permute-start.1 = (bf16[64,2432]{1,0:T(8,128)(2,1)}, bf16[64,2432]{1,0:T(8,128)(2,1)S(1)}, u32[]{:S(2)}, u32[]{:S(2)}) collective-permute-start(bf16[64,2432]{1,0:T(8,128)(2,1)} %get-tuple-element.21.rest_0_), channel_id=1, source_target_pairs={{0,4},{4,0},{8,12},{12,8},{16,20},{20,16},{24,28},{28,24},{1,5},{5... | collective-permute-start | bytes 933896 | tf_op jit(solution)/shard_map/ppermute | solution.py:331
  64.3 9.2 %collective-permute-start = (bf16[64,2432]{1,0:T(8,128)(2,1)}, bf16[64,2432]{1,0:T(8,128)(2,1)S(1)}, u32[]{:S(2)}, u32[]{:S(2)}) collective-permute-start(bf16[64,2432]{1,0:T(8,128)(2,1)} %get-tuple-element.21.rest_0_), channel_id=1, source_target_pairs={{0,2},{1,3},{2,0},{3,1},{4,6},{5,7},{6,4},{7,5},{8,10},{9,11},{10,... | collective-permute-start | bytes 933896 | tf_op jit(solution)/shard_map/ppermute | solution.py:331
  71.1 8.1 %collective-permute-start.2 = (bf16[64,2432]{1,0:T(8,128)(2,1)S(1)}, bf16[64,2432]{1,0:T(8,128)(2,1)S(1)}, u32[]{:S(2)}, u32[]{:S(2)}) collective-permute-start(bf16[64,2432]{1,0:T(8,128)(2,1)S(1)} %collective-permute-done.1.rest_2_), channel_id=1, source_target_pairs={{0,2},{1,3},{2,0},{3,1},{4,6},{5,7},{6,4},{7,5},{8,10},{9,11},{10,... | collective-permute-start | bytes 933896 | tf_op jit(solution)/shard_map/ppermute | solution.py:331
  72.6 7.4 %collective-permute-start.3 = (bf16[64,2432]{1,0:T(8,128)(2,1)}, bf16[64,2432]{1,0:T(8,128)(2,1)S(1)}, u32[]{:S(2)}, u32[]{:S(2)}) collective-permute-start(bf16[64,2432]{1,0:T(8,128)(2,1)} %get-tuple-element.21.rest_0_), channel_id=1, source_target_pairs={{0,1},{1,0},{2,3},{3,2},{4,5},{5,4},{6,7},{7,6},{8,9},{9,8},{10,11... | collective-permute-start | bytes 933896 | tf_op jit(solution)/shard_map/ppermute | solution.py:331
  72.6 10.0 %collective-permute-start.10 = (bf16[64,2432]{1,0:T(8,128)(2,1)}, bf16[64,2432]{1,0:T(8,128)(2,1)S(1)}, u32[]{:S(2)}, u32[]{:S(2)}) collective-permute-start(bf16[64,2432]{1,0:T(8,128)(2,1)} %get-tuple-element.21.rest_0_), channel_id=1, source_target_pairs={{0,8},{4,12},{8,0},{12,4},{16,24},{20,28},{24,16},{28,20},{1,9},{5... | collective-permute-start | bytes 933896 | tf_op jit(solution)/shard_map/ppermute | solution.py:331
  72.6 12.3 %collective-permute-start.5 = (bf16[64,2432]{1,0:T(8,128)(2,1)S(1)}, bf16[64,2432]{1,0:T(8,128)(2,1)S(1)}, u32[]{:S(2)}, u32[]{:S(2)}) collective-permute-start(bf16[64,2432]{1,0:T(8,128)(2,1)S(1)} %collective-permute-done.1.rest_2_), channel_id=1, source_target_pairs={{0,1},{1,0},{2,3},{3,2},{4,5},{5,4},{6,7},{7,6},{8,9},{9,8},{10,11... | collective-permute-start | bytes 933896 | tf_op jit(solution)/shard_map/ppermute | solution.py:331
  73.5 12.7 %collective-permute-start.4 = (bf16[64,2432]{1,0:T(8,128)(2,1)S(1)}, bf16[64,2432]{1,0:T(8,128)(2,1)S(1)}, u32[]{:S(2)}, u32[]{:S(2)}) collective-permute-start(bf16[64,2432]{1,0:T(8,128)(2,1)S(1)} %collective-permute-done.rest_1_), channel_id=1, source_target_pairs={{0,1},{1,0},{2,3},{3,2},{4,5},{5,4},{6,7},{7,6},{8,9},{9,8},{10,11... | collective-permute-start | bytes 933896 | tf_op jit(solution)/shard_map/ppermute | solution.py:331
  79.2 7.7 %collective-permute-start.6 = (bf16[64,2432]{1,0:T(8,128)(2,1)S(1)}, bf16[64,2432]{1,0:T(8,128)(2,1)S(1)}, u32[]{:S(2)}, u32[]{:S(2)}) collective-permute-start(bf16[64,2432]{1,0:T(8,128)(2,1)S(1)} %collective-permute-done.2.rest_3_), channel_id=1, source_target_pairs={{0,1},{1,0},{2,3},{3,2},{4,5},{5,4},{6,7},{7,6},{8,9},{9,8},{10,11... | collective-permute-start | bytes 933896 | tf_op jit(solution)/shard_map/ppermute | solution.py:331
  80.7 34.3 %collective-permute-start.22 = (bf16[64,2432]{1,0:T(8,128)(2,1)}, bf16[64,2432]{1,0:T(8,128)(2,1)}, u32[]{:S(2)}, u32[]{:S(2)}) collective-permute-start(bf16[64,2432]{1,0:T(8,128)(2,1)} %get-tuple-element.21.rest_0_), channel_id=1, source_target_pairs={{0,16},{4,20},{8,24},{12,28},{16,0},{20,4},{24,8},{28,12},{1,17},{... | collective-permute-start | bytes 933896 | tf_op jit(solution)/shard_map/ppermute | solution.py:331
  82.6 32.6 %collective-permute-start.34 = (bf16[64,2432]{1,0:T(8,128)(2,1)}, bf16[64,2432]{1,0:T(8,128)(2,1)}, u32[]{:S(2)}, u32[]{:S(2)}) collective-permute-start(bf16[64,2432]{1,0:T(8,128)(2,1)} %get-tuple-element.21.rest_0_), channel_id=1, source_target_pairs={{0,24},{4,28},{8,16},{12,20},{16,8},{20,12},{24,0},{28,4},{1,25},{... | collective-permute-start | bytes 933896 | tf_op jit(solution)/shard_map/ppermute | solution.py:331
  85.6 29.9 %collective-permute-start.12 = (bf16[64,2432]{1,0:T(8,128)(2,1)S(1)}, bf16[64,2432]{1,0:T(8,128)(2,1)S(1)}, u32[]{:S(2)}, u32[]{:S(2)}) collective-permute-start(bf16[64,2432]{1,0:T(8,128)(2,1)S(1)} %collective-permute-done.10.rest_0_), channel_id=1, source_target_pairs={{0,2},{1,3},{2,0},{3,1},{4,6},{5,7},{6,4},{7,5},{8,10},{9,11},{10,... | collective-permute-start | bytes 933896 | tf_op jit(solution)/shard_map/ppermute | solution.py:331
  113.1 56.9 %collective-permute-start.7 = (bf16[256,2304]{1,0:T(8,128)(2,1)S(1)}, bf16[256,2304]{1,0:T(8,128)(2,1)}, u32[]{:S(2)}, u32[]{:S(2)}) collective-permute-start(bf16[256,2304]{1,0:T(8,128)(2,1)S(1)} %get-tuple-element.23.late_ref), channel_id=1, source_target_pairs={{0,1},{1,0},{2,3},{3,2},{4,5},{5,4},{6,7},{7,6},{8,9},{9,8},{10,11... | collective-permute-start | bytes 3538952 | tf_op jit(solution)/shard_map/ppermute | solution.py:331
  113.2 10.3 %collective-permute-start.11 = (bf16[64,2432]{1,0:T(8,128)(2,1)S(1)}, bf16[64,2432]{1,0:T(8,128)(2,1)}, u32[]{:S(2)}, u32[]{:S(2)}) collective-permute-start(bf16[64,2432]{1,0:T(8,128)(2,1)S(1)} %collective-permute-done.10.rest_0_), channel_id=1, source_target_pairs={{0,4},{4,0},{8,12},{12,8},{16,20},{20,16},{24,28},{28,24},{1,5},{5... | collective-permute-start | bytes 933896 | tf_op jit(solution)/shard_map/ppermute | solution.py:331
  115.0 10.0 %collective-permute-start.14 = (bf16[64,2432]{1,0:T(8,128)(2,1)S(1)}, bf16[64,2432]{1,0:T(8,128)(2,1)S(1)}, u32[]{:S(2)}, u32[]{:S(2)}) collective-permute-start(bf16[64,2432]{1,0:T(8,128)(2,1)S(1)} %collective-permute-done.10.rest_0_), channel_id=1, source_target_pairs={{0,1},{1,0},{2,3},{3,2},{4,5},{5,4},{6,7},{7,6},{8,9},{9,8},{10,11... | collective-permute-start | bytes 933896 | tf_op jit(solution)/shard_map/ppermute | solution.py:331
  115.1 15.0 %collective-permute-start.24 = (bf16[64,2432]{1,0:T(8,128)(2,1)}, bf16[64,2432]{1,0:T(8,128)(2,1)}, u32[]{:S(2)}, u32[]{:S(2)}) collective-permute-start(bf16[64,2432]{1,0:T(8,128)(2,1)} %collective-permute-done.22.rest_0_), channel_id=1, source_target_pairs={{0,4},{4,0},{8,12},{12,8},{16,20},{20,16},{24,28},{28,24},{1,5},{5... | collective-permute-start | bytes 933896 | tf_op jit(solution)/shard_map/ppermute | solution.py:331
  115.5 20.9 %collective-permute-start.13 = (bf16[64,2432]{1,0:T(8,128)(2,1)S(1)}, bf16[64,2432]{1,0:T(8,128)(2,1)}, u32[]{:S(2)}, u32[]{:S(2)}) collective-permute-start(bf16[64,2432]{1,0:T(8,128)(2,1)S(1)} %collective-permute-done.12.rest_2_), channel_id=1, source_target_pairs={{0,4},{4,0},{8,12},{12,8},{16,20},{20,16},{24,28},{28,24},{1,5},{5... | collective-permute-start | bytes 933896 | tf_op jit(solution)/shard_map/ppermute | solution.py:331
  123.5 12.9 %collective-permute-start.23 = (bf16[64,2432]{1,0:T(8,128)(2,1)}, bf16[64,2432]{1,0:T(8,128)(2,1)S(1)}, u32[]{:S(2)}, u32[]{:S(2)}) collective-permute-start(bf16[64,2432]{1,0:T(8,128)(2,1)} %collective-permute-done.22.rest_0_), channel_id=1, source_target_pairs={{0,2},{1,3},{2,0},{3,1},{4,6},{5,7},{6,4},{7,5},{8,10},{9,11},{10,... | collective-permute-start | bytes 933896 | tf_op jit(solution)/shard_map/ppermute | solution.py:331
  125.7 11.2 %collective-permute-start.16 = (bf16[64,2432]{1,0:T(8,128)(2,1)S(1)}, bf16[64,2432]{1,0:T(8,128)(2,1)S(1)}, u32[]{:S(2)}, u32[]{:S(2)}) collective-permute-start(bf16[64,2432]{1,0:T(8,128)(2,1)S(1)} %collective-permute-done.12.rest_2_), channel_id=1, source_target_pairs={{0,1},{1,0},{2,3},{3,2},{4,5},{5,4},{6,7},{7,6},{8,9},{9,8},{10,11... | collective-permute-start | bytes 933896 | tf_op jit(solution)/shard_map/ppermute | solution.py:331
  130.2 9.0 %collective-permute-start.15 = (bf16[64,2432]{1,0:T(8,128)(2,1)}, bf16[64,2432]{1,0:T(8,128)(2,1)}, u32[]{:S(2)}, u32[]{:S(2)}) collective-permute-start(bf16[64,2432]{1,0:T(8,128)(2,1)} %collective-permute-done.11.rest_1_), channel_id=1, source_target_pairs={{0,1},{1,0},{2,3},{3,2},{4,5},{5,4},{6,7},{7,6},{8,9},{9,8},{10,11... | collective-permute-start | bytes 933896 | tf_op jit(solution)/shard_map/ppermute | solution.py:331
  136.4 29.0 %collective-permute-start.26 = (bf16[64,2432]{1,0:T(8,128)(2,1)}, bf16[64,2432]{1,0:T(8,128)(2,1)S(1)}, u32[]{:S(2)}, u32[]{:S(2)}) collective-permute-start(bf16[64,2432]{1,0:T(8,128)(2,1)} %collective-permute-done.22.rest_0_), channel_id=1, source_target_pairs={{0,1},{1,0},{2,3},{3,2},{4,5},{5,4},{6,7},{7,6},{8,9},{9,8},{10,11... | collective-permute-start | bytes 933896 | tf_op jit(solution)/shard_map/ppermute | solution.py:331
  137.6 31.4 %collective-permute-start.36 = (bf16[64,2432]{1,0:T(8,128)(2,1)}, bf16[64,2432]{1,0:T(8,128)(2,1)}, u32[]{:S(2)}, u32[]{:S(2)}) collective-permute-start(bf16[64,2432]{1,0:T(8,128)(2,1)} %collective-permute-done.34.rest_0_), channel_id=1, source_target_pairs={{0,2},{1,3},{2,0},{3,1},{4,6},{5,7},{6,4},{7,5},{8,10},{9,11},{10,... | collective-permute-start | bytes 933896 | tf_op jit(solution)/shard_map/ppermute | solution.py:331
  139.2 30.4 %collective-permute-start.35 = (bf16[64,2432]{1,0:T(8,128)(2,1)}, bf16[64,2432]{1,0:T(8,128)(2,1)}, u32[]{:S(2)}, u32[]{:S(2)}) collective-permute-start(bf16[64,2432]{1,0:T(8,128)(2,1)} %collective-permute-done.34.rest_0_), channel_id=1, source_target_pairs={{0,4},{4,0},{8,12},{12,8},{16,20},{20,16},{24,28},{28,24},{1,5},{5... | collective-permute-start | bytes 933896 | tf_op jit(solution)/shard_map/ppermute | solution.py:331
  140.9 28.7 %collective-permute-start.25 = (bf16[64,2432]{1,0:T(8,128)(2,1)}, bf16[64,2432]{1,0:T(8,128)(2,1)}, u32[]{:S(2)}, u32[]{:S(2)}) collective-permute-start(bf16[64,2432]{1,0:T(8,128)(2,1)} %collective-permute-done.24.rest_2_), channel_id=1, source_target_pairs={{0,2},{1,3},{2,0},{3,1},{4,6},{5,7},{6,4},{7,5},{8,10},{9,11},{10,... | collective-permute-start | bytes 933896 | tf_op jit(solution)/shard_map/ppermute | solution.py:331
  166.2 32.9 %collective-permute-start.18 = (bf16[256,2304]{1,0:T(8,128)(2,1)}, bf16[256,2304]{1,0:T(8,128)(2,1)}, u32[]{:S(2)}, u32[]{:S(2)}) collective-permute-start(bf16[256,2304]{1,0:T(8,128)(2,1)} %get-tuple-element.25), channel_id=1, source_target_pairs={{0,1},{1,0},{2,3},{3,2},{4,5},{5,4},{6,7},{7,6},{8,9},{9,8},{10,11... | collective-permute-start | bytes 3538952 | tf_op jit(solution)/shard_map/ppermute | solution.py:331
  169.7 9.9 %collective-permute-start.37 = (bf16[64,2432]{1,0:T(8,128)(2,1)}, bf16[64,2432]{1,0:T(8,128)(2,1)S(1)}, u32[]{:S(2)}, u32[]{:S(2)}) collective-permute-start(bf16[64,2432]{1,0:T(8,128)(2,1)} %collective-permute-done.36.rest_2_), channel_id=1, source_target_pairs={{0,4},{4,0},{8,12},{12,8},{16,20},{20,16},{24,28},{28,24},{1,5},{5... | collective-permute-start | bytes 933896 | tf_op jit(solution)/shard_map/ppermute | solution.py:331
  170.0 9.6 %collective-permute-start.29 = (bf16[64,2432]{1,0:T(8,128)(2,1)}, bf16[64,2432]{1,0:T(8,128)(2,1)S(1)}, u32[]{:S(2)}, u32[]{:S(2)}) collective-permute-start(bf16[64,2432]{1,0:T(8,128)(2,1)} %collective-permute-done.25.rest_3_), channel_id=1, source_target_pairs={{0,1},{1,0},{2,3},{3,2},{4,5},{5,4},{6,7},{7,6},{8,9},{9,8},{10,11... | collective-permute-start | bytes 933896 | tf_op jit(solution)/shard_map/ppermute | solution.py:331
  171.8 29.3 %collective-permute-start.38 = (bf16[64,2432]{1,0:T(8,128)(2,1)}, bf16[64,2432]{1,0:T(8,128)(2,1)S(1)}, u32[]{:S(2)}, u32[]{:S(2)}) collective-permute-start(bf16[64,2432]{1,0:T(8,128)(2,1)} %collective-permute-done.34.rest_0_), channel_id=1, source_target_pairs={{0,1},{1,0},{2,3},{3,2},{4,5},{5,4},{6,7},{7,6},{8,9},{9,8},{10,11... | collective-permute-start | bytes 933896 | tf_op jit(solution)/shard_map/ppermute | solution.py:331
  172.1 43.9 %collective-permute-start.40 = (bf16[64,2432]{1,0:T(8,128)(2,1)}, bf16[64,2432]{1,0:T(8,128)(2,1)S(1)}, u32[]{:S(2)}, u32[]{:S(2)}) collective-permute-start(bf16[64,2432]{1,0:T(8,128)(2,1)} %collective-permute-done.36.rest_2_), channel_id=1, source_target_pairs={{0,1},{1,0},{2,3},{3,2},{4,5},{5,4},{6,7},{7,6},{8,9},{9,8},{10,11... | collective-permute-start | bytes 933896 | tf_op jit(solution)/shard_map/ppermute | solution.py:331
  179.6 36.8 %collective-permute-start.39 = (bf16[64,2432]{1,0:T(8,128)(2,1)}, bf16[64,2432]{1,0:T(8,128)(2,1)S(1)}, u32[]{:S(2)}, u32[]{:S(2)}) collective-permute-start(bf16[64,2432]{1,0:T(8,128)(2,1)} %collective-permute-done.35.rest_1_), channel_id=1, source_target_pairs={{0,1},{1,0},{2,3},{3,2},{4,5},{5,4},{6,7},{7,6},{8,9},{9,8},{10,11... | collective-permute-start | bytes 933896 | tf_op jit(solution)/shard_map/ppermute | solution.py:331
  179.6 36.8 %collective-permute-start.41 = (bf16[64,2432]{1,0:T(8,128)(2,1)S(1)}, bf16[64,2432]{1,0:T(8,128)(2,1)S(1)}, u32[]{:S(2)}, u32[]{:S(2)}) collective-permute-start(bf16[64,2432]{1,0:T(8,128)(2,1)S(1)} %collective-permute-done.37.rest_3_), channel_id=1, source_target_pairs={{0,1},{1,0},{2,3},{3,2},{4,5},{5,4},{6,7},{7,6},{8,9},{9,8},{10,11... | collective-permute-start | bytes 933896 | tf_op jit(solution)/shard_map/ppermute | solution.py:331
  199.1 15.3 %collective-permute-start.8 = (bf16[128,2304]{1,0:T(8,128)(2,1)S(1)}, bf16[128,2304]{1,0:T(8,128)(2,1)S(1)}, u32[]{:S(2)}, u32[]{:S(2)}) collective-permute-start(bf16[128,2304]{1,0:T(8,128)(2,1)S(1)} %get-tuple-element.45.rest_8_), channel_id=1, source_target_pairs={{0,4},{4,0},{8,12},{12,8},{16,20},{20,16},{24,28},{28,24},{1,5},{5... | collective-permute-start | bytes 1769480 | tf_op jit(solution)/shard_map/ppermute | solution.py:331
  201.0 32.1 %collective-permute-start.30 = (bf16[256,2304]{1,0:T(8,128)(2,1)S(1)}, bf16[256,2304]{1,0:T(8,128)(2,1)S(1)}, u32[]{:S(2)}, u32[]{:S(2)}) collective-permute-start(bf16[256,2304]{1,0:T(8,128)(2,1)S(1)} %get-tuple-element.27), channel_id=1, source_target_pairs={{0,1},{1,0},{2,3},{3,2},{4,5},{5,4},{6,7},{7,6},{8,9},{9,8},{10,11... | collective-permute-start | bytes 3538952 | tf_op jit(solution)/shard_map/ppermute | solution.py:331
  214.4 18.5 %collective-permute-start.19 = (bf16[128,2304]{1,0:T(8,128)(2,1)S(1)}, bf16[128,2304]{1,0:T(8,128)(2,1)S(1)}, u32[]{:S(2)}, u32[]{:S(2)}) collective-permute-start(bf16[128,2304]{1,0:T(8,128)(2,1)S(1)} %get-tuple-element.39.rest_9_), channel_id=1, source_target_pairs={{0,2},{1,3},{2,0},{3,1},{4,6},{5,7},{6,4},{7,5},{8,10},{9,11},{10,... | collective-permute-start | bytes 1769480 | tf_op jit(solution)/shard_map/ppermute | solution.py:331
  216.0 70.6 %collective-permute-start.46 = (bf16[64,640]{1,0:T(8,128)(2,1)S(1)}, bf16[64,640]{1,0:T(8,128)(2,1)S(1)}, u32[]{:S(2)}, u32[]{:S(2)}) collective-permute-start(bf16[64,640]{1,0:T(8,128)(2,1)S(1)} %copy-done.55), channel_id=1, source_target_pairs={{0,4},{4,0},{8,12},{12,8},{16,20},{20,16},{24,28},{28,24},{1,5},{5... | collective-permute-start | bytes 245768 | tf_op jit(solution)/shard_map/ppermute | solution.py:331
  216.4 71.1 %collective-permute-start.47 = (bf16[64,640]{1,0:T(8,128)(2,1)S(1)}, bf16[64,640]{1,0:T(8,128)(2,1)S(1)}, u32[]{:S(2)}, u32[]{:S(2)}) collective-permute-start(bf16[64,640]{1,0:T(8,128)(2,1)S(1)} %copy-done.54), channel_id=1, source_target_pairs={{0,8},{4,12},{8,0},{12,4},{16,24},{20,28},{24,16},{28,20},{1,9},{5... | collective-permute-start | bytes 245768 | tf_op jit(solution)/shard_map/ppermute | solution.py:331
  216.4 72.0 %collective-permute-start.48 = (bf16[64,640]{1,0:T(8,128)(2,1)S(1)}, bf16[64,640]{1,0:T(8,128)(2,1)S(1)}, u32[]{:S(2)}, u32[]{:S(2)}) collective-permute-start(bf16[64,640]{1,0:T(8,128)(2,1)S(1)} %copy-done.53), channel_id=1, source_target_pairs={{0,12},{4,8},{8,4},{12,0},{16,28},{20,24},{24,20},{28,16},{1,13},{... | collective-permute-start | bytes 245768 | tf_op jit(solution)/shard_map/ppermute | solution.py:331
  232.9 10.1 %collective-permute-start.42 = (bf16[256,2304]{1,0:T(8,128)(2,1)S(1)}, bf16[256,2304]{1,0:T(8,128)(2,1)S(1)}, u32[]{:S(2)}, u32[]{:S(2)}) collective-permute-start(bf16[256,2304]{1,0:T(8,128)(2,1)S(1)} %get-tuple-element.29), channel_id=1, source_target_pairs={{0,1},{1,0},{2,3},{3,2},{4,5},{5,4},{6,7},{7,6},{8,9},{9,8},{10,11... | collective-permute-start | bytes 3538952 | tf_op jit(solution)/shard_map/ppermute | solution.py:331
  233.1 9.5 %collective-permute-start.20 = (bf16[64,2304]{1,0:T(8,128)(2,1)S(1)}, bf16[64,2304]{1,0:T(8,128)(2,1)S(1)}, u32[]{:S(2)}, u32[]{:S(2)}) collective-permute-start(bf16[64,2304]{1,0:T(8,128)(2,1)S(1)} %add_convert_fusion.16), channel_id=1, source_target_pairs={{0,4},{4,0},{8,12},{12,8},{16,20},{20,16},{24,28},{28,24},{1,5},{5... | collective-permute-start | bytes 884744 | tf_op jit(solution)/shard_map/ppermute | solution.py:331
  242.6 48.5 %collective-permute-start.49 = (bf16[64,640]{1,0:T(8,128)(2,1)S(1)}, bf16[64,640]{1,0:T(8,128)(2,1)S(1)}, u32[]{:S(2)}, u32[]{:S(2)}) collective-permute-start(bf16[64,640]{1,0:T(8,128)(2,1)S(1)} %copy-done.52), channel_id=1, source_target_pairs={{0,16},{4,20},{8,24},{12,28},{16,0},{20,4},{24,8},{28,12},{1,17},{... | collective-permute-start | bytes 245768 | tf_op jit(solution)/shard_map/ppermute | solution.py:331
  243.1 14.7 %collective-permute-start.31 = (bf16[128,2304]{1,0:T(8,128)(2,1)S(1)}, bf16[128,2304]{1,0:T(8,128)(2,1)S(1)}, u32[]{:S(2)}, u32[]{:S(2)}) collective-permute-start(bf16[128,2304]{1,0:T(8,128)(2,1)S(1)} %get-tuple-element.41), channel_id=1, source_target_pairs={{0,4},{4,0},{8,12},{12,8},{16,20},{20,16},{24,28},{28,24},{1,5},{5... | collective-permute-start | bytes 1769480 | tf_op jit(solution)/shard_map/ppermute | solution.py:331
  257.8 13.7 %collective-permute-start.43 = (bf16[128,2304]{1,0:T(8,128)(2,1)S(1)}, bf16[128,2304]{1,0:T(8,128)(2,1)S(1)}, u32[]{:S(2)}, u32[]{:S(2)}) collective-permute-start(bf16[128,2304]{1,0:T(8,128)(2,1)S(1)} %get-tuple-element.43), channel_id=1, source_target_pairs={{0,2},{1,3},{2,0},{3,1},{4,6},{5,7},{6,4},{7,5},{8,10},{9,11},{10,... | collective-permute-start | bytes 1769480 | tf_op jit(solution)/shard_map/ppermute | solution.py:331
  285.0 47.8 %collective-permute-start.9 = (bf16[64,2304]{1,0:T(8,128)(2,1)S(1)}, bf16[64,2304]{1,0:T(8,128)(2,1)S(1)}, u32[]{:S(2)}, u32[]{:S(2)}) collective-permute-start(bf16[64,2304]{1,0:T(8,128)(2,1)S(1)} %add_convert_fusion.19.rest_8_), channel_id=1, source_target_pairs={{0,2},{1,3},{2,0},{3,1},{4,6},{5,7},{6,4},{7,5},{8,10},{9,11},{10,... | collective-permute-start | bytes 884744 | tf_op jit(solution)/shard_map/ppermute | solution.py:331
  286.7 46.1 %collective-permute-start.21 = (bf16[64,2304]{1,0:T(8,128)(2,1)S(1)}, bf16[64,2304]{1,0:T(8,128)(2,1)S(1)}, u32[]{:S(2)}, u32[]{:S(2)}) collective-permute-start(bf16[64,2304]{1,0:T(8,128)(2,1)S(1)} %add_convert_fusion.15), channel_id=1, source_target_pairs={{0,8},{4,12},{8,0},{12,4},{16,24},{20,28},{24,16},{28,20},{1,9},{5... | collective-permute-start | bytes 884744 | tf_op jit(solution)/shard_map/ppermute | solution.py:331
  287.5 45.3 %collective-permute-start.33 = (bf16[64,2304]{1,0:T(8,128)(2,1)S(1)}, bf16[64,2304]{1,0:T(8,128)(2,1)}, u32[]{:S(2)}, u32[]{:S(2)}) collective-permute-start(bf16[64,2304]{1,0:T(8,128)(2,1)S(1)} %add_convert_fusion.12), channel_id=1, source_target_pairs={{0,16},{4,20},{8,24},{12,28},{16,0},{20,4},{24,8},{28,12},{1,17},{... | collective-permute-start | bytes 884744 | tf_op jit(solution)/shard_map/ppermute | solution.py:331
  288.4 44.4 %collective-permute-start.45 = (bf16[64,2304]{1,0:T(8,128)(2,1)S(1)}, bf16[64,2304]{1,0:T(8,128)(2,1)}, u32[]{:S(2)}, u32[]{:S(2)}) collective-permute-start(bf16[64,2304]{1,0:T(8,128)(2,1)S(1)} %add_convert_fusion.9), channel_id=1, source_target_pairs={{0,24},{4,28},{8,16},{12,20},{16,8},{20,12},{24,0},{28,4},{1,25},{... | collective-permute-start | bytes 884744 | tf_op jit(solution)/shard_map/ppermute | solution.py:331
  291.2 24.6 %collective-permute-start.50 = (bf16[64,640]{1,0:T(8,128)(2,1)S(1)}, bf16[64,640]{1,0:T(8,128)(2,1)S(1)}, u32[]{:S(2)}, u32[]{:S(2)}) collective-permute-start(bf16[64,640]{1,0:T(8,128)(2,1)S(1)} %copy-done.51), channel_id=1, source_target_pairs={{0,20},{4,16},{8,28},{12,24},{16,4},{20,0},{24,12},{28,8},{1,21},{... | collective-permute-start | bytes 245768 | tf_op jit(solution)/shard_map/ppermute | solution.py:331
  (64 other events, 645.4 us)

commit v4 on v3

--- a/solution.py
+++ b/solution.py
@@ -229,96 +229,121 @@
     return place
 
 
-def chunk_kernel(local, pieces, rows, tokens, parts, waits, first_ref, wg_ref, wu_ref, wd_ref, *rest):
+def chunk_kernel(local, pieces, waits, first_ref, wg_hbm, wu_hbm, wd_hbm, *rest):
     piece_refs = rest[:pieces]
-    keep_ref, send_ref, chosen_ref, weight_ref, sum_ref, y_ref = rest[pieces + waits :]
-    le = pl.program_id(0)
-    part = pl.program_id(1)
-    rows_dev = tokens // pieces
-    width = wd_ref.shape[2]
-
-    @pl.when(part == 0)
-    def _():
-        base = (first_ref[0] + le) * CAP
-        facts = jnp.concatenate([p[:, width:] for p in piece_refs], axis=0)
-        unit = lax.broadcasted_iota(jnp.int32, (8, 128), 0) == lax.broadcasted_iota(jnp.int32, (8, 128), 1)
-        facts = dot_t(unit.astype(jnp.float32).astype(jnp.bfloat16), facts)
-        shift = lax.broadcasted_iota(jnp.int32, (1, tokens), 1) // rows_dev * CAP
-        row_id = lax.broadcasted_iota(jnp.int32, (rows, tokens), 0)
-        pick, weights = None, None
-        for j in range(2):
-            hit = row_id == places_of([facts[j : j + 1]], base, shift)
-            gate = facts[2 + j : 3 + j] + facts[4 + j : 5 + j] + facts[6 + j : 7 + j]
-            weight = jnp.where(hit, gate, 0.0)
-            pick = hit if pick is None else pick | hit
-            weights = weight if weights is None else weights + weight
-        weight_ref[...] = jnp.sum(weights, axis=1, keepdims=True)
-        pick = pick.astype(jnp.float32).astype(jnp.bfloat16)
-        x = jnp.concatenate([p[:, :width] for p in piece_refs], axis=0)
-        chosen = jnp.dot(pick, x, preferred_element_type=jnp.float32)
-        chosen_ref[...] = chosen.T.astype(jnp.bfloat16)
-
-    chosen = chosen_ref[...]
-    gate = jnp.dot(wg_ref[0], chosen, preferred_element_type=jnp.float32)
-    upper = jnp.dot(wu_ref[0], chosen, preferred_element_type=jnp.float32)
-    hidden = (gate / (1.0 + jnp.exp(-gate)) * upper).T.astype(jnp.bfloat16)
-    y = jnp.dot(hidden, wd_ref[0], preferred_element_type=jnp.float32)
-
-    @pl.when(part == 0)
-    def _():
-        sum_ref[...] = y
-
-    @pl.when((part > 0) & (part < parts - 1))
-    def _():
-        sum_ref[...] += y
-
-    @pl.when(part == parts - 1)
-    def _():
-        here = pl.ds(pl.multiple_of(le * rows, rows), rows)
-        y_ref[here, :] = ((sum_ref[...] + y) * weight_ref[...]).astype(jnp.bfloat16)
-
-    @pl.when((part == parts - 1) & (le == local - 1))
-    def _():
-        facts = jnp.concatenate([p[:, width:] for p in piece_refs], axis=0).astype(jnp.float32)
-        shift = lax.broadcasted_iota(jnp.int32, (tokens, 1), 0) // rows_dev * CAP
-        lane = lax.broadcasted_iota(jnp.int32, (tokens, local * rows), 1)
+    keep_hbm, send_hbm, x, wg, wu, wd, rows_of, y, out, piece_sem, weight_sem, out_sem = rest[pieces + waits :]
+    rows_dev = piece_refs[0].shape[0]
+    width = wd.shape[2]
+    groups = pieces // 4
+    tokens = 4 * rows_dev
+    rows = 4 * CAP
+    piece_copies = [
+        pltpu.make_async_copy(ref, x.at[pl.ds(i * rows_dev, rows_dev), :], piece_sem.at[i])
+        for i, ref in enumerate(piece_refs)
+    ]
+    weight_copies = [
+        [
+            pltpu.make_async_copy(source.at[e], target.at[e], weight_sem.at[3 * e + i])
+            for i, (source, target) in enumerate(((wg_hbm, wg), (wu_hbm, wu), (wd_hbm, wd)))
+        ]
+        for e in range(local)
+    ]
+    for copy in piece_copies:
+        copy.start()
+    for copies in weight_copies:
+        for copy in copies:
+            copy.start()
+
+    unit = lax.broadcasted_iota(jnp.int32, (8, 128), 0) == lax.broadcasted_iota(jnp.int32, (8, 128), 1)
+    unit = unit.astype(jnp.float32).astype(jnp.bfloat16)
+    shift = lax.broadcasted_iota(jnp.int32, (1, tokens), 1) // rows_dev * CAP
+    row_id = lax.broadcasted_iota(jnp.int32, (rows, tokens), 0)
+    weights = [[] for _ in range(local)]
+    for g in range(groups):
+        for copy in piece_copies[4 * g : 4 * g + 4]:
+            copy.wait()
+        here = slice(g * tokens, (g + 1) * tokens)
+        facts = dot_t(unit, x[here, width:])
+        picks = []
+        for e in range(local):
+            base = (first_ref[0] + e) * CAP
+            pick, weight = None, None
+            for j in range(2):
+                hit = row_id == places_of([facts[j : j + 1]], base, shift)
+                gate = facts[2 + j : 3 + j] + facts[4 + j : 5 + j] + facts[6 + j : 7 + j]
+                gate = jnp.where(hit, gate, 0.0)
+                pick = hit if pick is None else pick | hit
+                weight = gate if weight is None else weight + gate
+            picks.append(pick.astype(jnp.float32))
+            weights[e].append(jnp.sum(weight, axis=1, keepdims=True))
+        picks = jnp.concatenate(picks, axis=0).astype(jnp.bfloat16)
+        chosen = jnp.dot(picks, x[here, :width], preferred_element_type=jnp.float32)
+        for e in range(local):
+            rows_of[e, g * rows : (g + 1) * rows, :] = chosen[e * rows : (e + 1) * rows].astype(jnp.bfloat16)
+
+    for e in range(local):
+        chosen = rows_of[e].T
+        weight_copies[e][0].wait()
+        gate = jnp.dot(wg[e], chosen, preferred_element_type=jnp.float32)
+        weight_copies[e][1].wait()
+        upper = jnp.dot(wu[e], chosen, preferred_element_type=jnp.float32)
+        hidden = (gate / (1.0 + jnp.exp(-gate)) * upper).T.astype(jnp.bfloat16)
+        weight_copies[e][2].wait()
+        result = jnp.dot(hidden, wd[e], preferred_element_type=jnp.float32)
+        result = (result * jnp.concatenate(weights[e], axis=0)).astype(jnp.bfloat16)
+        for g in range(groups):
+            y[g, e * rows : (e + 1) * rows, :] = result[g * rows : (g + 1) * rows]
+
+    shift = lax.broadcasted_iota(jnp.int32, (tokens, 1), 0) // rows_dev * CAP
+    lane = lax.broadcasted_iota(jnp.int32, (tokens, local * rows), 1)
+    out_copies = []
+    for g in reversed(range(groups)):
+        here = slice(g * tokens, (g + 1) * tokens)
+        facts = x[here, width:].astype(jnp.float32)
         put = None
         for e in range(local):
             base = (first_ref[0] + e) * CAP
             hit = lane == places_of([facts[:, j : j + 1] for j in range(2)], base, shift + e * rows)
             put = hit if put is None else put | hit
         put = put.astype(jnp.float32).astype(jnp.bfloat16)
-        half = tokens // 2
-        keep_ref[...] = jnp.dot(put[:half], y_ref[...], preferred_element_type=jnp.float32).astype(jnp.bfloat16)
-        send_ref[...] = jnp.dot(put[half:], y_ref[...], preferred_element_type=jnp.float32).astype(jnp.bfloat16)
+        out[here, :] = jnp.dot(put, y[g], preferred_element_type=jnp.float32).astype(jnp.bfloat16)
+        target, at = (keep_hbm, g) if g < groups // 2 else (send_hbm, g - groups // 2)
+        copy = pltpu.make_async_copy(
+            out.at[pl.ds(g * tokens, tokens), :], target.at[pl.ds(at * tokens, tokens), :], out_sem.at[g]
+        )
+        copy.start()
+        out_copies.append(copy)
+    for copy in out_copies:
+        copy.wait()
 
 
 def chunk_experts(pieces, w_gate, w_up, w_down, first, waits):
     local, hidden, width = w_gate.shape
-    rows_dev = pieces[0].shape[0]
+    rows_dev, wide = pieces[0].shape
     tokens = rows_dev * len(pieces)
     rows = len(pieces) * CAP
-    parts = 3
-    step = hidden // parts
-    whole = lambda e, f: (0, 0)
-    weights = pl.BlockSpec((1, step, width), lambda e, f: (e, f, 0))
-    piece = pl.BlockSpec(pieces[0].shape, whole)
+    groups = len(pieces) // 4
     half = jax.ShapeDtypeStruct((tokens // 2, width), jnp.bfloat16)
+    anywhere = pl.BlockSpec(memory_space=pl.ANY)
+    weights = pltpu.VMEM((local, hidden, width), jnp.bfloat16)
     return pl.pallas_call(
-        functools.partial(chunk_kernel, local, len(pieces), rows, tokens, parts, len(waits)),
+        functools.partial(chunk_kernel, local, len(pieces), len(waits)),
         out_shape=(half, half),
-        grid=(local, parts),
-        in_specs=[pl.BlockSpec(memory_space=pltpu.SMEM), weights, weights, weights]
-        + [piece] * len(pieces)
-        + [pl.BlockSpec(memory_space=pl.ANY)] * len(waits),
-        out_specs=(pl.BlockSpec(half.shape, whole), pl.BlockSpec(half.shape, whole)),
+        in_specs=[pl.BlockSpec(memory_space=pltpu.SMEM)] + [anywhere] * (3 + len(pieces) + len(waits)),
+        out_specs=(anywhere, anywhere),
         scratch_shapes=[
-            pltpu.VMEM((width, rows), jnp.bfloat16),
-            pltpu.VMEM((rows, 1), jnp.float32),
-            pltpu.VMEM((rows, width), jnp.float32),
-            pltpu.VMEM((local * rows, width), jnp.bfloat16),
+            pltpu.VMEM((tokens, wide), jnp.bfloat16),
+            weights,
+            weights,
+            weights,
+            pltpu.VMEM((local, rows, width), jnp.bfloat16),
+            pltpu.VMEM((groups, local * rows // groups, width), jnp.bfloat16),
+            pltpu.VMEM((tokens, width), jnp.bfloat16),
+            pltpu.SemaphoreType.DMA((len(pieces),)),
+            pltpu.SemaphoreType.DMA((3 * local,)),
+            pltpu.SemaphoreType.DMA((groups,)),
         ],
-        compiler_params=pltpu.CompilerParams(vmem_limit_bytes=32 * 1024 * 1024),
+        compiler_params=pltpu.CompilerParams(vmem_limit_bytes=58 * 1024 * 1024),
         cost_estimate=pl.CostEstimate(
             flops=6 * local * rows * width * hidden,
             bytes_accessed=6 * local * width * hidden + 4 * tokens * width,
@@ -331,59 +356,65 @@
     return lax.ppermute(a, axis, [(i, i ^ distance) for i in range(size)])
 
 
-def add(a, b):
-    return (a.astype(jnp.float32) + b.astype(jnp.float32)).astype(jnp.bfloat16)
+def fold_kernel(groups, count, waits, keep_ref, *rest):
+    got_refs, (kept_ref, *send_refs) = rest[:count], rest[count + waits :]
+    got = jnp.concatenate([r[...] for r in got_refs], axis=0) if count > 1 else got_refs[0][...]
+    total = (keep_ref[...].astype(jnp.float32) + got.astype(jnp.float32)).astype(jnp.bfloat16)
+    part = total.shape[0] // (2 * groups)
+    for i in range(groups):
+        kept_ref[i * part : (i + 1) * part, :] = total[2 * i * part : (2 * i + 1) * part]
+        send_refs[i][...] = total[(2 * i + 1) * part : (2 * i + 2) * part]
+
+
+def fold(keep, gots, groups, waits=()):
+    rows, width = keep.shape
+    part = rows // (2 * groups)
+    steps = 3 if width % (3 * 128) == 0 else 1
+    block = lambda n: pl.BlockSpec((n, width // steps), lambda i: (0, i))
+    shape = lambda n: jax.ShapeDtypeStruct((n, width), jnp.bfloat16)
+    out = pl.pallas_call(
+        functools.partial(fold_kernel, groups, len(gots), len(waits)),
+        out_shape=(shape(groups * part),) + (shape(part),) * groups,
+        grid=(steps,),
+        in_specs=[block(rows)]
+        + [block(g.shape[0]) for g in gots]
+        + [pl.BlockSpec(memory_space=pl.ANY)] * len(waits),
+        out_specs=(block(groups * part),) + (block(part),) * groups,
+        compiler_params=pltpu.CompilerParams(vmem_limit_bytes=58 * 1024 * 1024),
+        cost_estimate=pl.CostEstimate(flops=rows * width, bytes_accessed=6 * rows * width, transcendentals=0),
+    )(keep, *gots, *waits)
+    return out[0], out[1:]
 
 
 def exchange_experts(piece, w_gate, w_up, w_down, first, n_seq, n_exp, late_work):
-    one = piece.shape[0]
-    two = 2 * one
-    over = {
-        "x": lambda a: swap(a, "seq", n_seq, 1),
-        "y": lambda a: swap(a, "exp", n_exp, 2),
-        "c": lambda a: swap(a, "exp", n_exp, 1),
-    }
-    depth = n_seq // 2
-    axes = [("x", "y") if k % 2 == 0 else ("y", "x") for k in range(depth)]
-    starts = [piece] + [swap(piece, "seq", n_seq, 2 * k) for k in range(1, depth)]
-    gathered = []
-    for k, (f, g) in enumerate(axes):
-        by_f, by_g = over[f](starts[k]), over[g](starts[k])
-        near = [starts[k], by_g, by_f, over[g](by_f)]
-        gathered.append(near + [over["c"](p) for p in near])
-
-    kept, sent, lag = [None] * depth, [None] * depth, [None] * depth
-
-    def after_core(k):
-        got = over["c"](sent[k])
-        kept[k], sent[k] = add(kept[k][:two], got[:two]), add(kept[k][two:], got[two:])
-
-    def after_first(k):
-        got = over[axes[k][0]](sent[k])
-        kept[k], sent[k] = add(kept[k][:one], got[:one]), add(kept[k][one:], got[one:])
-
-    def after_second(k):
-        done = add(kept[k], over[axes[k][1]](sent[k]))
-        kept[k] = swap(done, "seq", n_seq, 2 * k) if k else done
-
-    steps = [after_core, after_first, after_second]
-    other = None
-    for turn in range(depth + len(steps)):
-        for late, stage in enumerate(steps):
-            k = turn - 2 - late
-            if 0 <= k < depth:
-                stage(k)
-        if turn < depth:
-            waits = [sent[k] for k in range(max(turn - 3, 0), turn - 1)]
-            kept[turn], sent[turn] = chunk_experts(gathered[turn], w_gate, w_up, w_down, first, waits)
-        if turn == 1:
-            other = late_work(sent[0])
-    for late, stage in enumerate(steps):
-        for k in range(depth):
-            if depth + len(steps) - 1 - 2 - late < k:
-                stage(k)
-    mixture = sum(k.astype(jnp.float32) for k in kept)
-    return mixture, other
+    x = lambda a: swap(a, "seq", n_seq, 1)
+    y = lambda a: swap(a, "exp", n_exp, 2)
+    core = lambda a: swap(a, "exp", n_exp, 1)
+    z = lambda a, k: swap(a, "seq", n_seq, 2 * k)
+    starts = [piece] + [z(piece, k) for k in range(1, 4)]
+
+    def gather(k):
+        near = []
+        for start, (f, g) in ((starts[k], (x, y)), (starts[k + 1], (y, x))):
+            by_f = f(start)
+            near += [start, g(start), by_f, g(by_f)]
+        return near + [core(p) for p in near]
+
+    experts_of = lambda pieces, waits: chunk_experts(pieces, w_gate, w_up, w_down, first, waits)
+    keep_a, send_a = experts_of(gather(0), [])
+    keep_a, (fx_a, fy_a) = fold(keep_a, [core(send_a)], 2)
+    keep_b, send_b = experts_of(gather(2), [fx_a])
+    got_b = core(send_b)
+    other = late_work(send_b)
+    keep_a, (gy_a, gx_a) = fold(keep_a, [x(fx_a), y(fy_a)], 2)
+    keep_b, (fx_b, fy_b) = fold(keep_b, [got_b], 2, [gy_a])
+    keep_a, (z_a,) = fold(keep_a, [y(gy_a), x(gx_a)], 1)
+    keep_b, (gy_b, gx_b) = fold(keep_b, [x(fx_b), y(fy_b)], 2, [z_a, other])
+    got_a = z(z_a, 1)
+    keep_b, (z_b,) = fold(keep_b, [y(gy_b), x(gx_b)], 1)
+    mine = keep_a.astype(jnp.float32) + got_a.astype(jnp.float32)
+    over_z = (keep_b.astype(jnp.float32) + z(z_b, 1).astype(jnp.float32)).astype(jnp.bfloat16)
+    return mine + z(over_z, 2).astype(jnp.float32), other
 
 
 def body(

time: 336 us -> 312 us (0.929)
  local copies, waits for them, and re-layouts: 42.3 us -> 13.3 us
  waiting for transfers between devices: 163 us -> 148 us
  starting transfers between devices: 53.5 us -> 67 us
  Pallas kernels: 66 us -> 77.5 us
  other arithmetic: 8.74 us -> 4.32 us
    unnamed x136 -> x128, local copies, waits for them, and re-layouts: 37.9 us -> 8.79 us
    ppermute x53 -> x51, waiting for transfers between devices: 128 us -> 112 us  [swap(): return lax.ppermute(a, axis, [(i, i ^ distance) for i in range(size)])]
    ppermute x53 -> x51, starting transfers between devices: 42.4 us -> 56.1 us  [swap(): return lax.ppermute(a, axis, [(i, i ^ distance) for i in range(size)])]
    pallas_call x4 -> x8, Pallas kernels: 53.8 us -> 65.2 us  [the longest x2 43.3 us: chunk_experts(): pl.pallas_call(functools.partial(chunk_kernel, local, len(pieces), len(wa...]
  transfers between devices with their start and end apart: 55 -> 53, of which waited for: 19 -> 25; matrix products, arithmetic and copies ran while one was open for 2% -> 1% of each run, Pallas kernels for 17% -> 5%
where the time goes in v4:
time: 312 us; the launch traced here: 311 us
  waiting for transfers between devices  148 us (47%)
  Pallas kernels  77.5 us (25%)
  starting transfers between devices  67 us (21%)
  local copies, waits for them, and re-layouts  13.3 us (4%)
  other arithmetic  4.32 us (1%)
    ppermute x51, waiting for transfers between devices, swap(): return lax.ppermute(a, axis, [(i, i ^ distance) for i in range(size)])  112 us
    ppermute x51, starting transfers between devices, swap(): return lax.ppermute(a, axis, [(i, i ^ distance) for i in range(size)])  56.1 us
    pallas_call x2, Pallas kernels, chunk_experts(): pl.pallas_call(functools.partial(chunk_kernel, local, len(pieces), len(wa...  43.3 us
    all_to_all x1, waiting for transfers between devices, body(): lax.all_to_all(packed, 'seq', split_axis=0, concat_axis=0, tiled=True)  25.3 us
    pallas_call x6, Pallas kernels, fold(): pl.pallas_call(functools.partial(fold_kernel, groups, len(gots), len(wait...  22 us
    all_to_all x1, waiting for transfers between devices, body(): lax.all_to_all(context.reshape(n_seq, rows_dev, span), 'seq', split_axis=...  9.8 us
    unnamed x128, local copies, waits for them, and re-layouts  8.79 us
    all_to_all x1, starting transfers between devices, body(): lax.all_to_all(packed, 'seq', split_axis=0, concat_axis=0, tiled=True)  7.25 us
  transfers between devices with their start and end apart: 53, of which 25 were waited for; matrix products, arithmetic and copies ran while one was open for 1% of the time, Pallas kernels for 5%

profile of v4, /device:TPU:0, one launch (start us, length us, event | category | flops | bytes accessed | tf_op | source)
XLA Modules:
  0.0 311.0 jit_solution(6187343506144961300)
XLA Ops:
  0.6 2.3 fusion.3
  5.7 7.3 %all-to-all-start = ((bf16[8,64,960]{2,1,0:T(8,128)(2,1)}), bf16[8,64,960]{2,1,0:T(8,128)(2,1)S(1)}, u32[]{:S(2)}, u32[]{:S(2)}) async-start(bf16[8,64,960]{2,1,0:T(8,128)(2,1)} %pad_maximum_fusion), calls=%async_computation | async-start | bytes 2097152 | tf_op jit(solution)/shard_map/all_to_all | solution.py:452
  13.4 25.3 %all-to-all-done = bf16[8,64,960]{2,1,0:T(8,128)(2,1)S(1)} async-done(((bf16[8,64,960]{2,1,0:T(8,128)(2,1)}), bf16[8,64,960]{2,1,0:T(8,128)(2,1)S(1)}, u32[]{:S(2)}, u32[]{:S(2)}) %all-to-all-start) | async-done | bytes 983072 | tf_op jit(solution)/shard_map/all_to_all | solution.py:452
  38.7 5.6 %shard_map.122 = bf16[512,320]{1,0:T(8,128)(2,1)} custom-call(bf16[512,960]{1,0:T(8,128)(2,1)S(1)} %bitcast.118, s32[1,512]{1,0:T(1,128)S(1)} %copy-done.1, s32[512,1]{1,0:T(8,128)S(1)} %copy.35.seg_col_ref), custom_call_target="tpu_custom_call" | custom-call | flops 335544320 | bytes 1310720 | tf_op jit(solution)/shard_map/pallas_call | solution.py:55
  44.3 3.6 %all-to-all-start.1 = ((bf16[8,64,320]{2,1,0:T(8,128)(2,1)}), bf16[8,64,320]{2,1,0:T(8,128)(2,1)S(1)}, u32[]{:S(2)}, u32[]{:S(2)}) async-start(bf16[8,64,320]{2,1,0:T(8,128)(2,1)} %bitcast.29), calls=%async_computation.1 | async-start | bytes 786432 | tf_op jit(solution)/shard_map/all_to_all | solution.py:455
  50.0 9.8 %all-to-all-done.1.context_ref = bf16[8,64,320]{2,1,0:T(8,128)(2,1)S(1)} async-done(((bf16[8,64,320]{2,1,0:T(8,128)(2,1)}), bf16[8,64,320]{2,1,0:T(8,128)(2,1)S(1)}, u32[]{:S(2)}, u32[]{:S(2)}) %all-to-all-start.1) | async-done | bytes 327712 | tf_op jit(solution)/shard_map/all_to_all | solution.py:455
  60.5 2.2 shard_map.123
  64.2 1.5 collective-permute-start
  65.7 4.1 %collective-permute-done.3.rest_4_ = bf16[64,2432]{1,0:T(8,128)(2,1)S(1)} collective-permute-done((bf16[64,2432]{1,0:T(8,128)(2,1)}, bf16[64,2432]{1,0:T(8,128)(2,1)S(1)}, u32[]{:S(2)}, u32[]{:S(2)}) %collective-permute-start.3) | collective-permute-done | bytes 311328 | tf_op jit(solution)/shard_map/ppermute | solution.py:356
  69.8 1.5 collective-permute-start.5
  71.4 2.9 collective-permute-start.4
  75.3 6.1 %collective-permute-done.5.rest_6_ = bf16[64,2432]{1,0:T(8,128)(2,1)S(1)} collective-permute-done((bf16[64,2432]{1,0:T(8,128)(2,1)S(1)}, bf16[64,2432]{1,0:T(8,128)(2,1)S(1)}, u32[]{:S(2)}, u32[]{:S(2)}) %collective-permute-start.5) | collective-permute-done | bytes 311328 | tf_op jit(solution)/shard_map/ppermute | solution.py:356
  81.4 1.7 collective-permute-start.6
  83.1 2.8 collective-permute-done.2.rest_3_
  86.4 2.0 collective-permute-done.6.rest_7_
  88.4 1.9 collective-permute-done.14.rest_15_
  90.4 21.6 %shard_map.124 = (bf16[512,2304]{1,0:T(8,128)(2,1)}, bf16[512,2304]{1,0:T(8,128)(2,1)}) custom-call(s32[1]{0:T(128)} %bitcast.33.first_ref, bf16[2,720,2304]{2,1,0:T(8,128)(2,1)} %bitcast.132, bf16[2,720,2304]{2,1,0:T(8,128)(2,1)} %bitcast.134, bf16[2,720,2304]{2,1,0:T(8,128)(2,1)} %wd_hbm.3, bf16[64,2432]{1,0:T(8,128)(2,1)} %get-tuple-element.33.rest_0_, ...), custom_call_target="tpu_custom_call" | custom-call | flops 7644119040 | bytes 29343744 | tf_op jit(solution)/shard_map/pallas_call | solution.py:329
  112.4 1.7 collective-permute-start.21
  114.2 2.7 collective-permute-start.25
  116.8 20.0 %collective-permute-done.21.rest_0_ = bf16[64,2432]{1,0:T(8,128)(2,1)S(1)} collective-permute-done((bf16[64,2432]{1,0:T(8,128)(2,1)S(1)}, bf16[64,2432]{1,0:T(8,128)(2,1)S(1)}, u32[]{:S(2)}, u32[]{:S(2)}) %collective-permute-start.21) | collective-permute-done | bytes 311328 | tf_op jit(solution)/shard_map/ppermute | solution.py:356
  137.9 1.5 collective-permute-start.27
  140.9 6.2 %collective-permute-done.23.rest_2_ = bf16[64,2432]{1,0:T(8,128)(2,1)S(1)} collective-permute-done((bf16[64,2432]{1,0:T(8,128)(2,1)S(1)}, bf16[64,2432]{1,0:T(8,128)(2,1)S(1)}, u32[]{:S(2)}, u32[]{:S(2)}) %collective-permute-start.23) | collective-permute-done | bytes 311328 | tf_op jit(solution)/shard_map/ppermute | solution.py:356
  148.1 5.4 %collective-permute-done.22.rest_1_ = bf16[64,2432]{1,0:T(8,128)(2,1)S(1)} collective-permute-done((bf16[64,2432]{1,0:T(8,128)(2,1)S(1)}, bf16[64,2432]{1,0:T(8,128)(2,1)S(1)}, u32[]{:S(2)}, u32[]{:S(2)}) %collective-permute-start.22) | collective-permute-done | bytes 311328 | tf_op jit(solution)/shard_map/ppermute | solution.py:356
  155.9 5.7 %collective-permute-done.24.rest_3_ = bf16[64,2432]{1,0:T(8,128)(2,1)S(1)} collective-permute-done((bf16[64,2432]{1,0:T(8,128)(2,1)S(1)}, bf16[64,2432]{1,0:T(8,128)(2,1)S(1)}, u32[]{:S(2)}, u32[]{:S(2)}) %collective-permute-start.24) | collective-permute-done | bytes 311328 | tf_op jit(solution)/shard_map/ppermute | solution.py:356
  164.8 4.5 %shard_map.125 = (bf16[256,2304]{1,0:T(8,128)(2,1)}, bf16[128,2304]{1,0:T(8,128)(2,1)}, bf16[128,2304]{1,0:T(8,128)(2,1)}) custom-call(bf16[512,2304]{1,0:T(8,128)(2,1)} %get-tuple-element.34.keep_ref, bf16[512,2304]{1,0:T(8,128)(2,1)} %copy-done.3), custom_call_target="tpu_custom_call" | custom-call | flops 1179648 | bytes 7077888 | tf_op jit(solution)/shard_map/pallas_call | solution.py:375
  169.5 21.7 %shard_map.128 = (bf16[512,2304]{1,0:T(8,128)(2,1)}, bf16[512,2304]{1,0:T(8,128)(2,1)}) custom-call(s32[1]{0:T(128)} %bitcast.33.first_ref, bf16[2,720,2304]{2,1,0:T(8,128)(2,1)} %bitcast.133, bf16[2,720,2304]{2,1,0:T(8,128)(2,1)} %bitcast.135, bf16[2,720,2304]{2,1,0:T(8,128)(2,1)} %wd_hbm.3, bf16[64,2432]{1,0:T(8,128)(2,1)} %copy-done.31, ...), custom_call_target="tpu_custom_call" | custom-call | flops 7644119040 | bytes 29343744 | tf_op jit(solution)/shard_map/pallas_call | solution.py:329
  192.2 14.8 %collective-permute-done.16.rest_0_ = bf16[128,2304]{1,0:T(8,128)(2,1)S(1)} collective-permute-done((bf16[128,2304]{1,0:T(8,128)(2,1)S(1)}, bf16[128,2304]{1,0:T(8,128)(2,1)S(1)}, u32[]{:S(2)}, u32[]{:S(2)}) %collective-permute-start.16) | collective-permute-done | bytes 589856 | tf_op jit(solution)/shard_map/ppermute | solution.py:356
  208.0 3.4 %shard_map.126 = (bf16[128,2304]{1,0:T(8,128)(2,1)}, bf16[64,2304]{1,0:T(8,128)(2,1)}, bf16[64,2304]{1,0:T(8,128)(2,1)}) custom-call(bf16[256,2304]{1,0:T(8,128)(2,1)} %get-tuple-element.36.keep_ref, bf16[128,2304]{1,0:T(8,128)(2,1)} %copy-done.8, bf16[128,2304]{1,0:T(8,128)(2,1)} %copy-done.9), custom_call_target="tpu_custom_call" | custom-call | flops 589824 | bytes 3538944 | tf_op jit(solution)/shard_map/pallas_call | solution.py:375
  212.9 4.5 %shard_map.129 = (bf16[256,2304]{1,0:T(8,128)(2,1)}, bf16[128,2304]{1,0:T(8,128)(2,1)}, bf16[128,2304]{1,0:T(8,128)(2,1)}) custom-call(bf16[512,2304]{1,0:T(8,128)(2,1)} %get-tuple-element.44.keep_ref, bf16[512,2304]{1,0:T(8,128)(2,1)} %copy-done.2, bf16[64,2304]{1,0:T(8,128)(2,1)} %get-tuple-element.40.rest_1_), custom_call_target="tpu_custom_call" | custom-call | flops 1179648 | bytes 7077888 | tf_op jit(solution)/shard_map/pallas_call | solution.py:375
  217.4 1.6 collective-permute-start.38
  220.2 2.2 shard_map.130
  222.9 7.4 %collective-permute-start.41 = (bf16[64,640]{1,0:T(8,128)(2,1)}, bf16[64,640]{1,0:T(8,128)(2,1)S(1)}, u32[]{:S(2)}, u32[]{:S(2)}) collective-permute-start(bf16[64,640]{1,0:T(8,128)(2,1)} %get-tuple-element.51), channel_id=1, source_target_pairs={{0,8},{4,12},{8,0},{12,4},{16,24},{20,28},{24,16},{28,20},{1,9},{5... | collective-permute-start | bytes 245768 | tf_op jit(solution)/shard_map/ppermute | solution.py:356
  230.3 5.7 %collective-permute-done.40.refs_1_ = bf16[64,640]{1,0:T(8,128)(2,1)S(1)} collective-permute-done((bf16[64,640]{1,0:T(8,128)(2,1)}, bf16[64,640]{1,0:T(8,128)(2,1)S(1)}, u32[]{:S(2)}, u32[]{:S(2)}) %collective-permute-start.40) | collective-permute-done | bytes 81952 | tf_op jit(solution)/shard_map/ppermute | solution.py:356
  236.1 7.9 %collective-permute-start.43 = (bf16[64,640]{1,0:T(8,128)(2,1)}, bf16[64,640]{1,0:T(8,128)(2,1)S(1)}, u32[]{:S(2)}, u32[]{:S(2)}) collective-permute-start(bf16[64,640]{1,0:T(8,128)(2,1)} %get-tuple-element.53), channel_id=1, source_target_pairs={{0,16},{4,20},{8,24},{12,28},{16,0},{20,4},{24,8},{28,12},{1,17},{... | collective-permute-start | bytes 245768 | tf_op jit(solution)/shard_map/ppermute | solution.py:356
  246.6 3.2 %collective-permute-start.44 = (bf16[64,640]{1,0:T(8,128)(2,1)}, bf16[64,640]{1,0:T(8,128)(2,1)S(1)}, u32[]{:S(2)}, u32[]{:S(2)}) collective-permute-start(bf16[64,640]{1,0:T(8,128)(2,1)} %get-tuple-element.54), channel_id=1, source_target_pairs={{0,20},{4,16},{8,28},{12,24},{16,4},{20,0},{24,12},{28,8},{1,21},{... | collective-permute-start | bytes 245768 | tf_op jit(solution)/shard_map/ppermute | solution.py:356
  249.8 3.3 %collective-permute-done.44.refs_5_ = bf16[64,640]{1,0:T(8,128)(2,1)S(1)} collective-permute-done((bf16[64,640]{1,0:T(8,128)(2,1)}, bf16[64,640]{1,0:T(8,128)(2,1)S(1)}, u32[]{:S(2)}, u32[]{:S(2)}) %collective-permute-start.44) | collective-permute-done | bytes 81952 | tf_op jit(solution)/shard_map/ppermute | solution.py:356
  253.0 2.1 collective-permute-start.45
  255.2 4.4 %collective-permute-done.45.refs_6_ = bf16[64,640]{1,0:T(8,128)(2,1)S(1)} collective-permute-done((bf16[64,640]{1,0:T(8,128)(2,1)}, bf16[64,640]{1,0:T(8,128)(2,1)S(1)}, u32[]{:S(2)}, u32[]{:S(2)}) %collective-permute-start.45) | collective-permute-done | bytes 81952 | tf_op jit(solution)/shard_map/ppermute | solution.py:356
  259.6 2.7 collective-permute-start.46
  262.3 4.7 %collective-permute-done.46.refs_7_ = bf16[64,640]{1,0:T(8,128)(2,1)S(1)} collective-permute-done((bf16[64,640]{1,0:T(8,128)(2,1)}, bf16[64,640]{1,0:T(8,128)(2,1)S(1)}, u32[]{:S(2)}, u32[]{:S(2)}) %collective-permute-start.46) | collective-permute-done | bytes 81952 | tf_op jit(solution)/shard_map/ppermute | solution.py:356
  267.6 2.2 shard_map.131.rest_3_
  270.6 3.0 shard_map.127
  274.7 3.5 %shard_map.132 = (bf16[128,2304]{1,0:T(8,128)(2,1)}, bf16[64,2304]{1,0:T(8,128)(2,1)}, bf16[64,2304]{1,0:T(8,128)(2,1)}) custom-call(bf16[256,2304]{1,0:T(8,128)(2,1)} %get-tuple-element.46.keep_ref, bf16[128,2304]{1,0:T(8,128)(2,1)} %copy-done.6, bf16[128,2304]{1,0:T(8,128)(2,1)} %copy-done.7, bf16[64,2304]{1,0:T(8,128)(2,1)} %get-tuple-element.43.rest_2_, ...), custom_call_target="tpu_custom_call" | custom-call | flops 589824 | bytes 3538944 | tf_op jit(solution)/shard_map/pallas_call | solution.py:375
  279.8 5.3 %collective-permute-done.47.rest_0_ = bf16[64,2304]{1,0:T(8,128)(2,1)S(1)} collective-permute-done((bf16[64,2304]{1,0:T(8,128)(2,1)}, bf16[64,2304]{1,0:T(8,128)(2,1)S(1)}, u32[]{:S(2)}, u32[]{:S(2)}) %collective-permute-start.47) | collective-permute-done | bytes 294944 | tf_op jit(solution)/shard_map/ppermute | solution.py:356
  286.3 3.0 shard_map.133
  291.3 6.9 %collective-permute-done.49 = bf16[64,2304]{1,0:T(8,128)(2,1)S(1)} collective-permute-done((bf16[64,2304]{1,0:T(8,128)(2,1)}, bf16[64,2304]{1,0:T(8,128)(2,1)S(1)}, u32[]{:S(2)}, u32[]{:S(2)}) %collective-permute-start.49) | collective-permute-done | bytes 294944 | tf_op jit(solution)/shard_map/ppermute | solution.py:356
  299.3 1.9 collective-permute-start.50
  302.6 7.6 %collective-permute-done.50 = bf16[64,2304]{1,0:T(8,128)(2,1)S(1)} collective-permute-done((bf16[64,2304]{1,0:T(8,128)(2,1)S(1)}, bf16[64,2304]{1,0:T(8,128)(2,1)S(1)}, u32[]{:S(2)}, u32[]{:S(2)}) %collective-permute-start.50) | collective-permute-done | bytes 294944 | tf_op jit(solution)/shard_map/ppermute | solution.py:356
  (219 shorter events, 36.7 us)
Async XLA Ops:
  5.7 33.0 %all-to-all-start = ((bf16[8,64,960]{2,1,0:T(8,128)(2,1)}), bf16[8,64,960]{2,1,0:T(8,128)(2,1)S(1)}, u32[]{:S(2)}, u32[]{:S(2)}) async-start(bf16[8,64,960]{2,1,0:T(8,128)(2,1)} %pad_maximum_fusion), calls=%async_computation | async-start | bytes 2097152 | tf_op jit(solution)/shard_map/all_to_all | solution.py:452
  44.3 15.4 %all-to-all-start.1 = ((bf16[8,64,320]{2,1,0:T(8,128)(2,1)}), bf16[8,64,320]{2,1,0:T(8,128)(2,1)S(1)}, u32[]{:S(2)}, u32[]{:S(2)}) async-start(bf16[8,64,320]{2,1,0:T(8,128)(2,1)} %bitcast.29), calls=%async_computation.1 | async-start | bytes 786432 | tf_op jit(solution)/shard_map/all_to_all | solution.py:455
  62.7 7.1 %collective-permute-start.3 = (bf16[64,2432]{1,0:T(8,128)(2,1)}, bf16[64,2432]{1,0:T(8,128)(2,1)S(1)}, u32[]{:S(2)}, u32[]{:S(2)}) collective-permute-start(bf16[64,2432]{1,0:T(8,128)(2,1)} %get-tuple-element.33.rest_0_), channel_id=1, source_target_pairs={{0,8},{4,12},{8,0},{12,4},{16,24},{20,28},{24,16},{28,20},{1,9},{5... | collective-permute-start | bytes 933896 | tf_op jit(solution)/shard_map/ppermute | solution.py:356
  63.7 10.6 %collective-permute-start.1 = (bf16[64,2432]{1,0:T(8,128)(2,1)}, bf16[64,2432]{1,0:T(8,128)(2,1)S(1)}, u32[]{:S(2)}, u32[]{:S(2)}) collective-permute-start(bf16[64,2432]{1,0:T(8,128)(2,1)} %get-tuple-element.33.rest_0_), channel_id=1, source_target_pairs={{0,4},{4,0},{8,12},{12,8},{16,20},{20,16},{24,28},{28,24},{1,5},{5... | collective-permute-start | bytes 933896 | tf_op jit(solution)/shard_map/ppermute | solution.py:356
  64.2 10.6 %collective-permute-start = (bf16[64,2432]{1,0:T(8,128)(2,1)}, bf16[64,2432]{1,0:T(8,128)(2,1)S(1)}, u32[]{:S(2)}, u32[]{:S(2)}) collective-permute-start(bf16[64,2432]{1,0:T(8,128)(2,1)} %get-tuple-element.33.rest_0_), channel_id=1, source_target_pairs={{0,2},{1,3},{2,0},{3,1},{4,6},{5,7},{6,4},{7,5},{8,10},{9,11},{10,... | collective-permute-start | bytes 933896 | tf_op jit(solution)/shard_map/ppermute | solution.py:356
  65.7 9.1 %collective-permute-start.7 = (bf16[64,2432]{1,0:T(8,128)(2,1)}, bf16[64,2432]{1,0:T(8,128)(2,1)S(1)}, u32[]{:S(2)}, u32[]{:S(2)}) collective-permute-start(bf16[64,2432]{1,0:T(8,128)(2,1)} %get-tuple-element.33.rest_0_), channel_id=1, source_target_pairs={{0,1},{1,0},{2,3},{3,2},{4,5},{5,4},{6,7},{7,6},{8,9},{9,8},{10,11... | collective-permute-start | bytes 933896 | tf_op jit(solution)/shard_map/ppermute | solution.py:356
  69.8 11.5 %collective-permute-start.5 = (bf16[64,2432]{1,0:T(8,128)(2,1)S(1)}, bf16[64,2432]{1,0:T(8,128)(2,1)S(1)}, u32[]{:S(2)}, u32[]{:S(2)}) collective-permute-start(bf16[64,2432]{1,0:T(8,128)(2,1)S(1)} %collective-permute-done.3.rest_4_), channel_id=1, source_target_pairs={{0,2},{1,3},{2,0},{3,1},{4,6},{5,7},{6,4},{7,5},{8,10},{9,11},{10,... | collective-permute-start | bytes 933896 | tf_op jit(solution)/shard_map/ppermute | solution.py:356
  71.4 11.7 %collective-permute-start.4 = (bf16[64,2432]{1,0:T(8,128)(2,1)S(1)}, bf16[64,2432]{1,0:T(8,128)(2,1)S(1)}, u32[]{:S(2)}, u32[]{:S(2)}) collective-permute-start(bf16[64,2432]{1,0:T(8,128)(2,1)S(1)} %collective-permute-done.3.rest_4_), channel_id=1, source_target_pairs={{0,4},{4,0},{8,12},{12,8},{16,20},{20,16},{24,28},{28,24},{1,5},{5... | collective-permute-start | bytes 933896 | tf_op jit(solution)/shard_map/ppermute | solution.py:356
  74.3 11.5 %collective-permute-start.2 = (bf16[64,2432]{1,0:T(8,128)(2,1)S(1)}, bf16[64,2432]{1,0:T(8,128)(2,1)S(1)}, u32[]{:S(2)}, u32[]{:S(2)}) collective-permute-start(bf16[64,2432]{1,0:T(8,128)(2,1)S(1)} %collective-permute-done.1.rest_2_), channel_id=1, source_target_pairs={{0,2},{1,3},{2,0},{3,1},{4,6},{5,7},{6,4},{7,5},{8,10},{9,11},{10,... | collective-permute-start | bytes 933896 | tf_op jit(solution)/shard_map/ppermute | solution.py:356
  74.8 11.0 %collective-permute-start.11 = (bf16[64,2432]{1,0:T(8,128)(2,1)S(1)}, bf16[64,2432]{1,0:T(8,128)(2,1)S(1)}, u32[]{:S(2)}, u32[]{:S(2)}) collective-permute-start(bf16[64,2432]{1,0:T(8,128)(2,1)S(1)} %collective-permute-done.3.rest_4_), channel_id=1, source_target_pairs={{0,1},{1,0},{2,3},{3,2},{4,5},{5,4},{6,7},{7,6},{8,9},{9,8},{10,11... | collective-permute-start | bytes 933896 | tf_op jit(solution)/shard_map/ppermute | solution.py:356
  74.8 11.5 %collective-permute-start.9 = (bf16[64,2432]{1,0:T(8,128)(2,1)S(1)}, bf16[64,2432]{1,0:T(8,128)(2,1)S(1)}, u32[]{:S(2)}, u32[]{:S(2)}) collective-permute-start(bf16[64,2432]{1,0:T(8,128)(2,1)S(1)} %collective-permute-done.1.rest_2_), channel_id=1, source_target_pairs={{0,1},{1,0},{2,3},{3,2},{4,5},{5,4},{6,7},{7,6},{8,9},{9,8},{10,11... | collective-permute-start | bytes 933896 | tf_op jit(solution)/shard_map/ppermute | solution.py:356
  81.4 7.0 %collective-permute-start.6 = (bf16[64,2432]{1,0:T(8,128)(2,1)S(1)}, bf16[64,2432]{1,0:T(8,128)(2,1)}, u32[]{:S(2)}, u32[]{:S(2)}) collective-permute-start(bf16[64,2432]{1,0:T(8,128)(2,1)S(1)} %collective-permute-done.5.rest_6_), channel_id=1, source_target_pairs={{0,4},{4,0},{8,12},{12,8},{16,20},{20,16},{24,28},{28,24},{1,5},{5... | collective-permute-start | bytes 933896 | tf_op jit(solution)/shard_map/ppermute | solution.py:356
  112.0 51.3 %collective-permute-start.15 = (bf16[512,2304]{1,0:T(8,128)(2,1)}, bf16[512,2304]{1,0:T(8,128)(2,1)S(1)}, u32[]{:S(2)}, u32[]{:S(2)}) collective-permute-start(bf16[512,2304]{1,0:T(8,128)(2,1)} %get-tuple-element.35), channel_id=1, source_target_pairs={{0,1},{1,0},{2,3},{3,2},{4,5},{5,4},{6,7},{7,6},{8,9},{9,8},{10,11... | collective-permute-start | bytes 7077896 | tf_op jit(solution)/shard_map/ppermute | solution.py:356
  112.4 24.4 %collective-permute-start.21 = (bf16[64,2432]{1,0:T(8,128)(2,1)S(1)}, bf16[64,2432]{1,0:T(8,128)(2,1)S(1)}, u32[]{:S(2)}, u32[]{:S(2)}) collective-permute-start(bf16[64,2432]{1,0:T(8,128)(2,1)S(1)} %copy-done.30), channel_id=1, source_target_pairs={{0,16},{4,20},{8,24},{12,28},{16,0},{20,4},{24,8},{28,12},{1,17},{... | collective-permute-start | bytes 933896 | tf_op jit(solution)/shard_map/ppermute | solution.py:356
  114.2 23.7 %collective-permute-start.25 = (bf16[64,2432]{1,0:T(8,128)(2,1)S(1)}, bf16[64,2432]{1,0:T(8,128)(2,1)S(1)}, u32[]{:S(2)}, u32[]{:S(2)}) collective-permute-start(bf16[64,2432]{1,0:T(8,128)(2,1)S(1)} %copy-done.30), channel_id=1, source_target_pairs={{0,24},{4,28},{8,16},{12,20},{16,8},{20,12},{24,0},{28,4},{1,25},{... | collective-permute-start | bytes 933896 | tf_op jit(solution)/shard_map/ppermute | solution.py:356
  136.9 10.3 %collective-permute-start.23 = (bf16[64,2432]{1,0:T(8,128)(2,1)S(1)}, bf16[64,2432]{1,0:T(8,128)(2,1)S(1)}, u32[]{:S(2)}, u32[]{:S(2)}) collective-permute-start(bf16[64,2432]{1,0:T(8,128)(2,1)S(1)} %collective-permute-done.21.rest_0_), channel_id=1, source_target_pairs={{0,4},{4,0},{8,12},{12,8},{16,20},{20,16},{24,28},{28,24},{1,5},{5... | collective-permute-start | bytes 933896 | tf_op jit(solution)/shard_map/ppermute | solution.py:356
  137.9 10.3 %collective-permute-start.27 = (bf16[64,2432]{1,0:T(8,128)(2,1)S(1)}, bf16[64,2432]{1,0:T(8,128)(2,1)S(1)}, u32[]{:S(2)}, u32[]{:S(2)}) collective-permute-start(bf16[64,2432]{1,0:T(8,128)(2,1)S(1)} %collective-permute-done.25.rest_4_), channel_id=1, source_target_pairs={{0,2},{1,3},{2,0},{3,1},{4,6},{5,7},{6,4},{7,5},{8,10},{9,11},{10,... | collective-permute-start | bytes 933896 | tf_op jit(solution)/shard_map/ppermute | solution.py:356
  139.4 14.1 %collective-permute-start.22 = (bf16[64,2432]{1,0:T(8,128)(2,1)S(1)}, bf16[64,2432]{1,0:T(8,128)(2,1)S(1)}, u32[]{:S(2)}, u32[]{:S(2)}) collective-permute-start(bf16[64,2432]{1,0:T(8,128)(2,1)S(1)} %collective-permute-done.21.rest_0_), channel_id=1, source_target_pairs={{0,2},{1,3},{2,0},{3,1},{4,6},{5,7},{6,4},{7,5},{8,10},{9,11},{10,... | collective-permute-start | bytes 933896 | tf_op jit(solution)/shard_map/ppermute | solution.py:356
  139.9 15.2 %collective-permute-start.26 = (bf16[64,2432]{1,0:T(8,128)(2,1)S(1)}, bf16[64,2432]{1,0:T(8,128)(2,1)S(1)}, u32[]{:S(2)}, u32[]{:S(2)}) collective-permute-start(bf16[64,2432]{1,0:T(8,128)(2,1)S(1)} %collective-permute-done.25.rest_4_), channel_id=1, source_target_pairs={{0,4},{4,0},{8,12},{12,8},{16,20},{20,16},{24,28},{28,24},{1,5},{5... | collective-permute-start | bytes 933896 | tf_op jit(solution)/shard_map/ppermute | solution.py:356
  147.2 8.2 %collective-permute-start.29 = (bf16[64,2432]{1,0:T(8,128)(2,1)S(1)}, bf16[64,2432]{1,0:T(8,128)(2,1)S(1)}, u32[]{:S(2)}, u32[]{:S(2)}) collective-permute-start(bf16[64,2432]{1,0:T(8,128)(2,1)S(1)} %collective-permute-done.21.rest_0_), channel_id=1, source_target_pairs={{0,1},{1,0},{2,3},{3,2},{4,5},{5,4},{6,7},{7,6},{8,9},{9,8},{10,11... | collective-permute-start | bytes 933896 | tf_op jit(solution)/shard_map/ppermute | solution.py:356
  148.1 7.3 %collective-permute-start.33 = (bf16[64,2432]{1,0:T(8,128)(2,1)S(1)}, bf16[64,2432]{1,0:T(8,128)(2,1)S(1)}, u32[]{:S(2)}, u32[]{:S(2)}) collective-permute-start(bf16[64,2432]{1,0:T(8,128)(2,1)S(1)} %collective-permute-done.25.rest_4_), channel_id=1, source_target_pairs={{0,1},{1,0},{2,3},{3,2},{4,5},{5,4},{6,7},{7,6},{8,9},{9,8},{10,11... | collective-permute-start | bytes 933896 | tf_op jit(solution)/shard_map/ppermute | solution.py:356
  153.5 8.1 %collective-permute-start.24 = (bf16[64,2432]{1,0:T(8,128)(2,1)S(1)}, bf16[64,2432]{1,0:T(8,128)(2,1)S(1)}, u32[]{:S(2)}, u32[]{:S(2)}) collective-permute-start(bf16[64,2432]{1,0:T(8,128)(2,1)S(1)} %collective-permute-done.23.rest_2_), channel_id=1, source_target_pairs={{0,2},{1,3},{2,0},{3,1},{4,6},{5,7},{6,4},{7,5},{8,10},{9,11},{10,... | collective-permute-start | bytes 933896 | tf_op jit(solution)/shard_map/ppermute | solution.py:356
  155.0 7.8 %collective-permute-start.28 = (bf16[64,2432]{1,0:T(8,128)(2,1)S(1)}, bf16[64,2432]{1,0:T(8,128)(2,1)S(1)}, u32[]{:S(2)}, u32[]{:S(2)}) collective-permute-start(bf16[64,2432]{1,0:T(8,128)(2,1)S(1)} %collective-permute-done.27.rest_6_), channel_id=1, source_target_pairs={{0,4},{4,0},{8,12},{12,8},{16,20},{20,16},{24,28},{28,24},{1,5},{5... | collective-permute-start | bytes 933896 | tf_op jit(solution)/shard_map/ppermute | solution.py:356
  155.4 7.5 %collective-permute-start.31 = (bf16[64,2432]{1,0:T(8,128)(2,1)S(1)}, bf16[64,2432]{1,0:T(8,128)(2,1)S(1)}, u32[]{:S(2)}, u32[]{:S(2)}) collective-permute-start(bf16[64,2432]{1,0:T(8,128)(2,1)S(1)} %collective-permute-done.23.rest_2_), channel_id=1, source_target_pairs={{0,1},{1,0},{2,3},{3,2},{4,5},{5,4},{6,7},{7,6},{8,9},{9,8},{10,11... | collective-permute-start | bytes 933896 | tf_op jit(solution)/shard_map/ppermute | solution.py:356
  155.4 13.9 %collective-permute-start.35 = (bf16[64,2432]{1,0:T(8,128)(2,1)S(1)}, bf16[64,2432]{1,0:T(8,128)(2,1)}, u32[]{:S(2)}, u32[]{:S(2)}) collective-permute-start(bf16[64,2432]{1,0:T(8,128)(2,1)S(1)} %collective-permute-done.27.rest_6_), channel_id=1, source_target_pairs={{0,1},{1,0},{2,3},{3,2},{4,5},{5,4},{6,7},{7,6},{8,9},{9,8},{10,11... | collective-permute-start | bytes 933896 | tf_op jit(solution)/shard_map/ppermute | solution.py:356
  161.6 7.7 %collective-permute-start.30 = (bf16[64,2432]{1,0:T(8,128)(2,1)S(1)}, bf16[64,2432]{1,0:T(8,128)(2,1)}, u32[]{:S(2)}, u32[]{:S(2)}) collective-permute-start(bf16[64,2432]{1,0:T(8,128)(2,1)S(1)} %collective-permute-done.22.rest_1_), channel_id=1, source_target_pairs={{0,1},{1,0},{2,3},{3,2},{4,5},{5,4},{6,7},{7,6},{8,9},{9,8},{10,11... | collective-permute-start | bytes 933896 | tf_op jit(solution)/shard_map/ppermute | solution.py:356
  162.9 6.5 %collective-permute-start.34 = (bf16[64,2432]{1,0:T(8,128)(2,1)S(1)}, bf16[64,2432]{1,0:T(8,128)(2,1)}, u32[]{:S(2)}, u32[]{:S(2)}) collective-permute-start(bf16[64,2432]{1,0:T(8,128)(2,1)S(1)} %collective-permute-done.26.rest_5_), channel_id=1, source_target_pairs={{0,1},{1,0},{2,3},{3,2},{4,5},{5,4},{6,7},{7,6},{8,9},{9,8},{10,11... | collective-permute-start | bytes 933896 | tf_op jit(solution)/shard_map/ppermute | solution.py:356
  162.9 6.4 %collective-permute-start.32 = (bf16[64,2432]{1,0:T(8,128)(2,1)S(1)}, bf16[64,2432]{1,0:T(8,128)(2,1)}, u32[]{:S(2)}, u32[]{:S(2)}) collective-permute-start(bf16[64,2432]{1,0:T(8,128)(2,1)S(1)} %collective-permute-done.24.rest_3_), channel_id=1, source_target_pairs={{0,1},{1,0},{2,3},{3,2},{4,5},{5,4},{6,7},{7,6},{8,9},{9,8},{10,11... | collective-permute-start | bytes 933896 | tf_op jit(solution)/shard_map/ppermute | solution.py:356
  163.4 6.0 %collective-permute-start.36 = (bf16[64,2432]{1,0:T(8,128)(2,1)S(1)}, bf16[64,2432]{1,0:T(8,128)(2,1)}, u32[]{:S(2)}, u32[]{:S(2)}) collective-permute-start(bf16[64,2432]{1,0:T(8,128)(2,1)S(1)} %collective-permute-done.28.rest_7_), channel_id=1, source_target_pairs={{0,1},{1,0},{2,3},{3,2},{4,5},{5,4},{6,7},{7,6},{8,9},{9,8},{10,11... | collective-permute-start | bytes 933896 | tf_op jit(solution)/shard_map/ppermute | solution.py:356
  191.1 20.2 %collective-permute-start.37 = (bf16[512,2304]{1,0:T(8,128)(2,1)}, bf16[512,2304]{1,0:T(8,128)(2,1)S(1)}, u32[]{:S(2)}, u32[]{:S(2)}) collective-permute-start(bf16[512,2304]{1,0:T(8,128)(2,1)} %get-tuple-element.45.late_ref), channel_id=1, source_target_pairs={{0,1},{1,0},{2,3},{3,2},{4,5},{5,4},{6,7},{7,6},{8,9},{9,8},{10,11... | collective-permute-start | bytes 7077896 | tf_op jit(solution)/shard_map/ppermute | solution.py:356
  191.3 15.7 %collective-permute-start.16 = (bf16[128,2304]{1,0:T(8,128)(2,1)S(1)}, bf16[128,2304]{1,0:T(8,128)(2,1)S(1)}, u32[]{:S(2)}, u32[]{:S(2)}) collective-permute-start(bf16[128,2304]{1,0:T(8,128)(2,1)S(1)} %copy-done.29), channel_id=1, source_target_pairs={{0,4},{4,0},{8,12},{12,8},{16,20},{20,16},{24,28},{28,24},{1,5},{5... | collective-permute-start | bytes 1769480 | tf_op jit(solution)/shard_map/ppermute | solution.py:356
  191.6 15.4 %collective-permute-start.17 = (bf16[128,2304]{1,0:T(8,128)(2,1)S(1)}, bf16[128,2304]{1,0:T(8,128)(2,1)S(1)}, u32[]{:S(2)}, u32[]{:S(2)}) collective-permute-start(bf16[128,2304]{1,0:T(8,128)(2,1)S(1)} %copy-done.28), channel_id=1, source_target_pairs={{0,2},{1,3},{2,0},{3,1},{4,6},{5,7},{6,4},{7,5},{8,10},{9,11},{10,... | collective-permute-start | bytes 1769480 | tf_op jit(solution)/shard_map/ppermute | solution.py:356
  217.4 56.2 %collective-permute-start.38 = (bf16[128,2304]{1,0:T(8,128)(2,1)}, bf16[128,2304]{1,0:T(8,128)(2,1)S(1)}, u32[]{:S(2)}, u32[]{:S(2)}) collective-permute-start(bf16[128,2304]{1,0:T(8,128)(2,1)} %get-tuple-element.47), channel_id=1, source_target_pairs={{0,4},{4,0},{8,12},{12,8},{16,20},{20,16},{24,28},{28,24},{1,5},{5... | collective-permute-start | bytes 1769480 | tf_op jit(solution)/shard_map/ppermute | solution.py:356
  219.0 54.6 %collective-permute-start.39 = (bf16[128,2304]{1,0:T(8,128)(2,1)}, bf16[128,2304]{1,0:T(8,128)(2,1)S(1)}, u32[]{:S(2)}, u32[]{:S(2)}) collective-permute-start(bf16[128,2304]{1,0:T(8,128)(2,1)} %get-tuple-element.48), channel_id=1, source_target_pairs={{0,2},{1,3},{2,0},{3,1},{4,6},{5,7},{6,4},{7,5},{8,10},{9,11},{10,... | collective-permute-start | bytes 1769480 | tf_op jit(solution)/shard_map/ppermute | solution.py:356
  222.4 13.6 %collective-permute-start.40 = (bf16[64,640]{1,0:T(8,128)(2,1)}, bf16[64,640]{1,0:T(8,128)(2,1)S(1)}, u32[]{:S(2)}, u32[]{:S(2)}) collective-permute-start(bf16[64,640]{1,0:T(8,128)(2,1)} %get-tuple-element.50), channel_id=1, source_target_pairs={{0,4},{4,0},{8,12},{12,8},{16,20},{20,16},{24,28},{28,24},{1,5},{5... | collective-permute-start | bytes 245768 | tf_op jit(solution)/shard_map/ppermute | solution.py:356
  222.9 21.1 %collective-permute-start.41 = (bf16[64,640]{1,0:T(8,128)(2,1)}, bf16[64,640]{1,0:T(8,128)(2,1)S(1)}, u32[]{:S(2)}, u32[]{:S(2)}) collective-permute-start(bf16[64,640]{1,0:T(8,128)(2,1)} %get-tuple-element.51), channel_id=1, source_target_pairs={{0,8},{4,12},{8,0},{12,4},{16,24},{20,28},{24,16},{28,20},{1,9},{5... | collective-permute-start | bytes 245768 | tf_op jit(solution)/shard_map/ppermute | solution.py:356
  230.3 14.0 %collective-permute-start.42 = (bf16[64,640]{1,0:T(8,128)(2,1)}, bf16[64,640]{1,0:T(8,128)(2,1)S(1)}, u32[]{:S(2)}, u32[]{:S(2)}) collective-permute-start(bf16[64,640]{1,0:T(8,128)(2,1)} %get-tuple-element.52), channel_id=1, source_target_pairs={{0,12},{4,8},{8,4},{12,0},{16,28},{20,24},{24,20},{28,16},{1,13},{... | collective-permute-start | bytes 245768 | tf_op jit(solution)/shard_map/ppermute | solution.py:356
  236.1 10.5 %collective-permute-start.43 = (bf16[64,640]{1,0:T(8,128)(2,1)}, bf16[64,640]{1,0:T(8,128)(2,1)S(1)}, u32[]{:S(2)}, u32[]{:S(2)}) collective-permute-start(bf16[64,640]{1,0:T(8,128)(2,1)} %get-tuple-element.53), channel_id=1, source_target_pairs={{0,16},{4,20},{8,24},{12,28},{16,0},{20,4},{24,8},{28,12},{1,17},{... | collective-permute-start | bytes 245768 | tf_op jit(solution)/shard_map/ppermute | solution.py:356
  244.0 25.9 %collective-permute-start.18 = (bf16[64,2304]{1,0:T(8,128)(2,1)S(1)}, bf16[64,2304]{1,0:T(8,128)(2,1)S(1)}, u32[]{:S(2)}, u32[]{:S(2)}) collective-permute-start(bf16[64,2304]{1,0:T(8,128)(2,1)S(1)} %copy-done.11), channel_id=1, source_target_pairs={{0,2},{1,3},{2,0},{3,1},{4,6},{5,7},{6,4},{7,5},{8,10},{9,11},{10,... | collective-permute-start | bytes 884744 | tf_op jit(solution)/shard_map/ppermute | solution.py:356
  244.3 25.5 %collective-permute-start.19 = (bf16[64,2304]{1,0:T(8,128)(2,1)S(1)}, bf16[64,2304]{1,0:T(8,128)(2,1)S(1)}, u32[]{:S(2)}, u32[]{:S(2)}) collective-permute-start(bf16[64,2304]{1,0:T(8,128)(2,1)S(1)} %copy-done.51), channel_id=1, source_target_pairs={{0,4},{4,0},{8,12},{12,8},{16,20},{20,16},{24,28},{28,24},{1,5},{5... | collective-permute-start | bytes 884744 | tf_op jit(solution)/shard_map/ppermute | solution.py:356
  246.6 6.4 %collective-permute-start.44 = (bf16[64,640]{1,0:T(8,128)(2,1)}, bf16[64,640]{1,0:T(8,128)(2,1)S(1)}, u32[]{:S(2)}, u32[]{:S(2)}) collective-permute-start(bf16[64,640]{1,0:T(8,128)(2,1)} %get-tuple-element.54), channel_id=1, source_target_pairs={{0,20},{4,16},{8,28},{12,24},{16,4},{20,0},{24,12},{28,8},{1,21},{... | collective-permute-start | bytes 245768 | tf_op jit(solution)/shard_map/ppermute | solution.py:356
  253.0 6.5 %collective-permute-start.45 = (bf16[64,640]{1,0:T(8,128)(2,1)}, bf16[64,640]{1,0:T(8,128)(2,1)S(1)}, u32[]{:S(2)}, u32[]{:S(2)}) collective-permute-start(bf16[64,640]{1,0:T(8,128)(2,1)} %get-tuple-element.55), channel_id=1, source_target_pairs={{0,24},{4,28},{8,16},{12,20},{16,8},{20,12},{24,0},{28,4},{1,25},{... | collective-permute-start | bytes 245768 | tf_op jit(solution)/shard_map/ppermute | solution.py:356
  259.6 7.4 %collective-permute-start.46 = (bf16[64,640]{1,0:T(8,128)(2,1)}, bf16[64,640]{1,0:T(8,128)(2,1)S(1)}, u32[]{:S(2)}, u32[]{:S(2)}) collective-permute-start(bf16[64,640]{1,0:T(8,128)(2,1)} %get-tuple-element.56), channel_id=1, source_target_pairs={{0,28},{4,24},{8,20},{12,16},{16,12},{20,8},{24,4},{28,0},{1,29},{... | collective-permute-start | bytes 245768 | tf_op jit(solution)/shard_map/ppermute | solution.py:356
  278.2 6.9 %collective-permute-start.47 = (bf16[64,2304]{1,0:T(8,128)(2,1)}, bf16[64,2304]{1,0:T(8,128)(2,1)S(1)}, u32[]{:S(2)}, u32[]{:S(2)}) collective-permute-start(bf16[64,2304]{1,0:T(8,128)(2,1)} %get-tuple-element.58), channel_id=1, source_target_pairs={{0,2},{1,3},{2,0},{3,1},{4,6},{5,7},{6,4},{7,5},{8,10},{9,11},{10,... | collective-permute-start | bytes 884744 | tf_op jit(solution)/shard_map/ppermute | solution.py:356
  278.6 6.9 %collective-permute-start.48 = (bf16[64,2304]{1,0:T(8,128)(2,1)}, bf16[64,2304]{1,0:T(8,128)(2,1)S(1)}, u32[]{:S(2)}, u32[]{:S(2)}) collective-permute-start(bf16[64,2304]{1,0:T(8,128)(2,1)} %get-tuple-element.59), channel_id=1, source_target_pairs={{0,4},{4,0},{8,12},{12,8},{16,20},{20,16},{24,28},{28,24},{1,5},{5... | collective-permute-start | bytes 884744 | tf_op jit(solution)/shard_map/ppermute | solution.py:356
  289.3 8.9 %collective-permute-start.49 = (bf16[64,2304]{1,0:T(8,128)(2,1)}, bf16[64,2304]{1,0:T(8,128)(2,1)S(1)}, u32[]{:S(2)}, u32[]{:S(2)}) collective-permute-start(bf16[64,2304]{1,0:T(8,128)(2,1)} %get-tuple-element.61), channel_id=1, source_target_pairs={{0,8},{4,12},{8,0},{12,4},{16,24},{20,28},{24,16},{28,20},{1,9},{5... | collective-permute-start | bytes 884744 | tf_op jit(solution)/shard_map/ppermute | solution.py:356
  290.7 11.9 %collective-permute-start.20 = (bf16[64,2304]{1,0:T(8,128)(2,1)S(1)}, bf16[64,2304]{1,0:T(8,128)(2,1)S(1)}, u32[]{:S(2)}, u32[]{:S(2)}) collective-permute-start(bf16[64,2304]{1,0:T(8,128)(2,1)S(1)} %copy-done.12), channel_id=1, source_target_pairs={{0,8},{4,12},{8,0},{12,4},{16,24},{20,28},{24,16},{28,20},{1,9},{5... | collective-permute-start | bytes 884744 | tf_op jit(solution)/shard_map/ppermute | solution.py:356
  299.3 10.8 %collective-permute-start.50 = (bf16[64,2304]{1,0:T(8,128)(2,1)S(1)}, bf16[64,2304]{1,0:T(8,128)(2,1)S(1)}, u32[]{:S(2)}, u32[]{:S(2)}) collective-permute-start(bf16[64,2304]{1,0:T(8,128)(2,1)S(1)} %add_convert_fusion.1), channel_id=1, source_target_pairs={{0,16},{4,20},{8,24},{12,28},{16,0},{20,4},{24,8},{28,12},{1,17},{... | collective-permute-start | bytes 884744 | tf_op jit(solution)/shard_map/ppermute | solution.py:356
  (58 other events, 805.6 us)

commit v5 on v4

--- a/solution.py
+++ b/solution.py
@@ -173,52 +173,42 @@
     )(context, residual, gain[None, :], facts)
 
 
-def pick_pages_kernel(per_device, first_lane, order_ref, me_ref, packed_ref, late_ref, *out_refs):
+def pick_pages_kernel(per_device, first_lane, order_ref, packed_ref, late_ref, out_ref):
     del late_ref
-    for j, out_ref in enumerate(out_refs):
-        peer = jnp.bitwise_xor(me_ref[0], j)
+    for j in range(out_ref.shape[0]):
         for i in range(per_device):
-            page = order_ref[peer * per_device + i]
-            rows = pl.ds(pl.multiple_of(page * PAGE, PAGE), PAGE)
-            out_ref[i * PAGE : (i + 1) * PAGE, :] = packed_ref[rows, first_lane:]
-
-
-def pick_pages(packed, order, me, late, n_seq, span):
+            rows = pl.ds(pl.multiple_of(order_ref[j * per_device + i] * PAGE, PAGE), PAGE)
+            out_ref[j, i * PAGE : (i + 1) * PAGE, :] = packed_ref[rows, first_lane:]
+
+
+def pick_pages(packed, order, late, n_seq, span):
     rows = packed.shape[0] // n_seq
-    smem = pl.BlockSpec(memory_space=pltpu.SMEM)
     vmem = pl.BlockSpec(memory_space=pltpu.VMEM)
-    out = jax.ShapeDtypeStruct((rows, 2 * span), jnp.bfloat16)
     return pl.pallas_call(
         functools.partial(pick_pages_kernel, rows // PAGE, span),
-        out_shape=(out,) * n_seq,
-        in_specs=[smem, smem, vmem, pl.BlockSpec(memory_space=pl.ANY)],
+        out_shape=jax.ShapeDtypeStruct((n_seq, rows, 2 * span), jnp.bfloat16),
+        in_specs=[pl.BlockSpec(memory_space=pltpu.SMEM), vmem, pl.BlockSpec(memory_space=pl.ANY)],
         cost_estimate=pl.CostEstimate(flops=0, bytes_accessed=10 * packed.shape[0] * span, transcendentals=0),
-    )(order, me, packed, late)
-
-
-def join_pages_kernel(share, offsets, span, me_ref, *refs):
-    piece_refs, out_ref, all_ref = refs[:-2], refs[-2], refs[-1]
-    for j, ref in enumerate(piece_refs):
-        all_ref[jnp.bitwise_xor(me_ref[0], j)] = ref[...]
+    )(order, packed, late)
+
+
+def join_pages_kernel(share, offsets, span, pages_ref, out_ref):
+    width = share * len(offsets)
     for part in range(2):
         parts = [
-            all_ref[j][:, part * span + offsets[j] : part * span + offsets[j] + share]
-            for j in range(len(piece_refs))
+            pages_ref[j][:, part * span + offsets[j] : part * span + offsets[j] + share]
+            for j in range(len(offsets))
         ]
-        width = share * len(piece_refs)
         out_ref[:, part * width : (part + 1) * width] = jnp.concatenate(parts, axis=1)
 
 
-def join_pages(pieces, me, share, offsets, span):
-    rows = pieces[0].shape[0]
-    n_seq = len(pieces)
+def join_pages(pages, share, offsets, span):
+    n_seq, rows, _ = pages.shape
     return pl.pallas_call(
         functools.partial(join_pages_kernel, share, offsets, span),
         out_shape=jax.ShapeDtypeStruct((rows, 2 * share * n_seq), jnp.bfloat16),
-        in_specs=[pl.BlockSpec(memory_space=pltpu.SMEM)] + [pl.BlockSpec(memory_space=pltpu.VMEM)] * n_seq,
-        scratch_shapes=[pltpu.VMEM((n_seq,) + pieces[0].shape, jnp.bfloat16)],
         cost_estimate=pl.CostEstimate(flops=0, bytes_accessed=8 * rows * n_seq * span, transcendentals=0),
-    )(me, *pieces)
+    )(pages)
 
 
 def places_of(slots, base, shift):
@@ -282,12 +272,12 @@
             rows_of[e, g * rows : (g + 1) * rows, :] = chosen[e * rows : (e + 1) * rows].astype(jnp.bfloat16)
 
     for e in range(local):
-        chosen = rows_of[e].T
+        chosen = rows_of[e]
         weight_copies[e][0].wait()
-        gate = jnp.dot(wg[e], chosen, preferred_element_type=jnp.float32)
+        gate = dot_t(chosen, wg[e])
         weight_copies[e][1].wait()
-        upper = jnp.dot(wu[e], chosen, preferred_element_type=jnp.float32)
-        hidden = (gate / (1.0 + jnp.exp(-gate)) * upper).T.astype(jnp.bfloat16)
+        upper = dot_t(chosen, wu[e])
+        hidden = (gate / (1.0 + jnp.exp(-gate)) * upper).astype(jnp.bfloat16)
         weight_copies[e][2].wait()
         result = jnp.dot(hidden, wd[e], preferred_element_type=jnp.float32)
         result = (result * jnp.concatenate(weights[e], axis=0)).astype(jnp.bfloat16)
@@ -358,29 +348,30 @@
 
 def fold_kernel(groups, count, waits, keep_ref, *rest):
     got_refs, (kept_ref, *send_refs) = rest[:count], rest[count + waits :]
-    got = jnp.concatenate([r[...] for r in got_refs], axis=0) if count > 1 else got_refs[0][...]
-    total = (keep_ref[...].astype(jnp.float32) + got.astype(jnp.float32)).astype(jnp.bfloat16)
-    part = total.shape[0] // (2 * groups)
-    for i in range(groups):
-        kept_ref[i * part : (i + 1) * part, :] = total[2 * i * part : (2 * i + 1) * part]
-        send_refs[i][...] = total[(2 * i + 1) * part : (2 * i + 2) * part]
+    part = keep_ref.shape[0] // (2 * groups)
+    span = got_refs[0].shape[0]
+    for i in range(2 * groups):
+        start = i * part
+        got = got_refs[start // span][start % span : start % span + part, :]
+        total = keep_ref[start : start + part, :].astype(jnp.float32) + got.astype(jnp.float32)
+        total = total.astype(jnp.bfloat16)
+        if i % 2 == 0:
+            kept_ref[i // 2 * part : (i // 2 + 1) * part, :] = total
+        else:
+            send_refs[i // 2][...] = total
 
 
 def fold(keep, gots, groups, waits=()):
     rows, width = keep.shape
     part = rows // (2 * groups)
-    steps = 3 if width % (3 * 128) == 0 else 1
-    block = lambda n: pl.BlockSpec((n, width // steps), lambda i: (0, i))
+    vmem = pl.BlockSpec(memory_space=pltpu.VMEM)
     shape = lambda n: jax.ShapeDtypeStruct((n, width), jnp.bfloat16)
     out = pl.pallas_call(
         functools.partial(fold_kernel, groups, len(gots), len(waits)),
         out_shape=(shape(groups * part),) + (shape(part),) * groups,
-        grid=(steps,),
-        in_specs=[block(rows)]
-        + [block(g.shape[0]) for g in gots]
-        + [pl.BlockSpec(memory_space=pl.ANY)] * len(waits),
-        out_specs=(block(groups * part),) + (block(part),) * groups,
-        compiler_params=pltpu.CompilerParams(vmem_limit_bytes=58 * 1024 * 1024),
+        in_specs=[vmem] * (1 + len(gots)) + [pl.BlockSpec(memory_space=pl.ANY)] * len(waits),
+        out_specs=(vmem,) * (1 + groups),
+        compiler_params=pltpu.CompilerParams(vmem_limit_bytes=24 * 1024 * 1024),
         cost_estimate=pl.CostEstimate(flops=rows * width, bytes_accessed=6 * rows * width, transcendentals=0),
     )(keep, *gots, *waits)
     return out[0], out[1:]
@@ -401,15 +392,16 @@
         return near + [core(p) for p in near]
 
     experts_of = lambda pieces, waits: chunk_experts(pieces, w_gate, w_up, w_down, first, waits)
-    keep_a, send_a = experts_of(gather(0), [])
+    chunk_a, chunk_b = gather(0), gather(2)
+    keep_a, send_a = experts_of(chunk_a, chunk_b)
+    pages, other = late_work(send_a)
+    keep_b, send_b = experts_of(chunk_b, [pages, send_a])
     keep_a, (fx_a, fy_a) = fold(keep_a, [core(send_a)], 2)
-    keep_b, send_b = experts_of(gather(2), [fx_a])
     got_b = core(send_b)
-    other = late_work(send_b)
     keep_a, (gy_a, gx_a) = fold(keep_a, [x(fx_a), y(fy_a)], 2)
-    keep_b, (fx_b, fy_b) = fold(keep_b, [got_b], 2, [gy_a])
+    keep_b, (fx_b, fy_b) = fold(keep_b, [got_b], 2, [gy_a, other])
     keep_a, (z_a,) = fold(keep_a, [y(gy_a), x(gx_a)], 1)
-    keep_b, (gy_b, gx_b) = fold(keep_b, [x(fx_b), y(fy_b)], 2, [z_a, other])
+    keep_b, (gy_b, gx_b) = fold(keep_b, [x(fx_b), y(fy_b)], 2, [z_a])
     got_a = z(z_a, 1)
     keep_b, (z_b,) = fold(keep_b, [y(gy_b), x(gx_b)], 1)
     mine = keep_a.astype(jnp.float32) + got_a.astype(jnp.float32)
@@ -458,7 +450,6 @@
     offsets = [j * share - firsts[j] * HEAD_DIM for j in range(n_seq)]
 
     first = (lax.axis_index("exp") * (EXPERTS // n_exp)).astype(jnp.int32).reshape(1)
-    me = lax.axis_index("seq").astype(jnp.int32).reshape(1)
     w_gate, w_up = jnp.swapaxes(w_gate, 1, 2), jnp.swapaxes(w_up, 1, 2)
     gates = gate_weights[0]
     facts = jnp.concatenate([target, gates, gates, gates], axis=1)
@@ -469,22 +460,14 @@
     order = jnp.sum(jnp.where(page_table[0][None, :] == slots[:, None], slots[None, :], 0), axis=1)
 
     def fill_cache(late):
-        if n_seq & (n_seq - 1) == 0:
-            pages = pick_pages(packed, order, me, late, n_seq, span)
-            pages = [pages[0]] + [swap(pages[j], "seq", n_seq, j) for j in range(1, n_seq)]
-            return join_pages(pages, me, share, offsets, span)
-        pages = jnp.take(packed[:, span:].reshape(group // PAGE, PAGE, 2 * span), order, axis=0)
-        pages = pages.reshape(n_seq, rows_dev, 2 * span)
-        pages = lax.all_to_all(pages, "seq", split_axis=0, concat_axis=0, tiled=True)
-        parts = [
-            pages[j][:, at + offsets[j] : at + offsets[j] + share] for at in (0, span) for j in range(n_seq)
-        ]
-        return jnp.concatenate(parts, axis=1)
+        pages = pick_pages(packed, order, late, n_seq, span)
+        sent = lax.all_to_all(pages, "seq", split_axis=0, concat_axis=0, tiled=True)
+        return pages, join_pages(sent, share, offsets, span)
 
     if (n_seq, n_exp) == (8, 4):
         mixture, cache = exchange_experts(piece, w_gate, w_up, w_down, first, n_seq, n_exp, fill_cache)
     else:
-        cache = fill_cache(piece)
+        _, cache = fill_cache(piece)
         blocks = n_seq * n_exp
         everything = lax.all_gather(piece, everyone, axis=0, tiled=True)
         facts = everything[:, width : width + 8].astype(jnp.float32)

time: 312 us -> 270 us (0.87)
  Pallas kernels: 77.5 us -> 64.5 us
  starting transfers between devices: 67 us -> 54 us
  waiting for transfers between devices: 148 us -> 139 us
  local copies, waits for them, and re-layouts: 13.3 us -> 6.85 us
    ppermute x51 -> x44, waiting for transfers between devices: 112 us -> 92.8 us  [swap(): return lax.ppermute(a, axis, [(i, i ^ distance) for i in range(size)])]
    ppermute x51 -> x44, starting transfers between devices: 56.1 us -> 36.5 us  [swap(): return lax.ppermute(a, axis, [(i, i ^ distance) for i in range(size)])]
    pallas_call x6, Pallas kernels: 22 us -> 7.08 us  [fold(): pl.pallas_call(functools.partial(fold_kernel, groups, len(gots), len(wait...]
    all_to_all x0 -> x1, waiting for transfers between devices: none -> 11.4 us  [fill_cache(): sent = lax.all_to_all(pages, 'seq', split_axis=0, concat_axis=0, tiled=True)]
    all_to_all x0 -> x1, starting transfers between devices: none -> 6.66 us  [fill_cache(): sent = lax.all_to_all(pages, 'seq', split_axis=0, concat_axis=0, tiled=True)]
    unnamed x128 -> x90, local copies, waits for them, and re-layouts: 8.79 us -> 2.39 us
  transfers between devices with their start and end apart: 53 -> 47, of which waited for: 25 -> 22; matrix products, arithmetic and copies ran while one was open for 1% -> 1% of each run, Pallas kernels for 5% -> 12%
where the time goes in v5:
time: 270 us; the launch traced here: 269 us
  waiting for transfers between devices  139 us (51%)
  Pallas kernels  64.5 us (24%)
  starting transfers between devices  54 us (20%)
  local copies, waits for them, and re-layouts  6.85 us (3%)
  other arithmetic  3.31 us (1%)
    ppermute x44, waiting for transfers between devices, swap(): return lax.ppermute(a, axis, [(i, i ^ distance) for i in range(size)])  92.8 us
    pallas_call x2, Pallas kernels, chunk_experts(): pl.pallas_call(functools.partial(chunk_kernel, local, len(pieces), len(wa...  45.2 us
    ppermute x44, starting transfers between devices, swap(): return lax.ppermute(a, axis, [(i, i ^ distance) for i in range(size)])  36.5 us
    all_to_all x1, waiting for transfers between devices, body(): lax.all_to_all(packed, 'seq', split_axis=0, concat_axis=0, tiled=True)  25.3 us
    all_to_all x1, waiting for transfers between devices, fill_cache(): sent = lax.all_to_all(pages, 'seq', split_axis=0, concat_axis=0, tiled=True)  11.4 us
    all_to_all x1, waiting for transfers between devices, body(): lax.all_to_all(context.reshape(n_seq, rows_dev, span), 'seq', split_axis=...  9.8 us
    all_to_all x1, starting transfers between devices, body(): lax.all_to_all(packed, 'seq', split_axis=0, concat_axis=0, tiled=True)  7.25 us
    pallas_call x6, Pallas kernels, fold(): pl.pallas_call(functools.partial(fold_kernel, groups, len(gots), len(wait...  7.08 us
  transfers between devices with their start and end apart: 47, of which 22 were waited for; matrix products, arithmetic and copies ran while one was open for 1% of the time, Pallas kernels for 12%

profile of v5, /device:TPU:0, one launch (start us, length us, event | category | flops | bytes accessed | tf_op | source)
XLA Modules:
  0.0 269.1 jit_solution(12355504263536556260)
XLA Ops:
  0.6 2.3 fusion.3
  4.4 1.3 pad_maximum_fusion
  5.7 7.3 %all-to-all-start = ((bf16[8,64,960]{2,1,0:T(8,128)(2,1)}), bf16[8,64,960]{2,1,0:T(8,128)(2,1)S(1)}, u32[]{:S(2)}, u32[]{:S(2)}) async-start(bf16[8,64,960]{2,1,0:T(8,128)(2,1)} %pad_maximum_fusion), calls=%async_computation | async-start | bytes 2097152 | tf_op jit(solution)/shard_map/all_to_all | solution.py:444
  13.4 25.3 %all-to-all-done = bf16[8,64,960]{2,1,0:T(8,128)(2,1)S(1)} async-done(((bf16[8,64,960]{2,1,0:T(8,128)(2,1)}), bf16[8,64,960]{2,1,0:T(8,128)(2,1)S(1)}, u32[]{:S(2)}, u32[]{:S(2)}) %all-to-all-start) | async-done | bytes 983072 | tf_op jit(solution)/shard_map/all_to_all | solution.py:444
  38.7 5.6 %shard_map.122 = bf16[512,320]{1,0:T(8,128)(2,1)} custom-call(bf16[512,960]{1,0:T(8,128)(2,1)S(1)} %bitcast.117, s32[1,512]{1,0:T(1,128)S(1)} %copy-done.4, s32[512,1]{1,0:T(8,128)S(1)} %copy.35.seg_col_ref), custom_call_target="tpu_custom_call" | custom-call | flops 335544320 | bytes 1310720 | tf_op jit(solution)/shard_map/pallas_call | solution.py:55
  44.3 3.6 %all-to-all-start.1 = ((bf16[8,64,320]{2,1,0:T(8,128)(2,1)}), bf16[8,64,320]{2,1,0:T(8,128)(2,1)S(1)}, u32[]{:S(2)}, u32[]{:S(2)}) async-start(bf16[8,64,320]{2,1,0:T(8,128)(2,1)} %bitcast.29), calls=%async_computation.1 | async-start | bytes 786432 | tf_op jit(solution)/shard_map/all_to_all | solution.py:447
  50.0 9.8 %all-to-all-done.1.context_ref = bf16[8,64,320]{2,1,0:T(8,128)(2,1)S(1)} async-done(((bf16[8,64,320]{2,1,0:T(8,128)(2,1)}), bf16[8,64,320]{2,1,0:T(8,128)(2,1)S(1)}, u32[]{:S(2)}, u32[]{:S(2)}) %all-to-all-start.1) | async-done | bytes 327712 | tf_op jit(solution)/shard_map/all_to_all | solution.py:447
  60.5 2.2 shard_map.123
  64.4 2.6 collective-permute-start.19
  67.1 1.5 collective-permute-start.1
  68.5 1.5 collective-permute-start
  70.1 4.6 %collective-permute-done.3.rest_4_ = bf16[64,2432]{1,0:T(8,128)(2,1)S(1)} collective-permute-done((bf16[64,2432]{1,0:T(8,128)(2,1)}, bf16[64,2432]{1,0:T(8,128)(2,1)S(1)}, u32[]{:S(2)}, u32[]{:S(2)}) %collective-permute-start.3) | collective-permute-done | bytes 311328 | tf_op jit(solution)/shard_map/ppermute | solution.py:346
  74.6 13.2 %collective-permute-done.15.rest_16_.rest_0_ = bf16[64,2432]{1,0:T(8,128)(2,1)S(1)} collective-permute-done((bf16[64,2432]{1,0:T(8,128)(2,1)}, bf16[64,2432]{1,0:T(8,128)(2,1)S(1)}, u32[]{:S(2)}, u32[]{:S(2)}) %collective-permute-start.15) | collective-permute-done | bytes 311328 | tf_op jit(solution)/shard_map/ppermute | solution.py:346
  87.9 1.5 collective-permute-start.5
  90.9 1.5 collective-permute-start.2
  93.5 4.7 %collective-permute-done.5.rest_6_ = bf16[64,2432]{1,0:T(8,128)(2,1)S(1)} collective-permute-done((bf16[64,2432]{1,0:T(8,128)(2,1)S(1)}, bf16[64,2432]{1,0:T(8,128)(2,1)S(1)}, u32[]{:S(2)}, u32[]{:S(2)}) %collective-permute-start.5) | collective-permute-done | bytes 311328 | tf_op jit(solution)/shard_map/ppermute | solution.py:346
  98.2 1.5 collective-permute-start.16
  99.7 1.0 collective-permute-start.20
  100.7 4.1 %collective-permute-done.21.rest_22_.rest_6_ = bf16[64,2432]{1,0:T(8,128)(2,1)S(1)} collective-permute-done((bf16[64,2432]{1,0:T(8,128)(2,1)S(1)}, bf16[64,2432]{1,0:T(8,128)(2,1)S(1)}, u32[]{:S(2)}, u32[]{:S(2)}) %collective-permute-start.21) | collective-permute-done | bytes 311328 | tf_op jit(solution)/shard_map/ppermute | solution.py:346
  104.8 3.5 %collective-permute-done.2.rest_3_ = bf16[64,2432]{1,0:T(8,128)(2,1)S(1)} collective-permute-done((bf16[64,2432]{1,0:T(8,128)(2,1)S(1)}, bf16[64,2432]{1,0:T(8,128)(2,1)S(1)}, u32[]{:S(2)}, u32[]{:S(2)}) %collective-permute-start.2) | collective-permute-done | bytes 311328 | tf_op jit(solution)/shard_map/ppermute | solution.py:346
  108.9 2.8 %collective-permute-done.16.rest_17_.rest_1_ = bf16[64,2432]{1,0:T(8,128)(2,1)S(1)} collective-permute-done((bf16[64,2432]{1,0:T(8,128)(2,1)S(1)}, bf16[64,2432]{1,0:T(8,128)(2,1)S(1)}, u32[]{:S(2)}, u32[]{:S(2)}) %collective-permute-start.16) | collective-permute-done | bytes 311328 | tf_op jit(solution)/shard_map/ppermute | solution.py:346
  112.6 1.5 collective-permute-start.18
  114.1 1.7 collective-permute-start.22
  116.3 6.2 %collective-permute-done.6.rest_7_ = bf16[64,2432]{1,0:T(8,128)(2,1)} collective-permute-done((bf16[64,2432]{1,0:T(8,128)(2,1)S(1)}, bf16[64,2432]{1,0:T(8,128)(2,1)}, u32[]{:S(2)}, u32[]{:S(2)}) %collective-permute-start.6) | collective-permute-done | bytes 311328 | tf_op jit(solution)/shard_map/ppermute | solution.py:346
  123.1 5.3 %collective-permute-done.22.rest_23_.rest_7_ = bf16[64,2432]{1,0:T(8,128)(2,1)} collective-permute-done((bf16[64,2432]{1,0:T(8,128)(2,1)S(1)}, bf16[64,2432]{1,0:T(8,128)(2,1)}, u32[]{:S(2)}, u32[]{:S(2)}) %collective-permute-start.22) | collective-permute-done | bytes 311328 | tf_op jit(solution)/shard_map/ppermute | solution.py:346
  132.6 23.0 %shard_map.124 = (bf16[512,2304]{1,0:T(8,128)(2,1)}, bf16[512,2304]{1,0:T(8,128)(2,1)}) custom-call(s32[1]{0:T(128)} %bitcast.33.first_ref, bf16[2,720,2304]{2,1,0:T(8,128)(2,1)} %bitcast.121, bf16[2,720,2304]{2,1,0:T(8,128)(2,1)} %bitcast.123, bf16[2,720,2304]{2,1,0:T(8,128)(2,1)} %wd_hbm.3, bf16[64,2432]{1,0:T(8,128)(2,1)} %get-tuple-element.25.rest_0_, ...), custom_call_target="tpu_custom_call" | custom-call | flops 7644119040 | bytes 29343744 | tf_op jit(solution)/shard_map/pallas_call | solution.py:319
  155.8 2.4 shard_map.128.rest_16_
  158.2 22.2 %shard_map.129 = (bf16[512,2304]{1,0:T(8,128)(2,1)}, bf16[512,2304]{1,0:T(8,128)(2,1)}) custom-call(s32[1]{0:T(128)} %bitcast.33.first_ref, bf16[2,720,2304]{2,1,0:T(8,128)(2,1)} %bitcast.122, bf16[2,720,2304]{2,1,0:T(8,128)(2,1)} %bitcast.124, bf16[2,720,2304]{2,1,0:T(8,128)(2,1)} %wd_hbm.3, bf16[64,2432]{1,0:T(8,128)(2,1)} %copy-done.8, ...), custom_call_target="tpu_custom_call" | custom-call | flops 7644119040 | bytes 29343744 | tf_op jit(solution)/shard_map/pallas_call | solution.py:319
  180.9 6.7 %all-to-all-start.2 = ((bf16[8,64,640]{2,1,0:T(8,128)(2,1)}), bf16[8,64,640]{2,1,0:T(8,128)(2,1)}, u32[]{:S(2)}, u32[]{:S(2)}) async-start(bf16[8,64,640]{2,1,0:T(8,128)(2,1)} %shard_map.128.rest_16_), calls=%async_computation.2 | async-start | bytes 1310720 | tf_op jit(solution)/shard_map/all_to_all | solution.py:464
  187.5 2.8 %shard_map.125 = (bf16[256,2304]{1,0:T(8,128)(2,1)S(1)}, bf16[128,2304]{1,0:T(8,128)(2,1)}, bf16[128,2304]{1,0:T(8,128)(2,1)}) custom-call(bf16[512,2304]{1,0:T(8,128)(2,1)S(1)} %copy-done.1, bf16[512,2304]{1,0:T(8,128)(2,1)} %collective-permute-done.31.rest_0_), custom_call_target="tpu_custom_call" | custom-call | flops 1179648 | bytes 7077888 | tf_op jit(solution)/shard_map/pallas_call | solution.py:369
  190.4 2.0 collective-permute-start.32
  192.4 1.5 collective-permute-start.33
  193.9 11.4 %all-to-all-done.2.pages_ref = bf16[8,64,640]{2,1,0:T(8,128)(2,1)} async-done(((bf16[8,64,640]{2,1,0:T(8,128)(2,1)}), bf16[8,64,640]{2,1,0:T(8,128)(2,1)}, u32[]{:S(2)}, u32[]{:S(2)}) %all-to-all-start.2) | async-done | bytes 655392 | tf_op jit(solution)/shard_map/all_to_all | solution.py:464
  205.2 2.1 shard_map.130.rest_2_
  207.3 2.9 %collective-permute-done.32.rest_0_ = bf16[128,2304]{1,0:T(8,128)(2,1)} collective-permute-done((bf16[128,2304]{1,0:T(8,128)(2,1)}, bf16[128,2304]{1,0:T(8,128)(2,1)}, u32[]{:S(2)}, u32[]{:S(2)}) %collective-permute-start.32) | collective-permute-done | bytes 589856 | tf_op jit(solution)/shard_map/ppermute | solution.py:346
  210.2 1.5 shard_map.126
  211.7 2.2 shard_map.131
  214.5 1.5 collective-permute-start.39
  216.6 1.5 collective-permute-start.35
  218.1 17.3 %collective-permute-done.34.rest_0_ = bf16[64,2304]{1,0:T(8,128)(2,1)S(1)} collective-permute-done((bf16[64,2304]{1,0:T(8,128)(2,1)S(1)}, bf16[64,2304]{1,0:T(8,128)(2,1)S(1)}, u32[]{:S(2)}, u32[]{:S(2)}) %collective-permute-start.34) | collective-permute-done | bytes 294944 | tf_op jit(solution)/shard_map/ppermute | solution.py:346
  235.8 1.6 collective-permute-start.40
  237.4 1.7 collective-permute-start.41
  239.1 4.5 %collective-permute-done.40.rest_0_ = bf16[64,2304]{1,0:T(8,128)(2,1)S(1)} collective-permute-done((bf16[64,2304]{1,0:T(8,128)(2,1)S(1)}, bf16[64,2304]{1,0:T(8,128)(2,1)S(1)}, u32[]{:S(2)}, u32[]{:S(2)}) %collective-permute-start.40) | collective-permute-done | bytes 294944 | tf_op jit(solution)/shard_map/ppermute | solution.py:346
  243.6 1.2 collective-permute-done.41.rest_1_
  245.8 1.2 collective-permute-start.36
  247.0 10.8 %collective-permute-done.42 = bf16[64,2304]{1,0:T(8,128)(2,1)S(1)} collective-permute-done((bf16[64,2304]{1,0:T(8,128)(2,1)S(1)}, bf16[64,2304]{1,0:T(8,128)(2,1)S(1)}, u32[]{:S(2)}, u32[]{:S(2)}) %collective-permute-start.42) | collective-permute-done | bytes 294944 | tf_op jit(solution)/shard_map/ppermute | solution.py:346
  258.5 2.5 collective-permute-done.36
  261.0 7.3 %collective-permute-done.43 = bf16[64,2304]{1,0:T(8,128)(2,1)S(1)} collective-permute-done((bf16[64,2304]{1,0:T(8,128)(2,1)S(1)}, bf16[64,2304]{1,0:T(8,128)(2,1)S(1)}, u32[]{:S(2)}, u32[]{:S(2)}) %collective-permute-start.43) | collective-permute-done | bytes 294944 | tf_op jit(solution)/shard_map/ppermute | solution.py:346
  (169 shorter events, 20.0 us)
Async XLA Ops:
  5.7 33.0 %all-to-all-start = ((bf16[8,64,960]{2,1,0:T(8,128)(2,1)}), bf16[8,64,960]{2,1,0:T(8,128)(2,1)S(1)}, u32[]{:S(2)}, u32[]{:S(2)}) async-start(bf16[8,64,960]{2,1,0:T(8,128)(2,1)} %pad_maximum_fusion), calls=%async_computation | async-start | bytes 2097152 | tf_op jit(solution)/shard_map/all_to_all | solution.py:444
  13.0 117.7 %copy-start.33 = (s32[1,32]{1,0:T(1,128)S(1)}, s32[1,32]{1,0:T(1,128)}, u32[]{:S(2)}) copy-start(s32[1,32]{1,0:T(1,128)} %param.18) | copy-start | bytes 388
  44.3 15.5 %all-to-all-start.1 = ((bf16[8,64,320]{2,1,0:T(8,128)(2,1)}), bf16[8,64,320]{2,1,0:T(8,128)(2,1)S(1)}, u32[]{:S(2)}, u32[]{:S(2)}) async-start(bf16[8,64,320]{2,1,0:T(8,128)(2,1)} %bitcast.29), calls=%async_computation.1 | async-start | bytes 786432 | tf_op jit(solution)/shard_map/all_to_all | solution.py:447
  62.7 12.0 %collective-permute-start.3 = (bf16[64,2432]{1,0:T(8,128)(2,1)}, bf16[64,2432]{1,0:T(8,128)(2,1)S(1)}, u32[]{:S(2)}, u32[]{:S(2)}) collective-permute-start(bf16[64,2432]{1,0:T(8,128)(2,1)} %get-tuple-element.25.rest_0_), channel_id=1, source_target_pairs={{0,8},{4,12},{8,0},{12,4},{16,24},{20,28},{24,16},{28,20},{1,9},{5... | collective-permute-start | bytes 933896 | tf_op jit(solution)/shard_map/ppermute | solution.py:346
  63.6 24.3 %collective-permute-start.15 = (bf16[64,2432]{1,0:T(8,128)(2,1)}, bf16[64,2432]{1,0:T(8,128)(2,1)S(1)}, u32[]{:S(2)}, u32[]{:S(2)}) collective-permute-start(bf16[64,2432]{1,0:T(8,128)(2,1)} %get-tuple-element.25.rest_0_), channel_id=1, source_target_pairs={{0,16},{4,20},{8,24},{12,28},{16,0},{20,4},{24,8},{28,12},{1,17},{... | collective-permute-start | bytes 933896 | tf_op jit(solution)/shard_map/ppermute | solution.py:346
  64.4 25.0 %collective-permute-start.19 = (bf16[64,2432]{1,0:T(8,128)(2,1)}, bf16[64,2432]{1,0:T(8,128)(2,1)S(1)}, u32[]{:S(2)}, u32[]{:S(2)}) collective-permute-start(bf16[64,2432]{1,0:T(8,128)(2,1)} %get-tuple-element.25.rest_0_), channel_id=1, source_target_pairs={{0,24},{4,28},{8,16},{12,20},{16,8},{20,12},{24,0},{28,4},{1,25},{... | collective-permute-start | bytes 933896 | tf_op jit(solution)/shard_map/ppermute | solution.py:346
  67.1 23.4 %collective-permute-start.1 = (bf16[64,2432]{1,0:T(8,128)(2,1)}, bf16[64,2432]{1,0:T(8,128)(2,1)S(1)}, u32[]{:S(2)}, u32[]{:S(2)}) collective-permute-start(bf16[64,2432]{1,0:T(8,128)(2,1)} %get-tuple-element.25.rest_0_), channel_id=1, source_target_pairs={{0,4},{4,0},{8,12},{12,8},{16,20},{20,16},{24,28},{28,24},{1,5},{5... | collective-permute-start | bytes 933896 | tf_op jit(solution)/shard_map/ppermute | solution.py:346
  68.5 22.4 %collective-permute-start = (bf16[64,2432]{1,0:T(8,128)(2,1)}, bf16[64,2432]{1,0:T(8,128)(2,1)S(1)}, u32[]{:S(2)}, u32[]{:S(2)}) collective-permute-start(bf16[64,2432]{1,0:T(8,128)(2,1)} %get-tuple-element.25.rest_0_), channel_id=1, source_target_pairs={{0,2},{1,3},{2,0},{3,1},{4,6},{5,7},{6,4},{7,5},{8,10},{9,11},{10,... | collective-permute-start | bytes 933896 | tf_op jit(solution)/shard_map/ppermute | solution.py:346
  74.6 17.8 %collective-permute-start.7 = (bf16[64,2432]{1,0:T(8,128)(2,1)}, bf16[64,2432]{1,0:T(8,128)(2,1)S(1)}, u32[]{:S(2)}, u32[]{:S(2)}) collective-permute-start(bf16[64,2432]{1,0:T(8,128)(2,1)} %get-tuple-element.25.rest_0_), channel_id=1, source_target_pairs={{0,1},{1,0},{2,3},{3,2},{4,5},{5,4},{6,7},{7,6},{8,9},{9,8},{10,11... | collective-permute-start | bytes 933896 | tf_op jit(solution)/shard_map/ppermute | solution.py:346
  87.9 10.3 %collective-permute-start.5 = (bf16[64,2432]{1,0:T(8,128)(2,1)S(1)}, bf16[64,2432]{1,0:T(8,128)(2,1)S(1)}, u32[]{:S(2)}, u32[]{:S(2)}) collective-permute-start(bf16[64,2432]{1,0:T(8,128)(2,1)S(1)} %collective-permute-done.3.rest_4_), channel_id=1, source_target_pairs={{0,2},{1,3},{2,0},{3,1},{4,6},{5,7},{6,4},{7,5},{8,10},{9,11},{10,... | collective-permute-start | bytes 933896 | tf_op jit(solution)/shard_map/ppermute | solution.py:346
  89.4 10.3 %collective-permute-start.17 = (bf16[64,2432]{1,0:T(8,128)(2,1)S(1)}, bf16[64,2432]{1,0:T(8,128)(2,1)S(1)}, u32[]{:S(2)}, u32[]{:S(2)}) collective-permute-start(bf16[64,2432]{1,0:T(8,128)(2,1)S(1)} %collective-permute-done.15.rest_16_.rest_0_), channel_id=1, source_target_pairs={{0,4},{4,0},{8,12},{12,8},{16,20},{20,16},{24,28},{28,24},{1,5},{5... | collective-permute-start | bytes 933896 | tf_op jit(solution)/shard_map/ppermute | solution.py:346
  90.4 14.4 %collective-permute-start.21 = (bf16[64,2432]{1,0:T(8,128)(2,1)S(1)}, bf16[64,2432]{1,0:T(8,128)(2,1)S(1)}, u32[]{:S(2)}, u32[]{:S(2)}) collective-permute-start(bf16[64,2432]{1,0:T(8,128)(2,1)S(1)} %collective-permute-done.19.rest_20_.rest_4_), channel_id=1, source_target_pairs={{0,2},{1,3},{2,0},{3,1},{4,6},{5,7},{6,4},{7,5},{8,10},{9,11},{10,... | collective-permute-start | bytes 933896 | tf_op jit(solution)/shard_map/ppermute | solution.py:346
  90.9 17.4 %collective-permute-start.2 = (bf16[64,2432]{1,0:T(8,128)(2,1)S(1)}, bf16[64,2432]{1,0:T(8,128)(2,1)S(1)}, u32[]{:S(2)}, u32[]{:S(2)}) collective-permute-start(bf16[64,2432]{1,0:T(8,128)(2,1)S(1)} %collective-permute-done.1.rest_2_), channel_id=1, source_target_pairs={{0,2},{1,3},{2,0},{3,1},{4,6},{5,7},{6,4},{7,5},{8,10},{9,11},{10,... | collective-permute-start | bytes 933896 | tf_op jit(solution)/shard_map/ppermute | solution.py:346
  92.5 15.9 %collective-permute-start.4 = (bf16[64,2432]{1,0:T(8,128)(2,1)S(1)}, bf16[64,2432]{1,0:T(8,128)(2,1)S(1)}, u32[]{:S(2)}, u32[]{:S(2)}) collective-permute-start(bf16[64,2432]{1,0:T(8,128)(2,1)S(1)} %collective-permute-done.3.rest_4_), channel_id=1, source_target_pairs={{0,4},{4,0},{8,12},{12,8},{16,20},{20,16},{24,28},{28,24},{1,5},{5... | collective-permute-start | bytes 933896 | tf_op jit(solution)/shard_map/ppermute | solution.py:346
  98.2 13.6 %collective-permute-start.16 = (bf16[64,2432]{1,0:T(8,128)(2,1)S(1)}, bf16[64,2432]{1,0:T(8,128)(2,1)S(1)}, u32[]{:S(2)}, u32[]{:S(2)}) collective-permute-start(bf16[64,2432]{1,0:T(8,128)(2,1)S(1)} %collective-permute-done.15.rest_16_.rest_0_), channel_id=1, source_target_pairs={{0,2},{1,3},{2,0},{3,1},{4,6},{5,7},{6,4},{7,5},{8,10},{9,11},{10,... | collective-permute-start | bytes 933896 | tf_op jit(solution)/shard_map/ppermute | solution.py:346
  99.7 12.0 %collective-permute-start.20 = (bf16[64,2432]{1,0:T(8,128)(2,1)S(1)}, bf16[64,2432]{1,0:T(8,128)(2,1)}, u32[]{:S(2)}, u32[]{:S(2)}) collective-permute-start(bf16[64,2432]{1,0:T(8,128)(2,1)S(1)} %collective-permute-done.19.rest_20_.rest_4_), channel_id=1, source_target_pairs={{0,4},{4,0},{8,12},{12,8},{16,20},{20,16},{24,28},{28,24},{1,5},{5... | collective-permute-start | bytes 933896 | tf_op jit(solution)/shard_map/ppermute | solution.py:346
  104.8 7.4 %collective-permute-start.11 = (bf16[64,2432]{1,0:T(8,128)(2,1)S(1)}, bf16[64,2432]{1,0:T(8,128)(2,1)S(1)}, u32[]{:S(2)}, u32[]{:S(2)}) collective-permute-start(bf16[64,2432]{1,0:T(8,128)(2,1)S(1)} %collective-permute-done.3.rest_4_), channel_id=1, source_target_pairs={{0,1},{1,0},{2,3},{3,2},{4,5},{5,4},{6,7},{7,6},{8,9},{9,8},{10,11... | collective-permute-start | bytes 933896 | tf_op jit(solution)/shard_map/ppermute | solution.py:346
  108.4 4.2 %collective-permute-start.23 = (bf16[64,2432]{1,0:T(8,128)(2,1)S(1)}, bf16[64,2432]{1,0:T(8,128)(2,1)S(1)}, u32[]{:S(2)}, u32[]{:S(2)}) collective-permute-start(bf16[64,2432]{1,0:T(8,128)(2,1)S(1)} %collective-permute-done.15.rest_16_.rest_0_), channel_id=1, source_target_pairs={{0,1},{1,0},{2,3},{3,2},{4,5},{5,4},{6,7},{7,6},{8,9},{9,8},{10,11... | collective-permute-start | bytes 933896 | tf_op jit(solution)/shard_map/ppermute | solution.py:346
  108.4 5.7 %collective-permute-start.27 = (bf16[64,2432]{1,0:T(8,128)(2,1)S(1)}, bf16[64,2432]{1,0:T(8,128)(2,1)S(1)}, u32[]{:S(2)}, u32[]{:S(2)}) collective-permute-start(bf16[64,2432]{1,0:T(8,128)(2,1)S(1)} %collective-permute-done.19.rest_20_.rest_4_), channel_id=1, source_target_pairs={{0,1},{1,0},{2,3},{3,2},{4,5},{5,4},{6,7},{7,6},{8,9},{9,8},{10,11... | collective-permute-start | bytes 933896 | tf_op jit(solution)/shard_map/ppermute | solution.py:346
  111.7 4.1 %collective-permute-start.8 = (bf16[64,2432]{1,0:T(8,128)(2,1)S(1)}, bf16[64,2432]{1,0:T(8,128)(2,1)S(1)}, u32[]{:S(2)}, u32[]{:S(2)}) collective-permute-start(bf16[64,2432]{1,0:T(8,128)(2,1)S(1)} %collective-permute-done.rest_1_), channel_id=1, source_target_pairs={{0,1},{1,0},{2,3},{3,2},{4,5},{5,4},{6,7},{7,6},{8,9},{9,8},{10,11... | collective-permute-start | bytes 933896 | tf_op jit(solution)/shard_map/ppermute | solution.py:346
  111.7 4.1 %collective-permute-start.9 = (bf16[64,2432]{1,0:T(8,128)(2,1)S(1)}, bf16[64,2432]{1,0:T(8,128)(2,1)S(1)}, u32[]{:S(2)}, u32[]{:S(2)}) collective-permute-start(bf16[64,2432]{1,0:T(8,128)(2,1)S(1)} %collective-permute-done.1.rest_2_), channel_id=1, source_target_pairs={{0,1},{1,0},{2,3},{3,2},{4,5},{5,4},{6,7},{7,6},{8,9},{9,8},{10,11... | collective-permute-start | bytes 933896 | tf_op jit(solution)/shard_map/ppermute | solution.py:346
  112.3 10.3 %collective-permute-start.6 = (bf16[64,2432]{1,0:T(8,128)(2,1)S(1)}, bf16[64,2432]{1,0:T(8,128)(2,1)}, u32[]{:S(2)}, u32[]{:S(2)}) collective-permute-start(bf16[64,2432]{1,0:T(8,128)(2,1)S(1)} %collective-permute-done.5.rest_6_), channel_id=1, source_target_pairs={{0,4},{4,0},{8,12},{12,8},{16,20},{20,16},{24,28},{28,24},{1,5},{5... | collective-permute-start | bytes 933896 | tf_op jit(solution)/shard_map/ppermute | solution.py:346
  112.6 10.0 %collective-permute-start.18 = (bf16[64,2432]{1,0:T(8,128)(2,1)S(1)}, bf16[64,2432]{1,0:T(8,128)(2,1)}, u32[]{:S(2)}, u32[]{:S(2)}) collective-permute-start(bf16[64,2432]{1,0:T(8,128)(2,1)S(1)} %collective-permute-done.17.rest_18_.rest_2_), channel_id=1, source_target_pairs={{0,2},{1,3},{2,0},{3,1},{4,6},{5,7},{6,4},{7,5},{8,10},{9,11},{10,... | collective-permute-start | bytes 933896 | tf_op jit(solution)/shard_map/ppermute | solution.py:346
  114.1 14.2 %collective-permute-start.22 = (bf16[64,2432]{1,0:T(8,128)(2,1)S(1)}, bf16[64,2432]{1,0:T(8,128)(2,1)}, u32[]{:S(2)}, u32[]{:S(2)}) collective-permute-start(bf16[64,2432]{1,0:T(8,128)(2,1)S(1)} %collective-permute-done.21.rest_22_.rest_6_), channel_id=1, source_target_pairs={{0,4},{4,0},{8,12},{12,8},{16,20},{20,16},{24,28},{28,24},{1,5},{5... | collective-permute-start | bytes 933896 | tf_op jit(solution)/shard_map/ppermute | solution.py:346
  115.8 12.6 %collective-permute-start.10 = (bf16[64,2432]{1,0:T(8,128)(2,1)S(1)}, bf16[64,2432]{1,0:T(8,128)(2,1)S(1)}, u32[]{:S(2)}, u32[]{:S(2)}) collective-permute-start(bf16[64,2432]{1,0:T(8,128)(2,1)S(1)} %collective-permute-done.2.rest_3_), channel_id=1, source_target_pairs={{0,1},{1,0},{2,3},{3,2},{4,5},{5,4},{6,7},{7,6},{8,9},{9,8},{10,11... | collective-permute-start | bytes 933896 | tf_op jit(solution)/shard_map/ppermute | solution.py:346
  115.8 13.1 %collective-permute-start.12 = (bf16[64,2432]{1,0:T(8,128)(2,1)S(1)}, bf16[64,2432]{1,0:T(8,128)(2,1)S(1)}, u32[]{:S(2)}, u32[]{:S(2)}) collective-permute-start(bf16[64,2432]{1,0:T(8,128)(2,1)S(1)} %collective-permute-done.4.rest_5_), channel_id=1, source_target_pairs={{0,1},{1,0},{2,3},{3,2},{4,5},{5,4},{6,7},{7,6},{8,9},{9,8},{10,11... | collective-permute-start | bytes 933896 | tf_op jit(solution)/shard_map/ppermute | solution.py:346
  122.6 6.4 %collective-permute-start.13 = (bf16[64,2432]{1,0:T(8,128)(2,1)S(1)}, bf16[64,2432]{1,0:T(8,128)(2,1)S(1)}, u32[]{:S(2)}, u32[]{:S(2)}) collective-permute-start(bf16[64,2432]{1,0:T(8,128)(2,1)S(1)} %collective-permute-done.5.rest_6_), channel_id=1, source_target_pairs={{0,1},{1,0},{2,3},{3,2},{4,5},{5,4},{6,7},{7,6},{8,9},{9,8},{10,11... | collective-permute-start | bytes 933896 | tf_op jit(solution)/shard_map/ppermute | solution.py:346
  122.6 6.8 %collective-permute-start.24 = (bf16[64,2432]{1,0:T(8,128)(2,1)S(1)}, bf16[64,2432]{1,0:T(8,128)(2,1)S(1)}, u32[]{:S(2)}, u32[]{:S(2)}) collective-permute-start(bf16[64,2432]{1,0:T(8,128)(2,1)S(1)} %collective-permute-done.16.rest_17_.rest_1_), channel_id=1, source_target_pairs={{0,1},{1,0},{2,3},{3,2},{4,5},{5,4},{6,7},{7,6},{8,9},{9,8},{10,11... | collective-permute-start | bytes 933896 | tf_op jit(solution)/shard_map/ppermute | solution.py:346
  128.4 1.6 collective-permute-start.25
  128.4 3.0 %collective-permute-start.29 = (bf16[64,2432]{1,0:T(8,128)(2,1)S(1)}, bf16[64,2432]{1,0:T(8,128)(2,1)}, u32[]{:S(2)}, u32[]{:S(2)}) collective-permute-start(bf16[64,2432]{1,0:T(8,128)(2,1)S(1)} %collective-permute-done.21.rest_22_.rest_6_), channel_id=1, source_target_pairs={{0,1},{1,0},{2,3},{3,2},{4,5},{5,4},{6,7},{7,6},{8,9},{9,8},{10,11... | collective-permute-start | bytes 933896 | tf_op jit(solution)/shard_map/ppermute | solution.py:346
  128.9 2.5 collective-permute-start.28
  129.0 2.7 collective-permute-start.14
  129.4 2.7 collective-permute-start.26
  130.0 2.6 collective-permute-start.30
  155.6 31.9 %collective-permute-start.31 = (bf16[512,2304]{1,0:T(8,128)(2,1)}, bf16[512,2304]{1,0:T(8,128)(2,1)}, u32[]{:S(2)}, u32[]{:S(2)}) collective-permute-start(bf16[512,2304]{1,0:T(8,128)(2,1)} %get-tuple-element.27.late_ref.rest_17_), channel_id=1, source_target_pairs={{0,1},{1,0},{2,3},{3,2},{4,5},{5,4},{6,7},{7,6},{8,9},{9,8},{10,11... | collective-permute-start | bytes 7077896 | tf_op jit(solution)/shard_map/ppermute | solution.py:346
  180.4 31.3 %collective-permute-start.37 = (bf16[512,2304]{1,0:T(8,128)(2,1)}, bf16[512,2304]{1,0:T(8,128)(2,1)}, u32[]{:S(2)}, u32[]{:S(2)}) collective-permute-start(bf16[512,2304]{1,0:T(8,128)(2,1)} %get-tuple-element.37), channel_id=1, source_target_pairs={{0,1},{1,0},{2,3},{3,2},{4,5},{5,4},{6,7},{7,6},{8,9},{9,8},{10,11... | collective-permute-start | bytes 7077896 | tf_op jit(solution)/shard_map/ppermute | solution.py:346
  180.9 24.4 %all-to-all-start.2 = ((bf16[8,64,640]{2,1,0:T(8,128)(2,1)}), bf16[8,64,640]{2,1,0:T(8,128)(2,1)}, u32[]{:S(2)}, u32[]{:S(2)}) async-start(bf16[8,64,640]{2,1,0:T(8,128)(2,1)} %shard_map.128.rest_16_), calls=%async_computation.2 | async-start | bytes 1310720 | tf_op jit(solution)/shard_map/all_to_all | solution.py:464
  190.4 19.8 %collective-permute-start.32 = (bf16[128,2304]{1,0:T(8,128)(2,1)}, bf16[128,2304]{1,0:T(8,128)(2,1)}, u32[]{:S(2)}, u32[]{:S(2)}) collective-permute-start(bf16[128,2304]{1,0:T(8,128)(2,1)} %get-tuple-element.29), channel_id=1, source_target_pairs={{0,4},{4,0},{8,12},{12,8},{16,20},{20,16},{24,28},{28,24},{1,5},{5... | collective-permute-start | bytes 1769480 | tf_op jit(solution)/shard_map/ppermute | solution.py:346
  192.4 17.8 %collective-permute-start.33 = (bf16[128,2304]{1,0:T(8,128)(2,1)}, bf16[128,2304]{1,0:T(8,128)(2,1)}, u32[]{:S(2)}, u32[]{:S(2)}) collective-permute-start(bf16[128,2304]{1,0:T(8,128)(2,1)} %get-tuple-element.30), channel_id=1, source_target_pairs={{0,2},{1,3},{2,0},{3,1},{4,6},{5,7},{6,4},{7,5},{8,10},{9,11},{10,... | collective-permute-start | bytes 1769480 | tf_op jit(solution)/shard_map/ppermute | solution.py:346
  213.9 21.6 %collective-permute-start.38 = (bf16[128,2304]{1,0:T(8,128)(2,1)S(1)}, bf16[128,2304]{1,0:T(8,128)(2,1)S(1)}, u32[]{:S(2)}, u32[]{:S(2)}) collective-permute-start(bf16[128,2304]{1,0:T(8,128)(2,1)S(1)} %get-tuple-element.39), channel_id=1, source_target_pairs={{0,4},{4,0},{8,12},{12,8},{16,20},{20,16},{24,28},{28,24},{1,5},{5... | collective-permute-start | bytes 1769480 | tf_op jit(solution)/shard_map/ppermute | solution.py:346
  214.5 21.0 %collective-permute-start.39 = (bf16[128,2304]{1,0:T(8,128)(2,1)S(1)}, bf16[128,2304]{1,0:T(8,128)(2,1)S(1)}, u32[]{:S(2)}, u32[]{:S(2)}) collective-permute-start(bf16[128,2304]{1,0:T(8,128)(2,1)S(1)} %get-tuple-element.40), channel_id=1, source_target_pairs={{0,2},{1,3},{2,0},{3,1},{4,6},{5,7},{6,4},{7,5},{8,10},{9,11},{10,... | collective-permute-start | bytes 1769480 | tf_op jit(solution)/shard_map/ppermute | solution.py:346
  216.0 19.3 %collective-permute-start.34 = (bf16[64,2304]{1,0:T(8,128)(2,1)S(1)}, bf16[64,2304]{1,0:T(8,128)(2,1)S(1)}, u32[]{:S(2)}, u32[]{:S(2)}) collective-permute-start(bf16[64,2304]{1,0:T(8,128)(2,1)S(1)} %get-tuple-element.32.rest_1_), channel_id=1, source_target_pairs={{0,2},{1,3},{2,0},{3,1},{4,6},{5,7},{6,4},{7,5},{8,10},{9,11},{10,... | collective-permute-start | bytes 884744 | tf_op jit(solution)/shard_map/ppermute | solution.py:346
  216.6 18.8 %collective-permute-start.35 = (bf16[64,2304]{1,0:T(8,128)(2,1)S(1)}, bf16[64,2304]{1,0:T(8,128)(2,1)S(1)}, u32[]{:S(2)}, u32[]{:S(2)}) collective-permute-start(bf16[64,2304]{1,0:T(8,128)(2,1)S(1)} %get-tuple-element.33), channel_id=1, source_target_pairs={{0,4},{4,0},{8,12},{12,8},{16,20},{20,16},{24,28},{28,24},{1,5},{5... | collective-permute-start | bytes 884744 | tf_op jit(solution)/shard_map/ppermute | solution.py:346
  235.8 7.8 %collective-permute-start.40 = (bf16[64,2304]{1,0:T(8,128)(2,1)S(1)}, bf16[64,2304]{1,0:T(8,128)(2,1)S(1)}, u32[]{:S(2)}, u32[]{:S(2)}) collective-permute-start(bf16[64,2304]{1,0:T(8,128)(2,1)S(1)} %get-tuple-element.42), channel_id=1, source_target_pairs={{0,2},{1,3},{2,0},{3,1},{4,6},{5,7},{6,4},{7,5},{8,10},{9,11},{10,... | collective-permute-start | bytes 884744 | tf_op jit(solution)/shard_map/ppermute | solution.py:346
  237.4 7.4 %collective-permute-start.41 = (bf16[64,2304]{1,0:T(8,128)(2,1)S(1)}, bf16[64,2304]{1,0:T(8,128)(2,1)S(1)}, u32[]{:S(2)}, u32[]{:S(2)}) collective-permute-start(bf16[64,2304]{1,0:T(8,128)(2,1)S(1)} %get-tuple-element.43), channel_id=1, source_target_pairs={{0,4},{4,0},{8,12},{12,8},{16,20},{20,16},{24,28},{28,24},{1,5},{5... | collective-permute-start | bytes 884744 | tf_op jit(solution)/shard_map/ppermute | solution.py:346
  245.0 12.9 %collective-permute-start.42 = (bf16[64,2304]{1,0:T(8,128)(2,1)S(1)}, bf16[64,2304]{1,0:T(8,128)(2,1)S(1)}, u32[]{:S(2)}, u32[]{:S(2)}) collective-permute-start(bf16[64,2304]{1,0:T(8,128)(2,1)S(1)} %get-tuple-element.45), channel_id=1, source_target_pairs={{0,8},{4,12},{8,0},{12,4},{16,24},{20,28},{24,16},{28,20},{1,9},{5... | collective-permute-start | bytes 884744 | tf_op jit(solution)/shard_map/ppermute | solution.py:346
  245.8 15.2 %collective-permute-start.36 = (bf16[64,2304]{1,0:T(8,128)(2,1)S(1)}, bf16[64,2304]{1,0:T(8,128)(2,1)S(1)}, u32[]{:S(2)}, u32[]{:S(2)}) collective-permute-start(bf16[64,2304]{1,0:T(8,128)(2,1)S(1)} %get-tuple-element.35.rest_2_), channel_id=1, source_target_pairs={{0,8},{4,12},{8,0},{12,4},{16,24},{20,28},{24,16},{28,20},{1,9},{5... | collective-permute-start | bytes 884744 | tf_op jit(solution)/shard_map/ppermute | solution.py:346
  257.9 10.4 %collective-permute-start.43 = (bf16[64,2304]{1,0:T(8,128)(2,1)S(1)}, bf16[64,2304]{1,0:T(8,128)(2,1)S(1)}, u32[]{:S(2)}, u32[]{:S(2)}) collective-permute-start(bf16[64,2304]{1,0:T(8,128)(2,1)S(1)} %add_convert_fusion.1), channel_id=1, source_target_pairs={{0,16},{4,20},{8,24},{12,28},{16,0},{20,4},{24,8},{28,12},{1,17},{... | collective-permute-start | bytes 884744 | tf_op jit(solution)/shard_map/ppermute | solution.py:346
  (33 other events, 805.3 us)

commit v6 on v5

--- a/solution.py
+++ b/solution.py
@@ -219,127 +219,158 @@
     return place
 
 
-def chunk_kernel(local, pieces, waits, first_ref, wg_hbm, wu_hbm, wd_hbm, *rest):
-    piece_refs = rest[:pieces]
-    keep_hbm, send_hbm, x, wg, wu, wd, rows_of, y, out, piece_sem, weight_sem, out_sem = rest[pieces + waits :]
-    rows_dev = piece_refs[0].shape[0]
-    width = wd.shape[2]
-    groups = pieces // 4
-    tokens = 4 * rows_dev
-    rows = 4 * CAP
-    piece_copies = [
-        pltpu.make_async_copy(ref, x.at[pl.ds(i * rows_dev, rows_dev), :], piece_sem.at[i])
-        for i, ref in enumerate(piece_refs)
-    ]
-    weight_copies = [
+def facts_by_lane(x):
+    unit = lax.broadcasted_iota(jnp.int32, (8, 128), 0) == lax.broadcasted_iota(jnp.int32, (8, 128), 1)
+    return dot_t(unit.astype(jnp.float32).astype(jnp.bfloat16), x)
+
+
+def select_kernel(local, rows_dev, count, bases_ref, *refs):
+    piece_refs, own_ref, sib_ref = refs[:count], refs[-2], refs[-1]
+    width = own_ref.shape[2]
+    tokens, rows = 4 * rows_dev, 4 * CAP
+    shift = lax.broadcasted_iota(jnp.int32, (1, tokens), 1) // rows_dev * CAP
+    row_id = lax.broadcasted_iota(jnp.int32, (rows, tokens), 0)
+    for g in range(len(piece_refs) // 4):
+        x = jnp.concatenate([p[...] for p in piece_refs[4 * g : 4 * g + 4]], axis=0)
+        facts = facts_by_lane(x[:, width:])
+        picks = []
+        for core in range(2):
+            for e in range(local):
+                base = (bases_ref[core] + e) * CAP
+                hit = row_id == places_of([facts[j : j + 1] for j in range(2)], base, shift)
+                picks.append(hit.astype(jnp.float32))
+        picks = jnp.concatenate(picks, axis=0).astype(jnp.bfloat16)
+        chosen = jnp.dot(picks, x[:, :width], preferred_element_type=jnp.float32).astype(jnp.bfloat16)
+        for e in range(local):
+            own_ref[e, g * rows : (g + 1) * rows, :] = chosen[e * rows : (e + 1) * rows]
+            sib_ref[e, g * rows : (g + 1) * rows, :] = chosen[(local + e) * rows : (local + e + 1) * rows]
+
+
+def select_rows(pieces, bases, local, waits=()):
+    rows_dev, wide = pieces[0].shape
+    width = wide - 128
+    rows = len(pieces) * CAP
+    out = jax.ShapeDtypeStruct((local, rows, width), jnp.bfloat16)
+    vmem = pl.BlockSpec(memory_space=pltpu.VMEM)
+    return pl.pallas_call(
+        functools.partial(select_kernel, local, rows_dev, len(pieces)),
+        out_shape=(out, out),
+        in_specs=[pl.BlockSpec(memory_space=pltpu.SMEM)]
+        + [vmem] * len(pieces)
+        + [pl.BlockSpec(memory_space=pl.ANY)] * len(waits),
+        out_specs=(vmem, vmem),
+        compiler_params=pltpu.CompilerParams(vmem_limit_bytes=28 * 1024 * 1024),
+        cost_estimate=pl.CostEstimate(
+            flops=16 * local * CAP * rows_dev * len(pieces) * width,
+            bytes_accessed=2 * len(pieces) * rows_dev * wide + 4 * local * rows * width,
+            transcendentals=0,
+        ),
+    )(bases, *pieces, *waits)
+
+
+def rows_kernel(local, waits, own_ref, got_ref, wg_hbm, wu_hbm, wd_hbm, *rest):
+    y_own_ref, y_sib_ref, wg, wu, wd, weight_sem = rest[waits:]
+    half = own_ref.shape[1]
+    copies = [
         [
             pltpu.make_async_copy(source.at[e], target.at[e], weight_sem.at[3 * e + i])
             for i, (source, target) in enumerate(((wg_hbm, wg), (wu_hbm, wu), (wd_hbm, wd)))
         ]
         for e in range(local)
     ]
-    for copy in piece_copies:
-        copy.start()
-    for copies in weight_copies:
-        for copy in copies:
+    for group in copies:
+        for copy in group:
             copy.start()
-
-    unit = lax.broadcasted_iota(jnp.int32, (8, 128), 0) == lax.broadcasted_iota(jnp.int32, (8, 128), 1)
-    unit = unit.astype(jnp.float32).astype(jnp.bfloat16)
-    shift = lax.broadcasted_iota(jnp.int32, (1, tokens), 1) // rows_dev * CAP
-    row_id = lax.broadcasted_iota(jnp.int32, (rows, tokens), 0)
-    weights = [[] for _ in range(local)]
-    for g in range(groups):
-        for copy in piece_copies[4 * g : 4 * g + 4]:
-            copy.wait()
-        here = slice(g * tokens, (g + 1) * tokens)
-        facts = dot_t(unit, x[here, width:])
-        picks = []
-        for e in range(local):
-            base = (first_ref[0] + e) * CAP
-            pick, weight = None, None
-            for j in range(2):
-                hit = row_id == places_of([facts[j : j + 1]], base, shift)
-                gate = facts[2 + j : 3 + j] + facts[4 + j : 5 + j] + facts[6 + j : 7 + j]
-                gate = jnp.where(hit, gate, 0.0)
-                pick = hit if pick is None else pick | hit
-                weight = gate if weight is None else weight + gate
-            picks.append(pick.astype(jnp.float32))
-            weights[e].append(jnp.sum(weight, axis=1, keepdims=True))
-        picks = jnp.concatenate(picks, axis=0).astype(jnp.bfloat16)
-        chosen = jnp.dot(picks, x[here, :width], preferred_element_type=jnp.float32)
-        for e in range(local):
-            rows_of[e, g * rows : (g + 1) * rows, :] = chosen[e * rows : (e + 1) * rows].astype(jnp.bfloat16)
-
     for e in range(local):
-        chosen = rows_of[e]
-        weight_copies[e][0].wait()
-        gate = dot_t(chosen, wg[e])
-        weight_copies[e][1].wait()
-        upper = dot_t(chosen, wu[e])
+        rows = jnp.concatenate([own_ref[e], got_ref[e]], axis=0)
+        copies[e][0].wait()
+        gate = dot_t(rows, wg[e])
+        copies[e][1].wait()
+        upper = dot_t(rows, wu[e])
         hidden = (gate / (1.0 + jnp.exp(-gate)) * upper).astype(jnp.bfloat16)
-        weight_copies[e][2].wait()
-        result = jnp.dot(hidden, wd[e], preferred_element_type=jnp.float32)
-        result = (result * jnp.concatenate(weights[e], axis=0)).astype(jnp.bfloat16)
-        for g in range(groups):
-            y[g, e * rows : (e + 1) * rows, :] = result[g * rows : (g + 1) * rows]
-
-    shift = lax.broadcasted_iota(jnp.int32, (tokens, 1), 0) // rows_dev * CAP
-    lane = lax.broadcasted_iota(jnp.int32, (tokens, local * rows), 1)
-    out_copies = []
-    for g in reversed(range(groups)):
-        here = slice(g * tokens, (g + 1) * tokens)
-        facts = x[here, width:].astype(jnp.float32)
-        put = None
-        for e in range(local):
-            base = (first_ref[0] + e) * CAP
-            hit = lane == places_of([facts[:, j : j + 1] for j in range(2)], base, shift + e * rows)
-            put = hit if put is None else put | hit
-        put = put.astype(jnp.float32).astype(jnp.bfloat16)
-        out[here, :] = jnp.dot(put, y[g], preferred_element_type=jnp.float32).astype(jnp.bfloat16)
-        target, at = (keep_hbm, g) if g < groups // 2 else (send_hbm, g - groups // 2)
-        copy = pltpu.make_async_copy(
-            out.at[pl.ds(g * tokens, tokens), :], target.at[pl.ds(at * tokens, tokens), :], out_sem.at[g]
-        )
-        copy.start()
-        out_copies.append(copy)
-    for copy in out_copies:
-        copy.wait()
-
-
-def chunk_experts(pieces, w_gate, w_up, w_down, first, waits):
+        copies[e][2].wait()
+        y = jnp.dot(hidden, wd[e], preferred_element_type=jnp.float32).astype(jnp.bfloat16)
+        y_own_ref[e] = y[:half]
+        y_sib_ref[e] = y[half:]
+
+
+def expert_rows(own, got, w_gate, w_up, w_down, waits):
     local, hidden, width = w_gate.shape
-    rows_dev, wide = pieces[0].shape
-    tokens = rows_dev * len(pieces)
-    rows = len(pieces) * CAP
-    groups = len(pieces) // 4
-    half = jax.ShapeDtypeStruct((tokens // 2, width), jnp.bfloat16)
-    anywhere = pl.BlockSpec(memory_space=pl.ANY)
+    rows = 2 * own.shape[1]
+    out = jax.ShapeDtypeStruct(own.shape, jnp.bfloat16)
+    vmem = pl.BlockSpec(memory_space=pltpu.VMEM)
     weights = pltpu.VMEM((local, hidden, width), jnp.bfloat16)
     return pl.pallas_call(
-        functools.partial(chunk_kernel, local, len(pieces), len(waits)),
-        out_shape=(half, half),
-        in_specs=[pl.BlockSpec(memory_space=pltpu.SMEM)] + [anywhere] * (3 + len(pieces) + len(waits)),
-        out_specs=(anywhere, anywhere),
-        scratch_shapes=[
-            pltpu.VMEM((tokens, wide), jnp.bfloat16),
-            weights,
-            weights,
-            weights,
-            pltpu.VMEM((local, rows, width), jnp.bfloat16),
-            pltpu.VMEM((groups, local * rows // groups, width), jnp.bfloat16),
-            pltpu.VMEM((tokens, width), jnp.bfloat16),
-            pltpu.SemaphoreType.DMA((len(pieces),)),
-            pltpu.SemaphoreType.DMA((3 * local,)),
-            pltpu.SemaphoreType.DMA((groups,)),
-        ],
-        compiler_params=pltpu.CompilerParams(vmem_limit_bytes=58 * 1024 * 1024),
+        functools.partial(rows_kernel, local, len(waits)),
+        out_shape=(out, out),
+        in_specs=[vmem, vmem] + [pl.BlockSpec(memory_space=pl.ANY)] * (3 + len(waits)),
+        out_specs=(vmem, vmem),
+        scratch_shapes=[weights, weights, weights, pltpu.SemaphoreType.DMA((3 * local,))],
+        compiler_params=pltpu.CompilerParams(vmem_limit_bytes=44 * 1024 * 1024),
         cost_estimate=pl.CostEstimate(
             flops=6 * local * rows * width * hidden,
-            bytes_accessed=6 * local * width * hidden + 4 * tokens * width,
+            bytes_accessed=6 * local * width * hidden + 4 * local * rows * width,
             transcendentals=local * rows * hidden,
         ),
-    )(first, w_gate, w_up, w_down, *pieces, *waits)
+    )(own, got, w_gate, w_up, w_down, *waits)
+
+
+def put_kernel(local, rows_dev, count, waits, bases_ref, y_own_ref, y_got_ref, *rest):
+    fact_refs = rest[:count]
+    kept_ref, *send_refs = rest[count + waits :]
+    tokens, rows = 4 * rows_dev, 4 * CAP
+    total = 2 * local * rows
+    shift_lane = lax.broadcasted_iota(jnp.int32, (1, tokens), 1) // rows_dev * CAP
+    shift_row = lax.broadcasted_iota(jnp.int32, (tokens, 1), 0) // rows_dev * CAP
+    row_id = lax.broadcasted_iota(jnp.int32, (rows, tokens), 0)
+    lane = lax.broadcasted_iota(jnp.int32, (tokens, total), 1)
+    for g in range(count // 4):
+        facts = jnp.concatenate([f[...] for f in fact_refs[4 * g : 4 * g + 4]], axis=0)
+        by_lane = facts_by_lane(facts)
+        by_row = facts.astype(jnp.float32)
+        here = slice(g * rows, (g + 1) * rows)
+        weighed, put = [], None
+        for core, y_ref in enumerate((y_own_ref, y_got_ref)):
+            for e in range(local):
+                base = (bases_ref[core] + e) * CAP
+                weight = jnp.zeros((rows, tokens), jnp.float32)
+                for j in range(2):
+                    hit = row_id == places_of([by_lane[j : j + 1]], base, shift_lane)
+                    gate = by_lane[2 + j : 3 + j] + by_lane[4 + j : 5 + j] + by_lane[6 + j : 7 + j]
+                    weight = weight + jnp.where(hit, gate, 0.0)
+                weight = jnp.sum(weight, axis=1, keepdims=True)
+                weighed.append((y_ref[e, here, :].astype(jnp.float32) * weight).astype(jnp.bfloat16))
+                first = (core * local + e) * rows
+                hit = lane == places_of([by_row[:, j : j + 1] for j in range(2)], base, shift_row + first)
+                put = hit if put is None else put | hit
+        put = put.astype(jnp.float32).astype(jnp.bfloat16)
+        out = jnp.dot(put, jnp.concatenate(weighed, axis=0), preferred_element_type=jnp.float32)
+        out = out.astype(jnp.bfloat16)
+        kept_ref[g * tokens // 2 : (g + 1) * tokens // 2, :] = out[: tokens // 2]
+        send_refs[g][...] = out[tokens // 2 :]
+
+
+def put_rows(y_own, y_got, pieces, bases, waits):
+    local, _, width = y_own.shape
+    rows_dev = pieces[0].shape[0]
+    planes = len(pieces) // 4
+    vmem = pl.BlockSpec(memory_space=pltpu.VMEM)
+    shape = lambda n: jax.ShapeDtypeStruct((n, width), jnp.bfloat16)
+    out = pl.pallas_call(
+        functools.partial(put_kernel, local, rows_dev, len(pieces), len(waits)),
+        out_shape=(shape(2 * planes * rows_dev),) + (shape(2 * rows_dev),) * planes,
+        in_specs=[pl.BlockSpec(memory_space=pltpu.SMEM), vmem, vmem]
+        + [vmem] * len(pieces)
+        + [pl.BlockSpec(memory_space=pl.ANY)] * len(waits),
+        out_specs=(vmem,) * (1 + planes),
+        compiler_params=pltpu.CompilerParams(vmem_limit_bytes=28 * 1024 * 1024),
+        cost_estimate=pl.CostEstimate(
+            flops=16 * local * CAP * rows_dev * len(pieces) * width,
+            bytes_accessed=8 * local * len(pieces) * CAP * width,
+            transcendentals=0,
+        ),
+    )(bases, y_own, y_got, *[p[:, width:] for p in pieces], *waits)
+    return out[0], out[1:]
 
 
 def swap(a, axis, size, distance):
@@ -377,34 +408,42 @@
     return out[0], out[1:]
 
 
-def exchange_experts(piece, w_gate, w_up, w_down, first, n_seq, n_exp, late_work):
+def exchange_experts(piece, w_gate, w_up, w_down, n_seq, n_exp, late_work):
     x = lambda a: swap(a, "seq", n_seq, 1)
     y = lambda a: swap(a, "exp", n_exp, 2)
     core = lambda a: swap(a, "exp", n_exp, 1)
     z = lambda a, k: swap(a, "seq", n_seq, 2 * k)
-    starts = [piece] + [z(piece, k) for k in range(1, 4)]
+    local = w_gate.shape[0]
+    me = lax.axis_index("exp").astype(jnp.int32)
+    bases = jnp.stack([me, me ^ 1]) * local
+    starts = [piece, z(piece, 1), z(piece, 2)]
+    starts.append(z(starts[2], 1))
 
     def gather(k):
         near = []
         for start, (f, g) in ((starts[k], (x, y)), (starts[k + 1], (y, x))):
             by_f = f(start)
             near += [start, g(start), by_f, g(by_f)]
-        return near + [core(p) for p in near]
-
-    experts_of = lambda pieces, waits: chunk_experts(pieces, w_gate, w_up, w_down, first, waits)
-    chunk_a, chunk_b = gather(0), gather(2)
-    keep_a, send_a = experts_of(chunk_a, chunk_b)
-    pages, other = late_work(send_a)
-    keep_b, send_b = experts_of(chunk_b, [pages, send_a])
-    keep_a, (fx_a, fy_a) = fold(keep_a, [core(send_a)], 2)
-    got_b = core(send_b)
+        return near
+
+    near_a, near_b = gather(0), gather(2)
+    own_a, sib_a = select_rows(near_a, bases, local, starts[2:])
+    got_a = core(sib_a)
+    own_b, sib_b = select_rows(near_b, bases, local)
+    got_b = core(sib_b)
+    own_a, sib_a = expert_rows(own_a, got_a, w_gate, w_up, w_down, [sib_b])
+    pages, other = late_work(sib_a)
+    got_a = core(sib_a)
+    own_b, sib_b = expert_rows(own_b, got_b, w_gate, w_up, w_down, [pages, sib_a])
+    got_b = core(sib_b)
+    keep_a, (fx_a, fy_a) = put_rows(own_a, got_a, near_a, bases, [sib_b])
     keep_a, (gy_a, gx_a) = fold(keep_a, [x(fx_a), y(fy_a)], 2)
-    keep_b, (fx_b, fy_b) = fold(keep_b, [got_b], 2, [gy_a, other])
+    keep_b, (fx_b, fy_b) = put_rows(own_b, got_b, near_b, bases, [other])
     keep_a, (z_a,) = fold(keep_a, [y(gy_a), x(gx_a)], 1)
     keep_b, (gy_b, gx_b) = fold(keep_b, [x(fx_b), y(fy_b)], 2, [z_a])
-    got_a = z(z_a, 1)
+    back_a = z(z_a, 1)
     keep_b, (z_b,) = fold(keep_b, [y(gy_b), x(gx_b)], 1)
-    mine = keep_a.astype(jnp.float32) + got_a.astype(jnp.float32)
+    mine = keep_a.astype(jnp.float32) + back_a.astype(jnp.float32)
     over_z = (keep_b.astype(jnp.float32) + z(z_b, 1).astype(jnp.float32)).astype(jnp.bfloat16)
     return mine + z(over_z, 2).astype(jnp.float32), other
 
@@ -465,7 +504,7 @@
         return pages, join_pages(sent, share, offsets, span)
 
     if (n_seq, n_exp) == (8, 4):
-        mixture, cache = exchange_experts(piece, w_gate, w_up, w_down, first, n_seq, n_exp, fill_cache)
+        mixture, cache = exchange_experts(piece, w_gate, w_up, w_down, n_seq, n_exp, fill_cache)
     else:
         _, cache = fill_cache(piece)
         blocks = n_seq * n_exp

time: 270 us -> 274 us (1.015)
  local copies, waits for them, and re-layouts: 6.85 us -> 42.8 us
  waiting for transfers between devices: 139 us -> 117 us
  Pallas kernels: 64.5 us -> 57.9 us
  starting transfers between devices: 54 us -> 50 us
    unnamed x90 -> x102, local copies, waits for them, and re-layouts: 2.39 us -> 21.9 us
    slice x0 -> x16, local copies, waits for them, and re-layouts: none -> 15.7 us  [put_rows(): p[:, width:]]
    all_to_all x1, waiting for transfers between devices: 11.4 us -> 0.01 us  [fill_cache(): sent = lax.all_to_all(pages, 'seq', split_axis=0, concat_axis=0, tiled=True)]
    ppermute x44 -> x30, waiting for transfers between devices: 92.8 us -> 81.4 us  [swap(): return lax.ppermute(a, axis, [(i, i ^ distance) for i in range(size)])]
    pallas_call x6 -> x4, Pallas kernels: 7.08 us -> 2.06 us  [fold(): pl.pallas_call(functools.partial(fold_kernel, groups, len(gots), len(wait...]
    ppermute x44 -> x30, starting transfers between devices: 36.5 us -> 34.6 us  [swap(): return lax.ppermute(a, axis, [(i, i ^ distance) for i in range(size)])]
    pallas_call x2 -> x6, Pallas kernels: 45.2 us -> 43.5 us  [the longest x2 29.6 us: expert_rows(): pl.pallas_call(functools.partial(rows_kernel, local, len(waits)), out_sha...]
  transfers between devices with their start and end apart: 47 -> 33, of which waited for: 22 -> 16; matrix products, arithmetic and copies ran while one was open for 1% -> 7% of each run, Pallas kernels for 12% -> 18%
where the time goes in v6:
time: 274 us; the launch traced here: 272 us
  waiting for transfers between devices  117 us (43%)
  Pallas kernels  57.9 us (21%)
  starting transfers between devices  50 us (18%)
  local copies, waits for them, and re-layouts  42.8 us (16%)
  other arithmetic  3.38 us (1%)
    ppermute x30, waiting for transfers between devices, swap(): return lax.ppermute(a, axis, [(i, i ^ distance) for i in range(size)])  81.4 us
    ppermute x30, starting transfers between devices, swap(): return lax.ppermute(a, axis, [(i, i ^ distance) for i in range(size)])  34.6 us
    pallas_call x2, Pallas kernels, expert_rows(): pl.pallas_call(functools.partial(rows_kernel, local, len(waits)), out_sha...  29.6 us
    all_to_all x1, waiting for transfers between devices, body(): lax.all_to_all(packed, 'seq', split_axis=0, concat_axis=0, tiled=True)  24.8 us
    unnamed x102, local copies, waits for them, and re-layouts  21.9 us
    slice x16, local copies, waits for them, and re-layouts, put_rows(): p[:, width:]  15.7 us
    all_to_all x1, waiting for transfers between devices, body(): lax.all_to_all(context.reshape(n_seq, rows_dev, span), 'seq', split_axis=...  10.4 us
    pallas_call x2, Pallas kernels, put_rows(): pl.pallas_call(functools.partial(put_kernel, local, rows_dev, len(pieces)...  8.84 us
  transfers between devices with their start and end apart: 33, of which 16 were waited for; matrix products, arithmetic and copies ran while one was open for 7% of the time, Pallas kernels for 18%

profile of v6, /device:TPU:0, one launch (start us, length us, event | category | flops | bytes accessed | tf_op | source)
XLA Modules:
  0.0 271.9 jit_solution(14209944414105294265)
XLA Ops:
  7.6 2.3 fusion.3
  12.2 7.3 %all-to-all-start = ((bf16[8,64,960]{2,1,0:T(8,128)(2,1)}), bf16[8,64,960]{2,1,0:T(8,128)(2,1)S(1)}, u32[]{:S(2)}, u32[]{:S(2)}) async-start(bf16[8,64,960]{2,1,0:T(8,128)(2,1)} %pad_maximum_fusion), calls=%async_computation | async-start | bytes 2097152 | tf_op jit(solution)/shard_map/all_to_all | solution.py:483
  20.4 24.8 %all-to-all-done = bf16[8,64,960]{2,1,0:T(8,128)(2,1)S(1)} async-done(((bf16[8,64,960]{2,1,0:T(8,128)(2,1)}), bf16[8,64,960]{2,1,0:T(8,128)(2,1)S(1)}, u32[]{:S(2)}, u32[]{:S(2)}) %all-to-all-start) | async-done | bytes 983072 | tf_op jit(solution)/shard_map/all_to_all | solution.py:483
  45.2 5.6 %shard_map.122 = bf16[512,320]{1,0:T(8,128)(2,1)} custom-call(bf16[512,960]{1,0:T(8,128)(2,1)S(1)} %bitcast.118, s32[1,512]{1,0:T(1,128)S(1)} %copy-done.13, s32[512,1]{1,0:T(8,128)S(1)} %copy.35.seg_col_ref), custom_call_target="tpu_custom_call" | custom-call | flops 335544320 | bytes 1310720 | tf_op jit(solution)/shard_map/pallas_call | solution.py:55
  50.8 3.6 %all-to-all-start.1 = ((bf16[8,64,320]{2,1,0:T(8,128)(2,1)}), bf16[8,64,320]{2,1,0:T(8,128)(2,1)S(1)}, u32[]{:S(2)}, u32[]{:S(2)}) async-start(bf16[8,64,320]{2,1,0:T(8,128)(2,1)} %bitcast.29), calls=%async_computation.1 | async-start | bytes 786432 | tf_op jit(solution)/shard_map/all_to_all | solution.py:486
  55.9 10.4 %all-to-all-done.1.context_ref = bf16[8,64,320]{2,1,0:T(8,128)(2,1)S(1)} async-done(((bf16[8,64,320]{2,1,0:T(8,128)(2,1)}), bf16[8,64,320]{2,1,0:T(8,128)(2,1)S(1)}, u32[]{:S(2)}, u32[]{:S(2)}) %all-to-all-start.1) | async-done | bytes 327712 | tf_op jit(solution)/shard_map/all_to_all | solution.py:486
  67.0 2.2 shard_map.123
  70.9 1.7 collective-permute-start.1
  72.7 9.9 %collective-permute-done.3.refs_4_ = bf16[64,2432]{1,0:T(8,128)(2,1)S(1)} collective-permute-done((bf16[64,2432]{1,0:T(8,128)(2,1)}, bf16[64,2432]{1,0:T(8,128)(2,1)S(1)}, u32[]{:S(2)}, u32[]{:S(2)}) %collective-permute-start.3) | collective-permute-done | bytes 311328 | tf_op jit(solution)/shard_map/ppermute | solution.py:377
  82.6 1.5 collective-permute-start.5
  84.7 2.9 %collective-permute-start.4 = (bf16[64,2432]{1,0:T(8,128)(2,1)S(1)}, bf16[64,2432]{1,0:T(8,128)(2,1)S(1)}, u32[]{:S(2)}, u32[]{:S(2)}) collective-permute-start(bf16[64,2432]{1,0:T(8,128)(2,1)S(1)} %collective-permute-done.3.refs_4_), channel_id=1, source_target_pairs={{0,4},{4,0},{8,12},{12,8},{16,20},{20,16},{24,28},{28,24},{1,5},{5... | collective-permute-start | bytes 933896 | tf_op jit(solution)/shard_map/ppermute | solution.py:377
  87.6 1.6 collective-permute-start.2
  89.2 3.7 %collective-permute-done.5.refs_6_ = bf16[64,2432]{1,0:T(8,128)(2,1)S(1)} collective-permute-done((bf16[64,2432]{1,0:T(8,128)(2,1)S(1)}, bf16[64,2432]{1,0:T(8,128)(2,1)S(1)}, u32[]{:S(2)}, u32[]{:S(2)}) %collective-permute-start.5) | collective-permute-done | bytes 311328 | tf_op jit(solution)/shard_map/ppermute | solution.py:377
  92.9 2.9 %collective-permute-start.6 = (bf16[64,2432]{1,0:T(8,128)(2,1)S(1)}, bf16[64,2432]{1,0:T(8,128)(2,1)S(1)}, u32[]{:S(2)}, u32[]{:S(2)}) collective-permute-start(bf16[64,2432]{1,0:T(8,128)(2,1)S(1)} %collective-permute-done.5.refs_6_), channel_id=1, source_target_pairs={{0,4},{4,0},{8,12},{12,8},{16,20},{20,16},{24,28},{28,24},{1,5},{5... | collective-permute-start | bytes 933896 | tf_op jit(solution)/shard_map/ppermute | solution.py:377
  96.0 3.6 %collective-permute-done.refs_1_ = bf16[64,2432]{1,0:T(8,128)(2,1)S(1)} collective-permute-done((bf16[64,2432]{1,0:T(8,128)(2,1)}, bf16[64,2432]{1,0:T(8,128)(2,1)S(1)}, u32[]{:S(2)}, u32[]{:S(2)}) %collective-permute-start) | collective-permute-done | bytes 311328 | tf_op jit(solution)/shard_map/ppermute | solution.py:377
  99.6 3.9 %collective-permute-done.2.refs_3_ = bf16[64,2432]{1,0:T(8,128)(2,1)S(1)} collective-permute-done((bf16[64,2432]{1,0:T(8,128)(2,1)S(1)}, bf16[64,2432]{1,0:T(8,128)(2,1)S(1)}, u32[]{:S(2)}, u32[]{:S(2)}) %collective-permute-start.2) | collective-permute-done | bytes 311328 | tf_op jit(solution)/shard_map/ppermute | solution.py:377
  104.6 1.9 shard_map.124
  106.6 3.8 %collective-permute-start.11 = (bf16[64,2432]{1,0:T(8,128)(2,1)S(1)}, bf16[64,2432]{1,0:T(8,128)(2,1)S(1)}, u32[]{:S(2)}, u32[]{:S(2)}) collective-permute-start(bf16[64,2432]{1,0:T(8,128)(2,1)S(1)} %collective-permute-done.7.refs_8_.refs_0_), channel_id=1, source_target_pairs={{0,4},{4,0},{8,12},{12,8},{16,20},{20,16},{24,28},{28,24},{1,5},{5... | collective-permute-start | bytes 933896 | tf_op jit(solution)/shard_map/ppermute | solution.py:377
  110.4 1.6 collective-permute-start.14
  112.5 6.1 %collective-permute-done.11.refs_2_ = bf16[64,2432]{1,0:T(8,128)(2,1)S(1)} collective-permute-done((bf16[64,2432]{1,0:T(8,128)(2,1)S(1)}, bf16[64,2432]{1,0:T(8,128)(2,1)S(1)}, u32[]{:S(2)}, u32[]{:S(2)}) %collective-permute-start.11) | collective-permute-done | bytes 311328 | tf_op jit(solution)/shard_map/ppermute | solution.py:377
  118.6 1.5 collective-permute-start.12
  120.6 1.5 collective-permute-start.15
  122.1 5.2 %collective-permute-done.10.refs_1_ = bf16[64,2432]{1,0:T(8,128)(2,1)S(1)} collective-permute-done((bf16[64,2432]{1,0:T(8,128)(2,1)S(1)}, bf16[64,2432]{1,0:T(8,128)(2,1)S(1)}, u32[]{:S(2)}, u32[]{:S(2)}) %collective-permute-start.10) | collective-permute-done | bytes 311328 | tf_op jit(solution)/shard_map/ppermute | solution.py:377
  127.3 5.9 %collective-permute-done.12.refs_3_ = bf16[64,2432]{1,0:T(8,128)(2,1)S(1)} collective-permute-done((bf16[64,2432]{1,0:T(8,128)(2,1)S(1)}, bf16[64,2432]{1,0:T(8,128)(2,1)S(1)}, u32[]{:S(2)}, u32[]{:S(2)}) %collective-permute-start.12) | collective-permute-done | bytes 311328 | tf_op jit(solution)/shard_map/ppermute | solution.py:377
  133.2 3.1 %shard_map.125 = (bf16[2,192,2304]{2,1,0:T(8,128)(2,1)S(1)}, bf16[2,192,2304]{2,1,0:T(8,128)(2,1)}) custom-call(s32[2]{0:T(128)S(1)} %add_multiply_fusion.bases_ref, bf16[64,2432]{1,0:T(8,128)(2,1)S(1)} %collective-permute-done.7.refs_8_.refs_0_, bf16[64,2432]{1,0:T(8,128)(2,1)S(1)} %collective-permute-done.10.refs_1_, ...), custom_call_target="tpu_custom_call" | custom-call | flops 905969664 | bytes 6029312 | tf_op jit(solution)/shard_map/pallas_call | solution.py:255
  138.3 14.8 %shard_map.126 = (bf16[2,192,2304]{2,1,0:T(8,128)(2,1)S(1)}, bf16[2,192,2304]{2,1,0:T(8,128)(2,1)}) custom-call(bf16[2,192,2304]{2,1,0:T(8,128)(2,1)S(1)} %get-tuple-element.30.own_ref, bf16[2,192,2304]{2,1,0:T(8,128)(2,1)S(1)} %collective-permute-done.9.got_ref, bf16[2,720,2304]{2,1,0:T(8,128)(2,1)} %bitcast.132, bf16[2,720,2304]{2,1,0:T(8,128)(2,1)} %bitcast.134, ...), custom_call_target="tpu_custom_call" | custom-call | flops 7644119040 | bytes 26984448 | tf_op jit(solution)/shard_map/pallas_call | solution.py:303
  154.9 2.6 shard_map.127.rest_0_
  157.4 1.5 copy-done.33
  158.9 14.8 %shard_map.128 = (bf16[2,192,2304]{2,1,0:T(8,128)(2,1)S(1)}, bf16[2,192,2304]{2,1,0:T(8,128)(2,1)}) custom-call(bf16[2,192,2304]{2,1,0:T(8,128)(2,1)S(1)} %copy-done.33, bf16[2,192,2304]{2,1,0:T(8,128)(2,1)S(1)} %collective-permute-done.17.got_ref, bf16[2,720,2304]{2,1,0:T(8,128)(2,1)} %bitcast.133, bf16[2,720,2304]{2,1,0:T(8,128)(2,1)} %bitcast.135, ...), custom_call_target="tpu_custom_call" | custom-call | flops 7644119040 | bytes 26984448 | tf_op jit(solution)/shard_map/pallas_call | solution.py:303
  173.8 4.5 %all-to-all-start.2 = ((bf16[8,64,640]{2,1,0:T(8,128)(2,1)}), bf16[8,64,640]{2,1,0:T(8,128)(2,1)}, u32[]{:S(2)}, u32[]{:S(2)}) async-start(bf16[8,64,640]{2,1,0:T(8,128)(2,1)} %shard_map.127.rest_0_), calls=%async_computation.2 | async-start | bytes 1310720 | tf_op jit(solution)/shard_map/all_to_all | solution.py:503
  184.0 1.5 copy-done.3
  185.5 5.3 %shard_map.129 = (bf16[256,2304]{1,0:T(8,128)(2,1)S(1)}, bf16[128,2304]{1,0:T(8,128)(2,1)}, bf16[128,2304]{1,0:T(8,128)(2,1)}) custom-call(s32[2]{0:T(128)S(1)} %add_multiply_fusion.bases_ref, bf16[2,192,2304]{2,1,0:T(8,128)(2,1)S(1)} %copy-done.3, bf16[2,192,2304]{2,1,0:T(8,128)(2,1)} %collective-permute-done.16.y_got_ref, ...), custom_call_target="tpu_custom_call" | custom-call | flops 905969664 | bytes 7077888 | tf_op jit(solution)/shard_map/pallas_call | solution.py:359
  191.8 1.6 collective-permute-start.18
  193.5 1.5 collective-permute-start.19
  197.0 1.3 slice.200.rest_1_
  198.3 1.3 slice.203.rest_4_
  202.3 1.3 slice.204.rest_5_
  204.9 2.1 shard_map.132.rest_8_
  213.8 3.5 %shard_map.133 = (bf16[256,2304]{1,0:T(8,128)(2,1)S(1)}, bf16[128,2304]{1,0:T(8,128)(2,1)S(1)}, bf16[128,2304]{1,0:T(8,128)(2,1)S(1)}) custom-call(s32[2]{0:T(128)S(1)} %copy-done.15, bf16[2,192,2304]{2,1,0:T(8,128)(2,1)S(1)} %get-tuple-element.45.y_own_ref, bf16[2,192,2304]{2,1,0:T(8,128)(2,1)S(1)} %collective-permute-done.23.y_got_ref, ...), custom_call_target="tpu_custom_call" | custom-call | flops 905969664 | bytes 7077888 | tf_op jit(solution)/shard_map/pallas_call | solution.py:359
  218.3 1.5 shard_map.130
  219.8 1.6 collective-permute-start.20
  221.4 1.6 collective-permute-start.21
  223.0 15.9 %collective-permute-done.20.rest_0_ = bf16[64,2304]{1,0:T(8,128)(2,1)S(1)} collective-permute-done((bf16[64,2304]{1,0:T(8,128)(2,1)S(1)}, bf16[64,2304]{1,0:T(8,128)(2,1)S(1)}, u32[]{:S(2)}, u32[]{:S(2)}) %collective-permute-start.20) | collective-permute-done | bytes 294944 | tf_op jit(solution)/shard_map/ppermute | solution.py:377
  240.0 1.4 collective-permute-start.27
  241.3 5.8 %collective-permute-done.26.rest_0_ = bf16[64,2304]{1,0:T(8,128)(2,1)S(1)} collective-permute-done((bf16[64,2304]{1,0:T(8,128)(2,1)S(1)}, bf16[64,2304]{1,0:T(8,128)(2,1)S(1)}, u32[]{:S(2)}, u32[]{:S(2)}) %collective-permute-start.26) | collective-permute-done | bytes 294944 | tf_op jit(solution)/shard_map/ppermute | solution.py:377
  249.6 10.8 %collective-permute-done.28 = bf16[64,2304]{1,0:T(8,128)(2,1)S(1)} collective-permute-done((bf16[64,2304]{1,0:T(8,128)(2,1)S(1)}, bf16[64,2304]{1,0:T(8,128)(2,1)S(1)}, u32[]{:S(2)}, u32[]{:S(2)}) %collective-permute-start.28) | collective-permute-done | bytes 294944 | tf_op jit(solution)/shard_map/ppermute | solution.py:377
  261.2 2.3 collective-permute-done.22
  263.6 7.5 %collective-permute-done.29 = bf16[64,2304]{1,0:T(8,128)(2,1)S(1)} collective-permute-done((bf16[64,2304]{1,0:T(8,128)(2,1)S(1)}, bf16[64,2304]{1,0:T(8,128)(2,1)S(1)}, u32[]{:S(2)}, u32[]{:S(2)}) %collective-permute-start.29) | collective-permute-done | bytes 294944 | tf_op jit(solution)/shard_map/ppermute | solution.py:377
  (172 shorter events, 46.1 us)
Async XLA Ops:
  12.2 33.0 %all-to-all-start = ((bf16[8,64,960]{2,1,0:T(8,128)(2,1)}), bf16[8,64,960]{2,1,0:T(8,128)(2,1)S(1)}, u32[]{:S(2)}, u32[]{:S(2)}) async-start(bf16[8,64,960]{2,1,0:T(8,128)(2,1)} %pad_maximum_fusion), calls=%async_computation | async-start | bytes 2097152 | tf_op jit(solution)/shard_map/all_to_all | solution.py:483
  50.8 15.4 %all-to-all-start.1 = ((bf16[8,64,320]{2,1,0:T(8,128)(2,1)}), bf16[8,64,320]{2,1,0:T(8,128)(2,1)S(1)}, u32[]{:S(2)}, u32[]{:S(2)}) async-start(bf16[8,64,320]{2,1,0:T(8,128)(2,1)} %bitcast.29), calls=%async_computation.1 | async-start | bytes 786432 | tf_op jit(solution)/shard_map/all_to_all | solution.py:486
  69.2 13.4 %collective-permute-start.3 = (bf16[64,2432]{1,0:T(8,128)(2,1)}, bf16[64,2432]{1,0:T(8,128)(2,1)S(1)}, u32[]{:S(2)}, u32[]{:S(2)}) collective-permute-start(bf16[64,2432]{1,0:T(8,128)(2,1)} %get-tuple-element.29.refs_0_), channel_id=1, source_target_pairs={{0,8},{4,12},{8,0},{12,4},{16,24},{20,28},{24,16},{28,20},{1,9},{5... | collective-permute-start | bytes 933896 | tf_op jit(solution)/shard_map/ppermute | solution.py:377
  70.1 17.5 %collective-permute-start.7 = (bf16[64,2432]{1,0:T(8,128)(2,1)}, bf16[64,2432]{1,0:T(8,128)(2,1)S(1)}, u32[]{:S(2)}, u32[]{:S(2)}) collective-permute-start(bf16[64,2432]{1,0:T(8,128)(2,1)} %get-tuple-element.29.refs_0_), channel_id=1, source_target_pairs={{0,16},{4,20},{8,24},{12,28},{16,0},{20,4},{24,8},{28,12},{1,17},{... | collective-permute-start | bytes 933896 | tf_op jit(solution)/shard_map/ppermute | solution.py:377
  70.9 16.7 %collective-permute-start.1 = (bf16[64,2432]{1,0:T(8,128)(2,1)}, bf16[64,2432]{1,0:T(8,128)(2,1)S(1)}, u32[]{:S(2)}, u32[]{:S(2)}) collective-permute-start(bf16[64,2432]{1,0:T(8,128)(2,1)} %get-tuple-element.29.refs_0_), channel_id=1, source_target_pairs={{0,4},{4,0},{8,12},{12,8},{16,20},{20,16},{24,28},{28,24},{1,5},{5... | collective-permute-start | bytes 933896 | tf_op jit(solution)/shard_map/ppermute | solution.py:377
  82.6 70.5 %copy-start.19 = (bf16[64,2432]{1,0:T(8,128)(2,1)}, bf16[64,2432]{1,0:T(8,128)(2,1)S(1)}, u32[]{:S(2)}) copy-start(bf16[64,2432]{1,0:T(8,128)(2,1)S(1)} %collective-permute-done.3.refs_4_) | copy-start | bytes 933892
  82.6 10.3 %collective-permute-start.5 = (bf16[64,2432]{1,0:T(8,128)(2,1)S(1)}, bf16[64,2432]{1,0:T(8,128)(2,1)S(1)}, u32[]{:S(2)}, u32[]{:S(2)}) collective-permute-start(bf16[64,2432]{1,0:T(8,128)(2,1)S(1)} %collective-permute-done.3.refs_4_), channel_id=1, source_target_pairs={{0,2},{1,3},{2,0},{3,1},{4,6},{5,7},{6,4},{7,5},{8,10},{9,11},{10,... | collective-permute-start | bytes 933896 | tf_op jit(solution)/shard_map/ppermute | solution.py:377
  84.2 15.4 %collective-permute-start = (bf16[64,2432]{1,0:T(8,128)(2,1)}, bf16[64,2432]{1,0:T(8,128)(2,1)S(1)}, u32[]{:S(2)}, u32[]{:S(2)}) collective-permute-start(bf16[64,2432]{1,0:T(8,128)(2,1)} %get-tuple-element.29.refs_0_), channel_id=1, source_target_pairs={{0,2},{1,3},{2,0},{3,1},{4,6},{5,7},{6,4},{7,5},{8,10},{9,11},{10,... | collective-permute-start | bytes 933896 | tf_op jit(solution)/shard_map/ppermute | solution.py:377
  84.7 15.0 %collective-permute-start.4 = (bf16[64,2432]{1,0:T(8,128)(2,1)S(1)}, bf16[64,2432]{1,0:T(8,128)(2,1)S(1)}, u32[]{:S(2)}, u32[]{:S(2)}) collective-permute-start(bf16[64,2432]{1,0:T(8,128)(2,1)S(1)} %collective-permute-done.3.refs_4_), channel_id=1, source_target_pairs={{0,4},{4,0},{8,12},{12,8},{16,20},{20,16},{24,28},{28,24},{1,5},{5... | collective-permute-start | bytes 933896 | tf_op jit(solution)/shard_map/ppermute | solution.py:377
  87.6 48.7 %copy-start.16 = (bf16[64,2432]{1,0:T(8,128)(2,1)}, bf16[64,2432]{1,0:T(8,128)(2,1)S(1)}, u32[]{:S(2)}) copy-start(bf16[64,2432]{1,0:T(8,128)(2,1)S(1)} %collective-permute-done.7.refs_8_.refs_0_) | copy-start | bytes 933892
  87.6 12.0 %collective-permute-start.8 = (bf16[64,2432]{1,0:T(8,128)(2,1)S(1)}, bf16[64,2432]{1,0:T(8,128)(2,1)S(1)}, u32[]{:S(2)}, u32[]{:S(2)}) collective-permute-start(bf16[64,2432]{1,0:T(8,128)(2,1)S(1)} %collective-permute-done.7.refs_8_.refs_0_), channel_id=1, source_target_pairs={{0,8},{4,12},{8,0},{12,4},{16,24},{20,28},{24,16},{28,20},{1,9},{5... | collective-permute-start | bytes 933896 | tf_op jit(solution)/shard_map/ppermute | solution.py:377
  87.6 65.5 %copy-start.20 = (bf16[64,2432]{1,0:T(8,128)(2,1)}, bf16[64,2432]{1,0:T(8,128)(2,1)S(1)}, u32[]{:S(2)}) copy-start(bf16[64,2432]{1,0:T(8,128)(2,1)S(1)} %collective-permute-done.1.refs_2_) | copy-start | bytes 933892
  87.6 15.9 %collective-permute-start.2 = (bf16[64,2432]{1,0:T(8,128)(2,1)S(1)}, bf16[64,2432]{1,0:T(8,128)(2,1)S(1)}, u32[]{:S(2)}, u32[]{:S(2)}) collective-permute-start(bf16[64,2432]{1,0:T(8,128)(2,1)S(1)} %collective-permute-done.1.refs_2_), channel_id=1, source_target_pairs={{0,2},{1,3},{2,0},{3,1},{4,6},{5,7},{6,4},{7,5},{8,10},{9,11},{10,... | collective-permute-start | bytes 933896 | tf_op jit(solution)/shard_map/ppermute | solution.py:377
  92.9 60.2 %copy-start.21 = (bf16[64,2432]{1,0:T(8,128)(2,1)}, bf16[64,2432]{1,0:T(8,128)(2,1)S(1)}, u32[]{:S(2)}) copy-start(bf16[64,2432]{1,0:T(8,128)(2,1)S(1)} %collective-permute-done.5.refs_6_) | copy-start | bytes 933892
  92.9 10.6 %collective-permute-start.6 = (bf16[64,2432]{1,0:T(8,128)(2,1)S(1)}, bf16[64,2432]{1,0:T(8,128)(2,1)S(1)}, u32[]{:S(2)}, u32[]{:S(2)}) collective-permute-start(bf16[64,2432]{1,0:T(8,128)(2,1)S(1)} %collective-permute-done.5.refs_6_), channel_id=1, source_target_pairs={{0,4},{4,0},{8,12},{12,8},{16,20},{20,16},{24,28},{28,24},{1,5},{5... | collective-permute-start | bytes 933896 | tf_op jit(solution)/shard_map/ppermute | solution.py:377
  96.0 88.0 %copy-start.14 = (s32[2]{0:T(128)}, s32[2]{0:T(128)S(1)}, u32[]{:S(2)}) copy-start(s32[2]{0:T(128)S(1)} %add_multiply_fusion.bases_ref) | copy-start | bytes 28
  99.6 36.7 %copy-start.22 = (bf16[64,2432]{1,0:T(8,128)(2,1)}, bf16[64,2432]{1,0:T(8,128)(2,1)S(1)}, u32[]{:S(2)}) copy-start(bf16[64,2432]{1,0:T(8,128)(2,1)S(1)} %collective-permute-done.refs_1_) | copy-start | bytes 933892
  99.6 36.7 %copy-start.17 = (bf16[64,2432]{1,0:T(8,128)(2,1)}, bf16[64,2432]{1,0:T(8,128)(2,1)S(1)}, u32[]{:S(2)}) copy-start(bf16[64,2432]{1,0:T(8,128)(2,1)S(1)} %collective-permute-done.8.refs_9_.refs_4_) | copy-start | bytes 933892
  99.6 36.7 %copy-start.23 = (bf16[64,2432]{1,0:T(8,128)(2,1)}, bf16[64,2432]{1,0:T(8,128)(2,1)S(1)}, u32[]{:S(2)}) copy-start(bf16[64,2432]{1,0:T(8,128)(2,1)S(1)} %collective-permute-done.4.refs_5_) | copy-start | bytes 933892
  103.5 32.8 %copy-start.24 = (bf16[64,2432]{1,0:T(8,128)(2,1)}, bf16[64,2432]{1,0:T(8,128)(2,1)S(1)}, u32[]{:S(2)}) copy-start(bf16[64,2432]{1,0:T(8,128)(2,1)S(1)} %collective-permute-done.2.refs_3_) | copy-start | bytes 933892
  104.6 31.8 %copy-start.25 = (bf16[64,2432]{1,0:T(8,128)(2,1)}, bf16[64,2432]{1,0:T(8,128)(2,1)S(1)}, u32[]{:S(2)}) copy-start(bf16[64,2432]{1,0:T(8,128)(2,1)S(1)} %collective-permute-done.6.refs_7_) | copy-start | bytes 933892
  106.5 31.1 %copy-start.39 = (s32[1,32]{1,0:T(1,128)S(1)}, s32[1,32]{1,0:T(1,128)}, u32[]{:S(2)}) copy-start(s32[1,32]{1,0:T(1,128)} %param.18) | copy-start | bytes 388
  106.5 31.7 %collective-permute-start.9 = (bf16[2,192,2304]{2,1,0:T(8,128)(2,1)S(1)}, bf16[2,192,2304]{2,1,0:T(8,128)(2,1)S(1)}, u32[]{:S(2)}, u32[]{:S(2)}) collective-permute-start(bf16[2,192,2304]{2,1,0:T(8,128)(2,1)S(1)} %get-tuple-element.31), channel_id=1, source_target_pairs={{0,1},{1,0},{2,3},{3,2},{4,5},{5,4},{6,7},{7,6},{8,9},{9,8},{10,11... | collective-permute-start | bytes 5308424 | tf_op jit(solution)/shard_map/ppermute | solution.py:377
  106.6 12.0 %collective-permute-start.11 = (bf16[64,2432]{1,0:T(8,128)(2,1)S(1)}, bf16[64,2432]{1,0:T(8,128)(2,1)S(1)}, u32[]{:S(2)}, u32[]{:S(2)}) collective-permute-start(bf16[64,2432]{1,0:T(8,128)(2,1)S(1)} %collective-permute-done.7.refs_8_.refs_0_), channel_id=1, source_target_pairs={{0,4},{4,0},{8,12},{12,8},{16,20},{20,16},{24,28},{28,24},{1,5},{5... | collective-permute-start | bytes 933896 | tf_op jit(solution)/shard_map/ppermute | solution.py:377
  110.4 10.2 %collective-permute-start.14 = (bf16[64,2432]{1,0:T(8,128)(2,1)S(1)}, bf16[64,2432]{1,0:T(8,128)(2,1)S(1)}, u32[]{:S(2)}, u32[]{:S(2)}) collective-permute-start(bf16[64,2432]{1,0:T(8,128)(2,1)S(1)} %collective-permute-done.8.refs_9_.refs_4_), channel_id=1, source_target_pairs={{0,2},{1,3},{2,0},{3,1},{4,6},{5,7},{6,4},{7,5},{8,10},{9,11},{10,... | collective-permute-start | bytes 933896 | tf_op jit(solution)/shard_map/ppermute | solution.py:377
  111.9 15.3 %collective-permute-start.10 = (bf16[64,2432]{1,0:T(8,128)(2,1)S(1)}, bf16[64,2432]{1,0:T(8,128)(2,1)S(1)}, u32[]{:S(2)}, u32[]{:S(2)}) collective-permute-start(bf16[64,2432]{1,0:T(8,128)(2,1)S(1)} %collective-permute-done.7.refs_8_.refs_0_), channel_id=1, source_target_pairs={{0,2},{1,3},{2,0},{3,1},{4,6},{5,7},{6,4},{7,5},{8,10},{9,11},{10,... | collective-permute-start | bytes 933896 | tf_op jit(solution)/shard_map/ppermute | solution.py:377
  112.4 20.8 %collective-permute-start.13 = (bf16[64,2432]{1,0:T(8,128)(2,1)S(1)}, bf16[64,2432]{1,0:T(8,128)(2,1)S(1)}, u32[]{:S(2)}, u32[]{:S(2)}) collective-permute-start(bf16[64,2432]{1,0:T(8,128)(2,1)S(1)} %collective-permute-done.8.refs_9_.refs_4_), channel_id=1, source_target_pairs={{0,4},{4,0},{8,12},{12,8},{16,20},{20,16},{24,28},{28,24},{1,5},{5... | collective-permute-start | bytes 933896 | tf_op jit(solution)/shard_map/ppermute | solution.py:377
  118.6 19.7 %copy-start.27 = (bf16[64,2432]{1,0:T(8,128)(2,1)}, bf16[64,2432]{1,0:T(8,128)(2,1)S(1)}, u32[]{:S(2)}) copy-start(bf16[64,2432]{1,0:T(8,128)(2,1)S(1)} %collective-permute-done.11.refs_2_) | copy-start | bytes 933892
  118.6 14.6 %collective-permute-start.12 = (bf16[64,2432]{1,0:T(8,128)(2,1)S(1)}, bf16[64,2432]{1,0:T(8,128)(2,1)S(1)}, u32[]{:S(2)}, u32[]{:S(2)}) collective-permute-start(bf16[64,2432]{1,0:T(8,128)(2,1)S(1)} %collective-permute-done.11.refs_2_), channel_id=1, source_target_pairs={{0,2},{1,3},{2,0},{3,1},{4,6},{5,7},{6,4},{7,5},{8,10},{9,11},{10,... | collective-permute-start | bytes 933896 | tf_op jit(solution)/shard_map/ppermute | solution.py:377
  120.6 17.7 %copy-start.26 = (bf16[64,2432]{1,0:T(8,128)(2,1)}, bf16[64,2432]{1,0:T(8,128)(2,1)S(1)}, u32[]{:S(2)}) copy-start(bf16[64,2432]{1,0:T(8,128)(2,1)S(1)} %collective-permute-done.14.refs_6_) | copy-start | bytes 933892
  120.6 12.6 %collective-permute-start.15 = (bf16[64,2432]{1,0:T(8,128)(2,1)S(1)}, bf16[64,2432]{1,0:T(8,128)(2,1)S(1)}, u32[]{:S(2)}, u32[]{:S(2)}) collective-permute-start(bf16[64,2432]{1,0:T(8,128)(2,1)S(1)} %collective-permute-done.14.refs_6_), channel_id=1, source_target_pairs={{0,4},{4,0},{8,12},{12,8},{16,20},{20,16},{24,28},{28,24},{1,5},{5... | collective-permute-start | bytes 933896 | tf_op jit(solution)/shard_map/ppermute | solution.py:377
  127.3 11.0 %copy-start.29 = (bf16[64,2432]{1,0:T(8,128)(2,1)}, bf16[64,2432]{1,0:T(8,128)(2,1)S(1)}, u32[]{:S(2)}) copy-start(bf16[64,2432]{1,0:T(8,128)(2,1)S(1)} %collective-permute-done.10.refs_1_) | copy-start | bytes 933892
  137.6 19.8 %collective-permute-start.17 = (bf16[2,192,2304]{2,1,0:T(8,128)(2,1)}, bf16[2,192,2304]{2,1,0:T(8,128)(2,1)S(1)}, u32[]{:S(2)}, u32[]{:S(2)}) collective-permute-start(bf16[2,192,2304]{2,1,0:T(8,128)(2,1)} %get-tuple-element.32.rest_0_), channel_id=1, source_target_pairs={{0,1},{1,0},{2,3},{3,2},{4,5},{5,4},{6,7},{7,6},{8,9},{9,8},{10,11... | collective-permute-start | bytes 5308424 | tf_op jit(solution)/shard_map/ppermute | solution.py:377
  154.4 29.6 %collective-permute-start.16 = (bf16[2,192,2304]{2,1,0:T(8,128)(2,1)}, bf16[2,192,2304]{2,1,0:T(8,128)(2,1)}, u32[]{:S(2)}, u32[]{:S(2)}) collective-permute-start(bf16[2,192,2304]{2,1,0:T(8,128)(2,1)} %get-tuple-element.34.late_ref.rest_1_), channel_id=1, source_target_pairs={{0,1},{1,0},{2,3},{3,2},{4,5},{5,4},{6,7},{7,6},{8,9},{9,8},{10,11... | collective-permute-start | bytes 5308424 | tf_op jit(solution)/shard_map/ppermute | solution.py:377
  173.7 33.3 %collective-permute-start.23 = (bf16[2,192,2304]{2,1,0:T(8,128)(2,1)}, bf16[2,192,2304]{2,1,0:T(8,128)(2,1)S(1)}, u32[]{:S(2)}, u32[]{:S(2)}) collective-permute-start(bf16[2,192,2304]{2,1,0:T(8,128)(2,1)} %get-tuple-element.36.rest_8_), channel_id=1, source_target_pairs={{0,1},{1,0},{2,3},{3,2},{4,5},{5,4},{6,7},{7,6},{8,9},{9,8},{10,11... | collective-permute-start | bytes 5308424 | tf_op jit(solution)/shard_map/ppermute | solution.py:377
  173.8 31.2 %all-to-all-start.2 = ((bf16[8,64,640]{2,1,0:T(8,128)(2,1)}), bf16[8,64,640]{2,1,0:T(8,128)(2,1)}, u32[]{:S(2)}, u32[]{:S(2)}) async-start(bf16[8,64,640]{2,1,0:T(8,128)(2,1)} %shard_map.127.rest_0_), calls=%async_computation.2 | async-start | bytes 1310720 | tf_op jit(solution)/shard_map/all_to_all | solution.py:503
  191.8 26.4 %collective-permute-start.18 = (bf16[128,2304]{1,0:T(8,128)(2,1)}, bf16[128,2304]{1,0:T(8,128)(2,1)}, u32[]{:S(2)}, u32[]{:S(2)}) collective-permute-start(bf16[128,2304]{1,0:T(8,128)(2,1)} %get-tuple-element.38), channel_id=1, source_target_pairs={{0,4},{4,0},{8,12},{12,8},{16,20},{20,16},{24,28},{28,24},{1,5},{5... | collective-permute-start | bytes 1769480 | tf_op jit(solution)/shard_map/ppermute | solution.py:377
  193.5 24.8 %collective-permute-start.19 = (bf16[128,2304]{1,0:T(8,128)(2,1)}, bf16[128,2304]{1,0:T(8,128)(2,1)}, u32[]{:S(2)}, u32[]{:S(2)}) collective-permute-start(bf16[128,2304]{1,0:T(8,128)(2,1)} %get-tuple-element.39), channel_id=1, source_target_pairs={{0,2},{1,3},{2,0},{3,1},{4,6},{5,7},{6,4},{7,5},{8,10},{9,11},{10,... | collective-permute-start | bytes 1769480 | tf_op jit(solution)/shard_map/ppermute | solution.py:377
  217.3 21.8 %collective-permute-start.24 = (bf16[128,2304]{1,0:T(8,128)(2,1)S(1)}, bf16[128,2304]{1,0:T(8,128)(2,1)S(1)}, u32[]{:S(2)}, u32[]{:S(2)}) collective-permute-start(bf16[128,2304]{1,0:T(8,128)(2,1)S(1)} %get-tuple-element.47), channel_id=1, source_target_pairs={{0,4},{4,0},{8,12},{12,8},{16,20},{20,16},{24,28},{28,24},{1,5},{5... | collective-permute-start | bytes 1769480 | tf_op jit(solution)/shard_map/ppermute | solution.py:377
  217.7 21.4 %collective-permute-start.25 = (bf16[128,2304]{1,0:T(8,128)(2,1)S(1)}, bf16[128,2304]{1,0:T(8,128)(2,1)S(1)}, u32[]{:S(2)}, u32[]{:S(2)}) collective-permute-start(bf16[128,2304]{1,0:T(8,128)(2,1)S(1)} %get-tuple-element.48), channel_id=1, source_target_pairs={{0,2},{1,3},{2,0},{3,1},{4,6},{5,7},{6,4},{7,5},{8,10},{9,11},{10,... | collective-permute-start | bytes 1769480 | tf_op jit(solution)/shard_map/ppermute | solution.py:377
  219.8 19.2 %collective-permute-start.20 = (bf16[64,2304]{1,0:T(8,128)(2,1)S(1)}, bf16[64,2304]{1,0:T(8,128)(2,1)S(1)}, u32[]{:S(2)}, u32[]{:S(2)}) collective-permute-start(bf16[64,2304]{1,0:T(8,128)(2,1)S(1)} %get-tuple-element.41), channel_id=1, source_target_pairs={{0,2},{1,3},{2,0},{3,1},{4,6},{5,7},{6,4},{7,5},{8,10},{9,11},{10,... | collective-permute-start | bytes 884744 | tf_op jit(solution)/shard_map/ppermute | solution.py:377
  221.4 17.6 %collective-permute-start.21 = (bf16[64,2304]{1,0:T(8,128)(2,1)S(1)}, bf16[64,2304]{1,0:T(8,128)(2,1)S(1)}, u32[]{:S(2)}, u32[]{:S(2)}) collective-permute-start(bf16[64,2304]{1,0:T(8,128)(2,1)S(1)} %get-tuple-element.42), channel_id=1, source_target_pairs={{0,4},{4,0},{8,12},{12,8},{16,20},{20,16},{24,28},{28,24},{1,5},{5... | collective-permute-start | bytes 884744 | tf_op jit(solution)/shard_map/ppermute | solution.py:377
  239.1 31.9 %copy-start.35 = (f32[64,2304]{1,0:T(8,128)S(1)}, f32[64,2304]{1,0:T(8,128)}, u32[]{:S(2)}) copy-start(f32[64,2304]{1,0:T(8,128)} %get-tuple-element.28) | copy-start | bytes 1769476
  239.4 7.7 %collective-permute-start.26 = (bf16[64,2304]{1,0:T(8,128)(2,1)S(1)}, bf16[64,2304]{1,0:T(8,128)(2,1)S(1)}, u32[]{:S(2)}, u32[]{:S(2)}) collective-permute-start(bf16[64,2304]{1,0:T(8,128)(2,1)S(1)} %get-tuple-element.50), channel_id=1, source_target_pairs={{0,2},{1,3},{2,0},{3,1},{4,6},{5,7},{6,4},{7,5},{8,10},{9,11},{10,... | collective-permute-start | bytes 884744 | tf_op jit(solution)/shard_map/ppermute | solution.py:377
  240.0 7.4 %collective-permute-start.27 = (bf16[64,2304]{1,0:T(8,128)(2,1)S(1)}, bf16[64,2304]{1,0:T(8,128)(2,1)S(1)}, u32[]{:S(2)}, u32[]{:S(2)}) collective-permute-start(bf16[64,2304]{1,0:T(8,128)(2,1)S(1)} %get-tuple-element.51), channel_id=1, source_target_pairs={{0,4},{4,0},{8,12},{12,8},{16,20},{20,16},{24,28},{28,24},{1,5},{5... | collective-permute-start | bytes 884744 | tf_op jit(solution)/shard_map/ppermute | solution.py:377
  247.5 12.9 %collective-permute-start.28 = (bf16[64,2304]{1,0:T(8,128)(2,1)S(1)}, bf16[64,2304]{1,0:T(8,128)(2,1)S(1)}, u32[]{:S(2)}, u32[]{:S(2)}) collective-permute-start(bf16[64,2304]{1,0:T(8,128)(2,1)S(1)} %get-tuple-element.53), channel_id=1, source_target_pairs={{0,8},{4,12},{8,0},{12,4},{16,24},{20,28},{24,16},{28,20},{1,9},{5... | collective-permute-start | bytes 884744 | tf_op jit(solution)/shard_map/ppermute | solution.py:377
  248.6 14.9 %collective-permute-start.22 = (bf16[64,2304]{1,0:T(8,128)(2,1)S(1)}, bf16[64,2304]{1,0:T(8,128)(2,1)S(1)}, u32[]{:S(2)}, u32[]{:S(2)}) collective-permute-start(bf16[64,2304]{1,0:T(8,128)(2,1)S(1)} %get-tuple-element.44.rest_2_), channel_id=1, source_target_pairs={{0,8},{4,12},{8,0},{12,4},{16,24},{20,28},{24,16},{28,20},{1,9},{5... | collective-permute-start | bytes 884744 | tf_op jit(solution)/shard_map/ppermute | solution.py:377
  260.5 10.5 %collective-permute-start.29 = (bf16[64,2304]{1,0:T(8,128)(2,1)S(1)}, bf16[64,2304]{1,0:T(8,128)(2,1)S(1)}, u32[]{:S(2)}, u32[]{:S(2)}) collective-permute-start(bf16[64,2304]{1,0:T(8,128)(2,1)S(1)} %add_convert_fusion.1), channel_id=1, source_target_pairs={{0,16},{4,20},{8,24},{12,28},{16,0},{20,4},{24,8},{28,12},{1,17},{... | collective-permute-start | bytes 884744 | tf_op jit(solution)/shard_map/ppermute | solution.py:377
  (25 other events, 81.9 us)

commit v7 on v6

--- a/solution.py
+++ b/solution.py
@@ -140,6 +140,22 @@
     )(first, x, tgt, gates, w_gate, w_up, w_down)
 
 
+def pack_kernel(firsts, span, q_ref, k_ref, v_ref, out_ref):
+    for j, first in enumerate(firsts):
+        lanes = slice(first * HEAD_DIM, first * HEAD_DIM + span)
+        out_ref[j] = jnp.concatenate([r[:, lanes] for r in (q_ref, k_ref, v_ref)], axis=1)
+
+
+def pack_heads(query, keys, values, firsts, span):
+    rows_dev = query.shape[0]
+    n_seq = len(firsts)
+    return pl.pallas_call(
+        functools.partial(pack_kernel, firsts, span),
+        out_shape=jax.ShapeDtypeStruct((n_seq, rows_dev, 3 * span), jnp.bfloat16),
+        cost_estimate=pl.CostEstimate(flops=0, bytes_accessed=12 * n_seq * rows_dev * span, transcendentals=0),
+    )(query, keys, values)
+
+
 def norm_kernel(share, offsets, context_ref, residual_ref, gain_ref, facts_ref, stream_ref, piece_ref):
     n_seq, _, _ = context_ref.shape
     width = residual_ref.shape[1]
@@ -225,13 +241,14 @@
 
 
 def select_kernel(local, rows_dev, count, bases_ref, *refs):
-    piece_refs, own_ref, sib_ref = refs[:count], refs[-2], refs[-1]
+    piece_refs, (own_ref, sib_ref, facts_ref) = refs[:count], refs[-3:]
     width = own_ref.shape[2]
     tokens, rows = 4 * rows_dev, 4 * CAP
     shift = lax.broadcasted_iota(jnp.int32, (1, tokens), 1) // rows_dev * CAP
     row_id = lax.broadcasted_iota(jnp.int32, (rows, tokens), 0)
     for g in range(len(piece_refs) // 4):
         x = jnp.concatenate([p[...] for p in piece_refs[4 * g : 4 * g + 4]], axis=0)
+        facts_ref[g * tokens : (g + 1) * tokens, :] = x[:, width:]
         facts = facts_by_lane(x[:, width:])
         picks = []
         for core in range(2):
@@ -254,11 +271,11 @@
     vmem = pl.BlockSpec(memory_space=pltpu.VMEM)
     return pl.pallas_call(
         functools.partial(select_kernel, local, rows_dev, len(pieces)),
-        out_shape=(out, out),
+        out_shape=(out, out, jax.ShapeDtypeStruct((len(pieces) * rows_dev, 128), jnp.bfloat16)),
         in_specs=[pl.BlockSpec(memory_space=pltpu.SMEM)]
         + [vmem] * len(pieces)
         + [pl.BlockSpec(memory_space=pl.ANY)] * len(waits),
-        out_specs=(vmem, vmem),
+        out_specs=(vmem, vmem, vmem),
         compiler_params=pltpu.CompilerParams(vmem_limit_bytes=28 * 1024 * 1024),
         cost_estimate=pl.CostEstimate(
             flops=16 * local * CAP * rows_dev * len(pieces) * width,
@@ -315,17 +332,16 @@
     )(own, got, w_gate, w_up, w_down, *waits)
 
 
-def put_kernel(local, rows_dev, count, waits, bases_ref, y_own_ref, y_got_ref, *rest):
-    fact_refs = rest[:count]
-    kept_ref, *send_refs = rest[count + waits :]
+def put_kernel(local, rows_dev, planes, waits, bases_ref, y_own_ref, y_got_ref, facts_ref, *rest):
+    kept_ref, *send_refs = rest[waits:]
     tokens, rows = 4 * rows_dev, 4 * CAP
     total = 2 * local * rows
     shift_lane = lax.broadcasted_iota(jnp.int32, (1, tokens), 1) // rows_dev * CAP
     shift_row = lax.broadcasted_iota(jnp.int32, (tokens, 1), 0) // rows_dev * CAP
     row_id = lax.broadcasted_iota(jnp.int32, (rows, tokens), 0)
     lane = lax.broadcasted_iota(jnp.int32, (tokens, total), 1)
-    for g in range(count // 4):
-        facts = jnp.concatenate([f[...] for f in fact_refs[4 * g : 4 * g + 4]], axis=0)
+    for g in range(planes):
+        facts = facts_ref[g * tokens : (g + 1) * tokens, :]
         by_lane = facts_by_lane(facts)
         by_row = facts.astype(jnp.float32)
         here = slice(g * rows, (g + 1) * rows)
@@ -350,26 +366,25 @@
         send_refs[g][...] = out[tokens // 2 :]
 
 
-def put_rows(y_own, y_got, pieces, bases, waits):
+def put_rows(y_own, y_got, facts, bases, rows_dev, waits):
     local, _, width = y_own.shape
-    rows_dev = pieces[0].shape[0]
-    planes = len(pieces) // 4
+    tokens = facts.shape[0]
+    planes = tokens // (4 * rows_dev)
     vmem = pl.BlockSpec(memory_space=pltpu.VMEM)
     shape = lambda n: jax.ShapeDtypeStruct((n, width), jnp.bfloat16)
     out = pl.pallas_call(
-        functools.partial(put_kernel, local, rows_dev, len(pieces), len(waits)),
+        functools.partial(put_kernel, local, rows_dev, planes, len(waits)),
         out_shape=(shape(2 * planes * rows_dev),) + (shape(2 * rows_dev),) * planes,
-        in_specs=[pl.BlockSpec(memory_space=pltpu.SMEM), vmem, vmem]
-        + [vmem] * len(pieces)
+        in_specs=[pl.BlockSpec(memory_space=pltpu.SMEM), vmem, vmem, vmem]
         + [pl.BlockSpec(memory_space=pl.ANY)] * len(waits),
         out_specs=(vmem,) * (1 + planes),
         compiler_params=pltpu.CompilerParams(vmem_limit_bytes=28 * 1024 * 1024),
         cost_estimate=pl.CostEstimate(
-            flops=16 * local * CAP * rows_dev * len(pieces) * width,
-            bytes_accessed=8 * local * len(pieces) * CAP * width,
+            flops=16 * local * CAP * tokens * width,
+            bytes_accessed=8 * local * tokens * width,
             transcendentals=0,
         ),
-    )(bases, y_own, y_got, *[p[:, width:] for p in pieces], *waits)
+    )(bases, y_own, y_got, facts, *waits)
     return out[0], out[1:]
 
 
@@ -427,22 +442,23 @@
         return near
 
     near_a, near_b = gather(0), gather(2)
-    own_a, sib_a = select_rows(near_a, bases, local, starts[2:])
+    first_b = [near_b[1], near_b[2], near_b[5], near_b[6]]
+    own_a, sib_a, facts_a = select_rows(near_a, bases, local, first_b)
     got_a = core(sib_a)
-    own_b, sib_b = select_rows(near_b, bases, local)
+    own_b, sib_b, facts_b = select_rows(near_b, bases, local)
     got_b = core(sib_b)
     own_a, sib_a = expert_rows(own_a, got_a, w_gate, w_up, w_down, [sib_b])
     pages, other = late_work(sib_a)
     got_a = core(sib_a)
     own_b, sib_b = expert_rows(own_b, got_b, w_gate, w_up, w_down, [pages, sib_a])
     got_b = core(sib_b)
-    keep_a, (fx_a, fy_a) = put_rows(own_a, got_a, near_a, bases, [sib_b])
+    keep_a, (fx_a, fy_a) = put_rows(own_a, got_a, facts_a, bases, piece.shape[0], [sib_b])
     keep_a, (gy_a, gx_a) = fold(keep_a, [x(fx_a), y(fy_a)], 2)
-    keep_b, (fx_b, fy_b) = put_rows(own_b, got_b, near_b, bases, [other])
+    keep_b, (fx_b, fy_b) = put_rows(own_b, got_b, facts_b, bases, piece.shape[0], [other])
     keep_a, (z_a,) = fold(keep_a, [y(gy_a), x(gx_a)], 1)
     keep_b, (gy_b, gx_b) = fold(keep_b, [x(fx_b), y(fy_b)], 2, [z_a])
     back_a = z(z_a, 1)
-    keep_b, (z_b,) = fold(keep_b, [y(gy_b), x(gx_b)], 1)
+    keep_b, (z_b,) = fold(keep_b, [y(gy_b), x(gx_b)], 1, [back_a])
     mine = keep_a.astype(jnp.float32) + back_a.astype(jnp.float32)
     over_z = (keep_b.astype(jnp.float32) + z(z_b, 1).astype(jnp.float32)).astype(jnp.bfloat16)
     return mine + z(over_z, 2).astype(jnp.float32), other
@@ -476,10 +492,7 @@
 
     keys, values = key_value[0, :, 0], key_value[0, :, 1]
 
-    def spans(a):
-        return jnp.stack([a[:, f * HEAD_DIM : f * HEAD_DIM + span] for f in firsts])
-
-    packed = jnp.concatenate([spans(query[0]), spans(keys), spans(values)], axis=2)
+    packed = pack_heads(query[0], keys, values, firsts, span)
     packed = lax.all_to_all(packed, "seq", split_axis=0, concat_axis=0, tiled=True)
     packed = packed.reshape(group, 3 * span)
     context = attention(packed, segment_ids[0], heads)

time: 274 us -> 247 us (0.901)
  local copies, waits for them, and re-layouts: 42.8 us -> 17.6 us
  starting transfers between devices: 50 us -> 44.6 us
  waiting for transfers between devices: 117 us -> 120 us
    slice x16 -> x0, local copies, waits for them, and re-layouts: 15.7 us -> none  [put_rows(): p[:, width:]]
    unnamed x102 -> x45, local copies, waits for them, and re-layouts: 21.9 us -> 12.6 us
    all_to_all x1, waiting for transfers between devices: 0.01 us -> 7.17 us  [fill_cache(): sent = lax.all_to_all(pages, 'seq', split_axis=0, concat_axis=0, tiled=True)]
    ppermute x30, starting transfers between devices: 34.6 us -> 29.3 us  [swap(): return lax.ppermute(a, axis, [(i, i ^ distance) for i in range(size)])]
    ppermute x30, waiting for transfers between devices: 81.4 us -> 78 us  [swap(): return lax.ppermute(a, axis, [(i, i ^ distance) for i in range(size)])]
    pallas_call x2 -> x3, Pallas kernels: 8.84 us -> 11.3 us  [the longest x2 8.84 us: put_rows(): pl.pallas_call(functools.partial(put_kernel, local, rows_dev, planes, len...]
  transfers between devices with their start and end apart: 33 -> 33, of which waited for: 16 -> 17; matrix products, arithmetic and copies ran while one was open for 7% -> 1% of each run, Pallas kernels for 18% -> 20%
where the time goes in v7:
time: 247 us; the launch traced here: 246 us
  waiting for transfers between devices  120 us (49%)
  Pallas kernels  60.5 us (24%)
  starting transfers between devices  44.6 us (18%)
  local copies, waits for them, and re-layouts  17.6 us (7%)
    ppermute x30, waiting for transfers between devices, swap(): return lax.ppermute(a, axis, [(i, i ^ distance) for i in range(size)])  78 us
    pallas_call x2, Pallas kernels, expert_rows(): pl.pallas_call(functools.partial(rows_kernel, local, len(waits)), out_sha...  29.5 us
    ppermute x30, starting transfers between devices, swap(): return lax.ppermute(a, axis, [(i, i ^ distance) for i in range(size)])  29.3 us
    all_to_all x1, waiting for transfers between devices, body(): lax.all_to_all(packed, 'seq', split_axis=0, concat_axis=0, tiled=True)  25.4 us
    unnamed x45, local copies, waits for them, and re-layouts  12.6 us
    all_to_all x1, waiting for transfers between devices, body(): lax.all_to_all(context.reshape(n_seq, rows_dev, span), 'seq', split_axis=...  9.79 us
    pallas_call x2, Pallas kernels, put_rows(): pl.pallas_call(functools.partial(put_kernel, local, rows_dev, planes, len...  8.84 us
    all_to_all x1, starting transfers between devices, body(): lax.all_to_all(packed, 'seq', split_axis=0, concat_axis=0, tiled=True)  7.25 us
  transfers between devices with their start and end apart: 33, of which 17 were waited for; matrix products, arithmetic and copies ran while one was open for 1% of the time, Pallas kernels for 20%

profile of v7, /device:TPU:0, one launch (start us, length us, event | category | flops | bytes accessed | tf_op | source)
XLA Modules:
  0.0 246.1 jit_solution(15593693891325114009)
XLA Ops:
  0.6 2.3 fusion.3
  3.8 2.4 shard_map.122
  6.2 7.3 %all-to-all-start = ((bf16[8,64,960]{2,1,0:T(8,128)(2,1)}), bf16[8,64,960]{2,1,0:T(8,128)(2,1)S(1)}, u32[]{:S(2)}, u32[]{:S(2)}) async-start(bf16[8,64,960]{2,1,0:T(8,128)(2,1)} %shard_map.122), calls=%async_computation | async-start | bytes 2097152 | tf_op jit(solution)/shard_map/all_to_all | solution.py:496
  13.9 25.4 %all-to-all-done = bf16[8,64,960]{2,1,0:T(8,128)(2,1)S(1)} async-done(((bf16[8,64,960]{2,1,0:T(8,128)(2,1)}), bf16[8,64,960]{2,1,0:T(8,128)(2,1)S(1)}, u32[]{:S(2)}, u32[]{:S(2)}) %all-to-all-start) | async-done | bytes 983072 | tf_op jit(solution)/shard_map/all_to_all | solution.py:496
  39.3 5.6 %shard_map.123 = bf16[512,320]{1,0:T(8,128)(2,1)} custom-call(bf16[512,960]{1,0:T(8,128)(2,1)S(1)} %bitcast.22, s32[1,512]{1,0:T(1,128)S(1)} %copy-done.11, s32[512,1]{1,0:T(8,128)S(1)} %copy.36.seg_col_ref), custom_call_target="tpu_custom_call" | custom-call | flops 335544320 | bytes 1310720 | tf_op jit(solution)/shard_map/pallas_call | solution.py:55
  44.9 3.6 %all-to-all-start.1 = ((bf16[8,64,320]{2,1,0:T(8,128)(2,1)}), bf16[8,64,320]{2,1,0:T(8,128)(2,1)S(1)}, u32[]{:S(2)}, u32[]{:S(2)}) async-start(bf16[8,64,320]{2,1,0:T(8,128)(2,1)} %bitcast.5), calls=%async_computation.1 | async-start | bytes 786432 | tf_op jit(solution)/shard_map/all_to_all | solution.py:499
  50.5 9.8 %all-to-all-done.1.context_ref = bf16[8,64,320]{2,1,0:T(8,128)(2,1)S(1)} async-done(((bf16[8,64,320]{2,1,0:T(8,128)(2,1)}), bf16[8,64,320]{2,1,0:T(8,128)(2,1)S(1)}, u32[]{:S(2)}, u32[]{:S(2)}) %all-to-all-start.1) | async-done | bytes 327712 | tf_op jit(solution)/shard_map/all_to_all | solution.py:499
  61.1 2.1 shard_map.124
  63.8 1.2 collective-permute-start.3
  64.9 1.7 collective-permute-start.1
  66.7 1.5 collective-permute-start
  68.2 9.8 %collective-permute-done.7.refs_0_ = bf16[64,2432]{1,0:T(8,128)(2,1)S(1)} collective-permute-done((bf16[64,2432]{1,0:T(8,128)(2,1)}, bf16[64,2432]{1,0:T(8,128)(2,1)S(1)}, u32[]{:S(2)}, u32[]{:S(2)}) %collective-permute-start.7) | collective-permute-done | bytes 311328 | tf_op jit(solution)/shard_map/ppermute | solution.py:392
  78.0 2.6 %collective-permute-start.9 = (bf16[64,2432]{1,0:T(8,128)(2,1)S(1)}, bf16[64,2432]{1,0:T(8,128)(2,1)S(1)}, u32[]{:S(2)}, u32[]{:S(2)}) collective-permute-start(bf16[64,2432]{1,0:T(8,128)(2,1)S(1)} %collective-permute-done.7.refs_0_), channel_id=1, source_target_pairs={{0,4},{4,0},{8,12},{12,8},{16,20},{20,16},{24,28},{28,24},{1,5},{5... | collective-permute-start | bytes 933896 | tf_op jit(solution)/shard_map/ppermute | solution.py:392
  80.6 1.5 collective-permute-start.8
  83.5 3.7 %collective-permute-done.10.refs_4_ = bf16[64,2432]{1,0:T(8,128)(2,1)} collective-permute-done((bf16[64,2432]{1,0:T(8,128)(2,1)S(1)}, bf16[64,2432]{1,0:T(8,128)(2,1)}, u32[]{:S(2)}, u32[]{:S(2)}) %collective-permute-start.10) | collective-permute-done | bytes 311328 | tf_op jit(solution)/shard_map/ppermute | solution.py:392
  87.2 1.5 collective-permute-start.2
  88.8 1.5 collective-permute-start.12
  90.8 1.5 collective-permute-start.11
  92.3 5.2 %collective-permute-done.5.refs_6_ = bf16[64,2432]{1,0:T(8,128)(2,1)S(1)} collective-permute-done((bf16[64,2432]{1,0:T(8,128)(2,1)S(1)}, bf16[64,2432]{1,0:T(8,128)(2,1)S(1)}, u32[]{:S(2)}, u32[]{:S(2)}) %collective-permute-start.5) | collective-permute-done | bytes 311328 | tf_op jit(solution)/shard_map/ppermute | solution.py:392
  97.8 6.4 %collective-permute-done.2.refs_3_ = bf16[64,2432]{1,0:T(8,128)(2,1)S(1)} collective-permute-done((bf16[64,2432]{1,0:T(8,128)(2,1)S(1)}, bf16[64,2432]{1,0:T(8,128)(2,1)S(1)}, u32[]{:S(2)}, u32[]{:S(2)}) %collective-permute-start.2) | collective-permute-done | bytes 311328 | tf_op jit(solution)/shard_map/ppermute | solution.py:392
  104.2 5.3 %collective-permute-done.12.refs_11_.refs_6_ = bf16[64,2432]{1,0:T(8,128)(2,1)S(1)} collective-permute-done((bf16[64,2432]{1,0:T(8,128)(2,1)}, bf16[64,2432]{1,0:T(8,128)(2,1)S(1)}, u32[]{:S(2)}, u32[]{:S(2)}) %collective-permute-start.12) | collective-permute-done | bytes 311328 | tf_op jit(solution)/shard_map/ppermute | solution.py:392
  110.5 1.9 shard_map.125
  112.5 1.6 collective-permute-start.14
  114.5 7.8 %collective-permute-done.14.refs_3_ = bf16[64,2432]{1,0:T(8,128)(2,1)S(1)} collective-permute-done((bf16[64,2432]{1,0:T(8,128)(2,1)S(1)}, bf16[64,2432]{1,0:T(8,128)(2,1)S(1)}, u32[]{:S(2)}, u32[]{:S(2)}) %collective-permute-start.14) | collective-permute-done | bytes 311328 | tf_op jit(solution)/shard_map/ppermute | solution.py:392
  122.3 1.2 collective-permute-done.15.refs_7_
  123.5 3.6 %shard_map.126 = (bf16[2,192,2304]{2,1,0:T(8,128)(2,1)S(1)}, bf16[2,192,2304]{2,1,0:T(8,128)(2,1)}, bf16[512,128]{1,0:T(8,128)(2,1)S(1)}) custom-call(s32[2]{0:T(128)S(1)} %add_multiply_fusion.bases_ref, bf16[64,2432]{1,0:T(8,128)(2,1)S(1)} %copy-done.13, bf16[64,2432]{1,0:T(8,128)(2,1)S(1)} %collective-permute-done.8.refs_8_.refs_1_, ...), custom_call_target="tpu_custom_call" | custom-call | flops 905969664 | bytes 6029312 | tf_op jit(solution)/shard_map/pallas_call | solution.py:272
  127.8 1.3 copy-done.14
  129.8 14.7 %shard_map.127 = (bf16[2,192,2304]{2,1,0:T(8,128)(2,1)S(1)}, bf16[2,192,2304]{2,1,0:T(8,128)(2,1)}) custom-call(bf16[2,192,2304]{2,1,0:T(8,128)(2,1)S(1)} %get-tuple-element.32.own_ref, bf16[2,192,2304]{2,1,0:T(8,128)(2,1)S(1)} %collective-permute-done.13.got_ref, bf16[2,720,2304]{2,1,0:T(8,128)(2,1)} %bitcast.29, bf16[2,720,2304]{2,1,0:T(8,128)(2,1)} %bitcast.31, ...), custom_call_target="tpu_custom_call" | custom-call | flops 7644119040 | bytes 26984448 | tf_op jit(solution)/shard_map/pallas_call | solution.py:320
  144.5 1.2 copy-done.2
  146.2 2.4 shard_map.128.rest_0_
  148.6 1.5 copy-done.15
  150.1 14.8 %shard_map.129 = (bf16[2,192,2304]{2,1,0:T(8,128)(2,1)S(1)}, bf16[2,192,2304]{2,1,0:T(8,128)(2,1)}) custom-call(bf16[2,192,2304]{2,1,0:T(8,128)(2,1)S(1)} %copy-done.15, bf16[2,192,2304]{2,1,0:T(8,128)(2,1)S(1)} %collective-permute-done.17.got_ref, bf16[2,720,2304]{2,1,0:T(8,128)(2,1)} %bitcast.30, bf16[2,720,2304]{2,1,0:T(8,128)(2,1)} %bitcast.32, ...), custom_call_target="tpu_custom_call" | custom-call | flops 7644119040 | bytes 26984448 | tf_op jit(solution)/shard_map/pallas_call | solution.py:320
  165.0 4.5 %all-to-all-start.2 = ((bf16[8,64,640]{2,1,0:T(8,128)(2,1)}), bf16[8,64,640]{2,1,0:T(8,128)(2,1)}, u32[]{:S(2)}, u32[]{:S(2)}) async-start(bf16[8,64,640]{2,1,0:T(8,128)(2,1)} %shard_map.128.rest_0_), calls=%async_computation.2 | async-start | bytes 1310720 | tf_op jit(solution)/shard_map/all_to_all | solution.py:516
  169.5 1.5 copy-done.3
  171.8 5.3 %shard_map.130 = (bf16[256,2304]{1,0:T(8,128)(2,1)S(1)}, bf16[128,2304]{1,0:T(8,128)(2,1)}, bf16[128,2304]{1,0:T(8,128)(2,1)}) custom-call(s32[2]{0:T(128)S(1)} %add_multiply_fusion.bases_ref, bf16[2,192,2304]{2,1,0:T(8,128)(2,1)S(1)} %copy-done.3, bf16[2,192,2304]{2,1,0:T(8,128)(2,1)} %collective-permute-done.16.y_got_ref, bf16[512,128]{1,0:T(8,128)(2,1)S(1)} %copy-done.8, ...), custom_call_target="tpu_custom_call" | custom-call | flops 905969664 | bytes 18874368 | tf_op jit(solution)/shard_map/pallas_call | solution.py:375
  178.1 1.6 collective-permute-start.18
  180.3 7.2 %all-to-all-done.2.pages_ref = bf16[8,64,640]{2,1,0:T(8,128)(2,1)} async-done(((bf16[8,64,640]{2,1,0:T(8,128)(2,1)}), bf16[8,64,640]{2,1,0:T(8,128)(2,1)}, u32[]{:S(2)}, u32[]{:S(2)}) %all-to-all-start.2) | async-done | bytes 655392 | tf_op jit(solution)/shard_map/all_to_all | solution.py:516
  187.5 2.1 shard_map.133.rest_0_
  191.5 3.6 %shard_map.134 = (bf16[256,2304]{1,0:T(8,128)(2,1)S(1)}, bf16[128,2304]{1,0:T(8,128)(2,1)S(1)}, bf16[128,2304]{1,0:T(8,128)(2,1)S(1)}) custom-call(s32[2]{0:T(128)S(1)} %add_multiply_fusion.bases_ref, bf16[2,192,2304]{2,1,0:T(8,128)(2,1)S(1)} %get-tuple-element.48.y_own_ref, bf16[2,192,2304]{2,1,0:T(8,128)(2,1)S(1)} %collective-permute-done.23.y_got_ref, ...), custom_call_target="tpu_custom_call" | custom-call | flops 905969664 | bytes 18874368 | tf_op jit(solution)/shard_map/pallas_call | solution.py:375
  195.1 1.5 collective-permute-start.24
  197.1 1.5 shard_map.131
  198.6 1.6 collective-permute-start.20
  200.8 16.8 %collective-permute-done.20.rest_0_ = bf16[64,2304]{1,0:T(8,128)(2,1)S(1)} collective-permute-done((bf16[64,2304]{1,0:T(8,128)(2,1)S(1)}, bf16[64,2304]{1,0:T(8,128)(2,1)S(1)}, u32[]{:S(2)}, u32[]{:S(2)}) %collective-permute-start.20) | collective-permute-done | bytes 294944 | tf_op jit(solution)/shard_map/ppermute | solution.py:392
  219.2 5.9 %collective-permute-done.22.rest_2_ = bf16[64,2304]{1,0:T(8,128)(2,1)S(1)} collective-permute-done((bf16[64,2304]{1,0:T(8,128)(2,1)S(1)}, bf16[64,2304]{1,0:T(8,128)(2,1)S(1)}, u32[]{:S(2)}, u32[]{:S(2)}) %collective-permute-start.22) | collective-permute-done | bytes 294944 | tf_op jit(solution)/shard_map/ppermute | solution.py:392
  225.9 1.8 collective-permute-start.28
  227.7 6.0 %collective-permute-done.28 = bf16[64,2304]{1,0:T(8,128)(2,1)S(1)} collective-permute-done((bf16[64,2304]{1,0:T(8,128)(2,1)S(1)}, bf16[64,2304]{1,0:T(8,128)(2,1)S(1)}, u32[]{:S(2)}, u32[]{:S(2)}) %collective-permute-start.28) | collective-permute-done | bytes 294944 | tf_op jit(solution)/shard_map/ppermute | solution.py:392
  233.8 2.9 %collective-permute-start.29 = (bf16[64,2304]{1,0:T(8,128)(2,1)S(1)}, bf16[64,2304]{1,0:T(8,128)(2,1)S(1)}, u32[]{:S(2)}, u32[]{:S(2)}) collective-permute-start(bf16[64,2304]{1,0:T(8,128)(2,1)S(1)} %add_convert_fusion.1), channel_id=1, source_target_pairs={{0,16},{4,20},{8,24},{12,28},{16,0},{20,4},{24,8},{28,12},{1,17},{... | collective-permute-start | bytes 884744 | tf_op jit(solution)/shard_map/ppermute | solution.py:392
  236.6 8.6 %collective-permute-done.29 = bf16[64,2304]{1,0:T(8,128)(2,1)S(1)} collective-permute-done((bf16[64,2304]{1,0:T(8,128)(2,1)S(1)}, bf16[64,2304]{1,0:T(8,128)(2,1)S(1)}, u32[]{:S(2)}, u32[]{:S(2)}) %collective-permute-start.29) | collective-permute-done | bytes 294944 | tf_op jit(solution)/shard_map/ppermute | solution.py:392
  (96 shorter events, 19.0 us)
Async XLA Ops:
  3.8 9.7 %copy-start.11 = (s32[1,512]{1,0:T(1,128)S(1)}, s32[1,512]{1,0:T(1,128)}, u32[]{:S(2)}) copy-start(s32[1,512]{1,0:T(1,128)} %seg_row_ref.1) | copy-start | bytes 6148
  3.8 9.8 %copy-start.19 = (s32[1,64,2]{1,2,0:T(2,128)S(1)}, s32[1,64,2]{1,2,0:T(2,128)}, u32[]{:S(2)}) copy-start(s32[1,64,2]{1,2,0:T(2,128)} %param.16) | copy-start | bytes 1540
  6.2 33.0 %all-to-all-start = ((bf16[8,64,960]{2,1,0:T(8,128)(2,1)}), bf16[8,64,960]{2,1,0:T(8,128)(2,1)S(1)}, u32[]{:S(2)}, u32[]{:S(2)}) async-start(bf16[8,64,960]{2,1,0:T(8,128)(2,1)} %shard_map.122), calls=%async_computation | async-start | bytes 2097152 | tf_op jit(solution)/shard_map/all_to_all | solution.py:496
  39.3 9.8 %copy-start = (bf16[8,64,960]{2,1,0:T(8,128)(2,1)}, bf16[8,64,960]{2,1,0:T(8,128)(2,1)S(1)}, u32[]{:S(2)}) copy-start(bf16[8,64,960]{2,1,0:T(8,128)(2,1)S(1)} %all-to-all-done) | copy-start | bytes 2949124
  39.3 9.9 %copy-start.20 = (f32[1,64,2]{1,2,0:T(2,128)S(1)}, f32[1,64,2]{1,2,0:T(2,128)}, u32[]{:S(2)}) copy-start(f32[1,64,2]{1,2,0:T(2,128)} %param.17) | copy-start | bytes 1540
  39.3 10.0 %copy-start.18 = (bf16[2304]{0:T(1024)(128)(2,1)S(1)}, bf16[2304]{0:T(1024)(128)(2,1)}, u32[]{:S(2)}) copy-start(bf16[2304]{0:T(1024)(128)(2,1)} %param.14) | copy-start | bytes 13828
  44.9 15.5 %all-to-all-start.1 = ((bf16[8,64,320]{2,1,0:T(8,128)(2,1)}), bf16[8,64,320]{2,1,0:T(8,128)(2,1)S(1)}, u32[]{:S(2)}, u32[]{:S(2)}) async-start(bf16[8,64,320]{2,1,0:T(8,128)(2,1)} %bitcast.5), calls=%async_computation.1 | async-start | bytes 786432 | tf_op jit(solution)/shard_map/all_to_all | solution.py:499
  63.2 14.8 %collective-permute-start.7 = (bf16[64,2432]{1,0:T(8,128)(2,1)}, bf16[64,2432]{1,0:T(8,128)(2,1)S(1)}, u32[]{:S(2)}, u32[]{:S(2)}) collective-permute-start(bf16[64,2432]{1,0:T(8,128)(2,1)} %get-tuple-element.31.refs_0_), channel_id=1, source_target_pairs={{0,16},{4,20},{8,24},{12,28},{16,0},{20,4},{24,8},{28,12},{1,17},{... | collective-permute-start | bytes 933896 | tf_op jit(solution)/shard_map/ppermute | solution.py:392
  63.8 16.8 %collective-permute-start.3 = (bf16[64,2432]{1,0:T(8,128)(2,1)}, bf16[64,2432]{1,0:T(8,128)(2,1)S(1)}, u32[]{:S(2)}, u32[]{:S(2)}) collective-permute-start(bf16[64,2432]{1,0:T(8,128)(2,1)} %get-tuple-element.31.refs_0_), channel_id=1, source_target_pairs={{0,8},{4,12},{8,0},{12,4},{16,24},{20,28},{24,16},{28,20},{1,9},{5... | collective-permute-start | bytes 933896 | tf_op jit(solution)/shard_map/ppermute | solution.py:392
  64.9 17.9 %collective-permute-start.1 = (bf16[64,2432]{1,0:T(8,128)(2,1)}, bf16[64,2432]{1,0:T(8,128)(2,1)S(1)}, u32[]{:S(2)}, u32[]{:S(2)}) collective-permute-start(bf16[64,2432]{1,0:T(8,128)(2,1)} %get-tuple-element.31.refs_0_), channel_id=1, source_target_pairs={{0,4},{4,0},{8,12},{12,8},{16,20},{20,16},{24,28},{28,24},{1,5},{5... | collective-permute-start | bytes 933896 | tf_op jit(solution)/shard_map/ppermute | solution.py:392
  66.7 16.6 %collective-permute-start = (bf16[64,2432]{1,0:T(8,128)(2,1)}, bf16[64,2432]{1,0:T(8,128)(2,1)S(1)}, u32[]{:S(2)}, u32[]{:S(2)}) collective-permute-start(bf16[64,2432]{1,0:T(8,128)(2,1)} %get-tuple-element.31.refs_0_), channel_id=1, source_target_pairs={{0,2},{1,3},{2,0},{3,1},{4,6},{5,7},{6,4},{7,5},{8,10},{9,11},{10,... | collective-permute-start | bytes 933896 | tf_op jit(solution)/shard_map/ppermute | solution.py:392
  78.0 9.2 %collective-permute-start.10 = (bf16[64,2432]{1,0:T(8,128)(2,1)S(1)}, bf16[64,2432]{1,0:T(8,128)(2,1)}, u32[]{:S(2)}, u32[]{:S(2)}) collective-permute-start(bf16[64,2432]{1,0:T(8,128)(2,1)S(1)} %collective-permute-done.7.refs_0_), channel_id=1, source_target_pairs={{0,8},{4,12},{8,0},{12,4},{16,24},{20,28},{24,16},{28,20},{1,9},{5... | collective-permute-start | bytes 933896 | tf_op jit(solution)/shard_map/ppermute | solution.py:392
  78.0 10.8 %collective-permute-start.9 = (bf16[64,2432]{1,0:T(8,128)(2,1)S(1)}, bf16[64,2432]{1,0:T(8,128)(2,1)S(1)}, u32[]{:S(2)}, u32[]{:S(2)}) collective-permute-start(bf16[64,2432]{1,0:T(8,128)(2,1)S(1)} %collective-permute-done.7.refs_0_), channel_id=1, source_target_pairs={{0,4},{4,0},{8,12},{12,8},{16,20},{20,16},{24,28},{28,24},{1,5},{5... | collective-permute-start | bytes 933896 | tf_op jit(solution)/shard_map/ppermute | solution.py:392
  80.6 10.3 %collective-permute-start.8 = (bf16[64,2432]{1,0:T(8,128)(2,1)S(1)}, bf16[64,2432]{1,0:T(8,128)(2,1)S(1)}, u32[]{:S(2)}, u32[]{:S(2)}) collective-permute-start(bf16[64,2432]{1,0:T(8,128)(2,1)S(1)} %collective-permute-done.7.refs_0_), channel_id=1, source_target_pairs={{0,2},{1,3},{2,0},{3,1},{4,6},{5,7},{6,4},{7,5},{8,10},{9,11},{10,... | collective-permute-start | bytes 933896 | tf_op jit(solution)/shard_map/ppermute | solution.py:392
  82.8 14.7 %collective-permute-start.5 = (bf16[64,2432]{1,0:T(8,128)(2,1)S(1)}, bf16[64,2432]{1,0:T(8,128)(2,1)S(1)}, u32[]{:S(2)}, u32[]{:S(2)}) collective-permute-start(bf16[64,2432]{1,0:T(8,128)(2,1)S(1)} %collective-permute-done.3.refs_4_), channel_id=1, source_target_pairs={{0,2},{1,3},{2,0},{3,1},{4,6},{5,7},{6,4},{7,5},{8,10},{9,11},{10,... | collective-permute-start | bytes 933896 | tf_op jit(solution)/shard_map/ppermute | solution.py:392
  83.3 14.4 %collective-permute-start.4 = (bf16[64,2432]{1,0:T(8,128)(2,1)S(1)}, bf16[64,2432]{1,0:T(8,128)(2,1)S(1)}, u32[]{:S(2)}, u32[]{:S(2)}) collective-permute-start(bf16[64,2432]{1,0:T(8,128)(2,1)S(1)} %collective-permute-done.3.refs_4_), channel_id=1, source_target_pairs={{0,4},{4,0},{8,12},{12,8},{16,20},{20,16},{24,28},{28,24},{1,5},{5... | collective-permute-start | bytes 933896 | tf_op jit(solution)/shard_map/ppermute | solution.py:392
  87.2 16.9 %collective-permute-start.2 = (bf16[64,2432]{1,0:T(8,128)(2,1)S(1)}, bf16[64,2432]{1,0:T(8,128)(2,1)S(1)}, u32[]{:S(2)}, u32[]{:S(2)}) collective-permute-start(bf16[64,2432]{1,0:T(8,128)(2,1)S(1)} %collective-permute-done.1.refs_2_), channel_id=1, source_target_pairs={{0,2},{1,3},{2,0},{3,1},{4,6},{5,7},{6,4},{7,5},{8,10},{9,11},{10,... | collective-permute-start | bytes 933896 | tf_op jit(solution)/shard_map/ppermute | solution.py:392
  88.8 20.8 %collective-permute-start.12 = (bf16[64,2432]{1,0:T(8,128)(2,1)}, bf16[64,2432]{1,0:T(8,128)(2,1)S(1)}, u32[]{:S(2)}, u32[]{:S(2)}) collective-permute-start(bf16[64,2432]{1,0:T(8,128)(2,1)} %collective-permute-done.10.refs_4_), channel_id=1, source_target_pairs={{0,2},{1,3},{2,0},{3,1},{4,6},{5,7},{6,4},{7,5},{8,10},{9,11},{10,... | collective-permute-start | bytes 933896 | tf_op jit(solution)/shard_map/ppermute | solution.py:392
  90.8 18.7 %collective-permute-start.11 = (bf16[64,2432]{1,0:T(8,128)(2,1)}, bf16[64,2432]{1,0:T(8,128)(2,1)S(1)}, u32[]{:S(2)}, u32[]{:S(2)}) collective-permute-start(bf16[64,2432]{1,0:T(8,128)(2,1)} %collective-permute-done.10.refs_4_), channel_id=1, source_target_pairs={{0,4},{4,0},{8,12},{12,8},{16,20},{20,16},{24,28},{28,24},{1,5},{5... | collective-permute-start | bytes 933896 | tf_op jit(solution)/shard_map/ppermute | solution.py:392
  97.5 12.0 %collective-permute-start.6 = (bf16[64,2432]{1,0:T(8,128)(2,1)S(1)}, bf16[64,2432]{1,0:T(8,128)(2,1)S(1)}, u32[]{:S(2)}, u32[]{:S(2)}) collective-permute-start(bf16[64,2432]{1,0:T(8,128)(2,1)S(1)} %collective-permute-done.5.refs_6_), channel_id=1, source_target_pairs={{0,4},{4,0},{8,12},{12,8},{16,20},{20,16},{24,28},{28,24},{1,5},{5... | collective-permute-start | bytes 933896 | tf_op jit(solution)/shard_map/ppermute | solution.py:392
  110.5 13.0 %copy-start.13 = (bf16[64,2432]{1,0:T(8,128)(2,1)S(1)}, bf16[64,2432]{1,0:T(8,128)(2,1)}, u32[]{:S(2)}) copy-start(bf16[64,2432]{1,0:T(8,128)(2,1)} %copy-done.12) | copy-start | bytes 933892
  112.4 17.3 %copy-start.7 = (bf16[512,128]{1,0:T(8,128)(2,1)}, bf16[512,128]{1,0:T(8,128)(2,1)S(1)}, u32[]{:S(2)}) copy-start(bf16[512,128]{1,0:T(8,128)(2,1)S(1)} %get-tuple-element.37.facts_ref) | copy-start | bytes 393220
  112.4 16.7 %copy-start.21 = (s32[1,32]{1,0:T(1,128)S(1)}, s32[1,32]{1,0:T(1,128)}, u32[]{:S(2)}) copy-start(s32[1,32]{1,0:T(1,128)} %param.18) | copy-start | bytes 388
  112.4 17.3 %collective-permute-start.13 = (bf16[2,192,2304]{2,1,0:T(8,128)(2,1)S(1)}, bf16[2,192,2304]{2,1,0:T(8,128)(2,1)S(1)}, u32[]{:S(2)}, u32[]{:S(2)}) collective-permute-start(bf16[2,192,2304]{2,1,0:T(8,128)(2,1)S(1)} %get-tuple-element.33), channel_id=1, source_target_pairs={{0,1},{1,0},{2,3},{3,2},{4,5},{5,4},{6,7},{7,6},{8,9},{9,8},{10,11... | collective-permute-start | bytes 5308424 | tf_op jit(solution)/shard_map/ppermute | solution.py:392
  112.5 9.8 %collective-permute-start.14 = (bf16[64,2432]{1,0:T(8,128)(2,1)S(1)}, bf16[64,2432]{1,0:T(8,128)(2,1)S(1)}, u32[]{:S(2)}, u32[]{:S(2)}) collective-permute-start(bf16[64,2432]{1,0:T(8,128)(2,1)S(1)} %collective-permute-done.9.refs_9_.refs_2_), channel_id=1, source_target_pairs={{0,2},{1,3},{2,0},{3,1},{4,6},{5,7},{6,4},{7,5},{8,10},{9,11},{10,... | collective-permute-start | bytes 933896 | tf_op jit(solution)/shard_map/ppermute | solution.py:392
  114.1 9.4 %collective-permute-start.15 = (bf16[64,2432]{1,0:T(8,128)(2,1)S(1)}, bf16[64,2432]{1,0:T(8,128)(2,1)S(1)}, u32[]{:S(2)}, u32[]{:S(2)}) collective-permute-start(bf16[64,2432]{1,0:T(8,128)(2,1)S(1)} %collective-permute-done.12.refs_11_.refs_6_), channel_id=1, source_target_pairs={{0,4},{4,0},{8,12},{12,8},{16,20},{20,16},{24,28},{28,24},{1,5},{5... | collective-permute-start | bytes 933896 | tf_op jit(solution)/shard_map/ppermute | solution.py:392
  127.8 1.3 copy-start.14
  129.1 19.5 %collective-permute-start.17 = (bf16[2,192,2304]{2,1,0:T(8,128)(2,1)}, bf16[2,192,2304]{2,1,0:T(8,128)(2,1)S(1)}, u32[]{:S(2)}, u32[]{:S(2)}) collective-permute-start(bf16[2,192,2304]{2,1,0:T(8,128)(2,1)} %get-tuple-element.34.rest_0_), channel_id=1, source_target_pairs={{0,1},{1,0},{2,3},{3,2},{4,5},{5,4},{6,7},{7,6},{8,9},{9,8},{10,11... | collective-permute-start | bytes 5308424 | tf_op jit(solution)/shard_map/ppermute | solution.py:392
  144.5 1.2 copy-start.2
  145.7 23.7 %collective-permute-start.16 = (bf16[2,192,2304]{2,1,0:T(8,128)(2,1)}, bf16[2,192,2304]{2,1,0:T(8,128)(2,1)}, u32[]{:S(2)}, u32[]{:S(2)}) collective-permute-start(bf16[2,192,2304]{2,1,0:T(8,128)(2,1)} %get-tuple-element.36.late_ref.rest_1_), channel_id=1, source_target_pairs={{0,1},{1,0},{2,3},{3,2},{4,5},{5,4},{6,7},{7,6},{8,9},{9,8},{10,11... | collective-permute-start | bytes 5308424 | tf_op jit(solution)/shard_map/ppermute | solution.py:392
  148.6 1.5 copy-start.15
  164.9 24.6 %collective-permute-start.23 = (bf16[2,192,2304]{2,1,0:T(8,128)(2,1)}, bf16[2,192,2304]{2,1,0:T(8,128)(2,1)S(1)}, u32[]{:S(2)}, u32[]{:S(2)}) collective-permute-start(bf16[2,192,2304]{2,1,0:T(8,128)(2,1)} %get-tuple-element.39.rest_0_), channel_id=1, source_target_pairs={{0,1},{1,0},{2,3},{3,2},{4,5},{5,4},{6,7},{7,6},{8,9},{9,8},{10,11... | collective-permute-start | bytes 5308424 | tf_op jit(solution)/shard_map/ppermute | solution.py:392
  165.0 22.5 %all-to-all-start.2 = ((bf16[8,64,640]{2,1,0:T(8,128)(2,1)}), bf16[8,64,640]{2,1,0:T(8,128)(2,1)}, u32[]{:S(2)}, u32[]{:S(2)}) async-start(bf16[8,64,640]{2,1,0:T(8,128)(2,1)} %shard_map.128.rest_0_), calls=%async_computation.2 | async-start | bytes 1310720 | tf_op jit(solution)/shard_map/all_to_all | solution.py:516
  169.5 1.5 copy-start.3
  178.1 18.9 %collective-permute-start.18 = (bf16[128,2304]{1,0:T(8,128)(2,1)}, bf16[128,2304]{1,0:T(8,128)(2,1)}, u32[]{:S(2)}, u32[]{:S(2)}) collective-permute-start(bf16[128,2304]{1,0:T(8,128)(2,1)} %get-tuple-element.41), channel_id=1, source_target_pairs={{0,4},{4,0},{8,12},{12,8},{16,20},{20,16},{24,28},{28,24},{1,5},{5... | collective-permute-start | bytes 1769480 | tf_op jit(solution)/shard_map/ppermute | solution.py:392
  179.8 17.3 %collective-permute-start.19 = (bf16[128,2304]{1,0:T(8,128)(2,1)}, bf16[128,2304]{1,0:T(8,128)(2,1)}, u32[]{:S(2)}, u32[]{:S(2)}) collective-permute-start(bf16[128,2304]{1,0:T(8,128)(2,1)} %get-tuple-element.42), channel_id=1, source_target_pairs={{0,2},{1,3},{2,0},{3,1},{4,6},{5,7},{6,4},{7,5},{8,10},{9,11},{10,... | collective-permute-start | bytes 1769480 | tf_op jit(solution)/shard_map/ppermute | solution.py:392
  189.5 1.1 copy-start.1
  191.5 5.6 %copy-start.5 = (bf16[256,2304]{1,0:T(8,128)(2,1)S(1)}, bf16[256,2304]{1,0:T(8,128)(2,1)}, u32[]{:S(2)}) copy-start(bf16[256,2304]{1,0:T(8,128)(2,1)} %copy-done.4) | copy-start | bytes 3538948
  195.1 22.7 %collective-permute-start.24 = (bf16[128,2304]{1,0:T(8,128)(2,1)S(1)}, bf16[128,2304]{1,0:T(8,128)(2,1)S(1)}, u32[]{:S(2)}, u32[]{:S(2)}) collective-permute-start(bf16[128,2304]{1,0:T(8,128)(2,1)S(1)} %get-tuple-element.51), channel_id=1, source_target_pairs={{0,4},{4,0},{8,12},{12,8},{16,20},{20,16},{24,28},{28,24},{1,5},{5... | collective-permute-start | bytes 1769480 | tf_op jit(solution)/shard_map/ppermute | solution.py:392
  196.6 21.2 %collective-permute-start.25 = (bf16[128,2304]{1,0:T(8,128)(2,1)S(1)}, bf16[128,2304]{1,0:T(8,128)(2,1)S(1)}, u32[]{:S(2)}, u32[]{:S(2)}) collective-permute-start(bf16[128,2304]{1,0:T(8,128)(2,1)S(1)} %get-tuple-element.52), channel_id=1, source_target_pairs={{0,2},{1,3},{2,0},{3,1},{4,6},{5,7},{6,4},{7,5},{8,10},{9,11},{10,... | collective-permute-start | bytes 1769480 | tf_op jit(solution)/shard_map/ppermute | solution.py:392
  198.6 18.9 %collective-permute-start.20 = (bf16[64,2304]{1,0:T(8,128)(2,1)S(1)}, bf16[64,2304]{1,0:T(8,128)(2,1)S(1)}, u32[]{:S(2)}, u32[]{:S(2)}) collective-permute-start(bf16[64,2304]{1,0:T(8,128)(2,1)S(1)} %get-tuple-element.44), channel_id=1, source_target_pairs={{0,2},{1,3},{2,0},{3,1},{4,6},{5,7},{6,4},{7,5},{8,10},{9,11},{10,... | collective-permute-start | bytes 884744 | tf_op jit(solution)/shard_map/ppermute | solution.py:392
  200.2 17.4 %collective-permute-start.21 = (bf16[64,2304]{1,0:T(8,128)(2,1)S(1)}, bf16[64,2304]{1,0:T(8,128)(2,1)S(1)}, u32[]{:S(2)}, u32[]{:S(2)}) collective-permute-start(bf16[64,2304]{1,0:T(8,128)(2,1)S(1)} %get-tuple-element.45), channel_id=1, source_target_pairs={{0,4},{4,0},{8,12},{12,8},{16,20},{20,16},{24,28},{28,24},{1,5},{5... | collective-permute-start | bytes 884744 | tf_op jit(solution)/shard_map/ppermute | solution.py:392
  217.7 7.5 %collective-permute-start.22 = (bf16[64,2304]{1,0:T(8,128)(2,1)S(1)}, bf16[64,2304]{1,0:T(8,128)(2,1)S(1)}, u32[]{:S(2)}, u32[]{:S(2)}) collective-permute-start(bf16[64,2304]{1,0:T(8,128)(2,1)S(1)} %get-tuple-element.47.rest_2_), channel_id=1, source_target_pairs={{0,8},{4,12},{8,0},{12,4},{16,24},{20,28},{24,16},{28,20},{1,9},{5... | collective-permute-start | bytes 884744 | tf_op jit(solution)/shard_map/ppermute | solution.py:392
  218.1 27.2 %copy-start.17 = (f32[64,2304]{1,0:T(8,128)S(1)}, f32[64,2304]{1,0:T(8,128)}, u32[]{:S(2)}) copy-start(f32[64,2304]{1,0:T(8,128)} %get-tuple-element.30) | copy-start | bytes 1769476
  218.1 7.5 %collective-permute-start.26 = (bf16[64,2304]{1,0:T(8,128)(2,1)S(1)}, bf16[64,2304]{1,0:T(8,128)(2,1)S(1)}, u32[]{:S(2)}, u32[]{:S(2)}) collective-permute-start(bf16[64,2304]{1,0:T(8,128)(2,1)S(1)} %get-tuple-element.54), channel_id=1, source_target_pairs={{0,2},{1,3},{2,0},{3,1},{4,6},{5,7},{6,4},{7,5},{8,10},{9,11},{10,... | collective-permute-start | bytes 884744 | tf_op jit(solution)/shard_map/ppermute | solution.py:392
  218.6 7.1 %collective-permute-start.27 = (bf16[64,2304]{1,0:T(8,128)(2,1)S(1)}, bf16[64,2304]{1,0:T(8,128)(2,1)S(1)}, u32[]{:S(2)}, u32[]{:S(2)}) collective-permute-start(bf16[64,2304]{1,0:T(8,128)(2,1)S(1)} %get-tuple-element.55), channel_id=1, source_target_pairs={{0,4},{4,0},{8,12},{12,8},{16,20},{20,16},{24,28},{28,24},{1,5},{5... | collective-permute-start | bytes 884744 | tf_op jit(solution)/shard_map/ppermute | solution.py:392
  225.9 7.8 %collective-permute-start.28 = (bf16[64,2304]{1,0:T(8,128)(2,1)S(1)}, bf16[64,2304]{1,0:T(8,128)(2,1)S(1)}, u32[]{:S(2)}, u32[]{:S(2)}) collective-permute-start(bf16[64,2304]{1,0:T(8,128)(2,1)S(1)} %get-tuple-element.57), channel_id=1, source_target_pairs={{0,8},{4,12},{8,0},{12,4},{16,24},{20,28},{24,16},{28,20},{1,9},{5... | collective-permute-start | bytes 884744 | tf_op jit(solution)/shard_map/ppermute | solution.py:392
  233.8 11.5 %collective-permute-start.29 = (bf16[64,2304]{1,0:T(8,128)(2,1)S(1)}, bf16[64,2304]{1,0:T(8,128)(2,1)S(1)}, u32[]{:S(2)}, u32[]{:S(2)}) collective-permute-start(bf16[64,2304]{1,0:T(8,128)(2,1)S(1)} %add_convert_fusion.1), channel_id=1, source_target_pairs={{0,16},{4,20},{8,24},{12,28},{16,0},{20,4},{24,8},{28,12},{1,17},{... | collective-permute-start | bytes 884744 | tf_op jit(solution)/shard_map/ppermute | solution.py:392
  (7 other events, 5.9 us)

commit v8 on v7

--- a/solution.py
+++ b/solution.py
@@ -208,7 +208,8 @@
     )(order, packed, late)
 
 
-def join_pages_kernel(share, offsets, span, pages_ref, out_ref):
+def join_pages_kernel(share, offsets, span, pages_ref, behind_ref, out_ref):
+    del behind_ref
     width = share * len(offsets)
     for part in range(2):
         parts = [
@@ -218,13 +219,14 @@
         out_ref[:, part * width : (part + 1) * width] = jnp.concatenate(parts, axis=1)
 
 
-def join_pages(pages, share, offsets, span):
+def join_pages(pages, share, offsets, span, behind):
     n_seq, rows, _ = pages.shape
     return pl.pallas_call(
         functools.partial(join_pages_kernel, share, offsets, span),
         out_shape=jax.ShapeDtypeStruct((rows, 2 * share * n_seq), jnp.bfloat16),
+        in_specs=[pl.BlockSpec(memory_space=pltpu.VMEM), pl.BlockSpec(memory_space=pl.ANY)],
         cost_estimate=pl.CostEstimate(flops=0, bytes_accessed=8 * rows * n_seq * span, transcendentals=0),
-    )(pages)
+    )(pages, behind)
 
 
 def places_of(slots, base, shift):
@@ -233,6 +235,19 @@
         slot = slot.astype(jnp.int32) - base
         place = jnp.where((slot >= 0) & (slot < CAP), shift + slot, place)
     return place
+
+
+def hold_kernel(a_ref, *rest):
+    rest[-1][...] = a_ref[...]
+
+
+def hold(a, waits):
+    return pl.pallas_call(
+        hold_kernel,
+        out_shape=jax.ShapeDtypeStruct(a.shape, a.dtype),
+        in_specs=[pl.BlockSpec(memory_space=pltpu.VMEM)] + [pl.BlockSpec(memory_space=pl.ANY)] * len(waits),
+        cost_estimate=pl.CostEstimate(flops=0, bytes_accessed=4 * a.size, transcendentals=0),
+    )(a, *waits)
 
 
 def facts_by_lane(x):
@@ -432,35 +447,39 @@
     me = lax.axis_index("exp").astype(jnp.int32)
     bases = jnp.stack([me, me ^ 1]) * local
     starts = [piece, z(piece, 1), z(piece, 2)]
+    ways = [("xy", "yx")[k % 2] for k in range(4)]
+    over = {"x": x, "y": y}
+    single = [[over[way](starts[k]) for way in ways[k]] for k in range(2)]
+    starts[2] = hold(starts[2], single[0] + single[1])
     starts.append(z(starts[2], 1))
+    single += [[over[way](starts[k]) for way in ways[k]] for k in range(2, 4)]
 
     def gather(k):
         near = []
-        for start, (f, g) in ((starts[k], (x, y)), (starts[k + 1], (y, x))):
-            by_f = f(start)
-            near += [start, g(start), by_f, g(by_f)]
+        for i in (k, k + 1):
+            by_f, by_g = single[i]
+            near += [starts[i], by_g, by_f, over[ways[i][1]](by_f)]
         return near
 
-    near_a, near_b = gather(0), gather(2)
-    first_b = [near_b[1], near_b[2], near_b[5], near_b[6]]
-    own_a, sib_a, facts_a = select_rows(near_a, bases, local, first_b)
+    near_b, near_a = gather(0), gather(2)
+    own_a, sib_a, facts_a = select_rows(near_a, bases, local)
     got_a = core(sib_a)
     own_b, sib_b, facts_b = select_rows(near_b, bases, local)
     got_b = core(sib_b)
-    own_a, sib_a = expert_rows(own_a, got_a, w_gate, w_up, w_down, [sib_b])
-    pages, other = late_work(sib_a)
+    pages, fill = late_work(sib_b)
+    own_a, sib_a = expert_rows(own_a, got_a, w_gate, w_up, w_down, [sib_b, pages])
+    other = fill(sib_a)
     got_a = core(sib_a)
-    own_b, sib_b = expert_rows(own_b, got_b, w_gate, w_up, w_down, [pages, sib_a])
+    own_b, sib_b = expert_rows(own_b, got_b, w_gate, w_up, w_down, [other, sib_a])
     got_b = core(sib_b)
     keep_a, (fx_a, fy_a) = put_rows(own_a, got_a, facts_a, bases, piece.shape[0], [sib_b])
     keep_a, (gy_a, gx_a) = fold(keep_a, [x(fx_a), y(fy_a)], 2)
-    keep_b, (fx_b, fy_b) = put_rows(own_b, got_b, facts_b, bases, piece.shape[0], [other])
+    keep_b, (fx_b, fy_b) = put_rows(own_b, got_b, facts_b, bases, piece.shape[0], [gy_a])
     keep_a, (z_a,) = fold(keep_a, [y(gy_a), x(gx_a)], 1)
     keep_b, (gy_b, gx_b) = fold(keep_b, [x(fx_b), y(fy_b)], 2, [z_a])
-    back_a = z(z_a, 1)
-    keep_b, (z_b,) = fold(keep_b, [y(gy_b), x(gx_b)], 1, [back_a])
-    mine = keep_a.astype(jnp.float32) + back_a.astype(jnp.float32)
-    over_z = (keep_b.astype(jnp.float32) + z(z_b, 1).astype(jnp.float32)).astype(jnp.bfloat16)
+    over_z = (keep_a.astype(jnp.float32) + z(z_a, 1).astype(jnp.float32)).astype(jnp.bfloat16)
+    keep_b, (z_b,) = fold(keep_b, [y(gy_b), x(gx_b)], 1, [over_z])
+    mine = keep_b.astype(jnp.float32) + z(z_b, 1).astype(jnp.float32)
     return mine + z(over_z, 2).astype(jnp.float32), other
 
 
@@ -514,12 +533,12 @@
     def fill_cache(late):
         pages = pick_pages(packed, order, late, n_seq, span)
         sent = lax.all_to_all(pages, "seq", split_axis=0, concat_axis=0, tiled=True)
-        return pages, join_pages(sent, share, offsets, span)
+        return pages, lambda behind: join_pages(sent, share, offsets, span, behind)
 
     if (n_seq, n_exp) == (8, 4):
         mixture, cache = exchange_experts(piece, w_gate, w_up, w_down, n_seq, n_exp, fill_cache)
     else:
-        _, cache = fill_cache(piece)
+        cache = fill_cache(piece)[1](piece)
         blocks = n_seq * n_exp
         everything = lax.all_gather(piece, everyone, axis=0, tiled=True)
         facts = everything[:, width : width + 8].astype(jnp.float32)

time: 247 us -> 258 us (1.045)
  local copies, waits for them, and re-layouts: 17.6 us -> 25.9 us
  starting transfers between devices: 44.6 us -> 52.4 us
  waiting for transfers between devices: 120 us -> 114 us
    unnamed x45 -> x83, local copies, waits for them, and re-layouts: 12.6 us -> 21 us
    ppermute x30, starting transfers between devices: 29.3 us -> 36.8 us  [swap(): return lax.ppermute(a, axis, [(i, i ^ distance) for i in range(size)])]
    all_to_all x1, waiting for transfers between devices: 7.17 us -> 0.01 us  [fill_cache(): sent = lax.all_to_all(pages, 'seq', split_axis=0, concat_axis=0, tiled=True)]
  transfers between devices with their start and end apart: 33 -> 33, of which waited for: 17 -> 17; matrix products, arithmetic and copies ran while one was open for 1% -> 1% of each run, Pallas kernels for 20% -> 17%
where the time goes in v8:
time: 258 us; the launch traced here: 257 us
  waiting for transfers between devices  114 us (44%)
  Pallas kernels  61.5 us (24%)
  starting transfers between devices  52.4 us (20%)
  local copies, waits for them, and re-layouts  25.9 us (10%)
    ppermute x30, waiting for transfers between devices, swap(): return lax.ppermute(a, axis, [(i, i ^ distance) for i in range(size)])  78.7 us
    ppermute x30, starting transfers between devices, swap(): return lax.ppermute(a, axis, [(i, i ^ distance) for i in range(size)])  36.8 us
    pallas_call x2, Pallas kernels, expert_rows(): pl.pallas_call(functools.partial(rows_kernel, local, len(waits)), out_sha...  31.7 us
    all_to_all x1, waiting for transfers between devices, body(): lax.all_to_all(packed, 'seq', split_axis=0, concat_axis=0, tiled=True)  25.4 us
    unnamed x83, local copies, waits for them, and re-layouts  21 us
    all_to_all x1, waiting for transfers between devices, body(): lax.all_to_all(context.reshape(n_seq, rows_dev, span), 'seq', split_axis=...  9.84 us
    all_to_all x1, starting transfers between devices, body(): lax.all_to_all(packed, 'seq', split_axis=0, concat_axis=0, tiled=True)  7.25 us
    pallas_call x2, Pallas kernels, put_rows(): pl.pallas_call(functools.partial(put_kernel, local, rows_dev, planes, len...  7.08 us
  transfers between devices with their start and end apart: 33, of which 17 were waited for; matrix products, arithmetic and copies ran while one was open for 1% of the time, Pallas kernels for 17%

profile of v8, /device:TPU:0, one launch (start us, length us, event | category | flops | bytes accessed | tf_op | source)
XLA Modules:
  0.0 256.7 jit_solution(15689608639162909261)
XLA Ops:
  0.6 2.3 fusion.3
  3.8 2.4 shard_map.122
  6.2 7.3 %all-to-all-start = ((bf16[8,64,960]{2,1,0:T(8,128)(2,1)}), bf16[8,64,960]{2,1,0:T(8,128)(2,1)S(1)}, u32[]{:S(2)}, u32[]{:S(2)}) async-start(bf16[8,64,960]{2,1,0:T(8,128)(2,1)} %shard_map.122), calls=%async_computation | async-start | bytes 2097152 | tf_op jit(solution)/shard_map/all_to_all | solution.py:515
  13.9 25.4 %all-to-all-done = bf16[8,64,960]{2,1,0:T(8,128)(2,1)S(1)} async-done(((bf16[8,64,960]{2,1,0:T(8,128)(2,1)}), bf16[8,64,960]{2,1,0:T(8,128)(2,1)S(1)}, u32[]{:S(2)}, u32[]{:S(2)}) %all-to-all-start) | async-done | bytes 983072 | tf_op jit(solution)/shard_map/all_to_all | solution.py:515
  39.2 5.6 %shard_map.123 = bf16[512,320]{1,0:T(8,128)(2,1)} custom-call(bf16[512,960]{1,0:T(8,128)(2,1)S(1)} %bitcast.22, s32[1,512]{1,0:T(1,128)S(1)} %copy-done.16, s32[512,1]{1,0:T(8,128)S(1)} %copy.36.seg_col_ref), custom_call_target="tpu_custom_call" | custom-call | flops 335544320 | bytes 1310720 | tf_op jit(solution)/shard_map/pallas_call | solution.py:55
  44.8 3.6 %all-to-all-start.1 = ((bf16[8,64,320]{2,1,0:T(8,128)(2,1)}), bf16[8,64,320]{2,1,0:T(8,128)(2,1)S(1)}, u32[]{:S(2)}, u32[]{:S(2)}) async-start(bf16[8,64,320]{2,1,0:T(8,128)(2,1)} %bitcast.5), calls=%async_computation.1 | async-start | bytes 786432 | tf_op jit(solution)/shard_map/all_to_all | solution.py:518
  50.4 9.8 %all-to-all-done.1.context_ref = bf16[8,64,320]{2,1,0:T(8,128)(2,1)S(1)} async-done(((bf16[8,64,320]{2,1,0:T(8,128)(2,1)}), bf16[8,64,320]{2,1,0:T(8,128)(2,1)S(1)}, u32[]{:S(2)}, u32[]{:S(2)}) %all-to-all-start.1) | async-done | bytes 327712 | tf_op jit(solution)/shard_map/all_to_all | solution.py:518
  61.0 2.1 shard_map.124
  64.6 1.5 collective-permute-start
  66.1 2.0 collective-permute-start.8
  68.2 6.2 %collective-permute-done.3.refs_4_ = bf16[64,2432]{1,0:T(8,128)(2,1)S(1)} collective-permute-done((bf16[64,2432]{1,0:T(8,128)(2,1)}, bf16[64,2432]{1,0:T(8,128)(2,1)S(1)}, u32[]{:S(2)}, u32[]{:S(2)}) %collective-permute-start.3) | collective-permute-done | bytes 311328 | tf_op jit(solution)/shard_map/ppermute | solution.py:407
  74.3 2.5 collective-permute-start.5
  76.9 3.7 %collective-permute-start.4 = (bf16[64,2432]{1,0:T(8,128)(2,1)S(1)}, bf16[64,2432]{1,0:T(8,128)(2,1)S(1)}, u32[]{:S(2)}, u32[]{:S(2)}) collective-permute-start(bf16[64,2432]{1,0:T(8,128)(2,1)S(1)} %collective-permute-done.3.refs_4_), channel_id=1, source_target_pairs={{0,4},{4,0},{8,12},{12,8},{16,20},{20,16},{24,28},{28,24},{1,5},{5... | collective-permute-start | bytes 933896 | tf_op jit(solution)/shard_map/ppermute | solution.py:407
  81.8 4.8 %collective-permute-done.4.refs_5_.rest_3_ = bf16[64,2432]{1,0:T(8,128)(2,1)S(1)} collective-permute-done((bf16[64,2432]{1,0:T(8,128)(2,1)S(1)}, bf16[64,2432]{1,0:T(8,128)(2,1)S(1)}, u32[]{:S(2)}, u32[]{:S(2)}) %collective-permute-start.4) | collective-permute-done | bytes 311328 | tf_op jit(solution)/shard_map/ppermute | solution.py:407
  87.3 1.8 shard_map.127.refs_0_
  89.2 1.8 collective-permute-start.10
  91.0 5.5 %collective-permute-done.12.refs_4_ = bf16[64,2432]{1,0:T(8,128)(2,1)S(1)} collective-permute-done((bf16[64,2432]{1,0:T(8,128)(2,1)}, bf16[64,2432]{1,0:T(8,128)(2,1)S(1)}, u32[]{:S(2)}, u32[]{:S(2)}) %collective-permute-start.12) | collective-permute-done | bytes 311328 | tf_op jit(solution)/shard_map/ppermute | solution.py:407
  97.0 1.5 collective-permute-start.9
  98.5 1.6 collective-permute-start.13
  102.7 4.1 %collective-permute-done.14.refs_6_ = bf16[64,2432]{1,0:T(8,128)(2,1)S(1)} collective-permute-done((bf16[64,2432]{1,0:T(8,128)(2,1)S(1)}, bf16[64,2432]{1,0:T(8,128)(2,1)S(1)}, u32[]{:S(2)}, u32[]{:S(2)}) %collective-permute-start.14) | collective-permute-done | bytes 311328 | tf_op jit(solution)/shard_map/ppermute | solution.py:407
  106.8 1.6 collective-permute-start.15
  109.1 3.5 %collective-permute-done.9.refs_1_ = bf16[64,2432]{1,0:T(8,128)(2,1)S(1)} collective-permute-done((bf16[64,2432]{1,0:T(8,128)(2,1)}, bf16[64,2432]{1,0:T(8,128)(2,1)S(1)}, u32[]{:S(2)}, u32[]{:S(2)}) %collective-permute-start.9) | collective-permute-done | bytes 311328 | tf_op jit(solution)/shard_map/ppermute | solution.py:407
  114.1 2.0 collective-permute-done.11.refs_3_
  121.9 2.4 shard_map.128
  124.4 1.2 copy-done.30
  126.5 1.9 collective-permute-start.6
  128.4 7.0 %collective-permute-done.2.refs_3_ = bf16[64,2432]{1,0:T(8,128)(2,1)S(1)} collective-permute-done((bf16[64,2432]{1,0:T(8,128)(2,1)S(1)}, bf16[64,2432]{1,0:T(8,128)(2,1)S(1)}, u32[]{:S(2)}, u32[]{:S(2)}) %collective-permute-start.2) | collective-permute-done | bytes 311328 | tf_op jit(solution)/shard_map/ppermute | solution.py:407
  137.0 3.2 %shard_map.125 = (bf16[2,192,2304]{2,1,0:T(8,128)(2,1)S(1)}, bf16[2,192,2304]{2,1,0:T(8,128)(2,1)}, bf16[512,128]{1,0:T(8,128)(2,1)S(1)}) custom-call(s32[2]{0:T(128)S(1)} %add_multiply_fusion.bases_ref, bf16[64,2432]{1,0:T(8,128)(2,1)S(1)} %copy-done.17, bf16[64,2432]{1,0:T(8,128)(2,1)S(1)} %copy-done.6, bf16[64,2432]{1,0:T(8,128)(2,1)S(1)} %copy-done.4, ...), custom_call_target="tpu_custom_call" | custom-call | flops 905969664 | bytes 6029312 | tf_op jit(solution)/shard_map/pallas_call | solution.py:287
  142.7 2.3 shard_map.126.rest_1_
  145.0 4.8 %all-to-all-start.2 = ((bf16[8,64,640]{2,1,0:T(8,128)(2,1)}), bf16[8,64,640]{2,1,0:T(8,128)(2,1)}, u32[]{:S(2)}, u32[]{:S(2)}) async-start(bf16[8,64,640]{2,1,0:T(8,128)(2,1)} %shard_map.126.rest_1_), calls=%async_computation.2 | async-start | bytes 1310720 | tf_op jit(solution)/shard_map/all_to_all | solution.py:535
  151.0 1.5 copy-done.31
  152.4 16.3 %shard_map.129 = (bf16[2,192,2304]{2,1,0:T(8,128)(2,1)S(1)}, bf16[2,192,2304]{2,1,0:T(8,128)(2,1)}) custom-call(bf16[2,192,2304]{2,1,0:T(8,128)(2,1)S(1)} %copy-done.31, bf16[2,192,2304]{2,1,0:T(8,128)(2,1)} %collective-permute-done.16.got_ref, bf16[2,720,2304]{2,1,0:T(8,128)(2,1)} %bitcast.29, bf16[2,720,2304]{2,1,0:T(8,128)(2,1)} %bitcast.31, ...), custom_call_target="tpu_custom_call" | custom-call | flops 7644119040 | bytes 26984448 | tf_op jit(solution)/shard_map/pallas_call | solution.py:335
  169.1 2.1 shard_map.130.rest_0_
  172.2 1.5 copy-done.33
  173.7 15.4 %shard_map.131 = (bf16[2,192,2304]{2,1,0:T(8,128)(2,1)S(1)}, bf16[2,192,2304]{2,1,0:T(8,128)(2,1)S(1)}) custom-call(bf16[2,192,2304]{2,1,0:T(8,128)(2,1)S(1)} %copy-done.33, bf16[2,192,2304]{2,1,0:T(8,128)(2,1)} %collective-permute-done.7.got_ref, bf16[2,720,2304]{2,1,0:T(8,128)(2,1)} %bitcast.30, bf16[2,720,2304]{2,1,0:T(8,128)(2,1)} %bitcast.32, ...), custom_call_target="tpu_custom_call" | custom-call | flops 7644119040 | bytes 26984448 | tf_op jit(solution)/shard_map/pallas_call | solution.py:335
  189.4 3.6 %shard_map.132 = (bf16[256,2304]{1,0:T(8,128)(2,1)S(1)}, bf16[128,2304]{1,0:T(8,128)(2,1)S(1)}, bf16[128,2304]{1,0:T(8,128)(2,1)S(1)}) custom-call(s32[2]{0:T(128)S(1)} %add_multiply_fusion.bases_ref, bf16[2,192,2304]{2,1,0:T(8,128)(2,1)S(1)} %get-tuple-element.40.y_own_ref, bf16[2,192,2304]{2,1,0:T(8,128)(2,1)S(1)} %collective-permute-done.18.y_got_ref, ...), custom_call_target="tpu_custom_call" | custom-call | flops 905969664 | bytes 18874368 | tf_op jit(solution)/shard_map/pallas_call | solution.py:390
  193.0 2.1 collective-permute-start.19
  195.6 13.0 %collective-permute-done.19.rest_0_ = bf16[128,2304]{1,0:T(8,128)(2,1)S(1)} collective-permute-done((bf16[128,2304]{1,0:T(8,128)(2,1)S(1)}, bf16[128,2304]{1,0:T(8,128)(2,1)S(1)}, u32[]{:S(2)}, u32[]{:S(2)}) %collective-permute-start.19) | collective-permute-done | bytes 589856 | tf_op jit(solution)/shard_map/ppermute | solution.py:407
  208.6 1.5 collective-permute-done.20.rest_1_
  210.4 3.5 %shard_map.134 = (bf16[256,2304]{1,0:T(8,128)(2,1)S(1)}, bf16[128,2304]{1,0:T(8,128)(2,1)S(1)}, bf16[128,2304]{1,0:T(8,128)(2,1)S(1)}) custom-call(s32[2]{0:T(128)S(1)} %add_multiply_fusion.bases_ref, bf16[2,192,2304]{2,1,0:T(8,128)(2,1)S(1)} %get-tuple-element.37.y_own_ref, bf16[2,192,2304]{2,1,0:T(8,128)(2,1)S(1)} %collective-permute-done.17.y_got_ref, ...), custom_call_target="tpu_custom_call" | custom-call | flops 905969664 | bytes 18874368 | tf_op jit(solution)/shard_map/pallas_call | solution.py:390
  215.1 1.3 collective-permute-start.23
  216.4 1.7 collective-permute-start.24
  218.0 16.8 %collective-permute-done.23.rest_0_ = bf16[64,2304]{1,0:T(8,128)(2,1)S(1)} collective-permute-done((bf16[64,2304]{1,0:T(8,128)(2,1)S(1)}, bf16[64,2304]{1,0:T(8,128)(2,1)S(1)}, u32[]{:S(2)}, u32[]{:S(2)}) %collective-permute-start.23) | collective-permute-done | bytes 294944 | tf_op jit(solution)/shard_map/ppermute | solution.py:407
  234.9 1.5 collective-permute-start.27
  237.3 1.4 collective-permute-start.26
  238.8 3.1 %collective-permute-done.27 = bf16[64,2304]{1,0:T(8,128)(2,1)S(1)} collective-permute-done((bf16[64,2304]{1,0:T(8,128)(2,1)S(1)}, bf16[64,2304]{1,0:T(8,128)(2,1)S(1)}, u32[]{:S(2)}, u32[]{:S(2)}) %collective-permute-start.27) | collective-permute-done | bytes 294944 | tf_op jit(solution)/shard_map/ppermute | solution.py:407
  242.0 2.8 %collective-permute-start.29 = (bf16[64,2304]{1,0:T(8,128)(2,1)S(1)}, bf16[64,2304]{1,0:T(8,128)(2,1)S(1)}, u32[]{:S(2)}, u32[]{:S(2)}) collective-permute-start(bf16[64,2304]{1,0:T(8,128)(2,1)S(1)} %add_convert_fusion.1.rest_2_), channel_id=1, source_target_pairs={{0,16},{4,20},{8,24},{12,28},{16,0},{20,4},{24,8},{28,12},{1,17},{... | collective-permute-start | bytes 884744 | tf_op jit(solution)/shard_map/ppermute | solution.py:407
  245.8 9.5 %collective-permute-done.29 = bf16[64,2304]{1,0:T(8,128)(2,1)S(1)} collective-permute-done((bf16[64,2304]{1,0:T(8,128)(2,1)S(1)}, bf16[64,2304]{1,0:T(8,128)(2,1)S(1)}, u32[]{:S(2)}, u32[]{:S(2)}) %collective-permute-start.29) | collective-permute-done | bytes 294944 | tf_op jit(solution)/shard_map/ppermute | solution.py:407
  (135 shorter events, 32.2 us)
Async XLA Ops:
  3.8 9.6 %copy-start.16 = (s32[1,512]{1,0:T(1,128)S(1)}, s32[1,512]{1,0:T(1,128)}, u32[]{:S(2)}) copy-start(s32[1,512]{1,0:T(1,128)} %seg_row_ref.1) | copy-start | bytes 6148
  3.8 9.8 %copy-start.38 = (s32[1,64,2]{1,2,0:T(2,128)S(1)}, s32[1,64,2]{1,2,0:T(2,128)}, u32[]{:S(2)}) copy-start(s32[1,64,2]{1,2,0:T(2,128)} %param.16) | copy-start | bytes 1540
  6.2 33.0 %all-to-all-start = ((bf16[8,64,960]{2,1,0:T(8,128)(2,1)}), bf16[8,64,960]{2,1,0:T(8,128)(2,1)S(1)}, u32[]{:S(2)}, u32[]{:S(2)}) async-start(bf16[8,64,960]{2,1,0:T(8,128)(2,1)} %shard_map.122), calls=%async_computation | async-start | bytes 2097152 | tf_op jit(solution)/shard_map/all_to_all | solution.py:515
  39.2 9.8 %copy-start = (bf16[8,64,960]{2,1,0:T(8,128)(2,1)}, bf16[8,64,960]{2,1,0:T(8,128)(2,1)S(1)}, u32[]{:S(2)}) copy-start(bf16[8,64,960]{2,1,0:T(8,128)(2,1)S(1)} %all-to-all-done) | copy-start | bytes 2949124
  39.2 9.9 %copy-start.39 = (f32[1,64,2]{1,2,0:T(2,128)S(1)}, f32[1,64,2]{1,2,0:T(2,128)}, u32[]{:S(2)}) copy-start(f32[1,64,2]{1,2,0:T(2,128)} %param.17) | copy-start | bytes 1540
  39.2 10.0 %copy-start.37 = (bf16[2304]{0:T(1024)(128)(2,1)S(1)}, bf16[2304]{0:T(1024)(128)(2,1)}, u32[]{:S(2)}) copy-start(bf16[2304]{0:T(1024)(128)(2,1)} %param.14) | copy-start | bytes 13828
  44.8 15.4 %all-to-all-start.1 = ((bf16[8,64,320]{2,1,0:T(8,128)(2,1)}), bf16[8,64,320]{2,1,0:T(8,128)(2,1)S(1)}, u32[]{:S(2)}, u32[]{:S(2)}) async-start(bf16[8,64,320]{2,1,0:T(8,128)(2,1)} %bitcast.5), calls=%async_computation.1 | async-start | bytes 786432 | tf_op jit(solution)/shard_map/all_to_all | solution.py:518
  63.2 11.2 %collective-permute-start.3 = (bf16[64,2432]{1,0:T(8,128)(2,1)}, bf16[64,2432]{1,0:T(8,128)(2,1)S(1)}, u32[]{:S(2)}, u32[]{:S(2)}) collective-permute-start(bf16[64,2432]{1,0:T(8,128)(2,1)} %get-tuple-element.31.refs_0_), channel_id=1, source_target_pairs={{0,8},{4,12},{8,0},{12,4},{16,24},{20,28},{24,16},{28,20},{1,9},{5... | collective-permute-start | bytes 933896 | tf_op jit(solution)/shard_map/ppermute | solution.py:407
  64.1 17.2 %collective-permute-start.1 = (bf16[64,2432]{1,0:T(8,128)(2,1)}, bf16[64,2432]{1,0:T(8,128)(2,1)S(1)}, u32[]{:S(2)}, u32[]{:S(2)}) collective-permute-start(bf16[64,2432]{1,0:T(8,128)(2,1)} %get-tuple-element.31.refs_0_), channel_id=1, source_target_pairs={{0,4},{4,0},{8,12},{12,8},{16,20},{20,16},{24,28},{28,24},{1,5},{5... | collective-permute-start | bytes 933896 | tf_op jit(solution)/shard_map/ppermute | solution.py:407
  64.6 16.7 %collective-permute-start = (bf16[64,2432]{1,0:T(8,128)(2,1)}, bf16[64,2432]{1,0:T(8,128)(2,1)S(1)}, u32[]{:S(2)}, u32[]{:S(2)}) collective-permute-start(bf16[64,2432]{1,0:T(8,128)(2,1)} %get-tuple-element.31.refs_0_), channel_id=1, source_target_pairs={{0,2},{1,3},{2,0},{3,1},{4,6},{5,7},{6,4},{7,5},{8,10},{9,11},{10,... | collective-permute-start | bytes 933896 | tf_op jit(solution)/shard_map/ppermute | solution.py:407
  66.1 15.6 %collective-permute-start.8 = (bf16[64,2432]{1,0:T(8,128)(2,1)}, bf16[64,2432]{1,0:T(8,128)(2,1)S(1)}, u32[]{:S(2)}, u32[]{:S(2)}) collective-permute-start(bf16[64,2432]{1,0:T(8,128)(2,1)} %get-tuple-element.31.refs_0_), channel_id=1, source_target_pairs={{0,16},{4,20},{8,24},{12,28},{16,0},{20,4},{24,8},{28,12},{1,17},{... | collective-permute-start | bytes 933896 | tf_op jit(solution)/shard_map/ppermute | solution.py:407
  74.3 7.4 %collective-permute-start.5 = (bf16[64,2432]{1,0:T(8,128)(2,1)S(1)}, bf16[64,2432]{1,0:T(8,128)(2,1)S(1)}, u32[]{:S(2)}, u32[]{:S(2)}) collective-permute-start(bf16[64,2432]{1,0:T(8,128)(2,1)S(1)} %collective-permute-done.3.refs_4_), channel_id=1, source_target_pairs={{0,2},{1,3},{2,0},{3,1},{4,6},{5,7},{6,4},{7,5},{8,10},{9,11},{10,... | collective-permute-start | bytes 933896 | tf_op jit(solution)/shard_map/ppermute | solution.py:407
  76.9 9.7 %collective-permute-start.4 = (bf16[64,2432]{1,0:T(8,128)(2,1)S(1)}, bf16[64,2432]{1,0:T(8,128)(2,1)S(1)}, u32[]{:S(2)}, u32[]{:S(2)}) collective-permute-start(bf16[64,2432]{1,0:T(8,128)(2,1)S(1)} %collective-permute-done.3.refs_4_), channel_id=1, source_target_pairs={{0,4},{4,0},{8,12},{12,8},{16,20},{20,16},{24,28},{28,24},{1,5},{5... | collective-permute-start | bytes 933896 | tf_op jit(solution)/shard_map/ppermute | solution.py:407
  87.3 48.7 %copy-start.17 = (bf16[64,2432]{1,0:T(8,128)(2,1)S(1)}, bf16[64,2432]{1,0:T(8,128)(2,1)}, u32[]{:S(2)}) copy-start(bf16[64,2432]{1,0:T(8,128)(2,1)} %get-tuple-element.31.refs_0_) | copy-start | bytes 933892
  89.1 36.5 %copy-start.4 = (bf16[64,2432]{1,0:T(8,128)(2,1)S(1)}, bf16[64,2432]{1,0:T(8,128)(2,1)}, u32[]{:S(2)}) copy-start(bf16[64,2432]{1,0:T(8,128)(2,1)} %copy-done.3) | copy-start | bytes 933892
  89.1 37.4 %copy-start.8 = (bf16[64,2432]{1,0:T(8,128)(2,1)S(1)}, bf16[64,2432]{1,0:T(8,128)(2,1)}, u32[]{:S(2)}) copy-start(bf16[64,2432]{1,0:T(8,128)(2,1)} %copy-done.7) | copy-start | bytes 933892
  89.1 47.0 %copy-start.6 = (bf16[64,2432]{1,0:T(8,128)(2,1)S(1)}, bf16[64,2432]{1,0:T(8,128)(2,1)}, u32[]{:S(2)}) copy-start(bf16[64,2432]{1,0:T(8,128)(2,1)} %copy-done.5) | copy-start | bytes 933892
  89.1 47.0 %copy-start.10 = (bf16[64,2432]{1,0:T(8,128)(2,1)S(1)}, bf16[64,2432]{1,0:T(8,128)(2,1)}, u32[]{:S(2)}) copy-start(bf16[64,2432]{1,0:T(8,128)(2,1)} %copy-done.9) | copy-start | bytes 933892
  89.1 7.4 %collective-permute-start.12 = (bf16[64,2432]{1,0:T(8,128)(2,1)}, bf16[64,2432]{1,0:T(8,128)(2,1)S(1)}, u32[]{:S(2)}, u32[]{:S(2)}) collective-permute-start(bf16[64,2432]{1,0:T(8,128)(2,1)} %shard_map.127.refs_0_), channel_id=1, source_target_pairs={{0,8},{4,12},{8,0},{12,4},{16,24},{20,28},{24,16},{28,20},{1,9},{5... | collective-permute-start | bytes 933896 | tf_op jit(solution)/shard_map/ppermute | solution.py:407
  89.2 11.6 %collective-permute-start.10 = (bf16[64,2432]{1,0:T(8,128)(2,1)}, bf16[64,2432]{1,0:T(8,128)(2,1)S(1)}, u32[]{:S(2)}, u32[]{:S(2)}) collective-permute-start(bf16[64,2432]{1,0:T(8,128)(2,1)} %shard_map.127.refs_0_), channel_id=1, source_target_pairs={{0,4},{4,0},{8,12},{12,8},{16,20},{20,16},{24,28},{28,24},{1,5},{5... | collective-permute-start | bytes 933896 | tf_op jit(solution)/shard_map/ppermute | solution.py:407
  96.5 10.3 %collective-permute-start.14 = (bf16[64,2432]{1,0:T(8,128)(2,1)S(1)}, bf16[64,2432]{1,0:T(8,128)(2,1)S(1)}, u32[]{:S(2)}, u32[]{:S(2)}) collective-permute-start(bf16[64,2432]{1,0:T(8,128)(2,1)S(1)} %collective-permute-done.12.refs_4_), channel_id=1, source_target_pairs={{0,2},{1,3},{2,0},{3,1},{4,6},{5,7},{6,4},{7,5},{8,10},{9,11},{10,... | collective-permute-start | bytes 933896 | tf_op jit(solution)/shard_map/ppermute | solution.py:407
  97.0 15.6 %collective-permute-start.9 = (bf16[64,2432]{1,0:T(8,128)(2,1)}, bf16[64,2432]{1,0:T(8,128)(2,1)S(1)}, u32[]{:S(2)}, u32[]{:S(2)}) collective-permute-start(bf16[64,2432]{1,0:T(8,128)(2,1)} %shard_map.127.refs_0_), channel_id=1, source_target_pairs={{0,2},{1,3},{2,0},{3,1},{4,6},{5,7},{6,4},{7,5},{8,10},{9,11},{10,... | collective-permute-start | bytes 933896 | tf_op jit(solution)/shard_map/ppermute | solution.py:407
  98.5 14.9 %collective-permute-start.13 = (bf16[64,2432]{1,0:T(8,128)(2,1)S(1)}, bf16[64,2432]{1,0:T(8,128)(2,1)S(1)}, u32[]{:S(2)}, u32[]{:S(2)}) collective-permute-start(bf16[64,2432]{1,0:T(8,128)(2,1)S(1)} %collective-permute-done.12.refs_4_), channel_id=1, source_target_pairs={{0,4},{4,0},{8,12},{12,8},{16,20},{20,16},{24,28},{28,24},{1,5},{5... | collective-permute-start | bytes 933896 | tf_op jit(solution)/shard_map/ppermute | solution.py:407
  100.8 15.3 %collective-permute-start.11 = (bf16[64,2432]{1,0:T(8,128)(2,1)S(1)}, bf16[64,2432]{1,0:T(8,128)(2,1)}, u32[]{:S(2)}, u32[]{:S(2)}) collective-permute-start(bf16[64,2432]{1,0:T(8,128)(2,1)S(1)} %collective-permute-done.10.refs_2_), channel_id=1, source_target_pairs={{0,2},{1,3},{2,0},{3,1},{4,6},{5,7},{6,4},{7,5},{8,10},{9,11},{10,... | collective-permute-start | bytes 933896 | tf_op jit(solution)/shard_map/ppermute | solution.py:407
  106.8 9.3 %collective-permute-start.15 = (bf16[64,2432]{1,0:T(8,128)(2,1)S(1)}, bf16[64,2432]{1,0:T(8,128)(2,1)}, u32[]{:S(2)}, u32[]{:S(2)}) collective-permute-start(bf16[64,2432]{1,0:T(8,128)(2,1)S(1)} %collective-permute-done.14.refs_6_), channel_id=1, source_target_pairs={{0,4},{4,0},{8,12},{12,8},{16,20},{20,16},{24,28},{28,24},{1,5},{5... | collective-permute-start | bytes 933896 | tf_op jit(solution)/shard_map/ppermute | solution.py:407
  125.6 14.6 %copy-start.14 = (bf16[512,128]{1,0:T(8,128)(2,1)}, bf16[512,128]{1,0:T(8,128)(2,1)S(1)}, u32[]{:S(2)}) copy-start(bf16[512,128]{1,0:T(8,128)(2,1)S(1)} %get-tuple-element.41.facts_ref) | copy-start | bytes 393220
  125.6 16.5 %copy-start.40 = (s32[1,32]{1,0:T(1,128)S(1)}, s32[1,32]{1,0:T(1,128)}, u32[]{:S(2)}) copy-start(s32[1,32]{1,0:T(1,128)} %param.18) | copy-start | bytes 388
  125.6 24.3 %collective-permute-start.16 = (bf16[2,192,2304]{2,1,0:T(8,128)(2,1)S(1)}, bf16[2,192,2304]{2,1,0:T(8,128)(2,1)}, u32[]{:S(2)}, u32[]{:S(2)}) collective-permute-start(bf16[2,192,2304]{2,1,0:T(8,128)(2,1)S(1)} %get-tuple-element.35), channel_id=1, source_target_pairs={{0,1},{1,0},{2,3},{3,2},{4,5},{5,4},{6,7},{7,6},{8,9},{9,8},{10,11... | collective-permute-start | bytes 5308424 | tf_op jit(solution)/shard_map/ppermute | solution.py:407
  125.6 9.8 %collective-permute-start.2 = (bf16[64,2432]{1,0:T(8,128)(2,1)S(1)}, bf16[64,2432]{1,0:T(8,128)(2,1)S(1)}, u32[]{:S(2)}, u32[]{:S(2)}) collective-permute-start(bf16[64,2432]{1,0:T(8,128)(2,1)S(1)} %copy-done.4), channel_id=1, source_target_pairs={{0,2},{1,3},{2,0},{3,1},{4,6},{5,7},{6,4},{7,5},{8,10},{9,11},{10,... | collective-permute-start | bytes 933896 | tf_op jit(solution)/shard_map/ppermute | solution.py:407
  126.5 9.5 %collective-permute-start.6 = (bf16[64,2432]{1,0:T(8,128)(2,1)S(1)}, bf16[64,2432]{1,0:T(8,128)(2,1)S(1)}, u32[]{:S(2)}, u32[]{:S(2)}) collective-permute-start(bf16[64,2432]{1,0:T(8,128)(2,1)S(1)} %copy-done.8), channel_id=1, source_target_pairs={{0,4},{4,0},{8,12},{12,8},{16,20},{20,16},{24,28},{28,24},{1,5},{5... | collective-permute-start | bytes 933896 | tf_op jit(solution)/shard_map/ppermute | solution.py:407
  142.1 29.1 %collective-permute-start.7 = (bf16[2,192,2304]{2,1,0:T(8,128)(2,1)}, bf16[2,192,2304]{2,1,0:T(8,128)(2,1)}, u32[]{:S(2)}, u32[]{:S(2)}) collective-permute-start(bf16[2,192,2304]{2,1,0:T(8,128)(2,1)} %get-tuple-element.33.late_ref.rest_0_), channel_id=1, source_target_pairs={{0,1},{1,0},{2,3},{3,2},{4,5},{5,4},{6,7},{7,6},{8,9},{9,8},{10,11... | collective-permute-start | bytes 5308424 | tf_op jit(solution)/shard_map/ppermute | solution.py:407
  145.0 24.1 %all-to-all-start.2 = ((bf16[8,64,640]{2,1,0:T(8,128)(2,1)}), bf16[8,64,640]{2,1,0:T(8,128)(2,1)}, u32[]{:S(2)}, u32[]{:S(2)}) async-start(bf16[8,64,640]{2,1,0:T(8,128)(2,1)} %shard_map.126.rest_1_), calls=%async_computation.2 | async-start | bytes 1310720 | tf_op jit(solution)/shard_map/all_to_all | solution.py:535
  168.8 20.7 %collective-permute-start.18 = (bf16[2,192,2304]{2,1,0:T(8,128)(2,1)}, bf16[2,192,2304]{2,1,0:T(8,128)(2,1)S(1)}, u32[]{:S(2)}, u32[]{:S(2)}) collective-permute-start(bf16[2,192,2304]{2,1,0:T(8,128)(2,1)} %get-tuple-element.36.behind_ref.rest_1_), channel_id=1, source_target_pairs={{0,1},{1,0},{2,3},{3,2},{4,5},{5,4},{6,7},{7,6},{8,9},{9,8},{10,11... | collective-permute-start | bytes 5308424 | tf_op jit(solution)/shard_map/ppermute | solution.py:407
  173.7 15.7 %copy-start.15 = (bf16[512,128]{1,0:T(8,128)(2,1)S(1)}, bf16[512,128]{1,0:T(8,128)(2,1)}, u32[]{:S(2)}) copy-start(bf16[512,128]{1,0:T(8,128)(2,1)} %copy-done.14) | copy-start | bytes 393220
  189.1 21.3 %collective-permute-start.17 = (bf16[2,192,2304]{2,1,0:T(8,128)(2,1)S(1)}, bf16[2,192,2304]{2,1,0:T(8,128)(2,1)S(1)}, u32[]{:S(2)}, u32[]{:S(2)}) collective-permute-start(bf16[2,192,2304]{2,1,0:T(8,128)(2,1)S(1)} %get-tuple-element.38.rest_0_), channel_id=1, source_target_pairs={{0,1},{1,0},{2,3},{3,2},{4,5},{5,4},{6,7},{7,6},{8,9},{9,8},{10,11... | collective-permute-start | bytes 5308424 | tf_op jit(solution)/shard_map/ppermute | solution.py:407
  193.0 17.4 %copy-start.13 = (bf16[512,128]{1,0:T(8,128)(2,1)S(1)}, bf16[512,128]{1,0:T(8,128)(2,1)}, u32[]{:S(2)}) copy-start(bf16[512,128]{1,0:T(8,128)(2,1)} %copy-done.12) | copy-start | bytes 393220
  193.0 15.6 %collective-permute-start.19 = (bf16[128,2304]{1,0:T(8,128)(2,1)S(1)}, bf16[128,2304]{1,0:T(8,128)(2,1)S(1)}, u32[]{:S(2)}, u32[]{:S(2)}) collective-permute-start(bf16[128,2304]{1,0:T(8,128)(2,1)S(1)} %get-tuple-element.43), channel_id=1, source_target_pairs={{0,4},{4,0},{8,12},{12,8},{16,20},{20,16},{24,28},{28,24},{1,5},{5... | collective-permute-start | bytes 1769480 | tf_op jit(solution)/shard_map/ppermute | solution.py:407
  195.1 15.0 %collective-permute-start.20 = (bf16[128,2304]{1,0:T(8,128)(2,1)S(1)}, bf16[128,2304]{1,0:T(8,128)(2,1)S(1)}, u32[]{:S(2)}, u32[]{:S(2)}) collective-permute-start(bf16[128,2304]{1,0:T(8,128)(2,1)S(1)} %get-tuple-element.44), channel_id=1, source_target_pairs={{0,2},{1,3},{2,0},{3,1},{4,6},{5,7},{6,4},{7,5},{8,10},{9,11},{10,... | collective-permute-start | bytes 1769480 | tf_op jit(solution)/shard_map/ppermute | solution.py:407
  213.9 22.5 %collective-permute-start.21 = (bf16[128,2304]{1,0:T(8,128)(2,1)S(1)}, bf16[128,2304]{1,0:T(8,128)(2,1)S(1)}, u32[]{:S(2)}, u32[]{:S(2)}) collective-permute-start(bf16[128,2304]{1,0:T(8,128)(2,1)S(1)} %get-tuple-element.47), channel_id=1, source_target_pairs={{0,4},{4,0},{8,12},{12,8},{16,20},{20,16},{24,28},{28,24},{1,5},{5... | collective-permute-start | bytes 1769480 | tf_op jit(solution)/shard_map/ppermute | solution.py:407
  214.3 22.1 %collective-permute-start.22 = (bf16[128,2304]{1,0:T(8,128)(2,1)S(1)}, bf16[128,2304]{1,0:T(8,128)(2,1)S(1)}, u32[]{:S(2)}, u32[]{:S(2)}) collective-permute-start(bf16[128,2304]{1,0:T(8,128)(2,1)S(1)} %get-tuple-element.48), channel_id=1, source_target_pairs={{0,2},{1,3},{2,0},{3,1},{4,6},{5,7},{6,4},{7,5},{8,10},{9,11},{10,... | collective-permute-start | bytes 1769480 | tf_op jit(solution)/shard_map/ppermute | solution.py:407
  215.1 19.7 %collective-permute-start.23 = (bf16[64,2304]{1,0:T(8,128)(2,1)S(1)}, bf16[64,2304]{1,0:T(8,128)(2,1)S(1)}, u32[]{:S(2)}, u32[]{:S(2)}) collective-permute-start(bf16[64,2304]{1,0:T(8,128)(2,1)S(1)} %get-tuple-element.45.rest_0_), channel_id=1, source_target_pairs={{0,2},{1,3},{2,0},{3,1},{4,6},{5,7},{6,4},{7,5},{8,10},{9,11},{10,... | collective-permute-start | bytes 884744 | tf_op jit(solution)/shard_map/ppermute | solution.py:407
  216.4 18.4 %collective-permute-start.24 = (bf16[64,2304]{1,0:T(8,128)(2,1)S(1)}, bf16[64,2304]{1,0:T(8,128)(2,1)S(1)}, u32[]{:S(2)}, u32[]{:S(2)}) collective-permute-start(bf16[64,2304]{1,0:T(8,128)(2,1)S(1)} %get-tuple-element.50), channel_id=1, source_target_pairs={{0,4},{4,0},{8,12},{12,8},{16,20},{20,16},{24,28},{28,24},{1,5},{5... | collective-permute-start | bytes 884744 | tf_op jit(solution)/shard_map/ppermute | solution.py:407
  234.9 7.0 %collective-permute-start.27 = (bf16[64,2304]{1,0:T(8,128)(2,1)S(1)}, bf16[64,2304]{1,0:T(8,128)(2,1)S(1)}, u32[]{:S(2)}, u32[]{:S(2)}) collective-permute-start(bf16[64,2304]{1,0:T(8,128)(2,1)S(1)} %get-tuple-element.51.rest_2_), channel_id=1, source_target_pairs={{0,8},{4,12},{8,0},{12,4},{16,24},{20,28},{24,16},{28,20},{1,9},{5... | collective-permute-start | bytes 884744 | tf_op jit(solution)/shard_map/ppermute | solution.py:407
  236.7 19.2 %copy-start.35 = (f32[64,2304]{1,0:T(8,128)S(1)}, f32[64,2304]{1,0:T(8,128)}, u32[]{:S(2)}) copy-start(f32[64,2304]{1,0:T(8,128)} %get-tuple-element.30) | copy-start | bytes 1769476
  236.7 8.1 %collective-permute-start.25 = (bf16[64,2304]{1,0:T(8,128)(2,1)S(1)}, bf16[64,2304]{1,0:T(8,128)(2,1)S(1)}, u32[]{:S(2)}, u32[]{:S(2)}) collective-permute-start(bf16[64,2304]{1,0:T(8,128)(2,1)S(1)} %get-tuple-element.53), channel_id=1, source_target_pairs={{0,2},{1,3},{2,0},{3,1},{4,6},{5,7},{6,4},{7,5},{8,10},{9,11},{10,... | collective-permute-start | bytes 884744 | tf_op jit(solution)/shard_map/ppermute | solution.py:407
  237.3 7.5 %collective-permute-start.26 = (bf16[64,2304]{1,0:T(8,128)(2,1)S(1)}, bf16[64,2304]{1,0:T(8,128)(2,1)S(1)}, u32[]{:S(2)}, u32[]{:S(2)}) collective-permute-start(bf16[64,2304]{1,0:T(8,128)(2,1)S(1)} %get-tuple-element.54), channel_id=1, source_target_pairs={{0,4},{4,0},{8,12},{12,8},{16,20},{20,16},{24,28},{28,24},{1,5},{5... | collective-permute-start | bytes 884744 | tf_op jit(solution)/shard_map/ppermute | solution.py:407
  242.0 13.4 %collective-permute-start.29 = (bf16[64,2304]{1,0:T(8,128)(2,1)S(1)}, bf16[64,2304]{1,0:T(8,128)(2,1)S(1)}, u32[]{:S(2)}, u32[]{:S(2)}) collective-permute-start(bf16[64,2304]{1,0:T(8,128)(2,1)S(1)} %add_convert_fusion.1.rest_2_), channel_id=1, source_target_pairs={{0,16},{4,20},{8,24},{12,28},{16,0},{20,4},{24,8},{28,12},{1,17},{... | collective-permute-start | bytes 884744 | tf_op jit(solution)/shard_map/ppermute | solution.py:407
  244.9 11.0 %collective-permute-start.28 = (bf16[64,2304]{1,0:T(8,128)(2,1)S(1)}, bf16[64,2304]{1,0:T(8,128)(2,1)S(1)}, u32[]{:S(2)}, u32[]{:S(2)}) collective-permute-start(bf16[64,2304]{1,0:T(8,128)(2,1)S(1)} %get-tuple-element.57), channel_id=1, source_target_pairs={{0,8},{4,12},{8,0},{12,4},{16,24},{20,28},{24,16},{28,20},{1,9},{5... | collective-permute-start | bytes 884744 | tf_op jit(solution)/shard_map/ppermute | solution.py:407
  (26 other events, 40.9 us)

commit v9 on v8

--- a/solution.py
+++ b/solution.py
@@ -13,6 +13,7 @@
 EXPERTS = 8
 PAGE = 16
 CAP = 24
+MIB = 1024 * 1024
 CHUNK_BLOCKS = 8
 
 
@@ -55,7 +56,7 @@
     return pl.pallas_call(
         functools.partial(attention_kernel, heads, 128),
         out_shape=jax.ShapeDtypeStruct((total, span), jnp.bfloat16),
-        compiler_params=pltpu.CompilerParams(vmem_limit_bytes=40 * 1024 * 1024),
+        compiler_params=pltpu.CompilerParams(vmem_limit_bytes=24 * MIB),
         cost_estimate=pl.CostEstimate(
             flops=4 * total * total * span, bytes_accessed=8 * total * span, transcendentals=total * total * heads
         ),
@@ -131,7 +132,7 @@
         ],
         out_specs=pl.BlockSpec((tokens, width), lambda e, c: (jnp.where(e == last, c, 0), 0)),
         scratch_shapes=[pltpu.VMEM((max(last, 1), chunks if last else 1, rows, width), jnp.bfloat16)],
-        compiler_params=pltpu.CompilerParams(vmem_limit_bytes=58 * 1024 * 1024),
+        compiler_params=pltpu.CompilerParams(vmem_limit_bytes=58 * MIB),
         cost_estimate=pl.CostEstimate(
             flops=6 * local * chunks * rows * width * hidden,
             bytes_accessed=6 * local * width * hidden + 6 * chunks * tokens * width,
@@ -152,6 +153,7 @@
     return pl.pallas_call(
         functools.partial(pack_kernel, firsts, span),
         out_shape=jax.ShapeDtypeStruct((n_seq, rows_dev, 3 * span), jnp.bfloat16),
+        compiler_params=pltpu.CompilerParams(vmem_limit_bytes=12 * MIB),
         cost_estimate=pl.CostEstimate(flops=0, bytes_accessed=12 * n_seq * rows_dev * span, transcendentals=0),
     )(query, keys, values)
 
@@ -183,6 +185,7 @@
             jax.ShapeDtypeStruct((rows_dev, width), jnp.float32),
             jax.ShapeDtypeStruct((rows_dev, width + facts.shape[1]), jnp.bfloat16),
         ),
+        compiler_params=pltpu.CompilerParams(vmem_limit_bytes=12 * MIB),
         cost_estimate=pl.CostEstimate(
             flops=10 * rows_dev * width, bytes_accessed=10 * rows_dev * width, transcendentals=rows_dev
         ),
@@ -204,6 +207,7 @@
         functools.partial(pick_pages_kernel, rows // PAGE, span),
         out_shape=jax.ShapeDtypeStruct((n_seq, rows, 2 * span), jnp.bfloat16),
         in_specs=[pl.BlockSpec(memory_space=pltpu.SMEM), vmem, pl.BlockSpec(memory_space=pl.ANY)],
+        compiler_params=pltpu.CompilerParams(vmem_limit_bytes=8 * MIB),
         cost_estimate=pl.CostEstimate(flops=0, bytes_accessed=10 * packed.shape[0] * span, transcendentals=0),
     )(order, packed, late)
 
@@ -225,6 +229,7 @@
         functools.partial(join_pages_kernel, share, offsets, span),
         out_shape=jax.ShapeDtypeStruct((rows, 2 * share * n_seq), jnp.bfloat16),
         in_specs=[pl.BlockSpec(memory_space=pltpu.VMEM), pl.BlockSpec(memory_space=pl.ANY)],
+        compiler_params=pltpu.CompilerParams(vmem_limit_bytes=12 * MIB),
         cost_estimate=pl.CostEstimate(flops=0, bytes_accessed=8 * rows * n_seq * span, transcendentals=0),
     )(pages, behind)
 
@@ -237,16 +242,20 @@
     return place
 
 
-def hold_kernel(a_ref, *rest):
-    rest[-1][...] = a_ref[...]
+def hold_kernel(*refs):
+    del refs
 
 
 def hold(a, waits):
+    anywhere = pl.BlockSpec(memory_space=pl.ANY)
     return pl.pallas_call(
         hold_kernel,
         out_shape=jax.ShapeDtypeStruct(a.shape, a.dtype),
-        in_specs=[pl.BlockSpec(memory_space=pltpu.VMEM)] + [pl.BlockSpec(memory_space=pl.ANY)] * len(waits),
-        cost_estimate=pl.CostEstimate(flops=0, bytes_accessed=4 * a.size, transcendentals=0),
+        in_specs=[anywhere] * (1 + len(waits)),
+        out_specs=anywhere,
+        input_output_aliases={0: 0},
+        compiler_params=pltpu.CompilerParams(vmem_limit_bytes=MIB),
+        cost_estimate=pl.CostEstimate(flops=0, bytes_accessed=0, transcendentals=0),
     )(a, *waits)
 
 
@@ -291,7 +300,7 @@
         + [vmem] * len(pieces)
         + [pl.BlockSpec(memory_space=pl.ANY)] * len(waits),
         out_specs=(vmem, vmem, vmem),
-        compiler_params=pltpu.CompilerParams(vmem_limit_bytes=28 * 1024 * 1024),
+        compiler_params=pltpu.CompilerParams(vmem_limit_bytes=20 * MIB),
         cost_estimate=pl.CostEstimate(
             flops=16 * local * CAP * rows_dev * len(pieces) * width,
             bytes_accessed=2 * len(pieces) * rows_dev * wide + 4 * local * rows * width,
@@ -338,7 +347,7 @@
         in_specs=[vmem, vmem] + [pl.BlockSpec(memory_space=pl.ANY)] * (3 + len(waits)),
         out_specs=(vmem, vmem),
         scratch_shapes=[weights, weights, weights, pltpu.SemaphoreType.DMA((3 * local,))],
-        compiler_params=pltpu.CompilerParams(vmem_limit_bytes=44 * 1024 * 1024),
+        compiler_params=pltpu.CompilerParams(vmem_limit_bytes=36 * MIB),
         cost_estimate=pl.CostEstimate(
             flops=6 * local * rows * width * hidden,
             bytes_accessed=6 * local * width * hidden + 4 * local * rows * width,
@@ -393,7 +402,7 @@
         in_specs=[pl.BlockSpec(memory_space=pltpu.SMEM), vmem, vmem, vmem]
         + [pl.BlockSpec(memory_space=pl.ANY)] * len(waits),
         out_specs=(vmem,) * (1 + planes),
-        compiler_params=pltpu.CompilerParams(vmem_limit_bytes=28 * 1024 * 1024),
+        compiler_params=pltpu.CompilerParams(vmem_limit_bytes=20 * MIB),
         cost_estimate=pl.CostEstimate(
             flops=16 * local * CAP * tokens * width,
             bytes_accessed=8 * local * tokens * width,
@@ -432,7 +441,7 @@
         out_shape=(shape(groups * part),) + (shape(part),) * groups,
         in_specs=[vmem] * (1 + len(gots)) + [pl.BlockSpec(memory_space=pl.ANY)] * len(waits),
         out_specs=(vmem,) * (1 + groups),
-        compiler_params=pltpu.CompilerParams(vmem_limit_bytes=24 * 1024 * 1024),
+        compiler_params=pltpu.CompilerParams(vmem_limit_bytes=10 * MIB),
         cost_estimate=pl.CostEstimate(flops=rows * width, bytes_accessed=6 * rows * width, transcendentals=0),
     )(keep, *gots, *waits)
     return out[0], out[1:]
@@ -451,8 +460,9 @@
     over = {"x": x, "y": y}
     single = [[over[way](starts[k]) for way in ways[k]] for k in range(2)]
     starts[2] = hold(starts[2], single[0] + single[1])
-    starts.append(z(starts[2], 1))
-    single += [[over[way](starts[k]) for way in ways[k]] for k in range(2, 4)]
+    single.append([over[way](starts[2]) for way in ways[2]])
+    starts.append(hold(z(starts[2], 1), single[2]))
+    single.append([over[way](starts[3]) for way in ways[3]])
 
     def gather(k):
         near = []
@@ -475,7 +485,9 @@
     keep_a, (fx_a, fy_a) = put_rows(own_a, got_a, facts_a, bases, piece.shape[0], [sib_b])
     keep_a, (gy_a, gx_a) = fold(keep_a, [x(fx_a), y(fy_a)], 2)
     keep_b, (fx_b, fy_b) = put_rows(own_b, got_b, facts_b, bases, piece.shape[0], [gy_a])
-    keep_a, (z_a,) = fold(keep_a, [y(gy_a), x(gx_a)], 1)
+    gy_a, gx_a = y(gy_a), x(gx_a)
+    fx_b, fy_b = hold(fx_b, [gy_a, gx_a]), hold(fy_b, [gy_a, gx_a])
+    keep_a, (z_a,) = fold(keep_a, [gy_a, gx_a], 1)
     keep_b, (gy_b, gx_b) = fold(keep_b, [x(fx_b), y(fy_b)], 2, [z_a])
     over_z = (keep_a.astype(jnp.float32) + z(z_a, 1).astype(jnp.float32)).astype(jnp.bfloat16)
     keep_b, (z_b,) = fold(keep_b, [y(gy_b), x(gx_b)], 1, [over_z])

time: 258 us -> 240 us (0.930)
  local copies, waits for them, and re-layouts: 25.9 us -> 17.2 us
  Pallas kernels: 61.5 us -> 55.4 us
  starting transfers between devices: 52.4 us -> 46.5 us
  waiting for transfers between devices: 114 us -> 118 us
    unnamed x83 -> x41, local copies, waits for them, and re-layouts: 21 us -> 14.2 us
    ppermute x30, starting transfers between devices: 36.8 us -> 31.9 us  [swap(): return lax.ppermute(a, axis, [(i, i ^ distance) for i in range(size)])]
    ppermute x30, waiting for transfers between devices: 78.7 us -> 81.7 us  [swap(): return lax.ppermute(a, axis, [(i, i ^ distance) for i in range(size)])]
  transfers between devices with their start and end apart: 33 -> 33, of which waited for: 17 -> 24; matrix products, arithmetic and copies ran while one was open for 1% -> 1% of each run, Pallas kernels for 17% -> 18%
where the time goes in v9:
time: 240 us
  waiting for transfers between devices  118 us (49%)
  Pallas kernels  55.4 us (23%)
  starting transfers between devices  46.5 us (19%)
  local copies, waits for them, and re-layouts  17.2 us (7%)
    ppermute x30, waiting for transfers between devices, swap(): return lax.ppermute(a, axis, [(i, i ^ distance) for i in range(size)])  81.7 us
    ppermute x30, starting transfers between devices, swap(): return lax.ppermute(a, axis, [(i, i ^ distance) for i in range(size)])  31.9 us
    pallas_call x2, Pallas kernels, expert_rows(): pl.pallas_call(functools.partial(rows_kernel, local, len(waits)), out_sha...  29.6 us
    all_to_all x1, waiting for transfers between devices, body(): lax.all_to_all(packed, 'seq', split_axis=0, concat_axis=0, tiled=True)  25.4 us
    unnamed x41, local copies, waits for them, and re-layouts  14.2 us
    all_to_all x1, waiting for transfers between devices, body(): lax.all_to_all(context.reshape(n_seq, rows_dev, span), 'seq', split_axis=...  11 us
    pallas_call x2, Pallas kernels, put_rows(): pl.pallas_call(functools.partial(put_kernel, local, rows_dev, planes, len...  8.01 us
    pallas_call x2, Pallas kernels, select_rows(): pl.pallas_call(functools.partial(select_kernel, local, rows_dev, len(piec...  7.26 us
  transfers between devices with their start and end apart: 33, of which 24 were waited for; matrix products, arithmetic and copies ran while one was open for 1% of the time, Pallas kernels for 18%

profile of v9, /device:TPU:0, one launch (start us, length us, event | category | flops | bytes accessed | tf_op | source)
XLA Modules:
  0.0 239.6 jit_solution(1668576317691873939)
XLA Ops:
  0.6 2.3 fusion.3
  3.1 1.2 shard_map.122
  4.3 7.3 %all-to-all-start = ((bf16[8,64,960]{2,1,0:T(8,128)(2,1)}), bf16[8,64,960]{2,1,0:T(8,128)(2,1)S(1)}, u32[]{:S(2)}, u32[]{:S(2)}) async-start(bf16[8,64,960]{2,1,0:T(8,128)(2,1)} %shard_map.122), calls=%async_computation | async-start | bytes 2097152 | tf_op jit(solution)/shard_map/all_to_all | solution.py:527
  12.0 25.4 %all-to-all-done = bf16[8,64,960]{2,1,0:T(8,128)(2,1)S(1)} async-done(((bf16[8,64,960]{2,1,0:T(8,128)(2,1)}), bf16[8,64,960]{2,1,0:T(8,128)(2,1)S(1)}, u32[]{:S(2)}, u32[]{:S(2)}) %all-to-all-start) | async-done | bytes 983072 | tf_op jit(solution)/shard_map/all_to_all | solution.py:527
  37.3 5.6 %shard_map.123 = bf16[512,320]{1,0:T(8,128)(2,1)} custom-call(bf16[512,960]{1,0:T(8,128)(2,1)S(1)} %bitcast.22, s32[1,512]{1,0:T(1,128)S(1)} %copy-done.5, s32[512,1]{1,0:T(8,128)S(1)} %copy.40.seg_col_ref), custom_call_target="tpu_custom_call" | custom-call | flops 335544320 | bytes 1310720 | tf_op jit(solution)/shard_map/pallas_call | solution.py:56
  42.9 3.6 %all-to-all-start.1 = ((bf16[8,64,320]{2,1,0:T(8,128)(2,1)}), bf16[8,64,320]{2,1,0:T(8,128)(2,1)S(1)}, u32[]{:S(2)}, u32[]{:S(2)}) async-start(bf16[8,64,320]{2,1,0:T(8,128)(2,1)} %bitcast.5), calls=%async_computation.1 | async-start | bytes 786432 | tf_op jit(solution)/shard_map/all_to_all | solution.py:530
  47.3 11.0 %all-to-all-done.1.context_ref = bf16[8,64,320]{2,1,0:T(8,128)(2,1)S(1)} async-done(((bf16[8,64,320]{2,1,0:T(8,128)(2,1)}), bf16[8,64,320]{2,1,0:T(8,128)(2,1)S(1)}, u32[]{:S(2)}, u32[]{:S(2)}) %all-to-all-start.1) | async-done | bytes 327712 | tf_op jit(solution)/shard_map/all_to_all | solution.py:530
  60.3 1.5 collective-permute-start
  61.8 1.9 collective-permute-start.8
  63.7 5.9 %collective-permute-done.3.refs_4_ = bf16[64,2432]{1,0:T(8,128)(2,1)S(1)} collective-permute-done((bf16[64,2432]{1,0:T(8,128)(2,1)S(1)}, bf16[64,2432]{1,0:T(8,128)(2,1)S(1)}, u32[]{:S(2)}, u32[]{:S(2)}) %collective-permute-start.3) | collective-permute-done | bytes 311328 | tf_op jit(solution)/shard_map/ppermute | solution.py:416
  69.6 2.5 %collective-permute-start.5 = (bf16[64,2432]{1,0:T(8,128)(2,1)S(1)}, bf16[64,2432]{1,0:T(8,128)(2,1)S(1)}, u32[]{:S(2)}, u32[]{:S(2)}) collective-permute-start(bf16[64,2432]{1,0:T(8,128)(2,1)S(1)} %collective-permute-done.3.refs_4_), channel_id=1, source_target_pairs={{0,2},{1,3},{2,0},{3,1},{4,6},{5,7},{6,4},{7,5},{8,10},{9,11},{10,... | collective-permute-start | bytes 933896 | tf_op jit(solution)/shard_map/ppermute | solution.py:416
  72.2 3.8 %collective-permute-start.4 = (bf16[64,2432]{1,0:T(8,128)(2,1)S(1)}, bf16[64,2432]{1,0:T(8,128)(2,1)S(1)}, u32[]{:S(2)}, u32[]{:S(2)}) collective-permute-start(bf16[64,2432]{1,0:T(8,128)(2,1)S(1)} %collective-permute-done.3.refs_4_), channel_id=1, source_target_pairs={{0,4},{4,0},{8,12},{12,8},{16,20},{20,16},{24,28},{28,24},{1,5},{5... | collective-permute-start | bytes 933896 | tf_op jit(solution)/shard_map/ppermute | solution.py:416
  75.9 1.2 collective-permute-done.8.refs_0_
  77.2 4.6 %collective-permute-done.4.refs_5_.refs_4_ = bf16[64,2432]{1,0:T(8,128)(2,1)S(1)} collective-permute-done((bf16[64,2432]{1,0:T(8,128)(2,1)S(1)}, bf16[64,2432]{1,0:T(8,128)(2,1)S(1)}, u32[]{:S(2)}, u32[]{:S(2)}) %collective-permute-start.4) | collective-permute-done | bytes 311328 | tf_op jit(solution)/shard_map/ppermute | solution.py:416
  81.8 1.7 collective-permute-start.10
  83.9 5.1 %collective-permute-done.10.refs_1_.refs_2_ = bf16[64,2432]{1,0:T(8,128)(2,1)} collective-permute-done((bf16[64,2432]{1,0:T(8,128)(2,1)S(1)}, bf16[64,2432]{1,0:T(8,128)(2,1)}, u32[]{:S(2)}, u32[]{:S(2)}) %collective-permute-start.10) | collective-permute-done | bytes 311328 | tf_op jit(solution)/shard_map/ppermute | solution.py:416
  89.0 1.5 collective-permute-done.9.refs_2_.refs_1_
  91.6 1.7 collective-permute-start.14
  93.9 6.9 %collective-permute-done.14.refs_6_ = bf16[64,2432]{1,0:T(8,128)(2,1)} collective-permute-done((bf16[64,2432]{1,0:T(8,128)(2,1)}, bf16[64,2432]{1,0:T(8,128)(2,1)}, u32[]{:S(2)}, u32[]{:S(2)}) %collective-permute-start.14) | collective-permute-done | bytes 311328 | tf_op jit(solution)/shard_map/ppermute | solution.py:416
  101.5 2.1 collective-permute-done.13.refs_5_
  104.2 3.9 %collective-permute-done.15.refs_7_ = bf16[64,2432]{1,0:T(8,128)(2,1)} collective-permute-done((bf16[64,2432]{1,0:T(8,128)(2,1)}, bf16[64,2432]{1,0:T(8,128)(2,1)}, u32[]{:S(2)}, u32[]{:S(2)}) %collective-permute-start.15) | collective-permute-done | bytes 311328 | tf_op jit(solution)/shard_map/ppermute | solution.py:416
  109.0 4.1 %shard_map.129 = (bf16[2,192,2304]{2,1,0:T(8,128)(2,1)S(1)}, bf16[2,192,2304]{2,1,0:T(8,128)(2,1)}, bf16[512,128]{1,0:T(8,128)(2,1)S(1)}) custom-call(s32[2]{0:T(128)S(1)} %add_multiply_fusion.bases_ref, bf16[64,2432]{1,0:T(8,128)(2,1)S(1)} %shard_map.127.refs_0_, bf16[64,2432]{1,0:T(8,128)(2,1)S(1)} %copy-done.2, ...), custom_call_target="tpu_custom_call" | custom-call | flops 905969664 | bytes 6029312 | tf_op jit(solution)/shard_map/pallas_call | solution.py:296
  113.2 1.2 copy-done.12
  114.4 1.5 collective-permute-start.2
  116.4 7.7 %collective-permute-done.2.refs_3_ = bf16[64,2432]{1,0:T(8,128)(2,1)S(1)} collective-permute-done((bf16[64,2432]{1,0:T(8,128)(2,1)S(1)}, bf16[64,2432]{1,0:T(8,128)(2,1)S(1)}, u32[]{:S(2)}, u32[]{:S(2)}) %collective-permute-start.2) | collective-permute-done | bytes 311328 | tf_op jit(solution)/shard_map/ppermute | solution.py:416
  126.3 3.1 %shard_map.125 = (bf16[2,192,2304]{2,1,0:T(8,128)(2,1)S(1)}, bf16[2,192,2304]{2,1,0:T(8,128)(2,1)}, bf16[512,128]{1,0:T(8,128)(2,1)S(1)}) custom-call(s32[2]{0:T(128)S(1)} %add_multiply_fusion.bases_ref, bf16[64,2432]{1,0:T(8,128)(2,1)S(1)} %copy-done.9, bf16[64,2432]{1,0:T(8,128)(2,1)S(1)} %collective-permute-done.refs_1_.refs_2_, ...), custom_call_target="tpu_custom_call" | custom-call | flops 905969664 | bytes 6029312 | tf_op jit(solution)/shard_map/pallas_call | solution.py:296
  129.4 1.2 copy-done.14
  130.8 1.7 shard_map.126.rest_1_
  132.4 3.7 %all-to-all-start.2 = ((bf16[8,64,640]{2,1,0:T(8,128)(2,1)}), bf16[8,64,640]{2,1,0:T(8,128)(2,1)S(1)}, u32[]{:S(2)}, u32[]{:S(2)}) async-start(bf16[8,64,640]{2,1,0:T(8,128)(2,1)} %shard_map.126.rest_1_), calls=%async_computation.2 | async-start | bytes 1310720 | tf_op jit(solution)/shard_map/all_to_all | solution.py:547
  136.2 2.9 %copy-done.6 = bf16[2,2304,720]{1,2,0:T(8,128)(2,1)S(1)} copy-done((bf16[2,2304,720]{1,2,0:T(8,128)(2,1)S(1)}, bf16[2,2304,720]{1,2,0:T(8,128)(2,1)}, u32[]{:S(2)}) %copy-start.6) | copy-done | bytes 6635544
  139.1 1.5 copy-done.13
  140.5 15.3 %shard_map.130 = (bf16[2,192,2304]{2,1,0:T(8,128)(2,1)S(1)}, bf16[2,192,2304]{2,1,0:T(8,128)(2,1)}) custom-call(bf16[2,192,2304]{2,1,0:T(8,128)(2,1)S(1)} %copy-done.13, bf16[2,192,2304]{2,1,0:T(8,128)(2,1)} %collective-permute-done.16.got_ref, bf16[2,720,2304]{2,1,0:T(8,128)(2,1)S(1)} %bitcast.28, bf16[2,720,2304]{2,1,0:T(8,128)(2,1)} %bitcast.31, ...), custom_call_target="tpu_custom_call" | custom-call | flops 7644119040 | bytes 26984448 | tf_op jit(solution)/shard_map/pallas_call | solution.py:344
  159.2 2.9 %copy-done.7 = bf16[2,2304,720]{1,2,0:T(8,128)(2,1)S(1)} copy-done((bf16[2,2304,720]{1,2,0:T(8,128)(2,1)S(1)}, bf16[2,2304,720]{1,2,0:T(8,128)(2,1)}, u32[]{:S(2)}) %copy-start.7) | copy-done | bytes 6635544
  162.1 14.3 %shard_map.132 = (bf16[2,192,2304]{2,1,0:T(8,128)(2,1)S(1)}, bf16[2,192,2304]{2,1,0:T(8,128)(2,1)S(1)}) custom-call(bf16[2,192,2304]{2,1,0:T(8,128)(2,1)S(1)} %copy-done.15, bf16[2,192,2304]{2,1,0:T(8,128)(2,1)} %collective-permute-done.7.got_ref, bf16[2,720,2304]{2,1,0:T(8,128)(2,1)S(1)} %bitcast.29, bf16[2,720,2304]{2,1,0:T(8,128)(2,1)} %bitcast.32, ...), custom_call_target="tpu_custom_call" | custom-call | flops 7644119040 | bytes 26984448 | tf_op jit(solution)/shard_map/pallas_call | solution.py:344
  176.4 4.5 %shard_map.133 = (bf16[256,2304]{1,0:T(8,128)(2,1)S(1)}, bf16[128,2304]{1,0:T(8,128)(2,1)S(1)}, bf16[128,2304]{1,0:T(8,128)(2,1)S(1)}) custom-call(s32[2]{0:T(128)S(1)} %add_multiply_fusion.bases_ref, bf16[2,192,2304]{2,1,0:T(8,128)(2,1)S(1)} %get-tuple-element.40.y_own_ref, bf16[2,192,2304]{2,1,0:T(8,128)(2,1)} %collective-permute-done.18.y_got_ref, ...), custom_call_target="tpu_custom_call" | custom-call | flops 905969664 | bytes 18874368 | tf_op jit(solution)/shard_map/pallas_call | solution.py:399
  180.9 1.8 collective-permute-start.19
  183.4 13.2 %collective-permute-done.19.rest_0_ = bf16[128,2304]{1,0:T(8,128)(2,1)S(1)} collective-permute-done((bf16[128,2304]{1,0:T(8,128)(2,1)S(1)}, bf16[128,2304]{1,0:T(8,128)(2,1)S(1)}, u32[]{:S(2)}, u32[]{:S(2)}) %collective-permute-start.19) | collective-permute-done | bytes 589856 | tf_op jit(solution)/shard_map/ppermute | solution.py:416
  199.3 3.5 %shard_map.135 = (bf16[256,2304]{1,0:T(8,128)(2,1)S(1)}, bf16[128,2304]{1,0:T(8,128)(2,1)S(1)}, bf16[128,2304]{1,0:T(8,128)(2,1)S(1)}) custom-call(s32[2]{0:T(128)S(1)} %add_multiply_fusion.bases_ref, bf16[2,192,2304]{2,1,0:T(8,128)(2,1)S(1)} %get-tuple-element.37.y_own_ref, bf16[2,192,2304]{2,1,0:T(8,128)(2,1)S(1)} %collective-permute-done.17.y_got_ref, ...), custom_call_target="tpu_custom_call" | custom-call | flops 905969664 | bytes 18874368 | tf_op jit(solution)/shard_map/pallas_call | solution.py:399
  202.9 3.3 %collective-permute-done.21.refs_1_.rest_0_ = bf16[64,2304]{1,0:T(8,128)(2,1)S(1)} collective-permute-done((bf16[64,2304]{1,0:T(8,128)(2,1)S(1)}, bf16[64,2304]{1,0:T(8,128)(2,1)S(1)}, u32[]{:S(2)}, u32[]{:S(2)}) %collective-permute-start.21) | collective-permute-done | bytes 294944 | tf_op jit(solution)/shard_map/ppermute | solution.py:416
  206.3 1.7 collective-permute-start.24
  209.0 1.3 collective-permute-start.27
  210.2 9.3 %collective-permute-done.24.rest_1_ = bf16[128,2304]{1,0:T(8,128)(2,1)S(1)} collective-permute-done((bf16[128,2304]{1,0:T(8,128)(2,1)S(1)}, bf16[128,2304]{1,0:T(8,128)(2,1)S(1)}, u32[]{:S(2)}, u32[]{:S(2)}) %collective-permute-start.24) | collective-permute-done | bytes 589856 | tf_op jit(solution)/shard_map/ppermute | solution.py:416
  221.6 1.2 collective-permute-start.26
  222.9 1.9 collective-permute-start.29
  224.9 2.9 %collective-permute-done.25.rest_0_ = bf16[64,2304]{1,0:T(8,128)(2,1)S(1)} collective-permute-done((bf16[64,2304]{1,0:T(8,128)(2,1)S(1)}, bf16[64,2304]{1,0:T(8,128)(2,1)S(1)}, u32[]{:S(2)}, u32[]{:S(2)}) %collective-permute-start.25) | collective-permute-done | bytes 294944 | tf_op jit(solution)/shard_map/ppermute | solution.py:416
  228.5 1.6 collective-permute-start.28
  230.1 5.6 %collective-permute-done.29 = bf16[64,2304]{1,0:T(8,128)(2,1)S(1)} collective-permute-done((bf16[64,2304]{1,0:T(8,128)(2,1)S(1)}, bf16[64,2304]{1,0:T(8,128)(2,1)S(1)}, u32[]{:S(2)}, u32[]{:S(2)}) %collective-permute-start.29) | collective-permute-done | bytes 294944 | tf_op jit(solution)/shard_map/ppermute | solution.py:416
  235.7 3.1 %collective-permute-done.28 = bf16[64,2304]{1,0:T(8,128)(2,1)S(1)} collective-permute-done((bf16[64,2304]{1,0:T(8,128)(2,1)S(1)}, bf16[64,2304]{1,0:T(8,128)(2,1)S(1)}, u32[]{:S(2)}, u32[]{:S(2)}) %collective-permute-start.28) | collective-permute-done | bytes 294944 | tf_op jit(solution)/shard_map/ppermute | solution.py:416
  (96 shorter events, 21.8 us)
Async XLA Ops:
  0.6 2.4 copy-start.4
  3.0 8.5 %copy-start.5 = (s32[1,512]{1,0:T(1,128)S(1)}, s32[1,512]{1,0:T(1,128)}, u32[]{:S(2)}) copy-start(s32[1,512]{1,0:T(1,128)} %seg_row_ref.1) | copy-start | bytes 6148
  3.0 8.7 %copy-start.17 = (s32[1,64,2]{1,2,0:T(2,128)S(1)}, s32[1,64,2]{1,2,0:T(2,128)}, u32[]{:S(2)}) copy-start(s32[1,64,2]{1,2,0:T(2,128)} %param.16) | copy-start | bytes 1540
  4.3 33.0 %all-to-all-start = ((bf16[8,64,960]{2,1,0:T(8,128)(2,1)}), bf16[8,64,960]{2,1,0:T(8,128)(2,1)S(1)}, u32[]{:S(2)}, u32[]{:S(2)}) async-start(bf16[8,64,960]{2,1,0:T(8,128)(2,1)} %shard_map.122), calls=%async_computation | async-start | bytes 2097152 | tf_op jit(solution)/shard_map/all_to_all | solution.py:527
  37.3 9.9 %copy-start.18 = (f32[1,64,2]{1,2,0:T(2,128)S(1)}, f32[1,64,2]{1,2,0:T(2,128)}, u32[]{:S(2)}) copy-start(f32[1,64,2]{1,2,0:T(2,128)} %param.17) | copy-start | bytes 1540
  37.3 10.0 %copy-start.16 = (bf16[2304]{0:T(1024)(128)(2,1)S(1)}, bf16[2304]{0:T(1024)(128)(2,1)}, u32[]{:S(2)}) copy-start(bf16[2304]{0:T(1024)(128)(2,1)} %param.14) | copy-start | bytes 13828
  37.3 21.1 %copy-start.3 = (bf16[1,64,2304]{2,1,0:T(8,128)(2,1)S(1)}, bf16[1,64,2304]{2,1,0:T(8,128)(2,1)}, u32[]{:S(2)}) copy-start(bf16[1,64,2304]{2,1,0:T(8,128)(2,1)} %param.13) | copy-start | bytes 884740
  42.9 15.5 %all-to-all-start.1 = ((bf16[8,64,320]{2,1,0:T(8,128)(2,1)}), bf16[8,64,320]{2,1,0:T(8,128)(2,1)S(1)}, u32[]{:S(2)}, u32[]{:S(2)}) async-start(bf16[8,64,320]{2,1,0:T(8,128)(2,1)} %bitcast.5), calls=%async_computation.1 | async-start | bytes 786432 | tf_op jit(solution)/shard_map/all_to_all | solution.py:530
  58.7 32.2 %copy-start.8 = (bf16[64,2432]{1,0:T(8,128)(2,1)}, bf16[64,2432]{1,0:T(8,128)(2,1)S(1)}, u32[]{:S(2)}) copy-start(bf16[64,2432]{1,0:T(8,128)(2,1)S(1)} %get-tuple-element.31.refs_0_) | copy-start | bytes 933892
  58.7 11.0 %collective-permute-start.3 = (bf16[64,2432]{1,0:T(8,128)(2,1)S(1)}, bf16[64,2432]{1,0:T(8,128)(2,1)S(1)}, u32[]{:S(2)}, u32[]{:S(2)}) collective-permute-start(bf16[64,2432]{1,0:T(8,128)(2,1)S(1)} %get-tuple-element.31.refs_0_), channel_id=1, source_target_pairs={{0,8},{4,12},{8,0},{12,4},{16,24},{20,28},{24,16},{28,20},{1,9},{5... | collective-permute-start | bytes 933896 | tf_op jit(solution)/shard_map/ppermute | solution.py:416
  59.7 16.3 %collective-permute-start.1 = (bf16[64,2432]{1,0:T(8,128)(2,1)S(1)}, bf16[64,2432]{1,0:T(8,128)(2,1)S(1)}, u32[]{:S(2)}, u32[]{:S(2)}) collective-permute-start(bf16[64,2432]{1,0:T(8,128)(2,1)S(1)} %get-tuple-element.31.refs_0_), channel_id=1, source_target_pairs={{0,4},{4,0},{8,12},{12,8},{16,20},{20,16},{24,28},{28,24},{1,5},{5... | collective-permute-start | bytes 933896 | tf_op jit(solution)/shard_map/ppermute | solution.py:416
  60.3 15.7 %collective-permute-start = (bf16[64,2432]{1,0:T(8,128)(2,1)S(1)}, bf16[64,2432]{1,0:T(8,128)(2,1)S(1)}, u32[]{:S(2)}, u32[]{:S(2)}) collective-permute-start(bf16[64,2432]{1,0:T(8,128)(2,1)S(1)} %get-tuple-element.31.refs_0_), channel_id=1, source_target_pairs={{0,2},{1,3},{2,0},{3,1},{4,6},{5,7},{6,4},{7,5},{8,10},{9,11},{10,... | collective-permute-start | bytes 933896 | tf_op jit(solution)/shard_map/ppermute | solution.py:416
  61.8 15.4 %collective-permute-start.8 = (bf16[64,2432]{1,0:T(8,128)(2,1)S(1)}, bf16[64,2432]{1,0:T(8,128)(2,1)S(1)}, u32[]{:S(2)}, u32[]{:S(2)}) collective-permute-start(bf16[64,2432]{1,0:T(8,128)(2,1)S(1)} %get-tuple-element.31.refs_0_), channel_id=1, source_target_pairs={{0,16},{4,20},{8,24},{12,28},{16,0},{20,4},{24,8},{28,12},{1,17},{... | collective-permute-start | bytes 933896 | tf_op jit(solution)/shard_map/ppermute | solution.py:416
  69.6 12.2 %copy-start.10 = (bf16[64,2432]{1,0:T(8,128)(2,1)}, bf16[64,2432]{1,0:T(8,128)(2,1)S(1)}, u32[]{:S(2)}) copy-start(bf16[64,2432]{1,0:T(8,128)(2,1)S(1)} %collective-permute-done.3.refs_4_) | copy-start | bytes 933892
  69.6 7.5 %collective-permute-start.5 = (bf16[64,2432]{1,0:T(8,128)(2,1)S(1)}, bf16[64,2432]{1,0:T(8,128)(2,1)S(1)}, u32[]{:S(2)}, u32[]{:S(2)}) collective-permute-start(bf16[64,2432]{1,0:T(8,128)(2,1)S(1)} %collective-permute-done.3.refs_4_), channel_id=1, source_target_pairs={{0,2},{1,3},{2,0},{3,1},{4,6},{5,7},{6,4},{7,5},{8,10},{9,11},{10,... | collective-permute-start | bytes 933896 | tf_op jit(solution)/shard_map/ppermute | solution.py:416
  72.2 9.7 %collective-permute-start.4 = (bf16[64,2432]{1,0:T(8,128)(2,1)S(1)}, bf16[64,2432]{1,0:T(8,128)(2,1)S(1)}, u32[]{:S(2)}, u32[]{:S(2)}) collective-permute-start(bf16[64,2432]{1,0:T(8,128)(2,1)S(1)} %collective-permute-done.3.refs_4_), channel_id=1, source_target_pairs={{0,4},{4,0},{8,12},{12,8},{16,20},{20,16},{24,28},{28,24},{1,5},{5... | collective-permute-start | bytes 933896 | tf_op jit(solution)/shard_map/ppermute | solution.py:416
  81.8 7.1 %collective-permute-start.10 = (bf16[64,2432]{1,0:T(8,128)(2,1)S(1)}, bf16[64,2432]{1,0:T(8,128)(2,1)}, u32[]{:S(2)}, u32[]{:S(2)}) collective-permute-start(bf16[64,2432]{1,0:T(8,128)(2,1)S(1)} %shard_map.127.refs_0_), channel_id=1, source_target_pairs={{0,4},{4,0},{8,12},{12,8},{16,20},{20,16},{24,28},{28,24},{1,5},{5... | collective-permute-start | bytes 933896 | tf_op jit(solution)/shard_map/ppermute | solution.py:416
  83.6 6.9 %collective-permute-start.9 = (bf16[64,2432]{1,0:T(8,128)(2,1)S(1)}, bf16[64,2432]{1,0:T(8,128)(2,1)S(1)}, u32[]{:S(2)}, u32[]{:S(2)}) collective-permute-start(bf16[64,2432]{1,0:T(8,128)(2,1)S(1)} %shard_map.127.refs_0_), channel_id=1, source_target_pairs={{0,2},{1,3},{2,0},{3,1},{4,6},{5,7},{6,4},{7,5},{8,10},{9,11},{10,... | collective-permute-start | bytes 933896 | tf_op jit(solution)/shard_map/ppermute | solution.py:416
  83.9 7.0 %collective-permute-start.12 = (bf16[64,2432]{1,0:T(8,128)(2,1)S(1)}, bf16[64,2432]{1,0:T(8,128)(2,1)}, u32[]{:S(2)}, u32[]{:S(2)}) collective-permute-start(bf16[64,2432]{1,0:T(8,128)(2,1)S(1)} %shard_map.127.refs_0_), channel_id=1, source_target_pairs={{0,8},{4,12},{8,0},{12,4},{16,24},{20,28},{24,16},{28,20},{1,9},{5... | collective-permute-start | bytes 933896 | tf_op jit(solution)/shard_map/ppermute | solution.py:416
  91.6 9.2 %collective-permute-start.14 = (bf16[64,2432]{1,0:T(8,128)(2,1)}, bf16[64,2432]{1,0:T(8,128)(2,1)}, u32[]{:S(2)}, u32[]{:S(2)}) collective-permute-start(bf16[64,2432]{1,0:T(8,128)(2,1)} %shard_map.128.refs_4_), channel_id=1, source_target_pairs={{0,2},{1,3},{2,0},{3,1},{4,6},{5,7},{6,4},{7,5},{8,10},{9,11},{10,... | collective-permute-start | bytes 933896 | tf_op jit(solution)/shard_map/ppermute | solution.py:416
  93.3 10.2 %collective-permute-start.13 = (bf16[64,2432]{1,0:T(8,128)(2,1)}, bf16[64,2432]{1,0:T(8,128)(2,1)}, u32[]{:S(2)}, u32[]{:S(2)}) collective-permute-start(bf16[64,2432]{1,0:T(8,128)(2,1)} %shard_map.128.refs_4_), channel_id=1, source_target_pairs={{0,4},{4,0},{8,12},{12,8},{16,20},{20,16},{24,28},{28,24},{1,5},{5... | collective-permute-start | bytes 933896 | tf_op jit(solution)/shard_map/ppermute | solution.py:416
  93.6 10.6 %collective-permute-start.11 = (bf16[64,2432]{1,0:T(8,128)(2,1)}, bf16[64,2432]{1,0:T(8,128)(2,1)}, u32[]{:S(2)}, u32[]{:S(2)}) collective-permute-start(bf16[64,2432]{1,0:T(8,128)(2,1)} %collective-permute-done.10.refs_1_.refs_2_), channel_id=1, source_target_pairs={{0,2},{1,3},{2,0},{3,1},{4,6},{5,7},{6,4},{7,5},{8,10},{9,11},{10,... | collective-permute-start | bytes 933896 | tf_op jit(solution)/shard_map/ppermute | solution.py:416
  100.8 7.2 %collective-permute-start.15 = (bf16[64,2432]{1,0:T(8,128)(2,1)}, bf16[64,2432]{1,0:T(8,128)(2,1)}, u32[]{:S(2)}, u32[]{:S(2)}) collective-permute-start(bf16[64,2432]{1,0:T(8,128)(2,1)} %collective-permute-done.14.refs_6_), channel_id=1, source_target_pairs={{0,4},{4,0},{8,12},{12,8},{16,20},{20,16},{24,28},{28,24},{1,5},{5... | collective-permute-start | bytes 933896 | tf_op jit(solution)/shard_map/ppermute | solution.py:416
  109.0 16.3 %copy-start.9 = (bf16[64,2432]{1,0:T(8,128)(2,1)S(1)}, bf16[64,2432]{1,0:T(8,128)(2,1)}, u32[]{:S(2)}) copy-start(bf16[64,2432]{1,0:T(8,128)(2,1)} %copy-done.8) | copy-start | bytes 933892
  114.4 16.3 %copy-start.19 = (s32[1,32]{1,0:T(1,128)S(1)}, s32[1,32]{1,0:T(1,128)}, u32[]{:S(2)}) copy-start(s32[1,32]{1,0:T(1,128)} %param.18) | copy-start | bytes 388
  114.4 21.8 %collective-permute-start.16 = (bf16[2,192,2304]{2,1,0:T(8,128)(2,1)}, bf16[2,192,2304]{2,1,0:T(8,128)(2,1)}, u32[]{:S(2)}, u32[]{:S(2)}) collective-permute-start(bf16[2,192,2304]{2,1,0:T(8,128)(2,1)} %get-tuple-element.35), channel_id=1, source_target_pairs={{0,1},{1,0},{2,3},{3,2},{4,5},{5,4},{6,7},{7,6},{8,9},{9,8},{10,11... | collective-permute-start | bytes 5308424 | tf_op jit(solution)/shard_map/ppermute | solution.py:416
  114.4 9.8 %collective-permute-start.2 = (bf16[64,2432]{1,0:T(8,128)(2,1)S(1)}, bf16[64,2432]{1,0:T(8,128)(2,1)S(1)}, u32[]{:S(2)}, u32[]{:S(2)}) collective-permute-start(bf16[64,2432]{1,0:T(8,128)(2,1)S(1)} %collective-permute-done.1.refs_2_.refs_1_), channel_id=1, source_target_pairs={{0,2},{1,3},{2,0},{3,1},{4,6},{5,7},{6,4},{7,5},{8,10},{9,11},{10,... | collective-permute-start | bytes 933896 | tf_op jit(solution)/shard_map/ppermute | solution.py:416
  115.8 9.5 %collective-permute-start.6 = (bf16[64,2432]{1,0:T(8,128)(2,1)S(1)}, bf16[64,2432]{1,0:T(8,128)(2,1)S(1)}, u32[]{:S(2)}, u32[]{:S(2)}) collective-permute-start(bf16[64,2432]{1,0:T(8,128)(2,1)S(1)} %collective-permute-done.5.refs_6_.refs_3_), channel_id=1, source_target_pairs={{0,4},{4,0},{8,12},{12,8},{16,20},{20,16},{24,28},{28,24},{1,5},{5... | collective-permute-start | bytes 933896 | tf_op jit(solution)/shard_map/ppermute | solution.py:416
  129.4 1.2 copy-start.14
  130.7 26.8 %collective-permute-start.7 = (bf16[2,192,2304]{2,1,0:T(8,128)(2,1)}, bf16[2,192,2304]{2,1,0:T(8,128)(2,1)}, u32[]{:S(2)}, u32[]{:S(2)}) collective-permute-start(bf16[2,192,2304]{2,1,0:T(8,128)(2,1)} %get-tuple-element.33.late_ref.rest_0_), channel_id=1, source_target_pairs={{0,1},{1,0},{2,3},{3,2},{4,5},{5,4},{6,7},{7,6},{8,9},{9,8},{10,11... | collective-permute-start | bytes 5308424 | tf_op jit(solution)/shard_map/ppermute | solution.py:416
  132.4 24.0 %all-to-all-start.2 = ((bf16[8,64,640]{2,1,0:T(8,128)(2,1)}), bf16[8,64,640]{2,1,0:T(8,128)(2,1)S(1)}, u32[]{:S(2)}, u32[]{:S(2)}) async-start(bf16[8,64,640]{2,1,0:T(8,128)(2,1)} %shard_map.126.rest_1_), calls=%async_computation.2 | async-start | bytes 1310720 | tf_op jit(solution)/shard_map/all_to_all | solution.py:547
  136.2 2.9 %copy-start.6 = (bf16[2,2304,720]{1,2,0:T(8,128)(2,1)S(1)}, bf16[2,2304,720]{1,2,0:T(8,128)(2,1)}, u32[]{:S(2)}) copy-start(bf16[2,2304,720]{1,2,0:T(8,128)(2,1)} %param.19) | copy-start | bytes 19906564
  139.1 1.5 copy-start.13
  155.8 20.6 %collective-permute-start.18 = (bf16[2,192,2304]{2,1,0:T(8,128)(2,1)}, bf16[2,192,2304]{2,1,0:T(8,128)(2,1)}, u32[]{:S(2)}, u32[]{:S(2)}) collective-permute-start(bf16[2,192,2304]{2,1,0:T(8,128)(2,1)} %get-tuple-element.36.behind_ref.rest_1_), channel_id=1, source_target_pairs={{0,1},{1,0},{2,3},{3,2},{4,5},{5,4},{6,7},{7,6},{8,9},{9,8},{10,11... | collective-permute-start | bytes 5308424 | tf_op jit(solution)/shard_map/ppermute | solution.py:416
  156.4 1.7 copy-start.15
  159.2 2.9 %copy-start.7 = (bf16[2,2304,720]{1,2,0:T(8,128)(2,1)S(1)}, bf16[2,2304,720]{1,2,0:T(8,128)(2,1)}, u32[]{:S(2)}) copy-start(bf16[2,2304,720]{1,2,0:T(8,128)(2,1)} %param.19) | copy-start | bytes 19906564
  176.3 23.0 %collective-permute-start.17 = (bf16[2,192,2304]{2,1,0:T(8,128)(2,1)S(1)}, bf16[2,192,2304]{2,1,0:T(8,128)(2,1)S(1)}, u32[]{:S(2)}, u32[]{:S(2)}) collective-permute-start(bf16[2,192,2304]{2,1,0:T(8,128)(2,1)S(1)} %get-tuple-element.38.rest_0_), channel_id=1, source_target_pairs={{0,1},{1,0},{2,3},{3,2},{4,5},{5,4},{6,7},{7,6},{8,9},{9,8},{10,11... | collective-permute-start | bytes 5308424 | tf_op jit(solution)/shard_map/ppermute | solution.py:416
  180.9 15.8 %collective-permute-start.19 = (bf16[128,2304]{1,0:T(8,128)(2,1)S(1)}, bf16[128,2304]{1,0:T(8,128)(2,1)S(1)}, u32[]{:S(2)}, u32[]{:S(2)}) collective-permute-start(bf16[128,2304]{1,0:T(8,128)(2,1)S(1)} %get-tuple-element.43), channel_id=1, source_target_pairs={{0,4},{4,0},{8,12},{12,8},{16,20},{20,16},{24,28},{28,24},{1,5},{5... | collective-permute-start | bytes 1769480 | tf_op jit(solution)/shard_map/ppermute | solution.py:416
  182.7 15.2 %collective-permute-start.20 = (bf16[128,2304]{1,0:T(8,128)(2,1)S(1)}, bf16[128,2304]{1,0:T(8,128)(2,1)S(1)}, u32[]{:S(2)}, u32[]{:S(2)}) collective-permute-start(bf16[128,2304]{1,0:T(8,128)(2,1)S(1)} %get-tuple-element.44), channel_id=1, source_target_pairs={{0,2},{1,3},{2,0},{3,1},{4,6},{5,7},{6,4},{7,5},{8,10},{9,11},{10,... | collective-permute-start | bytes 1769480 | tf_op jit(solution)/shard_map/ppermute | solution.py:416
  198.1 8.0 %collective-permute-start.21 = (bf16[64,2304]{1,0:T(8,128)(2,1)S(1)}, bf16[64,2304]{1,0:T(8,128)(2,1)S(1)}, u32[]{:S(2)}, u32[]{:S(2)}) collective-permute-start(bf16[64,2304]{1,0:T(8,128)(2,1)S(1)} %get-tuple-element.45.rest_0_), channel_id=1, source_target_pairs={{0,2},{1,3},{2,0},{3,1},{4,6},{5,7},{6,4},{7,5},{8,10},{9,11},{10,... | collective-permute-start | bytes 884744 | tf_op jit(solution)/shard_map/ppermute | solution.py:416
  198.8 7.5 %collective-permute-start.22 = (bf16[64,2304]{1,0:T(8,128)(2,1)S(1)}, bf16[64,2304]{1,0:T(8,128)(2,1)S(1)}, u32[]{:S(2)}, u32[]{:S(2)}) collective-permute-start(bf16[64,2304]{1,0:T(8,128)(2,1)S(1)} %get-tuple-element.48), channel_id=1, source_target_pairs={{0,4},{4,0},{8,12},{12,8},{16,20},{20,16},{24,28},{28,24},{1,5},{5... | collective-permute-start | bytes 884744 | tf_op jit(solution)/shard_map/ppermute | solution.py:416
  206.3 13.3 %collective-permute-start.24 = (bf16[128,2304]{1,0:T(8,128)(2,1)S(1)}, bf16[128,2304]{1,0:T(8,128)(2,1)S(1)}, u32[]{:S(2)}, u32[]{:S(2)}) collective-permute-start(bf16[128,2304]{1,0:T(8,128)(2,1)S(1)} %shard_map.137), channel_id=1, source_target_pairs={{0,2},{1,3},{2,0},{3,1},{4,6},{5,7},{6,4},{7,5},{8,10},{9,11},{10,... | collective-permute-start | bytes 1769480 | tf_op jit(solution)/shard_map/ppermute | solution.py:416
  207.9 12.8 %collective-permute-start.23 = (bf16[128,2304]{1,0:T(8,128)(2,1)S(1)}, bf16[128,2304]{1,0:T(8,128)(2,1)S(1)}, u32[]{:S(2)}, u32[]{:S(2)}) collective-permute-start(bf16[128,2304]{1,0:T(8,128)(2,1)S(1)} %shard_map.136), channel_id=1, source_target_pairs={{0,4},{4,0},{8,12},{12,8},{16,20},{20,16},{24,28},{28,24},{1,5},{5... | collective-permute-start | bytes 1769480 | tf_op jit(solution)/shard_map/ppermute | solution.py:416
  209.0 13.9 %collective-permute-start.27 = (bf16[64,2304]{1,0:T(8,128)(2,1)S(1)}, bf16[64,2304]{1,0:T(8,128)(2,1)S(1)}, u32[]{:S(2)}, u32[]{:S(2)}) collective-permute-start(bf16[64,2304]{1,0:T(8,128)(2,1)S(1)} %get-tuple-element.51.rest_2_), channel_id=1, source_target_pairs={{0,8},{4,12},{8,0},{12,4},{16,24},{20,28},{24,16},{28,20},{1,9},{5... | collective-permute-start | bytes 884744 | tf_op jit(solution)/shard_map/ppermute | solution.py:416
  221.0 6.8 %collective-permute-start.25 = (bf16[64,2304]{1,0:T(8,128)(2,1)S(1)}, bf16[64,2304]{1,0:T(8,128)(2,1)S(1)}, u32[]{:S(2)}, u32[]{:S(2)}) collective-permute-start(bf16[64,2304]{1,0:T(8,128)(2,1)S(1)} %get-tuple-element.53), channel_id=1, source_target_pairs={{0,2},{1,3},{2,0},{3,1},{4,6},{5,7},{6,4},{7,5},{8,10},{9,11},{10,... | collective-permute-start | bytes 884744 | tf_op jit(solution)/shard_map/ppermute | solution.py:416
  221.6 6.7 %collective-permute-start.26 = (bf16[64,2304]{1,0:T(8,128)(2,1)S(1)}, bf16[64,2304]{1,0:T(8,128)(2,1)S(1)}, u32[]{:S(2)}, u32[]{:S(2)}) collective-permute-start(bf16[64,2304]{1,0:T(8,128)(2,1)S(1)} %get-tuple-element.54), channel_id=1, source_target_pairs={{0,4},{4,0},{8,12},{12,8},{16,20},{20,16},{24,28},{28,24},{1,5},{5... | collective-permute-start | bytes 884744 | tf_op jit(solution)/shard_map/ppermute | solution.py:416
  222.9 12.7 %collective-permute-start.29 = (bf16[64,2304]{1,0:T(8,128)(2,1)S(1)}, bf16[64,2304]{1,0:T(8,128)(2,1)S(1)}, u32[]{:S(2)}, u32[]{:S(2)}) collective-permute-start(bf16[64,2304]{1,0:T(8,128)(2,1)S(1)} %add_convert_fusion.1.rest_2_), channel_id=1, source_target_pairs={{0,16},{4,20},{8,24},{12,28},{16,0},{20,4},{24,8},{28,12},{1,17},{... | collective-permute-start | bytes 884744 | tf_op jit(solution)/shard_map/ppermute | solution.py:416
  228.5 10.2 %collective-permute-start.28 = (bf16[64,2304]{1,0:T(8,128)(2,1)S(1)}, bf16[64,2304]{1,0:T(8,128)(2,1)S(1)}, u32[]{:S(2)}, u32[]{:S(2)}) collective-permute-start(bf16[64,2304]{1,0:T(8,128)(2,1)S(1)} %get-tuple-element.57), channel_id=1, source_target_pairs={{0,8},{4,12},{8,0},{12,4},{16,24},{20,28},{24,16},{28,20},{1,9},{5... | collective-permute-start | bytes 884744 | tf_op jit(solution)/shard_map/ppermute | solution.py:416
  (5 other events, 4.9 us)

commit v10 on v9

--- a/solution.py
+++ b/solution.py
@@ -212,8 +212,9 @@
     )(order, packed, late)
 
 
-def join_pages_kernel(share, offsets, span, pages_ref, behind_ref, out_ref):
+def join_pages_kernel(share, offsets, span, pages_ref, behind_ref, out_ref, ended_ref):
     del behind_ref
+    ended_ref[...] = jnp.zeros_like(ended_ref)
     width = share * len(offsets)
     for part in range(2):
         parts = [
@@ -227,7 +228,10 @@
     n_seq, rows, _ = pages.shape
     return pl.pallas_call(
         functools.partial(join_pages_kernel, share, offsets, span),
-        out_shape=jax.ShapeDtypeStruct((rows, 2 * share * n_seq), jnp.bfloat16),
+        out_shape=(
+            jax.ShapeDtypeStruct((rows, 2 * share * n_seq), jnp.bfloat16),
+            jax.ShapeDtypeStruct((8, 128), jnp.float32),
+        ),
         in_specs=[pl.BlockSpec(memory_space=pltpu.VMEM), pl.BlockSpec(memory_space=pl.ANY)],
         compiler_params=pltpu.CompilerParams(vmem_limit_bytes=12 * MIB),
         cost_estimate=pl.CostEstimate(flops=0, bytes_accessed=8 * rows * n_seq * span, transcendentals=0),
@@ -309,9 +313,12 @@
     )(bases, *pieces, *waits)
 
 
-def rows_kernel(local, waits, own_ref, got_ref, wg_hbm, wu_hbm, wd_hbm, *rest):
-    y_own_ref, y_sib_ref, wg, wu, wd, weight_sem = rest[waits:]
-    half = own_ref.shape[1]
+def rows_kernel(local, waits, own_hbm, got_ref, wg_hbm, wu_hbm, wd_hbm, *rest):
+    y_own_ref, y_sib_ref, ended_ref, own_ref, wg, wu, wd, own_sem, weight_sem = rest[waits:]
+    ended_ref[...] = jnp.zeros_like(ended_ref)
+    half = got_ref.shape[1]
+    own_copy = pltpu.make_async_copy(own_hbm, own_ref, own_sem)
+    own_copy.start()
     copies = [
         [
             pltpu.make_async_copy(source.at[e], target.at[e], weight_sem.at[3 * e + i])
@@ -322,6 +329,7 @@
     for group in copies:
         for copy in group:
             copy.start()
+    own_copy.wait()
     for e in range(local):
         rows = jnp.concatenate([own_ref[e], got_ref[e]], axis=0)
         copies[e][0].wait()
@@ -343,11 +351,19 @@
     weights = pltpu.VMEM((local, hidden, width), jnp.bfloat16)
     return pl.pallas_call(
         functools.partial(rows_kernel, local, len(waits)),
-        out_shape=(out, out),
-        in_specs=[vmem, vmem] + [pl.BlockSpec(memory_space=pl.ANY)] * (3 + len(waits)),
-        out_specs=(vmem, vmem),
-        scratch_shapes=[weights, weights, weights, pltpu.SemaphoreType.DMA((3 * local,))],
-        compiler_params=pltpu.CompilerParams(vmem_limit_bytes=36 * MIB),
+        out_shape=(out, out, jax.ShapeDtypeStruct((8, 128), jnp.float32)),
+        in_specs=[pl.BlockSpec(memory_space=pl.ANY), vmem]
+        + [pl.BlockSpec(memory_space=pl.ANY)] * (3 + len(waits)),
+        out_specs=(vmem, vmem, vmem),
+        scratch_shapes=[
+            pltpu.VMEM(own.shape, jnp.bfloat16),
+            weights,
+            weights,
+            weights,
+            pltpu.SemaphoreType.DMA,
+            pltpu.SemaphoreType.DMA((3 * local,)),
+        ],
+        compiler_params=pltpu.CompilerParams(vmem_limit_bytes=46 * MIB),
         cost_estimate=pl.CostEstimate(
             flops=6 * local * rows * width * hidden,
             bytes_accessed=6 * local * width * hidden + 4 * local * rows * width,
@@ -476,23 +492,23 @@
     got_a = core(sib_a)
     own_b, sib_b, facts_b = select_rows(near_b, bases, local)
     got_b = core(sib_b)
-    pages, fill = late_work(sib_b)
-    own_a, sib_a = expert_rows(own_a, got_a, w_gate, w_up, w_down, [sib_b, pages])
-    other = fill(sib_a)
+    pages, fill = late_work(facts_b)
+    own_a, sib_a, ended = expert_rows(own_a, got_a, w_gate, w_up, w_down, [facts_b, pages])
+    cache, filled = fill(ended)
     got_a = core(sib_a)
-    own_b, sib_b = expert_rows(own_b, got_b, w_gate, w_up, w_down, [other, sib_a])
+    own_b, sib_b, ended = expert_rows(own_b, got_b, w_gate, w_up, w_down, [filled])
     got_b = core(sib_b)
-    keep_a, (fx_a, fy_a) = put_rows(own_a, got_a, facts_a, bases, piece.shape[0], [sib_b])
+    keep_a, (fx_a, fy_a) = put_rows(own_a, got_a, facts_a, bases, piece.shape[0], [ended])
     keep_a, (gy_a, gx_a) = fold(keep_a, [x(fx_a), y(fy_a)], 2)
     keep_b, (fx_b, fy_b) = put_rows(own_b, got_b, facts_b, bases, piece.shape[0], [gy_a])
     gy_a, gx_a = y(gy_a), x(gx_a)
     fx_b, fy_b = hold(fx_b, [gy_a, gx_a]), hold(fy_b, [gy_a, gx_a])
     keep_a, (z_a,) = fold(keep_a, [gy_a, gx_a], 1)
-    keep_b, (gy_b, gx_b) = fold(keep_b, [x(fx_b), y(fy_b)], 2, [z_a])
     over_z = (keep_a.astype(jnp.float32) + z(z_a, 1).astype(jnp.float32)).astype(jnp.bfloat16)
-    keep_b, (z_b,) = fold(keep_b, [y(gy_b), x(gx_b)], 1, [over_z])
+    keep_b, (gy_b, gx_b) = fold(keep_b, [x(fx_b), y(fy_b)], 2, [over_z])
+    keep_b, (z_b,) = fold(keep_b, [y(gy_b), x(gx_b)], 1)
     mine = keep_b.astype(jnp.float32) + z(z_b, 1).astype(jnp.float32)
-    return mine + z(over_z, 2).astype(jnp.float32), other
+    return mine + z(over_z, 2).astype(jnp.float32), cache
 
 
 def body(
@@ -550,7 +566,7 @@
     if (n_seq, n_exp) == (8, 4):
         mixture, cache = exchange_experts(piece, w_gate, w_up, w_down, n_seq, n_exp, fill_cache)
     else:
-        cache = fill_cache(piece)[1](piece)
+        cache, _ = fill_cache(piece)[1](piece)
         blocks = n_seq * n_exp
         everything = lax.all_gather(piece, everyone, axis=0, tiled=True)
         facts = everything[:, width : width + 8].astype(jnp.float32)

time: 240 us -> 243 us (1.012)
  waiting for transfers between devices: 118 us -> 124 us
  local copies, waits for them, and re-layouts: 17.2 us -> 11.9 us
  Pallas kernels: 55.4 us -> 58.1 us
    ppermute x30, waiting for transfers between devices: 81.7 us -> 87.8 us  [swap(): return lax.ppermute(a, axis, [(i, i ^ distance) for i in range(size)])]
    unnamed x41 -> x35, local copies, waits for them, and re-layouts: 14.2 us -> 8.91 us
    pallas_call x2, Pallas kernels: 29.6 us -> 32.2 us  [expert_rows(): pl.pallas_call(functools.partial(rows_kernel, local, len(waits)), out_sha...]
  transfers between devices with their start and end apart: 33 -> 33, of which waited for: 24 -> 23; matrix products, arithmetic and copies ran while one was open for 1% -> 1% of each run, Pallas kernels for 18% -> 19%
where the time goes in v10:
time: 243 us; the launch traced here: 242 us
  waiting for transfers between devices  124 us (51%)
  Pallas kernels  58.1 us (24%)
  starting transfers between devices  45.2 us (19%)
  local copies, waits for them, and re-layouts  11.9 us (5%)
    ppermute x30, waiting for transfers between devices, swap(): return lax.ppermute(a, axis, [(i, i ^ distance) for i in range(size)])  87.8 us
    pallas_call x2, Pallas kernels, expert_rows(): pl.pallas_call(functools.partial(rows_kernel, local, len(waits)), out_sha...  32.2 us
    ppermute x30, starting transfers between devices, swap(): return lax.ppermute(a, axis, [(i, i ^ distance) for i in range(size)])  30.7 us
    all_to_all x1, waiting for transfers between devices, body(): lax.all_to_all(packed, 'seq', split_axis=0, concat_axis=0, tiled=True)  25.3 us
    all_to_all x1, waiting for transfers between devices, body(): lax.all_to_all(context.reshape(n_seq, rows_dev, span), 'seq', split_axis=...  11.1 us
    unnamed x35, local copies, waits for them, and re-layouts  8.91 us
    pallas_call x2, Pallas kernels, put_rows(): pl.pallas_call(functools.partial(put_kernel, local, rows_dev, planes, len...  8.02 us
    pallas_call x2, Pallas kernels, select_rows(): pl.pallas_call(functools.partial(select_kernel, local, rows_dev, len(piec...  7.29 us
  transfers between devices with their start and end apart: 33, of which 23 were waited for; matrix products, arithmetic and copies ran while one was open for 1% of the time, Pallas kernels for 19%

profile of v10, /device:TPU:0, one launch (start us, length us, event | category | flops | bytes accessed | tf_op | source)
XLA Modules:
  0.0 241.9 jit_solution(15499955497474770599)
XLA Ops:
  0.6 2.3 fusion.3
  3.1 1.3 shard_map.122
  4.3 7.3 %all-to-all-start = ((bf16[8,64,960]{2,1,0:T(8,128)(2,1)}), bf16[8,64,960]{2,1,0:T(8,128)(2,1)S(1)}, u32[]{:S(2)}, u32[]{:S(2)}) async-start(bf16[8,64,960]{2,1,0:T(8,128)(2,1)} %shard_map.122), calls=%async_computation | async-start | bytes 2097152 | tf_op jit(solution)/shard_map/all_to_all | solution.py:543
  12.0 25.3 %all-to-all-done = bf16[8,64,960]{2,1,0:T(8,128)(2,1)S(1)} async-done(((bf16[8,64,960]{2,1,0:T(8,128)(2,1)}), bf16[8,64,960]{2,1,0:T(8,128)(2,1)S(1)}, u32[]{:S(2)}, u32[]{:S(2)}) %all-to-all-start) | async-done | bytes 983072 | tf_op jit(solution)/shard_map/all_to_all | solution.py:543
  37.3 5.6 %shard_map.123 = bf16[512,320]{1,0:T(8,128)(2,1)} custom-call(bf16[512,960]{1,0:T(8,128)(2,1)S(1)} %bitcast.22, s32[1,512]{1,0:T(1,128)S(1)} %copy-done.4, s32[512,1]{1,0:T(8,128)S(1)} %copy.40.seg_col_ref), custom_call_target="tpu_custom_call" | custom-call | flops 335544320 | bytes 1310720 | tf_op jit(solution)/shard_map/pallas_call | solution.py:56
  42.9 3.6 %all-to-all-start.1 = ((bf16[8,64,320]{2,1,0:T(8,128)(2,1)}), bf16[8,64,320]{2,1,0:T(8,128)(2,1)S(1)}, u32[]{:S(2)}, u32[]{:S(2)}) async-start(bf16[8,64,320]{2,1,0:T(8,128)(2,1)} %bitcast.5), calls=%async_computation.1 | async-start | bytes 786432 | tf_op jit(solution)/shard_map/all_to_all | solution.py:546
  47.3 11.1 %all-to-all-done.1.context_ref = bf16[8,64,320]{2,1,0:T(8,128)(2,1)S(1)} async-done(((bf16[8,64,320]{2,1,0:T(8,128)(2,1)}), bf16[8,64,320]{2,1,0:T(8,128)(2,1)S(1)}, u32[]{:S(2)}, u32[]{:S(2)}) %all-to-all-start.1) | async-done | bytes 327712 | tf_op jit(solution)/shard_map/all_to_all | solution.py:546
  60.5 1.7 collective-permute-start.1
  62.2 1.5 collective-permute-start
  63.8 8.2 %collective-permute-done.3.refs_4_ = bf16[64,2432]{1,0:T(8,128)(2,1)S(1)} collective-permute-done((bf16[64,2432]{1,0:T(8,128)(2,1)S(1)}, bf16[64,2432]{1,0:T(8,128)(2,1)S(1)}, u32[]{:S(2)}, u32[]{:S(2)}) %collective-permute-start.3) | collective-permute-done | bytes 311328 | tf_op jit(solution)/shard_map/ppermute | solution.py:432
  72.0 1.5 collective-permute-start.5
  73.5 2.9 %collective-permute-start.4 = (bf16[64,2432]{1,0:T(8,128)(2,1)S(1)}, bf16[64,2432]{1,0:T(8,128)(2,1)S(1)}, u32[]{:S(2)}, u32[]{:S(2)}) collective-permute-start(bf16[64,2432]{1,0:T(8,128)(2,1)S(1)} %collective-permute-done.3.refs_4_), channel_id=1, source_target_pairs={{0,4},{4,0},{8,12},{12,8},{16,20},{20,16},{24,28},{28,24},{1,5},{5... | collective-permute-start | bytes 933896 | tf_op jit(solution)/shard_map/ppermute | solution.py:432
  77.2 2.4 collective-permute-done.5.refs_6_.refs_3_
  79.5 3.1 %collective-permute-done.4.refs_5_.refs_4_ = bf16[64,2432]{1,0:T(8,128)(2,1)S(1)} collective-permute-done((bf16[64,2432]{1,0:T(8,128)(2,1)S(1)}, bf16[64,2432]{1,0:T(8,128)(2,1)S(1)}, u32[]{:S(2)}, u32[]{:S(2)}) %collective-permute-start.4) | collective-permute-done | bytes 311328 | tf_op jit(solution)/shard_map/ppermute | solution.py:432
  83.1 1.7 collective-permute-start.10
  84.9 5.1 %collective-permute-done.9.refs_2_.refs_1_ = bf16[64,2432]{1,0:T(8,128)(2,1)S(1)} collective-permute-done((bf16[64,2432]{1,0:T(8,128)(2,1)S(1)}, bf16[64,2432]{1,0:T(8,128)(2,1)S(1)}, u32[]{:S(2)}, u32[]{:S(2)}) %collective-permute-start.9) | collective-permute-done | bytes 311328 | tf_op jit(solution)/shard_map/ppermute | solution.py:432
  90.3 1.6 collective-permute-done.12.refs_0_
  92.6 1.5 collective-permute-start.14
  94.9 7.0 %collective-permute-done.14.refs_6_ = bf16[64,2432]{1,0:T(8,128)(2,1)} collective-permute-done((bf16[64,2432]{1,0:T(8,128)(2,1)}, bf16[64,2432]{1,0:T(8,128)(2,1)}, u32[]{:S(2)}, u32[]{:S(2)}) %collective-permute-start.14) | collective-permute-done | bytes 311328 | tf_op jit(solution)/shard_map/ppermute | solution.py:432
  102.5 2.8 %collective-permute-done.11.refs_3_ = bf16[64,2432]{1,0:T(8,128)(2,1)} collective-permute-done((bf16[64,2432]{1,0:T(8,128)(2,1)}, bf16[64,2432]{1,0:T(8,128)(2,1)}, u32[]{:S(2)}, u32[]{:S(2)}) %collective-permute-start.11) | collective-permute-done | bytes 311328 | tf_op jit(solution)/shard_map/ppermute | solution.py:432
  105.3 3.9 %collective-permute-done.15.refs_7_ = bf16[64,2432]{1,0:T(8,128)(2,1)} collective-permute-done((bf16[64,2432]{1,0:T(8,128)(2,1)}, bf16[64,2432]{1,0:T(8,128)(2,1)}, u32[]{:S(2)}, u32[]{:S(2)}) %collective-permute-start.15) | collective-permute-done | bytes 311328 | tf_op jit(solution)/shard_map/ppermute | solution.py:432
  110.1 4.1 %shard_map.129 = (bf16[2,192,2304]{2,1,0:T(8,128)(2,1)S(1)}, bf16[2,192,2304]{2,1,0:T(8,128)(2,1)}, bf16[512,128]{1,0:T(8,128)(2,1)S(1)}) custom-call(s32[2]{0:T(128)S(1)} %add_multiply_fusion.bases_ref, bf16[64,2432]{1,0:T(8,128)(2,1)S(1)} %shard_map.127.refs_0_, bf16[64,2432]{1,0:T(8,128)(2,1)S(1)} %copy-done.1, ...), custom_call_target="tpu_custom_call" | custom-call | flops 905969664 | bytes 6029312 | tf_op jit(solution)/shard_map/pallas_call | solution.py:300
  114.2 1.2 copy-done.9
  115.5 1.5 collective-permute-start.2
  117.5 7.7 %collective-permute-done.2.refs_3_ = bf16[64,2432]{1,0:T(8,128)(2,1)S(1)} collective-permute-done((bf16[64,2432]{1,0:T(8,128)(2,1)S(1)}, bf16[64,2432]{1,0:T(8,128)(2,1)S(1)}, u32[]{:S(2)}, u32[]{:S(2)}) %collective-permute-start.2) | collective-permute-done | bytes 311328 | tf_op jit(solution)/shard_map/ppermute | solution.py:432
  127.4 3.2 %shard_map.125 = (bf16[2,192,2304]{2,1,0:T(8,128)(2,1)S(1)}, bf16[2,192,2304]{2,1,0:T(8,128)(2,1)}, bf16[512,128]{1,0:T(8,128)(2,1)S(1)}) custom-call(s32[2]{0:T(128)S(1)} %add_multiply_fusion.bases_ref, bf16[64,2432]{1,0:T(8,128)(2,1)S(1)} %copy-done.6, bf16[64,2432]{1,0:T(8,128)(2,1)S(1)} %collective-permute-done.refs_1_.refs_2_, ...), custom_call_target="tpu_custom_call" | custom-call | flops 905969664 | bytes 6029312 | tf_op jit(solution)/shard_map/pallas_call | solution.py:300
  130.6 1.2 copy-done.11
  131.9 1.6 shard_map.126.rest_1_
  133.5 3.7 %all-to-all-start.2 = ((bf16[8,64,640]{2,1,0:T(8,128)(2,1)}), bf16[8,64,640]{2,1,0:T(8,128)(2,1)S(1)}, u32[]{:S(2)}, u32[]{:S(2)}) async-start(bf16[8,64,640]{2,1,0:T(8,128)(2,1)} %shard_map.126.rest_1_), calls=%async_computation.2 | async-start | bytes 1310720 | tf_op jit(solution)/shard_map/all_to_all | solution.py:563
  137.3 1.5 copy-done.10
  138.8 16.6 %shard_map.130 = (bf16[2,192,2304]{2,1,0:T(8,128)(2,1)S(1)}, bf16[2,192,2304]{2,1,0:T(8,128)(2,1)}, f32[8,128]{1,0:T(8,128)S(1)}) custom-call(bf16[2,192,2304]{2,1,0:T(8,128)(2,1)S(1)} %copy-done.10, bf16[2,192,2304]{2,1,0:T(8,128)(2,1)} %collective-permute-done.16.got_ref, bf16[2,720,2304]{2,1,0:T(8,128)(2,1)} %bitcast.28, bf16[2,720,2304]{2,1,0:T(8,128)(2,1)} %bitcast.30, ...), custom_call_target="tpu_custom_call" | custom-call | flops 7644119040 | bytes 26984448 | tf_op jit(solution)/shard_map/pallas_call | solution.py:352
  157.0 1.5 copy-done.12
  158.4 15.6 %shard_map.132 = (bf16[2,192,2304]{2,1,0:T(8,128)(2,1)S(1)}, bf16[2,192,2304]{2,1,0:T(8,128)(2,1)S(1)}, f32[8,128]{1,0:T(8,128)S(1)}) custom-call(bf16[2,192,2304]{2,1,0:T(8,128)(2,1)S(1)} %copy-done.12, bf16[2,192,2304]{2,1,0:T(8,128)(2,1)} %collective-permute-done.7.got_ref, bf16[2,720,2304]{2,1,0:T(8,128)(2,1)} %bitcast.29, ...), custom_call_target="tpu_custom_call" | custom-call | flops 7644119040 | bytes 26984448 | tf_op jit(solution)/shard_map/pallas_call | solution.py:352
  174.1 4.5 %shard_map.133 = (bf16[256,2304]{1,0:T(8,128)(2,1)S(1)}, bf16[128,2304]{1,0:T(8,128)(2,1)S(1)}, bf16[128,2304]{1,0:T(8,128)(2,1)S(1)}) custom-call(s32[2]{0:T(128)S(1)} %add_multiply_fusion.bases_ref, bf16[2,192,2304]{2,1,0:T(8,128)(2,1)S(1)} %get-tuple-element.45.y_own_ref, bf16[2,192,2304]{2,1,0:T(8,128)(2,1)} %collective-permute-done.18.y_got_ref, ...), custom_call_target="tpu_custom_call" | custom-call | flops 905969664 | bytes 18874368 | tf_op jit(solution)/shard_map/pallas_call | solution.py:415
  178.6 1.8 collective-permute-start.19
  180.9 13.5 %collective-permute-done.19.rest_0_ = bf16[128,2304]{1,0:T(8,128)(2,1)S(1)} collective-permute-done((bf16[128,2304]{1,0:T(8,128)(2,1)S(1)}, bf16[128,2304]{1,0:T(8,128)(2,1)S(1)}, u32[]{:S(2)}, u32[]{:S(2)}) %collective-permute-start.19) | collective-permute-done | bytes 589856 | tf_op jit(solution)/shard_map/ppermute | solution.py:432
  197.0 6.9 %collective-permute-done.21.refs_1_.rest_0_ = bf16[64,2304]{1,0:T(8,128)(2,1)S(1)} collective-permute-done((bf16[64,2304]{1,0:T(8,128)(2,1)S(1)}, bf16[64,2304]{1,0:T(8,128)(2,1)S(1)}, u32[]{:S(2)}, u32[]{:S(2)}) %collective-permute-start.21) | collective-permute-done | bytes 294944 | tf_op jit(solution)/shard_map/ppermute | solution.py:432
  204.3 1.5 collective-permute-start.25
  205.9 3.6 %shard_map.135 = (bf16[256,2304]{1,0:T(8,128)(2,1)S(1)}, bf16[128,2304]{1,0:T(8,128)(2,1)S(1)}, bf16[128,2304]{1,0:T(8,128)(2,1)S(1)}) custom-call(s32[2]{0:T(128)S(1)} %add_multiply_fusion.bases_ref, bf16[2,192,2304]{2,1,0:T(8,128)(2,1)S(1)} %get-tuple-element.43.y_own_ref, bf16[2,192,2304]{2,1,0:T(8,128)(2,1)S(1)} %collective-permute-done.17.y_got_ref, ...), custom_call_target="tpu_custom_call" | custom-call | flops 905969664 | bytes 18874368 | tf_op jit(solution)/shard_map/pallas_call | solution.py:415
  210.1 1.5 collective-permute-start.24
  211.7 10.7 %collective-permute-done.23.rest_0_ = bf16[128,2304]{1,0:T(8,128)(2,1)S(1)} collective-permute-done((bf16[128,2304]{1,0:T(8,128)(2,1)S(1)}, bf16[128,2304]{1,0:T(8,128)(2,1)S(1)}, u32[]{:S(2)}, u32[]{:S(2)}) %collective-permute-start.23) | collective-permute-done | bytes 589856 | tf_op jit(solution)/shard_map/ppermute | solution.py:432
  223.6 1.5 collective-permute-start.26
  225.1 1.4 collective-permute-start.27
  226.5 2.4 collective-permute-start.29
  228.9 1.4 collective-permute-done.26.rest_0_
  230.3 1.5 collective-permute-done.27.rest_1_
  232.8 5.1 %collective-permute-done.29 = bf16[64,2304]{1,0:T(8,128)(2,1)S(1)} collective-permute-done((bf16[64,2304]{1,0:T(8,128)(2,1)S(1)}, bf16[64,2304]{1,0:T(8,128)(2,1)S(1)}, u32[]{:S(2)}, u32[]{:S(2)}) %collective-permute-start.29) | collective-permute-done | bytes 294944 | tf_op jit(solution)/shard_map/ppermute | solution.py:432
  238.0 3.1 %collective-permute-done.28 = bf16[64,2304]{1,0:T(8,128)(2,1)S(1)} collective-permute-done((bf16[64,2304]{1,0:T(8,128)(2,1)S(1)}, bf16[64,2304]{1,0:T(8,128)(2,1)S(1)}, u32[]{:S(2)}, u32[]{:S(2)}) %collective-permute-start.28) | collective-permute-done | bytes 294944 | tf_op jit(solution)/shard_map/ppermute | solution.py:432
  (90 shorter events, 19.8 us)
Async XLA Ops:
  0.6 2.4 copy-start.3
  3.0 8.6 %copy-start.4 = (s32[1,512]{1,0:T(1,128)S(1)}, s32[1,512]{1,0:T(1,128)}, u32[]{:S(2)}) copy-start(s32[1,512]{1,0:T(1,128)} %seg_row_ref.1) | copy-start | bytes 6148
  3.0 8.7 %copy-start.13 = (bf16[2304]{0:T(1024)(128)(2,1)S(1)}, bf16[2304]{0:T(1024)(128)(2,1)}, u32[]{:S(2)}) copy-start(bf16[2304]{0:T(1024)(128)(2,1)} %param.14) | copy-start | bytes 13828
  3.1 8.7 %copy-start.14 = (s32[1,64,2]{1,2,0:T(2,128)S(1)}, s32[1,64,2]{1,2,0:T(2,128)}, u32[]{:S(2)}) copy-start(s32[1,64,2]{1,2,0:T(2,128)} %param.16) | copy-start | bytes 1540
  4.3 33.0 %all-to-all-start = ((bf16[8,64,960]{2,1,0:T(8,128)(2,1)}), bf16[8,64,960]{2,1,0:T(8,128)(2,1)S(1)}, u32[]{:S(2)}, u32[]{:S(2)}) async-start(bf16[8,64,960]{2,1,0:T(8,128)(2,1)} %shard_map.122), calls=%async_computation | async-start | bytes 2097152 | tf_op jit(solution)/shard_map/all_to_all | solution.py:543
  37.3 9.9 %copy-start.15 = (f32[1,64,2]{1,2,0:T(2,128)S(1)}, f32[1,64,2]{1,2,0:T(2,128)}, u32[]{:S(2)}) copy-start(f32[1,64,2]{1,2,0:T(2,128)} %param.17) | copy-start | bytes 1540
  37.3 21.1 %copy-start.2 = (bf16[1,64,2304]{2,1,0:T(8,128)(2,1)S(1)}, bf16[1,64,2304]{2,1,0:T(8,128)(2,1)}, u32[]{:S(2)}) copy-start(bf16[1,64,2304]{2,1,0:T(8,128)(2,1)} %param.13) | copy-start | bytes 884740
  42.9 15.5 %all-to-all-start.1 = ((bf16[8,64,320]{2,1,0:T(8,128)(2,1)}), bf16[8,64,320]{2,1,0:T(8,128)(2,1)S(1)}, u32[]{:S(2)}, u32[]{:S(2)}) async-start(bf16[8,64,320]{2,1,0:T(8,128)(2,1)} %bitcast.5), calls=%async_computation.1 | async-start | bytes 786432 | tf_op jit(solution)/shard_map/all_to_all | solution.py:546
  58.7 33.2 %copy-start.5 = (bf16[64,2432]{1,0:T(8,128)(2,1)}, bf16[64,2432]{1,0:T(8,128)(2,1)S(1)}, u32[]{:S(2)}) copy-start(bf16[64,2432]{1,0:T(8,128)(2,1)S(1)} %get-tuple-element.35.refs_0_) | copy-start | bytes 933892
  58.7 13.3 %collective-permute-start.3 = (bf16[64,2432]{1,0:T(8,128)(2,1)S(1)}, bf16[64,2432]{1,0:T(8,128)(2,1)S(1)}, u32[]{:S(2)}, u32[]{:S(2)}) collective-permute-start(bf16[64,2432]{1,0:T(8,128)(2,1)S(1)} %get-tuple-element.35.refs_0_), channel_id=1, source_target_pairs={{0,8},{4,12},{8,0},{12,4},{16,24},{20,28},{24,16},{28,20},{1,9},{5... | collective-permute-start | bytes 933896 | tf_op jit(solution)/shard_map/ppermute | solution.py:432
  59.7 17.5 %collective-permute-start.8 = (bf16[64,2432]{1,0:T(8,128)(2,1)S(1)}, bf16[64,2432]{1,0:T(8,128)(2,1)S(1)}, u32[]{:S(2)}, u32[]{:S(2)}) collective-permute-start(bf16[64,2432]{1,0:T(8,128)(2,1)S(1)} %get-tuple-element.35.refs_0_), channel_id=1, source_target_pairs={{0,16},{4,20},{8,24},{12,28},{16,0},{20,4},{24,8},{28,12},{1,17},{... | collective-permute-start | bytes 933896 | tf_op jit(solution)/shard_map/ppermute | solution.py:432
  60.5 16.6 %collective-permute-start.1 = (bf16[64,2432]{1,0:T(8,128)(2,1)S(1)}, bf16[64,2432]{1,0:T(8,128)(2,1)S(1)}, u32[]{:S(2)}, u32[]{:S(2)}) collective-permute-start(bf16[64,2432]{1,0:T(8,128)(2,1)S(1)} %get-tuple-element.35.refs_0_), channel_id=1, source_target_pairs={{0,4},{4,0},{8,12},{12,8},{16,20},{20,16},{24,28},{28,24},{1,5},{5... | collective-permute-start | bytes 933896 | tf_op jit(solution)/shard_map/ppermute | solution.py:432
  62.2 14.9 %collective-permute-start = (bf16[64,2432]{1,0:T(8,128)(2,1)S(1)}, bf16[64,2432]{1,0:T(8,128)(2,1)S(1)}, u32[]{:S(2)}, u32[]{:S(2)}) collective-permute-start(bf16[64,2432]{1,0:T(8,128)(2,1)S(1)} %get-tuple-element.35.refs_0_), channel_id=1, source_target_pairs={{0,2},{1,3},{2,0},{3,1},{4,6},{5,7},{6,4},{7,5},{8,10},{9,11},{10,... | collective-permute-start | bytes 933896 | tf_op jit(solution)/shard_map/ppermute | solution.py:432
  72.0 7.6 %collective-permute-start.5 = (bf16[64,2432]{1,0:T(8,128)(2,1)S(1)}, bf16[64,2432]{1,0:T(8,128)(2,1)S(1)}, u32[]{:S(2)}, u32[]{:S(2)}) collective-permute-start(bf16[64,2432]{1,0:T(8,128)(2,1)S(1)} %collective-permute-done.3.refs_4_), channel_id=1, source_target_pairs={{0,2},{1,3},{2,0},{3,1},{4,6},{5,7},{6,4},{7,5},{8,10},{9,11},{10,... | collective-permute-start | bytes 933896 | tf_op jit(solution)/shard_map/ppermute | solution.py:432
  73.5 9.1 %collective-permute-start.4 = (bf16[64,2432]{1,0:T(8,128)(2,1)S(1)}, bf16[64,2432]{1,0:T(8,128)(2,1)S(1)}, u32[]{:S(2)}, u32[]{:S(2)}) collective-permute-start(bf16[64,2432]{1,0:T(8,128)(2,1)S(1)} %collective-permute-done.3.refs_4_), channel_id=1, source_target_pairs={{0,4},{4,0},{8,12},{12,8},{16,20},{20,16},{24,28},{28,24},{1,5},{5... | collective-permute-start | bytes 933896 | tf_op jit(solution)/shard_map/ppermute | solution.py:432
  82.6 7.3 %collective-permute-start.9 = (bf16[64,2432]{1,0:T(8,128)(2,1)S(1)}, bf16[64,2432]{1,0:T(8,128)(2,1)S(1)}, u32[]{:S(2)}, u32[]{:S(2)}) collective-permute-start(bf16[64,2432]{1,0:T(8,128)(2,1)S(1)} %shard_map.127.refs_0_), channel_id=1, source_target_pairs={{0,2},{1,3},{2,0},{3,1},{4,6},{5,7},{6,4},{7,5},{8,10},{9,11},{10,... | collective-permute-start | bytes 933896 | tf_op jit(solution)/shard_map/ppermute | solution.py:432
  83.1 7.1 %collective-permute-start.10 = (bf16[64,2432]{1,0:T(8,128)(2,1)S(1)}, bf16[64,2432]{1,0:T(8,128)(2,1)}, u32[]{:S(2)}, u32[]{:S(2)}) collective-permute-start(bf16[64,2432]{1,0:T(8,128)(2,1)S(1)} %shard_map.127.refs_0_), channel_id=1, source_target_pairs={{0,4},{4,0},{8,12},{12,8},{16,20},{20,16},{24,28},{28,24},{1,5},{5... | collective-permute-start | bytes 933896 | tf_op jit(solution)/shard_map/ppermute | solution.py:432
  84.9 7.0 %collective-permute-start.12 = (bf16[64,2432]{1,0:T(8,128)(2,1)S(1)}, bf16[64,2432]{1,0:T(8,128)(2,1)}, u32[]{:S(2)}, u32[]{:S(2)}) collective-permute-start(bf16[64,2432]{1,0:T(8,128)(2,1)S(1)} %shard_map.127.refs_0_), channel_id=1, source_target_pairs={{0,8},{4,12},{8,0},{12,4},{16,24},{20,28},{24,16},{28,20},{1,9},{5... | collective-permute-start | bytes 933896 | tf_op jit(solution)/shard_map/ppermute | solution.py:432
  92.6 9.3 %collective-permute-start.14 = (bf16[64,2432]{1,0:T(8,128)(2,1)}, bf16[64,2432]{1,0:T(8,128)(2,1)}, u32[]{:S(2)}, u32[]{:S(2)}) collective-permute-start(bf16[64,2432]{1,0:T(8,128)(2,1)} %shard_map.128.refs_4_), channel_id=1, source_target_pairs={{0,2},{1,3},{2,0},{3,1},{4,6},{5,7},{6,4},{7,5},{8,10},{9,11},{10,... | collective-permute-start | bytes 933896 | tf_op jit(solution)/shard_map/ppermute | solution.py:432
  94.1 11.1 %collective-permute-start.13 = (bf16[64,2432]{1,0:T(8,128)(2,1)}, bf16[64,2432]{1,0:T(8,128)(2,1)}, u32[]{:S(2)}, u32[]{:S(2)}) collective-permute-start(bf16[64,2432]{1,0:T(8,128)(2,1)} %shard_map.128.refs_4_), channel_id=1, source_target_pairs={{0,4},{4,0},{8,12},{12,8},{16,20},{20,16},{24,28},{28,24},{1,5},{5... | collective-permute-start | bytes 933896 | tf_op jit(solution)/shard_map/ppermute | solution.py:432
  94.4 10.9 %collective-permute-start.11 = (bf16[64,2432]{1,0:T(8,128)(2,1)}, bf16[64,2432]{1,0:T(8,128)(2,1)}, u32[]{:S(2)}, u32[]{:S(2)}) collective-permute-start(bf16[64,2432]{1,0:T(8,128)(2,1)} %collective-permute-done.10.refs_1_.refs_2_), channel_id=1, source_target_pairs={{0,2},{1,3},{2,0},{3,1},{4,6},{5,7},{6,4},{7,5},{8,10},{9,11},{10,... | collective-permute-start | bytes 933896 | tf_op jit(solution)/shard_map/ppermute | solution.py:432
  101.9 7.2 %collective-permute-start.15 = (bf16[64,2432]{1,0:T(8,128)(2,1)}, bf16[64,2432]{1,0:T(8,128)(2,1)}, u32[]{:S(2)}, u32[]{:S(2)}) collective-permute-start(bf16[64,2432]{1,0:T(8,128)(2,1)} %collective-permute-done.14.refs_6_), channel_id=1, source_target_pairs={{0,4},{4,0},{8,12},{12,8},{16,20},{20,16},{24,28},{28,24},{1,5},{5... | collective-permute-start | bytes 933896 | tf_op jit(solution)/shard_map/ppermute | solution.py:432
  109.1 1.0 copy-start.1
  110.1 16.3 %copy-start.6 = (bf16[64,2432]{1,0:T(8,128)(2,1)S(1)}, bf16[64,2432]{1,0:T(8,128)(2,1)}, u32[]{:S(2)}) copy-start(bf16[64,2432]{1,0:T(8,128)(2,1)} %copy-done.5) | copy-start | bytes 933892
  114.2 1.2 copy-start.9
  115.5 16.3 %copy-start.16 = (s32[1,32]{1,0:T(1,128)S(1)}, s32[1,32]{1,0:T(1,128)}, u32[]{:S(2)}) copy-start(s32[1,32]{1,0:T(1,128)} %param.18) | copy-start | bytes 388
  115.5 21.8 %collective-permute-start.16 = (bf16[2,192,2304]{2,1,0:T(8,128)(2,1)}, bf16[2,192,2304]{2,1,0:T(8,128)(2,1)}, u32[]{:S(2)}, u32[]{:S(2)}) collective-permute-start(bf16[2,192,2304]{2,1,0:T(8,128)(2,1)} %get-tuple-element.40), channel_id=1, source_target_pairs={{0,1},{1,0},{2,3},{3,2},{4,5},{5,4},{6,7},{7,6},{8,9},{9,8},{10,11... | collective-permute-start | bytes 5308424 | tf_op jit(solution)/shard_map/ppermute | solution.py:432
  115.5 9.8 %collective-permute-start.2 = (bf16[64,2432]{1,0:T(8,128)(2,1)S(1)}, bf16[64,2432]{1,0:T(8,128)(2,1)S(1)}, u32[]{:S(2)}, u32[]{:S(2)}) collective-permute-start(bf16[64,2432]{1,0:T(8,128)(2,1)S(1)} %collective-permute-done.1.refs_2_.refs_1_), channel_id=1, source_target_pairs={{0,2},{1,3},{2,0},{3,1},{4,6},{5,7},{6,4},{7,5},{8,10},{9,11},{10,... | collective-permute-start | bytes 933896 | tf_op jit(solution)/shard_map/ppermute | solution.py:432
  116.9 9.5 %collective-permute-start.6 = (bf16[64,2432]{1,0:T(8,128)(2,1)S(1)}, bf16[64,2432]{1,0:T(8,128)(2,1)S(1)}, u32[]{:S(2)}, u32[]{:S(2)}) collective-permute-start(bf16[64,2432]{1,0:T(8,128)(2,1)S(1)} %collective-permute-done.5.refs_6_.refs_3_), channel_id=1, source_target_pairs={{0,4},{4,0},{8,12},{12,8},{16,20},{20,16},{24,28},{28,24},{1,5},{5... | collective-permute-start | bytes 933896 | tf_op jit(solution)/shard_map/ppermute | solution.py:432
  126.4 1.0 copy-start.8
  130.5 1.2 copy-start.11
  131.8 25.2 %collective-permute-start.7 = (bf16[2,192,2304]{2,1,0:T(8,128)(2,1)}, bf16[2,192,2304]{2,1,0:T(8,128)(2,1)}, u32[]{:S(2)}, u32[]{:S(2)}) collective-permute-start(bf16[2,192,2304]{2,1,0:T(8,128)(2,1)} %get-tuple-element.37), channel_id=1, source_target_pairs={{0,1},{1,0},{2,3},{3,2},{4,5},{5,4},{6,7},{7,6},{8,9},{9,8},{10,11... | collective-permute-start | bytes 5308424 | tf_op jit(solution)/shard_map/ppermute | solution.py:432
  133.5 22.4 %all-to-all-start.2 = ((bf16[8,64,640]{2,1,0:T(8,128)(2,1)}), bf16[8,64,640]{2,1,0:T(8,128)(2,1)S(1)}, u32[]{:S(2)}, u32[]{:S(2)}) async-start(bf16[8,64,640]{2,1,0:T(8,128)(2,1)} %shard_map.126.rest_1_), calls=%async_computation.2 | async-start | bytes 1310720 | tf_op jit(solution)/shard_map/all_to_all | solution.py:563
  137.3 1.5 copy-start.10
  155.4 18.7 %collective-permute-start.18 = (bf16[2,192,2304]{2,1,0:T(8,128)(2,1)}, bf16[2,192,2304]{2,1,0:T(8,128)(2,1)}, u32[]{:S(2)}, u32[]{:S(2)}) collective-permute-start(bf16[2,192,2304]{2,1,0:T(8,128)(2,1)} %get-tuple-element.46), channel_id=1, source_target_pairs={{0,1},{1,0},{2,3},{3,2},{4,5},{5,4},{6,7},{7,6},{8,9},{9,8},{10,11... | collective-permute-start | bytes 5308424 | tf_op jit(solution)/shard_map/ppermute | solution.py:432
  157.0 1.5 copy-start.12
  174.0 31.8 %collective-permute-start.17 = (bf16[2,192,2304]{2,1,0:T(8,128)(2,1)S(1)}, bf16[2,192,2304]{2,1,0:T(8,128)(2,1)S(1)}, u32[]{:S(2)}, u32[]{:S(2)}) collective-permute-start(bf16[2,192,2304]{2,1,0:T(8,128)(2,1)S(1)} %get-tuple-element.44), channel_id=1, source_target_pairs={{0,1},{1,0},{2,3},{3,2},{4,5},{5,4},{6,7},{7,6},{8,9},{9,8},{10,11... | collective-permute-start | bytes 5308424 | tf_op jit(solution)/shard_map/ppermute | solution.py:432
  178.6 15.8 %collective-permute-start.19 = (bf16[128,2304]{1,0:T(8,128)(2,1)S(1)}, bf16[128,2304]{1,0:T(8,128)(2,1)S(1)}, u32[]{:S(2)}, u32[]{:S(2)}) collective-permute-start(bf16[128,2304]{1,0:T(8,128)(2,1)S(1)} %get-tuple-element.50), channel_id=1, source_target_pairs={{0,4},{4,0},{8,12},{12,8},{16,20},{20,16},{24,28},{28,24},{1,5},{5... | collective-permute-start | bytes 1769480 | tf_op jit(solution)/shard_map/ppermute | solution.py:432
  180.4 15.2 %collective-permute-start.20 = (bf16[128,2304]{1,0:T(8,128)(2,1)S(1)}, bf16[128,2304]{1,0:T(8,128)(2,1)S(1)}, u32[]{:S(2)}, u32[]{:S(2)}) collective-permute-start(bf16[128,2304]{1,0:T(8,128)(2,1)S(1)} %get-tuple-element.51), channel_id=1, source_target_pairs={{0,2},{1,3},{2,0},{3,1},{4,6},{5,7},{6,4},{7,5},{8,10},{9,11},{10,... | collective-permute-start | bytes 1769480 | tf_op jit(solution)/shard_map/ppermute | solution.py:432
  195.8 8.1 %collective-permute-start.21 = (bf16[64,2304]{1,0:T(8,128)(2,1)S(1)}, bf16[64,2304]{1,0:T(8,128)(2,1)S(1)}, u32[]{:S(2)}, u32[]{:S(2)}) collective-permute-start(bf16[64,2304]{1,0:T(8,128)(2,1)S(1)} %get-tuple-element.52.rest_0_), channel_id=1, source_target_pairs={{0,2},{1,3},{2,0},{3,1},{4,6},{5,7},{6,4},{7,5},{8,10},{9,11},{10,... | collective-permute-start | bytes 884744 | tf_op jit(solution)/shard_map/ppermute | solution.py:432
  196.5 7.7 %collective-permute-start.22 = (bf16[64,2304]{1,0:T(8,128)(2,1)S(1)}, bf16[64,2304]{1,0:T(8,128)(2,1)S(1)}, u32[]{:S(2)}, u32[]{:S(2)}) collective-permute-start(bf16[64,2304]{1,0:T(8,128)(2,1)S(1)} %get-tuple-element.55), channel_id=1, source_target_pairs={{0,4},{4,0},{8,12},{12,8},{16,20},{20,16},{24,28},{28,24},{1,5},{5... | collective-permute-start | bytes 884744 | tf_op jit(solution)/shard_map/ppermute | solution.py:432
  204.3 7.3 %collective-permute-start.25 = (bf16[64,2304]{1,0:T(8,128)(2,1)S(1)}, bf16[64,2304]{1,0:T(8,128)(2,1)S(1)}, u32[]{:S(2)}, u32[]{:S(2)}) collective-permute-start(bf16[64,2304]{1,0:T(8,128)(2,1)S(1)} %get-tuple-element.59), channel_id=1, source_target_pairs={{0,8},{4,12},{8,0},{12,4},{16,24},{20,28},{24,16},{28,20},{1,9},{5... | collective-permute-start | bytes 884744 | tf_op jit(solution)/shard_map/ppermute | solution.py:432
  209.5 12.9 %collective-permute-start.23 = (bf16[128,2304]{1,0:T(8,128)(2,1)S(1)}, bf16[128,2304]{1,0:T(8,128)(2,1)S(1)}, u32[]{:S(2)}, u32[]{:S(2)}) collective-permute-start(bf16[128,2304]{1,0:T(8,128)(2,1)S(1)} %shard_map.136), channel_id=1, source_target_pairs={{0,4},{4,0},{8,12},{12,8},{16,20},{20,16},{24,28},{28,24},{1,5},{5... | collective-permute-start | bytes 1769480 | tf_op jit(solution)/shard_map/ppermute | solution.py:432
  210.1 13.2 %collective-permute-start.24 = (bf16[128,2304]{1,0:T(8,128)(2,1)S(1)}, bf16[128,2304]{1,0:T(8,128)(2,1)S(1)}, u32[]{:S(2)}, u32[]{:S(2)}) collective-permute-start(bf16[128,2304]{1,0:T(8,128)(2,1)S(1)} %shard_map.137), channel_id=1, source_target_pairs={{0,2},{1,3},{2,0},{3,1},{4,6},{5,7},{6,4},{7,5},{8,10},{9,11},{10,... | collective-permute-start | bytes 1769480 | tf_op jit(solution)/shard_map/ppermute | solution.py:432
  223.6 6.8 %collective-permute-start.26 = (bf16[64,2304]{1,0:T(8,128)(2,1)S(1)}, bf16[64,2304]{1,0:T(8,128)(2,1)S(1)}, u32[]{:S(2)}, u32[]{:S(2)}) collective-permute-start(bf16[64,2304]{1,0:T(8,128)(2,1)S(1)} %get-tuple-element.61), channel_id=1, source_target_pairs={{0,2},{1,3},{2,0},{3,1},{4,6},{5,7},{6,4},{7,5},{8,10},{9,11},{10,... | collective-permute-start | bytes 884744 | tf_op jit(solution)/shard_map/ppermute | solution.py:432
  225.1 6.7 %collective-permute-start.27 = (bf16[64,2304]{1,0:T(8,128)(2,1)S(1)}, bf16[64,2304]{1,0:T(8,128)(2,1)S(1)}, u32[]{:S(2)}, u32[]{:S(2)}) collective-permute-start(bf16[64,2304]{1,0:T(8,128)(2,1)S(1)} %get-tuple-element.62), channel_id=1, source_target_pairs={{0,4},{4,0},{8,12},{12,8},{16,20},{20,16},{24,28},{28,24},{1,5},{5... | collective-permute-start | bytes 884744 | tf_op jit(solution)/shard_map/ppermute | solution.py:432
  226.5 11.5 %collective-permute-start.29 = (bf16[64,2304]{1,0:T(8,128)(2,1)S(1)}, bf16[64,2304]{1,0:T(8,128)(2,1)S(1)}, u32[]{:S(2)}, u32[]{:S(2)}) collective-permute-start(bf16[64,2304]{1,0:T(8,128)(2,1)S(1)} %add_convert_fusion.1.rest_2_), channel_id=1, source_target_pairs={{0,16},{4,20},{8,24},{12,28},{16,0},{20,4},{24,8},{28,12},{1,17},{... | collective-permute-start | bytes 884744 | tf_op jit(solution)/shard_map/ppermute | solution.py:432
  232.0 9.1 %collective-permute-start.28 = (bf16[64,2304]{1,0:T(8,128)(2,1)S(1)}, bf16[64,2304]{1,0:T(8,128)(2,1)S(1)}, u32[]{:S(2)}, u32[]{:S(2)}) collective-permute-start(bf16[64,2304]{1,0:T(8,128)(2,1)S(1)} %get-tuple-element.64), channel_id=1, source_target_pairs={{0,8},{4,12},{8,0},{12,4},{16,24},{20,28},{24,16},{28,20},{1,9},{5... | collective-permute-start | bytes 884744 | tf_op jit(solution)/shard_map/ppermute | solution.py:432
  (2 other events, 1.5 us)

commit v11 on v10

--- a/solution.py
+++ b/solution.py
@@ -269,8 +269,9 @@
 
 
 def select_kernel(local, rows_dev, count, bases_ref, *refs):
-    piece_refs, (own_ref, sib_ref, facts_ref) = refs[:count], refs[-3:]
+    piece_refs, (own_hbm, sib_ref, facts_ref, own_ref, own_sem) = refs[:count], refs[-5:]
     width = own_ref.shape[2]
+    own_copies = []
     tokens, rows = 4 * rows_dev, 4 * CAP
     shift = lax.broadcasted_iota(jnp.int32, (1, tokens), 1) // rows_dev * CAP
     row_id = lax.broadcasted_iota(jnp.int32, (rows, tokens), 0)
@@ -289,6 +290,13 @@
         for e in range(local):
             own_ref[e, g * rows : (g + 1) * rows, :] = chosen[e * rows : (e + 1) * rows]
             sib_ref[e, g * rows : (g + 1) * rows, :] = chosen[(local + e) * rows : (local + e + 1) * rows]
+        for e in range(local):
+            here = (e, pl.ds(g * rows, rows), slice(None))
+            copy = pltpu.make_async_copy(own_ref.at[here], own_hbm.at[here], own_sem.at[g * local + e])
+            copy.start()
+            own_copies.append(copy)
+    for copy in own_copies:
+        copy.wait()
 
 
 def select_rows(pieces, bases, local, waits=()):
@@ -303,7 +311,11 @@
         in_specs=[pl.BlockSpec(memory_space=pltpu.SMEM)]
         + [vmem] * len(pieces)
         + [pl.BlockSpec(memory_space=pl.ANY)] * len(waits),
-        out_specs=(vmem, vmem, vmem),
+        out_specs=(pl.BlockSpec(memory_space=pl.ANY), vmem, vmem),
+        scratch_shapes=[
+            pltpu.VMEM(out.shape, jnp.bfloat16),
+            pltpu.SemaphoreType.DMA((len(pieces) // 4 * local,)),
+        ],
         compiler_params=pltpu.CompilerParams(vmem_limit_bytes=20 * MIB),
         cost_estimate=pl.CostEstimate(
             flops=16 * local * CAP * rows_dev * len(pieces) * width,
@@ -373,7 +385,8 @@
 
 
 def put_kernel(local, rows_dev, planes, waits, bases_ref, y_own_ref, y_got_ref, facts_ref, *rest):
-    kept_ref, *send_refs = rest[waits:]
+    kept_ref, *send_refs, ended_ref = rest[waits:]
+    ended_ref[...] = jnp.zeros_like(ended_ref)
     tokens, rows = 4 * rows_dev, 4 * CAP
     total = 2 * local * rows
     shift_lane = lax.broadcasted_iota(jnp.int32, (1, tokens), 1) // rows_dev * CAP
@@ -414,10 +427,12 @@
     shape = lambda n: jax.ShapeDtypeStruct((n, width), jnp.bfloat16)
     out = pl.pallas_call(
         functools.partial(put_kernel, local, rows_dev, planes, len(waits)),
-        out_shape=(shape(2 * planes * rows_dev),) + (shape(2 * rows_dev),) * planes,
+        out_shape=(shape(2 * planes * rows_dev),)
+        + (shape(2 * rows_dev),) * planes
+        + (jax.ShapeDtypeStruct((8, 128), jnp.float32),),
         in_specs=[pl.BlockSpec(memory_space=pltpu.SMEM), vmem, vmem, vmem]
         + [pl.BlockSpec(memory_space=pl.ANY)] * len(waits),
-        out_specs=(vmem,) * (1 + planes),
+        out_specs=(vmem,) * (2 + planes),
         compiler_params=pltpu.CompilerParams(vmem_limit_bytes=20 * MIB),
         cost_estimate=pl.CostEstimate(
             flops=16 * local * CAP * tokens * width,
@@ -425,7 +440,7 @@
             transcendentals=0,
         ),
     )(bases, y_own, y_got, facts, *waits)
-    return out[0], out[1:]
+    return out[0], out[1:-1], out[-1]
 
 
 def swap(a, axis, size, distance):
@@ -490,25 +505,26 @@
     near_b, near_a = gather(0), gather(2)
     own_a, sib_a, facts_a = select_rows(near_a, bases, local)
     got_a = core(sib_a)
-    own_b, sib_b, facts_b = select_rows(near_b, bases, local)
+    pages, fill = late_work(facts_a)
+    own_b, sib_b, facts_b = select_rows(near_b, bases, local, [pages])
     got_b = core(sib_b)
-    pages, fill = late_work(facts_b)
     own_a, sib_a, ended = expert_rows(own_a, got_a, w_gate, w_up, w_down, [facts_b, pages])
     cache, filled = fill(ended)
     got_a = core(sib_a)
     own_b, sib_b, ended = expert_rows(own_b, got_b, w_gate, w_up, w_down, [filled])
     got_b = core(sib_b)
-    keep_a, (fx_a, fy_a) = put_rows(own_a, got_a, facts_a, bases, piece.shape[0], [ended])
+    keep_a, (fx_a, fy_a), _ = put_rows(own_a, got_a, facts_a, bases, piece.shape[0], [ended])
     keep_a, (gy_a, gx_a) = fold(keep_a, [x(fx_a), y(fy_a)], 2)
-    keep_b, (fx_b, fy_b) = put_rows(own_b, got_b, facts_b, bases, piece.shape[0], [gy_a])
+    keep_b, (fx_b, fy_b), put_b = put_rows(own_b, got_b, facts_b, bases, piece.shape[0], [gy_a])
     gy_a, gx_a = y(gy_a), x(gx_a)
     fx_b, fy_b = hold(fx_b, [gy_a, gx_a]), hold(fy_b, [gy_a, gx_a])
-    keep_a, (z_a,) = fold(keep_a, [gy_a, gx_a], 1)
+    keep_a, (z_a,) = fold(keep_a, [gy_a, gx_a], 1, [put_b])
     over_z = (keep_a.astype(jnp.float32) + z(z_a, 1).astype(jnp.float32)).astype(jnp.bfloat16)
     keep_b, (gy_b, gx_b) = fold(keep_b, [x(fx_b), y(fy_b)], 2, [over_z])
-    keep_b, (z_b,) = fold(keep_b, [y(gy_b), x(gx_b)], 1)
+    back_a = z(over_z, 2)
+    keep_b, (z_b,) = fold(keep_b, [y(gy_b), x(gx_b)], 1, [back_a])
     mine = keep_b.astype(jnp.float32) + z(z_b, 1).astype(jnp.float32)
-    return mine + z(over_z, 2).astype(jnp.float32), cache
+    return mine + back_a.astype(jnp.float32), cache
 
 
 def body(

time: 243 us -> 237 us (0.975)
  waiting for transfers between devices: 124 us -> 116 us
  Pallas kernels: 58.1 us -> 61.1 us
    ppermute x30, waiting for transfers between devices: 87.8 us -> 79.9 us  [swap(): return lax.ppermute(a, axis, [(i, i ^ distance) for i in range(size)])]
    pallas_call x2, Pallas kernels: 7.29 us -> 9.87 us  [select_rows(): pl.pallas_call(functools.partial(select_kernel, local, rows_dev, len(piec...]
  transfers between devices with their start and end apart: 33 -> 33, of which waited for: 23 -> 24; matrix products, arithmetic and copies ran while one was open for 1% -> 1% of each run, Pallas kernels for 19% -> 20%
where the time goes in v11:
time: 237 us; the launch traced here: 236 us
  waiting for transfers between devices  116 us (49%)
  Pallas kernels  61.1 us (26%)
  starting transfers between devices  45.4 us (19%)
  local copies, waits for them, and re-layouts  11 us (5%)
    ppermute x30, waiting for transfers between devices, swap(): return lax.ppermute(a, axis, [(i, i ^ distance) for i in range(size)])  79.9 us
    pallas_call x2, Pallas kernels, expert_rows(): pl.pallas_call(functools.partial(rows_kernel, local, len(waits)), out_sha...  32.2 us
    ppermute x30, starting transfers between devices, swap(): return lax.ppermute(a, axis, [(i, i ^ distance) for i in range(size)])  30.8 us
    all_to_all x1, waiting for transfers between devices, body(): lax.all_to_all(packed, 'seq', split_axis=0, concat_axis=0, tiled=True)  25.3 us
    all_to_all x1, waiting for transfers between devices, body(): lax.all_to_all(context.reshape(n_seq, rows_dev, span), 'seq', split_axis=...  11.1 us
    pallas_call x2, Pallas kernels, select_rows(): pl.pallas_call(functools.partial(select_kernel, local, rows_dev, len(piec...  9.87 us
    pallas_call x2, Pallas kernels, put_rows(): pl.pallas_call(functools.partial(put_kernel, local, rows_dev, planes, len...  8.42 us
    unnamed x35, local copies, waits for them, and re-layouts  8.03 us
  transfers between devices with their start and end apart: 33, of which 24 were waited for; matrix products, arithmetic and copies ran while one was open for 1% of the time, Pallas kernels for 20%

profile of v11, /device:TPU:0, one launch (start us, length us, event | category | flops | bytes accessed | tf_op | source)
XLA Modules:
  0.0 236.2 jit_solution(2622226335015074549)
XLA Ops:
  0.6 2.3 fusion.3
  3.1 1.3 shard_map.122
  4.3 7.3 %all-to-all-start = ((bf16[8,64,960]{2,1,0:T(8,128)(2,1)}), bf16[8,64,960]{2,1,0:T(8,128)(2,1)S(1)}, u32[]{:S(2)}, u32[]{:S(2)}) async-start(bf16[8,64,960]{2,1,0:T(8,128)(2,1)} %shard_map.122), calls=%async_computation | async-start | bytes 2097152 | tf_op jit(solution)/shard_map/all_to_all | solution.py:559
  12.0 25.3 %all-to-all-done = bf16[8,64,960]{2,1,0:T(8,128)(2,1)S(1)} async-done(((bf16[8,64,960]{2,1,0:T(8,128)(2,1)}), bf16[8,64,960]{2,1,0:T(8,128)(2,1)S(1)}, u32[]{:S(2)}, u32[]{:S(2)}) %all-to-all-start) | async-done | bytes 983072 | tf_op jit(solution)/shard_map/all_to_all | solution.py:559
  37.3 5.6 %shard_map.123 = bf16[512,320]{1,0:T(8,128)(2,1)} custom-call(bf16[512,960]{1,0:T(8,128)(2,1)S(1)} %bitcast.22, s32[1,512]{1,0:T(1,128)S(1)} %copy-done.4, s32[512,1]{1,0:T(8,128)S(1)} %copy.40.seg_col_ref), custom_call_target="tpu_custom_call" | custom-call | flops 335544320 | bytes 1310720 | tf_op jit(solution)/shard_map/pallas_call | solution.py:56
  42.9 3.6 %all-to-all-start.1 = ((bf16[8,64,320]{2,1,0:T(8,128)(2,1)}), bf16[8,64,320]{2,1,0:T(8,128)(2,1)S(1)}, u32[]{:S(2)}, u32[]{:S(2)}) async-start(bf16[8,64,320]{2,1,0:T(8,128)(2,1)} %bitcast.5), calls=%async_computation.1 | async-start | bytes 786432 | tf_op jit(solution)/shard_map/all_to_all | solution.py:562
  47.3 11.1 %all-to-all-done.1.context_ref = bf16[8,64,320]{2,1,0:T(8,128)(2,1)S(1)} async-done(((bf16[8,64,320]{2,1,0:T(8,128)(2,1)}), bf16[8,64,320]{2,1,0:T(8,128)(2,1)S(1)}, u32[]{:S(2)}, u32[]{:S(2)}) %all-to-all-start.1) | async-done | bytes 327712 | tf_op jit(solution)/shard_map/all_to_all | solution.py:562
  60.5 1.7 collective-permute-start.1
  62.2 1.5 collective-permute-start
  63.8 8.2 %collective-permute-done.3.refs_4_ = bf16[64,2432]{1,0:T(8,128)(2,1)S(1)} collective-permute-done((bf16[64,2432]{1,0:T(8,128)(2,1)S(1)}, bf16[64,2432]{1,0:T(8,128)(2,1)S(1)}, u32[]{:S(2)}, u32[]{:S(2)}) %collective-permute-start.3) | collective-permute-done | bytes 311328 | tf_op jit(solution)/shard_map/ppermute | solution.py:447
  72.0 1.5 collective-permute-start.5
  73.5 2.9 %collective-permute-start.4 = (bf16[64,2432]{1,0:T(8,128)(2,1)S(1)}, bf16[64,2432]{1,0:T(8,128)(2,1)S(1)}, u32[]{:S(2)}, u32[]{:S(2)}) collective-permute-start(bf16[64,2432]{1,0:T(8,128)(2,1)S(1)} %collective-permute-done.3.refs_4_), channel_id=1, source_target_pairs={{0,4},{4,0},{8,12},{12,8},{16,20},{20,16},{24,28},{28,24},{1,5},{5... | collective-permute-start | bytes 933896 | tf_op jit(solution)/shard_map/ppermute | solution.py:447
  77.2 2.4 %collective-permute-done.5.refs_3_.refs_6_ = bf16[64,2432]{1,0:T(8,128)(2,1)S(1)} collective-permute-done((bf16[64,2432]{1,0:T(8,128)(2,1)S(1)}, bf16[64,2432]{1,0:T(8,128)(2,1)S(1)}, u32[]{:S(2)}, u32[]{:S(2)}) %collective-permute-start.5) | collective-permute-done | bytes 311328 | tf_op jit(solution)/shard_map/ppermute | solution.py:447
  79.5 3.1 %collective-permute-done.4.refs_4_.refs_5_ = bf16[64,2432]{1,0:T(8,128)(2,1)S(1)} collective-permute-done((bf16[64,2432]{1,0:T(8,128)(2,1)S(1)}, bf16[64,2432]{1,0:T(8,128)(2,1)S(1)}, u32[]{:S(2)}, u32[]{:S(2)}) %collective-permute-start.4) | collective-permute-done | bytes 311328 | tf_op jit(solution)/shard_map/ppermute | solution.py:447
  83.1 1.7 collective-permute-start.9
  84.9 5.1 %collective-permute-done.8.refs_2_.refs_1_ = bf16[64,2432]{1,0:T(8,128)(2,1)S(1)} collective-permute-done((bf16[64,2432]{1,0:T(8,128)(2,1)S(1)}, bf16[64,2432]{1,0:T(8,128)(2,1)S(1)}, u32[]{:S(2)}, u32[]{:S(2)}) %collective-permute-start.8) | collective-permute-done | bytes 311328 | tf_op jit(solution)/shard_map/ppermute | solution.py:447
  90.3 1.6 collective-permute-done.11.refs_0_
  92.6 1.5 collective-permute-start.13
  94.9 7.0 %collective-permute-done.13.refs_6_ = bf16[64,2432]{1,0:T(8,128)(2,1)} collective-permute-done((bf16[64,2432]{1,0:T(8,128)(2,1)}, bf16[64,2432]{1,0:T(8,128)(2,1)}, u32[]{:S(2)}, u32[]{:S(2)}) %collective-permute-start.13) | collective-permute-done | bytes 311328 | tf_op jit(solution)/shard_map/ppermute | solution.py:447
  102.5 2.8 %collective-permute-done.10.refs_3_ = bf16[64,2432]{1,0:T(8,128)(2,1)} collective-permute-done((bf16[64,2432]{1,0:T(8,128)(2,1)}, bf16[64,2432]{1,0:T(8,128)(2,1)}, u32[]{:S(2)}, u32[]{:S(2)}) %collective-permute-start.10) | collective-permute-done | bytes 311328 | tf_op jit(solution)/shard_map/ppermute | solution.py:447
  105.3 3.9 %collective-permute-done.14.refs_7_ = bf16[64,2432]{1,0:T(8,128)(2,1)} collective-permute-done((bf16[64,2432]{1,0:T(8,128)(2,1)}, bf16[64,2432]{1,0:T(8,128)(2,1)}, u32[]{:S(2)}, u32[]{:S(2)}) %collective-permute-start.14) | collective-permute-done | bytes 311328 | tf_op jit(solution)/shard_map/ppermute | solution.py:447
  110.1 5.4 %shard_map.127 = (bf16[2,192,2304]{2,1,0:T(8,128)(2,1)S(1)}, bf16[2,192,2304]{2,1,0:T(8,128)(2,1)}, bf16[512,128]{1,0:T(8,128)(2,1)S(1)}) custom-call(s32[2]{0:T(128)S(1)} %add_multiply_fusion.bases_ref, bf16[64,2432]{1,0:T(8,128)(2,1)S(1)} %shard_map.125.refs_0_, bf16[64,2432]{1,0:T(8,128)(2,1)S(1)} %copy-done.1, ...), custom_call_target="tpu_custom_call" | custom-call | flops 905969664 | bytes 6029312 | tf_op jit(solution)/shard_map/pallas_call | solution.py:308
  116.8 1.5 collective-permute-start.2
  118.9 1.6 shard_map.128.refs_8_.rest_1_
  120.6 6.0 %collective-permute-done.2.refs_3_ = bf16[64,2432]{1,0:T(8,128)(2,1)S(1)} collective-permute-done((bf16[64,2432]{1,0:T(8,128)(2,1)S(1)}, bf16[64,2432]{1,0:T(8,128)(2,1)S(1)}, u32[]{:S(2)}, u32[]{:S(2)}) %collective-permute-start.2) | collective-permute-done | bytes 311328 | tf_op jit(solution)/shard_map/ppermute | solution.py:447
  127.8 4.4 %shard_map.129 = (bf16[2,192,2304]{2,1,0:T(8,128)(2,1)S(1)}, bf16[2,192,2304]{2,1,0:T(8,128)(2,1)}, bf16[512,128]{1,0:T(8,128)(2,1)S(1)}) custom-call(s32[2]{0:T(128)S(1)} %add_multiply_fusion.bases_ref, bf16[64,2432]{1,0:T(8,128)(2,1)S(1)} %copy-done.6, bf16[64,2432]{1,0:T(8,128)(2,1)S(1)} %collective-permute-done.refs_2_.refs_1_, ...), custom_call_target="tpu_custom_call" | custom-call | flops 905969664 | bytes 6029312 | tf_op jit(solution)/shard_map/pallas_call | solution.py:308
  132.2 1.3 copy-done.9
  133.5 3.7 %all-to-all-start.2 = ((bf16[8,64,640]{2,1,0:T(8,128)(2,1)}), bf16[8,64,640]{2,1,0:T(8,128)(2,1)S(1)}, u32[]{:S(2)}, u32[]{:S(2)}) async-start(bf16[8,64,640]{2,1,0:T(8,128)(2,1)} %shard_map.128.refs_8_.rest_1_), calls=%async_computation.2 | async-start | bytes 1310720 | tf_op jit(solution)/shard_map/all_to_all | solution.py:579
  137.2 1.5 copy-done.12
  138.7 16.6 %shard_map.130 = (bf16[2,192,2304]{2,1,0:T(8,128)(2,1)S(1)}, bf16[2,192,2304]{2,1,0:T(8,128)(2,1)}, f32[8,128]{1,0:T(8,128)S(1)}) custom-call(bf16[2,192,2304]{2,1,0:T(8,128)(2,1)S(1)} %copy-done.12, bf16[2,192,2304]{2,1,0:T(8,128)(2,1)} %collective-permute-done.16.got_ref, bf16[2,720,2304]{2,1,0:T(8,128)(2,1)} %bitcast.28, bf16[2,720,2304]{2,1,0:T(8,128)(2,1)} %bitcast.30, ...), custom_call_target="tpu_custom_call" | custom-call | flops 7644119040 | bytes 26984448 | tf_op jit(solution)/shard_map/pallas_call | solution.py:364
  156.9 1.5 copy-done.10
  158.4 15.6 %shard_map.132 = (bf16[2,192,2304]{2,1,0:T(8,128)(2,1)S(1)}, bf16[2,192,2304]{2,1,0:T(8,128)(2,1)S(1)}, f32[8,128]{1,0:T(8,128)S(1)}) custom-call(bf16[2,192,2304]{2,1,0:T(8,128)(2,1)S(1)} %copy-done.10, bf16[2,192,2304]{2,1,0:T(8,128)(2,1)} %collective-permute-done.15.got_ref, bf16[2,720,2304]{2,1,0:T(8,128)(2,1)} %bitcast.29, ...), custom_call_target="tpu_custom_call" | custom-call | flops 7644119040 | bytes 26984448 | tf_op jit(solution)/shard_map/pallas_call | solution.py:364
  174.1 4.9 %shard_map.133 = (bf16[256,2304]{1,0:T(8,128)(2,1)S(1)}, bf16[128,2304]{1,0:T(8,128)(2,1)S(1)}, bf16[128,2304]{1,0:T(8,128)(2,1)S(1)}, f32[8,128]{1,0:T(8,128)}) custom-call(s32[2]{0:T(128)S(1)} %add_multiply_fusion.bases_ref, bf16[2,192,2304]{2,1,0:T(8,128)(2,1)S(1)} %get-tuple-element.47.y_own_ref, ...), custom_call_target="tpu_custom_call" | custom-call | flops 905969664 | bytes 18874368 | tf_op jit(solution)/shard_map/pallas_call | solution.py:428
  179.0 1.7 collective-permute-start.19
  181.2 13.4 %collective-permute-done.19.rest_0_ = bf16[128,2304]{1,0:T(8,128)(2,1)S(1)} collective-permute-done((bf16[128,2304]{1,0:T(8,128)(2,1)S(1)}, bf16[128,2304]{1,0:T(8,128)(2,1)S(1)}, u32[]{:S(2)}, u32[]{:S(2)}) %collective-permute-start.19) | collective-permute-done | bytes 589856 | tf_op jit(solution)/shard_map/ppermute | solution.py:447
  197.3 3.6 %shard_map.135 = (bf16[256,2304]{1,0:T(8,128)(2,1)S(1)}, bf16[128,2304]{1,0:T(8,128)(2,1)S(1)}, bf16[128,2304]{1,0:T(8,128)(2,1)S(1)}, f32[8,128]{1,0:T(8,128)S(1)}) custom-call(s32[2]{0:T(128)S(1)} %add_multiply_fusion.bases_ref, bf16[2,192,2304]{2,1,0:T(8,128)(2,1)S(1)} %get-tuple-element.45.y_own_ref, ...), custom_call_target="tpu_custom_call" | custom-call | flops 905969664 | bytes 18874368 | tf_op jit(solution)/shard_map/pallas_call | solution.py:428
  200.9 3.3 %collective-permute-done.21.refs_1_.rest_0_ = bf16[64,2304]{1,0:T(8,128)(2,1)S(1)} collective-permute-done((bf16[64,2304]{1,0:T(8,128)(2,1)S(1)}, bf16[64,2304]{1,0:T(8,128)(2,1)S(1)}, u32[]{:S(2)}, u32[]{:S(2)}) %collective-permute-start.21) | collective-permute-done | bytes 294944 | tf_op jit(solution)/shard_map/ppermute | solution.py:447
  204.6 1.5 collective-permute-start.25
  206.8 1.5 collective-permute-start.24
  208.2 3.3 %collective-permute-done.25 = bf16[64,2304]{1,0:T(8,128)(2,1)S(1)} collective-permute-done((bf16[64,2304]{1,0:T(8,128)(2,1)S(1)}, bf16[64,2304]{1,0:T(8,128)(2,1)S(1)}, u32[]{:S(2)}, u32[]{:S(2)}) %collective-permute-start.25) | collective-permute-done | bytes 294944 | tf_op jit(solution)/shard_map/ppermute | solution.py:447
  211.6 2.7 %collective-permute-start.28 = (bf16[64,2304]{1,0:T(8,128)(2,1)S(1)}, bf16[64,2304]{1,0:T(8,128)(2,1)S(1)}, u32[]{:S(2)}, u32[]{:S(2)}) collective-permute-start(bf16[64,2304]{1,0:T(8,128)(2,1)S(1)} %add_convert_fusion.1.rest_2_), channel_id=1, source_target_pairs={{0,16},{4,20},{8,24},{12,28},{16,0},{20,4},{24,8},{28,12},{1,17},{... | collective-permute-start | bytes 884744 | tf_op jit(solution)/shard_map/ppermute | solution.py:447
  214.3 4.7 %collective-permute-done.23.rest_0_ = bf16[128,2304]{1,0:T(8,128)(2,1)S(1)} collective-permute-done((bf16[128,2304]{1,0:T(8,128)(2,1)S(1)}, bf16[128,2304]{1,0:T(8,128)(2,1)S(1)}, u32[]{:S(2)}, u32[]{:S(2)}) %collective-permute-start.23) | collective-permute-done | bytes 589856 | tf_op jit(solution)/shard_map/ppermute | solution.py:447
  220.2 1.5 collective-permute-start.26
  221.7 1.4 collective-permute-start.27
  223.1 1.6 collective-permute-done.28.rest_2_
  224.7 2.2 collective-permute-done.26.rest_0_
  227.0 1.5 collective-permute-done.27.rest_1_
  229.5 5.9 %collective-permute-done.29 = bf16[64,2304]{1,0:T(8,128)(2,1)S(1)} collective-permute-done((bf16[64,2304]{1,0:T(8,128)(2,1)S(1)}, bf16[64,2304]{1,0:T(8,128)(2,1)S(1)}, u32[]{:S(2)}, u32[]{:S(2)}) %collective-permute-start.29) | collective-permute-done | bytes 294944 | tf_op jit(solution)/shard_map/ppermute | solution.py:447
  (90 shorter events, 20.0 us)
Async XLA Ops:
  0.6 2.4 %copy-start.3 = (bf16[1,64,2304]{2,1,0:T(8,128)(2,1)S(1)}, bf16[1,64,2304]{2,1,0:T(8,128)(2,1)}, u32[]{:S(2)}) copy-start(bf16[1,64,2304]{2,1,0:T(8,128)(2,1)} %param.11) | copy-start | bytes 884740
  3.0 8.6 %copy-start.4 = (s32[1,512]{1,0:T(1,128)S(1)}, s32[1,512]{1,0:T(1,128)}, u32[]{:S(2)}) copy-start(s32[1,512]{1,0:T(1,128)} %seg_row_ref.1) | copy-start | bytes 6148
  3.0 8.7 %copy-start.13 = (bf16[2304]{0:T(1024)(128)(2,1)S(1)}, bf16[2304]{0:T(1024)(128)(2,1)}, u32[]{:S(2)}) copy-start(bf16[2304]{0:T(1024)(128)(2,1)} %param.14) | copy-start | bytes 13828
  3.1 8.7 %copy-start.14 = (s32[1,64,2]{1,2,0:T(2,128)S(1)}, s32[1,64,2]{1,2,0:T(2,128)}, u32[]{:S(2)}) copy-start(s32[1,64,2]{1,2,0:T(2,128)} %param.16) | copy-start | bytes 1540
  4.3 33.0 %all-to-all-start = ((bf16[8,64,960]{2,1,0:T(8,128)(2,1)}), bf16[8,64,960]{2,1,0:T(8,128)(2,1)S(1)}, u32[]{:S(2)}, u32[]{:S(2)}) async-start(bf16[8,64,960]{2,1,0:T(8,128)(2,1)} %shard_map.122), calls=%async_computation | async-start | bytes 2097152 | tf_op jit(solution)/shard_map/all_to_all | solution.py:559
  37.3 9.9 %copy-start.15 = (f32[1,64,2]{1,2,0:T(2,128)S(1)}, f32[1,64,2]{1,2,0:T(2,128)}, u32[]{:S(2)}) copy-start(f32[1,64,2]{1,2,0:T(2,128)} %param.17) | copy-start | bytes 1540
  37.3 21.1 %copy-start.2 = (bf16[1,64,2304]{2,1,0:T(8,128)(2,1)S(1)}, bf16[1,64,2304]{2,1,0:T(8,128)(2,1)}, u32[]{:S(2)}) copy-start(bf16[1,64,2304]{2,1,0:T(8,128)(2,1)} %param.13) | copy-start | bytes 884740
  42.9 15.5 %all-to-all-start.1 = ((bf16[8,64,320]{2,1,0:T(8,128)(2,1)}), bf16[8,64,320]{2,1,0:T(8,128)(2,1)S(1)}, u32[]{:S(2)}, u32[]{:S(2)}) async-start(bf16[8,64,320]{2,1,0:T(8,128)(2,1)} %bitcast.5), calls=%async_computation.1 | async-start | bytes 786432 | tf_op jit(solution)/shard_map/all_to_all | solution.py:562
  58.7 33.2 %copy-start.5 = (bf16[64,2432]{1,0:T(8,128)(2,1)}, bf16[64,2432]{1,0:T(8,128)(2,1)S(1)}, u32[]{:S(2)}) copy-start(bf16[64,2432]{1,0:T(8,128)(2,1)S(1)} %get-tuple-element.36.refs_0_) | copy-start | bytes 933892
  58.7 13.3 %collective-permute-start.3 = (bf16[64,2432]{1,0:T(8,128)(2,1)S(1)}, bf16[64,2432]{1,0:T(8,128)(2,1)S(1)}, u32[]{:S(2)}, u32[]{:S(2)}) collective-permute-start(bf16[64,2432]{1,0:T(8,128)(2,1)S(1)} %get-tuple-element.36.refs_0_), channel_id=1, source_target_pairs={{0,8},{4,12},{8,0},{12,4},{16,24},{20,28},{24,16},{28,20},{1,9},{5... | collective-permute-start | bytes 933896 | tf_op jit(solution)/shard_map/ppermute | solution.py:447
  59.7 17.5 %collective-permute-start.7 = (bf16[64,2432]{1,0:T(8,128)(2,1)S(1)}, bf16[64,2432]{1,0:T(8,128)(2,1)S(1)}, u32[]{:S(2)}, u32[]{:S(2)}) collective-permute-start(bf16[64,2432]{1,0:T(8,128)(2,1)S(1)} %get-tuple-element.36.refs_0_), channel_id=1, source_target_pairs={{0,16},{4,20},{8,24},{12,28},{16,0},{20,4},{24,8},{28,12},{1,17},{... | collective-permute-start | bytes 933896 | tf_op jit(solution)/shard_map/ppermute | solution.py:447
  60.5 16.7 %collective-permute-start.1 = (bf16[64,2432]{1,0:T(8,128)(2,1)S(1)}, bf16[64,2432]{1,0:T(8,128)(2,1)S(1)}, u32[]{:S(2)}, u32[]{:S(2)}) collective-permute-start(bf16[64,2432]{1,0:T(8,128)(2,1)S(1)} %get-tuple-element.36.refs_0_), channel_id=1, source_target_pairs={{0,4},{4,0},{8,12},{12,8},{16,20},{20,16},{24,28},{28,24},{1,5},{5... | collective-permute-start | bytes 933896 | tf_op jit(solution)/shard_map/ppermute | solution.py:447
  62.2 14.9 %collective-permute-start = (bf16[64,2432]{1,0:T(8,128)(2,1)S(1)}, bf16[64,2432]{1,0:T(8,128)(2,1)S(1)}, u32[]{:S(2)}, u32[]{:S(2)}) collective-permute-start(bf16[64,2432]{1,0:T(8,128)(2,1)S(1)} %get-tuple-element.36.refs_0_), channel_id=1, source_target_pairs={{0,2},{1,3},{2,0},{3,1},{4,6},{5,7},{6,4},{7,5},{8,10},{9,11},{10,... | collective-permute-start | bytes 933896 | tf_op jit(solution)/shard_map/ppermute | solution.py:447
  72.0 7.6 %collective-permute-start.5 = (bf16[64,2432]{1,0:T(8,128)(2,1)S(1)}, bf16[64,2432]{1,0:T(8,128)(2,1)S(1)}, u32[]{:S(2)}, u32[]{:S(2)}) collective-permute-start(bf16[64,2432]{1,0:T(8,128)(2,1)S(1)} %collective-permute-done.3.refs_4_), channel_id=1, source_target_pairs={{0,2},{1,3},{2,0},{3,1},{4,6},{5,7},{6,4},{7,5},{8,10},{9,11},{10,... | collective-permute-start | bytes 933896 | tf_op jit(solution)/shard_map/ppermute | solution.py:447
  73.5 9.1 %collective-permute-start.4 = (bf16[64,2432]{1,0:T(8,128)(2,1)S(1)}, bf16[64,2432]{1,0:T(8,128)(2,1)S(1)}, u32[]{:S(2)}, u32[]{:S(2)}) collective-permute-start(bf16[64,2432]{1,0:T(8,128)(2,1)S(1)} %collective-permute-done.3.refs_4_), channel_id=1, source_target_pairs={{0,4},{4,0},{8,12},{12,8},{16,20},{20,16},{24,28},{28,24},{1,5},{5... | collective-permute-start | bytes 933896 | tf_op jit(solution)/shard_map/ppermute | solution.py:447
  82.6 7.3 %collective-permute-start.8 = (bf16[64,2432]{1,0:T(8,128)(2,1)S(1)}, bf16[64,2432]{1,0:T(8,128)(2,1)S(1)}, u32[]{:S(2)}, u32[]{:S(2)}) collective-permute-start(bf16[64,2432]{1,0:T(8,128)(2,1)S(1)} %shard_map.125.refs_0_), channel_id=1, source_target_pairs={{0,2},{1,3},{2,0},{3,1},{4,6},{5,7},{6,4},{7,5},{8,10},{9,11},{10,... | collective-permute-start | bytes 933896 | tf_op jit(solution)/shard_map/ppermute | solution.py:447
  83.1 7.1 %collective-permute-start.9 = (bf16[64,2432]{1,0:T(8,128)(2,1)S(1)}, bf16[64,2432]{1,0:T(8,128)(2,1)}, u32[]{:S(2)}, u32[]{:S(2)}) collective-permute-start(bf16[64,2432]{1,0:T(8,128)(2,1)S(1)} %shard_map.125.refs_0_), channel_id=1, source_target_pairs={{0,4},{4,0},{8,12},{12,8},{16,20},{20,16},{24,28},{28,24},{1,5},{5... | collective-permute-start | bytes 933896 | tf_op jit(solution)/shard_map/ppermute | solution.py:447
  84.9 7.0 %collective-permute-start.11 = (bf16[64,2432]{1,0:T(8,128)(2,1)S(1)}, bf16[64,2432]{1,0:T(8,128)(2,1)}, u32[]{:S(2)}, u32[]{:S(2)}) collective-permute-start(bf16[64,2432]{1,0:T(8,128)(2,1)S(1)} %shard_map.125.refs_0_), channel_id=1, source_target_pairs={{0,8},{4,12},{8,0},{12,4},{16,24},{20,28},{24,16},{28,20},{1,9},{5... | collective-permute-start | bytes 933896 | tf_op jit(solution)/shard_map/ppermute | solution.py:447
  92.6 26.2 %copy-start.16 = (s32[1,32]{1,0:T(1,128)S(1)}, s32[1,32]{1,0:T(1,128)}, u32[]{:S(2)}) copy-start(s32[1,32]{1,0:T(1,128)} %param.18) | copy-start | bytes 388
  92.6 9.3 %collective-permute-start.13 = (bf16[64,2432]{1,0:T(8,128)(2,1)}, bf16[64,2432]{1,0:T(8,128)(2,1)}, u32[]{:S(2)}, u32[]{:S(2)}) collective-permute-start(bf16[64,2432]{1,0:T(8,128)(2,1)} %shard_map.126.refs_4_), channel_id=1, source_target_pairs={{0,2},{1,3},{2,0},{3,1},{4,6},{5,7},{6,4},{7,5},{8,10},{9,11},{10,... | collective-permute-start | bytes 933896 | tf_op jit(solution)/shard_map/ppermute | solution.py:447
  94.1 11.1 %collective-permute-start.12 = (bf16[64,2432]{1,0:T(8,128)(2,1)}, bf16[64,2432]{1,0:T(8,128)(2,1)}, u32[]{:S(2)}, u32[]{:S(2)}) collective-permute-start(bf16[64,2432]{1,0:T(8,128)(2,1)} %shard_map.126.refs_4_), channel_id=1, source_target_pairs={{0,4},{4,0},{8,12},{12,8},{16,20},{20,16},{24,28},{28,24},{1,5},{5... | collective-permute-start | bytes 933896 | tf_op jit(solution)/shard_map/ppermute | solution.py:447
  94.4 10.9 %collective-permute-start.10 = (bf16[64,2432]{1,0:T(8,128)(2,1)}, bf16[64,2432]{1,0:T(8,128)(2,1)}, u32[]{:S(2)}, u32[]{:S(2)}) collective-permute-start(bf16[64,2432]{1,0:T(8,128)(2,1)} %collective-permute-done.9.refs_1_.refs_2_), channel_id=1, source_target_pairs={{0,2},{1,3},{2,0},{3,1},{4,6},{5,7},{6,4},{7,5},{8,10},{9,11},{10,... | collective-permute-start | bytes 933896 | tf_op jit(solution)/shard_map/ppermute | solution.py:447
  101.9 7.2 %collective-permute-start.14 = (bf16[64,2432]{1,0:T(8,128)(2,1)}, bf16[64,2432]{1,0:T(8,128)(2,1)}, u32[]{:S(2)}, u32[]{:S(2)}) collective-permute-start(bf16[64,2432]{1,0:T(8,128)(2,1)} %collective-permute-done.13.refs_6_), channel_id=1, source_target_pairs={{0,4},{4,0},{8,12},{12,8},{16,20},{20,16},{24,28},{28,24},{1,5},{5... | collective-permute-start | bytes 933896 | tf_op jit(solution)/shard_map/ppermute | solution.py:447
  109.1 1.0 copy-start.1
  110.1 17.6 %copy-start.6 = (bf16[64,2432]{1,0:T(8,128)(2,1)S(1)}, bf16[64,2432]{1,0:T(8,128)(2,1)}, u32[]{:S(2)}) copy-start(bf16[64,2432]{1,0:T(8,128)(2,1)} %copy-done.5) | copy-start | bytes 933892
  110.1 17.6 %copy-start.8 = (bf16[64,2432]{1,0:T(8,128)(2,1)S(1)}, bf16[64,2432]{1,0:T(8,128)(2,1)}, u32[]{:S(2)}) copy-start(bf16[64,2432]{1,0:T(8,128)(2,1)} %copy-done.7) | copy-start | bytes 933892
  115.6 1.2 copy-start.11
  116.8 20.4 %collective-permute-start.16 = (bf16[2,192,2304]{2,1,0:T(8,128)(2,1)}, bf16[2,192,2304]{2,1,0:T(8,128)(2,1)}, u32[]{:S(2)}, u32[]{:S(2)}) collective-permute-start(bf16[2,192,2304]{2,1,0:T(8,128)(2,1)} %get-tuple-element.41), channel_id=1, source_target_pairs={{0,1},{1,0},{2,3},{3,2},{4,5},{5,4},{6,7},{7,6},{8,9},{9,8},{10,11... | collective-permute-start | bytes 5308424 | tf_op jit(solution)/shard_map/ppermute | solution.py:447
  116.8 9.8 %collective-permute-start.2 = (bf16[64,2432]{1,0:T(8,128)(2,1)S(1)}, bf16[64,2432]{1,0:T(8,128)(2,1)S(1)}, u32[]{:S(2)}, u32[]{:S(2)}) collective-permute-start(bf16[64,2432]{1,0:T(8,128)(2,1)S(1)} %collective-permute-done.1.refs_1_.refs_2_), channel_id=1, source_target_pairs={{0,2},{1,3},{2,0},{3,1},{4,6},{5,7},{6,4},{7,5},{8,10},{9,11},{10,... | collective-permute-start | bytes 933896 | tf_op jit(solution)/shard_map/ppermute | solution.py:447
  118.3 9.5 %collective-permute-start.6 = (bf16[64,2432]{1,0:T(8,128)(2,1)S(1)}, bf16[64,2432]{1,0:T(8,128)(2,1)S(1)}, u32[]{:S(2)}, u32[]{:S(2)}) collective-permute-start(bf16[64,2432]{1,0:T(8,128)(2,1)S(1)} %collective-permute-done.5.refs_3_.refs_6_), channel_id=1, source_target_pairs={{0,4},{4,0},{8,12},{12,8},{16,20},{20,16},{24,28},{28,24},{1,5},{5... | collective-permute-start | bytes 933896 | tf_op jit(solution)/shard_map/ppermute | solution.py:447
  132.2 1.3 copy-start.9
  133.5 23.4 %collective-permute-start.15 = (bf16[2,192,2304]{2,1,0:T(8,128)(2,1)}, bf16[2,192,2304]{2,1,0:T(8,128)(2,1)}, u32[]{:S(2)}, u32[]{:S(2)}) collective-permute-start(bf16[2,192,2304]{2,1,0:T(8,128)(2,1)} %get-tuple-element.39), channel_id=1, source_target_pairs={{0,1},{1,0},{2,3},{3,2},{4,5},{5,4},{6,7},{7,6},{8,9},{9,8},{10,11... | collective-permute-start | bytes 5308424 | tf_op jit(solution)/shard_map/ppermute | solution.py:447
  133.5 22.4 %all-to-all-start.2 = ((bf16[8,64,640]{2,1,0:T(8,128)(2,1)}), bf16[8,64,640]{2,1,0:T(8,128)(2,1)S(1)}, u32[]{:S(2)}, u32[]{:S(2)}) async-start(bf16[8,64,640]{2,1,0:T(8,128)(2,1)} %shard_map.128.refs_8_.rest_1_), calls=%async_computation.2 | async-start | bytes 1310720 | tf_op jit(solution)/shard_map/all_to_all | solution.py:579
  137.2 1.5 copy-start.12
  155.4 18.7 %collective-permute-start.18 = (bf16[2,192,2304]{2,1,0:T(8,128)(2,1)}, bf16[2,192,2304]{2,1,0:T(8,128)(2,1)}, u32[]{:S(2)}, u32[]{:S(2)}) collective-permute-start(bf16[2,192,2304]{2,1,0:T(8,128)(2,1)} %get-tuple-element.48), channel_id=1, source_target_pairs={{0,1},{1,0},{2,3},{3,2},{4,5},{5,4},{6,7},{7,6},{8,9},{9,8},{10,11... | collective-permute-start | bytes 5308424 | tf_op jit(solution)/shard_map/ppermute | solution.py:447
  156.9 1.5 copy-start.10
  174.0 23.3 %collective-permute-start.17 = (bf16[2,192,2304]{2,1,0:T(8,128)(2,1)S(1)}, bf16[2,192,2304]{2,1,0:T(8,128)(2,1)S(1)}, u32[]{:S(2)}, u32[]{:S(2)}) collective-permute-start(bf16[2,192,2304]{2,1,0:T(8,128)(2,1)S(1)} %get-tuple-element.46), channel_id=1, source_target_pairs={{0,1},{1,0},{2,3},{3,2},{4,5},{5,4},{6,7},{7,6},{8,9},{9,8},{10,11... | collective-permute-start | bytes 5308424 | tf_op jit(solution)/shard_map/ppermute | solution.py:447
  179.0 15.7 %collective-permute-start.19 = (bf16[128,2304]{1,0:T(8,128)(2,1)S(1)}, bf16[128,2304]{1,0:T(8,128)(2,1)S(1)}, u32[]{:S(2)}, u32[]{:S(2)}) collective-permute-start(bf16[128,2304]{1,0:T(8,128)(2,1)S(1)} %get-tuple-element.51), channel_id=1, source_target_pairs={{0,4},{4,0},{8,12},{12,8},{16,20},{20,16},{24,28},{28,24},{1,5},{5... | collective-permute-start | bytes 1769480 | tf_op jit(solution)/shard_map/ppermute | solution.py:447
  180.7 15.2 %collective-permute-start.20 = (bf16[128,2304]{1,0:T(8,128)(2,1)S(1)}, bf16[128,2304]{1,0:T(8,128)(2,1)S(1)}, u32[]{:S(2)}, u32[]{:S(2)}) collective-permute-start(bf16[128,2304]{1,0:T(8,128)(2,1)S(1)} %get-tuple-element.52), channel_id=1, source_target_pairs={{0,2},{1,3},{2,0},{3,1},{4,6},{5,7},{6,4},{7,5},{8,10},{9,11},{10,... | collective-permute-start | bytes 1769480 | tf_op jit(solution)/shard_map/ppermute | solution.py:447
  196.1 8.1 %collective-permute-start.21 = (bf16[64,2304]{1,0:T(8,128)(2,1)S(1)}, bf16[64,2304]{1,0:T(8,128)(2,1)S(1)}, u32[]{:S(2)}, u32[]{:S(2)}) collective-permute-start(bf16[64,2304]{1,0:T(8,128)(2,1)S(1)} %get-tuple-element.53.rest_0_), channel_id=1, source_target_pairs={{0,2},{1,3},{2,0},{3,1},{4,6},{5,7},{6,4},{7,5},{8,10},{9,11},{10,... | collective-permute-start | bytes 884744 | tf_op jit(solution)/shard_map/ppermute | solution.py:447
  196.8 7.7 %collective-permute-start.22 = (bf16[64,2304]{1,0:T(8,128)(2,1)S(1)}, bf16[64,2304]{1,0:T(8,128)(2,1)S(1)}, u32[]{:S(2)}, u32[]{:S(2)}) collective-permute-start(bf16[64,2304]{1,0:T(8,128)(2,1)S(1)} %get-tuple-element.56), channel_id=1, source_target_pairs={{0,4},{4,0},{8,12},{12,8},{16,20},{20,16},{24,28},{28,24},{1,5},{5... | collective-permute-start | bytes 884744 | tf_op jit(solution)/shard_map/ppermute | solution.py:447
  204.6 6.9 %collective-permute-start.25 = (bf16[64,2304]{1,0:T(8,128)(2,1)S(1)}, bf16[64,2304]{1,0:T(8,128)(2,1)S(1)}, u32[]{:S(2)}, u32[]{:S(2)}) collective-permute-start(bf16[64,2304]{1,0:T(8,128)(2,1)S(1)} %get-tuple-element.61), channel_id=1, source_target_pairs={{0,8},{4,12},{8,0},{12,4},{16,24},{20,28},{24,16},{28,20},{1,9},{5... | collective-permute-start | bytes 884744 | tf_op jit(solution)/shard_map/ppermute | solution.py:447
  206.2 12.8 %collective-permute-start.23 = (bf16[128,2304]{1,0:T(8,128)(2,1)S(1)}, bf16[128,2304]{1,0:T(8,128)(2,1)S(1)}, u32[]{:S(2)}, u32[]{:S(2)}) collective-permute-start(bf16[128,2304]{1,0:T(8,128)(2,1)S(1)} %shard_map.136), channel_id=1, source_target_pairs={{0,4},{4,0},{8,12},{12,8},{16,20},{20,16},{24,28},{28,24},{1,5},{5... | collective-permute-start | bytes 1769480 | tf_op jit(solution)/shard_map/ppermute | solution.py:447
  206.8 13.2 %collective-permute-start.24 = (bf16[128,2304]{1,0:T(8,128)(2,1)S(1)}, bf16[128,2304]{1,0:T(8,128)(2,1)S(1)}, u32[]{:S(2)}, u32[]{:S(2)}) collective-permute-start(bf16[128,2304]{1,0:T(8,128)(2,1)S(1)} %shard_map.137), channel_id=1, source_target_pairs={{0,2},{1,3},{2,0},{3,1},{4,6},{5,7},{6,4},{7,5},{8,10},{9,11},{10,... | collective-permute-start | bytes 1769480 | tf_op jit(solution)/shard_map/ppermute | solution.py:447
  211.6 13.2 %collective-permute-start.28 = (bf16[64,2304]{1,0:T(8,128)(2,1)S(1)}, bf16[64,2304]{1,0:T(8,128)(2,1)S(1)}, u32[]{:S(2)}, u32[]{:S(2)}) collective-permute-start(bf16[64,2304]{1,0:T(8,128)(2,1)S(1)} %add_convert_fusion.1.rest_2_), channel_id=1, source_target_pairs={{0,16},{4,20},{8,24},{12,28},{16,0},{20,4},{24,8},{28,12},{1,17},{... | collective-permute-start | bytes 884744 | tf_op jit(solution)/shard_map/ppermute | solution.py:447
  220.2 6.8 %collective-permute-start.26 = (bf16[64,2304]{1,0:T(8,128)(2,1)S(1)}, bf16[64,2304]{1,0:T(8,128)(2,1)S(1)}, u32[]{:S(2)}, u32[]{:S(2)}) collective-permute-start(bf16[64,2304]{1,0:T(8,128)(2,1)S(1)} %get-tuple-element.63), channel_id=1, source_target_pairs={{0,2},{1,3},{2,0},{3,1},{4,6},{5,7},{6,4},{7,5},{8,10},{9,11},{10,... | collective-permute-start | bytes 884744 | tf_op jit(solution)/shard_map/ppermute | solution.py:447
  221.7 6.7 %collective-permute-start.27 = (bf16[64,2304]{1,0:T(8,128)(2,1)S(1)}, bf16[64,2304]{1,0:T(8,128)(2,1)S(1)}, u32[]{:S(2)}, u32[]{:S(2)}) collective-permute-start(bf16[64,2304]{1,0:T(8,128)(2,1)S(1)} %get-tuple-element.64), channel_id=1, source_target_pairs={{0,4},{4,0},{8,12},{12,8},{16,20},{20,16},{24,28},{28,24},{1,5},{5... | collective-permute-start | bytes 884744 | tf_op jit(solution)/shard_map/ppermute | solution.py:447
  228.6 6.8 %collective-permute-start.29 = (bf16[64,2304]{1,0:T(8,128)(2,1)S(1)}, bf16[64,2304]{1,0:T(8,128)(2,1)S(1)}, u32[]{:S(2)}, u32[]{:S(2)}) collective-permute-start(bf16[64,2304]{1,0:T(8,128)(2,1)S(1)} %get-tuple-element.66), channel_id=1, source_target_pairs={{0,8},{4,12},{8,0},{12,4},{16,24},{20,28},{24,16},{28,20},{1,9},{5... | collective-permute-start | bytes 884744 | tf_op jit(solution)/shard_map/ppermute | solution.py:447
  (2 other events, 1.5 us)

commit v12 on v11

--- a/solution.py
+++ b/solution.py
@@ -269,9 +269,8 @@
 
 
 def select_kernel(local, rows_dev, count, bases_ref, *refs):
-    piece_refs, (own_hbm, sib_ref, facts_ref, own_ref, own_sem) = refs[:count], refs[-5:]
+    piece_refs, (own_ref, sib_ref, facts_ref) = refs[:count], refs[-3:]
     width = own_ref.shape[2]
-    own_copies = []
     tokens, rows = 4 * rows_dev, 4 * CAP
     shift = lax.broadcasted_iota(jnp.int32, (1, tokens), 1) // rows_dev * CAP
     row_id = lax.broadcasted_iota(jnp.int32, (rows, tokens), 0)
@@ -290,13 +289,6 @@
         for e in range(local):
             own_ref[e, g * rows : (g + 1) * rows, :] = chosen[e * rows : (e + 1) * rows]
             sib_ref[e, g * rows : (g + 1) * rows, :] = chosen[(local + e) * rows : (local + e + 1) * rows]
-        for e in range(local):
-            here = (e, pl.ds(g * rows, rows), slice(None))
-            copy = pltpu.make_async_copy(own_ref.at[here], own_hbm.at[here], own_sem.at[g * local + e])
-            copy.start()
-            own_copies.append(copy)
-    for copy in own_copies:
-        copy.wait()
 
 
 def select_rows(pieces, bases, local, waits=()):
@@ -311,11 +303,7 @@
         in_specs=[pl.BlockSpec(memory_space=pltpu.SMEM)]
         + [vmem] * len(pieces)
         + [pl.BlockSpec(memory_space=pl.ANY)] * len(waits),
-        out_specs=(pl.BlockSpec(memory_space=pl.ANY), vmem, vmem),
-        scratch_shapes=[
-            pltpu.VMEM(out.shape, jnp.bfloat16),
-            pltpu.SemaphoreType.DMA((len(pieces) // 4 * local,)),
-        ],
+        out_specs=(vmem, vmem, vmem),
         compiler_params=pltpu.CompilerParams(vmem_limit_bytes=20 * MIB),
         cost_estimate=pl.CostEstimate(
             flops=16 * local * CAP * rows_dev * len(pieces) * width,
@@ -325,12 +313,10 @@
     )(bases, *pieces, *waits)
 
 
-def rows_kernel(local, waits, own_hbm, got_ref, wg_hbm, wu_hbm, wd_hbm, *rest):
-    y_own_ref, y_sib_ref, ended_ref, own_ref, wg, wu, wd, own_sem, weight_sem = rest[waits:]
+def rows_kernel(local, waits, own_ref, got_ref, wg_hbm, wu_hbm, wd_hbm, *rest):
+    y_own_ref, y_sib_ref, ended_ref, wg, wu, wd, weight_sem = rest[waits:]
     ended_ref[...] = jnp.zeros_like(ended_ref)
     half = got_ref.shape[1]
-    own_copy = pltpu.make_async_copy(own_hbm, own_ref, own_sem)
-    own_copy.start()
     copies = [
         [
             pltpu.make_async_copy(source.at[e], target.at[e], weight_sem.at[3 * e + i])
@@ -341,7 +327,6 @@
     for group in copies:
         for copy in group:
             copy.start()
-    own_copy.wait()
     for e in range(local):
         rows = jnp.concatenate([own_ref[e], got_ref[e]], axis=0)
         copies[e][0].wait()
@@ -364,18 +349,16 @@
     return pl.pallas_call(
         functools.partial(rows_kernel, local, len(waits)),
         out_shape=(out, out, jax.ShapeDtypeStruct((8, 128), jnp.float32)),
-        in_specs=[pl.BlockSpec(memory_space=pl.ANY), vmem]
+        in_specs=[vmem, vmem]
         + [pl.BlockSpec(memory_space=pl.ANY)] * (3 + len(waits)),
         out_specs=(vmem, vmem, vmem),
         scratch_shapes=[
-            pltpu.VMEM(own.shape, jnp.bfloat16),
             weights,
             weights,
             weights,
-            pltpu.SemaphoreType.DMA,
             pltpu.SemaphoreType.DMA((3 * local,)),
         ],
-        compiler_params=pltpu.CompilerParams(vmem_limit_bytes=46 * MIB),
+        compiler_params=pltpu.CompilerParams(vmem_limit_bytes=44 * MIB),
         cost_estimate=pl.CostEstimate(
             flops=6 * local * rows * width * hidden,
             bytes_accessed=6 * local * width * hidden + 4 * local * rows * width,
@@ -492,14 +475,20 @@
     single = [[over[way](starts[k]) for way in ways[k]] for k in range(2)]
     starts[2] = hold(starts[2], single[0] + single[1])
     single.append([over[way](starts[2]) for way in ways[2]])
-    starts.append(hold(z(starts[2], 1), single[2]))
+
+    def both(k):
+        return over[ways[k][1]](single[k][0])
+
+    double = [both(0), both(1)]
+    starts.append(hold(z(starts[2], 1), double))
     single.append([over[way](starts[3]) for way in ways[3]])
+    double += [both(2), both(3)]
 
     def gather(k):
         near = []
         for i in (k, k + 1):
             by_f, by_g = single[i]
-            near += [starts[i], by_g, by_f, over[ways[i][1]](by_f)]
+            near += [starts[i], by_g, by_f, double[i]]
         return near
 
     near_b, near_a = gather(0), gather(2)

time: 237 us -> 225 us (0.949)
  waiting for transfers between devices: 116 us -> 106 us
  starting transfers between devices: 45.4 us -> 49.9 us
  Pallas kernels: 61.1 us -> 58 us
  local copies, waits for them, and re-layouts: 11 us -> 8.59 us
    ppermute x30, waiting for transfers between devices: 79.9 us -> 69.2 us  [swap(): return lax.ppermute(a, axis, [(i, i ^ distance) for i in range(size)])]
    ppermute x30, starting transfers between devices: 30.8 us -> 35.3 us  [swap(): return lax.ppermute(a, axis, [(i, i ^ distance) for i in range(size)])]
    pallas_call x2, Pallas kernels: 9.87 us -> 7.3 us  [select_rows(): pl.pallas_call(functools.partial(select_kernel, local, rows_dev, len(piec...]
    unnamed x35 -> x39, local copies, waits for them, and re-layouts: 8.03 us -> 5.63 us
  transfers between devices with their start and end apart: 33 -> 33, of which waited for: 24 -> 23; matrix products, arithmetic and copies ran while one was open for 1% -> 1% of each run, Pallas kernels for 20% -> 21%
where the time goes in v12:
time: 225 us
  waiting for transfers between devices  106 us (47%)
  Pallas kernels  58 us (26%)
  starting transfers between devices  49.9 us (22%)
  local copies, waits for them, and re-layouts  8.59 us (4%)
    ppermute x30, waiting for transfers between devices, swap(): return lax.ppermute(a, axis, [(i, i ^ distance) for i in range(size)])  69.2 us
    ppermute x30, starting transfers between devices, swap(): return lax.ppermute(a, axis, [(i, i ^ distance) for i in range(size)])  35.3 us
    pallas_call x2, Pallas kernels, expert_rows(): pl.pallas_call(functools.partial(rows_kernel, local, len(waits)), out_sha...  31.7 us
    all_to_all x1, waiting for transfers between devices, body(): lax.all_to_all(packed, 'seq', split_axis=0, concat_axis=0, tiled=True)  25.3 us
    all_to_all x1, waiting for transfers between devices, body(): lax.all_to_all(context.reshape(n_seq, rows_dev, span), 'seq', split_axis=...  11.1 us
    pallas_call x2, Pallas kernels, put_rows(): pl.pallas_call(functools.partial(put_kernel, local, rows_dev, planes, len...  8.42 us
    pallas_call x2, Pallas kernels, select_rows(): pl.pallas_call(functools.partial(select_kernel, local, rows_dev, len(piec...  7.3 us
    all_to_all x1, starting transfers between devices, body(): lax.all_to_all(packed, 'seq', split_axis=0, concat_axis=0, tiled=True)  7.25 us
  transfers between devices with their start and end apart: 33, of which 23 were waited for; matrix products, arithmetic and copies ran while one was open for 1% of the time, Pallas kernels for 21%

profile of v12, /device:TPU:0, one launch (start us, length us, event | category | flops | bytes accessed | tf_op | source)
XLA Modules:
  0.0 224.5 jit_solution(12400908473027106017)
XLA Ops:
  0.6 2.3 %fusion.3 = (bf16[1,64,1,2304]{3,2,1,0:T(2,128)(2,1)S(1)}, bf16[1,64,1,2304]{3,2,1,0:T(2,128)(2,1)S(1)}) fusion(bf16[1,64,2,2304]{3,2,1,0:T(2,128)(2,1)} %param.12), kind=kLoop, calls=%fused_computation.14 | loop fusion | bytes 1179648 | tf_op jit(solution)/shard_map/slice | solution.py:545
  3.1 1.2 shard_map.122
  4.3 7.3 %all-to-all-start = ((bf16[8,64,960]{2,1,0:T(8,128)(2,1)}), bf16[8,64,960]{2,1,0:T(8,128)(2,1)S(1)}, u32[]{:S(2)}, u32[]{:S(2)}) async-start(bf16[8,64,960]{2,1,0:T(8,128)(2,1)} %shard_map.122), calls=%async_computation | async-start | bytes 2097152 | tf_op jit(solution)/shard_map/all_to_all | solution.py:548
  12.0 25.3 %all-to-all-done = bf16[8,64,960]{2,1,0:T(8,128)(2,1)S(1)} async-done(((bf16[8,64,960]{2,1,0:T(8,128)(2,1)}), bf16[8,64,960]{2,1,0:T(8,128)(2,1)S(1)}, u32[]{:S(2)}, u32[]{:S(2)}) %all-to-all-start) | async-done | bytes 983072 | tf_op jit(solution)/shard_map/all_to_all | solution.py:548
  37.3 5.6 %shard_map.123 = bf16[512,320]{1,0:T(8,128)(2,1)} custom-call(bf16[512,960]{1,0:T(8,128)(2,1)S(1)} %bitcast.22, s32[1,512]{1,0:T(1,128)S(1)} %copy-done.6, s32[512,1]{1,0:T(8,128)S(1)} %copy.40.seg_col_ref), custom_call_target="tpu_custom_call" | custom-call | flops 335544320 | bytes 1310720 | tf_op jit(solution)/shard_map/pallas_call | solution.py:56
  42.9 3.6 %all-to-all-start.1 = ((bf16[8,64,320]{2,1,0:T(8,128)(2,1)}), bf16[8,64,320]{2,1,0:T(8,128)(2,1)S(1)}, u32[]{:S(2)}, u32[]{:S(2)}) async-start(bf16[8,64,320]{2,1,0:T(8,128)(2,1)} %bitcast.5), calls=%async_computation.1 | async-start | bytes 786432 | tf_op jit(solution)/shard_map/all_to_all | solution.py:551
  47.3 11.1 %all-to-all-done.1.context_ref = bf16[8,64,320]{2,1,0:T(8,128)(2,1)S(1)} async-done(((bf16[8,64,320]{2,1,0:T(8,128)(2,1)}), bf16[8,64,320]{2,1,0:T(8,128)(2,1)S(1)}, u32[]{:S(2)}, u32[]{:S(2)}) %all-to-all-start.1) | async-done | bytes 327712 | tf_op jit(solution)/shard_map/all_to_all | solution.py:551
  60.3 1.9 collective-permute-start.7
  62.2 1.5 collective-permute-start
  63.8 7.1 %collective-permute-done.3.refs_4_ = bf16[64,2432]{1,0:T(8,128)(2,1)S(1)} collective-permute-done((bf16[64,2432]{1,0:T(8,128)(2,1)S(1)}, bf16[64,2432]{1,0:T(8,128)(2,1)S(1)}, u32[]{:S(2)}, u32[]{:S(2)}) %collective-permute-start.3) | collective-permute-done | bytes 311328 | tf_op jit(solution)/shard_map/ppermute | solution.py:430
  70.9 1.5 collective-permute-start.5
  72.4 3.9 %collective-permute-start.4 = (bf16[64,2432]{1,0:T(8,128)(2,1)S(1)}, bf16[64,2432]{1,0:T(8,128)(2,1)S(1)}, u32[]{:S(2)}, u32[]{:S(2)}) collective-permute-start(bf16[64,2432]{1,0:T(8,128)(2,1)S(1)} %collective-permute-done.3.refs_4_), channel_id=1, source_target_pairs={{0,4},{4,0},{8,12},{12,8},{16,20},{20,16},{24,28},{28,24},{1,5},{5... | collective-permute-start | bytes 933896 | tf_op jit(solution)/shard_map/ppermute | solution.py:430
  76.8 1.5 collective-permute-done.5.refs_3_.refs_6_
  78.3 4.1 %collective-permute-done.4.refs_4_.refs_5_ = bf16[64,2432]{1,0:T(8,128)(2,1)S(1)} collective-permute-done((bf16[64,2432]{1,0:T(8,128)(2,1)S(1)}, bf16[64,2432]{1,0:T(8,128)(2,1)S(1)}, u32[]{:S(2)}, u32[]{:S(2)}) %collective-permute-start.4) | collective-permute-done | bytes 311328 | tf_op jit(solution)/shard_map/ppermute | solution.py:430
  82.5 2.7 %collective-permute-start.6 = (bf16[64,2432]{1,0:T(8,128)(2,1)S(1)}, bf16[64,2432]{1,0:T(8,128)(2,1)S(1)}, u32[]{:S(2)}, u32[]{:S(2)}) collective-permute-start(bf16[64,2432]{1,0:T(8,128)(2,1)S(1)} %collective-permute-done.5.refs_3_.refs_6_), channel_id=1, source_target_pairs={{0,4},{4,0},{8,12},{12,8},{16,20},{20,16},{24,28},{28,24},{1,5},{5... | collective-permute-start | bytes 933896 | tf_op jit(solution)/shard_map/ppermute | solution.py:430
  85.3 4.5 %collective-permute-done.11.refs_0_ = bf16[64,2432]{1,0:T(8,128)(2,1)} collective-permute-done((bf16[64,2432]{1,0:T(8,128)(2,1)S(1)}, bf16[64,2432]{1,0:T(8,128)(2,1)}, u32[]{:S(2)}, u32[]{:S(2)}) %collective-permute-start.11) | collective-permute-done | bytes 311328 | tf_op jit(solution)/shard_map/ppermute | solution.py:430
  89.8 3.7 %collective-permute-done.6.refs_2_.refs_7_ = bf16[64,2432]{1,0:T(8,128)(2,1)S(1)} collective-permute-done((bf16[64,2432]{1,0:T(8,128)(2,1)S(1)}, bf16[64,2432]{1,0:T(8,128)(2,1)S(1)}, u32[]{:S(2)}, u32[]{:S(2)}) %collective-permute-start.6) | collective-permute-done | bytes 311328 | tf_op jit(solution)/shard_map/ppermute | solution.py:430
  93.5 1.5 collective-permute-start.13
  95.5 2.0 collective-permute-start.12
  97.5 2.7 %collective-permute-done.9.refs_2_ = bf16[64,2432]{1,0:T(8,128)(2,1)} collective-permute-done((bf16[64,2432]{1,0:T(8,128)(2,1)S(1)}, bf16[64,2432]{1,0:T(8,128)(2,1)}, u32[]{:S(2)}, u32[]{:S(2)}) %collective-permute-start.9) | collective-permute-done | bytes 311328 | tf_op jit(solution)/shard_map/ppermute | solution.py:430
  100.2 1.5 collective-permute-start.10
  101.8 1.4 collective-permute-done.13.refs_6_
  104.3 2.2 collective-permute-done.8.refs_1_
  106.5 3.3 %collective-permute-done.10.refs_3_ = bf16[64,2432]{1,0:T(8,128)(2,1)} collective-permute-done((bf16[64,2432]{1,0:T(8,128)(2,1)}, bf16[64,2432]{1,0:T(8,128)(2,1)}, u32[]{:S(2)}, u32[]{:S(2)}) %collective-permute-start.10) | collective-permute-done | bytes 311328 | tf_op jit(solution)/shard_map/ppermute | solution.py:430
  110.4 4.2 %shard_map.127 = (bf16[2,192,2304]{2,1,0:T(8,128)(2,1)S(1)}, bf16[2,192,2304]{2,1,0:T(8,128)(2,1)}, bf16[512,128]{1,0:T(8,128)(2,1)S(1)}) custom-call(s32[2]{0:T(128)S(1)} %add_multiply_fusion.bases_ref, bf16[64,2432]{1,0:T(8,128)(2,1)S(1)} %shard_map.125.refs_0_, bf16[64,2432]{1,0:T(8,128)(2,1)} %collective-permute-done.8.refs_1_, ...), custom_call_target="tpu_custom_call" | custom-call | flops 905969664 | bytes 6029312 | tf_op jit(solution)/shard_map/pallas_call | solution.py:300
  114.6 1.2 copy-done.13
  115.9 1.7 shard_map.128.refs_8_.rest_1_
  117.6 3.1 %shard_map.129 = (bf16[2,192,2304]{2,1,0:T(8,128)(2,1)S(1)}, bf16[2,192,2304]{2,1,0:T(8,128)(2,1)}, bf16[512,128]{1,0:T(8,128)(2,1)S(1)}) custom-call(s32[2]{0:T(128)S(1)} %add_multiply_fusion.bases_ref, bf16[64,2432]{1,0:T(8,128)(2,1)S(1)} %copy-done.8, bf16[64,2432]{1,0:T(8,128)(2,1)S(1)} %collective-permute-done.refs_2_.refs_1_, ...), custom_call_target="tpu_custom_call" | custom-call | flops 905969664 | bytes 6029312 | tf_op jit(solution)/shard_map/pallas_call | solution.py:300
  120.7 1.3 copy-done.11
  122.5 3.7 %all-to-all-start.2 = ((bf16[8,64,640]{2,1,0:T(8,128)(2,1)}), bf16[8,64,640]{2,1,0:T(8,128)(2,1)S(1)}, u32[]{:S(2)}, u32[]{:S(2)}) async-start(bf16[8,64,640]{2,1,0:T(8,128)(2,1)} %shard_map.128.refs_8_.rest_1_), calls=%async_computation.2 | async-start | bytes 1310720 | tf_op jit(solution)/shard_map/all_to_all | solution.py:568
  126.3 1.5 copy-done.14
  127.7 16.4 %shard_map.130 = (bf16[2,192,2304]{2,1,0:T(8,128)(2,1)S(1)}, bf16[2,192,2304]{2,1,0:T(8,128)(2,1)}, f32[8,128]{1,0:T(8,128)S(1)}) custom-call(bf16[2,192,2304]{2,1,0:T(8,128)(2,1)S(1)} %copy-done.14, bf16[2,192,2304]{2,1,0:T(8,128)(2,1)} %collective-permute-done.16.got_ref, bf16[2,720,2304]{2,1,0:T(8,128)(2,1)} %bitcast.28, bf16[2,720,2304]{2,1,0:T(8,128)(2,1)} %bitcast.30, ...), custom_call_target="tpu_custom_call" | custom-call | flops 7644119040 | bytes 26984448 | tf_op jit(solution)/shard_map/pallas_call | solution.py:349
  145.2 1.5 copy-done.12
  146.7 15.3 %shard_map.132 = (bf16[2,192,2304]{2,1,0:T(8,128)(2,1)S(1)}, bf16[2,192,2304]{2,1,0:T(8,128)(2,1)S(1)}, f32[8,128]{1,0:T(8,128)S(1)}) custom-call(bf16[2,192,2304]{2,1,0:T(8,128)(2,1)S(1)} %copy-done.12, bf16[2,192,2304]{2,1,0:T(8,128)(2,1)} %collective-permute-done.15.got_ref, bf16[2,720,2304]{2,1,0:T(8,128)(2,1)} %bitcast.29, ...), custom_call_target="tpu_custom_call" | custom-call | flops 7644119040 | bytes 26984448 | tf_op jit(solution)/shard_map/pallas_call | solution.py:349
  162.6 4.9 %shard_map.133 = (bf16[256,2304]{1,0:T(8,128)(2,1)S(1)}, bf16[128,2304]{1,0:T(8,128)(2,1)S(1)}, bf16[128,2304]{1,0:T(8,128)(2,1)S(1)}, f32[8,128]{1,0:T(8,128)}) custom-call(s32[2]{0:T(128)S(1)} %add_multiply_fusion.bases_ref, bf16[2,192,2304]{2,1,0:T(8,128)(2,1)S(1)} %get-tuple-element.47.y_own_ref, ...), custom_call_target="tpu_custom_call" | custom-call | flops 905969664 | bytes 18874368 | tf_op jit(solution)/shard_map/pallas_call | solution.py:411
  167.4 2.0 collective-permute-start.19
  170.4 12.6 %collective-permute-done.19.rest_0_ = bf16[128,2304]{1,0:T(8,128)(2,1)S(1)} collective-permute-done((bf16[128,2304]{1,0:T(8,128)(2,1)S(1)}, bf16[128,2304]{1,0:T(8,128)(2,1)S(1)}, u32[]{:S(2)}, u32[]{:S(2)}) %collective-permute-start.19) | collective-permute-done | bytes 589856 | tf_op jit(solution)/shard_map/ppermute | solution.py:430
  183.0 1.5 collective-permute-done.20.rest_1_
  186.0 3.6 %shard_map.135 = (bf16[256,2304]{1,0:T(8,128)(2,1)S(1)}, bf16[128,2304]{1,0:T(8,128)(2,1)S(1)}, bf16[128,2304]{1,0:T(8,128)(2,1)S(1)}, f32[8,128]{1,0:T(8,128)S(1)}) custom-call(s32[2]{0:T(128)S(1)} %add_multiply_fusion.bases_ref, bf16[2,192,2304]{2,1,0:T(8,128)(2,1)S(1)} %get-tuple-element.45.y_own_ref, ...), custom_call_target="tpu_custom_call" | custom-call | flops 905969664 | bytes 18874368 | tf_op jit(solution)/shard_map/pallas_call | solution.py:411
  189.5 3.0 %collective-permute-done.21.refs_1_.rest_0_ = bf16[64,2304]{1,0:T(8,128)(2,1)S(1)} collective-permute-done((bf16[64,2304]{1,0:T(8,128)(2,1)S(1)}, bf16[64,2304]{1,0:T(8,128)(2,1)S(1)}, u32[]{:S(2)}, u32[]{:S(2)}) %collective-permute-start.21) | collective-permute-done | bytes 294944 | tf_op jit(solution)/shard_map/ppermute | solution.py:430
  193.3 1.5 collective-permute-start.25
  196.6 3.5 %collective-permute-done.25 = bf16[64,2304]{1,0:T(8,128)(2,1)S(1)} collective-permute-done((bf16[64,2304]{1,0:T(8,128)(2,1)S(1)}, bf16[64,2304]{1,0:T(8,128)(2,1)S(1)}, u32[]{:S(2)}, u32[]{:S(2)}) %collective-permute-start.25) | collective-permute-done | bytes 294944 | tf_op jit(solution)/shard_map/ppermute | solution.py:430
  200.2 3.1 %collective-permute-start.28 = (bf16[64,2304]{1,0:T(8,128)(2,1)S(1)}, bf16[64,2304]{1,0:T(8,128)(2,1)S(1)}, u32[]{:S(2)}, u32[]{:S(2)}) collective-permute-start(bf16[64,2304]{1,0:T(8,128)(2,1)S(1)} %add_convert_fusion.1.rest_2_), channel_id=1, source_target_pairs={{0,16},{4,20},{8,24},{12,28},{16,0},{20,4},{24,8},{28,12},{1,17},{... | collective-permute-start | bytes 884744 | tf_op jit(solution)/shard_map/ppermute | solution.py:430
  203.3 4.2 %collective-permute-done.23.rest_0_ = bf16[128,2304]{1,0:T(8,128)(2,1)S(1)} collective-permute-done((bf16[128,2304]{1,0:T(8,128)(2,1)S(1)}, bf16[128,2304]{1,0:T(8,128)(2,1)S(1)}, u32[]{:S(2)}, u32[]{:S(2)}) %collective-permute-start.23) | collective-permute-done | bytes 589856 | tf_op jit(solution)/shard_map/ppermute | solution.py:430
  210.0 1.4 collective-permute-start.27
  211.5 1.4 collective-permute-done.28.rest_2_
  212.9 2.8 %collective-permute-done.26.rest_0_ = bf16[64,2304]{1,0:T(8,128)(2,1)S(1)} collective-permute-done((bf16[64,2304]{1,0:T(8,128)(2,1)S(1)}, bf16[64,2304]{1,0:T(8,128)(2,1)S(1)}, u32[]{:S(2)}, u32[]{:S(2)}) %collective-permute-start.26) | collective-permute-done | bytes 294944 | tf_op jit(solution)/shard_map/ppermute | solution.py:430
  217.5 6.2 %collective-permute-done.29 = bf16[64,2304]{1,0:T(8,128)(2,1)S(1)} collective-permute-done((bf16[64,2304]{1,0:T(8,128)(2,1)S(1)}, bf16[64,2304]{1,0:T(8,128)(2,1)S(1)}, u32[]{:S(2)}, u32[]{:S(2)}) %collective-permute-start.29) | collective-permute-done | bytes 294944 | tf_op jit(solution)/shard_map/ppermute | solution.py:430
  (94 shorter events, 18.5 us)
Async XLA Ops:
  0.6 2.4 %copy-start.5 = (bf16[1,64,2304]{2,1,0:T(8,128)(2,1)S(1)}, bf16[1,64,2304]{2,1,0:T(8,128)(2,1)}, u32[]{:S(2)}) copy-start(bf16[1,64,2304]{2,1,0:T(8,128)(2,1)} %param.11) | copy-start | bytes 884740
  3.0 8.5 %copy-start.6 = (s32[1,512]{1,0:T(1,128)S(1)}, s32[1,512]{1,0:T(1,128)}, u32[]{:S(2)}) copy-start(s32[1,512]{1,0:T(1,128)} %seg_row_ref.1) | copy-start | bytes 6148
  3.0 8.7 %copy-start.15 = (bf16[2304]{0:T(1024)(128)(2,1)S(1)}, bf16[2304]{0:T(1024)(128)(2,1)}, u32[]{:S(2)}) copy-start(bf16[2304]{0:T(1024)(128)(2,1)} %param.14) | copy-start | bytes 13828
  3.1 8.7 %copy-start.16 = (s32[1,64,2]{1,2,0:T(2,128)S(1)}, s32[1,64,2]{1,2,0:T(2,128)}, u32[]{:S(2)}) copy-start(s32[1,64,2]{1,2,0:T(2,128)} %param.16) | copy-start | bytes 1540
  4.3 33.0 %all-to-all-start = ((bf16[8,64,960]{2,1,0:T(8,128)(2,1)}), bf16[8,64,960]{2,1,0:T(8,128)(2,1)S(1)}, u32[]{:S(2)}, u32[]{:S(2)}) async-start(bf16[8,64,960]{2,1,0:T(8,128)(2,1)} %shard_map.122), calls=%async_computation | async-start | bytes 2097152 | tf_op jit(solution)/shard_map/all_to_all | solution.py:548
  37.3 9.9 %copy-start.17 = (f32[1,64,2]{1,2,0:T(2,128)S(1)}, f32[1,64,2]{1,2,0:T(2,128)}, u32[]{:S(2)}) copy-start(f32[1,64,2]{1,2,0:T(2,128)} %param.17) | copy-start | bytes 1540
  37.3 21.1 %copy-start.4 = (bf16[1,64,2304]{2,1,0:T(8,128)(2,1)S(1)}, bf16[1,64,2304]{2,1,0:T(8,128)(2,1)}, u32[]{:S(2)}) copy-start(bf16[1,64,2304]{2,1,0:T(8,128)(2,1)} %param.13) | copy-start | bytes 884740
  42.9 15.5 %all-to-all-start.1 = ((bf16[8,64,320]{2,1,0:T(8,128)(2,1)}), bf16[8,64,320]{2,1,0:T(8,128)(2,1)S(1)}, u32[]{:S(2)}, u32[]{:S(2)}) async-start(bf16[8,64,320]{2,1,0:T(8,128)(2,1)} %bitcast.5), calls=%async_computation.1 | async-start | bytes 786432 | tf_op jit(solution)/shard_map/all_to_all | solution.py:551
  58.7 44.5 %copy-start.7 = (bf16[64,2432]{1,0:T(8,128)(2,1)}, bf16[64,2432]{1,0:T(8,128)(2,1)S(1)}, u32[]{:S(2)}) copy-start(bf16[64,2432]{1,0:T(8,128)(2,1)S(1)} %get-tuple-element.36.refs_0_) | copy-start | bytes 933892
  58.7 12.2 %collective-permute-start.3 = (bf16[64,2432]{1,0:T(8,128)(2,1)S(1)}, bf16[64,2432]{1,0:T(8,128)(2,1)S(1)}, u32[]{:S(2)}, u32[]{:S(2)}) collective-permute-start(bf16[64,2432]{1,0:T(8,128)(2,1)S(1)} %get-tuple-element.36.refs_0_), channel_id=1, source_target_pairs={{0,8},{4,12},{8,0},{12,4},{16,24},{20,28},{24,16},{28,20},{1,9},{5... | collective-permute-start | bytes 933896 | tf_op jit(solution)/shard_map/ppermute | solution.py:430
  59.7 16.6 %collective-permute-start.1 = (bf16[64,2432]{1,0:T(8,128)(2,1)S(1)}, bf16[64,2432]{1,0:T(8,128)(2,1)S(1)}, u32[]{:S(2)}, u32[]{:S(2)}) collective-permute-start(bf16[64,2432]{1,0:T(8,128)(2,1)S(1)} %get-tuple-element.36.refs_0_), channel_id=1, source_target_pairs={{0,4},{4,0},{8,12},{12,8},{16,20},{20,16},{24,28},{28,24},{1,5},{5... | collective-permute-start | bytes 933896 | tf_op jit(solution)/shard_map/ppermute | solution.py:430
  60.3 16.5 %collective-permute-start.7 = (bf16[64,2432]{1,0:T(8,128)(2,1)S(1)}, bf16[64,2432]{1,0:T(8,128)(2,1)S(1)}, u32[]{:S(2)}, u32[]{:S(2)}) collective-permute-start(bf16[64,2432]{1,0:T(8,128)(2,1)S(1)} %get-tuple-element.36.refs_0_), channel_id=1, source_target_pairs={{0,16},{4,20},{8,24},{12,28},{16,0},{20,4},{24,8},{28,12},{1,17},{... | collective-permute-start | bytes 933896 | tf_op jit(solution)/shard_map/ppermute | solution.py:430
  62.2 14.6 %collective-permute-start = (bf16[64,2432]{1,0:T(8,128)(2,1)S(1)}, bf16[64,2432]{1,0:T(8,128)(2,1)S(1)}, u32[]{:S(2)}, u32[]{:S(2)}) collective-permute-start(bf16[64,2432]{1,0:T(8,128)(2,1)S(1)} %get-tuple-element.36.refs_0_), channel_id=1, source_target_pairs={{0,2},{1,3},{2,0},{3,1},{4,6},{5,7},{6,4},{7,5},{8,10},{9,11},{10,... | collective-permute-start | bytes 933896 | tf_op jit(solution)/shard_map/ppermute | solution.py:430
  70.9 11.6 %copy-start.9 = (bf16[64,2432]{1,0:T(8,128)(2,1)}, bf16[64,2432]{1,0:T(8,128)(2,1)S(1)}, u32[]{:S(2)}) copy-start(bf16[64,2432]{1,0:T(8,128)(2,1)S(1)} %collective-permute-done.3.refs_4_) | copy-start | bytes 933892
  70.9 7.4 %collective-permute-start.5 = (bf16[64,2432]{1,0:T(8,128)(2,1)S(1)}, bf16[64,2432]{1,0:T(8,128)(2,1)S(1)}, u32[]{:S(2)}, u32[]{:S(2)}) collective-permute-start(bf16[64,2432]{1,0:T(8,128)(2,1)S(1)} %collective-permute-done.3.refs_4_), channel_id=1, source_target_pairs={{0,2},{1,3},{2,0},{3,1},{4,6},{5,7},{6,4},{7,5},{8,10},{9,11},{10,... | collective-permute-start | bytes 933896 | tf_op jit(solution)/shard_map/ppermute | solution.py:430
  72.4 10.0 %collective-permute-start.4 = (bf16[64,2432]{1,0:T(8,128)(2,1)S(1)}, bf16[64,2432]{1,0:T(8,128)(2,1)S(1)}, u32[]{:S(2)}, u32[]{:S(2)}) collective-permute-start(bf16[64,2432]{1,0:T(8,128)(2,1)S(1)} %collective-permute-done.3.refs_4_), channel_id=1, source_target_pairs={{0,4},{4,0},{8,12},{12,8},{16,20},{20,16},{24,28},{28,24},{1,5},{5... | collective-permute-start | bytes 933896 | tf_op jit(solution)/shard_map/ppermute | solution.py:430
  76.3 8.9 %collective-permute-start.2 = (bf16[64,2432]{1,0:T(8,128)(2,1)S(1)}, bf16[64,2432]{1,0:T(8,128)(2,1)S(1)}, u32[]{:S(2)}, u32[]{:S(2)}) collective-permute-start(bf16[64,2432]{1,0:T(8,128)(2,1)S(1)} %collective-permute-done.1.refs_1_.refs_2_), channel_id=1, source_target_pairs={{0,2},{1,3},{2,0},{3,1},{4,6},{5,7},{6,4},{7,5},{8,10},{9,11},{10,... | collective-permute-start | bytes 933896 | tf_op jit(solution)/shard_map/ppermute | solution.py:430
  82.5 7.3 %collective-permute-start.11 = (bf16[64,2432]{1,0:T(8,128)(2,1)S(1)}, bf16[64,2432]{1,0:T(8,128)(2,1)}, u32[]{:S(2)}, u32[]{:S(2)}) collective-permute-start(bf16[64,2432]{1,0:T(8,128)(2,1)S(1)} %shard_map.125.refs_0_), channel_id=1, source_target_pairs={{0,8},{4,12},{8,0},{12,4},{16,24},{20,28},{24,16},{28,20},{1,9},{5... | collective-permute-start | bytes 933896 | tf_op jit(solution)/shard_map/ppermute | solution.py:430
  82.5 11.0 %collective-permute-start.6 = (bf16[64,2432]{1,0:T(8,128)(2,1)S(1)}, bf16[64,2432]{1,0:T(8,128)(2,1)S(1)}, u32[]{:S(2)}, u32[]{:S(2)}) collective-permute-start(bf16[64,2432]{1,0:T(8,128)(2,1)S(1)} %collective-permute-done.5.refs_3_.refs_6_), channel_id=1, source_target_pairs={{0,4},{4,0},{8,12},{12,8},{16,20},{20,16},{24,28},{28,24},{1,5},{5... | collective-permute-start | bytes 933896 | tf_op jit(solution)/shard_map/ppermute | solution.py:430
  85.2 15.1 %collective-permute-start.9 = (bf16[64,2432]{1,0:T(8,128)(2,1)S(1)}, bf16[64,2432]{1,0:T(8,128)(2,1)}, u32[]{:S(2)}, u32[]{:S(2)}) collective-permute-start(bf16[64,2432]{1,0:T(8,128)(2,1)S(1)} %shard_map.125.refs_0_), channel_id=1, source_target_pairs={{0,4},{4,0},{8,12},{12,8},{16,20},{20,16},{24,28},{28,24},{1,5},{5... | collective-permute-start | bytes 933896 | tf_op jit(solution)/shard_map/ppermute | solution.py:430
  85.3 15.0 %copy-start = (bf16[64,2432]{1,0:T(8,128)(2,1)}, bf16[64,2432]{1,0:T(8,128)(2,1)S(1)}, u32[]{:S(2)}) copy-start(bf16[64,2432]{1,0:T(8,128)(2,1)S(1)} %collective-permute-done.2.refs_1_.refs_3_) | copy-start | bytes 933892
  93.5 8.3 %copy-start.2 = (bf16[64,2432]{1,0:T(8,128)(2,1)}, bf16[64,2432]{1,0:T(8,128)(2,1)S(1)}, u32[]{:S(2)}) copy-start(bf16[64,2432]{1,0:T(8,128)(2,1)S(1)} %collective-permute-done.6.refs_2_.refs_7_) | copy-start | bytes 933892
  93.5 22.3 %copy-start.18 = (s32[1,32]{1,0:T(1,128)S(1)}, s32[1,32]{1,0:T(1,128)}, u32[]{:S(2)}) copy-start(s32[1,32]{1,0:T(1,128)} %param.18) | copy-start | bytes 388
  93.5 9.7 %collective-permute-start.13 = (bf16[64,2432]{1,0:T(8,128)(2,1)}, bf16[64,2432]{1,0:T(8,128)(2,1)}, u32[]{:S(2)}, u32[]{:S(2)}) collective-permute-start(bf16[64,2432]{1,0:T(8,128)(2,1)} %shard_map.126.refs_4_), channel_id=1, source_target_pairs={{0,2},{1,3},{2,0},{3,1},{4,6},{5,7},{6,4},{7,5},{8,10},{9,11},{10,... | collective-permute-start | bytes 933896 | tf_op jit(solution)/shard_map/ppermute | solution.py:430
  95.0 11.5 %collective-permute-start.8 = (bf16[64,2432]{1,0:T(8,128)(2,1)S(1)}, bf16[64,2432]{1,0:T(8,128)(2,1)}, u32[]{:S(2)}, u32[]{:S(2)}) collective-permute-start(bf16[64,2432]{1,0:T(8,128)(2,1)S(1)} %shard_map.125.refs_0_), channel_id=1, source_target_pairs={{0,2},{1,3},{2,0},{3,1},{4,6},{5,7},{6,4},{7,5},{8,10},{9,11},{10,... | collective-permute-start | bytes 933896 | tf_op jit(solution)/shard_map/ppermute | solution.py:430
  95.5 14.4 %collective-permute-start.12 = (bf16[64,2432]{1,0:T(8,128)(2,1)}, bf16[64,2432]{1,0:T(8,128)(2,1)}, u32[]{:S(2)}, u32[]{:S(2)}) collective-permute-start(bf16[64,2432]{1,0:T(8,128)(2,1)} %shard_map.126.refs_4_), channel_id=1, source_target_pairs={{0,4},{4,0},{8,12},{12,8},{16,20},{20,16},{24,28},{28,24},{1,5},{5... | collective-permute-start | bytes 933896 | tf_op jit(solution)/shard_map/ppermute | solution.py:430
  100.2 9.6 %collective-permute-start.10 = (bf16[64,2432]{1,0:T(8,128)(2,1)}, bf16[64,2432]{1,0:T(8,128)(2,1)}, u32[]{:S(2)}, u32[]{:S(2)}) collective-permute-start(bf16[64,2432]{1,0:T(8,128)(2,1)} %collective-permute-done.9.refs_2_), channel_id=1, source_target_pairs={{0,2},{1,3},{2,0},{3,1},{4,6},{5,7},{6,4},{7,5},{8,10},{9,11},{10,... | collective-permute-start | bytes 933896 | tf_op jit(solution)/shard_map/ppermute | solution.py:430
  103.2 7.2 %collective-permute-start.14 = (bf16[64,2432]{1,0:T(8,128)(2,1)}, bf16[64,2432]{1,0:T(8,128)(2,1)}, u32[]{:S(2)}, u32[]{:S(2)}) collective-permute-start(bf16[64,2432]{1,0:T(8,128)(2,1)} %collective-permute-done.13.refs_6_), channel_id=1, source_target_pairs={{0,4},{4,0},{8,12},{12,8},{16,20},{20,16},{24,28},{28,24},{1,5},{5... | collective-permute-start | bytes 933896 | tf_op jit(solution)/shard_map/ppermute | solution.py:430
  104.3 13.2 %copy-start.1 = (bf16[64,2432]{1,0:T(8,128)(2,1)S(1)}, bf16[64,2432]{1,0:T(8,128)(2,1)}, u32[]{:S(2)}) copy-start(bf16[64,2432]{1,0:T(8,128)(2,1)} %copy-done) | copy-start | bytes 933892
  104.3 13.2 %copy-start.3 = (bf16[64,2432]{1,0:T(8,128)(2,1)S(1)}, bf16[64,2432]{1,0:T(8,128)(2,1)}, u32[]{:S(2)}) copy-start(bf16[64,2432]{1,0:T(8,128)(2,1)} %copy-done.2) | copy-start | bytes 933892
  104.3 13.2 %copy-start.8 = (bf16[64,2432]{1,0:T(8,128)(2,1)S(1)}, bf16[64,2432]{1,0:T(8,128)(2,1)}, u32[]{:S(2)}) copy-start(bf16[64,2432]{1,0:T(8,128)(2,1)} %copy-done.7) | copy-start | bytes 933892
  104.3 13.2 %copy-start.10 = (bf16[64,2432]{1,0:T(8,128)(2,1)S(1)}, bf16[64,2432]{1,0:T(8,128)(2,1)}, u32[]{:S(2)}) copy-start(bf16[64,2432]{1,0:T(8,128)(2,1)} %copy-done.9) | copy-start | bytes 933892
  115.8 10.5 %collective-permute-start.16 = (bf16[2,192,2304]{2,1,0:T(8,128)(2,1)}, bf16[2,192,2304]{2,1,0:T(8,128)(2,1)}, u32[]{:S(2)}, u32[]{:S(2)}) collective-permute-start(bf16[2,192,2304]{2,1,0:T(8,128)(2,1)} %get-tuple-element.41), channel_id=1, source_target_pairs={{0,1},{1,0},{2,3},{3,2},{4,5},{5,4},{6,7},{7,6},{8,9},{9,8},{10,11... | collective-permute-start | bytes 5308424 | tf_op jit(solution)/shard_map/ppermute | solution.py:430
  122.0 23.2 %collective-permute-start.15 = (bf16[2,192,2304]{2,1,0:T(8,128)(2,1)}, bf16[2,192,2304]{2,1,0:T(8,128)(2,1)}, u32[]{:S(2)}, u32[]{:S(2)}) collective-permute-start(bf16[2,192,2304]{2,1,0:T(8,128)(2,1)} %get-tuple-element.39), channel_id=1, source_target_pairs={{0,1},{1,0},{2,3},{3,2},{4,5},{5,4},{6,7},{7,6},{8,9},{9,8},{10,11... | collective-permute-start | bytes 5308424 | tf_op jit(solution)/shard_map/ppermute | solution.py:430
  122.5 21.7 %all-to-all-start.2 = ((bf16[8,64,640]{2,1,0:T(8,128)(2,1)}), bf16[8,64,640]{2,1,0:T(8,128)(2,1)S(1)}, u32[]{:S(2)}, u32[]{:S(2)}) async-start(bf16[8,64,640]{2,1,0:T(8,128)(2,1)} %shard_map.128.refs_8_.rest_1_), calls=%async_computation.2 | async-start | bytes 1310720 | tf_op jit(solution)/shard_map/all_to_all | solution.py:568
  144.1 18.5 %collective-permute-start.18 = (bf16[2,192,2304]{2,1,0:T(8,128)(2,1)}, bf16[2,192,2304]{2,1,0:T(8,128)(2,1)}, u32[]{:S(2)}, u32[]{:S(2)}) collective-permute-start(bf16[2,192,2304]{2,1,0:T(8,128)(2,1)} %get-tuple-element.48), channel_id=1, source_target_pairs={{0,1},{1,0},{2,3},{3,2},{4,5},{5,4},{6,7},{7,6},{8,9},{9,8},{10,11... | collective-permute-start | bytes 5308424 | tf_op jit(solution)/shard_map/ppermute | solution.py:430
  162.0 23.9 %collective-permute-start.17 = (bf16[2,192,2304]{2,1,0:T(8,128)(2,1)S(1)}, bf16[2,192,2304]{2,1,0:T(8,128)(2,1)S(1)}, u32[]{:S(2)}, u32[]{:S(2)}) collective-permute-start(bf16[2,192,2304]{2,1,0:T(8,128)(2,1)S(1)} %get-tuple-element.46), channel_id=1, source_target_pairs={{0,1},{1,0},{2,3},{3,2},{4,5},{5,4},{6,7},{7,6},{8,9},{9,8},{10,11... | collective-permute-start | bytes 5308424 | tf_op jit(solution)/shard_map/ppermute | solution.py:430
  167.4 15.5 %collective-permute-start.19 = (bf16[128,2304]{1,0:T(8,128)(2,1)S(1)}, bf16[128,2304]{1,0:T(8,128)(2,1)S(1)}, u32[]{:S(2)}, u32[]{:S(2)}) collective-permute-start(bf16[128,2304]{1,0:T(8,128)(2,1)S(1)} %get-tuple-element.51), channel_id=1, source_target_pairs={{0,4},{4,0},{8,12},{12,8},{16,20},{20,16},{24,28},{28,24},{1,5},{5... | collective-permute-start | bytes 1769480 | tf_op jit(solution)/shard_map/ppermute | solution.py:430
  169.4 15.0 %collective-permute-start.20 = (bf16[128,2304]{1,0:T(8,128)(2,1)S(1)}, bf16[128,2304]{1,0:T(8,128)(2,1)S(1)}, u32[]{:S(2)}, u32[]{:S(2)}) collective-permute-start(bf16[128,2304]{1,0:T(8,128)(2,1)S(1)} %get-tuple-element.52), channel_id=1, source_target_pairs={{0,2},{1,3},{2,0},{3,1},{4,6},{5,7},{6,4},{7,5},{8,10},{9,11},{10,... | collective-permute-start | bytes 1769480 | tf_op jit(solution)/shard_map/ppermute | solution.py:430
  184.7 7.8 %collective-permute-start.21 = (bf16[64,2304]{1,0:T(8,128)(2,1)S(1)}, bf16[64,2304]{1,0:T(8,128)(2,1)S(1)}, u32[]{:S(2)}, u32[]{:S(2)}) collective-permute-start(bf16[64,2304]{1,0:T(8,128)(2,1)S(1)} %get-tuple-element.53.rest_0_), channel_id=1, source_target_pairs={{0,2},{1,3},{2,0},{3,1},{4,6},{5,7},{6,4},{7,5},{8,10},{9,11},{10,... | collective-permute-start | bytes 884744 | tf_op jit(solution)/shard_map/ppermute | solution.py:430
  185.7 7.5 %collective-permute-start.22 = (bf16[64,2304]{1,0:T(8,128)(2,1)S(1)}, bf16[64,2304]{1,0:T(8,128)(2,1)S(1)}, u32[]{:S(2)}, u32[]{:S(2)}) collective-permute-start(bf16[64,2304]{1,0:T(8,128)(2,1)S(1)} %get-tuple-element.56), channel_id=1, source_target_pairs={{0,4},{4,0},{8,12},{12,8},{16,20},{20,16},{24,28},{28,24},{1,5},{5... | collective-permute-start | bytes 884744 | tf_op jit(solution)/shard_map/ppermute | solution.py:430
  193.3 6.8 %collective-permute-start.25 = (bf16[64,2304]{1,0:T(8,128)(2,1)S(1)}, bf16[64,2304]{1,0:T(8,128)(2,1)S(1)}, u32[]{:S(2)}, u32[]{:S(2)}) collective-permute-start(bf16[64,2304]{1,0:T(8,128)(2,1)S(1)} %get-tuple-element.61), channel_id=1, source_target_pairs={{0,8},{4,12},{8,0},{12,4},{16,24},{20,28},{24,16},{28,20},{1,9},{5... | collective-permute-start | bytes 884744 | tf_op jit(solution)/shard_map/ppermute | solution.py:430
  194.8 12.6 %collective-permute-start.23 = (bf16[128,2304]{1,0:T(8,128)(2,1)S(1)}, bf16[128,2304]{1,0:T(8,128)(2,1)S(1)}, u32[]{:S(2)}, u32[]{:S(2)}) collective-permute-start(bf16[128,2304]{1,0:T(8,128)(2,1)S(1)} %shard_map.136), channel_id=1, source_target_pairs={{0,4},{4,0},{8,12},{12,8},{16,20},{20,16},{24,28},{28,24},{1,5},{5... | collective-permute-start | bytes 1769480 | tf_op jit(solution)/shard_map/ppermute | solution.py:430
  195.4 13.2 %collective-permute-start.24 = (bf16[128,2304]{1,0:T(8,128)(2,1)S(1)}, bf16[128,2304]{1,0:T(8,128)(2,1)S(1)}, u32[]{:S(2)}, u32[]{:S(2)}) collective-permute-start(bf16[128,2304]{1,0:T(8,128)(2,1)S(1)} %shard_map.137), channel_id=1, source_target_pairs={{0,2},{1,3},{2,0},{3,1},{4,6},{5,7},{6,4},{7,5},{8,10},{9,11},{10,... | collective-permute-start | bytes 1769480 | tf_op jit(solution)/shard_map/ppermute | solution.py:430
  200.2 12.7 %collective-permute-start.28 = (bf16[64,2304]{1,0:T(8,128)(2,1)S(1)}, bf16[64,2304]{1,0:T(8,128)(2,1)S(1)}, u32[]{:S(2)}, u32[]{:S(2)}) collective-permute-start(bf16[64,2304]{1,0:T(8,128)(2,1)S(1)} %add_convert_fusion.1.rest_2_), channel_id=1, source_target_pairs={{0,16},{4,20},{8,24},{12,28},{16,0},{20,4},{24,8},{28,12},{1,17},{... | collective-permute-start | bytes 884744 | tf_op jit(solution)/shard_map/ppermute | solution.py:430
  208.9 6.8 %collective-permute-start.26 = (bf16[64,2304]{1,0:T(8,128)(2,1)S(1)}, bf16[64,2304]{1,0:T(8,128)(2,1)S(1)}, u32[]{:S(2)}, u32[]{:S(2)}) collective-permute-start(bf16[64,2304]{1,0:T(8,128)(2,1)S(1)} %get-tuple-element.63), channel_id=1, source_target_pairs={{0,2},{1,3},{2,0},{3,1},{4,6},{5,7},{6,4},{7,5},{8,10},{9,11},{10,... | collective-permute-start | bytes 884744 | tf_op jit(solution)/shard_map/ppermute | solution.py:430
  210.0 6.7 %collective-permute-start.27 = (bf16[64,2304]{1,0:T(8,128)(2,1)S(1)}, bf16[64,2304]{1,0:T(8,128)(2,1)S(1)}, u32[]{:S(2)}, u32[]{:S(2)}) collective-permute-start(bf16[64,2304]{1,0:T(8,128)(2,1)S(1)} %get-tuple-element.64), channel_id=1, source_target_pairs={{0,4},{4,0},{8,12},{12,8},{16,20},{20,16},{24,28},{28,24},{1,5},{5... | collective-permute-start | bytes 884744 | tf_op jit(solution)/shard_map/ppermute | solution.py:430
  216.9 6.8 %collective-permute-start.29 = (bf16[64,2304]{1,0:T(8,128)(2,1)S(1)}, bf16[64,2304]{1,0:T(8,128)(2,1)S(1)}, u32[]{:S(2)}, u32[]{:S(2)}) collective-permute-start(bf16[64,2304]{1,0:T(8,128)(2,1)S(1)} %get-tuple-element.66), channel_id=1, source_target_pairs={{0,8},{4,12},{8,0},{12,4},{16,24},{20,28},{24,16},{28,20},{1,9},{5... | collective-permute-start | bytes 884744 | tf_op jit(solution)/shard_map/ppermute | solution.py:430
  (4 other events, 5.5 us)

commit v13 on v12

--- a/solution.py
+++ b/solution.py
@@ -318,23 +318,26 @@
     ended_ref[...] = jnp.zeros_like(ended_ref)
     half = got_ref.shape[1]
     copies = [
-        [
-            pltpu.make_async_copy(source.at[e], target.at[e], weight_sem.at[3 * e + i])
-            for i, (source, target) in enumerate(((wg_hbm, wg), (wu_hbm, wu), (wd_hbm, wd)))
-        ]
+        pltpu.make_async_copy(source.at[e], target.at[e], weight_sem.at[3 * e + i])
         for e in range(local)
+        for i, (source, target) in enumerate(((wg_hbm, wg), (wu_hbm, wu), (wd_hbm, wd)))
     ]
-    for group in copies:
-        for copy in group:
-            copy.start()
+    for copy in copies[:2]:
+        copy.start()
+
+    def arrived(number):
+        copies[number].wait()
+        if number + 2 < len(copies):
+            copies[number + 2].start()
+
     for e in range(local):
         rows = jnp.concatenate([own_ref[e], got_ref[e]], axis=0)
-        copies[e][0].wait()
+        arrived(3 * e)
         gate = dot_t(rows, wg[e])
-        copies[e][1].wait()
+        arrived(3 * e + 1)
         upper = dot_t(rows, wu[e])
         hidden = (gate / (1.0 + jnp.exp(-gate)) * upper).astype(jnp.bfloat16)
-        copies[e][2].wait()
+        arrived(3 * e + 2)
         y = jnp.dot(hidden, wd[e], preferred_element_type=jnp.float32).astype(jnp.bfloat16)
         y_own_ref[e] = y[:half]
         y_sib_ref[e] = y[half:]

time: 225 us -> 225 us (level)
  no operation moved by 1% of the time
where the time goes in v13:
time: 225 us
  waiting for transfers between devices  106 us (47%)
  Pallas kernels  58 us (26%)
  starting transfers between devices  49.9 us (22%)
  local copies, waits for them, and re-layouts  8.59 us (4%)
    ppermute x30, waiting for transfers between devices, swap(): return lax.ppermute(a, axis, [(i, i ^ distance) for i in range(size)])  69.2 us
    ppermute x30, starting transfers between devices, swap(): return lax.ppermute(a, axis, [(i, i ^ distance) for i in range(size)])  35.4 us
    pallas_call x2, Pallas kernels, expert_rows(): pl.pallas_call(functools.partial(rows_kernel, local, len(waits)), out_sha...  31.7 us
    all_to_all x1, waiting for transfers between devices, body(): lax.all_to_all(packed, 'seq', split_axis=0, concat_axis=0, tiled=True)  25.3 us
    all_to_all x1, waiting for transfers between devices, body(): lax.all_to_all(context.reshape(n_seq, rows_dev, span), 'seq', split_axis=...  11.1 us
    pallas_call x2, Pallas kernels, put_rows(): pl.pallas_call(functools.partial(put_kernel, local, rows_dev, planes, len...  8.42 us
    pallas_call x2, Pallas kernels, select_rows(): pl.pallas_call(functools.partial(select_kernel, local, rows_dev, len(piec...  7.3 us
    all_to_all x1, starting transfers between devices, body(): lax.all_to_all(packed, 'seq', split_axis=0, concat_axis=0, tiled=True)  7.25 us
  transfers between devices with their start and end apart: 33, of which 23 were waited for; matrix products, arithmetic and copies ran while one was open for 1% of the time, Pallas kernels for 21%

profile of v13, /device:TPU:0, one launch (start us, length us, event | category | flops | bytes accessed | tf_op | source)
XLA Modules:
  0.0 224.5 jit_solution(15832383309384186627)
XLA Ops:
  0.6 2.3 %fusion.3 = (bf16[1,64,1,2304]{3,2,1,0:T(2,128)(2,1)S(1)}, bf16[1,64,1,2304]{3,2,1,0:T(2,128)(2,1)S(1)}) fusion(bf16[1,64,2,2304]{3,2,1,0:T(2,128)(2,1)} %param.12), kind=kLoop, calls=%fused_computation.14 | loop fusion | bytes 1179648 | tf_op jit(solution)/shard_map/slice | solution.py:548
  3.1 1.2 shard_map.122
  4.3 7.3 %all-to-all-start = ((bf16[8,64,960]{2,1,0:T(8,128)(2,1)}), bf16[8,64,960]{2,1,0:T(8,128)(2,1)S(1)}, u32[]{:S(2)}, u32[]{:S(2)}) async-start(bf16[8,64,960]{2,1,0:T(8,128)(2,1)} %shard_map.122), calls=%async_computation | async-start | bytes 2097152 | tf_op jit(solution)/shard_map/all_to_all | solution.py:551
  12.0 25.3 %all-to-all-done = bf16[8,64,960]{2,1,0:T(8,128)(2,1)S(1)} async-done(((bf16[8,64,960]{2,1,0:T(8,128)(2,1)}), bf16[8,64,960]{2,1,0:T(8,128)(2,1)S(1)}, u32[]{:S(2)}, u32[]{:S(2)}) %all-to-all-start) | async-done | bytes 983072 | tf_op jit(solution)/shard_map/all_to_all | solution.py:551
  37.3 5.6 %shard_map.123 = bf16[512,320]{1,0:T(8,128)(2,1)} custom-call(bf16[512,960]{1,0:T(8,128)(2,1)S(1)} %bitcast.22, s32[1,512]{1,0:T(1,128)S(1)} %copy-done.6, s32[512,1]{1,0:T(8,128)S(1)} %copy.40.seg_col_ref), custom_call_target="tpu_custom_call" | custom-call | flops 335544320 | bytes 1310720 | tf_op jit(solution)/shard_map/pallas_call | solution.py:56
  42.9 3.6 %all-to-all-start.1 = ((bf16[8,64,320]{2,1,0:T(8,128)(2,1)}), bf16[8,64,320]{2,1,0:T(8,128)(2,1)S(1)}, u32[]{:S(2)}, u32[]{:S(2)}) async-start(bf16[8,64,320]{2,1,0:T(8,128)(2,1)} %bitcast.5), calls=%async_computation.1 | async-start | bytes 786432 | tf_op jit(solution)/shard_map/all_to_all | solution.py:554
  47.3 11.1 %all-to-all-done.1.context_ref = bf16[8,64,320]{2,1,0:T(8,128)(2,1)S(1)} async-done(((bf16[8,64,320]{2,1,0:T(8,128)(2,1)}), bf16[8,64,320]{2,1,0:T(8,128)(2,1)S(1)}, u32[]{:S(2)}, u32[]{:S(2)}) %all-to-all-start.1) | async-done | bytes 327712 | tf_op jit(solution)/shard_map/all_to_all | solution.py:554
  60.3 1.9 collective-permute-start.7
  62.2 1.5 collective-permute-start
  63.8 7.1 %collective-permute-done.3.refs_4_ = bf16[64,2432]{1,0:T(8,128)(2,1)S(1)} collective-permute-done((bf16[64,2432]{1,0:T(8,128)(2,1)S(1)}, bf16[64,2432]{1,0:T(8,128)(2,1)S(1)}, u32[]{:S(2)}, u32[]{:S(2)}) %collective-permute-start.3) | collective-permute-done | bytes 311328 | tf_op jit(solution)/shard_map/ppermute | solution.py:433
  70.9 1.5 collective-permute-start.5
  72.4 3.9 %collective-permute-start.4 = (bf16[64,2432]{1,0:T(8,128)(2,1)S(1)}, bf16[64,2432]{1,0:T(8,128)(2,1)S(1)}, u32[]{:S(2)}, u32[]{:S(2)}) collective-permute-start(bf16[64,2432]{1,0:T(8,128)(2,1)S(1)} %collective-permute-done.3.refs_4_), channel_id=1, source_target_pairs={{0,4},{4,0},{8,12},{12,8},{16,20},{20,16},{24,28},{28,24},{1,5},{5... | collective-permute-start | bytes 933896 | tf_op jit(solution)/shard_map/ppermute | solution.py:433
  76.8 1.5 collective-permute-done.5.refs_3_.refs_6_
  78.3 4.1 %collective-permute-done.4.refs_4_.refs_5_ = bf16[64,2432]{1,0:T(8,128)(2,1)S(1)} collective-permute-done((bf16[64,2432]{1,0:T(8,128)(2,1)S(1)}, bf16[64,2432]{1,0:T(8,128)(2,1)S(1)}, u32[]{:S(2)}, u32[]{:S(2)}) %collective-permute-start.4) | collective-permute-done | bytes 311328 | tf_op jit(solution)/shard_map/ppermute | solution.py:433
  82.5 2.7 %collective-permute-start.6 = (bf16[64,2432]{1,0:T(8,128)(2,1)S(1)}, bf16[64,2432]{1,0:T(8,128)(2,1)S(1)}, u32[]{:S(2)}, u32[]{:S(2)}) collective-permute-start(bf16[64,2432]{1,0:T(8,128)(2,1)S(1)} %collective-permute-done.5.refs_3_.refs_6_), channel_id=1, source_target_pairs={{0,4},{4,0},{8,12},{12,8},{16,20},{20,16},{24,28},{28,24},{1,5},{5... | collective-permute-start | bytes 933896 | tf_op jit(solution)/shard_map/ppermute | solution.py:433
  85.3 4.5 %collective-permute-done.11.refs_0_ = bf16[64,2432]{1,0:T(8,128)(2,1)} collective-permute-done((bf16[64,2432]{1,0:T(8,128)(2,1)S(1)}, bf16[64,2432]{1,0:T(8,128)(2,1)}, u32[]{:S(2)}, u32[]{:S(2)}) %collective-permute-start.11) | collective-permute-done | bytes 311328 | tf_op jit(solution)/shard_map/ppermute | solution.py:433
  89.8 3.7 %collective-permute-done.6.refs_2_.refs_7_ = bf16[64,2432]{1,0:T(8,128)(2,1)S(1)} collective-permute-done((bf16[64,2432]{1,0:T(8,128)(2,1)S(1)}, bf16[64,2432]{1,0:T(8,128)(2,1)S(1)}, u32[]{:S(2)}, u32[]{:S(2)}) %collective-permute-start.6) | collective-permute-done | bytes 311328 | tf_op jit(solution)/shard_map/ppermute | solution.py:433
  93.5 1.5 collective-permute-start.13
  95.5 2.0 collective-permute-start.12
  97.5 2.7 %collective-permute-done.9.refs_2_ = bf16[64,2432]{1,0:T(8,128)(2,1)} collective-permute-done((bf16[64,2432]{1,0:T(8,128)(2,1)S(1)}, bf16[64,2432]{1,0:T(8,128)(2,1)}, u32[]{:S(2)}, u32[]{:S(2)}) %collective-permute-start.9) | collective-permute-done | bytes 311328 | tf_op jit(solution)/shard_map/ppermute | solution.py:433
  100.2 1.5 collective-permute-start.10
  101.8 1.4 collective-permute-done.13.refs_6_
  104.3 2.2 collective-permute-done.8.refs_1_
  106.5 3.3 %collective-permute-done.10.refs_3_ = bf16[64,2432]{1,0:T(8,128)(2,1)} collective-permute-done((bf16[64,2432]{1,0:T(8,128)(2,1)}, bf16[64,2432]{1,0:T(8,128)(2,1)}, u32[]{:S(2)}, u32[]{:S(2)}) %collective-permute-start.10) | collective-permute-done | bytes 311328 | tf_op jit(solution)/shard_map/ppermute | solution.py:433
  110.4 4.2 %shard_map.127 = (bf16[2,192,2304]{2,1,0:T(8,128)(2,1)S(1)}, bf16[2,192,2304]{2,1,0:T(8,128)(2,1)}, bf16[512,128]{1,0:T(8,128)(2,1)S(1)}) custom-call(s32[2]{0:T(128)S(1)} %add_multiply_fusion.bases_ref, bf16[64,2432]{1,0:T(8,128)(2,1)S(1)} %shard_map.125.refs_0_, bf16[64,2432]{1,0:T(8,128)(2,1)} %collective-permute-done.8.refs_1_, ...), custom_call_target="tpu_custom_call" | custom-call | flops 905969664 | bytes 6029312 | tf_op jit(solution)/shard_map/pallas_call | solution.py:300
  114.6 1.2 copy-done.13
  115.9 1.7 shard_map.128.refs_8_.rest_1_
  117.6 3.1 %shard_map.129 = (bf16[2,192,2304]{2,1,0:T(8,128)(2,1)S(1)}, bf16[2,192,2304]{2,1,0:T(8,128)(2,1)}, bf16[512,128]{1,0:T(8,128)(2,1)S(1)}) custom-call(s32[2]{0:T(128)S(1)} %add_multiply_fusion.bases_ref, bf16[64,2432]{1,0:T(8,128)(2,1)S(1)} %copy-done.8, bf16[64,2432]{1,0:T(8,128)(2,1)S(1)} %collective-permute-done.refs_2_.refs_1_, ...), custom_call_target="tpu_custom_call" | custom-call | flops 905969664 | bytes 6029312 | tf_op jit(solution)/shard_map/pallas_call | solution.py:300
  120.7 1.3 copy-done.11
  122.5 3.7 %all-to-all-start.2 = ((bf16[8,64,640]{2,1,0:T(8,128)(2,1)}), bf16[8,64,640]{2,1,0:T(8,128)(2,1)S(1)}, u32[]{:S(2)}, u32[]{:S(2)}) async-start(bf16[8,64,640]{2,1,0:T(8,128)(2,1)} %shard_map.128.refs_8_.rest_1_), calls=%async_computation.2 | async-start | bytes 1310720 | tf_op jit(solution)/shard_map/all_to_all | solution.py:571
  126.3 1.5 copy-done.14
  127.7 16.4 %shard_map.130 = (bf16[2,192,2304]{2,1,0:T(8,128)(2,1)S(1)}, bf16[2,192,2304]{2,1,0:T(8,128)(2,1)}, f32[8,128]{1,0:T(8,128)S(1)}) custom-call(bf16[2,192,2304]{2,1,0:T(8,128)(2,1)S(1)} %copy-done.14, bf16[2,192,2304]{2,1,0:T(8,128)(2,1)} %collective-permute-done.16.got_ref, bf16[2,720,2304]{2,1,0:T(8,128)(2,1)} %bitcast.28, bf16[2,720,2304]{2,1,0:T(8,128)(2,1)} %bitcast.30, ...), custom_call_target="tpu_custom_call" | custom-call | flops 7644119040 | bytes 26984448 | tf_op jit(solution)/shard_map/pallas_call | solution.py:352
  145.2 1.5 copy-done.12
  146.7 15.3 %shard_map.132 = (bf16[2,192,2304]{2,1,0:T(8,128)(2,1)S(1)}, bf16[2,192,2304]{2,1,0:T(8,128)(2,1)S(1)}, f32[8,128]{1,0:T(8,128)S(1)}) custom-call(bf16[2,192,2304]{2,1,0:T(8,128)(2,1)S(1)} %copy-done.12, bf16[2,192,2304]{2,1,0:T(8,128)(2,1)} %collective-permute-done.15.got_ref, bf16[2,720,2304]{2,1,0:T(8,128)(2,1)} %bitcast.29, ...), custom_call_target="tpu_custom_call" | custom-call | flops 7644119040 | bytes 26984448 | tf_op jit(solution)/shard_map/pallas_call | solution.py:352
  162.6 4.9 %shard_map.133 = (bf16[256,2304]{1,0:T(8,128)(2,1)S(1)}, bf16[128,2304]{1,0:T(8,128)(2,1)S(1)}, bf16[128,2304]{1,0:T(8,128)(2,1)S(1)}, f32[8,128]{1,0:T(8,128)}) custom-call(s32[2]{0:T(128)S(1)} %add_multiply_fusion.bases_ref, bf16[2,192,2304]{2,1,0:T(8,128)(2,1)S(1)} %get-tuple-element.47.y_own_ref, ...), custom_call_target="tpu_custom_call" | custom-call | flops 905969664 | bytes 18874368 | tf_op jit(solution)/shard_map/pallas_call | solution.py:414
  167.4 2.0 collective-permute-start.19
  170.3 12.6 %collective-permute-done.19.rest_0_ = bf16[128,2304]{1,0:T(8,128)(2,1)S(1)} collective-permute-done((bf16[128,2304]{1,0:T(8,128)(2,1)S(1)}, bf16[128,2304]{1,0:T(8,128)(2,1)S(1)}, u32[]{:S(2)}, u32[]{:S(2)}) %collective-permute-start.19) | collective-permute-done | bytes 589856 | tf_op jit(solution)/shard_map/ppermute | solution.py:433
  183.0 1.5 collective-permute-done.20.rest_1_
  186.0 3.6 %shard_map.135 = (bf16[256,2304]{1,0:T(8,128)(2,1)S(1)}, bf16[128,2304]{1,0:T(8,128)(2,1)S(1)}, bf16[128,2304]{1,0:T(8,128)(2,1)S(1)}, f32[8,128]{1,0:T(8,128)S(1)}) custom-call(s32[2]{0:T(128)S(1)} %add_multiply_fusion.bases_ref, bf16[2,192,2304]{2,1,0:T(8,128)(2,1)S(1)} %get-tuple-element.45.y_own_ref, ...), custom_call_target="tpu_custom_call" | custom-call | flops 905969664 | bytes 18874368 | tf_op jit(solution)/shard_map/pallas_call | solution.py:414
  189.5 3.0 %collective-permute-done.21.refs_1_.rest_0_ = bf16[64,2304]{1,0:T(8,128)(2,1)S(1)} collective-permute-done((bf16[64,2304]{1,0:T(8,128)(2,1)S(1)}, bf16[64,2304]{1,0:T(8,128)(2,1)S(1)}, u32[]{:S(2)}, u32[]{:S(2)}) %collective-permute-start.21) | collective-permute-done | bytes 294944 | tf_op jit(solution)/shard_map/ppermute | solution.py:433
  193.3 1.5 collective-permute-start.25
  196.6 3.5 %collective-permute-done.25 = bf16[64,2304]{1,0:T(8,128)(2,1)S(1)} collective-permute-done((bf16[64,2304]{1,0:T(8,128)(2,1)S(1)}, bf16[64,2304]{1,0:T(8,128)(2,1)S(1)}, u32[]{:S(2)}, u32[]{:S(2)}) %collective-permute-start.25) | collective-permute-done | bytes 294944 | tf_op jit(solution)/shard_map/ppermute | solution.py:433
  200.2 3.1 %collective-permute-start.28 = (bf16[64,2304]{1,0:T(8,128)(2,1)S(1)}, bf16[64,2304]{1,0:T(8,128)(2,1)S(1)}, u32[]{:S(2)}, u32[]{:S(2)}) collective-permute-start(bf16[64,2304]{1,0:T(8,128)(2,1)S(1)} %add_convert_fusion.1.rest_2_), channel_id=1, source_target_pairs={{0,16},{4,20},{8,24},{12,28},{16,0},{20,4},{24,8},{28,12},{1,17},{... | collective-permute-start | bytes 884744 | tf_op jit(solution)/shard_map/ppermute | solution.py:433
  203.3 4.2 %collective-permute-done.23.rest_0_ = bf16[128,2304]{1,0:T(8,128)(2,1)S(1)} collective-permute-done((bf16[128,2304]{1,0:T(8,128)(2,1)S(1)}, bf16[128,2304]{1,0:T(8,128)(2,1)S(1)}, u32[]{:S(2)}, u32[]{:S(2)}) %collective-permute-start.23) | collective-permute-done | bytes 589856 | tf_op jit(solution)/shard_map/ppermute | solution.py:433
  210.1 1.4 collective-permute-start.27
  211.5 1.4 collective-permute-done.28.rest_2_
  212.9 2.8 %collective-permute-done.26.rest_0_ = bf16[64,2304]{1,0:T(8,128)(2,1)S(1)} collective-permute-done((bf16[64,2304]{1,0:T(8,128)(2,1)S(1)}, bf16[64,2304]{1,0:T(8,128)(2,1)S(1)}, u32[]{:S(2)}, u32[]{:S(2)}) %collective-permute-start.26) | collective-permute-done | bytes 294944 | tf_op jit(solution)/shard_map/ppermute | solution.py:433
  217.5 6.2 %collective-permute-done.29 = bf16[64,2304]{1,0:T(8,128)(2,1)S(1)} collective-permute-done((bf16[64,2304]{1,0:T(8,128)(2,1)S(1)}, bf16[64,2304]{1,0:T(8,128)(2,1)S(1)}, u32[]{:S(2)}, u32[]{:S(2)}) %collective-permute-start.29) | collective-permute-done | bytes 294944 | tf_op jit(solution)/shard_map/ppermute | solution.py:433
  (94 shorter events, 18.5 us)
Async XLA Ops:
  0.6 2.4 %copy-start.5 = (bf16[1,64,2304]{2,1,0:T(8,128)(2,1)S(1)}, bf16[1,64,2304]{2,1,0:T(8,128)(2,1)}, u32[]{:S(2)}) copy-start(bf16[1,64,2304]{2,1,0:T(8,128)(2,1)} %param.11) | copy-start | bytes 884740
  3.0 8.5 %copy-start.6 = (s32[1,512]{1,0:T(1,128)S(1)}, s32[1,512]{1,0:T(1,128)}, u32[]{:S(2)}) copy-start(s32[1,512]{1,0:T(1,128)} %seg_row_ref.1) | copy-start | bytes 6148
  3.0 8.7 %copy-start.15 = (bf16[2304]{0:T(1024)(128)(2,1)S(1)}, bf16[2304]{0:T(1024)(128)(2,1)}, u32[]{:S(2)}) copy-start(bf16[2304]{0:T(1024)(128)(2,1)} %param.14) | copy-start | bytes 13828
  3.1 8.7 %copy-start.16 = (s32[1,64,2]{1,2,0:T(2,128)S(1)}, s32[1,64,2]{1,2,0:T(2,128)}, u32[]{:S(2)}) copy-start(s32[1,64,2]{1,2,0:T(2,128)} %param.16) | copy-start | bytes 1540
  4.3 33.0 %all-to-all-start = ((bf16[8,64,960]{2,1,0:T(8,128)(2,1)}), bf16[8,64,960]{2,1,0:T(8,128)(2,1)S(1)}, u32[]{:S(2)}, u32[]{:S(2)}) async-start(bf16[8,64,960]{2,1,0:T(8,128)(2,1)} %shard_map.122), calls=%async_computation | async-start | bytes 2097152 | tf_op jit(solution)/shard_map/all_to_all | solution.py:551
  37.3 9.9 %copy-start.17 = (f32[1,64,2]{1,2,0:T(2,128)S(1)}, f32[1,64,2]{1,2,0:T(2,128)}, u32[]{:S(2)}) copy-start(f32[1,64,2]{1,2,0:T(2,128)} %param.17) | copy-start | bytes 1540
  37.3 21.1 %copy-start.4 = (bf16[1,64,2304]{2,1,0:T(8,128)(2,1)S(1)}, bf16[1,64,2304]{2,1,0:T(8,128)(2,1)}, u32[]{:S(2)}) copy-start(bf16[1,64,2304]{2,1,0:T(8,128)(2,1)} %param.13) | copy-start | bytes 884740
  42.9 15.5 %all-to-all-start.1 = ((bf16[8,64,320]{2,1,0:T(8,128)(2,1)}), bf16[8,64,320]{2,1,0:T(8,128)(2,1)S(1)}, u32[]{:S(2)}, u32[]{:S(2)}) async-start(bf16[8,64,320]{2,1,0:T(8,128)(2,1)} %bitcast.5), calls=%async_computation.1 | async-start | bytes 786432 | tf_op jit(solution)/shard_map/all_to_all | solution.py:554
  58.7 44.5 %copy-start.7 = (bf16[64,2432]{1,0:T(8,128)(2,1)}, bf16[64,2432]{1,0:T(8,128)(2,1)S(1)}, u32[]{:S(2)}) copy-start(bf16[64,2432]{1,0:T(8,128)(2,1)S(1)} %get-tuple-element.36.refs_0_) | copy-start | bytes 933892
  58.7 12.2 %collective-permute-start.3 = (bf16[64,2432]{1,0:T(8,128)(2,1)S(1)}, bf16[64,2432]{1,0:T(8,128)(2,1)S(1)}, u32[]{:S(2)}, u32[]{:S(2)}) collective-permute-start(bf16[64,2432]{1,0:T(8,128)(2,1)S(1)} %get-tuple-element.36.refs_0_), channel_id=1, source_target_pairs={{0,8},{4,12},{8,0},{12,4},{16,24},{20,28},{24,16},{28,20},{1,9},{5... | collective-permute-start | bytes 933896 | tf_op jit(solution)/shard_map/ppermute | solution.py:433
  59.7 16.6 %collective-permute-start.1 = (bf16[64,2432]{1,0:T(8,128)(2,1)S(1)}, bf16[64,2432]{1,0:T(8,128)(2,1)S(1)}, u32[]{:S(2)}, u32[]{:S(2)}) collective-permute-start(bf16[64,2432]{1,0:T(8,128)(2,1)S(1)} %get-tuple-element.36.refs_0_), channel_id=1, source_target_pairs={{0,4},{4,0},{8,12},{12,8},{16,20},{20,16},{24,28},{28,24},{1,5},{5... | collective-permute-start | bytes 933896 | tf_op jit(solution)/shard_map/ppermute | solution.py:433
  60.3 16.5 %collective-permute-start.7 = (bf16[64,2432]{1,0:T(8,128)(2,1)S(1)}, bf16[64,2432]{1,0:T(8,128)(2,1)S(1)}, u32[]{:S(2)}, u32[]{:S(2)}) collective-permute-start(bf16[64,2432]{1,0:T(8,128)(2,1)S(1)} %get-tuple-element.36.refs_0_), channel_id=1, source_target_pairs={{0,16},{4,20},{8,24},{12,28},{16,0},{20,4},{24,8},{28,12},{1,17},{... | collective-permute-start | bytes 933896 | tf_op jit(solution)/shard_map/ppermute | solution.py:433
  62.2 14.6 %collective-permute-start = (bf16[64,2432]{1,0:T(8,128)(2,1)S(1)}, bf16[64,2432]{1,0:T(8,128)(2,1)S(1)}, u32[]{:S(2)}, u32[]{:S(2)}) collective-permute-start(bf16[64,2432]{1,0:T(8,128)(2,1)S(1)} %get-tuple-element.36.refs_0_), channel_id=1, source_target_pairs={{0,2},{1,3},{2,0},{3,1},{4,6},{5,7},{6,4},{7,5},{8,10},{9,11},{10,... | collective-permute-start | bytes 933896 | tf_op jit(solution)/shard_map/ppermute | solution.py:433
  70.9 11.6 %copy-start.9 = (bf16[64,2432]{1,0:T(8,128)(2,1)}, bf16[64,2432]{1,0:T(8,128)(2,1)S(1)}, u32[]{:S(2)}) copy-start(bf16[64,2432]{1,0:T(8,128)(2,1)S(1)} %collective-permute-done.3.refs_4_) | copy-start | bytes 933892
  70.9 7.4 %collective-permute-start.5 = (bf16[64,2432]{1,0:T(8,128)(2,1)S(1)}, bf16[64,2432]{1,0:T(8,128)(2,1)S(1)}, u32[]{:S(2)}, u32[]{:S(2)}) collective-permute-start(bf16[64,2432]{1,0:T(8,128)(2,1)S(1)} %collective-permute-done.3.refs_4_), channel_id=1, source_target_pairs={{0,2},{1,3},{2,0},{3,1},{4,6},{5,7},{6,4},{7,5},{8,10},{9,11},{10,... | collective-permute-start | bytes 933896 | tf_op jit(solution)/shard_map/ppermute | solution.py:433
  72.4 10.0 %collective-permute-start.4 = (bf16[64,2432]{1,0:T(8,128)(2,1)S(1)}, bf16[64,2432]{1,0:T(8,128)(2,1)S(1)}, u32[]{:S(2)}, u32[]{:S(2)}) collective-permute-start(bf16[64,2432]{1,0:T(8,128)(2,1)S(1)} %collective-permute-done.3.refs_4_), channel_id=1, source_target_pairs={{0,4},{4,0},{8,12},{12,8},{16,20},{20,16},{24,28},{28,24},{1,5},{5... | collective-permute-start | bytes 933896 | tf_op jit(solution)/shard_map/ppermute | solution.py:433
  76.3 8.9 %collective-permute-start.2 = (bf16[64,2432]{1,0:T(8,128)(2,1)S(1)}, bf16[64,2432]{1,0:T(8,128)(2,1)S(1)}, u32[]{:S(2)}, u32[]{:S(2)}) collective-permute-start(bf16[64,2432]{1,0:T(8,128)(2,1)S(1)} %collective-permute-done.1.refs_1_.refs_2_), channel_id=1, source_target_pairs={{0,2},{1,3},{2,0},{3,1},{4,6},{5,7},{6,4},{7,5},{8,10},{9,11},{10,... | collective-permute-start | bytes 933896 | tf_op jit(solution)/shard_map/ppermute | solution.py:433
  82.5 7.3 %collective-permute-start.11 = (bf16[64,2432]{1,0:T(8,128)(2,1)S(1)}, bf16[64,2432]{1,0:T(8,128)(2,1)}, u32[]{:S(2)}, u32[]{:S(2)}) collective-permute-start(bf16[64,2432]{1,0:T(8,128)(2,1)S(1)} %shard_map.125.refs_0_), channel_id=1, source_target_pairs={{0,8},{4,12},{8,0},{12,4},{16,24},{20,28},{24,16},{28,20},{1,9},{5... | collective-permute-start | bytes 933896 | tf_op jit(solution)/shard_map/ppermute | solution.py:433
  82.5 11.0 %collective-permute-start.6 = (bf16[64,2432]{1,0:T(8,128)(2,1)S(1)}, bf16[64,2432]{1,0:T(8,128)(2,1)S(1)}, u32[]{:S(2)}, u32[]{:S(2)}) collective-permute-start(bf16[64,2432]{1,0:T(8,128)(2,1)S(1)} %collective-permute-done.5.refs_3_.refs_6_), channel_id=1, source_target_pairs={{0,4},{4,0},{8,12},{12,8},{16,20},{20,16},{24,28},{28,24},{1,5},{5... | collective-permute-start | bytes 933896 | tf_op jit(solution)/shard_map/ppermute | solution.py:433
  85.2 15.1 %collective-permute-start.9 = (bf16[64,2432]{1,0:T(8,128)(2,1)S(1)}, bf16[64,2432]{1,0:T(8,128)(2,1)}, u32[]{:S(2)}, u32[]{:S(2)}) collective-permute-start(bf16[64,2432]{1,0:T(8,128)(2,1)S(1)} %shard_map.125.refs_0_), channel_id=1, source_target_pairs={{0,4},{4,0},{8,12},{12,8},{16,20},{20,16},{24,28},{28,24},{1,5},{5... | collective-permute-start | bytes 933896 | tf_op jit(solution)/shard_map/ppermute | solution.py:433
  85.3 15.0 %copy-start = (bf16[64,2432]{1,0:T(8,128)(2,1)}, bf16[64,2432]{1,0:T(8,128)(2,1)S(1)}, u32[]{:S(2)}) copy-start(bf16[64,2432]{1,0:T(8,128)(2,1)S(1)} %collective-permute-done.2.refs_1_.refs_3_) | copy-start | bytes 933892
  93.5 8.3 %copy-start.2 = (bf16[64,2432]{1,0:T(8,128)(2,1)}, bf16[64,2432]{1,0:T(8,128)(2,1)S(1)}, u32[]{:S(2)}) copy-start(bf16[64,2432]{1,0:T(8,128)(2,1)S(1)} %collective-permute-done.6.refs_2_.refs_7_) | copy-start | bytes 933892
  93.5 22.3 %copy-start.18 = (s32[1,32]{1,0:T(1,128)S(1)}, s32[1,32]{1,0:T(1,128)}, u32[]{:S(2)}) copy-start(s32[1,32]{1,0:T(1,128)} %param.18) | copy-start | bytes 388
  93.5 9.7 %collective-permute-start.13 = (bf16[64,2432]{1,0:T(8,128)(2,1)}, bf16[64,2432]{1,0:T(8,128)(2,1)}, u32[]{:S(2)}, u32[]{:S(2)}) collective-permute-start(bf16[64,2432]{1,0:T(8,128)(2,1)} %shard_map.126.refs_4_), channel_id=1, source_target_pairs={{0,2},{1,3},{2,0},{3,1},{4,6},{5,7},{6,4},{7,5},{8,10},{9,11},{10,... | collective-permute-start | bytes 933896 | tf_op jit(solution)/shard_map/ppermute | solution.py:433
  95.0 11.5 %collective-permute-start.8 = (bf16[64,2432]{1,0:T(8,128)(2,1)S(1)}, bf16[64,2432]{1,0:T(8,128)(2,1)}, u32[]{:S(2)}, u32[]{:S(2)}) collective-permute-start(bf16[64,2432]{1,0:T(8,128)(2,1)S(1)} %shard_map.125.refs_0_), channel_id=1, source_target_pairs={{0,2},{1,3},{2,0},{3,1},{4,6},{5,7},{6,4},{7,5},{8,10},{9,11},{10,... | collective-permute-start | bytes 933896 | tf_op jit(solution)/shard_map/ppermute | solution.py:433
  95.5 14.4 %collective-permute-start.12 = (bf16[64,2432]{1,0:T(8,128)(2,1)}, bf16[64,2432]{1,0:T(8,128)(2,1)}, u32[]{:S(2)}, u32[]{:S(2)}) collective-permute-start(bf16[64,2432]{1,0:T(8,128)(2,1)} %shard_map.126.refs_4_), channel_id=1, source_target_pairs={{0,4},{4,0},{8,12},{12,8},{16,20},{20,16},{24,28},{28,24},{1,5},{5... | collective-permute-start | bytes 933896 | tf_op jit(solution)/shard_map/ppermute | solution.py:433
  100.2 9.6 %collective-permute-start.10 = (bf16[64,2432]{1,0:T(8,128)(2,1)}, bf16[64,2432]{1,0:T(8,128)(2,1)}, u32[]{:S(2)}, u32[]{:S(2)}) collective-permute-start(bf16[64,2432]{1,0:T(8,128)(2,1)} %collective-permute-done.9.refs_2_), channel_id=1, source_target_pairs={{0,2},{1,3},{2,0},{3,1},{4,6},{5,7},{6,4},{7,5},{8,10},{9,11},{10,... | collective-permute-start | bytes 933896 | tf_op jit(solution)/shard_map/ppermute | solution.py:433
  103.2 7.2 %collective-permute-start.14 = (bf16[64,2432]{1,0:T(8,128)(2,1)}, bf16[64,2432]{1,0:T(8,128)(2,1)}, u32[]{:S(2)}, u32[]{:S(2)}) collective-permute-start(bf16[64,2432]{1,0:T(8,128)(2,1)} %collective-permute-done.13.refs_6_), channel_id=1, source_target_pairs={{0,4},{4,0},{8,12},{12,8},{16,20},{20,16},{24,28},{28,24},{1,5},{5... | collective-permute-start | bytes 933896 | tf_op jit(solution)/shard_map/ppermute | solution.py:433
  104.3 13.2 %copy-start.1 = (bf16[64,2432]{1,0:T(8,128)(2,1)S(1)}, bf16[64,2432]{1,0:T(8,128)(2,1)}, u32[]{:S(2)}) copy-start(bf16[64,2432]{1,0:T(8,128)(2,1)} %copy-done) | copy-start | bytes 933892
  104.3 13.2 %copy-start.3 = (bf16[64,2432]{1,0:T(8,128)(2,1)S(1)}, bf16[64,2432]{1,0:T(8,128)(2,1)}, u32[]{:S(2)}) copy-start(bf16[64,2432]{1,0:T(8,128)(2,1)} %copy-done.2) | copy-start | bytes 933892
  104.3 13.2 %copy-start.8 = (bf16[64,2432]{1,0:T(8,128)(2,1)S(1)}, bf16[64,2432]{1,0:T(8,128)(2,1)}, u32[]{:S(2)}) copy-start(bf16[64,2432]{1,0:T(8,128)(2,1)} %copy-done.7) | copy-start | bytes 933892
  104.3 13.2 %copy-start.10 = (bf16[64,2432]{1,0:T(8,128)(2,1)S(1)}, bf16[64,2432]{1,0:T(8,128)(2,1)}, u32[]{:S(2)}) copy-start(bf16[64,2432]{1,0:T(8,128)(2,1)} %copy-done.9) | copy-start | bytes 933892
  115.8 10.5 %collective-permute-start.16 = (bf16[2,192,2304]{2,1,0:T(8,128)(2,1)}, bf16[2,192,2304]{2,1,0:T(8,128)(2,1)}, u32[]{:S(2)}, u32[]{:S(2)}) collective-permute-start(bf16[2,192,2304]{2,1,0:T(8,128)(2,1)} %get-tuple-element.41), channel_id=1, source_target_pairs={{0,1},{1,0},{2,3},{3,2},{4,5},{5,4},{6,7},{7,6},{8,9},{9,8},{10,11... | collective-permute-start | bytes 5308424 | tf_op jit(solution)/shard_map/ppermute | solution.py:433
  122.0 23.2 %collective-permute-start.15 = (bf16[2,192,2304]{2,1,0:T(8,128)(2,1)}, bf16[2,192,2304]{2,1,0:T(8,128)(2,1)}, u32[]{:S(2)}, u32[]{:S(2)}) collective-permute-start(bf16[2,192,2304]{2,1,0:T(8,128)(2,1)} %get-tuple-element.39), channel_id=1, source_target_pairs={{0,1},{1,0},{2,3},{3,2},{4,5},{5,4},{6,7},{7,6},{8,9},{9,8},{10,11... | collective-permute-start | bytes 5308424 | tf_op jit(solution)/shard_map/ppermute | solution.py:433
  122.5 21.7 %all-to-all-start.2 = ((bf16[8,64,640]{2,1,0:T(8,128)(2,1)}), bf16[8,64,640]{2,1,0:T(8,128)(2,1)S(1)}, u32[]{:S(2)}, u32[]{:S(2)}) async-start(bf16[8,64,640]{2,1,0:T(8,128)(2,1)} %shard_map.128.refs_8_.rest_1_), calls=%async_computation.2 | async-start | bytes 1310720 | tf_op jit(solution)/shard_map/all_to_all | solution.py:571
  144.1 18.5 %collective-permute-start.18 = (bf16[2,192,2304]{2,1,0:T(8,128)(2,1)}, bf16[2,192,2304]{2,1,0:T(8,128)(2,1)}, u32[]{:S(2)}, u32[]{:S(2)}) collective-permute-start(bf16[2,192,2304]{2,1,0:T(8,128)(2,1)} %get-tuple-element.48), channel_id=1, source_target_pairs={{0,1},{1,0},{2,3},{3,2},{4,5},{5,4},{6,7},{7,6},{8,9},{9,8},{10,11... | collective-permute-start | bytes 5308424 | tf_op jit(solution)/shard_map/ppermute | solution.py:433
  162.0 23.9 %collective-permute-start.17 = (bf16[2,192,2304]{2,1,0:T(8,128)(2,1)S(1)}, bf16[2,192,2304]{2,1,0:T(8,128)(2,1)S(1)}, u32[]{:S(2)}, u32[]{:S(2)}) collective-permute-start(bf16[2,192,2304]{2,1,0:T(8,128)(2,1)S(1)} %get-tuple-element.46), channel_id=1, source_target_pairs={{0,1},{1,0},{2,3},{3,2},{4,5},{5,4},{6,7},{7,6},{8,9},{9,8},{10,11... | collective-permute-start | bytes 5308424 | tf_op jit(solution)/shard_map/ppermute | solution.py:433
  167.4 15.5 %collective-permute-start.19 = (bf16[128,2304]{1,0:T(8,128)(2,1)S(1)}, bf16[128,2304]{1,0:T(8,128)(2,1)S(1)}, u32[]{:S(2)}, u32[]{:S(2)}) collective-permute-start(bf16[128,2304]{1,0:T(8,128)(2,1)S(1)} %get-tuple-element.51), channel_id=1, source_target_pairs={{0,4},{4,0},{8,12},{12,8},{16,20},{20,16},{24,28},{28,24},{1,5},{5... | collective-permute-start | bytes 1769480 | tf_op jit(solution)/shard_map/ppermute | solution.py:433
  169.4 15.0 %collective-permute-start.20 = (bf16[128,2304]{1,0:T(8,128)(2,1)S(1)}, bf16[128,2304]{1,0:T(8,128)(2,1)S(1)}, u32[]{:S(2)}, u32[]{:S(2)}) collective-permute-start(bf16[128,2304]{1,0:T(8,128)(2,1)S(1)} %get-tuple-element.52), channel_id=1, source_target_pairs={{0,2},{1,3},{2,0},{3,1},{4,6},{5,7},{6,4},{7,5},{8,10},{9,11},{10,... | collective-permute-start | bytes 1769480 | tf_op jit(solution)/shard_map/ppermute | solution.py:433
  184.7 7.8 %collective-permute-start.21 = (bf16[64,2304]{1,0:T(8,128)(2,1)S(1)}, bf16[64,2304]{1,0:T(8,128)(2,1)S(1)}, u32[]{:S(2)}, u32[]{:S(2)}) collective-permute-start(bf16[64,2304]{1,0:T(8,128)(2,1)S(1)} %get-tuple-element.53.rest_0_), channel_id=1, source_target_pairs={{0,2},{1,3},{2,0},{3,1},{4,6},{5,7},{6,4},{7,5},{8,10},{9,11},{10,... | collective-permute-start | bytes 884744 | tf_op jit(solution)/shard_map/ppermute | solution.py:433
  185.7 7.5 %collective-permute-start.22 = (bf16[64,2304]{1,0:T(8,128)(2,1)S(1)}, bf16[64,2304]{1,0:T(8,128)(2,1)S(1)}, u32[]{:S(2)}, u32[]{:S(2)}) collective-permute-start(bf16[64,2304]{1,0:T(8,128)(2,1)S(1)} %get-tuple-element.56), channel_id=1, source_target_pairs={{0,4},{4,0},{8,12},{12,8},{16,20},{20,16},{24,28},{28,24},{1,5},{5... | collective-permute-start | bytes 884744 | tf_op jit(solution)/shard_map/ppermute | solution.py:433
  193.3 6.8 %collective-permute-start.25 = (bf16[64,2304]{1,0:T(8,128)(2,1)S(1)}, bf16[64,2304]{1,0:T(8,128)(2,1)S(1)}, u32[]{:S(2)}, u32[]{:S(2)}) collective-permute-start(bf16[64,2304]{1,0:T(8,128)(2,1)S(1)} %get-tuple-element.61), channel_id=1, source_target_pairs={{0,8},{4,12},{8,0},{12,4},{16,24},{20,28},{24,16},{28,20},{1,9},{5... | collective-permute-start | bytes 884744 | tf_op jit(solution)/shard_map/ppermute | solution.py:433
  194.8 12.6 %collective-permute-start.23 = (bf16[128,2304]{1,0:T(8,128)(2,1)S(1)}, bf16[128,2304]{1,0:T(8,128)(2,1)S(1)}, u32[]{:S(2)}, u32[]{:S(2)}) collective-permute-start(bf16[128,2304]{1,0:T(8,128)(2,1)S(1)} %shard_map.136), channel_id=1, source_target_pairs={{0,4},{4,0},{8,12},{12,8},{16,20},{20,16},{24,28},{28,24},{1,5},{5... | collective-permute-start | bytes 1769480 | tf_op jit(solution)/shard_map/ppermute | solution.py:433
  195.4 13.2 %collective-permute-start.24 = (bf16[128,2304]{1,0:T(8,128)(2,1)S(1)}, bf16[128,2304]{1,0:T(8,128)(2,1)S(1)}, u32[]{:S(2)}, u32[]{:S(2)}) collective-permute-start(bf16[128,2304]{1,0:T(8,128)(2,1)S(1)} %shard_map.137), channel_id=1, source_target_pairs={{0,2},{1,3},{2,0},{3,1},{4,6},{5,7},{6,4},{7,5},{8,10},{9,11},{10,... | collective-permute-start | bytes 1769480 | tf_op jit(solution)/shard_map/ppermute | solution.py:433
  200.2 12.7 %collective-permute-start.28 = (bf16[64,2304]{1,0:T(8,128)(2,1)S(1)}, bf16[64,2304]{1,0:T(8,128)(2,1)S(1)}, u32[]{:S(2)}, u32[]{:S(2)}) collective-permute-start(bf16[64,2304]{1,0:T(8,128)(2,1)S(1)} %add_convert_fusion.1.rest_2_), channel_id=1, source_target_pairs={{0,16},{4,20},{8,24},{12,28},{16,0},{20,4},{24,8},{28,12},{1,17},{... | collective-permute-start | bytes 884744 | tf_op jit(solution)/shard_map/ppermute | solution.py:433
  208.9 6.8 %collective-permute-start.26 = (bf16[64,2304]{1,0:T(8,128)(2,1)S(1)}, bf16[64,2304]{1,0:T(8,128)(2,1)S(1)}, u32[]{:S(2)}, u32[]{:S(2)}) collective-permute-start(bf16[64,2304]{1,0:T(8,128)(2,1)S(1)} %get-tuple-element.63), channel_id=1, source_target_pairs={{0,2},{1,3},{2,0},{3,1},{4,6},{5,7},{6,4},{7,5},{8,10},{9,11},{10,... | collective-permute-start | bytes 884744 | tf_op jit(solution)/shard_map/ppermute | solution.py:433
  210.1 6.7 %collective-permute-start.27 = (bf16[64,2304]{1,0:T(8,128)(2,1)S(1)}, bf16[64,2304]{1,0:T(8,128)(2,1)S(1)}, u32[]{:S(2)}, u32[]{:S(2)}) collective-permute-start(bf16[64,2304]{1,0:T(8,128)(2,1)S(1)} %get-tuple-element.64), channel_id=1, source_target_pairs={{0,4},{4,0},{8,12},{12,8},{16,20},{20,16},{24,28},{28,24},{1,5},{5... | collective-permute-start | bytes 884744 | tf_op jit(solution)/shard_map/ppermute | solution.py:433
  216.9 6.8 %collective-permute-start.29 = (bf16[64,2304]{1,0:T(8,128)(2,1)S(1)}, bf16[64,2304]{1,0:T(8,128)(2,1)S(1)}, u32[]{:S(2)}, u32[]{:S(2)}) collective-permute-start(bf16[64,2304]{1,0:T(8,128)(2,1)S(1)} %get-tuple-element.66), channel_id=1, source_target_pairs={{0,8},{4,12},{8,0},{12,4},{16,24},{20,28},{24,16},{28,20},{1,9},{5... | collective-permute-start | bytes 884744 | tf_op jit(solution)/shard_map/ppermute | solution.py:433
  (4 other events, 5.5 us)

commit v14 on v13

--- a/solution.py
+++ b/solution.py
@@ -331,12 +331,12 @@
             copies[number + 2].start()
 
     for e in range(local):
-        rows = jnp.concatenate([own_ref[e], got_ref[e]], axis=0)
+        rows = jnp.concatenate([own_ref[e], got_ref[e]], axis=0).T
         arrived(3 * e)
-        gate = dot_t(rows, wg[e])
+        gate = jnp.dot(wg[e], rows, preferred_element_type=jnp.float32)
         arrived(3 * e + 1)
-        upper = dot_t(rows, wu[e])
-        hidden = (gate / (1.0 + jnp.exp(-gate)) * upper).astype(jnp.bfloat16)
+        upper = jnp.dot(wu[e], rows, preferred_element_type=jnp.float32)
+        hidden = (gate / (1.0 + jnp.exp(-gate)) * upper).T.astype(jnp.bfloat16)
         arrived(3 * e + 2)
         y = jnp.dot(hidden, wd[e], preferred_element_type=jnp.float32).astype(jnp.bfloat16)
         y_own_ref[e] = y[:half]
@@ -375,31 +375,26 @@
     ended_ref[...] = jnp.zeros_like(ended_ref)
     tokens, rows = 4 * rows_dev, 4 * CAP
     total = 2 * local * rows
-    shift_lane = lax.broadcasted_iota(jnp.int32, (1, tokens), 1) // rows_dev * CAP
-    shift_row = lax.broadcasted_iota(jnp.int32, (tokens, 1), 0) // rows_dev * CAP
-    row_id = lax.broadcasted_iota(jnp.int32, (rows, tokens), 0)
+    shift = lax.broadcasted_iota(jnp.int32, (tokens, 1), 0) // rows_dev * CAP
     lane = lax.broadcasted_iota(jnp.int32, (tokens, total), 1)
     for g in range(planes):
-        facts = facts_ref[g * tokens : (g + 1) * tokens, :]
-        by_lane = facts_by_lane(facts)
-        by_row = facts.astype(jnp.float32)
+        facts = facts_ref[g * tokens : (g + 1) * tokens, :].astype(jnp.float32)
+        high, middle = jnp.zeros((tokens, total), jnp.float32), jnp.zeros((tokens, total), jnp.float32)
+        for j in range(2):
+            slot = facts[:, j : j + 1].astype(jnp.int32)
+            place = jnp.full((tokens, 1), -1, jnp.int32)
+            for core in range(2):
+                for e in range(local):
+                    near = slot - (bases_ref[core] + e) * CAP
+                    here = shift + near + (core * local + e) * rows
+                    place = jnp.where((near >= 0) & (near < CAP), here, place)
+            hit = lane == place
+            high = jnp.where(hit, facts[:, 2 + j : 3 + j], high)
+            middle = jnp.where(hit, facts[:, 4 + j : 5 + j], middle)
         here = slice(g * rows, (g + 1) * rows)
-        weighed, put = [], None
-        for core, y_ref in enumerate((y_own_ref, y_got_ref)):
-            for e in range(local):
-                base = (bases_ref[core] + e) * CAP
-                weight = jnp.zeros((rows, tokens), jnp.float32)
-                for j in range(2):
-                    hit = row_id == places_of([by_lane[j : j + 1]], base, shift_lane)
-                    gate = by_lane[2 + j : 3 + j] + by_lane[4 + j : 5 + j] + by_lane[6 + j : 7 + j]
-                    weight = weight + jnp.where(hit, gate, 0.0)
-                weight = jnp.sum(weight, axis=1, keepdims=True)
-                weighed.append((y_ref[e, here, :].astype(jnp.float32) * weight).astype(jnp.bfloat16))
-                first = (core * local + e) * rows
-                hit = lane == places_of([by_row[:, j : j + 1] for j in range(2)], base, shift_row + first)
-                put = hit if put is None else put | hit
-        put = put.astype(jnp.float32).astype(jnp.bfloat16)
-        out = jnp.dot(put, jnp.concatenate(weighed, axis=0), preferred_element_type=jnp.float32)
+        y = jnp.concatenate([ref[e, here, :] for ref in (y_own_ref, y_got_ref) for e in range(local)], axis=0)
+        out = jnp.dot(high.astype(jnp.bfloat16), y, preferred_element_type=jnp.float32)
+        out += jnp.dot(middle.astype(jnp.bfloat16), y, preferred_element_type=jnp.float32)
         out = out.astype(jnp.bfloat16)
         kept_ref[g * tokens // 2 : (g + 1) * tokens // 2, :] = out[: tokens // 2]
         send_refs[g][...] = out[tokens // 2 :]

time: 225 us -> 225 us (level)
  transfers between devices with their start and end apart: 33 -> 33, of which waited for: 23 -> 23; matrix products, arithmetic and copies ran while one was open for 1% -> 1% of each run, Pallas kernels for 21% -> 20%
where the time goes in v14:
time: 225 us; the launch traced here: 224 us
  waiting for transfers between devices  106 us (47%)
  Pallas kernels  57.4 us (26%)
  starting transfers between devices  49.9 us (22%)
  local copies, waits for them, and re-layouts  8.59 us (4%)
    ppermute x30, waiting for transfers between devices, swap(): return lax.ppermute(a, axis, [(i, i ^ distance) for i in range(size)])  69.3 us
    ppermute x30, starting transfers between devices, swap(): return lax.ppermute(a, axis, [(i, i ^ distance) for i in range(size)])  35.4 us
    pallas_call x2, Pallas kernels, expert_rows(): pl.pallas_call(functools.partial(rows_kernel, local, len(waits)), out_sha...  31.3 us
    all_to_all x1, waiting for transfers between devices, body(): lax.all_to_all(packed, 'seq', split_axis=0, concat_axis=0, tiled=True)  25.3 us
    all_to_all x1, waiting for transfers between devices, body(): lax.all_to_all(context.reshape(n_seq, rows_dev, span), 'seq', split_axis=...  11.1 us
    pallas_call x2, Pallas kernels, put_rows(): pl.pallas_call(functools.partial(put_kernel, local, rows_dev, planes, len...  8.15 us
    pallas_call x2, Pallas kernels, select_rows(): pl.pallas_call(functools.partial(select_kernel, local, rows_dev, len(piec...  7.3 us
    all_to_all x1, starting transfers between devices, body(): lax.all_to_all(packed, 'seq', split_axis=0, concat_axis=0, tiled=True)  7.25 us
  transfers between devices with their start and end apart: 33, of which 23 were waited for; matrix products, arithmetic and copies ran while one was open for 1% of the time, Pallas kernels for 20%

profile of v14, /device:TPU:0, one launch (start us, length us, event | category | flops | bytes accessed | tf_op | source)
XLA Modules:
  0.0 224.1 jit_solution(15713196504784855137)
XLA Ops:
  0.6 2.3 %fusion.3 = (bf16[1,64,1,2304]{3,2,1,0:T(2,128)(2,1)S(1)}, bf16[1,64,1,2304]{3,2,1,0:T(2,128)(2,1)S(1)}) fusion(bf16[1,64,2,2304]{3,2,1,0:T(2,128)(2,1)} %param.12), kind=kLoop, calls=%fused_computation.14 | loop fusion | bytes 1179648 | tf_op jit(solution)/shard_map/slice | solution.py:543
  3.1 1.2 shard_map.122
  4.3 7.3 %all-to-all-start = ((bf16[8,64,960]{2,1,0:T(8,128)(2,1)}), bf16[8,64,960]{2,1,0:T(8,128)(2,1)S(1)}, u32[]{:S(2)}, u32[]{:S(2)}) async-start(bf16[8,64,960]{2,1,0:T(8,128)(2,1)} %shard_map.122), calls=%async_computation | async-start | bytes 2097152 | tf_op jit(solution)/shard_map/all_to_all | solution.py:546
  12.0 25.3 %all-to-all-done = bf16[8,64,960]{2,1,0:T(8,128)(2,1)S(1)} async-done(((bf16[8,64,960]{2,1,0:T(8,128)(2,1)}), bf16[8,64,960]{2,1,0:T(8,128)(2,1)S(1)}, u32[]{:S(2)}, u32[]{:S(2)}) %all-to-all-start) | async-done | bytes 983072 | tf_op jit(solution)/shard_map/all_to_all | solution.py:546
  37.3 5.6 %shard_map.123 = bf16[512,320]{1,0:T(8,128)(2,1)} custom-call(bf16[512,960]{1,0:T(8,128)(2,1)S(1)} %bitcast.22, s32[1,512]{1,0:T(1,128)S(1)} %copy-done.6, s32[512,1]{1,0:T(8,128)S(1)} %copy.40.seg_col_ref), custom_call_target="tpu_custom_call" | custom-call | flops 335544320 | bytes 1310720 | tf_op jit(solution)/shard_map/pallas_call | solution.py:56
  42.9 3.6 %all-to-all-start.1 = ((bf16[8,64,320]{2,1,0:T(8,128)(2,1)}), bf16[8,64,320]{2,1,0:T(8,128)(2,1)S(1)}, u32[]{:S(2)}, u32[]{:S(2)}) async-start(bf16[8,64,320]{2,1,0:T(8,128)(2,1)} %bitcast.5), calls=%async_computation.1 | async-start | bytes 786432 | tf_op jit(solution)/shard_map/all_to_all | solution.py:549
  47.3 11.1 %all-to-all-done.1.context_ref = bf16[8,64,320]{2,1,0:T(8,128)(2,1)S(1)} async-done(((bf16[8,64,320]{2,1,0:T(8,128)(2,1)}), bf16[8,64,320]{2,1,0:T(8,128)(2,1)S(1)}, u32[]{:S(2)}, u32[]{:S(2)}) %all-to-all-start.1) | async-done | bytes 327712 | tf_op jit(solution)/shard_map/all_to_all | solution.py:549
  60.3 1.9 collective-permute-start.7
  62.2 1.5 collective-permute-start
  63.8 7.1 %collective-permute-done.3.refs_4_ = bf16[64,2432]{1,0:T(8,128)(2,1)S(1)} collective-permute-done((bf16[64,2432]{1,0:T(8,128)(2,1)S(1)}, bf16[64,2432]{1,0:T(8,128)(2,1)S(1)}, u32[]{:S(2)}, u32[]{:S(2)}) %collective-permute-start.3) | collective-permute-done | bytes 311328 | tf_op jit(solution)/shard_map/ppermute | solution.py:428
  70.9 1.5 collective-permute-start.5
  72.4 3.9 %collective-permute-start.4 = (bf16[64,2432]{1,0:T(8,128)(2,1)S(1)}, bf16[64,2432]{1,0:T(8,128)(2,1)S(1)}, u32[]{:S(2)}, u32[]{:S(2)}) collective-permute-start(bf16[64,2432]{1,0:T(8,128)(2,1)S(1)} %collective-permute-done.3.refs_4_), channel_id=1, source_target_pairs={{0,4},{4,0},{8,12},{12,8},{16,20},{20,16},{24,28},{28,24},{1,5},{5... | collective-permute-start | bytes 933896 | tf_op jit(solution)/shard_map/ppermute | solution.py:428
  76.8 1.5 collective-permute-done.5.refs_3_.refs_6_
  78.3 4.1 %collective-permute-done.4.refs_4_.refs_5_ = bf16[64,2432]{1,0:T(8,128)(2,1)S(1)} collective-permute-done((bf16[64,2432]{1,0:T(8,128)(2,1)S(1)}, bf16[64,2432]{1,0:T(8,128)(2,1)S(1)}, u32[]{:S(2)}, u32[]{:S(2)}) %collective-permute-start.4) | collective-permute-done | bytes 311328 | tf_op jit(solution)/shard_map/ppermute | solution.py:428
  82.5 2.7 %collective-permute-start.6 = (bf16[64,2432]{1,0:T(8,128)(2,1)S(1)}, bf16[64,2432]{1,0:T(8,128)(2,1)S(1)}, u32[]{:S(2)}, u32[]{:S(2)}) collective-permute-start(bf16[64,2432]{1,0:T(8,128)(2,1)S(1)} %collective-permute-done.5.refs_3_.refs_6_), channel_id=1, source_target_pairs={{0,4},{4,0},{8,12},{12,8},{16,20},{20,16},{24,28},{28,24},{1,5},{5... | collective-permute-start | bytes 933896 | tf_op jit(solution)/shard_map/ppermute | solution.py:428
  85.3 4.5 %collective-permute-done.11.refs_0_ = bf16[64,2432]{1,0:T(8,128)(2,1)} collective-permute-done((bf16[64,2432]{1,0:T(8,128)(2,1)S(1)}, bf16[64,2432]{1,0:T(8,128)(2,1)}, u32[]{:S(2)}, u32[]{:S(2)}) %collective-permute-start.11) | collective-permute-done | bytes 311328 | tf_op jit(solution)/shard_map/ppermute | solution.py:428
  89.8 3.7 %collective-permute-done.6.refs_2_.refs_7_ = bf16[64,2432]{1,0:T(8,128)(2,1)S(1)} collective-permute-done((bf16[64,2432]{1,0:T(8,128)(2,1)S(1)}, bf16[64,2432]{1,0:T(8,128)(2,1)S(1)}, u32[]{:S(2)}, u32[]{:S(2)}) %collective-permute-start.6) | collective-permute-done | bytes 311328 | tf_op jit(solution)/shard_map/ppermute | solution.py:428
  93.5 1.5 collective-permute-start.13
  95.5 2.0 collective-permute-start.12
  97.5 2.7 %collective-permute-done.9.refs_2_ = bf16[64,2432]{1,0:T(8,128)(2,1)} collective-permute-done((bf16[64,2432]{1,0:T(8,128)(2,1)S(1)}, bf16[64,2432]{1,0:T(8,128)(2,1)}, u32[]{:S(2)}, u32[]{:S(2)}) %collective-permute-start.9) | collective-permute-done | bytes 311328 | tf_op jit(solution)/shard_map/ppermute | solution.py:428
  100.2 1.5 collective-permute-start.10
  101.8 1.4 collective-permute-done.13.refs_6_
  104.3 2.2 collective-permute-done.8.refs_1_
  106.5 3.3 %collective-permute-done.10.refs_3_ = bf16[64,2432]{1,0:T(8,128)(2,1)} collective-permute-done((bf16[64,2432]{1,0:T(8,128)(2,1)}, bf16[64,2432]{1,0:T(8,128)(2,1)}, u32[]{:S(2)}, u32[]{:S(2)}) %collective-permute-start.10) | collective-permute-done | bytes 311328 | tf_op jit(solution)/shard_map/ppermute | solution.py:428
  110.4 4.2 %shard_map.127 = (bf16[2,192,2304]{2,1,0:T(8,128)(2,1)S(1)}, bf16[2,192,2304]{2,1,0:T(8,128)(2,1)}, bf16[512,128]{1,0:T(8,128)(2,1)S(1)}) custom-call(s32[2]{0:T(128)S(1)} %add_multiply_fusion.bases_ref, bf16[64,2432]{1,0:T(8,128)(2,1)S(1)} %shard_map.125.refs_0_, bf16[64,2432]{1,0:T(8,128)(2,1)} %collective-permute-done.8.refs_1_, ...), custom_call_target="tpu_custom_call" | custom-call | flops 905969664 | bytes 6029312 | tf_op jit(solution)/shard_map/pallas_call | solution.py:300
  114.6 1.2 copy-done.13
  115.9 1.7 shard_map.128.refs_8_.rest_1_
  117.6 3.1 %shard_map.129 = (bf16[2,192,2304]{2,1,0:T(8,128)(2,1)S(1)}, bf16[2,192,2304]{2,1,0:T(8,128)(2,1)}, bf16[512,128]{1,0:T(8,128)(2,1)S(1)}) custom-call(s32[2]{0:T(128)S(1)} %add_multiply_fusion.bases_ref, bf16[64,2432]{1,0:T(8,128)(2,1)S(1)} %copy-done.8, bf16[64,2432]{1,0:T(8,128)(2,1)S(1)} %collective-permute-done.refs_2_.refs_1_, ...), custom_call_target="tpu_custom_call" | custom-call | flops 905969664 | bytes 6029312 | tf_op jit(solution)/shard_map/pallas_call | solution.py:300
  120.7 1.3 copy-done.11
  122.5 3.7 %all-to-all-start.2 = ((bf16[8,64,640]{2,1,0:T(8,128)(2,1)}), bf16[8,64,640]{2,1,0:T(8,128)(2,1)S(1)}, u32[]{:S(2)}, u32[]{:S(2)}) async-start(bf16[8,64,640]{2,1,0:T(8,128)(2,1)} %shard_map.128.refs_8_.rest_1_), calls=%async_computation.2 | async-start | bytes 1310720 | tf_op jit(solution)/shard_map/all_to_all | solution.py:566
  126.3 1.5 copy-done.14
  127.7 16.2 %shard_map.130 = (bf16[2,192,2304]{2,1,0:T(8,128)(2,1)S(1)}, bf16[2,192,2304]{2,1,0:T(8,128)(2,1)}, f32[8,128]{1,0:T(8,128)S(1)}) custom-call(bf16[2,192,2304]{2,1,0:T(8,128)(2,1)S(1)} %copy-done.14, bf16[2,192,2304]{2,1,0:T(8,128)(2,1)} %collective-permute-done.16.got_ref, bf16[2,720,2304]{2,1,0:T(8,128)(2,1)} %bitcast.28, bf16[2,720,2304]{2,1,0:T(8,128)(2,1)} %bitcast.30, ...), custom_call_target="tpu_custom_call" | custom-call | flops 7644119040 | bytes 26984448 | tf_op jit(solution)/shard_map/pallas_call | solution.py:352
  145.0 1.5 copy-done.12
  146.5 15.2 %shard_map.132 = (bf16[2,192,2304]{2,1,0:T(8,128)(2,1)S(1)}, bf16[2,192,2304]{2,1,0:T(8,128)(2,1)S(1)}, f32[8,128]{1,0:T(8,128)S(1)}) custom-call(bf16[2,192,2304]{2,1,0:T(8,128)(2,1)S(1)} %copy-done.12, bf16[2,192,2304]{2,1,0:T(8,128)(2,1)} %collective-permute-done.15.got_ref, bf16[2,720,2304]{2,1,0:T(8,128)(2,1)} %bitcast.29, ...), custom_call_target="tpu_custom_call" | custom-call | flops 7644119040 | bytes 26984448 | tf_op jit(solution)/shard_map/pallas_call | solution.py:352
  162.2 4.8 %shard_map.133 = (bf16[256,2304]{1,0:T(8,128)(2,1)S(1)}, bf16[128,2304]{1,0:T(8,128)(2,1)S(1)}, bf16[128,2304]{1,0:T(8,128)(2,1)S(1)}, f32[8,128]{1,0:T(8,128)}) custom-call(s32[2]{0:T(128)S(1)} %add_multiply_fusion.bases_ref, bf16[2,192,2304]{2,1,0:T(8,128)(2,1)S(1)} %get-tuple-element.47.y_own_ref, ...), custom_call_target="tpu_custom_call" | custom-call | flops 905969664 | bytes 18874368 | tf_op jit(solution)/shard_map/pallas_call | solution.py:409
  167.0 2.0 collective-permute-start.19
  169.9 12.6 %collective-permute-done.19.rest_0_ = bf16[128,2304]{1,0:T(8,128)(2,1)S(1)} collective-permute-done((bf16[128,2304]{1,0:T(8,128)(2,1)S(1)}, bf16[128,2304]{1,0:T(8,128)(2,1)S(1)}, u32[]{:S(2)}, u32[]{:S(2)}) %collective-permute-start.19) | collective-permute-done | bytes 589856 | tf_op jit(solution)/shard_map/ppermute | solution.py:428
  182.5 1.5 collective-permute-done.20.rest_1_
  185.5 3.4 %shard_map.135 = (bf16[256,2304]{1,0:T(8,128)(2,1)S(1)}, bf16[128,2304]{1,0:T(8,128)(2,1)S(1)}, bf16[128,2304]{1,0:T(8,128)(2,1)S(1)}, f32[8,128]{1,0:T(8,128)S(1)}) custom-call(s32[2]{0:T(128)S(1)} %add_multiply_fusion.bases_ref, bf16[2,192,2304]{2,1,0:T(8,128)(2,1)S(1)} %get-tuple-element.45.y_own_ref, ...), custom_call_target="tpu_custom_call" | custom-call | flops 905969664 | bytes 18874368 | tf_op jit(solution)/shard_map/pallas_call | solution.py:409
  188.9 3.2 %collective-permute-done.21.refs_1_.rest_0_ = bf16[64,2304]{1,0:T(8,128)(2,1)S(1)} collective-permute-done((bf16[64,2304]{1,0:T(8,128)(2,1)S(1)}, bf16[64,2304]{1,0:T(8,128)(2,1)S(1)}, u32[]{:S(2)}, u32[]{:S(2)}) %collective-permute-start.21) | collective-permute-done | bytes 294944 | tf_op jit(solution)/shard_map/ppermute | solution.py:428
  192.8 1.5 collective-permute-start.25
  196.1 3.5 %collective-permute-done.25 = bf16[64,2304]{1,0:T(8,128)(2,1)S(1)} collective-permute-done((bf16[64,2304]{1,0:T(8,128)(2,1)S(1)}, bf16[64,2304]{1,0:T(8,128)(2,1)S(1)}, u32[]{:S(2)}, u32[]{:S(2)}) %collective-permute-start.25) | collective-permute-done | bytes 294944 | tf_op jit(solution)/shard_map/ppermute | solution.py:428
  199.7 3.1 %collective-permute-start.28 = (bf16[64,2304]{1,0:T(8,128)(2,1)S(1)}, bf16[64,2304]{1,0:T(8,128)(2,1)S(1)}, u32[]{:S(2)}, u32[]{:S(2)}) collective-permute-start(bf16[64,2304]{1,0:T(8,128)(2,1)S(1)} %add_convert_fusion.1.rest_2_), channel_id=1, source_target_pairs={{0,16},{4,20},{8,24},{12,28},{16,0},{20,4},{24,8},{28,12},{1,17},{... | collective-permute-start | bytes 884744 | tf_op jit(solution)/shard_map/ppermute | solution.py:428
  202.8 4.2 %collective-permute-done.23.rest_0_ = bf16[128,2304]{1,0:T(8,128)(2,1)S(1)} collective-permute-done((bf16[128,2304]{1,0:T(8,128)(2,1)S(1)}, bf16[128,2304]{1,0:T(8,128)(2,1)S(1)}, u32[]{:S(2)}, u32[]{:S(2)}) %collective-permute-start.23) | collective-permute-done | bytes 589856 | tf_op jit(solution)/shard_map/ppermute | solution.py:428
  209.6 1.4 collective-permute-start.27
  211.0 1.4 collective-permute-done.28.rest_2_
  212.4 2.8 %collective-permute-done.26.rest_0_ = bf16[64,2304]{1,0:T(8,128)(2,1)S(1)} collective-permute-done((bf16[64,2304]{1,0:T(8,128)(2,1)S(1)}, bf16[64,2304]{1,0:T(8,128)(2,1)S(1)}, u32[]{:S(2)}, u32[]{:S(2)}) %collective-permute-start.26) | collective-permute-done | bytes 294944 | tf_op jit(solution)/shard_map/ppermute | solution.py:428
  217.1 6.2 %collective-permute-done.29 = bf16[64,2304]{1,0:T(8,128)(2,1)S(1)} collective-permute-done((bf16[64,2304]{1,0:T(8,128)(2,1)S(1)}, bf16[64,2304]{1,0:T(8,128)(2,1)S(1)}, u32[]{:S(2)}, u32[]{:S(2)}) %collective-permute-start.29) | collective-permute-done | bytes 294944 | tf_op jit(solution)/shard_map/ppermute | solution.py:428
  (94 shorter events, 18.6 us)
Async XLA Ops:
  0.6 2.4 %copy-start.5 = (bf16[1,64,2304]{2,1,0:T(8,128)(2,1)S(1)}, bf16[1,64,2304]{2,1,0:T(8,128)(2,1)}, u32[]{:S(2)}) copy-start(bf16[1,64,2304]{2,1,0:T(8,128)(2,1)} %param.11) | copy-start | bytes 884740
  3.0 8.5 %copy-start.6 = (s32[1,512]{1,0:T(1,128)S(1)}, s32[1,512]{1,0:T(1,128)}, u32[]{:S(2)}) copy-start(s32[1,512]{1,0:T(1,128)} %seg_row_ref.1) | copy-start | bytes 6148
  3.0 8.7 %copy-start.15 = (bf16[2304]{0:T(1024)(128)(2,1)S(1)}, bf16[2304]{0:T(1024)(128)(2,1)}, u32[]{:S(2)}) copy-start(bf16[2304]{0:T(1024)(128)(2,1)} %param.14) | copy-start | bytes 13828
  3.1 8.7 %copy-start.16 = (s32[1,64,2]{1,2,0:T(2,128)S(1)}, s32[1,64,2]{1,2,0:T(2,128)}, u32[]{:S(2)}) copy-start(s32[1,64,2]{1,2,0:T(2,128)} %param.16) | copy-start | bytes 1540
  4.3 33.0 %all-to-all-start = ((bf16[8,64,960]{2,1,0:T(8,128)(2,1)}), bf16[8,64,960]{2,1,0:T(8,128)(2,1)S(1)}, u32[]{:S(2)}, u32[]{:S(2)}) async-start(bf16[8,64,960]{2,1,0:T(8,128)(2,1)} %shard_map.122), calls=%async_computation | async-start | bytes 2097152 | tf_op jit(solution)/shard_map/all_to_all | solution.py:546
  37.3 9.9 %copy-start.17 = (f32[1,64,2]{1,2,0:T(2,128)S(1)}, f32[1,64,2]{1,2,0:T(2,128)}, u32[]{:S(2)}) copy-start(f32[1,64,2]{1,2,0:T(2,128)} %param.17) | copy-start | bytes 1540
  37.3 21.1 %copy-start.4 = (bf16[1,64,2304]{2,1,0:T(8,128)(2,1)S(1)}, bf16[1,64,2304]{2,1,0:T(8,128)(2,1)}, u32[]{:S(2)}) copy-start(bf16[1,64,2304]{2,1,0:T(8,128)(2,1)} %param.13) | copy-start | bytes 884740
  42.9 15.5 %all-to-all-start.1 = ((bf16[8,64,320]{2,1,0:T(8,128)(2,1)}), bf16[8,64,320]{2,1,0:T(8,128)(2,1)S(1)}, u32[]{:S(2)}, u32[]{:S(2)}) async-start(bf16[8,64,320]{2,1,0:T(8,128)(2,1)} %bitcast.5), calls=%async_computation.1 | async-start | bytes 786432 | tf_op jit(solution)/shard_map/all_to_all | solution.py:549
  58.7 44.5 %copy-start.7 = (bf16[64,2432]{1,0:T(8,128)(2,1)}, bf16[64,2432]{1,0:T(8,128)(2,1)S(1)}, u32[]{:S(2)}) copy-start(bf16[64,2432]{1,0:T(8,128)(2,1)S(1)} %get-tuple-element.36.refs_0_) | copy-start | bytes 933892
  58.7 12.2 %collective-permute-start.3 = (bf16[64,2432]{1,0:T(8,128)(2,1)S(1)}, bf16[64,2432]{1,0:T(8,128)(2,1)S(1)}, u32[]{:S(2)}, u32[]{:S(2)}) collective-permute-start(bf16[64,2432]{1,0:T(8,128)(2,1)S(1)} %get-tuple-element.36.refs_0_), channel_id=1, source_target_pairs={{0,8},{4,12},{8,0},{12,4},{16,24},{20,28},{24,16},{28,20},{1,9},{5... | collective-permute-start | bytes 933896 | tf_op jit(solution)/shard_map/ppermute | solution.py:428
  59.7 16.6 %collective-permute-start.1 = (bf16[64,2432]{1,0:T(8,128)(2,1)S(1)}, bf16[64,2432]{1,0:T(8,128)(2,1)S(1)}, u32[]{:S(2)}, u32[]{:S(2)}) collective-permute-start(bf16[64,2432]{1,0:T(8,128)(2,1)S(1)} %get-tuple-element.36.refs_0_), channel_id=1, source_target_pairs={{0,4},{4,0},{8,12},{12,8},{16,20},{20,16},{24,28},{28,24},{1,5},{5... | collective-permute-start | bytes 933896 | tf_op jit(solution)/shard_map/ppermute | solution.py:428
  60.3 16.5 %collective-permute-start.7 = (bf16[64,2432]{1,0:T(8,128)(2,1)S(1)}, bf16[64,2432]{1,0:T(8,128)(2,1)S(1)}, u32[]{:S(2)}, u32[]{:S(2)}) collective-permute-start(bf16[64,2432]{1,0:T(8,128)(2,1)S(1)} %get-tuple-element.36.refs_0_), channel_id=1, source_target_pairs={{0,16},{4,20},{8,24},{12,28},{16,0},{20,4},{24,8},{28,12},{1,17},{... | collective-permute-start | bytes 933896 | tf_op jit(solution)/shard_map/ppermute | solution.py:428
  62.2 14.6 %collective-permute-start = (bf16[64,2432]{1,0:T(8,128)(2,1)S(1)}, bf16[64,2432]{1,0:T(8,128)(2,1)S(1)}, u32[]{:S(2)}, u32[]{:S(2)}) collective-permute-start(bf16[64,2432]{1,0:T(8,128)(2,1)S(1)} %get-tuple-element.36.refs_0_), channel_id=1, source_target_pairs={{0,2},{1,3},{2,0},{3,1},{4,6},{5,7},{6,4},{7,5},{8,10},{9,11},{10,... | collective-permute-start | bytes 933896 | tf_op jit(solution)/shard_map/ppermute | solution.py:428
  70.9 11.6 %copy-start.9 = (bf16[64,2432]{1,0:T(8,128)(2,1)}, bf16[64,2432]{1,0:T(8,128)(2,1)S(1)}, u32[]{:S(2)}) copy-start(bf16[64,2432]{1,0:T(8,128)(2,1)S(1)} %collective-permute-done.3.refs_4_) | copy-start | bytes 933892
  70.9 7.4 %collective-permute-start.5 = (bf16[64,2432]{1,0:T(8,128)(2,1)S(1)}, bf16[64,2432]{1,0:T(8,128)(2,1)S(1)}, u32[]{:S(2)}, u32[]{:S(2)}) collective-permute-start(bf16[64,2432]{1,0:T(8,128)(2,1)S(1)} %collective-permute-done.3.refs_4_), channel_id=1, source_target_pairs={{0,2},{1,3},{2,0},{3,1},{4,6},{5,7},{6,4},{7,5},{8,10},{9,11},{10,... | collective-permute-start | bytes 933896 | tf_op jit(solution)/shard_map/ppermute | solution.py:428
  72.4 10.0 %collective-permute-start.4 = (bf16[64,2432]{1,0:T(8,128)(2,1)S(1)}, bf16[64,2432]{1,0:T(8,128)(2,1)S(1)}, u32[]{:S(2)}, u32[]{:S(2)}) collective-permute-start(bf16[64,2432]{1,0:T(8,128)(2,1)S(1)} %collective-permute-done.3.refs_4_), channel_id=1, source_target_pairs={{0,4},{4,0},{8,12},{12,8},{16,20},{20,16},{24,28},{28,24},{1,5},{5... | collective-permute-start | bytes 933896 | tf_op jit(solution)/shard_map/ppermute | solution.py:428
  76.3 8.9 %collective-permute-start.2 = (bf16[64,2432]{1,0:T(8,128)(2,1)S(1)}, bf16[64,2432]{1,0:T(8,128)(2,1)S(1)}, u32[]{:S(2)}, u32[]{:S(2)}) collective-permute-start(bf16[64,2432]{1,0:T(8,128)(2,1)S(1)} %collective-permute-done.1.refs_1_.refs_2_), channel_id=1, source_target_pairs={{0,2},{1,3},{2,0},{3,1},{4,6},{5,7},{6,4},{7,5},{8,10},{9,11},{10,... | collective-permute-start | bytes 933896 | tf_op jit(solution)/shard_map/ppermute | solution.py:428
  82.5 7.3 %collective-permute-start.11 = (bf16[64,2432]{1,0:T(8,128)(2,1)S(1)}, bf16[64,2432]{1,0:T(8,128)(2,1)}, u32[]{:S(2)}, u32[]{:S(2)}) collective-permute-start(bf16[64,2432]{1,0:T(8,128)(2,1)S(1)} %shard_map.125.refs_0_), channel_id=1, source_target_pairs={{0,8},{4,12},{8,0},{12,4},{16,24},{20,28},{24,16},{28,20},{1,9},{5... | collective-permute-start | bytes 933896 | tf_op jit(solution)/shard_map/ppermute | solution.py:428
  82.5 11.0 %collective-permute-start.6 = (bf16[64,2432]{1,0:T(8,128)(2,1)S(1)}, bf16[64,2432]{1,0:T(8,128)(2,1)S(1)}, u32[]{:S(2)}, u32[]{:S(2)}) collective-permute-start(bf16[64,2432]{1,0:T(8,128)(2,1)S(1)} %collective-permute-done.5.refs_3_.refs_6_), channel_id=1, source_target_pairs={{0,4},{4,0},{8,12},{12,8},{16,20},{20,16},{24,28},{28,24},{1,5},{5... | collective-permute-start | bytes 933896 | tf_op jit(solution)/shard_map/ppermute | solution.py:428
  85.2 15.1 %collective-permute-start.9 = (bf16[64,2432]{1,0:T(8,128)(2,1)S(1)}, bf16[64,2432]{1,0:T(8,128)(2,1)}, u32[]{:S(2)}, u32[]{:S(2)}) collective-permute-start(bf16[64,2432]{1,0:T(8,128)(2,1)S(1)} %shard_map.125.refs_0_), channel_id=1, source_target_pairs={{0,4},{4,0},{8,12},{12,8},{16,20},{20,16},{24,28},{28,24},{1,5},{5... | collective-permute-start | bytes 933896 | tf_op jit(solution)/shard_map/ppermute | solution.py:428
  85.3 15.0 %copy-start = (bf16[64,2432]{1,0:T(8,128)(2,1)}, bf16[64,2432]{1,0:T(8,128)(2,1)S(1)}, u32[]{:S(2)}) copy-start(bf16[64,2432]{1,0:T(8,128)(2,1)S(1)} %collective-permute-done.2.refs_1_.refs_3_) | copy-start | bytes 933892
  93.5 8.3 %copy-start.2 = (bf16[64,2432]{1,0:T(8,128)(2,1)}, bf16[64,2432]{1,0:T(8,128)(2,1)S(1)}, u32[]{:S(2)}) copy-start(bf16[64,2432]{1,0:T(8,128)(2,1)S(1)} %collective-permute-done.6.refs_2_.refs_7_) | copy-start | bytes 933892
  93.5 22.3 %copy-start.18 = (s32[1,32]{1,0:T(1,128)S(1)}, s32[1,32]{1,0:T(1,128)}, u32[]{:S(2)}) copy-start(s32[1,32]{1,0:T(1,128)} %param.18) | copy-start | bytes 388
  93.5 9.7 %collective-permute-start.13 = (bf16[64,2432]{1,0:T(8,128)(2,1)}, bf16[64,2432]{1,0:T(8,128)(2,1)}, u32[]{:S(2)}, u32[]{:S(2)}) collective-permute-start(bf16[64,2432]{1,0:T(8,128)(2,1)} %shard_map.126.refs_4_), channel_id=1, source_target_pairs={{0,2},{1,3},{2,0},{3,1},{4,6},{5,7},{6,4},{7,5},{8,10},{9,11},{10,... | collective-permute-start | bytes 933896 | tf_op jit(solution)/shard_map/ppermute | solution.py:428
  95.0 11.5 %collective-permute-start.8 = (bf16[64,2432]{1,0:T(8,128)(2,1)S(1)}, bf16[64,2432]{1,0:T(8,128)(2,1)}, u32[]{:S(2)}, u32[]{:S(2)}) collective-permute-start(bf16[64,2432]{1,0:T(8,128)(2,1)S(1)} %shard_map.125.refs_0_), channel_id=1, source_target_pairs={{0,2},{1,3},{2,0},{3,1},{4,6},{5,7},{6,4},{7,5},{8,10},{9,11},{10,... | collective-permute-start | bytes 933896 | tf_op jit(solution)/shard_map/ppermute | solution.py:428
  95.5 14.4 %collective-permute-start.12 = (bf16[64,2432]{1,0:T(8,128)(2,1)}, bf16[64,2432]{1,0:T(8,128)(2,1)}, u32[]{:S(2)}, u32[]{:S(2)}) collective-permute-start(bf16[64,2432]{1,0:T(8,128)(2,1)} %shard_map.126.refs_4_), channel_id=1, source_target_pairs={{0,4},{4,0},{8,12},{12,8},{16,20},{20,16},{24,28},{28,24},{1,5},{5... | collective-permute-start | bytes 933896 | tf_op jit(solution)/shard_map/ppermute | solution.py:428
  100.2 9.6 %collective-permute-start.10 = (bf16[64,2432]{1,0:T(8,128)(2,1)}, bf16[64,2432]{1,0:T(8,128)(2,1)}, u32[]{:S(2)}, u32[]{:S(2)}) collective-permute-start(bf16[64,2432]{1,0:T(8,128)(2,1)} %collective-permute-done.9.refs_2_), channel_id=1, source_target_pairs={{0,2},{1,3},{2,0},{3,1},{4,6},{5,7},{6,4},{7,5},{8,10},{9,11},{10,... | collective-permute-start | bytes 933896 | tf_op jit(solution)/shard_map/ppermute | solution.py:428
  103.2 7.2 %collective-permute-start.14 = (bf16[64,2432]{1,0:T(8,128)(2,1)}, bf16[64,2432]{1,0:T(8,128)(2,1)}, u32[]{:S(2)}, u32[]{:S(2)}) collective-permute-start(bf16[64,2432]{1,0:T(8,128)(2,1)} %collective-permute-done.13.refs_6_), channel_id=1, source_target_pairs={{0,4},{4,0},{8,12},{12,8},{16,20},{20,16},{24,28},{28,24},{1,5},{5... | collective-permute-start | bytes 933896 | tf_op jit(solution)/shard_map/ppermute | solution.py:428
  104.3 13.2 %copy-start.1 = (bf16[64,2432]{1,0:T(8,128)(2,1)S(1)}, bf16[64,2432]{1,0:T(8,128)(2,1)}, u32[]{:S(2)}) copy-start(bf16[64,2432]{1,0:T(8,128)(2,1)} %copy-done) | copy-start | bytes 933892
  104.3 13.2 %copy-start.3 = (bf16[64,2432]{1,0:T(8,128)(2,1)S(1)}, bf16[64,2432]{1,0:T(8,128)(2,1)}, u32[]{:S(2)}) copy-start(bf16[64,2432]{1,0:T(8,128)(2,1)} %copy-done.2) | copy-start | bytes 933892
  104.3 13.2 %copy-start.8 = (bf16[64,2432]{1,0:T(8,128)(2,1)S(1)}, bf16[64,2432]{1,0:T(8,128)(2,1)}, u32[]{:S(2)}) copy-start(bf16[64,2432]{1,0:T(8,128)(2,1)} %copy-done.7) | copy-start | bytes 933892
  104.3 13.2 %copy-start.10 = (bf16[64,2432]{1,0:T(8,128)(2,1)S(1)}, bf16[64,2432]{1,0:T(8,128)(2,1)}, u32[]{:S(2)}) copy-start(bf16[64,2432]{1,0:T(8,128)(2,1)} %copy-done.9) | copy-start | bytes 933892
  115.8 10.5 %collective-permute-start.16 = (bf16[2,192,2304]{2,1,0:T(8,128)(2,1)}, bf16[2,192,2304]{2,1,0:T(8,128)(2,1)}, u32[]{:S(2)}, u32[]{:S(2)}) collective-permute-start(bf16[2,192,2304]{2,1,0:T(8,128)(2,1)} %get-tuple-element.41), channel_id=1, source_target_pairs={{0,1},{1,0},{2,3},{3,2},{4,5},{5,4},{6,7},{7,6},{8,9},{9,8},{10,11... | collective-permute-start | bytes 5308424 | tf_op jit(solution)/shard_map/ppermute | solution.py:428
  122.0 23.0 %collective-permute-start.15 = (bf16[2,192,2304]{2,1,0:T(8,128)(2,1)}, bf16[2,192,2304]{2,1,0:T(8,128)(2,1)}, u32[]{:S(2)}, u32[]{:S(2)}) collective-permute-start(bf16[2,192,2304]{2,1,0:T(8,128)(2,1)} %get-tuple-element.39), channel_id=1, source_target_pairs={{0,1},{1,0},{2,3},{3,2},{4,5},{5,4},{6,7},{7,6},{8,9},{9,8},{10,11... | collective-permute-start | bytes 5308424 | tf_op jit(solution)/shard_map/ppermute | solution.py:428
  122.5 21.5 %all-to-all-start.2 = ((bf16[8,64,640]{2,1,0:T(8,128)(2,1)}), bf16[8,64,640]{2,1,0:T(8,128)(2,1)S(1)}, u32[]{:S(2)}, u32[]{:S(2)}) async-start(bf16[8,64,640]{2,1,0:T(8,128)(2,1)} %shard_map.128.refs_8_.rest_1_), calls=%async_computation.2 | async-start | bytes 1310720 | tf_op jit(solution)/shard_map/all_to_all | solution.py:566
  143.9 18.3 %collective-permute-start.18 = (bf16[2,192,2304]{2,1,0:T(8,128)(2,1)}, bf16[2,192,2304]{2,1,0:T(8,128)(2,1)}, u32[]{:S(2)}, u32[]{:S(2)}) collective-permute-start(bf16[2,192,2304]{2,1,0:T(8,128)(2,1)} %get-tuple-element.48), channel_id=1, source_target_pairs={{0,1},{1,0},{2,3},{3,2},{4,5},{5,4},{6,7},{7,6},{8,9},{9,8},{10,11... | collective-permute-start | bytes 5308424 | tf_op jit(solution)/shard_map/ppermute | solution.py:428
  161.6 23.8 %collective-permute-start.17 = (bf16[2,192,2304]{2,1,0:T(8,128)(2,1)S(1)}, bf16[2,192,2304]{2,1,0:T(8,128)(2,1)S(1)}, u32[]{:S(2)}, u32[]{:S(2)}) collective-permute-start(bf16[2,192,2304]{2,1,0:T(8,128)(2,1)S(1)} %get-tuple-element.46), channel_id=1, source_target_pairs={{0,1},{1,0},{2,3},{3,2},{4,5},{5,4},{6,7},{7,6},{8,9},{9,8},{10,11... | collective-permute-start | bytes 5308424 | tf_op jit(solution)/shard_map/ppermute | solution.py:428
  167.0 15.5 %collective-permute-start.19 = (bf16[128,2304]{1,0:T(8,128)(2,1)S(1)}, bf16[128,2304]{1,0:T(8,128)(2,1)S(1)}, u32[]{:S(2)}, u32[]{:S(2)}) collective-permute-start(bf16[128,2304]{1,0:T(8,128)(2,1)S(1)} %get-tuple-element.51), channel_id=1, source_target_pairs={{0,4},{4,0},{8,12},{12,8},{16,20},{20,16},{24,28},{28,24},{1,5},{5... | collective-permute-start | bytes 1769480 | tf_op jit(solution)/shard_map/ppermute | solution.py:428
  169.0 15.0 %collective-permute-start.20 = (bf16[128,2304]{1,0:T(8,128)(2,1)S(1)}, bf16[128,2304]{1,0:T(8,128)(2,1)S(1)}, u32[]{:S(2)}, u32[]{:S(2)}) collective-permute-start(bf16[128,2304]{1,0:T(8,128)(2,1)S(1)} %get-tuple-element.52), channel_id=1, source_target_pairs={{0,2},{1,3},{2,0},{3,1},{4,6},{5,7},{6,4},{7,5},{8,10},{9,11},{10,... | collective-permute-start | bytes 1769480 | tf_op jit(solution)/shard_map/ppermute | solution.py:428
  184.2 7.8 %collective-permute-start.21 = (bf16[64,2304]{1,0:T(8,128)(2,1)S(1)}, bf16[64,2304]{1,0:T(8,128)(2,1)S(1)}, u32[]{:S(2)}, u32[]{:S(2)}) collective-permute-start(bf16[64,2304]{1,0:T(8,128)(2,1)S(1)} %get-tuple-element.53.rest_0_), channel_id=1, source_target_pairs={{0,2},{1,3},{2,0},{3,1},{4,6},{5,7},{6,4},{7,5},{8,10},{9,11},{10,... | collective-permute-start | bytes 884744 | tf_op jit(solution)/shard_map/ppermute | solution.py:428
  185.2 7.5 %collective-permute-start.22 = (bf16[64,2304]{1,0:T(8,128)(2,1)S(1)}, bf16[64,2304]{1,0:T(8,128)(2,1)S(1)}, u32[]{:S(2)}, u32[]{:S(2)}) collective-permute-start(bf16[64,2304]{1,0:T(8,128)(2,1)S(1)} %get-tuple-element.56), channel_id=1, source_target_pairs={{0,4},{4,0},{8,12},{12,8},{16,20},{20,16},{24,28},{28,24},{1,5},{5... | collective-permute-start | bytes 884744 | tf_op jit(solution)/shard_map/ppermute | solution.py:428
  192.8 6.8 %collective-permute-start.25 = (bf16[64,2304]{1,0:T(8,128)(2,1)S(1)}, bf16[64,2304]{1,0:T(8,128)(2,1)S(1)}, u32[]{:S(2)}, u32[]{:S(2)}) collective-permute-start(bf16[64,2304]{1,0:T(8,128)(2,1)S(1)} %get-tuple-element.61), channel_id=1, source_target_pairs={{0,8},{4,12},{8,0},{12,4},{16,24},{20,28},{24,16},{28,20},{1,9},{5... | collective-permute-start | bytes 884744 | tf_op jit(solution)/shard_map/ppermute | solution.py:428
  194.4 12.6 %collective-permute-start.23 = (bf16[128,2304]{1,0:T(8,128)(2,1)S(1)}, bf16[128,2304]{1,0:T(8,128)(2,1)S(1)}, u32[]{:S(2)}, u32[]{:S(2)}) collective-permute-start(bf16[128,2304]{1,0:T(8,128)(2,1)S(1)} %shard_map.136), channel_id=1, source_target_pairs={{0,4},{4,0},{8,12},{12,8},{16,20},{20,16},{24,28},{28,24},{1,5},{5... | collective-permute-start | bytes 1769480 | tf_op jit(solution)/shard_map/ppermute | solution.py:428
  195.0 13.2 %collective-permute-start.24 = (bf16[128,2304]{1,0:T(8,128)(2,1)S(1)}, bf16[128,2304]{1,0:T(8,128)(2,1)S(1)}, u32[]{:S(2)}, u32[]{:S(2)}) collective-permute-start(bf16[128,2304]{1,0:T(8,128)(2,1)S(1)} %shard_map.137), channel_id=1, source_target_pairs={{0,2},{1,3},{2,0},{3,1},{4,6},{5,7},{6,4},{7,5},{8,10},{9,11},{10,... | collective-permute-start | bytes 1769480 | tf_op jit(solution)/shard_map/ppermute | solution.py:428
  199.7 12.7 %collective-permute-start.28 = (bf16[64,2304]{1,0:T(8,128)(2,1)S(1)}, bf16[64,2304]{1,0:T(8,128)(2,1)S(1)}, u32[]{:S(2)}, u32[]{:S(2)}) collective-permute-start(bf16[64,2304]{1,0:T(8,128)(2,1)S(1)} %add_convert_fusion.1.rest_2_), channel_id=1, source_target_pairs={{0,16},{4,20},{8,24},{12,28},{16,0},{20,4},{24,8},{28,12},{1,17},{... | collective-permute-start | bytes 884744 | tf_op jit(solution)/shard_map/ppermute | solution.py:428
  208.4 6.8 %collective-permute-start.26 = (bf16[64,2304]{1,0:T(8,128)(2,1)S(1)}, bf16[64,2304]{1,0:T(8,128)(2,1)S(1)}, u32[]{:S(2)}, u32[]{:S(2)}) collective-permute-start(bf16[64,2304]{1,0:T(8,128)(2,1)S(1)} %get-tuple-element.63), channel_id=1, source_target_pairs={{0,2},{1,3},{2,0},{3,1},{4,6},{5,7},{6,4},{7,5},{8,10},{9,11},{10,... | collective-permute-start | bytes 884744 | tf_op jit(solution)/shard_map/ppermute | solution.py:428
  209.6 6.7 %collective-permute-start.27 = (bf16[64,2304]{1,0:T(8,128)(2,1)S(1)}, bf16[64,2304]{1,0:T(8,128)(2,1)S(1)}, u32[]{:S(2)}, u32[]{:S(2)}) collective-permute-start(bf16[64,2304]{1,0:T(8,128)(2,1)S(1)} %get-tuple-element.64), channel_id=1, source_target_pairs={{0,4},{4,0},{8,12},{12,8},{16,20},{20,16},{24,28},{28,24},{1,5},{5... | collective-permute-start | bytes 884744 | tf_op jit(solution)/shard_map/ppermute | solution.py:428
  216.4 6.8 %collective-permute-start.29 = (bf16[64,2304]{1,0:T(8,128)(2,1)S(1)}, bf16[64,2304]{1,0:T(8,128)(2,1)S(1)}, u32[]{:S(2)}, u32[]{:S(2)}) collective-permute-start(bf16[64,2304]{1,0:T(8,128)(2,1)S(1)} %get-tuple-element.66), channel_id=1, source_target_pairs={{0,8},{4,12},{8,0},{12,4},{16,24},{20,28},{24,16},{28,20},{1,9},{5... | collective-permute-start | bytes 884744 | tf_op jit(solution)/shard_map/ppermute | solution.py:428
  (4 other events, 5.5 us)

commit v15 on v14

--- a/solution.py
+++ b/solution.py
@@ -141,13 +141,14 @@
     )(first, x, tgt, gates, w_gate, w_up, w_down)
 
 
-def pack_kernel(firsts, span, q_ref, k_ref, v_ref, out_ref):
+def pack_kernel(firsts, span, q_ref, kv_ref, out_ref):
+    keys, values = kv_ref[:, 0, :], kv_ref[:, 1, :]
     for j, first in enumerate(firsts):
         lanes = slice(first * HEAD_DIM, first * HEAD_DIM + span)
-        out_ref[j] = jnp.concatenate([r[:, lanes] for r in (q_ref, k_ref, v_ref)], axis=1)
-
-
-def pack_heads(query, keys, values, firsts, span):
+        out_ref[j] = jnp.concatenate([q_ref[:, lanes], keys[:, lanes], values[:, lanes]], axis=1)
+
+
+def pack_heads(query, key_value, firsts, span):
     rows_dev = query.shape[0]
     n_seq = len(firsts)
     return pl.pallas_call(
@@ -155,7 +156,7 @@
         out_shape=jax.ShapeDtypeStruct((n_seq, rows_dev, 3 * span), jnp.bfloat16),
         compiler_params=pltpu.CompilerParams(vmem_limit_bytes=12 * MIB),
         cost_estimate=pl.CostEstimate(flops=0, bytes_accessed=12 * n_seq * rows_dev * span, transcendentals=0),
-    )(query, keys, values)
+    )(query, key_value)
 
 
 def norm_kernel(share, offsets, context_ref, residual_ref, gain_ref, facts_ref, stream_ref, piece_ref):
@@ -540,9 +541,8 @@
     before = jnp.cumsum(onehot, axis=0) - onehot
     target = (flat * CAP + jnp.sum(before * onehot, axis=1)).reshape(rows_dev, 2).astype(jnp.float32)
 
-    keys, values = key_value[0, :, 0], key_value[0, :, 1]
-
-    packed = pack_heads(query[0], keys, values, firsts, span)
+
+    packed = pack_heads(query[0], key_value[0], firsts, span)
     packed = lax.all_to_all(packed, "seq", split_axis=0, concat_axis=0, tiled=True)
     packed = packed.reshape(group, 3 * span)
     context = attention(packed, segment_ids[0], heads)

time: 225 us -> 225 us (level)
    slice x1 -> x0, local copies, waits for them, and re-layouts: 2.3 us -> none  [body(): keys, values = (key_value[0, :, 0], key_value[0, :, 1])]
    unnamed x39 -> x41, local copies, waits for them, and re-layouts: 5.63 us -> 7.64 us
where the time goes in v15:
time: 225 us
  waiting for transfers between devices  106 us (47%)
  Pallas kernels  58.5 us (26%)
  starting transfers between devices  50 us (22%)
  local copies, waits for them, and re-layouts  8.24 us (4%)
    ppermute x30, waiting for transfers between devices, swap(): return lax.ppermute(a, axis, [(i, i ^ distance) for i in range(size)])  69.3 us
    ppermute x30, starting transfers between devices, swap(): return lax.ppermute(a, axis, [(i, i ^ distance) for i in range(size)])  35.4 us
    pallas_call x2, Pallas kernels, expert_rows(): pl.pallas_call(functools.partial(rows_kernel, local, len(waits)), out_sha...  31.3 us
    all_to_all x1, waiting for transfers between devices, body(): lax.all_to_all(packed, 'seq', split_axis=0, concat_axis=0, tiled=True)  25.3 us
    all_to_all x1, waiting for transfers between devices, body(): lax.all_to_all(context.reshape(n_seq, rows_dev, span), 'seq', split_axis=...  11.1 us
    pallas_call x2, Pallas kernels, put_rows(): pl.pallas_call(functools.partial(put_kernel, local, rows_dev, planes, len...  8.15 us
    unnamed x41, local copies, waits for them, and re-layouts  7.64 us
    pallas_call x2, Pallas kernels, select_rows(): pl.pallas_call(functools.partial(select_kernel, local, rows_dev, len(piec...  7.31 us
  transfers between devices with their start and end apart: 33, of which 23 were waited for; matrix products, arithmetic and copies ran while one was open for 1% of the time, Pallas kernels for 20%

profile of v15, /device:TPU:0, one launch (start us, length us, event | category | flops | bytes accessed | tf_op | source)
XLA Modules:
  0.0 224.9 jit_solution(12716225600284785490)
XLA Ops:
  2.7 2.4 %shard_map.122 = bf16[8,64,960]{2,1,0:T(8,128)(2,1)} custom-call(bf16[64,2304]{1,0:T(8,128)(2,1)S(1)} %bitcast.23, bf16[64,2,2304]{2,1,0:T(2,128)(2,1)S(1)} %bitcast.21), custom_call_target="tpu_custom_call" | custom-call | bytes 1966080 | tf_op jit(solution)/shard_map/pallas_call | solution.py:154
  5.1 7.3 %all-to-all-start = ((bf16[8,64,960]{2,1,0:T(8,128)(2,1)}), bf16[8,64,960]{2,1,0:T(8,128)(2,1)S(1)}, u32[]{:S(2)}, u32[]{:S(2)}) async-start(bf16[8,64,960]{2,1,0:T(8,128)(2,1)} %shard_map.122), calls=%async_computation | async-start | bytes 2097152 | tf_op jit(solution)/shard_map/all_to_all | solution.py:546
  12.8 25.3 %all-to-all-done = bf16[8,64,960]{2,1,0:T(8,128)(2,1)S(1)} async-done(((bf16[8,64,960]{2,1,0:T(8,128)(2,1)}), bf16[8,64,960]{2,1,0:T(8,128)(2,1)S(1)}, u32[]{:S(2)}, u32[]{:S(2)}) %all-to-all-start) | async-done | bytes 983072 | tf_op jit(solution)/shard_map/all_to_all | solution.py:546
  38.1 5.6 %shard_map.123 = bf16[512,320]{1,0:T(8,128)(2,1)} custom-call(bf16[512,960]{1,0:T(8,128)(2,1)S(1)} %bitcast.19, s32[1,512]{1,0:T(1,128)S(1)} %copy-done.7, s32[512,1]{1,0:T(8,128)S(1)} %copy.32.seg_col_ref), custom_call_target="tpu_custom_call" | custom-call | flops 335544320 | bytes 1310720 | tf_op jit(solution)/shard_map/pallas_call | solution.py:56
  43.7 3.6 %all-to-all-start.1 = ((bf16[8,64,320]{2,1,0:T(8,128)(2,1)}), bf16[8,64,320]{2,1,0:T(8,128)(2,1)S(1)}, u32[]{:S(2)}, u32[]{:S(2)}) async-start(bf16[8,64,320]{2,1,0:T(8,128)(2,1)} %bitcast.4), calls=%async_computation.1 | async-start | bytes 786432 | tf_op jit(solution)/shard_map/all_to_all | solution.py:549
  48.1 11.1 %all-to-all-done.1.context_ref = bf16[8,64,320]{2,1,0:T(8,128)(2,1)S(1)} async-done(((bf16[8,64,320]{2,1,0:T(8,128)(2,1)}), bf16[8,64,320]{2,1,0:T(8,128)(2,1)S(1)}, u32[]{:S(2)}, u32[]{:S(2)}) %all-to-all-start.1) | async-done | bytes 327712 | tf_op jit(solution)/shard_map/all_to_all | solution.py:549
  61.0 1.9 collective-permute-start.7
  63.0 1.5 collective-permute-start
  64.5 7.1 %collective-permute-done.3.refs_4_ = bf16[64,2432]{1,0:T(8,128)(2,1)S(1)} collective-permute-done((bf16[64,2432]{1,0:T(8,128)(2,1)S(1)}, bf16[64,2432]{1,0:T(8,128)(2,1)S(1)}, u32[]{:S(2)}, u32[]{:S(2)}) %collective-permute-start.3) | collective-permute-done | bytes 311328 | tf_op jit(solution)/shard_map/ppermute | solution.py:429
  71.7 1.5 collective-permute-start.5
  73.2 3.9 %collective-permute-start.4 = (bf16[64,2432]{1,0:T(8,128)(2,1)S(1)}, bf16[64,2432]{1,0:T(8,128)(2,1)S(1)}, u32[]{:S(2)}, u32[]{:S(2)}) collective-permute-start(bf16[64,2432]{1,0:T(8,128)(2,1)S(1)} %collective-permute-done.3.refs_4_), channel_id=1, source_target_pairs={{0,4},{4,0},{8,12},{12,8},{16,20},{20,16},{24,28},{28,24},{1,5},{5... | collective-permute-start | bytes 933896 | tf_op jit(solution)/shard_map/ppermute | solution.py:429
  77.6 1.5 collective-permute-done.5.refs_3_.refs_6_
  79.1 4.1 %collective-permute-done.4.refs_4_.refs_5_ = bf16[64,2432]{1,0:T(8,128)(2,1)S(1)} collective-permute-done((bf16[64,2432]{1,0:T(8,128)(2,1)S(1)}, bf16[64,2432]{1,0:T(8,128)(2,1)S(1)}, u32[]{:S(2)}, u32[]{:S(2)}) %collective-permute-start.4) | collective-permute-done | bytes 311328 | tf_op jit(solution)/shard_map/ppermute | solution.py:429
  83.2 2.7 %collective-permute-start.6 = (bf16[64,2432]{1,0:T(8,128)(2,1)S(1)}, bf16[64,2432]{1,0:T(8,128)(2,1)S(1)}, u32[]{:S(2)}, u32[]{:S(2)}) collective-permute-start(bf16[64,2432]{1,0:T(8,128)(2,1)S(1)} %collective-permute-done.5.refs_3_.refs_6_), channel_id=1, source_target_pairs={{0,4},{4,0},{8,12},{12,8},{16,20},{20,16},{24,28},{28,24},{1,5},{5... | collective-permute-start | bytes 933896 | tf_op jit(solution)/shard_map/ppermute | solution.py:429
  86.0 4.5 %collective-permute-done.11.refs_0_ = bf16[64,2432]{1,0:T(8,128)(2,1)} collective-permute-done((bf16[64,2432]{1,0:T(8,128)(2,1)S(1)}, bf16[64,2432]{1,0:T(8,128)(2,1)}, u32[]{:S(2)}, u32[]{:S(2)}) %collective-permute-start.11) | collective-permute-done | bytes 311328 | tf_op jit(solution)/shard_map/ppermute | solution.py:429
  90.6 3.7 %collective-permute-done.6.refs_2_.refs_7_ = bf16[64,2432]{1,0:T(8,128)(2,1)S(1)} collective-permute-done((bf16[64,2432]{1,0:T(8,128)(2,1)S(1)}, bf16[64,2432]{1,0:T(8,128)(2,1)S(1)}, u32[]{:S(2)}, u32[]{:S(2)}) %collective-permute-start.6) | collective-permute-done | bytes 311328 | tf_op jit(solution)/shard_map/ppermute | solution.py:429
  94.2 1.5 collective-permute-start.13
  96.2 2.0 collective-permute-start.12
  98.3 2.7 %collective-permute-done.9.refs_2_ = bf16[64,2432]{1,0:T(8,128)(2,1)} collective-permute-done((bf16[64,2432]{1,0:T(8,128)(2,1)S(1)}, bf16[64,2432]{1,0:T(8,128)(2,1)}, u32[]{:S(2)}, u32[]{:S(2)}) %collective-permute-start.9) | collective-permute-done | bytes 311328 | tf_op jit(solution)/shard_map/ppermute | solution.py:429
  101.0 1.5 collective-permute-start.10
  102.5 1.4 collective-permute-done.13.refs_6_
  105.1 2.2 collective-permute-done.8.refs_1_
  107.3 3.3 %collective-permute-done.10.refs_3_ = bf16[64,2432]{1,0:T(8,128)(2,1)} collective-permute-done((bf16[64,2432]{1,0:T(8,128)(2,1)}, bf16[64,2432]{1,0:T(8,128)(2,1)}, u32[]{:S(2)}, u32[]{:S(2)}) %collective-permute-start.10) | collective-permute-done | bytes 311328 | tf_op jit(solution)/shard_map/ppermute | solution.py:429
  111.2 4.2 %shard_map.127 = (bf16[2,192,2304]{2,1,0:T(8,128)(2,1)S(1)}, bf16[2,192,2304]{2,1,0:T(8,128)(2,1)}, bf16[512,128]{1,0:T(8,128)(2,1)S(1)}) custom-call(s32[2]{0:T(128)S(1)} %add_multiply_fusion.bases_ref, bf16[64,2432]{1,0:T(8,128)(2,1)S(1)} %shard_map.125.refs_0_, bf16[64,2432]{1,0:T(8,128)(2,1)} %collective-permute-done.8.refs_1_, ...), custom_call_target="tpu_custom_call" | custom-call | flops 905969664 | bytes 6029312 | tf_op jit(solution)/shard_map/pallas_call | solution.py:301
  115.3 1.2 copy-done.14
  116.7 1.7 shard_map.128.refs_8_.rest_1_
  118.4 3.1 %shard_map.129 = (bf16[2,192,2304]{2,1,0:T(8,128)(2,1)S(1)}, bf16[2,192,2304]{2,1,0:T(8,128)(2,1)}, bf16[512,128]{1,0:T(8,128)(2,1)S(1)}) custom-call(s32[2]{0:T(128)S(1)} %add_multiply_fusion.bases_ref, bf16[64,2432]{1,0:T(8,128)(2,1)S(1)} %copy-done.9, bf16[64,2432]{1,0:T(8,128)(2,1)S(1)} %collective-permute-done.refs_2_.refs_1_, ...), custom_call_target="tpu_custom_call" | custom-call | flops 905969664 | bytes 6029312 | tf_op jit(solution)/shard_map/pallas_call | solution.py:301
  121.5 1.3 copy-done.12
  123.3 3.7 %all-to-all-start.2 = ((bf16[8,64,640]{2,1,0:T(8,128)(2,1)}), bf16[8,64,640]{2,1,0:T(8,128)(2,1)S(1)}, u32[]{:S(2)}, u32[]{:S(2)}) async-start(bf16[8,64,640]{2,1,0:T(8,128)(2,1)} %shard_map.128.refs_8_.rest_1_), calls=%async_computation.2 | async-start | bytes 1310720 | tf_op jit(solution)/shard_map/all_to_all | solution.py:566
  127.0 1.5 copy-done.15
  128.5 16.2 %shard_map.130 = (bf16[2,192,2304]{2,1,0:T(8,128)(2,1)S(1)}, bf16[2,192,2304]{2,1,0:T(8,128)(2,1)}, f32[8,128]{1,0:T(8,128)S(1)}) custom-call(bf16[2,192,2304]{2,1,0:T(8,128)(2,1)S(1)} %copy-done.15, bf16[2,192,2304]{2,1,0:T(8,128)(2,1)} %collective-permute-done.16.got_ref, bf16[2,720,2304]{2,1,0:T(8,128)(2,1)} %bitcast.26, bf16[2,720,2304]{2,1,0:T(8,128)(2,1)} %bitcast.28, ...), custom_call_target="tpu_custom_call" | custom-call | flops 7644119040 | bytes 26984448 | tf_op jit(solution)/shard_map/pallas_call | solution.py:353
  145.8 1.5 copy-done.13
  147.3 15.1 %shard_map.132 = (bf16[2,192,2304]{2,1,0:T(8,128)(2,1)S(1)}, bf16[2,192,2304]{2,1,0:T(8,128)(2,1)S(1)}, f32[8,128]{1,0:T(8,128)S(1)}) custom-call(bf16[2,192,2304]{2,1,0:T(8,128)(2,1)S(1)} %copy-done.13, bf16[2,192,2304]{2,1,0:T(8,128)(2,1)} %collective-permute-done.15.got_ref, bf16[2,720,2304]{2,1,0:T(8,128)(2,1)} %bitcast.27, ...), custom_call_target="tpu_custom_call" | custom-call | flops 7644119040 | bytes 26984448 | tf_op jit(solution)/shard_map/pallas_call | solution.py:353
  163.0 4.8 %shard_map.133 = (bf16[256,2304]{1,0:T(8,128)(2,1)S(1)}, bf16[128,2304]{1,0:T(8,128)(2,1)S(1)}, bf16[128,2304]{1,0:T(8,128)(2,1)S(1)}, f32[8,128]{1,0:T(8,128)}) custom-call(s32[2]{0:T(128)S(1)} %add_multiply_fusion.bases_ref, bf16[2,192,2304]{2,1,0:T(8,128)(2,1)S(1)} %get-tuple-element.47.y_own_ref, ...), custom_call_target="tpu_custom_call" | custom-call | flops 905969664 | bytes 18874368 | tf_op jit(solution)/shard_map/pallas_call | solution.py:410
  167.7 2.0 collective-permute-start.19
  170.7 12.6 %collective-permute-done.19.rest_0_ = bf16[128,2304]{1,0:T(8,128)(2,1)S(1)} collective-permute-done((bf16[128,2304]{1,0:T(8,128)(2,1)S(1)}, bf16[128,2304]{1,0:T(8,128)(2,1)S(1)}, u32[]{:S(2)}, u32[]{:S(2)}) %collective-permute-start.19) | collective-permute-done | bytes 589856 | tf_op jit(solution)/shard_map/ppermute | solution.py:429
  183.3 1.5 collective-permute-done.20.rest_1_
  186.3 3.4 %shard_map.135 = (bf16[256,2304]{1,0:T(8,128)(2,1)S(1)}, bf16[128,2304]{1,0:T(8,128)(2,1)S(1)}, bf16[128,2304]{1,0:T(8,128)(2,1)S(1)}, f32[8,128]{1,0:T(8,128)S(1)}) custom-call(s32[2]{0:T(128)S(1)} %add_multiply_fusion.bases_ref, bf16[2,192,2304]{2,1,0:T(8,128)(2,1)S(1)} %get-tuple-element.45.y_own_ref, ...), custom_call_target="tpu_custom_call" | custom-call | flops 905969664 | bytes 18874368 | tf_op jit(solution)/shard_map/pallas_call | solution.py:410
  189.7 3.2 %collective-permute-done.21.refs_1_.rest_0_ = bf16[64,2304]{1,0:T(8,128)(2,1)S(1)} collective-permute-done((bf16[64,2304]{1,0:T(8,128)(2,1)S(1)}, bf16[64,2304]{1,0:T(8,128)(2,1)S(1)}, u32[]{:S(2)}, u32[]{:S(2)}) %collective-permute-start.21) | collective-permute-done | bytes 294944 | tf_op jit(solution)/shard_map/ppermute | solution.py:429
  193.7 1.5 collective-permute-start.25
  196.9 3.5 %collective-permute-done.25 = bf16[64,2304]{1,0:T(8,128)(2,1)S(1)} collective-permute-done((bf16[64,2304]{1,0:T(8,128)(2,1)S(1)}, bf16[64,2304]{1,0:T(8,128)(2,1)S(1)}, u32[]{:S(2)}, u32[]{:S(2)}) %collective-permute-start.25) | collective-permute-done | bytes 294944 | tf_op jit(solution)/shard_map/ppermute | solution.py:429
  200.5 3.1 %collective-permute-start.28 = (bf16[64,2304]{1,0:T(8,128)(2,1)S(1)}, bf16[64,2304]{1,0:T(8,128)(2,1)S(1)}, u32[]{:S(2)}, u32[]{:S(2)}) collective-permute-start(bf16[64,2304]{1,0:T(8,128)(2,1)S(1)} %add_convert_fusion.1.rest_2_), channel_id=1, source_target_pairs={{0,16},{4,20},{8,24},{12,28},{16,0},{20,4},{24,8},{28,12},{1,17},{... | collective-permute-start | bytes 884744 | tf_op jit(solution)/shard_map/ppermute | solution.py:429
  203.7 4.1 %collective-permute-done.23.rest_0_ = bf16[128,2304]{1,0:T(8,128)(2,1)S(1)} collective-permute-done((bf16[128,2304]{1,0:T(8,128)(2,1)S(1)}, bf16[128,2304]{1,0:T(8,128)(2,1)S(1)}, u32[]{:S(2)}, u32[]{:S(2)}) %collective-permute-start.23) | collective-permute-done | bytes 589856 | tf_op jit(solution)/shard_map/ppermute | solution.py:429
  209.2 1.2 collective-permute-start.26
  210.4 1.4 collective-permute-start.27
  211.8 1.4 collective-permute-done.28.rest_2_
  213.2 2.7 %collective-permute-done.26.rest_0_ = bf16[64,2304]{1,0:T(8,128)(2,1)S(1)} collective-permute-done((bf16[64,2304]{1,0:T(8,128)(2,1)S(1)}, bf16[64,2304]{1,0:T(8,128)(2,1)S(1)}, u32[]{:S(2)}, u32[]{:S(2)}) %collective-permute-start.26) | collective-permute-done | bytes 294944 | tf_op jit(solution)/shard_map/ppermute | solution.py:429
  217.9 6.2 %collective-permute-done.29 = bf16[64,2304]{1,0:T(8,128)(2,1)S(1)} collective-permute-done((bf16[64,2304]{1,0:T(8,128)(2,1)S(1)}, bf16[64,2304]{1,0:T(8,128)(2,1)S(1)}, u32[]{:S(2)}, u32[]{:S(2)}) %collective-permute-start.29) | collective-permute-done | bytes 294944 | tf_op jit(solution)/shard_map/ppermute | solution.py:429
  (94 shorter events, 19.3 us)
Async XLA Ops:
  2.7 9.7 %copy-start.7 = (s32[1,512]{1,0:T(1,128)S(1)}, s32[1,512]{1,0:T(1,128)}, u32[]{:S(2)}) copy-start(s32[1,512]{1,0:T(1,128)} %seg_row_ref.1) | copy-start | bytes 6148
  2.7 9.8 %copy-start.16 = (bf16[2304]{0:T(1024)(128)(2,1)S(1)}, bf16[2304]{0:T(1024)(128)(2,1)}, u32[]{:S(2)}) copy-start(bf16[2304]{0:T(1024)(128)(2,1)} %param.14) | copy-start | bytes 13828
  2.7 9.8 %copy-start.17 = (s32[1,64,2]{1,2,0:T(2,128)S(1)}, s32[1,64,2]{1,2,0:T(2,128)}, u32[]{:S(2)}) copy-start(s32[1,64,2]{1,2,0:T(2,128)} %param.16) | copy-start | bytes 1540
  5.1 33.0 %all-to-all-start = ((bf16[8,64,960]{2,1,0:T(8,128)(2,1)}), bf16[8,64,960]{2,1,0:T(8,128)(2,1)S(1)}, u32[]{:S(2)}, u32[]{:S(2)}) async-start(bf16[8,64,960]{2,1,0:T(8,128)(2,1)} %shard_map.122), calls=%async_computation | async-start | bytes 2097152 | tf_op jit(solution)/shard_map/all_to_all | solution.py:546
  38.1 9.9 %copy-start.18 = (f32[1,64,2]{1,2,0:T(2,128)S(1)}, f32[1,64,2]{1,2,0:T(2,128)}, u32[]{:S(2)}) copy-start(f32[1,64,2]{1,2,0:T(2,128)} %param.17) | copy-start | bytes 1540
  38.1 21.1 %copy-start.5 = (bf16[1,64,2304]{2,1,0:T(8,128)(2,1)S(1)}, bf16[1,64,2304]{2,1,0:T(8,128)(2,1)}, u32[]{:S(2)}) copy-start(bf16[1,64,2304]{2,1,0:T(8,128)(2,1)} %param.13) | copy-start | bytes 884740
  43.7 15.4 %all-to-all-start.1 = ((bf16[8,64,320]{2,1,0:T(8,128)(2,1)}), bf16[8,64,320]{2,1,0:T(8,128)(2,1)S(1)}, u32[]{:S(2)}, u32[]{:S(2)}) async-start(bf16[8,64,320]{2,1,0:T(8,128)(2,1)} %bitcast.4), calls=%async_computation.1 | async-start | bytes 786432 | tf_op jit(solution)/shard_map/all_to_all | solution.py:549
  59.4 44.5 %copy-start.8 = (bf16[64,2432]{1,0:T(8,128)(2,1)}, bf16[64,2432]{1,0:T(8,128)(2,1)S(1)}, u32[]{:S(2)}) copy-start(bf16[64,2432]{1,0:T(8,128)(2,1)S(1)} %get-tuple-element.36.refs_0_) | copy-start | bytes 933892
  59.4 12.2 %collective-permute-start.3 = (bf16[64,2432]{1,0:T(8,128)(2,1)S(1)}, bf16[64,2432]{1,0:T(8,128)(2,1)S(1)}, u32[]{:S(2)}, u32[]{:S(2)}) collective-permute-start(bf16[64,2432]{1,0:T(8,128)(2,1)S(1)} %get-tuple-element.36.refs_0_), channel_id=1, source_target_pairs={{0,8},{4,12},{8,0},{12,4},{16,24},{20,28},{24,16},{28,20},{1,9},{5... | collective-permute-start | bytes 933896 | tf_op jit(solution)/shard_map/ppermute | solution.py:429
  60.4 16.6 %collective-permute-start.1 = (bf16[64,2432]{1,0:T(8,128)(2,1)S(1)}, bf16[64,2432]{1,0:T(8,128)(2,1)S(1)}, u32[]{:S(2)}, u32[]{:S(2)}) collective-permute-start(bf16[64,2432]{1,0:T(8,128)(2,1)S(1)} %get-tuple-element.36.refs_0_), channel_id=1, source_target_pairs={{0,4},{4,0},{8,12},{12,8},{16,20},{20,16},{24,28},{28,24},{1,5},{5... | collective-permute-start | bytes 933896 | tf_op jit(solution)/shard_map/ppermute | solution.py:429
  61.0 16.5 %collective-permute-start.7 = (bf16[64,2432]{1,0:T(8,128)(2,1)S(1)}, bf16[64,2432]{1,0:T(8,128)(2,1)S(1)}, u32[]{:S(2)}, u32[]{:S(2)}) collective-permute-start(bf16[64,2432]{1,0:T(8,128)(2,1)S(1)} %get-tuple-element.36.refs_0_), channel_id=1, source_target_pairs={{0,16},{4,20},{8,24},{12,28},{16,0},{20,4},{24,8},{28,12},{1,17},{... | collective-permute-start | bytes 933896 | tf_op jit(solution)/shard_map/ppermute | solution.py:429
  63.0 14.6 %collective-permute-start = (bf16[64,2432]{1,0:T(8,128)(2,1)S(1)}, bf16[64,2432]{1,0:T(8,128)(2,1)S(1)}, u32[]{:S(2)}, u32[]{:S(2)}) collective-permute-start(bf16[64,2432]{1,0:T(8,128)(2,1)S(1)} %get-tuple-element.36.refs_0_), channel_id=1, source_target_pairs={{0,2},{1,3},{2,0},{3,1},{4,6},{5,7},{6,4},{7,5},{8,10},{9,11},{10,... | collective-permute-start | bytes 933896 | tf_op jit(solution)/shard_map/ppermute | solution.py:429
  71.7 11.6 %copy-start.10 = (bf16[64,2432]{1,0:T(8,128)(2,1)}, bf16[64,2432]{1,0:T(8,128)(2,1)S(1)}, u32[]{:S(2)}) copy-start(bf16[64,2432]{1,0:T(8,128)(2,1)S(1)} %collective-permute-done.3.refs_4_) | copy-start | bytes 933892
  71.7 7.4 %collective-permute-start.5 = (bf16[64,2432]{1,0:T(8,128)(2,1)S(1)}, bf16[64,2432]{1,0:T(8,128)(2,1)S(1)}, u32[]{:S(2)}, u32[]{:S(2)}) collective-permute-start(bf16[64,2432]{1,0:T(8,128)(2,1)S(1)} %collective-permute-done.3.refs_4_), channel_id=1, source_target_pairs={{0,2},{1,3},{2,0},{3,1},{4,6},{5,7},{6,4},{7,5},{8,10},{9,11},{10,... | collective-permute-start | bytes 933896 | tf_op jit(solution)/shard_map/ppermute | solution.py:429
  73.2 10.0 %collective-permute-start.4 = (bf16[64,2432]{1,0:T(8,128)(2,1)S(1)}, bf16[64,2432]{1,0:T(8,128)(2,1)S(1)}, u32[]{:S(2)}, u32[]{:S(2)}) collective-permute-start(bf16[64,2432]{1,0:T(8,128)(2,1)S(1)} %collective-permute-done.3.refs_4_), channel_id=1, source_target_pairs={{0,4},{4,0},{8,12},{12,8},{16,20},{20,16},{24,28},{28,24},{1,5},{5... | collective-permute-start | bytes 933896 | tf_op jit(solution)/shard_map/ppermute | solution.py:429
  77.1 8.9 %collective-permute-start.2 = (bf16[64,2432]{1,0:T(8,128)(2,1)S(1)}, bf16[64,2432]{1,0:T(8,128)(2,1)S(1)}, u32[]{:S(2)}, u32[]{:S(2)}) collective-permute-start(bf16[64,2432]{1,0:T(8,128)(2,1)S(1)} %collective-permute-done.1.refs_1_.refs_2_), channel_id=1, source_target_pairs={{0,2},{1,3},{2,0},{3,1},{4,6},{5,7},{6,4},{7,5},{8,10},{9,11},{10,... | collective-permute-start | bytes 933896 | tf_op jit(solution)/shard_map/ppermute | solution.py:429
  83.2 7.3 %collective-permute-start.11 = (bf16[64,2432]{1,0:T(8,128)(2,1)S(1)}, bf16[64,2432]{1,0:T(8,128)(2,1)}, u32[]{:S(2)}, u32[]{:S(2)}) collective-permute-start(bf16[64,2432]{1,0:T(8,128)(2,1)S(1)} %shard_map.125.refs_0_), channel_id=1, source_target_pairs={{0,8},{4,12},{8,0},{12,4},{16,24},{20,28},{24,16},{28,20},{1,9},{5... | collective-permute-start | bytes 933896 | tf_op jit(solution)/shard_map/ppermute | solution.py:429
  83.2 11.0 %collective-permute-start.6 = (bf16[64,2432]{1,0:T(8,128)(2,1)S(1)}, bf16[64,2432]{1,0:T(8,128)(2,1)S(1)}, u32[]{:S(2)}, u32[]{:S(2)}) collective-permute-start(bf16[64,2432]{1,0:T(8,128)(2,1)S(1)} %collective-permute-done.5.refs_3_.refs_6_), channel_id=1, source_target_pairs={{0,4},{4,0},{8,12},{12,8},{16,20},{20,16},{24,28},{28,24},{1,5},{5... | collective-permute-start | bytes 933896 | tf_op jit(solution)/shard_map/ppermute | solution.py:429
  85.9 15.1 %collective-permute-start.9 = (bf16[64,2432]{1,0:T(8,128)(2,1)S(1)}, bf16[64,2432]{1,0:T(8,128)(2,1)}, u32[]{:S(2)}, u32[]{:S(2)}) collective-permute-start(bf16[64,2432]{1,0:T(8,128)(2,1)S(1)} %shard_map.125.refs_0_), channel_id=1, source_target_pairs={{0,4},{4,0},{8,12},{12,8},{16,20},{20,16},{24,28},{28,24},{1,5},{5... | collective-permute-start | bytes 933896 | tf_op jit(solution)/shard_map/ppermute | solution.py:429
  86.0 15.0 %copy-start.1 = (bf16[64,2432]{1,0:T(8,128)(2,1)}, bf16[64,2432]{1,0:T(8,128)(2,1)S(1)}, u32[]{:S(2)}) copy-start(bf16[64,2432]{1,0:T(8,128)(2,1)S(1)} %collective-permute-done.2.refs_1_.refs_3_) | copy-start | bytes 933892
  94.2 8.3 %copy-start.3 = (bf16[64,2432]{1,0:T(8,128)(2,1)}, bf16[64,2432]{1,0:T(8,128)(2,1)S(1)}, u32[]{:S(2)}) copy-start(bf16[64,2432]{1,0:T(8,128)(2,1)S(1)} %collective-permute-done.6.refs_2_.refs_7_) | copy-start | bytes 933892
  94.2 22.3 %copy-start.19 = (s32[1,32]{1,0:T(1,128)S(1)}, s32[1,32]{1,0:T(1,128)}, u32[]{:S(2)}) copy-start(s32[1,32]{1,0:T(1,128)} %param.18) | copy-start | bytes 388
  94.2 9.7 %collective-permute-start.13 = (bf16[64,2432]{1,0:T(8,128)(2,1)}, bf16[64,2432]{1,0:T(8,128)(2,1)}, u32[]{:S(2)}, u32[]{:S(2)}) collective-permute-start(bf16[64,2432]{1,0:T(8,128)(2,1)} %shard_map.126.refs_4_), channel_id=1, source_target_pairs={{0,2},{1,3},{2,0},{3,1},{4,6},{5,7},{6,4},{7,5},{8,10},{9,11},{10,... | collective-permute-start | bytes 933896 | tf_op jit(solution)/shard_map/ppermute | solution.py:429
  95.7 11.5 %collective-permute-start.8 = (bf16[64,2432]{1,0:T(8,128)(2,1)S(1)}, bf16[64,2432]{1,0:T(8,128)(2,1)}, u32[]{:S(2)}, u32[]{:S(2)}) collective-permute-start(bf16[64,2432]{1,0:T(8,128)(2,1)S(1)} %shard_map.125.refs_0_), channel_id=1, source_target_pairs={{0,2},{1,3},{2,0},{3,1},{4,6},{5,7},{6,4},{7,5},{8,10},{9,11},{10,... | collective-permute-start | bytes 933896 | tf_op jit(solution)/shard_map/ppermute | solution.py:429
  96.2 14.4 %collective-permute-start.12 = (bf16[64,2432]{1,0:T(8,128)(2,1)}, bf16[64,2432]{1,0:T(8,128)(2,1)}, u32[]{:S(2)}, u32[]{:S(2)}) collective-permute-start(bf16[64,2432]{1,0:T(8,128)(2,1)} %shard_map.126.refs_4_), channel_id=1, source_target_pairs={{0,4},{4,0},{8,12},{12,8},{16,20},{20,16},{24,28},{28,24},{1,5},{5... | collective-permute-start | bytes 933896 | tf_op jit(solution)/shard_map/ppermute | solution.py:429
  101.0 9.6 %collective-permute-start.10 = (bf16[64,2432]{1,0:T(8,128)(2,1)}, bf16[64,2432]{1,0:T(8,128)(2,1)}, u32[]{:S(2)}, u32[]{:S(2)}) collective-permute-start(bf16[64,2432]{1,0:T(8,128)(2,1)} %collective-permute-done.9.refs_2_), channel_id=1, source_target_pairs={{0,2},{1,3},{2,0},{3,1},{4,6},{5,7},{6,4},{7,5},{8,10},{9,11},{10,... | collective-permute-start | bytes 933896 | tf_op jit(solution)/shard_map/ppermute | solution.py:429
  103.9 7.2 %collective-permute-start.14 = (bf16[64,2432]{1,0:T(8,128)(2,1)}, bf16[64,2432]{1,0:T(8,128)(2,1)}, u32[]{:S(2)}, u32[]{:S(2)}) collective-permute-start(bf16[64,2432]{1,0:T(8,128)(2,1)} %collective-permute-done.13.refs_6_), channel_id=1, source_target_pairs={{0,4},{4,0},{8,12},{12,8},{16,20},{20,16},{24,28},{28,24},{1,5},{5... | collective-permute-start | bytes 933896 | tf_op jit(solution)/shard_map/ppermute | solution.py:429
  105.1 13.2 %copy-start.2 = (bf16[64,2432]{1,0:T(8,128)(2,1)S(1)}, bf16[64,2432]{1,0:T(8,128)(2,1)}, u32[]{:S(2)}) copy-start(bf16[64,2432]{1,0:T(8,128)(2,1)} %copy-done.1) | copy-start | bytes 933892
  105.1 13.2 %copy-start.4 = (bf16[64,2432]{1,0:T(8,128)(2,1)S(1)}, bf16[64,2432]{1,0:T(8,128)(2,1)}, u32[]{:S(2)}) copy-start(bf16[64,2432]{1,0:T(8,128)(2,1)} %copy-done.3) | copy-start | bytes 933892
  105.1 13.2 %copy-start.9 = (bf16[64,2432]{1,0:T(8,128)(2,1)S(1)}, bf16[64,2432]{1,0:T(8,128)(2,1)}, u32[]{:S(2)}) copy-start(bf16[64,2432]{1,0:T(8,128)(2,1)} %copy-done.8) | copy-start | bytes 933892
  105.1 13.2 %copy-start.11 = (bf16[64,2432]{1,0:T(8,128)(2,1)S(1)}, bf16[64,2432]{1,0:T(8,128)(2,1)}, u32[]{:S(2)}) copy-start(bf16[64,2432]{1,0:T(8,128)(2,1)} %copy-done.10) | copy-start | bytes 933892
  116.6 10.5 %collective-permute-start.16 = (bf16[2,192,2304]{2,1,0:T(8,128)(2,1)}, bf16[2,192,2304]{2,1,0:T(8,128)(2,1)}, u32[]{:S(2)}, u32[]{:S(2)}) collective-permute-start(bf16[2,192,2304]{2,1,0:T(8,128)(2,1)} %get-tuple-element.41), channel_id=1, source_target_pairs={{0,1},{1,0},{2,3},{3,2},{4,5},{5,4},{6,7},{7,6},{8,9},{9,8},{10,11... | collective-permute-start | bytes 5308424 | tf_op jit(solution)/shard_map/ppermute | solution.py:429
  122.8 23.0 %collective-permute-start.15 = (bf16[2,192,2304]{2,1,0:T(8,128)(2,1)}, bf16[2,192,2304]{2,1,0:T(8,128)(2,1)}, u32[]{:S(2)}, u32[]{:S(2)}) collective-permute-start(bf16[2,192,2304]{2,1,0:T(8,128)(2,1)} %get-tuple-element.39), channel_id=1, source_target_pairs={{0,1},{1,0},{2,3},{3,2},{4,5},{5,4},{6,7},{7,6},{8,9},{9,8},{10,11... | collective-permute-start | bytes 5308424 | tf_op jit(solution)/shard_map/ppermute | solution.py:429
  123.3 21.5 %all-to-all-start.2 = ((bf16[8,64,640]{2,1,0:T(8,128)(2,1)}), bf16[8,64,640]{2,1,0:T(8,128)(2,1)S(1)}, u32[]{:S(2)}, u32[]{:S(2)}) async-start(bf16[8,64,640]{2,1,0:T(8,128)(2,1)} %shard_map.128.refs_8_.rest_1_), calls=%async_computation.2 | async-start | bytes 1310720 | tf_op jit(solution)/shard_map/all_to_all | solution.py:566
  127.0 1.5 copy-start.15
  144.7 18.3 %collective-permute-start.18 = (bf16[2,192,2304]{2,1,0:T(8,128)(2,1)}, bf16[2,192,2304]{2,1,0:T(8,128)(2,1)}, u32[]{:S(2)}, u32[]{:S(2)}) collective-permute-start(bf16[2,192,2304]{2,1,0:T(8,128)(2,1)} %get-tuple-element.48), channel_id=1, source_target_pairs={{0,1},{1,0},{2,3},{3,2},{4,5},{5,4},{6,7},{7,6},{8,9},{9,8},{10,11... | collective-permute-start | bytes 5308424 | tf_op jit(solution)/shard_map/ppermute | solution.py:429
  162.4 23.9 %collective-permute-start.17 = (bf16[2,192,2304]{2,1,0:T(8,128)(2,1)S(1)}, bf16[2,192,2304]{2,1,0:T(8,128)(2,1)S(1)}, u32[]{:S(2)}, u32[]{:S(2)}) collective-permute-start(bf16[2,192,2304]{2,1,0:T(8,128)(2,1)S(1)} %get-tuple-element.46), channel_id=1, source_target_pairs={{0,1},{1,0},{2,3},{3,2},{4,5},{5,4},{6,7},{7,6},{8,9},{9,8},{10,11... | collective-permute-start | bytes 5308424 | tf_op jit(solution)/shard_map/ppermute | solution.py:429
  167.7 15.5 %collective-permute-start.19 = (bf16[128,2304]{1,0:T(8,128)(2,1)S(1)}, bf16[128,2304]{1,0:T(8,128)(2,1)S(1)}, u32[]{:S(2)}, u32[]{:S(2)}) collective-permute-start(bf16[128,2304]{1,0:T(8,128)(2,1)S(1)} %get-tuple-element.51), channel_id=1, source_target_pairs={{0,4},{4,0},{8,12},{12,8},{16,20},{20,16},{24,28},{28,24},{1,5},{5... | collective-permute-start | bytes 1769480 | tf_op jit(solution)/shard_map/ppermute | solution.py:429
  169.8 15.0 %collective-permute-start.20 = (bf16[128,2304]{1,0:T(8,128)(2,1)S(1)}, bf16[128,2304]{1,0:T(8,128)(2,1)S(1)}, u32[]{:S(2)}, u32[]{:S(2)}) collective-permute-start(bf16[128,2304]{1,0:T(8,128)(2,1)S(1)} %get-tuple-element.52), channel_id=1, source_target_pairs={{0,2},{1,3},{2,0},{3,1},{4,6},{5,7},{6,4},{7,5},{8,10},{9,11},{10,... | collective-permute-start | bytes 1769480 | tf_op jit(solution)/shard_map/ppermute | solution.py:429
  185.0 7.8 %collective-permute-start.21 = (bf16[64,2304]{1,0:T(8,128)(2,1)S(1)}, bf16[64,2304]{1,0:T(8,128)(2,1)S(1)}, u32[]{:S(2)}, u32[]{:S(2)}) collective-permute-start(bf16[64,2304]{1,0:T(8,128)(2,1)S(1)} %get-tuple-element.53.rest_0_), channel_id=1, source_target_pairs={{0,2},{1,3},{2,0},{3,1},{4,6},{5,7},{6,4},{7,5},{8,10},{9,11},{10,... | collective-permute-start | bytes 884744 | tf_op jit(solution)/shard_map/ppermute | solution.py:429
  186.0 7.5 %collective-permute-start.22 = (bf16[64,2304]{1,0:T(8,128)(2,1)S(1)}, bf16[64,2304]{1,0:T(8,128)(2,1)S(1)}, u32[]{:S(2)}, u32[]{:S(2)}) collective-permute-start(bf16[64,2304]{1,0:T(8,128)(2,1)S(1)} %get-tuple-element.56), channel_id=1, source_target_pairs={{0,4},{4,0},{8,12},{12,8},{16,20},{20,16},{24,28},{28,24},{1,5},{5... | collective-permute-start | bytes 884744 | tf_op jit(solution)/shard_map/ppermute | solution.py:429
  193.7 6.8 %collective-permute-start.25 = (bf16[64,2304]{1,0:T(8,128)(2,1)S(1)}, bf16[64,2304]{1,0:T(8,128)(2,1)S(1)}, u32[]{:S(2)}, u32[]{:S(2)}) collective-permute-start(bf16[64,2304]{1,0:T(8,128)(2,1)S(1)} %get-tuple-element.61), channel_id=1, source_target_pairs={{0,8},{4,12},{8,0},{12,4},{16,24},{20,28},{24,16},{28,20},{1,9},{5... | collective-permute-start | bytes 884744 | tf_op jit(solution)/shard_map/ppermute | solution.py:429
  195.2 12.6 %collective-permute-start.23 = (bf16[128,2304]{1,0:T(8,128)(2,1)S(1)}, bf16[128,2304]{1,0:T(8,128)(2,1)S(1)}, u32[]{:S(2)}, u32[]{:S(2)}) collective-permute-start(bf16[128,2304]{1,0:T(8,128)(2,1)S(1)} %shard_map.136), channel_id=1, source_target_pairs={{0,4},{4,0},{8,12},{12,8},{16,20},{20,16},{24,28},{28,24},{1,5},{5... | collective-permute-start | bytes 1769480 | tf_op jit(solution)/shard_map/ppermute | solution.py:429
  195.8 13.2 %collective-permute-start.24 = (bf16[128,2304]{1,0:T(8,128)(2,1)S(1)}, bf16[128,2304]{1,0:T(8,128)(2,1)S(1)}, u32[]{:S(2)}, u32[]{:S(2)}) collective-permute-start(bf16[128,2304]{1,0:T(8,128)(2,1)S(1)} %shard_map.137), channel_id=1, source_target_pairs={{0,2},{1,3},{2,0},{3,1},{4,6},{5,7},{6,4},{7,5},{8,10},{9,11},{10,... | collective-permute-start | bytes 1769480 | tf_op jit(solution)/shard_map/ppermute | solution.py:429
  200.5 12.7 %collective-permute-start.28 = (bf16[64,2304]{1,0:T(8,128)(2,1)S(1)}, bf16[64,2304]{1,0:T(8,128)(2,1)S(1)}, u32[]{:S(2)}, u32[]{:S(2)}) collective-permute-start(bf16[64,2304]{1,0:T(8,128)(2,1)S(1)} %add_convert_fusion.1.rest_2_), channel_id=1, source_target_pairs={{0,16},{4,20},{8,24},{12,28},{16,0},{20,4},{24,8},{28,12},{1,17},{... | collective-permute-start | bytes 884744 | tf_op jit(solution)/shard_map/ppermute | solution.py:429
  209.2 6.8 %collective-permute-start.26 = (bf16[64,2304]{1,0:T(8,128)(2,1)S(1)}, bf16[64,2304]{1,0:T(8,128)(2,1)S(1)}, u32[]{:S(2)}, u32[]{:S(2)}) collective-permute-start(bf16[64,2304]{1,0:T(8,128)(2,1)S(1)} %get-tuple-element.63), channel_id=1, source_target_pairs={{0,2},{1,3},{2,0},{3,1},{4,6},{5,7},{6,4},{7,5},{8,10},{9,11},{10,... | collective-permute-start | bytes 884744 | tf_op jit(solution)/shard_map/ppermute | solution.py:429
  210.4 6.7 %collective-permute-start.27 = (bf16[64,2304]{1,0:T(8,128)(2,1)S(1)}, bf16[64,2304]{1,0:T(8,128)(2,1)S(1)}, u32[]{:S(2)}, u32[]{:S(2)}) collective-permute-start(bf16[64,2304]{1,0:T(8,128)(2,1)S(1)} %get-tuple-element.64), channel_id=1, source_target_pairs={{0,4},{4,0},{8,12},{12,8},{16,20},{20,16},{24,28},{28,24},{1,5},{5... | collective-permute-start | bytes 884744 | tf_op jit(solution)/shard_map/ppermute | solution.py:429
  217.3 6.8 %collective-permute-start.29 = (bf16[64,2304]{1,0:T(8,128)(2,1)S(1)}, bf16[64,2304]{1,0:T(8,128)(2,1)S(1)}, u32[]{:S(2)}, u32[]{:S(2)}) collective-permute-start(bf16[64,2304]{1,0:T(8,128)(2,1)S(1)} %get-tuple-element.66), channel_id=1, source_target_pairs={{0,8},{4,12},{8,0},{12,4},{16,24},{20,28},{24,16},{28,20},{1,9},{5... | collective-permute-start | bytes 884744 | tf_op jit(solution)/shard_map/ppermute | solution.py:429
  (5 other events, 6.0 us)

commit v16 on v12

--- a/solution.py
+++ b/solution.py
@@ -28,7 +28,7 @@
 def attention_kernel(heads, q_rows, packed_ref, seg_row_ref, seg_col_ref, out_ref):
     total = packed_ref.shape[0]
     span = heads * HEAD_DIM
-    scale = 1.0 / math.sqrt(HEAD_DIM)
+    scale = jnp.bfloat16(1.0 / math.sqrt(HEAD_DIM))
     for start in range(0, total, q_rows):
         end = start + q_rows
         q_place = start + lax.broadcasted_iota(jnp.int32, (q_rows, end), 0)
@@ -37,11 +37,11 @@
         parts = []
         for h in range(heads):
             a = h * HEAD_DIM
-            q = packed_ref[start:end, a : a + HEAD_DIM]
+            q = packed_ref[start:end, a : a + HEAD_DIM] * scale
             k = packed_ref[:end, span + a : span + a + HEAD_DIM]
             v = packed_ref[:end, 2 * span + a : 2 * span + a + HEAD_DIM]
             s = lax.dot_general(q, k, (((1,), (1,)), ((), ())), preferred_element_type=jnp.float32)
-            s = jnp.where(visible, s * scale, -1e30)
+            s = jnp.where(visible, s, -1e30)
             top = jnp.max(s, axis=1, keepdims=True)
             p = jnp.exp(s - top)
             denominator = jnp.sum(p, axis=1, keepdims=True)
@@ -500,10 +500,10 @@
     own_a, sib_a, ended = expert_rows(own_a, got_a, w_gate, w_up, w_down, [facts_b, pages])
     cache, filled = fill(ended)
     got_a = core(sib_a)
-    own_b, sib_b, ended = expert_rows(own_b, got_b, w_gate, w_up, w_down, [filled])
+    own_b, sib_b, ended = expert_rows(own_b, got_b, w_gate, w_up, w_down, [ended])
     got_b = core(sib_b)
     keep_a, (fx_a, fy_a), _ = put_rows(own_a, got_a, facts_a, bases, piece.shape[0], [ended])
-    keep_a, (gy_a, gx_a) = fold(keep_a, [x(fx_a), y(fy_a)], 2)
+    keep_a, (gy_a, gx_a) = fold(keep_a, [x(fx_a), y(fy_a)], 2, [filled])
     keep_b, (fx_b, fy_b), put_b = put_rows(own_b, got_b, facts_b, bases, piece.shape[0], [gy_a])
     gy_a, gx_a = y(gy_a), x(gx_a)
     fx_b, fy_b = hold(fx_b, [gy_a, gx_a]), hold(fy_b, [gy_a, gx_a])

time: 225 us -> 221 us (0.982)
    ppermute x30, waiting for transfers between devices: 69.2 us -> 60.1 us  [swap(): return lax.ppermute(a, axis, [(i, i ^ distance) for i in range(size)])]
    all_to_all x1, waiting for transfers between devices: 0.01 us -> 8.17 us  [fill_cache(): sent = lax.all_to_all(pages, 'seq', split_axis=0, concat_axis=0, tiled=True)]
    pallas_call x2, Pallas kernels: 7.3 us -> 4.82 us  [select_rows(): pl.pallas_call(functools.partial(select_kernel, local, rows_dev, len(piec...]
  transfers between devices with their start and end apart: 33 -> 33, of which waited for: 23 -> 25; matrix products, arithmetic and copies ran while one was open for 1% -> 1% of each run, Pallas kernels for 21% -> 21%
where the time goes in v16:
time: 221 us; the launch traced here: 220 us
  waiting for transfers between devices  105 us (48%)
  Pallas kernels  56.1 us (25%)
  starting transfers between devices  50.4 us (23%)
  local copies, waits for them, and re-layouts  6.63 us (3%)
    ppermute x30, waiting for transfers between devices, swap(): return lax.ppermute(a, axis, [(i, i ^ distance) for i in range(size)])  60.1 us
    ppermute x30, starting transfers between devices, swap(): return lax.ppermute(a, axis, [(i, i ^ distance) for i in range(size)])  35 us
    pallas_call x2, Pallas kernels, expert_rows(): pl.pallas_call(functools.partial(rows_kernel, local, len(waits)), out_sha...  29.6 us
    all_to_all x1, waiting for transfers between devices, body(): lax.all_to_all(packed, 'seq', split_axis=0, concat_axis=0, tiled=True)  25.4 us
    all_to_all x1, waiting for transfers between devices, body(): lax.all_to_all(context.reshape(n_seq, rows_dev, span), 'seq', split_axis=...  11 us
    pallas_call x2, Pallas kernels, put_rows(): pl.pallas_call(functools.partial(put_kernel, local, rows_dev, planes, len...  9.82 us
    all_to_all x1, waiting for transfers between devices, fill_cache(): sent = lax.all_to_all(pages, 'seq', split_axis=0, concat_axis=0, tiled=True)  8.17 us
    all_to_all x1, starting transfers between devices, body(): lax.all_to_all(packed, 'seq', split_axis=0, concat_axis=0, tiled=True)  7.25 us
  transfers between devices with their start and end apart: 33, of which 25 were waited for; matrix products, arithmetic and copies ran while one was open for 1% of the time, Pallas kernels for 21%

profile of v16, /device:TPU:0, one launch (start us, length us, event | category | flops | bytes accessed | tf_op | source)
XLA Modules:
  0.0 220.2 jit_solution(10827185537345710189)
XLA Ops:
  0.6 2.3 %fusion.3 = (bf16[1,64,1,2304]{3,2,1,0:T(2,128)(2,1)S(1)}, bf16[1,64,1,2304]{3,2,1,0:T(2,128)(2,1)S(1)}) fusion(bf16[1,64,2,2304]{3,2,1,0:T(2,128)(2,1)} %param.12), kind=kLoop, calls=%fused_computation.14 | loop fusion | bytes 1179648 | tf_op jit(solution)/shard_map/slice | solution.py:545
  3.1 1.2 shard_map.122
  4.3 7.3 %all-to-all-start = ((bf16[8,64,960]{2,1,0:T(8,128)(2,1)}), bf16[8,64,960]{2,1,0:T(8,128)(2,1)S(1)}, u32[]{:S(2)}, u32[]{:S(2)}) async-start(bf16[8,64,960]{2,1,0:T(8,128)(2,1)} %shard_map.122), calls=%async_computation | async-start | bytes 2097152 | tf_op jit(solution)/shard_map/all_to_all | solution.py:548
  12.0 25.4 %all-to-all-done = bf16[8,64,960]{2,1,0:T(8,128)(2,1)S(1)} async-done(((bf16[8,64,960]{2,1,0:T(8,128)(2,1)}), bf16[8,64,960]{2,1,0:T(8,128)(2,1)S(1)}, u32[]{:S(2)}, u32[]{:S(2)}) %all-to-all-start) | async-done | bytes 983072 | tf_op jit(solution)/shard_map/all_to_all | solution.py:548
  37.3 5.6 %shard_map.123 = bf16[512,320]{1,0:T(8,128)(2,1)} custom-call(bf16[512,960]{1,0:T(8,128)(2,1)S(1)} %bitcast.22, s32[1,512]{1,0:T(1,128)S(1)} %copy-done.10, s32[512,1]{1,0:T(8,128)S(1)} %copy.40.seg_col_ref), custom_call_target="tpu_custom_call" | custom-call | flops 335544320 | bytes 1310720 | tf_op jit(solution)/shard_map/pallas_call | solution.py:56
  42.9 3.6 %all-to-all-start.1 = ((bf16[8,64,320]{2,1,0:T(8,128)(2,1)}), bf16[8,64,320]{2,1,0:T(8,128)(2,1)S(1)}, u32[]{:S(2)}, u32[]{:S(2)}) async-start(bf16[8,64,320]{2,1,0:T(8,128)(2,1)} %bitcast.5), calls=%async_computation.1 | async-start | bytes 786432 | tf_op jit(solution)/shard_map/all_to_all | solution.py:551
  47.4 11.0 %all-to-all-done.1.context_ref = bf16[8,64,320]{2,1,0:T(8,128)(2,1)S(1)} async-done(((bf16[8,64,320]{2,1,0:T(8,128)(2,1)}), bf16[8,64,320]{2,1,0:T(8,128)(2,1)S(1)}, u32[]{:S(2)}, u32[]{:S(2)}) %all-to-all-start.1) | async-done | bytes 327712 | tf_op jit(solution)/shard_map/all_to_all | solution.py:551
  60.3 1.5 collective-permute-start
  61.8 1.9 collective-permute-start.7
  63.7 5.9 %collective-permute-done.3.refs_4_ = bf16[64,2432]{1,0:T(8,128)(2,1)S(1)} collective-permute-done((bf16[64,2432]{1,0:T(8,128)(2,1)S(1)}, bf16[64,2432]{1,0:T(8,128)(2,1)S(1)}, u32[]{:S(2)}, u32[]{:S(2)}) %collective-permute-start.3) | collective-permute-done | bytes 311328 | tf_op jit(solution)/shard_map/ppermute | solution.py:430
  69.7 2.5 %collective-permute-start.5 = (bf16[64,2432]{1,0:T(8,128)(2,1)S(1)}, bf16[64,2432]{1,0:T(8,128)(2,1)S(1)}, u32[]{:S(2)}, u32[]{:S(2)}) collective-permute-start(bf16[64,2432]{1,0:T(8,128)(2,1)S(1)} %collective-permute-done.3.refs_4_), channel_id=1, source_target_pairs={{0,2},{1,3},{2,0},{3,1},{4,6},{5,7},{6,4},{7,5},{8,10},{9,11},{10,... | collective-permute-start | bytes 933896 | tf_op jit(solution)/shard_map/ppermute | solution.py:430
  72.2 3.8 %collective-permute-start.4 = (bf16[64,2432]{1,0:T(8,128)(2,1)S(1)}, bf16[64,2432]{1,0:T(8,128)(2,1)S(1)}, u32[]{:S(2)}, u32[]{:S(2)}) collective-permute-start(bf16[64,2432]{1,0:T(8,128)(2,1)S(1)} %collective-permute-done.3.refs_4_), channel_id=1, source_target_pairs={{0,4},{4,0},{8,12},{12,8},{16,20},{20,16},{24,28},{28,24},{1,5},{5... | collective-permute-start | bytes 933896 | tf_op jit(solution)/shard_map/ppermute | solution.py:430
  75.9 1.2 collective-permute-done.7.refs_0_
  77.2 1.5 collective-permute-done.5.refs_3_.refs_6_
  78.7 3.1 %collective-permute-done.4.refs_4_.refs_5_ = bf16[64,2432]{1,0:T(8,128)(2,1)S(1)} collective-permute-done((bf16[64,2432]{1,0:T(8,128)(2,1)S(1)}, bf16[64,2432]{1,0:T(8,128)(2,1)S(1)}, u32[]{:S(2)}, u32[]{:S(2)}) %collective-permute-start.4) | collective-permute-done | bytes 311328 | tf_op jit(solution)/shard_map/ppermute | solution.py:430
  81.8 2.5 %collective-permute-start.6 = (bf16[64,2432]{1,0:T(8,128)(2,1)S(1)}, bf16[64,2432]{1,0:T(8,128)(2,1)S(1)}, u32[]{:S(2)}, u32[]{:S(2)}) collective-permute-start(bf16[64,2432]{1,0:T(8,128)(2,1)S(1)} %collective-permute-done.5.refs_3_.refs_6_), channel_id=1, source_target_pairs={{0,4},{4,0},{8,12},{12,8},{16,20},{20,16},{24,28},{28,24},{1,5},{5... | collective-permute-start | bytes 933896 | tf_op jit(solution)/shard_map/ppermute | solution.py:430
  84.4 4.6 %collective-permute-done.11.refs_0_ = bf16[64,2432]{1,0:T(8,128)(2,1)} collective-permute-done((bf16[64,2432]{1,0:T(8,128)(2,1)S(1)}, bf16[64,2432]{1,0:T(8,128)(2,1)}, u32[]{:S(2)}, u32[]{:S(2)}) %collective-permute-start.11) | collective-permute-done | bytes 311328 | tf_op jit(solution)/shard_map/ppermute | solution.py:430
  88.9 3.6 %collective-permute-done.6.refs_2_.refs_7_ = bf16[64,2432]{1,0:T(8,128)(2,1)S(1)} collective-permute-done((bf16[64,2432]{1,0:T(8,128)(2,1)S(1)}, bf16[64,2432]{1,0:T(8,128)(2,1)S(1)}, u32[]{:S(2)}, u32[]{:S(2)}) %collective-permute-start.6) | collective-permute-done | bytes 311328 | tf_op jit(solution)/shard_map/ppermute | solution.py:430
  92.6 1.9 collective-permute-start.13
  94.6 2.0 collective-permute-start.12
  96.6 2.7 %collective-permute-done.9.refs_2_ = bf16[64,2432]{1,0:T(8,128)(2,1)} collective-permute-done((bf16[64,2432]{1,0:T(8,128)(2,1)S(1)}, bf16[64,2432]{1,0:T(8,128)(2,1)}, u32[]{:S(2)}, u32[]{:S(2)}) %collective-permute-start.9) | collective-permute-done | bytes 311328 | tf_op jit(solution)/shard_map/ppermute | solution.py:430
  99.3 1.9 collective-permute-start.10
  102.1 1.3 collective-permute-start.14
  103.5 1.9 collective-permute-done.8.refs_1_
  105.6 3.1 %collective-permute-done.10.refs_3_ = bf16[64,2432]{1,0:T(8,128)(2,1)} collective-permute-done((bf16[64,2432]{1,0:T(8,128)(2,1)}, bf16[64,2432]{1,0:T(8,128)(2,1)}, u32[]{:S(2)}, u32[]{:S(2)}) %collective-permute-start.10) | collective-permute-done | bytes 311328 | tf_op jit(solution)/shard_map/ppermute | solution.py:430
  109.3 2.9 %shard_map.127 = (bf16[2,192,2304]{2,1,0:T(8,128)(2,1)S(1)}, bf16[2,192,2304]{2,1,0:T(8,128)(2,1)S(1)}, bf16[512,128]{1,0:T(8,128)(2,1)S(1)}) custom-call(s32[2]{0:T(128)S(1)} %add_multiply_fusion.bases_ref, bf16[64,2432]{1,0:T(8,128)(2,1)S(1)} %shard_map.125.refs_0_, bf16[64,2432]{1,0:T(8,128)(2,1)} %collective-permute-done.8.refs_1_, ...), custom_call_target="tpu_custom_call" | custom-call | flops 905969664 | bytes 6029312 | tf_op jit(solution)/shard_map/pallas_call | solution.py:300
  112.4 1.7 shard_map.128.refs_8_.rest_1_
  114.1 1.9 shard_map.129
  116.6 14.8 %shard_map.130 = (bf16[2,192,2304]{2,1,0:T(8,128)(2,1)S(1)}, bf16[2,192,2304]{2,1,0:T(8,128)(2,1)}, f32[8,128]{1,0:T(8,128)S(1)}) custom-call(bf16[2,192,2304]{2,1,0:T(8,128)(2,1)S(1)} %get-tuple-element.40.own_ref, bf16[2,192,2304]{2,1,0:T(8,128)(2,1)S(1)} %collective-permute-done.16.got_ref, bf16[2,720,2304]{2,1,0:T(8,128)(2,1)} %bitcast.28, ...), custom_call_target="tpu_custom_call" | custom-call | flops 7644119040 | bytes 26984448 | tf_op jit(solution)/shard_map/pallas_call | solution.py:349
  131.5 14.8 %shard_map.131 = (bf16[2,192,2304]{2,1,0:T(8,128)(2,1)S(1)}, bf16[2,192,2304]{2,1,0:T(8,128)(2,1)}, f32[8,128]{1,0:T(8,128)S(1)}) custom-call(bf16[2,192,2304]{2,1,0:T(8,128)(2,1)S(1)} %get-tuple-element.38.own_ref, bf16[2,192,2304]{2,1,0:T(8,128)(2,1)S(1)} %collective-permute-done.15.got_ref, bf16[2,720,2304]{2,1,0:T(8,128)(2,1)} %bitcast.29, ...), custom_call_target="tpu_custom_call" | custom-call | flops 7644119040 | bytes 26984448 | tf_op jit(solution)/shard_map/pallas_call | solution.py:349
  146.3 1.2 copy-done
  148.0 4.6 %all-to-all-start.2 = ((bf16[8,64,640]{2,1,0:T(8,128)(2,1)}), bf16[8,64,640]{2,1,0:T(8,128)(2,1)S(1)}, u32[]{:S(2)}, u32[]{:S(2)}) async-start(bf16[8,64,640]{2,1,0:T(8,128)(2,1)} %shard_map.128.refs_8_.rest_1_), calls=%async_computation.2 | async-start | bytes 1310720 | tf_op jit(solution)/shard_map/all_to_all | solution.py:568
  152.6 5.4 %shard_map.132 = (bf16[256,2304]{1,0:T(8,128)(2,1)S(1)}, bf16[128,2304]{1,0:T(8,128)(2,1)}, bf16[128,2304]{1,0:T(8,128)(2,1)}, f32[8,128]{1,0:T(8,128)}) custom-call(s32[2]{0:T(128)S(1)} %add_multiply_fusion.bases_ref, bf16[2,192,2304]{2,1,0:T(8,128)(2,1)S(1)} %get-tuple-element.46.y_own_ref, bf16[2,192,2304]{2,1,0:T(8,128)(2,1)} %collective-permute-done.18.y_got_ref, ...), custom_call_target="tpu_custom_call" | custom-call | flops 905969664 | bytes 18874368 | tf_op jit(solution)/shard_map/pallas_call | solution.py:411
  158.9 2.0 collective-permute-start.19
  161.9 8.2 %all-to-all-done.2.pages_ref = bf16[8,64,640]{2,1,0:T(8,128)(2,1)S(1)} async-done(((bf16[8,64,640]{2,1,0:T(8,128)(2,1)}), bf16[8,64,640]{2,1,0:T(8,128)(2,1)S(1)}, u32[]{:S(2)}, u32[]{:S(2)}) %all-to-all-start.2) | async-done | bytes 655392 | tf_op jit(solution)/shard_map/all_to_all | solution.py:568
  171.0 5.5 %collective-permute-done.19.rest_0_ = bf16[128,2304]{1,0:T(8,128)(2,1)} collective-permute-done((bf16[128,2304]{1,0:T(8,128)(2,1)}, bf16[128,2304]{1,0:T(8,128)(2,1)}, u32[]{:S(2)}, u32[]{:S(2)}) %collective-permute-start.19) | collective-permute-done | bytes 589856 | tf_op jit(solution)/shard_map/ppermute | solution.py:430
  176.5 1.3 copy-done.3
  177.8 1.5 shard_map.134
  180.8 4.5 %shard_map.135 = (bf16[256,2304]{1,0:T(8,128)(2,1)S(1)}, bf16[128,2304]{1,0:T(8,128)(2,1)S(1)}, bf16[128,2304]{1,0:T(8,128)(2,1)S(1)}, f32[8,128]{1,0:T(8,128)S(1)}) custom-call(s32[2]{0:T(128)S(1)} %add_multiply_fusion.bases_ref, bf16[2,192,2304]{2,1,0:T(8,128)(2,1)S(1)} %copy-done.1, bf16[2,192,2304]{2,1,0:T(8,128)(2,1)} %collective-permute-done.17.y_got_ref, ...), custom_call_target="tpu_custom_call" | custom-call | flops 905969664 | bytes 18874368 | tf_op jit(solution)/shard_map/pallas_call | solution.py:411
  185.3 2.4 %collective-permute-done.21.refs_1_.rest_0_ = bf16[64,2304]{1,0:T(8,128)(2,1)S(1)} collective-permute-done((bf16[64,2304]{1,0:T(8,128)(2,1)S(1)}, bf16[64,2304]{1,0:T(8,128)(2,1)S(1)}, u32[]{:S(2)}, u32[]{:S(2)}) %collective-permute-start.21) | collective-permute-done | bytes 294944 | tf_op jit(solution)/shard_map/ppermute | solution.py:430
  188.5 2.2 collective-permute-start.25
  190.6 1.1 collective-permute-start.24
  192.2 3.6 %collective-permute-done.25 = bf16[64,2304]{1,0:T(8,128)(2,1)S(1)} collective-permute-done((bf16[64,2304]{1,0:T(8,128)(2,1)S(1)}, bf16[64,2304]{1,0:T(8,128)(2,1)S(1)}, u32[]{:S(2)}, u32[]{:S(2)}) %collective-permute-start.25) | collective-permute-done | bytes 294944 | tf_op jit(solution)/shard_map/ppermute | solution.py:430
  195.9 2.6 %collective-permute-start.28 = (bf16[64,2304]{1,0:T(8,128)(2,1)S(1)}, bf16[64,2304]{1,0:T(8,128)(2,1)S(1)}, u32[]{:S(2)}, u32[]{:S(2)}) collective-permute-start(bf16[64,2304]{1,0:T(8,128)(2,1)S(1)} %add_convert_fusion.1.rest_2_), channel_id=1, source_target_pairs={{0,16},{4,20},{8,24},{12,28},{16,0},{20,4},{24,8},{28,12},{1,17},{... | collective-permute-start | bytes 884744 | tf_op jit(solution)/shard_map/ppermute | solution.py:430
  198.5 5.1 %collective-permute-done.24.rest_1_ = bf16[128,2304]{1,0:T(8,128)(2,1)S(1)} collective-permute-done((bf16[128,2304]{1,0:T(8,128)(2,1)S(1)}, bf16[128,2304]{1,0:T(8,128)(2,1)S(1)}, u32[]{:S(2)}, u32[]{:S(2)}) %collective-permute-start.24) | collective-permute-done | bytes 589856 | tf_op jit(solution)/shard_map/ppermute | solution.py:430
  206.2 3.3 %collective-permute-done.28.rest_2_ = bf16[64,2304]{1,0:T(8,128)(2,1)S(1)} collective-permute-done((bf16[64,2304]{1,0:T(8,128)(2,1)S(1)}, bf16[64,2304]{1,0:T(8,128)(2,1)S(1)}, u32[]{:S(2)}, u32[]{:S(2)}) %collective-permute-start.28) | collective-permute-done | bytes 294944 | tf_op jit(solution)/shard_map/ppermute | solution.py:430
  209.6 2.0 collective-permute-done.26.rest_0_
  213.0 6.4 %collective-permute-done.29 = bf16[64,2304]{1,0:T(8,128)(2,1)S(1)} collective-permute-done((bf16[64,2304]{1,0:T(8,128)(2,1)S(1)}, bf16[64,2304]{1,0:T(8,128)(2,1)S(1)}, u32[]{:S(2)}, u32[]{:S(2)}) %collective-permute-start.29) | collective-permute-done | bytes 294944 | tf_op jit(solution)/shard_map/ppermute | solution.py:430
  (94 shorter events, 17.0 us)
Async XLA Ops:
  3.0 8.5 %copy-start.10 = (s32[1,512]{1,0:T(1,128)S(1)}, s32[1,512]{1,0:T(1,128)}, u32[]{:S(2)}) copy-start(s32[1,512]{1,0:T(1,128)} %seg_row_ref.1) | copy-start | bytes 6148
  3.0 8.7 %copy-start.16 = (s32[1,64,2]{1,2,0:T(2,128)S(1)}, s32[1,64,2]{1,2,0:T(2,128)}, u32[]{:S(2)}) copy-start(s32[1,64,2]{1,2,0:T(2,128)} %param.16) | copy-start | bytes 1540
  4.3 33.0 %all-to-all-start = ((bf16[8,64,960]{2,1,0:T(8,128)(2,1)}), bf16[8,64,960]{2,1,0:T(8,128)(2,1)S(1)}, u32[]{:S(2)}, u32[]{:S(2)}) async-start(bf16[8,64,960]{2,1,0:T(8,128)(2,1)} %shard_map.122), calls=%async_computation | async-start | bytes 2097152 | tf_op jit(solution)/shard_map/all_to_all | solution.py:548
  37.3 9.9 %copy-start.17 = (f32[1,64,2]{1,2,0:T(2,128)S(1)}, f32[1,64,2]{1,2,0:T(2,128)}, u32[]{:S(2)}) copy-start(f32[1,64,2]{1,2,0:T(2,128)} %param.17) | copy-start | bytes 1540
  37.3 10.0 %copy-start.15 = (bf16[2304]{0:T(1024)(128)(2,1)S(1)}, bf16[2304]{0:T(1024)(128)(2,1)}, u32[]{:S(2)}) copy-start(bf16[2304]{0:T(1024)(128)(2,1)} %param.14) | copy-start | bytes 13828
  37.3 21.0 %copy-start.8 = (bf16[1,64,2304]{2,1,0:T(8,128)(2,1)S(1)}, bf16[1,64,2304]{2,1,0:T(8,128)(2,1)}, u32[]{:S(2)}) copy-start(bf16[1,64,2304]{2,1,0:T(8,128)(2,1)} %param.13) | copy-start | bytes 884740
  42.9 15.4 %all-to-all-start.1 = ((bf16[8,64,320]{2,1,0:T(8,128)(2,1)}), bf16[8,64,320]{2,1,0:T(8,128)(2,1)S(1)}, u32[]{:S(2)}, u32[]{:S(2)}) async-start(bf16[8,64,320]{2,1,0:T(8,128)(2,1)} %bitcast.5), calls=%async_computation.1 | async-start | bytes 786432 | tf_op jit(solution)/shard_map/all_to_all | solution.py:551
  58.6 43.4 %copy-start.11 = (bf16[64,2432]{1,0:T(8,128)(2,1)}, bf16[64,2432]{1,0:T(8,128)(2,1)S(1)}, u32[]{:S(2)}) copy-start(bf16[64,2432]{1,0:T(8,128)(2,1)S(1)} %get-tuple-element.36.refs_0_) | copy-start | bytes 933892
  58.7 11.0 %collective-permute-start.3 = (bf16[64,2432]{1,0:T(8,128)(2,1)S(1)}, bf16[64,2432]{1,0:T(8,128)(2,1)S(1)}, u32[]{:S(2)}, u32[]{:S(2)}) collective-permute-start(bf16[64,2432]{1,0:T(8,128)(2,1)S(1)} %get-tuple-element.36.refs_0_), channel_id=1, source_target_pairs={{0,8},{4,12},{8,0},{12,4},{16,24},{20,28},{24,16},{28,20},{1,9},{5... | collective-permute-start | bytes 933896 | tf_op jit(solution)/shard_map/ppermute | solution.py:430
  59.7 16.3 %collective-permute-start.1 = (bf16[64,2432]{1,0:T(8,128)(2,1)S(1)}, bf16[64,2432]{1,0:T(8,128)(2,1)S(1)}, u32[]{:S(2)}, u32[]{:S(2)}) collective-permute-start(bf16[64,2432]{1,0:T(8,128)(2,1)S(1)} %get-tuple-element.36.refs_0_), channel_id=1, source_target_pairs={{0,4},{4,0},{8,12},{12,8},{16,20},{20,16},{24,28},{28,24},{1,5},{5... | collective-permute-start | bytes 933896 | tf_op jit(solution)/shard_map/ppermute | solution.py:430
  60.3 15.7 %collective-permute-start = (bf16[64,2432]{1,0:T(8,128)(2,1)S(1)}, bf16[64,2432]{1,0:T(8,128)(2,1)S(1)}, u32[]{:S(2)}, u32[]{:S(2)}) collective-permute-start(bf16[64,2432]{1,0:T(8,128)(2,1)S(1)} %get-tuple-element.36.refs_0_), channel_id=1, source_target_pairs={{0,2},{1,3},{2,0},{3,1},{4,6},{5,7},{6,4},{7,5},{8,10},{9,11},{10,... | collective-permute-start | bytes 933896 | tf_op jit(solution)/shard_map/ppermute | solution.py:430
  61.8 15.4 %collective-permute-start.7 = (bf16[64,2432]{1,0:T(8,128)(2,1)S(1)}, bf16[64,2432]{1,0:T(8,128)(2,1)S(1)}, u32[]{:S(2)}, u32[]{:S(2)}) collective-permute-start(bf16[64,2432]{1,0:T(8,128)(2,1)S(1)} %get-tuple-element.36.refs_0_), channel_id=1, source_target_pairs={{0,16},{4,20},{8,24},{12,28},{16,0},{20,4},{24,8},{28,12},{1,17},{... | collective-permute-start | bytes 933896 | tf_op jit(solution)/shard_map/ppermute | solution.py:430
  69.6 12.2 %copy-start.13 = (bf16[64,2432]{1,0:T(8,128)(2,1)}, bf16[64,2432]{1,0:T(8,128)(2,1)S(1)}, u32[]{:S(2)}) copy-start(bf16[64,2432]{1,0:T(8,128)(2,1)S(1)} %collective-permute-done.3.refs_4_) | copy-start | bytes 933892
  69.7 9.1 %collective-permute-start.5 = (bf16[64,2432]{1,0:T(8,128)(2,1)S(1)}, bf16[64,2432]{1,0:T(8,128)(2,1)S(1)}, u32[]{:S(2)}, u32[]{:S(2)}) collective-permute-start(bf16[64,2432]{1,0:T(8,128)(2,1)S(1)} %collective-permute-done.3.refs_4_), channel_id=1, source_target_pairs={{0,2},{1,3},{2,0},{3,1},{4,6},{5,7},{6,4},{7,5},{8,10},{9,11},{10,... | collective-permute-start | bytes 933896 | tf_op jit(solution)/shard_map/ppermute | solution.py:430
  72.2 9.7 %collective-permute-start.4 = (bf16[64,2432]{1,0:T(8,128)(2,1)S(1)}, bf16[64,2432]{1,0:T(8,128)(2,1)S(1)}, u32[]{:S(2)}, u32[]{:S(2)}) collective-permute-start(bf16[64,2432]{1,0:T(8,128)(2,1)S(1)} %collective-permute-done.3.refs_4_), channel_id=1, source_target_pairs={{0,4},{4,0},{8,12},{12,8},{16,20},{20,16},{24,28},{28,24},{1,5},{5... | collective-permute-start | bytes 933896 | tf_op jit(solution)/shard_map/ppermute | solution.py:430
  75.9 8.4 %collective-permute-start.2 = (bf16[64,2432]{1,0:T(8,128)(2,1)S(1)}, bf16[64,2432]{1,0:T(8,128)(2,1)S(1)}, u32[]{:S(2)}, u32[]{:S(2)}) collective-permute-start(bf16[64,2432]{1,0:T(8,128)(2,1)S(1)} %collective-permute-done.1.refs_1_.refs_2_), channel_id=1, source_target_pairs={{0,2},{1,3},{2,0},{3,1},{4,6},{5,7},{6,4},{7,5},{8,10},{9,11},{10,... | collective-permute-start | bytes 933896 | tf_op jit(solution)/shard_map/ppermute | solution.py:430
  81.8 7.1 %collective-permute-start.11 = (bf16[64,2432]{1,0:T(8,128)(2,1)S(1)}, bf16[64,2432]{1,0:T(8,128)(2,1)}, u32[]{:S(2)}, u32[]{:S(2)}) collective-permute-start(bf16[64,2432]{1,0:T(8,128)(2,1)S(1)} %shard_map.125.refs_0_), channel_id=1, source_target_pairs={{0,8},{4,12},{8,0},{12,4},{16,24},{20,28},{24,16},{28,20},{1,9},{5... | collective-permute-start | bytes 933896 | tf_op jit(solution)/shard_map/ppermute | solution.py:430
  81.8 10.7 %collective-permute-start.6 = (bf16[64,2432]{1,0:T(8,128)(2,1)S(1)}, bf16[64,2432]{1,0:T(8,128)(2,1)S(1)}, u32[]{:S(2)}, u32[]{:S(2)}) collective-permute-start(bf16[64,2432]{1,0:T(8,128)(2,1)S(1)} %collective-permute-done.5.refs_3_.refs_6_), channel_id=1, source_target_pairs={{0,4},{4,0},{8,12},{12,8},{16,20},{20,16},{24,28},{28,24},{1,5},{5... | collective-permute-start | bytes 933896 | tf_op jit(solution)/shard_map/ppermute | solution.py:430
  84.3 15.1 %collective-permute-start.9 = (bf16[64,2432]{1,0:T(8,128)(2,1)S(1)}, bf16[64,2432]{1,0:T(8,128)(2,1)}, u32[]{:S(2)}, u32[]{:S(2)}) collective-permute-start(bf16[64,2432]{1,0:T(8,128)(2,1)S(1)} %shard_map.125.refs_0_), channel_id=1, source_target_pairs={{0,4},{4,0},{8,12},{12,8},{16,20},{20,16},{24,28},{28,24},{1,5},{5... | collective-permute-start | bytes 933896 | tf_op jit(solution)/shard_map/ppermute | solution.py:430
  84.4 15.0 %copy-start.4 = (bf16[64,2432]{1,0:T(8,128)(2,1)}, bf16[64,2432]{1,0:T(8,128)(2,1)S(1)}, u32[]{:S(2)}) copy-start(bf16[64,2432]{1,0:T(8,128)(2,1)S(1)} %collective-permute-done.2.refs_1_.refs_3_) | copy-start | bytes 933892
  92.6 8.7 %copy-start.6 = (bf16[64,2432]{1,0:T(8,128)(2,1)}, bf16[64,2432]{1,0:T(8,128)(2,1)S(1)}, u32[]{:S(2)}) copy-start(bf16[64,2432]{1,0:T(8,128)(2,1)S(1)} %collective-permute-done.6.refs_2_.refs_7_) | copy-start | bytes 933892
  92.6 19.7 %copy-start.18 = (s32[1,32]{1,0:T(1,128)S(1)}, s32[1,32]{1,0:T(1,128)}, u32[]{:S(2)}) copy-start(s32[1,32]{1,0:T(1,128)} %param.18) | copy-start | bytes 388
  92.6 9.5 %collective-permute-start.13 = (bf16[64,2432]{1,0:T(8,128)(2,1)}, bf16[64,2432]{1,0:T(8,128)(2,1)}, u32[]{:S(2)}, u32[]{:S(2)}) collective-permute-start(bf16[64,2432]{1,0:T(8,128)(2,1)} %shard_map.126.refs_4_), channel_id=1, source_target_pairs={{0,2},{1,3},{2,0},{3,1},{4,6},{5,7},{6,4},{7,5},{8,10},{9,11},{10,... | collective-permute-start | bytes 933896 | tf_op jit(solution)/shard_map/ppermute | solution.py:430
  94.5 11.0 %collective-permute-start.8 = (bf16[64,2432]{1,0:T(8,128)(2,1)S(1)}, bf16[64,2432]{1,0:T(8,128)(2,1)}, u32[]{:S(2)}, u32[]{:S(2)}) collective-permute-start(bf16[64,2432]{1,0:T(8,128)(2,1)S(1)} %shard_map.125.refs_0_), channel_id=1, source_target_pairs={{0,2},{1,3},{2,0},{3,1},{4,6},{5,7},{6,4},{7,5},{8,10},{9,11},{10,... | collective-permute-start | bytes 933896 | tf_op jit(solution)/shard_map/ppermute | solution.py:430
  94.6 11.0 %collective-permute-start.12 = (bf16[64,2432]{1,0:T(8,128)(2,1)}, bf16[64,2432]{1,0:T(8,128)(2,1)}, u32[]{:S(2)}, u32[]{:S(2)}) collective-permute-start(bf16[64,2432]{1,0:T(8,128)(2,1)} %shard_map.126.refs_4_), channel_id=1, source_target_pairs={{0,4},{4,0},{8,12},{12,8},{16,20},{20,16},{24,28},{28,24},{1,5},{5... | collective-permute-start | bytes 933896 | tf_op jit(solution)/shard_map/ppermute | solution.py:430
  99.3 9.4 %collective-permute-start.10 = (bf16[64,2432]{1,0:T(8,128)(2,1)}, bf16[64,2432]{1,0:T(8,128)(2,1)}, u32[]{:S(2)}, u32[]{:S(2)}) collective-permute-start(bf16[64,2432]{1,0:T(8,128)(2,1)} %collective-permute-done.9.refs_2_), channel_id=1, source_target_pairs={{0,2},{1,3},{2,0},{3,1},{4,6},{5,7},{6,4},{7,5},{8,10},{9,11},{10,... | collective-permute-start | bytes 933896 | tf_op jit(solution)/shard_map/ppermute | solution.py:430
  102.1 7.2 %collective-permute-start.14 = (bf16[64,2432]{1,0:T(8,128)(2,1)}, bf16[64,2432]{1,0:T(8,128)(2,1)}, u32[]{:S(2)}, u32[]{:S(2)}) collective-permute-start(bf16[64,2432]{1,0:T(8,128)(2,1)} %collective-permute-done.13.refs_6_), channel_id=1, source_target_pairs={{0,4},{4,0},{8,12},{12,8},{16,20},{20,16},{24,28},{28,24},{1,5},{5... | collective-permute-start | bytes 933896 | tf_op jit(solution)/shard_map/ppermute | solution.py:430
  103.5 10.6 %copy-start.5 = (bf16[64,2432]{1,0:T(8,128)(2,1)S(1)}, bf16[64,2432]{1,0:T(8,128)(2,1)}, u32[]{:S(2)}) copy-start(bf16[64,2432]{1,0:T(8,128)(2,1)} %copy-done.4) | copy-start | bytes 933892
  103.5 10.6 %copy-start.7 = (bf16[64,2432]{1,0:T(8,128)(2,1)S(1)}, bf16[64,2432]{1,0:T(8,128)(2,1)}, u32[]{:S(2)}) copy-start(bf16[64,2432]{1,0:T(8,128)(2,1)} %copy-done.6) | copy-start | bytes 933892
  103.5 10.6 %copy-start.12 = (bf16[64,2432]{1,0:T(8,128)(2,1)S(1)}, bf16[64,2432]{1,0:T(8,128)(2,1)}, u32[]{:S(2)}) copy-start(bf16[64,2432]{1,0:T(8,128)(2,1)} %copy-done.11) | copy-start | bytes 933892
  103.5 10.6 %copy-start.14 = (bf16[64,2432]{1,0:T(8,128)(2,1)S(1)}, bf16[64,2432]{1,0:T(8,128)(2,1)}, u32[]{:S(2)}) copy-start(bf16[64,2432]{1,0:T(8,128)(2,1)} %copy-done.13) | copy-start | bytes 933892
  112.2 4.4 %collective-permute-start.16 = (bf16[2,192,2304]{2,1,0:T(8,128)(2,1)S(1)}, bf16[2,192,2304]{2,1,0:T(8,128)(2,1)S(1)}, u32[]{:S(2)}, u32[]{:S(2)}) collective-permute-start(bf16[2,192,2304]{2,1,0:T(8,128)(2,1)S(1)} %get-tuple-element.41), channel_id=1, source_target_pairs={{0,1},{1,0},{2,3},{3,2},{4,5},{5,4},{6,7},{7,6},{8,9},{9,8},{10,11... | collective-permute-start | bytes 5308424 | tf_op jit(solution)/shard_map/ppermute | solution.py:430
  116.0 15.5 %collective-permute-start.15 = (bf16[2,192,2304]{2,1,0:T(8,128)(2,1)S(1)}, bf16[2,192,2304]{2,1,0:T(8,128)(2,1)S(1)}, u32[]{:S(2)}, u32[]{:S(2)}) collective-permute-start(bf16[2,192,2304]{2,1,0:T(8,128)(2,1)S(1)} %get-tuple-element.39), channel_id=1, source_target_pairs={{0,1},{1,0},{2,3},{3,2},{4,5},{5,4},{6,7},{7,6},{8,9},{9,8},{10,11... | collective-permute-start | bytes 5308424 | tf_op jit(solution)/shard_map/ppermute | solution.py:430
  131.4 21.2 %collective-permute-start.18 = (bf16[2,192,2304]{2,1,0:T(8,128)(2,1)}, bf16[2,192,2304]{2,1,0:T(8,128)(2,1)}, u32[]{:S(2)}, u32[]{:S(2)}) collective-permute-start(bf16[2,192,2304]{2,1,0:T(8,128)(2,1)} %get-tuple-element.47), channel_id=1, source_target_pairs={{0,1},{1,0},{2,3},{3,2},{4,5},{5,4},{6,7},{7,6},{8,9},{9,8},{10,11... | collective-permute-start | bytes 5308424 | tf_op jit(solution)/shard_map/ppermute | solution.py:430
  147.5 33.3 %collective-permute-start.17 = (bf16[2,192,2304]{2,1,0:T(8,128)(2,1)}, bf16[2,192,2304]{2,1,0:T(8,128)(2,1)}, u32[]{:S(2)}, u32[]{:S(2)}) collective-permute-start(bf16[2,192,2304]{2,1,0:T(8,128)(2,1)} %get-tuple-element.45), channel_id=1, source_target_pairs={{0,1},{1,0},{2,3},{3,2},{4,5},{5,4},{6,7},{7,6},{8,9},{9,8},{10,11... | collective-permute-start | bytes 5308424 | tf_op jit(solution)/shard_map/ppermute | solution.py:430
  148.0 22.1 %all-to-all-start.2 = ((bf16[8,64,640]{2,1,0:T(8,128)(2,1)}), bf16[8,64,640]{2,1,0:T(8,128)(2,1)S(1)}, u32[]{:S(2)}, u32[]{:S(2)}) async-start(bf16[8,64,640]{2,1,0:T(8,128)(2,1)} %shard_map.128.refs_8_.rest_1_), calls=%async_computation.2 | async-start | bytes 1310720 | tf_op jit(solution)/shard_map/all_to_all | solution.py:568
  158.9 21.9 %copy-start.1 = (bf16[2,192,2304]{2,1,0:T(8,128)(2,1)S(1)}, bf16[2,192,2304]{2,1,0:T(8,128)(2,1)}, u32[]{:S(2)}) copy-start(bf16[2,192,2304]{2,1,0:T(8,128)(2,1)} %copy-done) | copy-start | bytes 5308420
  158.9 17.6 %collective-permute-start.19 = (bf16[128,2304]{1,0:T(8,128)(2,1)}, bf16[128,2304]{1,0:T(8,128)(2,1)}, u32[]{:S(2)}, u32[]{:S(2)}) collective-permute-start(bf16[128,2304]{1,0:T(8,128)(2,1)} %get-tuple-element.50), channel_id=1, source_target_pairs={{0,4},{4,0},{8,12},{12,8},{16,20},{20,16},{24,28},{28,24},{1,5},{5... | collective-permute-start | bytes 1769480 | tf_op jit(solution)/shard_map/ppermute | solution.py:430
  161.0 15.6 %collective-permute-start.20 = (bf16[128,2304]{1,0:T(8,128)(2,1)}, bf16[128,2304]{1,0:T(8,128)(2,1)}, u32[]{:S(2)}, u32[]{:S(2)}) collective-permute-start(bf16[128,2304]{1,0:T(8,128)(2,1)} %get-tuple-element.51), channel_id=1, source_target_pairs={{0,2},{1,3},{2,0},{3,1},{4,6},{5,7},{6,4},{7,5},{8,10},{9,11},{10,... | collective-permute-start | bytes 1769480 | tf_op jit(solution)/shard_map/ppermute | solution.py:430
  179.3 8.4 %collective-permute-start.21 = (bf16[64,2304]{1,0:T(8,128)(2,1)S(1)}, bf16[64,2304]{1,0:T(8,128)(2,1)S(1)}, u32[]{:S(2)}, u32[]{:S(2)}) collective-permute-start(bf16[64,2304]{1,0:T(8,128)(2,1)S(1)} %get-tuple-element.53.rest_0_), channel_id=1, source_target_pairs={{0,2},{1,3},{2,0},{3,1},{4,6},{5,7},{6,4},{7,5},{8,10},{9,11},{10,... | collective-permute-start | bytes 884744 | tf_op jit(solution)/shard_map/ppermute | solution.py:430
  180.3 8.0 %collective-permute-start.22 = (bf16[64,2304]{1,0:T(8,128)(2,1)S(1)}, bf16[64,2304]{1,0:T(8,128)(2,1)S(1)}, u32[]{:S(2)}, u32[]{:S(2)}) collective-permute-start(bf16[64,2304]{1,0:T(8,128)(2,1)S(1)} %get-tuple-element.56), channel_id=1, source_target_pairs={{0,4},{4,0},{8,12},{12,8},{16,20},{20,16},{24,28},{28,24},{1,5},{5... | collective-permute-start | bytes 884744 | tf_op jit(solution)/shard_map/ppermute | solution.py:430
  188.5 7.4 %collective-permute-start.25 = (bf16[64,2304]{1,0:T(8,128)(2,1)S(1)}, bf16[64,2304]{1,0:T(8,128)(2,1)S(1)}, u32[]{:S(2)}, u32[]{:S(2)}) collective-permute-start(bf16[64,2304]{1,0:T(8,128)(2,1)S(1)} %get-tuple-element.61), channel_id=1, source_target_pairs={{0,8},{4,12},{8,0},{12,4},{16,24},{20,28},{24,16},{28,20},{1,9},{5... | collective-permute-start | bytes 884744 | tf_op jit(solution)/shard_map/ppermute | solution.py:430
  190.6 13.0 %collective-permute-start.24 = (bf16[128,2304]{1,0:T(8,128)(2,1)S(1)}, bf16[128,2304]{1,0:T(8,128)(2,1)S(1)}, u32[]{:S(2)}, u32[]{:S(2)}) collective-permute-start(bf16[128,2304]{1,0:T(8,128)(2,1)S(1)} %shard_map.137), channel_id=1, source_target_pairs={{0,2},{1,3},{2,0},{3,1},{4,6},{5,7},{6,4},{7,5},{8,10},{9,11},{10,... | collective-permute-start | bytes 1769480 | tf_op jit(solution)/shard_map/ppermute | solution.py:430
  191.8 12.7 %collective-permute-start.23 = (bf16[128,2304]{1,0:T(8,128)(2,1)S(1)}, bf16[128,2304]{1,0:T(8,128)(2,1)S(1)}, u32[]{:S(2)}, u32[]{:S(2)}) collective-permute-start(bf16[128,2304]{1,0:T(8,128)(2,1)S(1)} %shard_map.136), channel_id=1, source_target_pairs={{0,4},{4,0},{8,12},{12,8},{16,20},{20,16},{24,28},{28,24},{1,5},{5... | collective-permute-start | bytes 1769480 | tf_op jit(solution)/shard_map/ppermute | solution.py:430
  195.9 13.6 %collective-permute-start.28 = (bf16[64,2304]{1,0:T(8,128)(2,1)S(1)}, bf16[64,2304]{1,0:T(8,128)(2,1)S(1)}, u32[]{:S(2)}, u32[]{:S(2)}) collective-permute-start(bf16[64,2304]{1,0:T(8,128)(2,1)S(1)} %add_convert_fusion.1.rest_2_), channel_id=1, source_target_pairs={{0,16},{4,20},{8,24},{12,28},{16,0},{20,4},{24,8},{28,12},{1,17},{... | collective-permute-start | bytes 884744 | tf_op jit(solution)/shard_map/ppermute | solution.py:430
  204.8 6.8 %collective-permute-start.26 = (bf16[64,2304]{1,0:T(8,128)(2,1)S(1)}, bf16[64,2304]{1,0:T(8,128)(2,1)S(1)}, u32[]{:S(2)}, u32[]{:S(2)}) collective-permute-start(bf16[64,2304]{1,0:T(8,128)(2,1)S(1)} %get-tuple-element.63), channel_id=1, source_target_pairs={{0,2},{1,3},{2,0},{3,1},{4,6},{5,7},{6,4},{7,5},{8,10},{9,11},{10,... | collective-permute-start | bytes 884744 | tf_op jit(solution)/shard_map/ppermute | solution.py:430
  205.7 6.7 %collective-permute-start.27 = (bf16[64,2304]{1,0:T(8,128)(2,1)S(1)}, bf16[64,2304]{1,0:T(8,128)(2,1)S(1)}, u32[]{:S(2)}, u32[]{:S(2)}) collective-permute-start(bf16[64,2304]{1,0:T(8,128)(2,1)S(1)} %get-tuple-element.64), channel_id=1, source_target_pairs={{0,4},{4,0},{8,12},{12,8},{16,20},{20,16},{24,28},{28,24},{1,5},{5... | collective-permute-start | bytes 884744 | tf_op jit(solution)/shard_map/ppermute | solution.py:430
  212.6 6.8 %collective-permute-start.29 = (bf16[64,2304]{1,0:T(8,128)(2,1)S(1)}, bf16[64,2304]{1,0:T(8,128)(2,1)S(1)}, u32[]{:S(2)}, u32[]{:S(2)}) collective-permute-start(bf16[64,2304]{1,0:T(8,128)(2,1)S(1)} %get-tuple-element.66), channel_id=1, source_target_pairs={{0,8},{4,12},{8,0},{12,4},{16,24},{20,28},{24,16},{28,20},{1,9},{5... | collective-permute-start | bytes 884744 | tf_op jit(solution)/shard_map/ppermute | solution.py:430
  (4 other events, 5.9 us)
